TPU v7x, 32 devices: a whole 2x2x4 slice. The times are simulated.
32 devices in a mesh: section: 4 (over z), expert: 2 (over y), dp: 4 (over x, core).
Axes of the slice: x: 2, y: 2, z: 4, core: 2. Of those that a mesh axis runs over, the one named last changes fastest.
Arguments:
- tokens: bfloat16 [1024, 2048], P(('expert', 'dp')), may hold values from -6 to 6
- expert_ids: int32 [1024, 2], P(('expert', 'dp')), may hold values from 0 to 7, all different within a row; in each aligned block of 128 rows (0 to 127, 128 to 255, ...) at most 48 rows name the same one
- gate_weights: float32 [1024, 2], P(('expert', 'dp')), may hold values from 0.1 to 0.9
- out_grad: bfloat16 [1024, 2048], P(('expert', 'dp')), may hold values from -6 to 6
- inner_weight: bfloat16 [8, 2048, 4096], P(('expert', 'dp'), None, 'section'), may hold values from -0.125 to 0.125
- outer_weight: bfloat16 [8, 4096, 2048], P(('expert', 'dp'), 'section'), may hold values from -0.09375 to 0.09375
- final_gain: float32 [2048], replicated, may hold values from 0.25 to 1.75
- dec_states: bfloat16 [4, 512, 2048], P('section', 'expert'), may hold values from -6 to 6
- src_lengths: int32 [4], P('expert'), may hold values from 64 to 256
- tgt_lengths: int32 [4], P('expert'), may hold values from 32 to 128
- norm_gain: float32 [4, 2048], P('section'), may hold values from 0.25 to 1.75
- query_weight: bfloat16 [4, 2048, 2048], P('section', 'expert', 'dp'), may hold values from -16 to 16
- key_weight: bfloat16 [4, 2048, 2048], P('section', 'expert', 'dp'), may hold values from -16 to 16
- value_weight: bfloat16 [4, 2048, 2048], P('section', 'expert', 'dp'), may hold values from -0.125 to 0.125
- out_weight: bfloat16 [4, 2048, 2048], P('section', 'dp', 'expert'), may hold values from -0.125 to 0.125
Outputs:
- dec_out: bfloat16 [4, 512, 2048], P('section', 'expert', 'dp')
- token_grad: bfloat16 [1024, 2048], P(('expert', 'dp'), 'section')
Inputs may be any that keep to these rules, and one draw needn't show every extreme that they name: `expert_ids`: each token names two different experts; among the 128 tokens of one device no expert is named more than 48 times.
All inputs are finite; a program needn't handle non-finite values.
Results may differ from a plain program's by a relative error of at most 0.014.
The roundings to bfloat16 on the way count: a program that leaves them out, or rounds other values in their place, can miss the bound.
Values may be sent and summed in bfloat16 or wider, within the bound.
No kernel may reach another device: no remote copies, remote signals or barrier semaphores. Data moves between devices by JAX's collectives and lax.ppermute only.
A program may use at most 128 MiB of HBM per device.

v0:
```python
import jax
import jax.numpy as jnp
from jax import lax
from jax.sharding import PartitionSpec as P

HEAD_DIM = 128
SRC_LEN = 256
TGT_LEN = 128


EPSILON = 1e-05


def normalize(values, gain):
    centre = jnp.mean(values, axis=-1, keepdims=True)
    centred = values - centre
    spread = jnp.mean(centred * centred, axis=-1, keepdims=True)
    return centred * lax.rsqrt(spread + EPSILON) * gain


def contract_last(left, right):
    return lax.dot_general(
        left, right, (((1,), (1,)), ((), ())), preferred_element_type=jnp.float32
    )


def place(values, position, group_size, capacity):
    feature_count = values.shape[1]
    buffer = jnp.zeros((group_size * capacity, feature_count), values.dtype)
    filled = buffer.at[position].set(jnp.repeat(values, 2, axis=0))
    return filled.reshape(group_size, capacity, feature_count)


def combine(arrived, position, gate_weights):
    feature_count = arrived.shape[-1]
    picked = arrived.reshape(-1, feature_count)[position]
    picked = picked.reshape(gate_weights.shape[0], 2, feature_count).astype(jnp.float32)
    return jnp.sum(gate_weights[:, :, None] * picked, axis=1)


def expert_forward(inputs, weight_in, weight_out):
    pre_act = jnp.dot(inputs, weight_in, preferred_element_type=jnp.float32)
    hidden = jax.nn.gelu(pre_act).astype(jnp.bfloat16)
    return (pre_act, jnp.dot(hidden, weight_out, preferred_element_type=jnp.float32))


def expert_backward(grads, pre_act, weight_in, weight_out):
    back = contract_last(grads, weight_out)
    slope = jax.vjp(jax.nn.gelu, pre_act)[1](back)[0].astype(jnp.bfloat16)
    return contract_last(slope, weight_in)


def attend(query, keys, values, key_mask):
    sequences = key_mask.shape[0]
    head_count = query.shape[1] // HEAD_DIM
    query_split = query.reshape(sequences, -1, head_count, HEAD_DIM)
    keys_split = keys.reshape(sequences, -1, head_count, HEAD_DIM)
    values_split = values.reshape(sequences, -1, head_count, HEAD_DIM)
    scores = jnp.einsum(
        "bqhd,bkhd->bhqk", query_split, keys_split, preferred_element_type=jnp.float32
    ) * HEAD_DIM ** (-0.5)
    scores = jnp.where(key_mask[:, None, None, :], scores, -1e30)
    highest = jnp.max(scores, axis=-1, keepdims=True)
    weights = jnp.exp(scores - highest)
    probs = (weights / jnp.sum(weights, axis=-1, keepdims=True)).astype(jnp.bfloat16)
    context = jnp.einsum("bhqk,bkhd->bqhd", probs, values_split, preferred_element_type=jnp.float32)
    return context.astype(jnp.bfloat16).reshape(-1, head_count * HEAD_DIM)


def body(
    tokens,
    expert_ids,
    gate_weights,
    out_grad,
    inner_weight,
    outer_weight,
    final_gain,
    dec_states,
    src_lengths,
    tgt_lengths,
    norm_gain,
    query_weight,
    key_weight,
    value_weight,
    out_weight,
):
    token_count, feature_count = tokens.shape
    group_size = lax.axis_size(("expert", "dp"))
    capacity = 3 * token_count // group_size
    target = expert_ids.reshape(-1)
    one_hot = (target[:, None] == jnp.arange(group_size, dtype=jnp.int32)[None, :]).astype(
        jnp.int32
    )
    earlier = jnp.cumsum(one_hot, axis=0) - one_hot
    position = target * capacity + jnp.sum(earlier * one_hot, axis=1)
    send_rows = place(tokens, position, group_size, capacity)
    send_grads = place(out_grad, position, group_size, capacity)
    weight_in = inner_weight[0]
    weight_out = outer_weight[0]
    arrived_rows = lax.all_to_all(
        send_rows, ("expert", "dp"), split_axis=0, concat_axis=0, tiled=True
    )
    pre_act, forward_part = expert_forward(
        arrived_rows.reshape(-1, feature_count), weight_in, weight_out
    )
    arrived_grads = lax.all_to_all(
        send_grads, ("expert", "dp"), split_axis=0, concat_axis=0, tiled=True
    )
    backward_part = expert_backward(
        arrived_grads.reshape(-1, feature_count), pre_act, weight_in, weight_out
    )
    section_width = feature_count // lax.axis_size("section")
    forward_total, backward_total = lax.psum((forward_part, backward_part), "section")
    outputs_home, grads_home = (
        lax.all_to_all(
            forward_total.astype(jnp.bfloat16).reshape(group_size, capacity, feature_count),
            ("expert", "dp"),
            split_axis=0,
            concat_axis=0,
            tiled=True,
        ),
        lax.all_to_all(
            backward_total.astype(jnp.bfloat16).reshape(group_size, capacity, feature_count),
            ("expert", "dp"),
            split_axis=0,
            concat_axis=0,
            tiled=True,
        ),
    )
    mixed = combine(outputs_home, position, gate_weights)
    full_grad = combine(grads_home, position, gate_weights)
    token_grad = lax.dynamic_slice_in_dim(
        full_grad, lax.axis_index("section") * section_width, section_width, 1
    ).astype(jnp.bfloat16)
    memory = normalize(tokens.astype(jnp.float32) + mixed, final_gain).astype(jnp.bfloat16)
    states = dec_states[0]
    normed = normalize(states.astype(jnp.float32), norm_gain[0]).astype(jnp.bfloat16)
    source = lax.all_gather(memory, "dp", axis=0, tiled=True)
    query_sum = jnp.dot(
        normed,
        lax.all_gather(query_weight, "expert", axis=1, tiled=True)[0],
        preferred_element_type=jnp.float32,
    )
    key_sum = jnp.dot(
        source,
        lax.all_gather(key_weight, "expert", axis=1, tiled=True)[0],
        preferred_element_type=jnp.float32,
    )
    value_sum = jnp.dot(
        source,
        lax.all_gather(value_weight, "expert", axis=1, tiled=True)[0],
        preferred_element_type=jnp.float32,
    )
    key_mask = jnp.arange(SRC_LEN, dtype=jnp.int32)[None, :] < src_lengths[:, None]
    context = attend(
        query_sum.astype(jnp.bfloat16),
        key_sum.astype(jnp.bfloat16),
        value_sum.astype(jnp.bfloat16),
        key_mask,
    )
    partial_out = jnp.dot(
        context,
        lax.all_gather(out_weight, "expert", axis=2, tiled=True)[0],
        preferred_element_type=jnp.float32,
    )
    attended = lax.psum_scatter(partial_out, "dp", scatter_dimension=1, tiled=True)
    my_columns = attended.shape[1]
    residual = lax.dynamic_slice_in_dim(
        states, lax.axis_index("dp") * my_columns, my_columns, 1
    ).astype(jnp.float32)
    row_mask = (jnp.arange(TGT_LEN, dtype=jnp.int32)[None, :] < tgt_lengths[:, None]).reshape(-1, 1)
    dec_out = (residual + jnp.where(row_mask, attended, 0.0)).astype(jnp.bfloat16)
    return (dec_out[None], token_grad)


def solution(mesh):
    in_specs = (
        P(("expert", "dp"), None),
        P(("expert", "dp"), None),
        P(("expert", "dp"), None),
        P(("expert", "dp"), None),
        P(("expert", "dp"), None, "section"),
        P(("expert", "dp"), "section", None),
        P(),
        P("section", "expert", None),
        P("expert"),
        P("expert"),
        P("section", None),
        P("section", "expert", "dp"),
        P("section", "expert", "dp"),
        P("section", "expert", "dp"),
        P("section", "dp", "expert"),
    )
    out_specs = (P("section", "expert", "dp"), P(("expert", "dp"), "section"))
    return jax.shard_map(body, mesh=mesh, in_specs=in_specs, out_specs=out_specs, check_vma=False)
```

profile of v0, /device:TPU:0, one launch (start us, length us, event | category | flops | bytes accessed | tf_op | source)
XLA Modules:
  0.0 527.0 jit_solution(2813622174870327155)
XLA Ops:
  7.2 0.8 copy.23
  8.0 0.1 eq.29
  8.1 0.1 eq.25
  8.2 0.7 broadcast_multiply_fusion.1
  8.9 0.6 reduce-window.6
  9.5 0.2 slice_reduce_fusion
  9.7 0.1 copy.22
  9.9 0.1 mul.138
  10.0 1.7 broadcast_in_dim.27
  11.7 0.4 reshape.222
  12.1 0.1 fusion.74
  12.2 3.4 scatter_custom_fusion
  15.7 5.3 %all-to-all-start = ((bf16[8,48,2048]{2,1,0:T(8,128)(2,1)}), bf16[8,48,2048]{2,1,0:T(8,128)(2,1)S(1)}, u32[]{:S(2)}, u32[]{:S(2)}) async-start(bf16[8,48,2048]{2,1,0:T(8,128)(2,1)} %bitcast.6), calls=%async_computation | async-start | bytes 3145728 | tf_op jit(solution)/shard_map/all_to_all | solution.py:100
  21.0 0.6 broadcast_in_dim.32
  21.6 1.2 reshape.230
  22.8 4.1 scatter_custom_fusion.1
  27.0 15.0 %all-to-all-done = bf16[8,48,2048]{2,1,0:T(8,128)(2,1)S(1)} async-done(((bf16[8,48,2048]{2,1,0:T(8,128)(2,1)}), bf16[8,48,2048]{2,1,0:T(8,128)(2,1)S(1)}, u32[]{:S(2)}, u32[]{:S(2)}) %all-to-all-start) | async-done | bytes 1572896 | tf_op jit(solution)/shard_map/all_to_all | solution.py:100
  42.0 4.5 all-to-all-start.2
  46.5 4.1 fusion.7
  50.6 1.2 copy-done.10
  51.8 2.0 fusion.3
  53.8 13.6 %all-to-all-done.2 = bf16[8,48,2048]{2,1,0:T(8,128)(2,1)} async-done(((bf16[8,48,2048]{2,1,0:T(8,128)(2,1)}), bf16[8,48,2048]{2,1,0:T(8,128)(2,1)}, u32[]{:S(2)}, u32[]{:S(2)}) %all-to-all-start.2) | async-done | bytes 1572896 | tf_op jit(solution)/shard_map/all_to_all | solution.py:106
  67.3 10.3 %fusion.5 = f32[384,2048]{1,0:T(8,128)} fusion(bf16[1,2048,1024]{2,1,0:T(8,128)(2,1)} %param.19, f32[384,1024]{1,0:T(8,128)} %copy-done.10, bf16[384,2048]{1,0:T(8,128)(2,1)} %bitcast.22, bf16[1,1024,2048]{2,1,0:T(8,128)(2,1)} %param.20), kind=kOutput, calls=%fused_computation.9 | convolution fusion | flops 3229089792 | bytes 14680064 | tf_op jit(solution)/shard_map/dot_general | solution.py:22
  77.6 212.1 %all-reduce.2 = (bf16[384,2048]{1,0:T(8,128)(2,1)}, bf16[384,2048]{1,0:T(8,128)(2,1)}) all-reduce(f32[384,2048]{1,0:T(8,128)} %fusion.5, f32[384,2048]{1,0:T(8,128)S(1)} %fusion.3), channel_id=1, replica_groups=mesh['section'=4,'expert'=2,'dp'=4] {'section'}, use_global_device_ids=true, to_apply=%region_14.15 | all-reduce | flops 1572864 | bytes 9437184 | tf_op jit(solution)/shard_map/psum | solution.py:113
  289.7 7.8 %all-to-all-start.1 = ((bf16[8,48,2048]{2,1,0:T(8,128)(2,1)}), bf16[8,48,2048]{2,1,0:T(8,128)(2,1)S(1)}, u32[]{:S(2)}, u32[]{:S(2)}) async-start(bf16[8,48,2048]{2,1,0:T(8,128)(2,1)} %bitcast.85), calls=%async_computation.1 | async-start | bytes 3145728 | tf_op jit(solution)/shard_map/all_to_all | solution.py:115
  297.5 0.7 all-gather.10.cloned.1.call-update
  298.2 22.9 %all-to-all-done.1 = bf16[8,48,2048]{2,1,0:T(8,128)(2,1)S(1)} async-done(((bf16[8,48,2048]{2,1,0:T(8,128)(2,1)}), bf16[8,48,2048]{2,1,0:T(8,128)(2,1)S(1)}, u32[]{:S(2)}, u32[]{:S(2)}) %all-to-all-start.1) | async-done | bytes 1572896 | tf_op jit(solution)/shard_map/all_to_all | solution.py:115
  321.1 3.7 all-to-all-start.3
  324.8 0.7 all-gather.12.cloned.1.call-update
  325.5 0.3 all-gather.6.cloned.1.call-start
  325.8 0.1 copy.21
  325.9 2.4 gather_fusion
  328.4 3.4 reshape.200
  331.8 21.8 %all-to-all-done.3 = bf16[8,48,2048]{2,1,0:T(8,128)(2,1)S(1)} async-done(((bf16[8,48,2048]{2,1,0:T(8,128)(2,1)}), bf16[8,48,2048]{2,1,0:T(8,128)(2,1)S(1)}, u32[]{:S(2)}, u32[]{:S(2)}) %all-to-all-start.3) | async-done | bytes 1572896 | tf_op jit(solution)/shard_map/all_to_all | solution.py:122
  353.5 2.4 gather_fusion.1
  356.0 3.5 reshape.201
  359.5 7.8 %multiply_reduce_fusion = (bf16[128,2048]{1,0:T(8,128)(2,1)S(1)}, f32[128,2048]{1,0:T(8,128)S(1)}) fusion(f32[128,2,2048]{2,1,0:T(2,128)} %reshape.201, f32[128,2]{1,0:T(8,128)S(1)} %copy.21, f32[128,2,2048]{2,1,0:T(2,128)S(1)} %copy-done.1), kind=kLoop, calls=%fused_computation.32 | loop fusion | flops 1572864 | bytes 5768192 | tf_op jit(solution)/shard_map/reduce_sum | solution.py:38
  367.2 0.2 fusion.64
  367.4 0.3 multiply_reduce_fusion.2
  367.7 0.2 copy-done.4
  367.9 1.0 multiply_convert_fusion.1
  369.1 0.5 all-gather.8.cloned.1.call-update
  369.6 0.5 all-gather.14.cloned.1.call-update
  370.2 0.3 reduce-scatter.2.cloned.1.call-start
  370.5 0.2 convert_reduce_fusion
  370.8 0.4 fusion.14
  371.3 2.3 fusion.41
  373.7 16.0 %all-gather.12.cloned.1.call-done = bf16[1,2048,512]{2,1,0:T(8,128)(2,1)} async-done(((bf16[1,1024,512]{2,1,0:T(8,128)(2,1)}), bf16[1,2048,512]{2,1,0:T(8,128)(2,1)}) %all-gather.12.cloned.1.call-update) | async-done | bytes 2097168 | tf_op jit(solution)/shard_map/all_gather | solution.py:146
  389.7 24.2 %all-gather.6.cloned.1.call-done = bf16[512,2048]{1,0:T(8,128)(2,1)} async-done(((bf16[128,2048]{1,0:T(8,128)(2,1)}), bf16[512,2048]{1,0:T(8,128)(2,1)}) %all-gather.6.cloned.1.call-update) | async-done | bytes 2097168 | tf_op jit(solution)/shard_map/all_gather | solution.py:138
  413.9 3.5 fusion.38
  417.4 0.1 reshape.192
  417.5 31.0 %all-gather.8.cloned.1.call-done = bf16[1,2048,512]{2,1,0:T(8,128)(2,1)} async-done(((bf16[1,1024,512]{2,1,0:T(8,128)(2,1)}), bf16[1,2048,512]{2,1,0:T(8,128)(2,1)}) %all-gather.8.cloned.1.call-update) | async-done | bytes 2097168 | tf_op jit(solution)/shard_map/all_gather | solution.py:151
  448.4 3.5 fusion.35
  451.9 0.9 reshape.190
  452.8 0.6 fusion.89
  453.4 0.3 fusion.34
  453.8 3.2 fusion.44
  456.9 0.2 copy.28
  457.1 25.8 %all-gather.14.cloned.1.call-done = bf16[1,512,2048]{2,1,0:T(8,128)(2,1)} async-done(((bf16[1,512,1024]{2,1,0:T(8,128)(2,1)}), bf16[1,512,2048]{2,1,0:T(8,128)(2,1)}) %all-gather.14.cloned.1.call-update) | async-done | bytes 2097168 | tf_op jit(solution)/shard_map/all_gather | solution.py:163
  483.0 3.7 fusion.15
  486.7 0.6 copy-done.9
  487.4 0.7 dynamic-slice_convert_fusion
  488.0 30.2 %reduce-scatter.2.cloned.1.call-done = f32[256,512]{1,0:T(8,128)} async-done(((f32[256,2048]{1,0:T(8,128)}), f32[256,512]{1,0:T(8,128)}) %reduce-scatter.2.cloned.1.call-update) | async-done | bytes 524304 | tf_op jit(solution)/shard_map/reduce_scatter | solution.py:166
  518.3 1.9 fusion.65
  (38 shorter events, 0.6 us)
Async XLA Ops:
  15.7 5.3 %copy-start.3 = (bf16[128,2048]{1,0:T(8,128)(2,1)S(1)}, bf16[128,2048]{1,0:T(8,128)(2,1)}, u32[]{:S(2)}) copy-start(bf16[128,2048]{1,0:T(8,128)(2,1)} %param.18) | copy-start | bytes 1572868
  15.7 26.3 %all-to-all-start = ((bf16[8,48,2048]{2,1,0:T(8,128)(2,1)}), bf16[8,48,2048]{2,1,0:T(8,128)(2,1)S(1)}, u32[]{:S(2)}, u32[]{:S(2)}) async-start(bf16[8,48,2048]{2,1,0:T(8,128)(2,1)} %bitcast.6), calls=%async_computation | async-start | bytes 3145728 | tf_op jit(solution)/shard_map/all_to_all | solution.py:100
  42.0 25.3 %all-to-all-start.2 = ((bf16[8,48,2048]{2,1,0:T(8,128)(2,1)}), bf16[8,48,2048]{2,1,0:T(8,128)(2,1)}, u32[]{:S(2)}, u32[]{:S(2)}) async-start(bf16[8,48,2048]{2,1,0:T(8,128)(2,1)} %bitcast.21), calls=%async_computation.3 | async-start | bytes 3145728 | tf_op jit(solution)/shard_map/all_to_all | solution.py:106
  46.5 5.3 %copy-start.6 = (bf16[1,1024,2048]{2,1,0:T(8,128)(2,1)S(1)}, bf16[1,1024,2048]{2,1,0:T(8,128)(2,1)}, u32[]{:S(2)}) copy-start(bf16[1,1024,2048]{2,1,0:T(8,128)(2,1)} %param.20) | copy-start | bytes 12582916
  50.6 1.2 copy-start.10
  289.7 31.4 %all-to-all-start.1 = ((bf16[8,48,2048]{2,1,0:T(8,128)(2,1)}), bf16[8,48,2048]{2,1,0:T(8,128)(2,1)S(1)}, u32[]{:S(2)}, u32[]{:S(2)}) async-start(bf16[8,48,2048]{2,1,0:T(8,128)(2,1)} %bitcast.85), calls=%async_computation.1 | async-start | bytes 3145728 | tf_op jit(solution)/shard_map/all_to_all | solution.py:115
  297.4 73.8 %all-gather.10.cloned.1.call-start = ((), (), s32[]{:S(2)}) async-start(), calls=%async_computation.7 | async-start | bytes 3145728 | tf_op jit(solution)/shard_map/all_gather | solution.py:141
  321.1 4.7 copy-start.5
  321.1 32.5 %all-to-all-start.3 = ((bf16[8,48,2048]{2,1,0:T(8,128)(2,1)}), bf16[8,48,2048]{2,1,0:T(8,128)(2,1)S(1)}, u32[]{:S(2)}, u32[]{:S(2)}) async-start(bf16[8,48,2048]{2,1,0:T(8,128)(2,1)} %bitcast.83), calls=%async_computation.4 | async-start | bytes 3145728 | tf_op jit(solution)/shard_map/all_to_all | solution.py:122
  324.8 64.9 %all-gather.12.cloned.1.call-start = ((), (), s32[]{:S(2)}) async-start(), calls=%async_computation.8 | async-start | bytes 3145728 | tf_op jit(solution)/shard_map/all_gather | solution.py:146
  325.5 88.3 %all-gather.6.cloned.1.call-start = ((), (), s32[]{:S(2)}) async-start(), calls=%async_computation.5 | async-start | bytes 2621440 | tf_op jit(solution)/shard_map/all_gather | solution.py:138
  356.0 3.5 copy-start.1
  359.5 7.8 %copy-start = (bf16[128,2048]{1,0:T(8,128)(2,1)S(1)}, bf16[128,2048]{1,0:T(8,128)(2,1)}, u32[]{:S(2)}) copy-start(bf16[128,2048]{1,0:T(8,128)(2,1)} %param.15) | copy-start | bytes 1572868
  367.2 0.7 copy-start.4
  369.0 1.5 copy-start.2
  369.0 1.7 copy-start.8
  369.0 79.4 %all-gather.8.cloned.1.call-start = ((), (), s32[]{:S(2)}) async-start(), calls=%async_computation.6 | async-start | bytes 3145728 | tf_op jit(solution)/shard_map/all_gather | solution.py:151
  369.6 1.7 copy-start.7
  369.6 113.4 %all-gather.14.cloned.1.call-start = ((), (), s32[]{:S(2)}) async-start(), calls=%async_computation.9 | async-start | bytes 3145728 | tf_op jit(solution)/shard_map/all_gather | solution.py:163
  370.2 148.1 %reduce-scatter.2.cloned.1.call-start = ((), (), s32[]{:S(2)}) async-start(), calls=%async_computation.10 | async-start | bytes 2621440 | tf_op jit(solution)/shard_map/reduce_scatter | solution.py:166
  486.6 0.7 copy-start.9
Sparse Core Ops, SparseCore 0:
  299.8 57.2 all-gather.9
  358.6 31.0 all-gather.11
  391.3 22.5 all-gather.5
  415.3 33.1 all-gather.7
  449.8 33.1 all-gather.13
  486.8 31.4 reduce-scatter.1
where the time goes:
time: 528 us; the launch traced here: 527 us
  blocking collectives  212 us (40%)
  waiting for transfers between devices  203 us (38%)
  matrix products  33.4 us (6%)
  local copies, waits for them, and re-layouts  28.9 us (5%)
  starting transfers between devices  22 us (4%)
  between operations  14.4 us (3%)
  other arithmetic  13.4 us (3%)
    psum x1, blocking collectives, body(): lax.psum((forward_part, backward_part), 'section')  212 us
    all_gather x1, waiting for transfers between devices, body(): lax.all_gather(value_weight, 'expert', axis=1, tiled=True)[0]  31 us
    reduce_scatter x1, waiting for transfers between devices, body(): lax.psum_scatter(partial_out, 'dp', scatter_dimension=1, tiled=True)  30.2 us
    all_gather x1, waiting for transfers between devices, body(): lax.all_gather(out_weight, 'expert', axis=2, tiled=True)[0]  25.8 us
    all_gather x1, waiting for transfers between devices, body(): source = lax.all_gather(memory, 'dp', axis=0, tiled=True)  24.2 us
    all_to_all x1, waiting for transfers between devices, body(): lax.all_to_all(forward_total.astype(jnp.bfloat16).reshape(group_size, cap...  22.9 us
    all_to_all x1, waiting for transfers between devices, body(): lax.all_to_all(backward_total.astype(jnp.bfloat16).reshape(group_size, ca...  21.8 us
    all_gather x1, waiting for transfers between devices, body(): lax.all_gather(key_weight, 'expert', axis=1, tiled=True)[0]  16 us
  transfers between devices with their start and end apart: 10, of which 9 were waited for; matrix products, arithmetic and copies ran while one was open for 9% of the time, Pallas kernels for 0%

commit v1 on v0

v1 whole, which is shorter than its diff:
```python
import jax
import jax.numpy as jnp
from jax import lax
from jax.sharding import PartitionSpec as P

HEAD_DIM = 128
SRC_LEN = 256
TGT_LEN = 128


EPSILON = 1e-05


def normalize(values, gain):
    centre = jnp.mean(values, axis=-1, keepdims=True)
    centred = values - centre
    spread = jnp.mean(centred * centred, axis=-1, keepdims=True)
    return centred * lax.rsqrt(spread + EPSILON) * gain


def contract_last(left, right):
    return lax.dot_general(
        left, right, (((1,), (1,)), ((), ())), preferred_element_type=jnp.float32
    )


def shift(value, axis, step):
    size = lax.axis_size(axis)
    return lax.ppermute(value, axis, [(i, (i + step) % size) for i in range(size)])


def swap(value, axis, mask):
    size = lax.axis_size(axis)
    return lax.ppermute(value, axis, [(i, i ^ mask) for i in range(size)])


def sum_sections(partial):
    count = lax.axis_size("section")
    me = lax.axis_index("section")
    width = partial.shape[1] // count

    def piece(owner):
        return lax.dynamic_slice_in_dim(partial, owner * width, width, 1)

    total = piece(me).astype(jnp.float32)
    for step in range(1, count):
        sent = piece(lax.rem(me + step, count)).astype(jnp.bfloat16)
        total = total + shift(sent, "section", step).astype(jnp.float32)
    return total


def gather_sections(mine):
    count = lax.axis_size("section")
    me = lax.axis_index("section")
    width = mine.shape[1]
    whole = jnp.zeros((mine.shape[0], width * count), mine.dtype)
    whole = lax.dynamic_update_slice_in_dim(whole, mine, me * width, 1)
    for step in range(1, count):
        owner = lax.rem(me - step + count, count)
        whole = lax.dynamic_update_slice_in_dim(
            whole, shift(mine, "section", step), owner * width, 1
        )
    return whole


def gather_rows(mine, axis):
    held = mine
    me = lax.axis_index(axis)
    mask = lax.axis_size(axis) // 2
    blocks = [mine]
    while mask >= 1:
        blocks = blocks + [swap(block, axis, mask) for block in blocks]
        mask //= 2
    codes = [0]
    mask = lax.axis_size(axis) // 2
    while mask >= 1:
        codes = codes + [code ^ mask for code in codes]
        mask //= 2
    ordered = []
    for place in range(len(blocks)):
        chosen = blocks[0]
        for code, block in zip(codes[1:], blocks[1:]):
            chosen = jnp.where((me ^ code) == place, block, chosen)
        ordered.append(chosen)
    return jnp.concatenate(ordered, axis=0)


def gather_weight(weight, dimension):
    if lax.axis_size("expert") != 2:
        return lax.all_gather(weight, "expert", axis=dimension, tiled=True)
    other = swap(weight, "expert", 1)
    first = lax.axis_index("expert") == 0
    return jnp.concatenate(
        [jnp.where(first, weight, other), jnp.where(first, other, weight)], axis=dimension
    )


def sum_heads(partial):
    me = lax.axis_index("dp")
    count = lax.axis_size("dp")
    rows, columns = partial.shape
    total = partial.reshape(rows, count, columns // count)
    mask = 1
    while mask < count:
        paired = total.reshape(rows, -1, 2, columns // count)
        bit = (me // mask) % 2
        sent = lax.dynamic_index_in_dim(paired, 1 - bit, 2, False).astype(jnp.bfloat16)
        kept = lax.dynamic_index_in_dim(paired, bit, 2, False)
        total = kept + swap(sent, "dp", mask).astype(jnp.float32)
        mask *= 2
    return total.reshape(rows, columns // count)


def slot_matrix(positions, slots):
    places = lax.broadcasted_iota(jnp.int32, (positions.shape[0], slots), 1)
    return (positions[:, None] == places).astype(jnp.bfloat16)


def attend(query, keys, values, key_mask):
    sequences = key_mask.shape[0]
    head_count = query.shape[1] // HEAD_DIM
    query_split = query.reshape(sequences, -1, head_count, HEAD_DIM)
    keys_split = keys.reshape(sequences, -1, head_count, HEAD_DIM)
    values_split = values.reshape(sequences, -1, head_count, HEAD_DIM)
    scores = jnp.einsum(
        "bqhd,bkhd->bhqk", query_split, keys_split, preferred_element_type=jnp.float32
    ) * HEAD_DIM ** (-0.5)
    scores = jnp.where(key_mask[:, None, None, :], scores, -1e30)
    highest = jnp.max(scores, axis=-1, keepdims=True)
    weights = jnp.exp(scores - highest)
    probs = (weights / jnp.sum(weights, axis=-1, keepdims=True)).astype(jnp.bfloat16)
    context = jnp.einsum("bhqk,bkhd->bqhd", probs, values_split, preferred_element_type=jnp.float32)
    return context.astype(jnp.bfloat16).reshape(-1, head_count * HEAD_DIM)


def exchange(values, group_size, capacity):
    sent = values.reshape(group_size, capacity, values.shape[1])
    arrived = lax.all_to_all(sent, ("expert", "dp"), split_axis=0, concat_axis=0, tiled=True)
    return arrived.reshape(values.shape)


def body(
    tokens,
    expert_ids,
    gate_weights,
    out_grad,
    inner_weight,
    outer_weight,
    final_gain,
    dec_states,
    src_lengths,
    tgt_lengths,
    norm_gain,
    query_weight,
    key_weight,
    value_weight,
    out_weight,
):
    token_count, feature_count = tokens.shape
    group_size = lax.axis_size(("expert", "dp"))
    capacity = 3 * token_count // group_size
    slots = group_size * capacity

    named = expert_ids[:, :, None] == jnp.arange(group_size, dtype=jnp.int32)[None, None, :]
    either = (named[:, 0] | named[:, 1]).astype(jnp.bfloat16)
    row = lax.broadcasted_iota(jnp.int32, (token_count, token_count), 0)
    column = lax.broadcasted_iota(jnp.int32, (token_count, token_count), 1)
    earlier = jnp.dot(
        (column < row).astype(jnp.bfloat16), either, preferred_element_type=jnp.float32
    ).astype(jnp.int32)
    rank = jnp.sum(jnp.where(named, earlier[:, None, :], 0), axis=2)
    position = expert_ids * capacity + rank
    pick_first = slot_matrix(position[:, 0], slots)
    pick_second = slot_matrix(position[:, 1], slots)
    fill = (pick_first + pick_second).T

    def place(values):
        return jnp.dot(fill, values, preferred_element_type=jnp.float32).astype(jnp.bfloat16)

    def combine(arrived):
        first = jnp.dot(pick_first, arrived, preferred_element_type=jnp.float32)
        second = jnp.dot(pick_second, arrived, preferred_element_type=jnp.float32)
        return gate_weights[:, :1] * first + gate_weights[:, 1:] * second

    weight_in = inner_weight[0]
    weight_out = outer_weight[0]
    arrived_rows = exchange(place(tokens), group_size, capacity)
    pre_act = jnp.dot(arrived_rows, weight_in, preferred_element_type=jnp.float32)
    hidden = jax.nn.gelu(pre_act).astype(jnp.bfloat16)
    forward_part = jnp.dot(hidden, weight_out, preferred_element_type=jnp.float32)
    arrived_grads = exchange(place(out_grad), group_size, capacity)
    outputs_home = exchange(forward_part.astype(jnp.bfloat16), group_size, capacity)
    mixed_slice = sum_sections(combine(outputs_home)).astype(jnp.bfloat16)
    mixed = gather_sections(mixed_slice).astype(jnp.float32)
    memory = normalize(tokens.astype(jnp.float32) + mixed, final_gain).astype(jnp.bfloat16)

    back = contract_last(arrived_grads, weight_out)
    slope = jax.vjp(jax.nn.gelu, pre_act)[1](back)[0].astype(jnp.bfloat16)
    backward_part = contract_last(slope, weight_in)
    backward_slice = sum_sections(backward_part).astype(jnp.bfloat16)
    grads_home = exchange(backward_slice, group_size, capacity)
    token_grad = combine(grads_home).astype(jnp.bfloat16)

    states = dec_states[0]
    normed = normalize(states.astype(jnp.float32), norm_gain[0]).astype(jnp.bfloat16)
    full_query = gather_weight(query_weight[0], 0)
    full_key = gather_weight(key_weight[0], 0)
    full_value = gather_weight(value_weight[0], 0)
    full_out = gather_weight(out_weight[0], 1)
    query_sum = jnp.dot(normed, full_query, preferred_element_type=jnp.float32)
    source = gather_rows(memory, "dp")
    key_sum = jnp.dot(source, full_key, preferred_element_type=jnp.float32)
    value_sum = jnp.dot(source, full_value, preferred_element_type=jnp.float32)
    key_mask = jnp.arange(SRC_LEN, dtype=jnp.int32)[None, :] < src_lengths[:, None]
    context = attend(
        query_sum.astype(jnp.bfloat16),
        key_sum.astype(jnp.bfloat16),
        value_sum.astype(jnp.bfloat16),
        key_mask,
    )
    attended = sum_heads(jnp.dot(context, full_out, preferred_element_type=jnp.float32))
    my_columns = attended.shape[1]
    residual = lax.dynamic_slice_in_dim(
        states, lax.axis_index("dp") * my_columns, my_columns, 1
    ).astype(jnp.float32)
    row_mask = (jnp.arange(TGT_LEN, dtype=jnp.int32)[None, :] < tgt_lengths[:, None]).reshape(-1, 1)
    dec_out = (residual + jnp.where(row_mask, attended, 0.0)).astype(jnp.bfloat16)
    return (dec_out[None], token_grad)


def solution(mesh):
    in_specs = (
        P(("expert", "dp"), None),
        P(("expert", "dp"), None),
        P(("expert", "dp"), None),
        P(("expert", "dp"), None),
        P(("expert", "dp"), None, "section"),
        P(("expert", "dp"), "section", None),
        P(),
        P("section", "expert", None),
        P("expert"),
        P("expert"),
        P("section", None),
        P("section", "expert", "dp"),
        P("section", "expert", "dp"),
        P("section", "expert", "dp"),
        P("section", "dp", "expert"),
    )
    out_specs = (P("section", "expert", "dp"), P(("expert", "dp"), "section"))
    return jax.shard_map(body, mesh=mesh, in_specs=in_specs, out_specs=out_specs, check_vma=False)
```

time: 528 us -> 257 us (0.49)
  the two profiles are of different devices: /device:TPU:0 before, /device:TPU:8 now
where the time goes in v1:
time: 257 us
  waiting for transfers between devices  149 us (58%)
  matrix products  38 us (15%)
  starting transfers between devices  35.4 us (14%)
  other arithmetic  21.5 us (8%)
  local copies, waits for them, and re-layouts  11.9 us (5%)
    ppermute x9, waiting for transfers between devices, swap(): return lax.ppermute(value, axis, [(i, i ^ mask) for i in range(size)])  68.5 us
    all_to_all x4, waiting for transfers between devices, exchange(): lax.all_to_all(sent, ('expert', 'dp'), split_axis=0, concat_axis=0, tiled...  49 us
    ppermute x9, waiting for transfers between devices, shift(): lax.ppermute(value, axis, [(i, (i + step) % size) for i in range(size)])  31 us
    all_to_all x4, starting transfers between devices, exchange(): lax.all_to_all(sent, ('expert', 'dp'), split_axis=0, concat_axis=0, tiled...  15.8 us
    ppermute x9, starting transfers between devices, shift(): lax.ppermute(value, axis, [(i, (i + step) % size) for i in range(size)])  11.9 us
    dot_general x1, matrix products, contract_last(): lax.dot_general(left, right, (((1,), (1,)), ((), ())), preferred_element_...  10.2 us
    select_n x3, other arithmetic, gather_weight(): jnp.where(first, weight, other)  8.38 us
    ppermute x9, starting transfers between devices, swap(): return lax.ppermute(value, axis, [(i, i ^ mask) for i in range(size)])  7.78 us
  transfers between devices with their start and end apart: 22, of which 14 were waited for; matrix products, arithmetic and copies ran while one was open for 24% of the time, Pallas kernels for 0%

profile of v1, /device:TPU:8, one launch (start us, length us, event | category | flops | bytes accessed | tf_op | source)
XLA Modules:
  0.0 256.5 jit_solution(12022953151131705527)
XLA Ops:
  0.6 0.7 iota_compare_fusion.8
  1.5 0.7 select_reduce_fusion
  2.2 0.7 multiply_add_fusion
  2.9 2.9 %convolution_convert_fusion.1 = bf16[384,2048]{1,0:T(8,128)(2,1)} fusion(bf16[128,2048]{1,0:T(8,128)(2,1)} %param.15, s32[128]{0:T(128)S(1)} %get-tuple-element.25, s32[128]{0:T(128)S(1)} %get-tuple-element.24), kind=kOutput, calls=%fused_computation.11 | convolution fusion | flops 202506240 | bytes 2098176 | tf_op jit(solution)/shard_map/dot_general | solution.py:178
  5.8 3.9 %all-to-all-start = ((bf16[8,48,2048]{2,1,0:T(8,128)(2,1)}), bf16[8,48,2048]{2,1,0:T(8,128)(2,1)S(1)}, u32[]{:S(2)}, u32[]{:S(2)}) async-start(bf16[8,48,2048]{2,1,0:T(8,128)(2,1)} %bitcast.5), calls=%async_computation | async-start | bytes 3145728 | tf_op jit(solution)/shard_map/all_to_all | solution.py:138
  9.7 2.0 collective-permute-start.11
  11.8 2.0 collective-permute-start.10
  14.0 16.8 %all-to-all-done = bf16[8,48,2048]{2,1,0:T(8,128)(2,1)S(1)} async-done(((bf16[8,48,2048]{2,1,0:T(8,128)(2,1)}), bf16[8,48,2048]{2,1,0:T(8,128)(2,1)S(1)}, u32[]{:S(2)}, u32[]{:S(2)}) %all-to-all-start) | async-done | bytes 1572896 | tf_op jit(solution)/shard_map/all_to_all | solution.py:138
  30.8 4.1 %fusion.7 = f32[384,1024]{1,0:T(8,128)S(1)} fusion(bf16[384,2048]{1,0:T(8,128)(2,1)S(1)} %bitcast.99, bf16[1,2048,1024]{2,1,0:T(8,128)(2,1)} %param.19), kind=kOutput, calls=%fused_computation.7 | convolution fusion | flops 1610612736 | bytes 7340032 | tf_op jit(solution)/shard_map/dot_general | solution.py:188
  35.0 3.1 %fusion.9 = bf16[384,2048]{1,0:T(8,128)(2,1)} fusion(bf16[1,1024,2048]{2,1,0:T(8,128)(2,1)S(1)} %copy-done.20, f32[384,1024]{1,0:T(8,128)S(1)} %fusion.7), kind=kOutput, calls=%fused_computation.9 | convolution fusion | flops 1614938112 | bytes 7340032 | tf_op jit(solution)/shard_map/dot_general | solution.py:190
  38.1 3.7 %all-to-all-start.1 = ((bf16[8,48,2048]{2,1,0:T(8,128)(2,1)}), bf16[8,48,2048]{2,1,0:T(8,128)(2,1)S(1)}, u32[]{:S(2)}, u32[]{:S(2)}) async-start(bf16[8,48,2048]{2,1,0:T(8,128)(2,1)} %bitcast.100), calls=%async_computation.1 | async-start | bytes 3145728 | tf_op jit(solution)/shard_map/all_to_all | solution.py:138
  41.8 0.4 fusion.16
  42.4 1.9 convolution_convert_fusion
  44.3 61.9 %collective-permute-done.10 = bf16[1024,512]{1,0:T(8,128)(2,1)} collective-permute-done((bf16[1024,512]{1,0:T(8,128)(2,1)}, bf16[1024,512]{1,0:T(8,128)(2,1)}, u32[]{:S(2)}, u32[]{:S(2)}) %collective-permute-start.10) | collective-permute-done | bytes 1048608 | tf_op jit(solution)/shard_map/ppermute | solution.py:34
  106.2 2.7 %broadcast_select_fusion.5 = (bf16[1024,512]{1,0:T(8,128)(2,1)}, bf16[1024,512]{1,0:T(8,128)(2,1)}) fusion(bf16[1024,512]{1,0:T(8,128)(2,1)} %collective-permute-done.10, pred[]{:T(512)S(6)} %eq.99, bf16[1,1024,512]{2,1,0:T(8,128)(2,1)S(1)} %copy-done.6), kind=kLoop, calls=%fused_computation.75 | loop fusion | flops 1048576 | bytes 4194305 | tf_op jit(solution)/shard_map/jit(_where)/select_n | solution.py:94
  108.9 27.6 %all-to-all-done.1 = bf16[8,48,2048]{2,1,0:T(8,128)(2,1)S(1)} async-done(((bf16[8,48,2048]{2,1,0:T(8,128)(2,1)}), bf16[8,48,2048]{2,1,0:T(8,128)(2,1)S(1)}, u32[]{:S(2)}, u32[]{:S(2)}) %all-to-all-start.1) | async-done | bytes 1572896 | tf_op jit(solution)/shard_map/all_to_all | solution.py:138
  136.5 4.3 %all-to-all-start.2 = ((bf16[8,48,2048]{2,1,0:T(8,128)(2,1)}), bf16[8,48,2048]{2,1,0:T(8,128)(2,1)}, u32[]{:S(2)}, u32[]{:S(2)}) async-start(bf16[8,48,2048]{2,1,0:T(8,128)(2,1)} %bitcast.96), calls=%async_computation.2 | async-start | bytes 3145728 | tf_op jit(solution)/shard_map/all_to_all | solution.py:138
  140.8 0.5 convolution_multiply_fusion.1
  141.3 0.5 fusion.12
  141.9 1.6 collective-permute-start
  143.5 1.2 collective-permute-start.1
  144.8 1.8 collective-permute-start.2
  146.6 1.4 broadcast_select_fusion.1
  148.0 4.8 %collective-permute-done = bf16[128,512]{1,0:T(8,128)(2,1)S(1)} collective-permute-done((bf16[128,512]{1,0:T(8,128)(2,1)S(1)}, bf16[128,512]{1,0:T(8,128)(2,1)S(1)}, u32[]{:S(2)}, u32[]{:S(2)}) %collective-permute-start) | collective-permute-done | bytes 131104 | tf_op jit(solution)/shard_map/ppermute | solution.py:29
  152.8 2.4 collective-permute-done.1
  155.3 1.7 collective-permute-done.2
  157.2 1.7 collective-permute-start.4
  158.9 1.5 fusion.49
  160.4 1.9 collective-permute-start.5
  162.3 1.2 collective-permute-done.3
  163.5 5.4 %collective-permute-done.4 = bf16[128,512]{1,0:T(8,128)(2,1)S(1)} collective-permute-done((bf16[128,512]{1,0:T(8,128)(2,1)S(1)}, bf16[128,512]{1,0:T(8,128)(2,1)S(1)}, u32[]{:S(2)}, u32[]{:S(2)}) %collective-permute-start.4) | collective-permute-done | bytes 131104 | tf_op jit(solution)/shard_map/ppermute | solution.py:29
  169.0 1.5 collective-permute-done.5
  171.4 1.6 collective-permute-start.6
  173.0 1.5 maximum_bitcast_fusion
  174.6 2.9 %copy.27 = bf16[2048,512]{1,0:T(8,128)(2,1)S(1)} copy(bf16[2048,512]{0,1:T(8,128)(2,1)} %maximum_bitcast_fusion) | data formatting | bytes 4194304 | tf_op jit(solution)/shard_map/dot_general | solution.py:221
  177.5 4.3 %broadcast_select_fusion.3 = (bf16[1024,512]{1,0:T(8,128)(2,1)}, bf16[1024,512]{1,0:T(8,128)(2,1)}, bf16[1024,512]{1,0:T(8,128)(2,1)}, bf16[1024,512]{1,0:T(8,128)(2,1)}) fusion(bf16[1024,512]{1,0:T(8,128)(2,1)} %collective-permute-done.11, pred[]{:T(512)S(6)} %eq.99, bf16[1,1024,512]{2,1,0:T(8,128)(2,1)} %param.27, ...), kind=kLoop, calls=%fused_computation.73 | loop fusion | flops 2097152 | bytes 8388609 | tf_op jit(solution)/shard_map/jit(_where)/select_n | solution.py:94
  181.8 3.6 %collective-permute-done.6 = bf16[128,2048]{1,0:T(8,128)(2,1)} collective-permute-done((bf16[128,2048]{1,0:T(8,128)(2,1)S(1)}, bf16[128,2048]{1,0:T(8,128)(2,1)}, u32[]{:S(2)}, u32[]{:S(2)}) %collective-permute-start.6) | collective-permute-done | bytes 524320 | tf_op jit(solution)/shard_map/ppermute | solution.py:34
  185.4 10.2 %fusion.5 = f32[384,2048]{1,0:T(8,128)} fusion(bf16[1,2048,1024]{2,1,0:T(8,128)(2,1)} %param.19, f32[384,1024]{1,0:T(8,128)} %copy-done.24, bf16[384,2048]{1,0:T(8,128)(2,1)} %bitcast.26, bf16[1,1024,2048]{2,1,0:T(8,128)(2,1)} %param.20), kind=kOutput, calls=%fused_computation.5 | convolution fusion | flops 3229089792 | bytes 14680064 | tf_op jit(solution)/shard_map/dot_general | solution.py:22
  195.6 2.7 %dynamic-slice_convert_fusion.3 = (bf16[384,512]{1,0:T(8,128)(2,1)}, bf16[384,512]{1,0:T(8,128)(2,1)}, bf16[384,512]{1,0:T(8,128)(2,1)}) fusion(f32[384,2048]{1,0:T(8,128)} %fusion.5, s32[]{:T(128)S(6)} %select_n.190, s32[]{:T(128)S(6)} %select_n.192, s32[]{:T(128)S(6)} %select_n.191), kind=kLoop, calls=%fused_computation.83 | loop fusion | bytes 2359308 | tf_op jit(solution)/shard_map/convert_element_type | solution.py:47
  198.3 1.5 collective-permute-start.16
  199.8 2.0 collective-permute-start.17
  201.8 1.6 select_select_fusion.3
  203.5 0.8 copy-done.12
  204.8 2.0 fusion.43
  206.8 1.2 reshape.152
  208.0 1.3 fusion.42
  209.3 0.6 fusion.112
  209.9 3.4 %fusion.46 = bf16[512,512]{1,0:T(8,128)(2,1)S(1)} fusion(bf16[1024,512]{1,0:T(8,128)(2,1)} %get-tuple-element.26, bf16[1024,512]{1,0:T(8,128)(2,1)} %get-tuple-element.27, bf16[128,2048]{1,0:T(8,128)(2,1)} %copy-done.13, bf16[128,2048]{1,0:T(8,128)(2,1)} %copy-done.14, bf16[128,2048]{1,0:T(8,128)(2,1)} %copy-done.15, bf16[128,2048]{1,0:T(8,128)(2,1)} %copy-done.12), kind=kOutput, calls=%fused_computation.52 | convolution fusion | flops 1086586880 | bytes 4718592 | tf_op jit(solution)/shard_map/dot_general | solution.py:213
  213.3 0.9 reshape.150
  214.3 3.8 %fusion.52 = bf16[2,128,4,128]{1,3,2,0:T(8,128)(2,1)S(1)} fusion(bf16[2,256,4,128]{3,2,1,0:T(4,128)(2,1)} %reshape.150, f32[2,4,128]{2,1,0:T(4,128)S(1)} %fusion.112, f32[2,4,128,256]{3,2,1,0:T(8,128)} %fusion.42), kind=kOutput, calls=%fused_computation.55 | convolution fusion | flops 68027648 | bytes 1839104 | tf_op jit(solution)/shard_map/bhqk,bkhd->bqhd/dot_general | solution.py:132
  218.4 0.7 fusion.73
  219.1 1.3 copy-done.2
  220.7 0.6 compare_bitcast_fusion
  221.3 12.0 %collective-permute-done.16 = bf16[384,512]{1,0:T(8,128)(2,1)} collective-permute-done((bf16[384,512]{1,0:T(8,128)(2,1)}, bf16[384,512]{1,0:T(8,128)(2,1)}, u32[]{:S(2)}, u32[]{:S(2)}) %collective-permute-start.16) | collective-permute-done | bytes 393248 | tf_op jit(solution)/shard_map/ppermute | solution.py:29
  233.2 2.0 collective-permute-done.17
  235.2 2.5 add_convert_fusion
  237.7 3.9 %all-to-all-start.3 = ((bf16[8,48,512]{2,1,0:T(8,128)(2,1)}), bf16[8,48,512]{2,1,0:T(8,128)(2,1)S(1)}, u32[]{:S(2)}, u32[]{:S(2)}) async-start(bf16[8,48,512]{2,1,0:T(8,128)(2,1)} %bitcast.27), calls=%async_computation.3 | async-start | bytes 786432 | tf_op jit(solution)/shard_map/all_to_all | solution.py:138
  241.5 1.2 bitcast_add_fusion
  242.8 0.9 copy-done.5
  243.8 2.0 collective-permute-start.14
  245.8 4.6 %all-to-all-done.3 = bf16[8,48,512]{2,1,0:T(8,128)(2,1)S(1)} async-done(((bf16[8,48,512]{2,1,0:T(8,128)(2,1)}), bf16[8,48,512]{2,1,0:T(8,128)(2,1)S(1)}, u32[]{:S(2)}, u32[]{:S(2)}) %all-to-all-start.3) | async-done | bytes 393248 | tf_op jit(solution)/shard_map/all_to_all | solution.py:138
  250.6 0.9 fusion.54
  251.5 3.0 %collective-permute-done.14 = bf16[256,1,512]{2,0,1:T(8,128)(2,1)S(1)} collective-permute-done((bf16[256,1,512]{2,0,1:T(8,128)(2,1)S(1)}, bf16[256,1,512]{2,0,1:T(8,128)(2,1)S(1)}, u32[]{:S(2)}, u32[]{:S(2)}) %collective-permute-start.14) | collective-permute-done | bytes 262176 | tf_op jit(solution)/shard_map/ppermute | solution.py:34
  254.6 1.9 fusion.69
  (86 shorter events, 3.1 us)
Async XLA Ops:
  0.6 41.7 %copy-start = (bf16[128,2048]{1,0:T(8,128)(2,1)S(1)}, bf16[128,2048]{1,0:T(8,128)(2,1)}, u32[]{:S(2)}) copy-start(bf16[128,2048]{1,0:T(8,128)(2,1)} %param.18) | copy-start | bytes 1572868
  5.8 8.0 %copy-start.4 = (bf16[1,256,2048]{2,1,0:T(8,128)(2,1)S(1)}, bf16[1,256,2048]{2,1,0:T(8,128)(2,1)}, u32[]{:S(2)}) copy-start(bf16[1,256,2048]{2,1,0:T(8,128)(2,1)} %param.22) | copy-start | bytes 3145732
  5.8 25.0 %all-to-all-start = ((bf16[8,48,2048]{2,1,0:T(8,128)(2,1)}), bf16[8,48,2048]{2,1,0:T(8,128)(2,1)S(1)}, u32[]{:S(2)}, u32[]{:S(2)}) async-start(bf16[8,48,2048]{2,1,0:T(8,128)(2,1)} %bitcast.5), calls=%async_computation | async-start | bytes 3145728 | tf_op jit(solution)/shard_map/all_to_all | solution.py:138
  9.7 167.8 %collective-permute-start.11 = (bf16[1024,512]{1,0:T(8,128)(2,1)}, bf16[1024,512]{1,0:T(8,128)(2,1)}, u32[]{:S(2)}, u32[]{:S(2)}) collective-permute-start(bf16[1024,512]{1,0:T(8,128)(2,1)} %bitcast.103), channel_id=1, source_target_pairs={{0,4},{4,0},{1,5},{5,1},{2,6},{6,2},{3,7},{7,3},{8,12},{12,8},{9,1... | collective-permute-start | bytes 3145736 | tf_op jit(solution)/shard_map/ppermute | solution.py:34
  11.7 165.7 %collective-permute-start.9 = (bf16[1024,512]{1,0:T(8,128)(2,1)}, bf16[1024,512]{1,0:T(8,128)(2,1)}, u32[]{:S(2)}, u32[]{:S(2)}) collective-permute-start(bf16[1024,512]{1,0:T(8,128)(2,1)} %bitcast.104), channel_id=1, source_target_pairs={{0,4},{4,0},{1,5},{5,1},{2,6},{6,2},{3,7},{7,3},{8,12},{12,8},{9,1... | collective-permute-start | bytes 3145736 | tf_op jit(solution)/shard_map/ppermute | solution.py:34
  11.8 94.4 %collective-permute-start.10 = (bf16[1024,512]{1,0:T(8,128)(2,1)}, bf16[1024,512]{1,0:T(8,128)(2,1)}, u32[]{:S(2)}, u32[]{:S(2)}) collective-permute-start(bf16[1024,512]{1,0:T(8,128)(2,1)} %bitcast.101), channel_id=1, source_target_pairs={{0,4},{4,0},{1,5},{5,1},{2,6},{6,2},{3,7},{7,3},{8,12},{12,8},{9,1... | collective-permute-start | bytes 3145736 | tf_op jit(solution)/shard_map/ppermute | solution.py:34
  13.7 131.1 %collective-permute-start.12 = (bf16[512,1024]{1,0:T(8,128)(2,1)}, bf16[512,1024]{1,0:T(8,128)(2,1)}, u32[]{:S(2)}, u32[]{:S(2)}) collective-permute-start(bf16[512,1024]{1,0:T(8,128)(2,1)} %bitcast.102), channel_id=1, source_target_pairs={{0,4},{4,0},{1,5},{5,1},{2,6},{6,2},{3,7},{7,3},{8,12},{12,8},{9,1... | collective-permute-start | bytes 3145736 | tf_op jit(solution)/shard_map/ppermute | solution.py:34
  30.8 4.1 %copy-start.20 = (bf16[1,1024,2048]{2,1,0:T(8,128)(2,1)S(1)}, bf16[1,1024,2048]{2,1,0:T(8,128)(2,1)}, u32[]{:S(2)}) copy-start(bf16[1,1024,2048]{2,1,0:T(8,128)(2,1)} %param.20) | copy-start | bytes 12582916
  35.0 3.2 %copy-start.24 = (f32[384,1024]{1,0:T(8,128)}, f32[384,1024]{1,0:T(8,128)S(1)}, u32[]{:S(2)}) copy-start(f32[384,1024]{1,0:T(8,128)S(1)} %fusion.7) | copy-start | bytes 4718596
  38.1 4.2 %copy-start.22 = (s32[2]{0:T(128)S(1)}, s32[2]{0:T(128)}, u32[]{:S(2)}) copy-start(s32[2]{0:T(128)} %param.23) | copy-start | bytes 28
  38.1 4.2 %copy-start.18 = (f32[128,2]{0,1:T(2,128)S(1)}, f32[128,2]{0,1:T(2,128)}, u32[]{:S(2)}) copy-start(f32[128,2]{0,1:T(2,128)} %param.17) | copy-start | bytes 3076
  38.1 98.4 %all-to-all-start.1 = ((bf16[8,48,2048]{2,1,0:T(8,128)(2,1)}), bf16[8,48,2048]{2,1,0:T(8,128)(2,1)S(1)}, u32[]{:S(2)}, u32[]{:S(2)}) async-start(bf16[8,48,2048]{2,1,0:T(8,128)(2,1)} %bitcast.100), calls=%async_computation.1 | async-start | bytes 3145728 | tf_op jit(solution)/shard_map/all_to_all | solution.py:138
  41.8 64.3 %copy-start.6 = (bf16[1,1024,512]{2,1,0:T(8,128)(2,1)S(1)}, bf16[1,1024,512]{2,1,0:T(8,128)(2,1)}, u32[]{:S(2)}) copy-start(bf16[1,1024,512]{2,1,0:T(8,128)(2,1)} %param.26) | copy-start | bytes 3145732
  136.5 48.9 %all-to-all-start.2 = ((bf16[8,48,2048]{2,1,0:T(8,128)(2,1)}), bf16[8,48,2048]{2,1,0:T(8,128)(2,1)}, u32[]{:S(2)}, u32[]{:S(2)}) async-start(bf16[8,48,2048]{2,1,0:T(8,128)(2,1)} %bitcast.96), calls=%async_computation.2 | async-start | bytes 3145728 | tf_op jit(solution)/shard_map/all_to_all | solution.py:138
  141.3 5.3 %copy-start.7 = (bf16[1,512,1024]{2,1,0:T(8,128)(2,1)S(1)}, bf16[1,512,1024]{2,1,0:T(8,128)(2,1)}, u32[]{:S(2)}) copy-start(bf16[1,512,1024]{2,1,0:T(8,128)(2,1)} %param.29) | copy-start | bytes 3145732
  141.9 10.9 %collective-permute-start = (bf16[128,512]{1,0:T(8,128)(2,1)S(1)}, bf16[128,512]{1,0:T(8,128)(2,1)S(1)}, u32[]{:S(2)}, u32[]{:S(2)}) collective-permute-start(bf16[128,512]{1,0:T(8,128)(2,1)S(1)} %get-tuple-element.19), channel_id=1, source_target_pairs={{0,8},{8,16},{16,24},{24,0},{1,9},{9,17},{17,25},{25,1},{2,10},{10... | collective-permute-start | bytes 393224 | tf_op jit(solution)/shard_map/ppermute | solution.py:29
  143.5 11.7 %collective-permute-start.1 = (bf16[128,512]{1,0:T(8,128)(2,1)S(1)}, bf16[128,512]{1,0:T(8,128)(2,1)S(1)}, u32[]{:S(2)}, u32[]{:S(2)}) collective-permute-start(bf16[128,512]{1,0:T(8,128)(2,1)S(1)} %get-tuple-element.21), channel_id=1, source_target_pairs={{0,16},{8,24},{16,0},{24,8},{1,17},{9,25},{17,1},{25,9},{2,18},{10... | collective-permute-start | bytes 393224 | tf_op jit(solution)/shard_map/ppermute | solution.py:29
  144.8 14.1 %copy-start.8 = (bf16[1024,512]{1,0:T(8,128)(2,1)S(1)}, bf16[1024,512]{1,0:T(8,128)(2,1)}, u32[]{:S(2)}) copy-start(bf16[1024,512]{1,0:T(8,128)(2,1)} %get-tuple-element.7) | copy-start | bytes 3145732
  144.8 14.1 %copy-start.9 = (bf16[1024,512]{1,0:T(8,128)(2,1)S(1)}, bf16[1024,512]{1,0:T(8,128)(2,1)}, u32[]{:S(2)}) copy-start(bf16[1024,512]{1,0:T(8,128)(2,1)} %get-tuple-element.8) | copy-start | bytes 3145732
  144.8 14.1 %copy-start.21 = (f32[1,2048]{1,0:T(1,128)S(1)}, f32[1,2048]{1,0:T(1,128)}, u32[]{:S(2)}) copy-start(f32[1,2048]{1,0:T(1,128)} %param.25) | copy-start | bytes 24580
  144.8 12.2 %collective-permute-start.2 = (bf16[128,512]{1,0:T(8,128)(2,1)S(1)}, bf16[128,512]{1,0:T(8,128)(2,1)S(1)}, u32[]{:S(2)}, u32[]{:S(2)}) collective-permute-start(bf16[128,512]{1,0:T(8,128)(2,1)S(1)} %get-tuple-element.20), channel_id=1, source_target_pairs={{0,24},{8,0},{16,8},{24,16},{1,25},{9,1},{17,9},{25,17},{2,26},{10... | collective-permute-start | bytes 393224 | tf_op jit(solution)/shard_map/ppermute | solution.py:29
  157.1 6.4 %collective-permute-start.3 = (bf16[128,512]{1,0:T(8,128)(2,1)S(1)}, bf16[128,512]{1,0:T(8,128)(2,1)S(1)}, u32[]{:S(2)}, u32[]{:S(2)}) collective-permute-start(bf16[128,512]{1,0:T(8,128)(2,1)S(1)} %get-tuple-element.3), channel_id=1, source_target_pairs={{0,8},{8,16},{16,24},{24,0},{1,9},{9,17},{17,25},{25,1},{2,10},{10... | collective-permute-start | bytes 393224 | tf_op jit(solution)/shard_map/ppermute | solution.py:29
  157.2 11.8 %collective-permute-start.4 = (bf16[128,512]{1,0:T(8,128)(2,1)S(1)}, bf16[128,512]{1,0:T(8,128)(2,1)S(1)}, u32[]{:S(2)}, u32[]{:S(2)}) collective-permute-start(bf16[128,512]{1,0:T(8,128)(2,1)S(1)} %get-tuple-element.3), channel_id=1, source_target_pairs={{0,16},{8,24},{16,0},{24,8},{1,17},{9,25},{17,1},{25,9},{2,18},{10... | collective-permute-start | bytes 393224 | tf_op jit(solution)/shard_map/ppermute | solution.py:29
  158.9 11.6 %copy-start.1 = (bf16[128,2048]{1,0:T(8,128)(2,1)S(1)}, bf16[128,2048]{1,0:T(8,128)(2,1)}, u32[]{:S(2)}) copy-start(bf16[128,2048]{1,0:T(8,128)(2,1)} %param.15) | copy-start | bytes 1572868
  160.4 10.7 %copy-start.17 = (f32[2048]{0:T(1024)S(1)}, f32[2048]{0:T(1024)}, u32[]{:S(2)}) copy-start(f32[2048]{0:T(1024)} %param.21) | copy-start | bytes 24580
  160.4 10.1 %collective-permute-start.5 = (bf16[128,512]{1,0:T(8,128)(2,1)S(1)}, bf16[128,512]{1,0:T(8,128)(2,1)S(1)}, u32[]{:S(2)}, u32[]{:S(2)}) collective-permute-start(bf16[128,512]{1,0:T(8,128)(2,1)S(1)} %get-tuple-element.3), channel_id=1, source_target_pairs={{0,24},{8,0},{16,8},{24,16},{1,25},{9,1},{17,9},{25,17},{2,26},{10... | collective-permute-start | bytes 393224 | tf_op jit(solution)/shard_map/ppermute | solution.py:29
  171.4 14.0 %collective-permute-start.6 = (bf16[128,2048]{1,0:T(8,128)(2,1)S(1)}, bf16[128,2048]{1,0:T(8,128)(2,1)}, u32[]{:S(2)}, u32[]{:S(2)}) collective-permute-start(bf16[128,2048]{1,0:T(8,128)(2,1)S(1)} %multiply_convert_fusion.1), channel_id=1, source_target_pairs={{0,2},{1,3},{2,0},{3,1},{4,6},{5,7},{6,4},{7,5},{8,10},{9,11},{10,... | collective-permute-start | bytes 1572872 | tf_op jit(solution)/shard_map/ppermute | solution.py:34
  173.0 1.5 copy-start.16
  181.8 20.0 %collective-permute-start.8 = (bf16[128,2048]{1,0:T(8,128)(2,1)S(1)}, bf16[128,2048]{1,0:T(8,128)(2,1)}, u32[]{:S(2)}, u32[]{:S(2)}) collective-permute-start(bf16[128,2048]{1,0:T(8,128)(2,1)S(1)} %multiply_convert_fusion.1), channel_id=1, source_target_pairs={{0,1},{1,0},{2,3},{3,2},{4,5},{5,4},{6,7},{7,6},{8,9},{9,8},{10,11... | collective-permute-start | bytes 1572872 | tf_op jit(solution)/shard_map/ppermute | solution.py:34
  185.4 16.4 %collective-permute-start.7 = (bf16[128,2048]{1,0:T(8,128)(2,1)}, bf16[128,2048]{1,0:T(8,128)(2,1)}, u32[]{:S(2)}, u32[]{:S(2)}) collective-permute-start(bf16[128,2048]{1,0:T(8,128)(2,1)} %collective-permute-done.6), channel_id=1, source_target_pairs={{0,1},{1,0},{2,3},{3,2},{4,5},{5,4},{6,7},{7,6},{8,9},{9,8},{10,11... | collective-permute-start | bytes 1572872 | tf_op jit(solution)/shard_map/ppermute | solution.py:34
  198.3 23.0 %collective-permute-start.15 = (bf16[384,512]{1,0:T(8,128)(2,1)}, bf16[384,512]{1,0:T(8,128)(2,1)}, u32[]{:S(2)}, u32[]{:S(2)}) collective-permute-start(bf16[384,512]{1,0:T(8,128)(2,1)} %get-tuple-element.4), channel_id=1, source_target_pairs={{0,8},{8,16},{16,24},{24,0},{1,9},{9,17},{17,25},{25,1},{2,10},{10... | collective-permute-start | bytes 1179656 | tf_op jit(solution)/shard_map/ppermute | solution.py:29
  198.3 34.9 %collective-permute-start.16 = (bf16[384,512]{1,0:T(8,128)(2,1)}, bf16[384,512]{1,0:T(8,128)(2,1)}, u32[]{:S(2)}, u32[]{:S(2)}) collective-permute-start(bf16[384,512]{1,0:T(8,128)(2,1)} %get-tuple-element.6), channel_id=1, source_target_pairs={{0,16},{8,24},{16,0},{24,8},{1,17},{9,25},{17,1},{25,9},{2,18},{10... | collective-permute-start | bytes 1179656 | tf_op jit(solution)/shard_map/ppermute | solution.py:29
  199.8 5.0 %copy-start.10 = (bf16[1024,512]{1,0:T(8,128)(2,1)S(1)}, bf16[1024,512]{1,0:T(8,128)(2,1)}, u32[]{:S(2)}) copy-start(bf16[1024,512]{1,0:T(8,128)(2,1)} %get-tuple-element.9) | copy-start | bytes 3145732
  199.8 5.0 %copy-start.11 = (bf16[1024,512]{1,0:T(8,128)(2,1)S(1)}, bf16[1024,512]{1,0:T(8,128)(2,1)}, u32[]{:S(2)}) copy-start(bf16[1024,512]{1,0:T(8,128)(2,1)} %get-tuple-element.10) | copy-start | bytes 3145732
  199.8 35.4 %collective-permute-start.17 = (bf16[384,512]{1,0:T(8,128)(2,1)}, bf16[384,512]{1,0:T(8,128)(2,1)}, u32[]{:S(2)}, u32[]{:S(2)}) collective-permute-start(bf16[384,512]{1,0:T(8,128)(2,1)} %get-tuple-element.5), channel_id=1, source_target_pairs={{0,24},{8,0},{16,8},{24,16},{1,25},{9,1},{17,9},{25,17},{2,26},{10... | collective-permute-start | bytes 1179656 | tf_op jit(solution)/shard_map/ppermute | solution.py:29
  203.4 0.8 copy-start.12
  203.4 1.0 copy-start.13
  203.4 1.2 copy-start.14
  203.5 1.3 copy-start.15
  218.4 2.3 copy-start.23
  219.1 1.3 copy-start.2
  220.6 21.0 %copy-start.3 = (f32[256,2,2,512]{3,0,2,1:T(8,128)S(1)}, f32[256,2,2,512]{3,0,2,1:T(8,128)}, u32[]{:S(2)}) copy-start(f32[256,2,2,512]{3,0,2,1:T(8,128)} %copy-done.2) | copy-start | bytes 6291460
  220.6 21.0 %collective-permute-start.13 = (bf16[256,2,512]{2,0,1:T(8,128)(2,1)S(1)}, bf16[256,2,512]{2,0,1:T(8,128)(2,1)}, u32[]{:S(2)}, u32[]{:S(2)}) collective-permute-start(bf16[256,2,512]{2,0,1:T(8,128)(2,1)S(1)} %fusion.67), channel_id=1, source_target_pairs={{0,1},{1,0},{2,3},{3,2},{4,5},{5,4},{6,7},{7,6},{8,9},{9,8},{10,11... | collective-permute-start | bytes 1572872 | tf_op jit(solution)/shard_map/ppermute | solution.py:34
  237.7 12.7 %all-to-all-start.3 = ((bf16[8,48,512]{2,1,0:T(8,128)(2,1)}), bf16[8,48,512]{2,1,0:T(8,128)(2,1)S(1)}, u32[]{:S(2)}, u32[]{:S(2)}) async-start(bf16[8,48,512]{2,1,0:T(8,128)(2,1)} %bitcast.27), calls=%async_computation.3 | async-start | bytes 786432 | tf_op jit(solution)/shard_map/all_to_all | solution.py:138
  241.5 13.0 %copy-start.19 = (pred[256]{0:T(512)(128)(4,1)S(1)}, pred[256]{0:T(512)(128)(4,1)}, u32[]{:S(2)}) copy-start(pred[256]{0:T(512)(128)(4,1)} %compare_bitcast_fusion) | copy-start | bytes 772
  242.8 1.0 copy-start.5
  243.8 10.8 %collective-permute-start.14 = (bf16[256,1,512]{2,0,1:T(8,128)(2,1)S(1)}, bf16[256,1,512]{2,0,1:T(8,128)(2,1)S(1)}, u32[]{:S(2)}, u32[]{:S(2)}) collective-permute-start(bf16[256,1,512]{2,0,1:T(8,128)(2,1)S(1)} %dynamic-slice_convert_fusion.4), channel_id=1, source_target_pairs={{0,2},{1,3},{2,0},{3,1},{4,6},{5,7},{6,4},{7,5},{8,10},{9,11},{10,... | collective-permute-start | bytes 786440 | tf_op jit(solution)/shard_map/ppermute | solution.py:34

commit v2 on v1

--- a/solution.py
+++ b/solution.py
@@ -1,6 +1,10 @@
+import functools
+
 import jax
 import jax.numpy as jnp
 from jax import lax
+from jax.experimental import pallas as pl
+from jax.experimental.pallas import tpu as pltpu
 from jax.sharding import PartitionSpec as P
 
 HEAD_DIM = 128
@@ -137,6 +141,222 @@
     sent = values.reshape(group_size, capacity, values.shape[1])
     arrived = lax.all_to_all(sent, ("expert", "dp"), split_axis=0, concat_axis=0, tiled=True)
     return arrived.reshape(values.shape)
+
+
+def gate(value, *after):
+    held = lax.optimization_barrier((value,) + after)
+    return held
+
+
+def plane_gather(own):
+    over_y = swap(own, "expert", 1)
+    over_x = swap(own, "dp", 2)
+    far = swap(over_y, "dp", 2)
+    near = [own, over_x, over_y, far]
+    blocks = []
+    for block in near:
+        blocks += [block, swap(block, "dp", 1)]
+    return blocks
+
+
+def plane_gather_shared(own, *after):
+    count = lax.axis_size("section")
+    me = lax.axis_index("section")
+    share = own.shape[0] // count
+    mine = lax.dynamic_slice_in_dim(own, me * share, share, 0)
+    fetched = swap(mine, "expert", 1)
+    over_y = lax.dynamic_update_slice_in_dim(jnp.zeros_like(own), fetched, me * share, 0)
+    for step in range(1, count):
+        owner = lax.rem(me - step + count, count)
+        over_y = lax.dynamic_update_slice_in_dim(
+            over_y, shift(fetched, "section", step), owner * share, 0
+        )
+    over_x = swap(own, "dp", 2)
+    return own, over_x, over_y
+
+
+def plane_gather_rest(own, over_x, over_y):
+    far = swap(over_y, "dp", 2)
+    blocks = []
+    for block in (own, over_x, over_y, far):
+        blocks += [block, swap(block, "dp", 1)]
+    return blocks
+
+
+def plane_ids(ids):
+    held = ids[None]
+    for axis, mask in (("dp", 1), ("dp", 2), ("expert", 1)):
+        held = jnp.concatenate([held, swap(held, axis, mask)], axis=0)
+    return held
+
+
+def dispatch_kernel(capacity, code_ref, *refs):
+    blocks, out_ref = refs[:-1], refs[-1]
+    for place, block in enumerate(blocks):
+        code = code_ref[place : place + 1, :]
+        slot = lax.broadcasted_iota(jnp.int32, (capacity, code.shape[1]), 0)
+        pick = jnp.where(slot == code, 1.0, 0.0).astype(jnp.bfloat16)
+        rows = jnp.dot(pick, block[...], preferred_element_type=jnp.float32)
+        out_ref[place * capacity : (place + 1) * capacity, :] = rows.astype(jnp.bfloat16)
+
+
+def dispatch(code, blocks, capacity):
+    features = blocks[0].shape[1]
+    return pl.pallas_call(
+        functools.partial(dispatch_kernel, capacity),
+        out_shape=jax.ShapeDtypeStruct((len(blocks) * capacity, features), jnp.bfloat16),
+        in_specs=[pl.BlockSpec(memory_space=pltpu.VMEM)] * (1 + len(blocks)),
+        out_specs=pl.BlockSpec(memory_space=pltpu.VMEM),
+        compiler_params=pltpu.CompilerParams(vmem_limit_bytes=40 * 1024 * 1024),
+        name="dispatch",
+    )(code, *blocks)
+
+
+def plane_return(values, capacity):
+    arrived = [values[:capacity]]
+    for place in range(1, values.shape[0] // capacity):
+        sent = values[place * capacity : (place + 1) * capacity]
+        size = lax.axis_size(("expert", "dp"))
+        arrived.append(
+            lax.ppermute(sent, ("expert", "dp"), [(i, i ^ place) for i in range(size)])
+        )
+    return jnp.concatenate(arrived, axis=0)
+
+
+def small_body(
+    tokens,
+    expert_ids,
+    gate_weights,
+    out_grad,
+    inner_weight,
+    outer_weight,
+    final_gain,
+    dec_states,
+    src_lengths,
+    tgt_lengths,
+    norm_gain,
+    query_weight,
+    key_weight,
+    value_weight,
+    out_weight,
+):
+    token_count, feature_count = tokens.shape
+    group_size = lax.axis_size(("expert", "dp"))
+    capacity = 3 * token_count // group_size
+    slots = group_size * capacity
+    here = lax.axis_index(("expert", "dp"))
+    y = lax.axis_index("expert")
+
+    token_blocks = plane_gather(tokens)
+    ids = plane_ids(expert_ids.T)
+    row = lax.broadcasted_iota(jnp.int32, (token_count, token_count), 0)
+    column = lax.broadcasted_iota(jnp.int32, (token_count, token_count), 1)
+    named_here = (ids == here).any(axis=1)
+    before = jnp.dot(
+        named_here.astype(jnp.bfloat16),
+        (row < column).astype(jnp.bfloat16),
+        preferred_element_type=jnp.float32,
+    ).astype(jnp.int32)
+    code = jnp.where(named_here, before, -1)
+
+    named = expert_ids[:, :, None] == jnp.arange(group_size, dtype=jnp.int32)[None, None, :]
+    either = (named[:, 0] | named[:, 1]).astype(jnp.bfloat16)
+    earlier = jnp.dot(
+        (column < row).astype(jnp.bfloat16), either, preferred_element_type=jnp.float32
+    ).astype(jnp.int32)
+    rank = jnp.sum(jnp.where(named, earlier[:, None, :], 0), axis=2)
+    position = (expert_ids ^ here) * capacity + rank
+    pick_first = slot_matrix(position[:, 0], slots)
+    pick_second = slot_matrix(position[:, 1], slots)
+
+    def combine(arrived):
+        first = jnp.dot(pick_first, arrived, preferred_element_type=jnp.float32)
+        second = jnp.dot(pick_second, arrived, preferred_element_type=jnp.float32)
+        return gate_weights[:, :1] * first + gate_weights[:, 1:] * second
+
+    weight_in = inner_weight[0]
+    weight_out = outer_weight[0]
+    rows = dispatch(code, token_blocks, capacity)
+
+    states = dec_states[0]
+    normed = normalize(states.astype(jnp.float32), norm_gain[0]).astype(jnp.bfloat16)
+    half = feature_count // 2
+    key_top, key_low = key_weight[0, : half // 2], key_weight[0, half // 2 :]
+    quarter = normed.shape[0] // lax.axis_size("dp")
+    d = lax.axis_index("dp")
+    asked = lax.dynamic_slice(normed, (d * quarter, (1 - y) * half), (quarter, half))
+    key_top, held_grad, asked, rows = gate(key_top, out_grad, asked, rows)
+    grad_parts = plane_gather_shared(held_grad)
+    key_top_other = swap(key_top, "expert", 1)
+    asked_here = swap(asked, "expert", 1)
+
+    pre_act = jnp.dot(rows, weight_in, preferred_element_type=jnp.float32)
+    hidden = jax.nn.gelu(pre_act).astype(jnp.bfloat16)
+    forward_part = jnp.dot(hidden, weight_out, preferred_element_type=jnp.float32)
+    outputs_home = plane_return(forward_part.astype(jnp.bfloat16), capacity)
+
+    value_own, out_own = value_weight[0], out_weight[0]
+    key_low, value_own, out_own, asked_here, over_y, outputs_home = gate(
+        key_low, value_own, out_own, asked_here, grad_parts[2], outputs_home
+    )
+    grad_blocks = plane_gather_rest(grad_parts[0], grad_parts[1], over_y)
+    asked_rows = gather_rows(asked_here, "dp")
+    query_own = query_weight[0]
+    query_there = jnp.dot(asked_rows, query_own, preferred_element_type=jnp.float32)
+    key_low_other = swap(key_low, "expert", 1)
+    value_other = swap(value_own, "expert", 1)
+    query_other = swap(query_there.astype(jnp.bfloat16), "expert", 1)
+    out_other = swap(out_own, "expert", 1)
+
+    mixed_slice = sum_sections(combine(outputs_home)).astype(jnp.bfloat16)
+    mixed = gather_sections(mixed_slice).astype(jnp.float32)
+    memory = normalize(tokens.astype(jnp.float32) + mixed, final_gain).astype(jnp.bfloat16)
+
+    arrived_grads = dispatch(code, grad_blocks, capacity)
+    back = contract_last(arrived_grads, weight_out)
+    slope = jax.vjp(jax.nn.gelu, pre_act)[1](back)[0].astype(jnp.bfloat16)
+    backward_part = contract_last(slope, weight_in).astype(jnp.bfloat16)
+    backward_part, memory = gate(backward_part, memory)
+    backward_slice = sum_sections(backward_part).astype(jnp.bfloat16)
+    grads_home = plane_return(backward_slice, capacity)
+    token_grad = combine(grads_home).astype(jnp.bfloat16)
+
+    normed_own = lax.dynamic_slice_in_dim(normed, y * half, half, 1)
+    query = (
+        jnp.dot(normed_own, query_own, preferred_element_type=jnp.float32)
+        + query_other.astype(jnp.float32)
+    ).astype(jnp.bfloat16)
+    source = gather_rows(memory, "dp")
+    first = y == 0
+
+    def ordered(own, other, dimension):
+        return jnp.concatenate(
+            [jnp.where(first, own, other), jnp.where(first, other, own)], axis=dimension
+        )
+
+    full_key = ordered(
+        key_weight[0], jnp.concatenate([key_top_other, key_low_other], axis=0), 0
+    )
+    full_value = ordered(value_own, value_other, 0)
+    full_out = ordered(out_own, out_other, 1)
+    key_sum = jnp.dot(source, full_key, preferred_element_type=jnp.float32)
+    value_sum = jnp.dot(source, full_value, preferred_element_type=jnp.float32)
+    key_mask = jnp.arange(SRC_LEN, dtype=jnp.int32)[None, :] < src_lengths[:, None]
+    context = attend(
+        query, key_sum.astype(jnp.bfloat16), value_sum.astype(jnp.bfloat16), key_mask
+    )
+    dec_out = finish(context, full_out, states, tgt_lengths)
+    return (dec_out[None], token_grad)
+
+
+def finish(context, full_out, states, tgt_lengths):
+    attended = sum_heads(jnp.dot(context, full_out, preferred_element_type=jnp.float32))
+    my_columns = attended.shape[1]
+    residual = lax.dynamic_slice_in_dim(
+        states, lax.axis_index("dp") * my_columns, my_columns, 1
+    ).astype(jnp.float32)
+    row_mask = (jnp.arange(TGT_LEN, dtype=jnp.int32)[None, :] < tgt_lengths[:, None]).reshape(-1, 1)
+    return (residual + jnp.where(row_mask, attended, 0.0)).astype(jnp.bfloat16)
 
 
 def body(
@@ -218,13 +438,7 @@
         value_sum.astype(jnp.bfloat16),
         key_mask,
     )
-    attended = sum_heads(jnp.dot(context, full_out, preferred_element_type=jnp.float32))
-    my_columns = attended.shape[1]
-    residual = lax.dynamic_slice_in_dim(
-        states, lax.axis_index("dp") * my_columns, my_columns, 1
-    ).astype(jnp.float32)
-    row_mask = (jnp.arange(TGT_LEN, dtype=jnp.int32)[None, :] < tgt_lengths[:, None]).reshape(-1, 1)
-    dec_out = (residual + jnp.where(row_mask, attended, 0.0)).astype(jnp.bfloat16)
+    dec_out = finish(context, full_out, states, tgt_lengths)
     return (dec_out[None], token_grad)
 
 
@@ -247,4 +461,6 @@
         P("section", "dp", "expert"),
     )
     out_specs = (P("section", "expert", "dp"), P(("expert", "dp"), "section"))
-    return jax.shard_map(body, mesh=mesh, in_specs=in_specs, out_specs=out_specs, check_vma=False)
+    small = mesh.shape["expert"] == 2 and mesh.shape["dp"] == 4
+    chosen = small_body if small else body
+    return jax.shard_map(chosen, mesh=mesh, in_specs=in_specs, out_specs=out_specs, check_vma=False)

time: 257 us -> 247 us (0.961)
  the two profiles are of different devices: /device:TPU:8 before, /device:TPU:12 now
where the time goes in v2:
time: 247 us; the launch traced here: 245 us
  waiting for transfers between devices  107 us (43%)
  starting transfers between devices  48.2 us (20%)
  local copies, waits for them, and re-layouts  29.5 us (12%)
  matrix products  28.1 us (11%)
  other arithmetic  26.9 us (11%)
  Pallas kernels  4.4 us (2%)
    ppermute x31, waiting for transfers between devices, swap(): return lax.ppermute(value, axis, [(i, i ^ mask) for i in range(size)])  59.3 us
    ppermute x12, waiting for transfers between devices, shift(): lax.ppermute(value, axis, [(i, (i + step) % size) for i in range(size)])  34.3 us
    ppermute x31, starting transfers between devices, swap(): return lax.ppermute(value, axis, [(i, i ^ mask) for i in range(size)])  17.2 us
    ppermute x12, starting transfers between devices, shift(): lax.ppermute(value, axis, [(i, (i + step) % size) for i in range(size)])  16.1 us
    ppermute x14, starting transfers between devices, plane_return(): lax.ppermute(sent, ('expert', 'dp'), [(i, i ^ place) for i in range(size)])  14.9 us
    unnamed x87, local copies, waits for them, and re-layouts  14 us
    ppermute x14, waiting for transfers between devices, plane_return(): lax.ppermute(sent, ('expert', 'dp'), [(i, i ^ place) for i in range(size)])  13.2 us
    dot_general x1, matrix products, contract_last(): lax.dot_general(left, right, (((1,), (1,)), ((), ())), preferred_element_...  8.17 us
  transfers between devices with their start and end apart: 57, of which 21 were waited for; matrix products, arithmetic and copies ran while one was open for 30% of the time, Pallas kernels for 1%

profile of v2, /device:TPU:12, one launch (start us, length us, event | category | flops | bytes accessed | tf_op | source)
XLA Modules:
  0.0 245.3 jit_solution(12728184141283743716)
XLA Ops:
  1.2 1.5 collective-permute-start.4
  3.9 1.5 convert_reduce_fusion
  6.1 2.6 %fusion.21 = bf16[256,2048]{1,0:T(8,128)(2,1)} fusion(bf16[1,256,2048]{2,1,0:T(8,128)(2,1)} %param.22, f32[2048]{0:T(1024)S(1)} %bitcast.97, f32[256]{0:T(256)S(1)} %add_rsqrt_fusion, f32[256]{0:T(256)S(1)} %broadcast_multiply_fusion), kind=kLoop, calls=%fused_computation.23 | loop fusion | flops 2621440 | bytes 2107392 | tf_op jit(solution)/shard_map/convert_element_type | solution.py:282
  8.7 2.4 slice_bitcast_fusion.1
  12.4 2.2 collective-permute-done.6.refs_4_
  14.6 1.5 collective-permute-start.8
  17.2 10.3 %collective-permute-done.8.refs_6_ = bf16[128,2048]{1,0:T(8,128)(2,1)} collective-permute-done((bf16[128,2048]{1,0:T(8,128)(2,1)S(1)}, bf16[128,2048]{1,0:T(8,128)(2,1)}, u32[]{:S(2)}, u32[]{:S(2)}) %collective-permute-start.8) | collective-permute-done | bytes 524320 | tf_op jit(solution)/shard_map/ppermute | solution.py:38
  29.1 2.1 collective-permute-done.2
  31.4 2.5 %dispatch.2 = bf16[384,2048]{1,0:T(8,128)(2,1)S(1)} custom-call(s32[8,128]{1,0:T(8,128)S(1)} %fusion.51.code_ref, bf16[128,2048]{1,0:T(8,128)(2,1)S(1)} %copy-done.2, bf16[128,2048]{1,0:T(8,128)(2,1)} %collective-permute-done.3.refs_1_, bf16[128,2048]{1,0:T(8,128)(2,1)S(1)} %collective-permute-done.4.refs_2_, ...), custom_call_target="tpu_custom_call" | custom-call | tf_op jit(solution)/shard_map/dispatch/pallas_call | solution.py:205
  34.6 1.8 fusion.7
  36.4 2.0 fusion.12
  38.6 1.6 collective-permute-start.19
  40.4 1.5 collective-permute-start.21
  42.2 2.5 %collective-permute-start.23 = (bf16[48,2048]{1,0:T(8,128)(2,1)S(1)}, bf16[48,2048]{1,0:T(8,128)(2,1)S(1)}, u32[]{:S(2)}, u32[]{:S(2)}) collective-permute-start(bf16[48,2048]{1,0:T(8,128)(2,1)S(1)} %get-tuple-element.42), channel_id=1, source_target_pairs={{0,6},{1,7},{2,4},{3,5},{4,2},{5,3},{6,0},{7,1},{8,14},{9,15},{10,... | collective-permute-start | bytes 589832 | tf_op jit(solution)/shard_map/ppermute | solution.py:221
  44.8 1.6 collective-permute-done.19
  47.6 2.0 collective-permute-done.20
  49.7 1.5 collective-permute-start.13
  51.8 8.0 %collective-permute-done.22 = bf16[48,2048]{1,0:T(8,128)(2,1)S(1)} collective-permute-done((bf16[48,2048]{1,0:T(8,128)(2,1)S(1)}, bf16[48,2048]{1,0:T(8,128)(2,1)S(1)}, u32[]{:S(2)}, u32[]{:S(2)}) %collective-permute-start.22) | collective-permute-done | bytes 196640 | tf_op jit(solution)/shard_map/ppermute | solution.py:221
  59.8 1.6 collective-permute-start.15
  62.8 1.9 collective-permute-start.17
  64.6 1.6 collective-permute-done.15
  66.2 7.3 %collective-permute-done.16 = bf16[32,2048]{1,0:T(8,128)(2,1)S(1)} collective-permute-done((bf16[32,2048]{1,0:T(8,128)(2,1)S(1)}, bf16[32,2048]{1,0:T(8,128)(2,1)S(1)}, u32[]{:S(2)}, u32[]{:S(2)}) %collective-permute-start.16) | collective-permute-done | bytes 131104 | tf_op jit(solution)/shard_map/ppermute | solution.py:33
  73.5 1.8 collective-permute-done.17
  77.5 1.7 collective-permute-start.29
  79.2 1.9 collective-permute-start.30
  81.7 2.1 collective-permute-done.28
  83.8 5.4 %collective-permute-done.29 = bf16[128,512]{1,0:T(8,128)(2,1)S(1)} collective-permute-done((bf16[128,512]{1,0:T(8,128)(2,1)S(1)}, bf16[128,512]{1,0:T(8,128)(2,1)S(1)}, u32[]{:S(2)}, u32[]{:S(2)}) %collective-permute-start.29) | collective-permute-done | bytes 131104 | tf_op jit(solution)/shard_map/ppermute | solution.py:33
  89.2 1.9 collective-permute-done.30
  91.9 1.7 constant_dynamic-update-slice_fusion.19
  94.9 1.5 collective-permute-start.11
  97.0 1.5 collective-permute-start.32
  98.5 1.9 constant_dynamic-update-slice_fusion.8
  100.3 2.0 collective-permute-start.33
  103.1 4.2 %collective-permute-done.32 = bf16[128,512]{1,0:T(8,128)(2,1)S(1)} collective-permute-done((bf16[128,512]{1,0:T(8,128)(2,1)S(1)}, bf16[128,512]{1,0:T(8,128)(2,1)S(1)}, u32[]{:S(2)}, u32[]{:S(2)}) %collective-permute-start.32) | collective-permute-done | bytes 131104 | tf_op jit(solution)/shard_map/ppermute | solution.py:33
  107.9 3.7 %collective-permute-done.38 = bf16[64,1024]{1,0:T(8,128)(2,1)S(1)} collective-permute-done((bf16[64,1024]{1,0:T(8,128)(2,1)S(1)}, bf16[64,1024]{1,0:T(8,128)(2,1)S(1)}, u32[]{:S(2)}, u32[]{:S(2)}) %collective-permute-start.38) | collective-permute-done | bytes 131104 | tf_op jit(solution)/shard_map/ppermute | solution.py:38
  111.6 1.5 collective-permute-start.26
  115.1 1.3 multiply_reduce_fusion
  116.4 1.8 collective-permute-start.43
  119.1 2.1 multiply_convert_fusion.1
  121.3 3.4 %collective-permute-done.26.refs_6_ = bf16[128,2048]{1,0:T(8,128)(2,1)} collective-permute-done((bf16[128,2048]{1,0:T(8,128)(2,1)S(1)}, bf16[128,2048]{1,0:T(8,128)(2,1)}, u32[]{:S(2)}, u32[]{:S(2)}) %collective-permute-start.26) | collective-permute-done | bytes 524320 | tf_op jit(solution)/shard_map/ppermute | solution.py:38
  124.7 11.9 %collective-permute-done.41 = bf16[256,512]{1,0:T(8,128)(2,1)S(1)} collective-permute-done((bf16[256,512]{1,0:T(8,128)(2,1)S(1)}, bf16[256,512]{1,0:T(8,128)(2,1)S(1)}, u32[]{:S(2)}, u32[]{:S(2)}) %collective-permute-start.41) | collective-permute-done | bytes 262176 | tf_op jit(solution)/shard_map/ppermute | solution.py:38
  138.4 1.8 collective-permute-start.37
  140.2 1.9 constant_dynamic-update-slice_fusion.7
  142.1 2.7 %bitcast_select_fusion.1 = (bf16[1024,512]{1,0:T(8,128)(2,1)}, bf16[1024,512]{1,0:T(8,128)(2,1)}) fusion(bf16[1024,512]{1,0:T(8,128)(2,1)} %constant_dynamic-update-slice_fusion.7, bf16[1,1024,512]{2,1,0:T(8,128)(2,1)S(1)} %copy-done.11, pred[]{:T(512)S(6)} %eq.116), kind=kLoop, calls=%fused_computation.60 | loop fusion | flops 1048576 | bytes 4194305 | tf_op jit(solution)/shard_map/jit(_where)/select_n | solution.py:334
  150.7 1.9 dispatch.3
  152.6 8.2 %fusion.9 = bf16[384,2048]{1,0:T(8,128)(2,1)S(1)} fusion(bf16[1,2048,1024]{2,1,0:T(8,128)(2,1)} %param.19, f32[384,1024]{1,0:T(8,128)} %copy-done.36, bf16[384,2048]{1,0:T(8,128)(2,1)S(1)} %dispatch.3, bf16[1,1024,2048]{2,1,0:T(8,128)(2,1)} %param.20), kind=kOutput, calls=%fused_computation.9 | convolution fusion | flops 3229876224 | bytes 13107200 | tf_op jit(solution)/shard_map/dot_general | solution.py:26
  162.2 2.9 %collective-permute-start.48 = (bf16[384,512]{1,0:T(8,128)(2,1)S(1)}, bf16[384,512]{1,0:T(8,128)(2,1)S(1)}, u32[]{:S(2)}, u32[]{:S(2)}) collective-permute-start(bf16[384,512]{1,0:T(8,128)(2,1)S(1)} %get-tuple-element.40), channel_id=1, source_target_pairs={{0,16},{8,24},{16,0},{24,8},{1,17},{9,25},{17,1},{25,9},{2,18},{10... | collective-permute-start | bytes 1179656 | tf_op jit(solution)/shard_map/ppermute | solution.py:33
  165.7 2.8 %broadcast_select_fusion.3 = (bf16[1024,512]{1,0:T(8,128)(2,1)}, bf16[1024,512]{1,0:T(8,128)(2,1)}) fusion(bf16[1024,512]{1,0:T(8,128)(2,1)S(1)} %bitcast.92, bf16[1024,512]{1,0:T(8,128)(2,1)} %collective-permute-done.37, pred[]{:T(512)S(6)} %eq.116), kind=kLoop, calls=%fused_computation.72 | loop fusion | flops 1048576 | bytes 4194305 | tf_op jit(solution)/shard_map/jit(_where)/select_n | solution.py:334
  168.5 18.4 %collective-permute-done.44 = bf16[512,1024]{1,0:T(8,128)(2,1)} collective-permute-done((bf16[512,1024]{1,0:T(8,128)(2,1)}, bf16[512,1024]{1,0:T(8,128)(2,1)}, u32[]{:S(2)}, u32[]{:S(2)}) %collective-permute-start.44) | collective-permute-done | bytes 1048608 | tf_op jit(solution)/shard_map/ppermute | solution.py:38
  186.9 1.7 broadcast_select_fusion.1
  188.6 7.5 %collective-permute-done.48 = bf16[384,512]{1,0:T(8,128)(2,1)S(1)} collective-permute-done((bf16[384,512]{1,0:T(8,128)(2,1)S(1)}, bf16[384,512]{1,0:T(8,128)(2,1)S(1)}, u32[]{:S(2)}, u32[]{:S(2)}) %collective-permute-start.48) | collective-permute-done | bytes 393248 | tf_op jit(solution)/shard_map/ppermute | solution.py:33
  196.0 2.6 %collective-permute-done.49 = bf16[384,512]{1,0:T(8,128)(2,1)S(1)} collective-permute-done((bf16[384,512]{1,0:T(8,128)(2,1)S(1)}, bf16[384,512]{1,0:T(8,128)(2,1)S(1)}, u32[]{:S(2)}, u32[]{:S(2)}) %collective-permute-start.49) | collective-permute-done | bytes 393248 | tf_op jit(solution)/shard_map/ppermute | solution.py:33
  200.1 1.5 maximum_bitcast_fusion
  201.6 3.9 %copy.27 = bf16[2048,512]{1,0:T(8,128)(2,1)} copy(bf16[2048,512]{0,1:T(8,128)(2,1)} %maximum_bitcast_fusion) | data formatting | bytes 4194304 | tf_op jit(solution)/shard_map/dot_general | solution.py:353
  206.9 1.6 collective-permute-start.53
  208.6 1.5 collective-permute-done.51
  211.4 2.7 %collective-permute-start.56 = (bf16[48,512]{1,0:T(8,128)(2,1)S(1)}, bf16[48,512]{1,0:T(8,128)(2,1)}, u32[]{:S(2)}, u32[]{:S(2)}) collective-permute-start(bf16[48,512]{1,0:T(8,128)(2,1)S(1)} %get-tuple-element.58), channel_id=1, source_target_pairs={{0,7},{1,6},{2,5},{3,4},{4,3},{5,2},{6,1},{7,0},{8,15},{9,14},{10,... | collective-permute-start | bytes 147464 | tf_op jit(solution)/shard_map/ppermute | solution.py:221
  214.1 1.4 select_select_fusion.3
  218.1 1.3 fusion.41
  221.0 2.8 %fusion.45 = bf16[512,512]{1,0:T(8,128)(2,1)S(1)} fusion(bf16[1024,512]{1,0:T(8,128)(2,1)S(1)} %copy-done.20, bf16[1024,512]{1,0:T(8,128)(2,1)S(1)} %copy-done.19, bf16[128,2048]{1,0:T(8,128)(2,1)} %copy-done.22, bf16[128,2048]{1,0:T(8,128)(2,1)} %copy-done.23, bf16[128,2048]{1,0:T(8,128)(2,1)} %copy-done.24, bf16[128,2048]{1,0:T(8,128)(2,1)} %copy-done.21), kind=kOutput, calls=%fused_computation.47 | convolution fusion | flops 1086586880 | bytes 4718592 | tf_op jit(solution)/shard_map/dot_general | solution.py:343
  223.9 3.7 %fusion.48 = bf16[2,128,4,128]{1,3,2,0:T(8,128)(2,1)S(1)} fusion(bf16[2,256,4,128]{3,2,1,0:T(4,128)(2,1)S(1)} %reshape.122, f32[2,4,128]{2,1,0:T(4,128)S(1)} %fusion.110, f32[2,4,128,256]{3,2,1,0:T(8,128)} %fusion.41), kind=kOutput, calls=%fused_computation.50 | convolution fusion | flops 68027648 | bytes 1839104 | tf_op jit(solution)/shard_map/bhqk,bkhd->bqhd/dot_general | solution.py:136
  227.9 2.3 fusion.77
  236.2 7.2 %collective-permute-done.46 = bf16[256,1,512]{2,0,1:T(8,128)(2,1)S(1)} collective-permute-done((bf16[256,1,512]{2,0,1:T(8,128)(2,1)S(1)}, bf16[256,1,512]{2,0,1:T(8,128)(2,1)S(1)}, u32[]{:S(2)}, u32[]{:S(2)}) %collective-permute-start.46) | collective-permute-done | bytes 262176 | tf_op jit(solution)/shard_map/ppermute | solution.py:38
  243.5 1.8 fusion.72
  (214 shorter events, 45.1 us)
Async XLA Ops:
  0.6 10.4 %copy-start = (bf16[1,1024,512]{2,1,0:T(8,128)(2,1)S(1)}, bf16[1,1024,512]{2,1,0:T(8,128)(2,1)}, u32[]{:S(2)}) copy-start(bf16[1,1024,512]{2,1,0:T(8,128)(2,1)} %param.26) | copy-start | bytes 3145732
  0.7 13.9 %collective-permute-start.6 = (bf16[128,2048]{1,0:T(8,128)(2,1)}, bf16[128,2048]{1,0:T(8,128)(2,1)S(1)}, u32[]{:S(2)}, u32[]{:S(2)}) collective-permute-start(bf16[128,2048]{1,0:T(8,128)(2,1)} %refs_0_.1), channel_id=1, source_target_pairs={{0,4},{4,0},{1,5},{5,1},{2,6},{6,2},{3,7},{7,3},{8,12},{12,8},{9,1... | collective-permute-start | bytes 1572872 | tf_op jit(solution)/shard_map/ppermute | solution.py:38
  1.2 15.5 %collective-permute-start.4 = (bf16[128,2048]{1,0:T(8,128)(2,1)}, bf16[128,2048]{1,0:T(8,128)(2,1)S(1)}, u32[]{:S(2)}, u32[]{:S(2)}) collective-permute-start(bf16[128,2048]{1,0:T(8,128)(2,1)} %refs_0_.1), channel_id=1, source_target_pairs={{0,2},{1,3},{2,0},{3,1},{4,6},{5,7},{6,4},{7,5},{8,10},{9,11},{10,... | collective-permute-start | bytes 1572872 | tf_op jit(solution)/shard_map/ppermute | solution.py:38
  2.7 28.6 %collective-permute-start.3 = (bf16[128,2048]{1,0:T(8,128)(2,1)}, bf16[128,2048]{1,0:T(8,128)(2,1)}, u32[]{:S(2)}, u32[]{:S(2)}) collective-permute-start(bf16[128,2048]{1,0:T(8,128)(2,1)} %refs_0_.1), channel_id=1, source_target_pairs={{0,1},{1,0},{2,3},{3,2},{4,5},{5,4},{6,7},{7,6},{8,9},{9,8},{10,11... | collective-permute-start | bytes 1572872 | tf_op jit(solution)/shard_map/ppermute | solution.py:38
  2.7 13.4 %collective-permute-start = (s32[1,2,128]{2,1,0:T(2,128)}, s32[1,2,128]{2,1,0:T(2,128)S(1)}, u32[]{:S(2)}, u32[]{:S(2)}) collective-permute-start(s32[1,2,128]{2,1,0:T(2,128)} %bitcast.93), channel_id=1, source_target_pairs={{0,1},{1,0},{2,3},{3,2},{4,5},{5,4},{6,7},{7,6},{8,9},{9,8},{10,11... | collective-permute-start | bytes 3080 | tf_op jit(solution)/shard_map/ppermute | solution.py:38
  11.1 17.0 %copy-start.31 = (f32[128,2]{0,1:T(2,128)S(1)}, f32[128,2]{0,1:T(2,128)}, u32[]{:S(2)}) copy-start(f32[128,2]{0,1:T(2,128)} %param.17) | copy-start | bytes 3076
  11.1 20.3 %copy-start.2 = (bf16[128,2048]{1,0:T(8,128)(2,1)S(1)}, bf16[128,2048]{1,0:T(8,128)(2,1)}, u32[]{:S(2)}) copy-start(bf16[128,2048]{1,0:T(8,128)(2,1)} %refs_0_.1) | copy-start | bytes 1572868
  14.6 12.9 %collective-permute-start.8 = (bf16[128,2048]{1,0:T(8,128)(2,1)S(1)}, bf16[128,2048]{1,0:T(8,128)(2,1)}, u32[]{:S(2)}, u32[]{:S(2)}) collective-permute-start(bf16[128,2048]{1,0:T(8,128)(2,1)S(1)} %collective-permute-done.6.refs_4_), channel_id=1, source_target_pairs={{0,2},{1,3},{2,0},{3,1},{4,6},{5,7},{6,4},{7,5},{8,10},{9,11},{10,... | collective-permute-start | bytes 1572872 | tf_op jit(solution)/shard_map/ppermute | solution.py:38
  16.1 11.4 %collective-permute-start.1 = (s32[2,2,128]{2,1,0:T(2,128)S(1)}, s32[2,2,128]{2,1,0:T(2,128)S(1)}, u32[]{:S(2)}, u32[]{:S(2)}) collective-permute-start(s32[2,2,128]{2,1,0:T(2,128)S(1)} %pad_add_fusion.1), channel_id=1, source_target_pairs={{0,2},{1,3},{2,0},{3,1},{4,6},{5,7},{6,4},{7,5},{8,10},{9,11},{10,... | collective-permute-start | bytes 6152 | tf_op jit(solution)/shard_map/ppermute | solution.py:38
  16.7 14.7 %collective-permute-start.7 = (bf16[128,2048]{1,0:T(8,128)(2,1)S(1)}, bf16[128,2048]{1,0:T(8,128)(2,1)}, u32[]{:S(2)}, u32[]{:S(2)}) collective-permute-start(bf16[128,2048]{1,0:T(8,128)(2,1)S(1)} %collective-permute-done.6.refs_4_), channel_id=1, source_target_pairs={{0,1},{1,0},{2,3},{3,2},{4,5},{5,4},{6,7},{7,6},{8,9},{9,8},{10,11... | collective-permute-start | bytes 1572872 | tf_op jit(solution)/shard_map/ppermute | solution.py:38
  16.7 14.7 %collective-permute-start.5 = (bf16[128,2048]{1,0:T(8,128)(2,1)S(1)}, bf16[128,2048]{1,0:T(8,128)(2,1)}, u32[]{:S(2)}, u32[]{:S(2)}) collective-permute-start(bf16[128,2048]{1,0:T(8,128)(2,1)S(1)} %collective-permute-done.4.refs_2_), channel_id=1, source_target_pairs={{0,1},{1,0},{2,3},{3,2},{4,5},{5,4},{6,7},{7,6},{8,9},{9,8},{10,11... | collective-permute-start | bytes 1572872 | tf_op jit(solution)/shard_map/ppermute | solution.py:38
  27.5 3.9 %collective-permute-start.9 = (bf16[128,2048]{1,0:T(8,128)(2,1)}, bf16[128,2048]{1,0:T(8,128)(2,1)}, u32[]{:S(2)}, u32[]{:S(2)}) collective-permute-start(bf16[128,2048]{1,0:T(8,128)(2,1)} %collective-permute-done.8.refs_6_), channel_id=1, source_target_pairs={{0,1},{1,0},{2,3},{3,2},{4,5},{5,4},{6,7},{7,6},{8,9},{9,8},{10,11... | collective-permute-start | bytes 1572872 | tf_op jit(solution)/shard_map/ppermute | solution.py:38
  27.5 3.7 %collective-permute-start.2 = (s32[4,2,128]{2,1,0:T(2,128)S(1)}, s32[4,2,128]{2,1,0:T(2,128)S(1)}, u32[]{:S(2)}, u32[]{:S(2)}) collective-permute-start(s32[4,2,128]{2,1,0:T(2,128)S(1)} %pad_add_fusion), channel_id=1, source_target_pairs={{0,4},{4,0},{1,5},{5,1},{2,6},{6,2},{3,7},{7,3},{8,12},{12,8},{9,1... | collective-permute-start | bytes 12296 | tf_op jit(solution)/shard_map/ppermute | solution.py:38
  28.1 47.2 %copy-start.28 = (f32[128]{0:T(128)}, f32[128]{0:T(128)S(1)}, u32[]{:S(2)}) copy-start(f32[128]{0:T(128)S(1)} %get-tuple-element.69) | copy-start | bytes 1540
  34.0 8.0 %collective-permute-start.14 = (bf16[32,2048]{1,0:T(8,128)(2,1)S(1)}, bf16[32,2048]{1,0:T(8,128)(2,1)S(1)}, u32[]{:S(2)}, u32[]{:S(2)}) collective-permute-start(bf16[32,2048]{1,0:T(8,128)(2,1)S(1)} %constant_dynamic-slice_fusion.3), channel_id=1, source_target_pairs={{0,4},{4,0},{1,5},{5,1},{2,6},{6,2},{3,7},{7,3},{8,12},{12,8},{9,1... | collective-permute-start | bytes 393224 | tf_op jit(solution)/shard_map/ppermute | solution.py:38
  38.5 3.7 %collective-permute-start.18 = (bf16[48,2048]{1,0:T(8,128)(2,1)S(1)}, bf16[48,2048]{1,0:T(8,128)(2,1)S(1)}, u32[]{:S(2)}, u32[]{:S(2)}) collective-permute-start(bf16[48,2048]{1,0:T(8,128)(2,1)S(1)} %get-tuple-element.47), channel_id=1, source_target_pairs={{0,1},{1,0},{2,3},{3,2},{4,5},{5,4},{6,7},{7,6},{8,9},{9,8},{10,11... | collective-permute-start | bytes 589832 | tf_op jit(solution)/shard_map/ppermute | solution.py:221
  38.6 7.8 %collective-permute-start.19 = (bf16[48,2048]{1,0:T(8,128)(2,1)S(1)}, bf16[48,2048]{1,0:T(8,128)(2,1)S(1)}, u32[]{:S(2)}, u32[]{:S(2)}) collective-permute-start(bf16[48,2048]{1,0:T(8,128)(2,1)S(1)} %get-tuple-element.46), channel_id=1, source_target_pairs={{0,2},{1,3},{2,0},{3,1},{4,6},{5,7},{6,4},{7,5},{8,10},{9,11},{10,... | collective-permute-start | bytes 589832 | tf_op jit(solution)/shard_map/ppermute | solution.py:221
  40.1 9.5 %collective-permute-start.20 = (bf16[48,2048]{1,0:T(8,128)(2,1)S(1)}, bf16[48,2048]{1,0:T(8,128)(2,1)S(1)}, u32[]{:S(2)}, u32[]{:S(2)}) collective-permute-start(bf16[48,2048]{1,0:T(8,128)(2,1)S(1)} %get-tuple-element.45), channel_id=1, source_target_pairs={{0,3},{1,2},{2,1},{3,0},{4,7},{5,6},{6,5},{7,4},{8,11},{9,10},{10,... | collective-permute-start | bytes 589832 | tf_op jit(solution)/shard_map/ppermute | solution.py:221
  40.4 10.8 %collective-permute-start.21 = (bf16[48,2048]{1,0:T(8,128)(2,1)S(1)}, bf16[48,2048]{1,0:T(8,128)(2,1)S(1)}, u32[]{:S(2)}, u32[]{:S(2)}) collective-permute-start(bf16[48,2048]{1,0:T(8,128)(2,1)S(1)} %get-tuple-element.44), channel_id=1, source_target_pairs={{0,4},{1,5},{2,6},{3,7},{4,0},{5,1},{6,2},{7,3},{8,12},{9,13},{10,... | collective-permute-start | bytes 589832 | tf_op jit(solution)/shard_map/ppermute | solution.py:221
  42.0 17.9 %collective-permute-start.22 = (bf16[48,2048]{1,0:T(8,128)(2,1)S(1)}, bf16[48,2048]{1,0:T(8,128)(2,1)S(1)}, u32[]{:S(2)}, u32[]{:S(2)}) collective-permute-start(bf16[48,2048]{1,0:T(8,128)(2,1)S(1)} %get-tuple-element.43), channel_id=1, source_target_pairs={{0,5},{1,4},{2,7},{3,6},{4,1},{5,0},{6,3},{7,2},{8,13},{9,12},{10,... | collective-permute-start | bytes 589832 | tf_op jit(solution)/shard_map/ppermute | solution.py:221
  42.2 19.2 %collective-permute-start.23 = (bf16[48,2048]{1,0:T(8,128)(2,1)S(1)}, bf16[48,2048]{1,0:T(8,128)(2,1)S(1)}, u32[]{:S(2)}, u32[]{:S(2)}) collective-permute-start(bf16[48,2048]{1,0:T(8,128)(2,1)S(1)} %get-tuple-element.42), channel_id=1, source_target_pairs={{0,6},{1,7},{2,4},{3,5},{4,2},{5,3},{6,0},{7,1},{8,14},{9,15},{10,... | collective-permute-start | bytes 589832 | tf_op jit(solution)/shard_map/ppermute | solution.py:221
  46.3 16.4 %collective-permute-start.24 = (bf16[48,2048]{1,0:T(8,128)(2,1)S(1)}, bf16[48,2048]{1,0:T(8,128)(2,1)S(1)}, u32[]{:S(2)}, u32[]{:S(2)}) collective-permute-start(bf16[48,2048]{1,0:T(8,128)(2,1)S(1)} %get-tuple-element.41), channel_id=1, source_target_pairs={{0,7},{1,6},{2,5},{3,4},{4,3},{5,2},{6,1},{7,0},{8,15},{9,14},{10,... | collective-permute-start | bytes 589832 | tf_op jit(solution)/shard_map/ppermute | solution.py:221
  49.7 25.7 %collective-permute-start.13 = (bf16[64,1024]{1,0:T(8,128)(2,1)S(1)}, bf16[64,1024]{1,0:T(8,128)(2,1)S(1)}, u32[]{:S(2)}, u32[]{:S(2)}) collective-permute-start(bf16[64,1024]{1,0:T(8,128)(2,1)S(1)} %dynamic_slice.47), channel_id=1, source_target_pairs={{0,4},{4,0},{1,5},{5,1},{2,6},{6,2},{3,7},{7,3},{8,12},{12,8},{9,1... | collective-permute-start | bytes 393224 | tf_op jit(solution)/shard_map/ppermute | solution.py:38
  51.2 45.8 %collective-permute-start.42 = (bf16[512,512]{1,0:T(8,128)(2,1)}, bf16[512,512]{1,0:T(8,128)(2,1)}, u32[]{:S(2)}, u32[]{:S(2)}) collective-permute-start(bf16[512,512]{1,0:T(8,128)(2,1)} %get-tuple-element.22), channel_id=1, source_target_pairs={{0,4},{4,0},{1,5},{5,1},{2,6},{6,2},{3,7},{7,3},{8,12},{12,8},{9,1... | collective-permute-start | bytes 1572872 | tf_op jit(solution)/shard_map/ppermute | solution.py:38
  59.8 6.4 %collective-permute-start.15 = (bf16[32,2048]{1,0:T(8,128)(2,1)S(1)}, bf16[32,2048]{1,0:T(8,128)(2,1)S(1)}, u32[]{:S(2)}, u32[]{:S(2)}) collective-permute-start(bf16[32,2048]{1,0:T(8,128)(2,1)S(1)} %collective-permute-done.14), channel_id=1, source_target_pairs={{0,8},{8,16},{16,24},{24,0},{1,9},{9,17},{17,25},{25,1},{2,10},{10... | collective-permute-start | bytes 393224 | tf_op jit(solution)/shard_map/ppermute | solution.py:33
  61.4 12.1 %collective-permute-start.16 = (bf16[32,2048]{1,0:T(8,128)(2,1)S(1)}, bf16[32,2048]{1,0:T(8,128)(2,1)S(1)}, u32[]{:S(2)}, u32[]{:S(2)}) collective-permute-start(bf16[32,2048]{1,0:T(8,128)(2,1)S(1)} %collective-permute-done.14), channel_id=1, source_target_pairs={{0,16},{8,24},{16,0},{24,8},{1,17},{9,25},{17,1},{25,9},{2,18},{10... | collective-permute-start | bytes 393224 | tf_op jit(solution)/shard_map/ppermute | solution.py:33
  62.8 12.6 %collective-permute-start.17 = (bf16[32,2048]{1,0:T(8,128)(2,1)S(1)}, bf16[32,2048]{1,0:T(8,128)(2,1)S(1)}, u32[]{:S(2)}, u32[]{:S(2)}) collective-permute-start(bf16[32,2048]{1,0:T(8,128)(2,1)S(1)} %collective-permute-done.14), channel_id=1, source_target_pairs={{0,24},{8,0},{16,8},{24,16},{1,25},{9,1},{17,9},{25,17},{2,26},{10... | collective-permute-start | bytes 393224 | tf_op jit(solution)/shard_map/ppermute | solution.py:33
  77.4 6.4 %collective-permute-start.28 = (bf16[128,512]{1,0:T(8,128)(2,1)S(1)}, bf16[128,512]{1,0:T(8,128)(2,1)S(1)}, u32[]{:S(2)}, u32[]{:S(2)}) collective-permute-start(bf16[128,512]{1,0:T(8,128)(2,1)S(1)} %get-tuple-element.49), channel_id=1, source_target_pairs={{0,8},{8,16},{16,24},{24,0},{1,9},{9,17},{17,25},{25,1},{2,10},{10... | collective-permute-start | bytes 393224 | tf_op jit(solution)/shard_map/ppermute | solution.py:33
  77.5 11.7 %collective-permute-start.29 = (bf16[128,512]{1,0:T(8,128)(2,1)S(1)}, bf16[128,512]{1,0:T(8,128)(2,1)S(1)}, u32[]{:S(2)}, u32[]{:S(2)}) collective-permute-start(bf16[128,512]{1,0:T(8,128)(2,1)S(1)} %get-tuple-element.51), channel_id=1, source_target_pairs={{0,16},{8,24},{16,0},{24,8},{1,17},{9,25},{17,1},{25,9},{2,18},{10... | collective-permute-start | bytes 393224 | tf_op jit(solution)/shard_map/ppermute | solution.py:33
  79.2 11.9 %collective-permute-start.30 = (bf16[128,512]{1,0:T(8,128)(2,1)S(1)}, bf16[128,512]{1,0:T(8,128)(2,1)S(1)}, u32[]{:S(2)}, u32[]{:S(2)}) collective-permute-start(bf16[128,512]{1,0:T(8,128)(2,1)S(1)} %get-tuple-element.50), channel_id=1, source_target_pairs={{0,24},{8,0},{16,8},{24,16},{1,25},{9,1},{17,9},{25,17},{2,26},{10... | collective-permute-start | bytes 393224 | tf_op jit(solution)/shard_map/ppermute | solution.py:33
  93.6 6.7 %collective-permute-start.31 = (bf16[128,512]{1,0:T(8,128)(2,1)S(1)}, bf16[128,512]{1,0:T(8,128)(2,1)S(1)}, u32[]{:S(2)}, u32[]{:S(2)}) collective-permute-start(bf16[128,512]{1,0:T(8,128)(2,1)S(1)} %get-tuple-element.27), channel_id=1, source_target_pairs={{0,8},{8,16},{16,24},{24,0},{1,9},{9,17},{17,25},{25,1},{2,10},{10... | collective-permute-start | bytes 393224 | tf_op jit(solution)/shard_map/ppermute | solution.py:33
  94.9 26.3 %collective-permute-start.11 = (bf16[128,2048]{1,0:T(8,128)(2,1)S(1)}, bf16[128,2048]{1,0:T(8,128)(2,1)S(1)}, u32[]{:S(2)}, u32[]{:S(2)}) collective-permute-start(bf16[128,2048]{1,0:T(8,128)(2,1)S(1)} %copy-done.3), channel_id=1, source_target_pairs={{0,2},{1,3},{2,0},{3,1},{4,6},{5,7},{6,4},{7,5},{8,10},{9,11},{10,... | collective-permute-start | bytes 1572872 | tf_op jit(solution)/shard_map/ppermute | solution.py:38
  96.5 48.4 %collective-permute-start.10 = (bf16[128,2048]{1,0:T(8,128)(2,1)S(1)}, bf16[128,2048]{1,0:T(8,128)(2,1)}, u32[]{:S(2)}, u32[]{:S(2)}) collective-permute-start(bf16[128,2048]{1,0:T(8,128)(2,1)S(1)} %copy-done.3), channel_id=1, source_target_pairs={{0,1},{1,0},{2,3},{3,2},{4,5},{5,4},{6,7},{7,6},{8,9},{9,8},{10,11... | collective-permute-start | bytes 1572872 | tf_op jit(solution)/shard_map/ppermute | solution.py:38
  96.5 15.1 %collective-permute-start.38 = (bf16[64,1024]{1,0:T(8,128)(2,1)S(1)}, bf16[64,1024]{1,0:T(8,128)(2,1)S(1)}, u32[]{:S(2)}, u32[]{:S(2)}) collective-permute-start(bf16[64,1024]{1,0:T(8,128)(2,1)S(1)} %collective-permute-done.13), channel_id=1, source_target_pairs={{0,2},{1,3},{2,0},{3,1},{4,6},{5,7},{6,4},{7,5},{8,10},{9,11},{10,... | collective-permute-start | bytes 393224 | tf_op jit(solution)/shard_map/ppermute | solution.py:38
  97.0 10.2 %collective-permute-start.32 = (bf16[128,512]{1,0:T(8,128)(2,1)S(1)}, bf16[128,512]{1,0:T(8,128)(2,1)S(1)}, u32[]{:S(2)}, u32[]{:S(2)}) collective-permute-start(bf16[128,512]{1,0:T(8,128)(2,1)S(1)} %get-tuple-element.27), channel_id=1, source_target_pairs={{0,16},{8,24},{16,0},{24,8},{1,17},{9,25},{17,1},{25,9},{2,18},{10... | collective-permute-start | bytes 393224 | tf_op jit(solution)/shard_map/ppermute | solution.py:33
  100.3 12.8 %collective-permute-start.33 = (bf16[128,512]{1,0:T(8,128)(2,1)S(1)}, bf16[128,512]{1,0:T(8,128)(2,1)S(1)}, u32[]{:S(2)}, u32[]{:S(2)}) collective-permute-start(bf16[128,512]{1,0:T(8,128)(2,1)S(1)} %get-tuple-element.27), channel_id=1, source_target_pairs={{0,24},{8,0},{16,8},{24,16},{1,25},{9,1},{17,9},{25,17},{2,26},{10... | collective-permute-start | bytes 393224 | tf_op jit(solution)/shard_map/ppermute | solution.py:33
  107.2 9.2 %collective-permute-start.40 = (bf16[64,1024]{1,0:T(8,128)(2,1)S(1)}, bf16[64,1024]{1,0:T(8,128)(2,1)S(1)}, u32[]{:S(2)}, u32[]{:S(2)}) collective-permute-start(bf16[64,1024]{1,0:T(8,128)(2,1)S(1)} %collective-permute-done.13), channel_id=1, source_target_pairs={{0,1},{1,0},{2,3},{3,2},{4,5},{5,4},{6,7},{7,6},{8,9},{9,8},{10,11... | collective-permute-start | bytes 393224 | tf_op jit(solution)/shard_map/ppermute | solution.py:38
  111.6 13.1 %collective-permute-start.26 = (bf16[128,2048]{1,0:T(8,128)(2,1)S(1)}, bf16[128,2048]{1,0:T(8,128)(2,1)}, u32[]{:S(2)}, u32[]{:S(2)}) collective-permute-start(bf16[128,2048]{1,0:T(8,128)(2,1)S(1)} %constant_dynamic-update-slice_fusion.20.refs_4_), channel_id=1, source_target_pairs={{0,2},{1,3},{2,0},{3,1},{4,6},{5,7},{6,4},{7,5},{8,10},{9,11},{10,... | collective-permute-start | bytes 1572872 | tf_op jit(solution)/shard_map/ppermute | solution.py:38
  113.1 5.1 %collective-permute-start.39 = (bf16[64,1024]{1,0:T(8,128)(2,1)S(1)}, bf16[64,1024]{1,0:T(8,128)(2,1)S(1)}, u32[]{:S(2)}, u32[]{:S(2)}) collective-permute-start(bf16[64,1024]{1,0:T(8,128)(2,1)S(1)} %collective-permute-done.38), channel_id=1, source_target_pairs={{0,1},{1,0},{2,3},{3,2},{4,5},{5,4},{6,7},{7,6},{8,9},{9,8},{10,11... | collective-permute-start | bytes 393224 | tf_op jit(solution)/shard_map/ppermute | solution.py:38
  116.4 22.0 %collective-permute-start.43 = (bf16[512,512]{1,0:T(8,128)(2,1)}, bf16[512,512]{1,0:T(8,128)(2,1)}, u32[]{:S(2)}, u32[]{:S(2)}) collective-permute-start(bf16[512,512]{1,0:T(8,128)(2,1)} %get-tuple-element.23), channel_id=1, source_target_pairs={{0,4},{4,0},{1,5},{5,1},{2,6},{6,2},{3,7},{7,3},{8,12},{12,8},{9,1... | collective-permute-start | bytes 1572872 | tf_op jit(solution)/shard_map/ppermute | solution.py:38
  118.7 17.9 %copy-start.14 = (f32[256,512]{1,0:T(8,128)S(1)}, f32[256,512]{1,0:T(8,128)}, u32[]{:S(2)}) copy-start(f32[256,512]{1,0:T(8,128)} %fusion.53) | copy-start | bytes 1572868
  118.7 17.9 %collective-permute-start.41 = (bf16[256,512]{1,0:T(8,128)(2,1)S(1)}, bf16[256,512]{1,0:T(8,128)(2,1)S(1)}, u32[]{:S(2)}, u32[]{:S(2)}) collective-permute-start(bf16[256,512]{1,0:T(8,128)(2,1)S(1)} %convolution_convert_fusion), channel_id=1, source_target_pairs={{0,4},{4,0},{1,5},{5,1},{2,6},{6,2},{3,7},{7,3},{8,12},{12,8},{9,1... | collective-permute-start | bytes 786440 | tf_op jit(solution)/shard_map/ppermute | solution.py:38
  121.2 23.9 %collective-permute-start.25 = (bf16[128,2048]{1,0:T(8,128)(2,1)S(1)}, bf16[128,2048]{1,0:T(8,128)(2,1)S(1)}, u32[]{:S(2)}, u32[]{:S(2)}) collective-permute-start(bf16[128,2048]{1,0:T(8,128)(2,1)S(1)} %constant_dynamic-update-slice_fusion.20.refs_4_), channel_id=1, source_target_pairs={{0,1},{1,0},{2,3},{3,2},{4,5},{5,4},{6,7},{7,6},{8,9},{9,8},{10,11... | collective-permute-start | bytes 1572872 | tf_op jit(solution)/shard_map/ppermute | solution.py:38
  124.7 21.3 %collective-permute-start.12 = (bf16[128,2048]{1,0:T(8,128)(2,1)S(1)}, bf16[128,2048]{1,0:T(8,128)(2,1)S(1)}, u32[]{:S(2)}, u32[]{:S(2)}) collective-permute-start(bf16[128,2048]{1,0:T(8,128)(2,1)S(1)} %collective-permute-done.11.refs_2_), channel_id=1, source_target_pairs={{0,1},{1,0},{2,3},{3,2},{4,5},{5,4},{6,7},{7,6},{8,9},{9,8},{10,11... | collective-permute-start | bytes 1572872 | tf_op jit(solution)/shard_map/ppermute | solution.py:38
  136.6 10.1 %collective-permute-start.27 = (bf16[128,2048]{1,0:T(8,128)(2,1)}, bf16[128,2048]{1,0:T(8,128)(2,1)S(1)}, u32[]{:S(2)}, u32[]{:S(2)}) collective-permute-start(bf16[128,2048]{1,0:T(8,128)(2,1)} %collective-permute-done.26.refs_6_), channel_id=1, source_target_pairs={{0,1},{1,0},{2,3},{3,2},{4,5},{5,4},{6,7},{7,6},{8,9},{9,8},{10,11... | collective-permute-start | bytes 1572872 | tf_op jit(solution)/shard_map/ppermute | solution.py:38
  138.4 26.7 %collective-permute-start.37 = (bf16[1024,512]{1,0:T(8,128)(2,1)}, bf16[1024,512]{1,0:T(8,128)(2,1)}, u32[]{:S(2)}, u32[]{:S(2)}) collective-permute-start(bf16[1024,512]{1,0:T(8,128)(2,1)} %bitcast.91), channel_id=1, source_target_pairs={{0,4},{4,0},{1,5},{5,1},{2,6},{6,2},{3,7},{7,3},{8,12},{12,8},{9,1... | collective-permute-start | bytes 3145736 | tf_op jit(solution)/shard_map/ppermute | solution.py:38
  144.8 42.1 %collective-permute-start.44 = (bf16[512,1024]{1,0:T(8,128)(2,1)}, bf16[512,1024]{1,0:T(8,128)(2,1)}, u32[]{:S(2)}, u32[]{:S(2)}) collective-permute-start(bf16[512,1024]{1,0:T(8,128)(2,1)} %bitcast.9), channel_id=1, source_target_pairs={{0,4},{4,0},{1,5},{5,1},{2,6},{6,2},{3,7},{7,3},{8,12},{12,8},{9,1... | collective-permute-start | bytes 3145736 | tf_op jit(solution)/shard_map/ppermute | solution.py:38
  160.9 27.6 %collective-permute-start.47 = (bf16[384,512]{1,0:T(8,128)(2,1)S(1)}, bf16[384,512]{1,0:T(8,128)(2,1)S(1)}, u32[]{:S(2)}, u32[]{:S(2)}) collective-permute-start(bf16[384,512]{1,0:T(8,128)(2,1)S(1)} %get-tuple-element.38), channel_id=1, source_target_pairs={{0,8},{8,16},{16,24},{24,0},{1,9},{9,17},{17,25},{25,1},{2,10},{10... | collective-permute-start | bytes 1179656 | tf_op jit(solution)/shard_map/ppermute | solution.py:33
  162.2 33.8 %collective-permute-start.48 = (bf16[384,512]{1,0:T(8,128)(2,1)S(1)}, bf16[384,512]{1,0:T(8,128)(2,1)S(1)}, u32[]{:S(2)}, u32[]{:S(2)}) collective-permute-start(bf16[384,512]{1,0:T(8,128)(2,1)S(1)} %get-tuple-element.40), channel_id=1, source_target_pairs={{0,16},{8,24},{16,0},{24,8},{1,17},{9,25},{17,1},{25,9},{2,18},{10... | collective-permute-start | bytes 1179656 | tf_op jit(solution)/shard_map/ppermute | solution.py:33
  165.1 33.5 %collective-permute-start.49 = (bf16[384,512]{1,0:T(8,128)(2,1)S(1)}, bf16[384,512]{1,0:T(8,128)(2,1)S(1)}, u32[]{:S(2)}, u32[]{:S(2)}) collective-permute-start(bf16[384,512]{1,0:T(8,128)(2,1)S(1)} %get-tuple-element.39), channel_id=1, source_target_pairs={{0,24},{8,0},{16,8},{24,16},{1,25},{9,1},{17,9},{25,17},{2,26},{10... | collective-permute-start | bytes 1179656 | tf_op jit(solution)/shard_map/ppermute | solution.py:33
  165.1 33.7 %collective-permute-start.34 = (bf16[128,2048]{1,0:T(8,128)(2,1)S(1)}, bf16[128,2048]{1,0:T(8,128)(2,1)}, u32[]{:S(2)}, u32[]{:S(2)}) collective-permute-start(bf16[128,2048]{1,0:T(8,128)(2,1)S(1)} %copy-done.15), channel_id=1, source_target_pairs={{0,2},{1,3},{2,0},{3,1},{4,6},{5,7},{6,4},{7,5},{8,10},{9,11},{10,... | collective-permute-start | bytes 1572872 | tf_op jit(solution)/shard_map/ppermute | solution.py:38
  186.9 23.2 %collective-permute-start.36 = (bf16[128,2048]{1,0:T(8,128)(2,1)S(1)}, bf16[128,2048]{1,0:T(8,128)(2,1)}, u32[]{:S(2)}, u32[]{:S(2)}) collective-permute-start(bf16[128,2048]{1,0:T(8,128)(2,1)S(1)} %copy-done.15), channel_id=1, source_target_pairs={{0,1},{1,0},{2,3},{3,2},{4,5},{5,4},{6,7},{7,6},{8,9},{9,8},{10,11... | collective-permute-start | bytes 1572872 | tf_op jit(solution)/shard_map/ppermute | solution.py:38
  198.9 12.5 %collective-permute-start.35 = (bf16[128,2048]{1,0:T(8,128)(2,1)}, bf16[128,2048]{1,0:T(8,128)(2,1)S(1)}, u32[]{:S(2)}, u32[]{:S(2)}) collective-permute-start(bf16[128,2048]{1,0:T(8,128)(2,1)} %collective-permute-done.34), channel_id=1, source_target_pairs={{0,1},{1,0},{2,3},{3,2},{4,5},{5,4},{6,7},{7,6},{8,9},{9,8},{10,11... | collective-permute-start | bytes 1572872 | tf_op jit(solution)/shard_map/ppermute | solution.py:38
  199.6 7.3 %collective-permute-start.50 = (bf16[48,512]{1,0:T(8,128)(2,1)S(1)}, bf16[48,512]{1,0:T(8,128)(2,1)S(1)}, u32[]{:S(2)}, u32[]{:S(2)}) collective-permute-start(bf16[48,512]{1,0:T(8,128)(2,1)S(1)} %get-tuple-element.64), channel_id=1, source_target_pairs={{0,1},{1,0},{2,3},{3,2},{4,5},{5,4},{6,7},{7,6},{8,9},{9,8},{10,11... | collective-permute-start | bytes 147464 | tf_op jit(solution)/shard_map/ppermute | solution.py:221
  205.6 4.5 %collective-permute-start.51 = (bf16[48,512]{1,0:T(8,128)(2,1)S(1)}, bf16[48,512]{1,0:T(8,128)(2,1)S(1)}, u32[]{:S(2)}, u32[]{:S(2)}) collective-permute-start(bf16[48,512]{1,0:T(8,128)(2,1)S(1)} %get-tuple-element.63), channel_id=1, source_target_pairs={{0,2},{1,3},{2,0},{3,1},{4,6},{5,7},{6,4},{7,5},{8,10},{9,11},{10,... | collective-permute-start | bytes 147464 | tf_op jit(solution)/shard_map/ppermute | solution.py:221
  206.1 24.2 %collective-permute-start.52 = (bf16[48,512]{1,0:T(8,128)(2,1)}, bf16[48,512]{1,0:T(8,128)(2,1)}, u32[]{:S(2)}, u32[]{:S(2)}) collective-permute-start(bf16[48,512]{1,0:T(8,128)(2,1)} %get-tuple-element.62), channel_id=1, source_target_pairs={{0,3},{1,2},{2,1},{3,0},{4,7},{5,6},{6,5},{7,4},{8,11},{9,10},{10,... | collective-permute-start | bytes 147464 | tf_op jit(solution)/shard_map/ppermute | solution.py:221
  206.9 24.3 %collective-permute-start.53 = (bf16[48,512]{1,0:T(8,128)(2,1)S(1)}, bf16[48,512]{1,0:T(8,128)(2,1)}, u32[]{:S(2)}, u32[]{:S(2)}) collective-permute-start(bf16[48,512]{1,0:T(8,128)(2,1)S(1)} %get-tuple-element.61), channel_id=1, source_target_pairs={{0,4},{1,5},{2,6},{3,7},{4,0},{5,1},{6,2},{7,3},{8,12},{9,13},{10,... | collective-permute-start | bytes 147464 | tf_op jit(solution)/shard_map/ppermute | solution.py:221
  210.0 22.0 %collective-permute-start.54 = (bf16[48,512]{1,0:T(8,128)(2,1)S(1)}, bf16[48,512]{1,0:T(8,128)(2,1)}, u32[]{:S(2)}, u32[]{:S(2)}) collective-permute-start(bf16[48,512]{1,0:T(8,128)(2,1)S(1)} %get-tuple-element.60), channel_id=1, source_target_pairs={{0,5},{1,4},{2,7},{3,6},{4,1},{5,0},{6,3},{7,2},{8,13},{9,12},{10,... | collective-permute-start | bytes 147464 | tf_op jit(solution)/shard_map/ppermute | solution.py:221
  210.1 22.8 %collective-permute-start.55 = (bf16[48,512]{1,0:T(8,128)(2,1)S(1)}, bf16[48,512]{1,0:T(8,128)(2,1)}, u32[]{:S(2)}, u32[]{:S(2)}) collective-permute-start(bf16[48,512]{1,0:T(8,128)(2,1)S(1)} %get-tuple-element.59), channel_id=1, source_target_pairs={{0,6},{1,7},{2,4},{3,5},{4,2},{5,3},{6,0},{7,1},{8,14},{9,15},{10,... | collective-permute-start | bytes 147464 | tf_op jit(solution)/shard_map/ppermute | solution.py:221
  211.4 22.3 %collective-permute-start.56 = (bf16[48,512]{1,0:T(8,128)(2,1)S(1)}, bf16[48,512]{1,0:T(8,128)(2,1)}, u32[]{:S(2)}, u32[]{:S(2)}) collective-permute-start(bf16[48,512]{1,0:T(8,128)(2,1)S(1)} %get-tuple-element.58), channel_id=1, source_target_pairs={{0,7},{1,6},{2,5},{3,4},{4,3},{5,2},{6,1},{7,0},{8,15},{9,14},{10,... | collective-permute-start | bytes 147464 | tf_op jit(solution)/shard_map/ppermute | solution.py:221
  230.3 4.1 %collective-permute-start.45 = (bf16[256,2,512]{2,0,1:T(8,128)(2,1)S(1)}, bf16[256,2,512]{2,0,1:T(8,128)(2,1)S(1)}, u32[]{:S(2)}, u32[]{:S(2)}) collective-permute-start(bf16[256,2,512]{2,0,1:T(8,128)(2,1)S(1)} %fusion.63), channel_id=1, source_target_pairs={{0,1},{1,0},{2,3},{3,2},{4,5},{5,4},{6,7},{7,6},{8,9},{9,8},{10,11... | collective-permute-start | bytes 1572872 | tf_op jit(solution)/shard_map/ppermute | solution.py:38
  234.4 10.8 %copy-start.1 = (bf16[1,1024,512]{2,1,0:T(8,128)(2,1)S(1)}, bf16[1,1024,512]{2,1,0:T(8,128)(2,1)}, u32[]{:S(2)}) copy-start(bf16[1,1024,512]{2,1,0:T(8,128)(2,1)} %param.26) | copy-start | bytes 3145732
  234.6 8.8 %copy-start.32 = (pred[256]{0:T(512)(128)(4,1)S(1)}, pred[256]{0:T(512)(128)(4,1)}, u32[]{:S(2)}) copy-start(pred[256]{0:T(512)(128)(4,1)} %compare_bitcast_fusion) | copy-start | bytes 772
  234.7 8.8 %collective-permute-start.46 = (bf16[256,1,512]{2,0,1:T(8,128)(2,1)S(1)}, bf16[256,1,512]{2,0,1:T(8,128)(2,1)S(1)}, u32[]{:S(2)}, u32[]{:S(2)}) collective-permute-start(bf16[256,1,512]{2,0,1:T(8,128)(2,1)S(1)} %dynamic-slice_convert_fusion.1), channel_id=1, source_target_pairs={{0,2},{1,3},{2,0},{3,1},{4,6},{5,7},{6,4},{7,5},{8,10},{9,11},{10,... | collective-permute-start | bytes 786440 | tf_op jit(solution)/shard_map/ppermute | solution.py:38
  (30 other events, 71.3 us)

commit v3 on v1

--- a/solution.py
+++ b/solution.py
@@ -1,6 +1,10 @@
+import functools
+
 import jax
 import jax.numpy as jnp
 from jax import lax
+from jax.experimental import pallas as pl
+from jax.experimental.pallas import tpu as pltpu
 from jax.sharding import PartitionSpec as P
 
 HEAD_DIM = 128
@@ -137,6 +141,428 @@
     sent = values.reshape(group_size, capacity, values.shape[1])
     arrived = lax.all_to_all(sent, ("expert", "dp"), split_axis=0, concat_axis=0, tiled=True)
     return arrived.reshape(values.shape)
+
+
+def gate(value, *after):
+    return lax.optimization_barrier((value,) + after)[0]
+
+
+def vmem(shape, dtype):
+    return pltpu.VMEM(shape, dtype)
+
+
+def dispatch_kernel(capacity, count, code_ref, *refs):
+    blocks, held, sems = refs[:count], refs[count + 2], refs[count + 3]
+    copies = [
+        pltpu.make_async_copy(block, held.at[place], sems.at[place])
+        for place, block in enumerate(blocks)
+    ]
+    for copy in copies:
+        copy.start()
+    for place, copy in enumerate(copies):
+        copy.wait()
+        for which, out_ref in enumerate(refs[count : count + 2]):
+            line = which * count + place
+            code = code_ref[line : line + 1, :]
+            slot = lax.broadcasted_iota(jnp.int32, (capacity, code.shape[1]), 0)
+            pick = jnp.where(slot == code, 1.0, 0.0).astype(jnp.bfloat16)
+            rows = jnp.dot(pick, held[place], preferred_element_type=jnp.float32)
+            out_ref[place * capacity : (place + 1) * capacity, :] = rows.astype(jnp.bfloat16)
+
+
+def dispatch(code, blocks, capacity):
+    rows, features = blocks[0].shape
+    count = len(blocks)
+    picked = jax.ShapeDtypeStruct((count * capacity, features), jnp.bfloat16)
+    return pl.pallas_call(
+        functools.partial(dispatch_kernel, capacity, count),
+        out_shape=(picked, picked),
+        in_specs=[pl.BlockSpec(memory_space=pltpu.VMEM)]
+        + [pl.BlockSpec(memory_space=pl.ANY)] * count,
+        out_specs=[pl.BlockSpec(memory_space=pltpu.VMEM)] * 2,
+        scratch_shapes=[
+            vmem((count, rows, features), jnp.bfloat16),
+            pltpu.SemaphoreType.DMA((count,)),
+        ],
+        compiler_params=pltpu.CompilerParams(vmem_limit_bytes=32 * 1024 * 1024),
+        cost_estimate=pl.CostEstimate(
+            flops=4 * count * capacity * rows * features,
+            bytes_accessed=2 * count * (rows + 2 * capacity) * features,
+            transcendentals=0,
+        ),
+        name="dispatch",
+    )(code, *blocks)
+
+
+def send_home(part, codes, capacity):
+    size = lax.axis_size(("expert", "dp"))
+    arrived = []
+    for place, code in enumerate(codes):
+        block = part[place * capacity : (place + 1) * capacity]
+        if code:
+            block = lax.ppermute(block, ("expert", "dp"), [(i, i ^ code) for i in range(size)])
+        arrived.append(block)
+    return arrived
+
+
+def combine_kernel(count, split, section_ref, position_ref, gates_ref, *refs):
+    blocks = refs[:count]
+    outs = refs[count : count + split]
+    held, total, sems = refs[count + split :]
+    capacity, features = blocks[0].shape
+    copies = [
+        pltpu.make_async_copy(block, held.at[pl.ds(i * capacity, capacity)], sems.at[i])
+        for i, block in enumerate(blocks)
+    ]
+    for copy in copies:
+        copy.start()
+    position = position_ref[...]
+    slot = lax.broadcasted_iota(jnp.int32, (position.shape[0], count * capacity), 1)
+    picks = [
+        jnp.where(position[:, k : k + 1] == slot, 1.0, 0.0).astype(jnp.bfloat16) for k in range(2)
+    ]
+    for copy in copies:
+        copy.wait()
+    first = jnp.dot(picks[0], held[...], preferred_element_type=jnp.float32)
+    second = jnp.dot(picks[1], held[...], preferred_element_type=jnp.float32)
+    total[...] = gates_ref[:, 0:1] * first + gates_ref[:, 1:2] * second
+    width = features // split
+    for step, out_ref in enumerate(outs):
+        owner = lax.rem(section_ref[0] + step, split)
+        start = pl.multiple_of(owner * width, width)
+        out_ref[...] = total[:, pl.ds(start, width)].astype(out_ref.dtype)
+
+
+def combine(section, position, gates, blocks, split, kept):
+    capacity, features = blocks[0].shape
+    rows = position.shape[0]
+    count = len(blocks)
+    width = features // split
+    types = [kept] + [jnp.bfloat16] * (split - 1)
+    full = pl.BlockSpec(memory_space=pltpu.VMEM)
+    return pl.pallas_call(
+        functools.partial(combine_kernel, count, split),
+        out_shape=tuple(jax.ShapeDtypeStruct((rows, width), kind) for kind in types),
+        in_specs=[pl.BlockSpec(memory_space=pltpu.SMEM), full, full]
+        + [pl.BlockSpec(memory_space=pl.ANY)] * count,
+        out_specs=[full] * split,
+        scratch_shapes=[
+            vmem((count * capacity, features), jnp.bfloat16),
+            vmem((rows, features), jnp.float32),
+            pltpu.SemaphoreType.DMA((count,)),
+        ],
+        compiler_params=pltpu.CompilerParams(vmem_limit_bytes=32 * 1024 * 1024),
+        cost_estimate=pl.CostEstimate(
+            flops=4 * rows * count * capacity * features,
+            bytes_accessed=2 * count * capacity * features,
+            transcendentals=0,
+        ),
+        name="combine",
+    )(section, position, gates, *blocks)
+
+
+def memory_kernel(count, section_ref, tokens_ref, gain_ref, *refs):
+    slices, out_ref, mixed = refs[:count], refs[count], refs[count + 1]
+    me = section_ref[0]
+    width = slices[0].shape[1]
+    for step, piece in enumerate(slices):
+        owner = lax.rem(me - step + count, count)
+        mixed[:, pl.ds(pl.multiple_of(owner * width, width), width)] = piece[...].astype(
+            jnp.float32
+        )
+    values = tokens_ref[...].astype(jnp.float32) + mixed[...]
+    out_ref[...] = normalize(values, gain_ref[...]).astype(jnp.bfloat16)
+
+
+def make_memory(tokens, slices, gain):
+    me = lax.axis_index("section").astype(jnp.int32).reshape(1)
+    return pl.pallas_call(
+        functools.partial(memory_kernel, len(slices)),
+        out_shape=jax.ShapeDtypeStruct(tokens.shape, jnp.bfloat16),
+        in_specs=[pl.BlockSpec(memory_space=pltpu.SMEM)]
+        + [pl.BlockSpec(memory_space=pltpu.VMEM)] * (2 + len(slices)),
+        out_specs=pl.BlockSpec(memory_space=pltpu.VMEM),
+        scratch_shapes=[vmem(tokens.shape, jnp.float32)],
+        compiler_params=pltpu.CompilerParams(vmem_limit_bytes=20 * 1024 * 1024),
+        name="memory",
+    )(me, tokens, gain[None], *slices)
+
+
+def attend_kernel(
+    place_ref,
+    lengths_ref,
+    query_ref,
+    near_ref,
+    far_ref,
+    key_own,
+    key_other,
+    value_own,
+    value_other,
+    out_ref,
+    source,
+    key_weight,
+    value_weight,
+    keys,
+    values,
+    sems,
+):
+    y, core, sentence = place_ref[0], place_ref[1], place_ref[2]
+    rows = near_ref.shape[0]
+    depth = key_own.shape[0]
+    moves = (
+        (near_ref, source.at[pl.ds(0, rows)]),
+        (far_ref, source.at[pl.ds(rows, rows)]),
+        (key_own, key_weight.at[y]),
+        (key_other, key_weight.at[1 - y]),
+        (value_own, value_weight.at[y]),
+        (value_other, value_weight.at[1 - y]),
+    )
+    copies = [
+        pltpu.make_async_copy(here, there, sems.at[i]) for i, (here, there) in enumerate(moves)
+    ]
+    for copy in copies:
+        copy.start()
+
+    def project(weight, result):
+        total = jnp.dot(source[:, :depth], weight[0], preferred_element_type=jnp.float32)
+        total += jnp.dot(source[:, depth:], weight[1], preferred_element_type=jnp.float32)
+        result[...] = total.astype(jnp.bfloat16)
+
+    for copy in copies[:4]:
+        copy.wait()
+    project(key_weight, keys)
+    for copy in copies[4:]:
+        copy.wait()
+    project(value_weight, values)
+
+    column = lax.broadcasted_iota(jnp.int32, (query_ref.shape[0], 2 * rows), 1)
+    position = jnp.where(column < rows, column + core * rows, column - core * rows)
+    valid = position < lengths_ref[sentence]
+    for head in range(query_ref.shape[1] // HEAD_DIM):
+        span = slice(head * HEAD_DIM, (head + 1) * HEAD_DIM)
+        scores = contract_last(query_ref[:, span], keys[:, span]) * HEAD_DIM ** (-0.5)
+        scores = jnp.where(valid, scores, -1e30)
+        weights = jnp.exp(scores - jnp.max(scores, axis=-1, keepdims=True))
+        probs = (weights / jnp.sum(weights, axis=-1, keepdims=True)).astype(jnp.bfloat16)
+        context = jnp.dot(probs, values[:, span], preferred_element_type=jnp.float32)
+        out_ref[:, span] = context.astype(jnp.bfloat16)
+
+
+def attend_sentence(place, lengths, query, near, far, key_pair, value_pair):
+    rows, features = near.shape
+    depth, width = key_pair[0].shape
+    hold = pl.BlockSpec(memory_space=pl.ANY)
+    smem = pl.BlockSpec(memory_space=pltpu.SMEM)
+    full = pl.BlockSpec(memory_space=pltpu.VMEM)
+    return pl.pallas_call(
+        attend_kernel,
+        out_shape=jax.ShapeDtypeStruct(query.shape, jnp.bfloat16),
+        in_specs=[smem, smem, full] + [hold] * 6,
+        out_specs=full,
+        scratch_shapes=[
+            vmem((2 * rows, features), jnp.bfloat16),
+            vmem((2, depth, width), jnp.bfloat16),
+            vmem((2, depth, width), jnp.bfloat16),
+            vmem((2 * rows, width), jnp.bfloat16),
+            vmem((2 * rows, width), jnp.bfloat16),
+            pltpu.SemaphoreType.DMA((6,)),
+        ],
+        compiler_params=pltpu.CompilerParams(vmem_limit_bytes=32 * 1024 * 1024),
+        cost_estimate=pl.CostEstimate(
+            flops=8 * rows * features * width,
+            bytes_accessed=4 * rows * features + 8 * depth * width,
+            transcendentals=query.shape[0] * 8 * rows,
+        ),
+        name="attend_sentence",
+    )(place, lengths, query, near, far, *key_pair, *value_pair)
+
+
+def small_body(
+    tokens,
+    expert_ids,
+    gate_weights,
+    out_grad,
+    inner_weight,
+    outer_weight,
+    final_gain,
+    dec_states,
+    src_lengths,
+    tgt_lengths,
+    norm_gain,
+    query_weight,
+    key_weight,
+    value_weight,
+    out_weight,
+):
+    token_count, feature_count = tokens.shape
+    group_size = lax.axis_size(("expert", "dp"))
+    capacity = 3 * token_count // group_size
+    here = lax.axis_index(("expert", "dp"))
+    y = lax.axis_index("expert")
+    d = lax.axis_index("dp")
+    section = lax.axis_index("section")
+    sections = lax.axis_size("section")
+    half = feature_count // 2
+    weight_in = inner_weight[0]
+    weight_out = outer_weight[0]
+    key_own, value_own, out_own = key_weight[0], value_weight[0], out_weight[0]
+    query_own = query_weight[0]
+
+    size = group_size
+    near_codes = (0, 2, 4, 6)
+    core_codes = (1, 3, 5, 7)
+
+    token_y = swap(tokens, "expert", 1)
+    token_x = swap(tokens, "dp", 2)
+    all_ids = lax.all_gather(expert_ids.T, ("expert", "dp"), axis=0)
+    token_far = swap(token_y, "dp", 2)
+
+    share = token_count // sections
+    grad_share = lax.dynamic_slice_in_dim(out_grad, section * share, share, 0)
+    grad_fetched = swap(gate(grad_share, token_y), "expert", 1)
+    key_other = swap(gate(key_own, token_y), "expert", 1)
+    grad_y = lax.all_gather(grad_fetched, "section", axis=0, tiled=True)
+    grad_x = swap(gate(out_grad, token_far), "dp", 2)
+
+    row = lax.broadcasted_iota(jnp.int32, (token_count, token_count), 0)
+    column = lax.broadcasted_iota(jnp.int32, (token_count, token_count), 1)
+    ids = jnp.stack(
+        [lax.dynamic_index_in_dim(all_ids, here ^ code, 0, False) for code in near_codes]
+    )
+    named_there = jnp.concatenate([(ids == here).any(axis=1), (ids == (here ^ 1)).any(axis=1)])
+    before = jnp.dot(
+        named_there.astype(jnp.bfloat16),
+        (row < column).astype(jnp.bfloat16),
+        preferred_element_type=jnp.float32,
+    ).astype(jnp.int32)
+    code = jnp.where(named_there, before, -1)
+
+    named = expert_ids[:, :, None] == jnp.arange(size, dtype=jnp.int32)[None, None, :]
+    either = (named[:, 0] | named[:, 1]).astype(jnp.bfloat16)
+    earlier = jnp.dot(
+        (column < row).astype(jnp.bfloat16), either, preferred_element_type=jnp.float32
+    ).astype(jnp.int32)
+    rank = jnp.sum(jnp.where(named, earlier[:, None, :], 0), axis=2)
+    codes_of = expert_ids ^ here
+    position = ((codes_of >> 1) + 4 * (codes_of & 1)) * capacity + rank
+
+    def forward(rows):
+        pre_act = jnp.dot(rows, weight_in, preferred_element_type=jnp.float32)
+        hidden = jax.nn.gelu(pre_act).astype(jnp.bfloat16)
+        part = jnp.dot(hidden, weight_out, preferred_element_type=jnp.float32)
+        return pre_act, part.astype(jnp.bfloat16)
+
+    def backward(grads, pre_act):
+        back = contract_last(grads, weight_out)
+        slope = jax.vjp(jax.nn.gelu, pre_act)[1](back)[0].astype(jnp.bfloat16)
+        return contract_last(slope, weight_in).astype(jnp.bfloat16)
+
+    rows_own, rows_sent = dispatch(code, [tokens, token_x, token_y, token_far], capacity)
+    rows_core = swap(rows_sent, "dp", 1)
+    pre_own, part_own = forward(rows_own)
+    pre_core, part_core = forward(rows_core)
+    part_core = gate(part_core, key_other, grad_x)
+    home = send_home(part_own, near_codes, capacity) + send_home(part_core, core_codes, capacity)
+
+    which_section = section.astype(jnp.int32).reshape(1)
+    cuts = combine(which_section, position, gate_weights, home, sections, jnp.float32)
+    mixed_sum = cuts[0]
+    for step in range(1, sections):
+        mixed_sum = mixed_sum + shift(cuts[step], "section", step).astype(jnp.float32)
+    mixed_slice = mixed_sum.astype(jnp.bfloat16)
+    slices = [mixed_slice] + [shift(mixed_slice, "section", step) for step in range(1, sections)]
+
+    value_other = swap(gate(value_own, *home), "expert", 1)
+    grad_far = swap(gate(grad_y, *home), "dp", 2)
+    states = dec_states[0]
+    normed = normalize(states.astype(jnp.float32), norm_gain[0]).astype(jnp.bfloat16)
+    quarter = normed.shape[0] // lax.axis_size("dp")
+    asked = lax.dynamic_slice(normed, (d * quarter, (1 - y) * half), (quarter, half))
+    asked_here = swap(gate(asked, *home), "expert", 1)
+    asked_rows = lax.all_gather(asked_here, "dp", axis=0, tiled=True)
+    query_there = jnp.dot(asked_rows, query_own, preferred_element_type=jnp.float32)
+    query_other = swap(query_there.astype(jnp.bfloat16), "expert", 1)
+    out_other = swap(gate(out_own, value_other), "expert", 1)
+    normed_own = lax.dynamic_slice_in_dim(normed, y * half, half, 1)
+    query = (
+        jnp.dot(normed_own, query_own, preferred_element_type=jnp.float32)
+        + query_other.astype(jnp.float32)
+    ).astype(jnp.bfloat16)
+
+    grads_own, grads_sent = dispatch(
+        gate(code, mixed_slice), [out_grad, grad_x, grad_y, grad_far], capacity
+    )
+    grads_core = swap(grads_sent, "dp", 1)
+    backward_own = backward(grads_own, pre_own)
+    backward_core = backward(grads_core, pre_core)
+    held_tokens = gate(tokens, value_other, backward_own, backward_core)
+    memory = make_memory(held_tokens, slices, final_gain)
+
+    core, x = d % 2, d // 2
+    memory_x = swap(memory, "dp", 2)
+    memory_core = swap(memory, "dp", 1)
+    memory_far = swap(memory_x, "dp", 1)
+
+    def sentence(which, near, far):
+        place = jnp.stack([y, core, which]).astype(jnp.int32)
+        rows_of = lax.dynamic_slice_in_dim(query, which * TGT_LEN, TGT_LEN, 0)
+        return attend_sentence(
+            place, src_lengths, rows_of, near, far, (key_own, key_other), (value_own, value_other)
+        )
+
+    context_own = sentence(x, memory, memory_core)
+    context_other = sentence(1 - x, gate(memory_x, out_other), memory_far)
+
+    backward_part = jnp.concatenate([backward_own, backward_core], axis=0)
+    backward_part = gate(backward_part, context_own)
+    width = half * 2 // sections
+
+    def piece(owner):
+        return lax.dynamic_slice_in_dim(backward_part, owner * width, width, 1)
+
+    arrived = [
+        shift(piece(lax.rem(section + step, sections)), "section", step)
+        for step in range(1, sections)
+    ]
+    backward_sum = gate(piece(section), context_other).astype(jnp.float32)
+    for part in arrived:
+        backward_sum = backward_sum + part.astype(jnp.float32)
+    backward_slice = backward_sum.astype(jnp.bfloat16)
+    grads_home = send_home(backward_slice, near_codes + core_codes, capacity)
+    (token_grad,) = combine(which_section, position, gate_weights, grads_home, 1, jnp.bfloat16)
+
+    context = jnp.concatenate(
+        [jnp.where(x == 0, context_own, context_other), jnp.where(x == 0, context_other, context_own)],
+        axis=0,
+    )
+    columns = feature_count // lax.axis_size("dp")
+
+    def project(weight, which):
+        part = lax.dynamic_slice_in_dim(weight, which * columns, columns, 1)
+        return jnp.dot(context, part, preferred_element_type=jnp.float32)
+
+    def by_x(which):
+        own, other = project(out_own, which), project(out_other, which)
+        first = y == 0
+        return jnp.stack([jnp.where(first, own, other), jnp.where(first, other, own)])
+
+    sent = by_x(1 - core).astype(jnp.bfloat16)
+    total = by_x(core) + swap(sent, "dp", 1).astype(jnp.float32)
+    last = lax.dynamic_index_in_dim(total, 1 - x, 0, False).astype(jnp.bfloat16)
+    attended = lax.dynamic_index_in_dim(total, x, 0, False) + swap(last, "dp", 2).astype(
+        jnp.float32
+    )
+    dec_out = add_residual(attended, states, tgt_lengths)
+    return (dec_out[None], token_grad)
+
+
+def add_residual(attended, states, tgt_lengths):
+    my_columns = attended.shape[1]
+    residual = lax.dynamic_slice_in_dim(
+        states, lax.axis_index("dp") * my_columns, my_columns, 1
+    ).astype(jnp.float32)
+    row_mask = (jnp.arange(TGT_LEN, dtype=jnp.int32)[None, :] < tgt_lengths[:, None]).reshape(-1, 1)
+    return (residual + jnp.where(row_mask, attended, 0.0)).astype(jnp.bfloat16)
 
 
 def body(
@@ -219,12 +645,7 @@
         key_mask,
     )
     attended = sum_heads(jnp.dot(context, full_out, preferred_element_type=jnp.float32))
-    my_columns = attended.shape[1]
-    residual = lax.dynamic_slice_in_dim(
-        states, lax.axis_index("dp") * my_columns, my_columns, 1
-    ).astype(jnp.float32)
-    row_mask = (jnp.arange(TGT_LEN, dtype=jnp.int32)[None, :] < tgt_lengths[:, None]).reshape(-1, 1)
-    dec_out = (residual + jnp.where(row_mask, attended, 0.0)).astype(jnp.bfloat16)
+    dec_out = add_residual(attended, states, tgt_lengths)
     return (dec_out[None], token_grad)
 
 
@@ -247,4 +668,6 @@
         P("section", "dp", "expert"),
     )
     out_specs = (P("section", "expert", "dp"), P(("expert", "dp"), "section"))
-    return jax.shard_map(body, mesh=mesh, in_specs=in_specs, out_specs=out_specs, check_vma=False)
+    small = mesh.shape["expert"] == 2 and mesh.shape["dp"] == 4
+    chosen = small_body if small else body
+    return jax.shard_map(chosen, mesh=mesh, in_specs=in_specs, out_specs=out_specs, check_vma=False)

time: 257 us -> 220 us (0.86)
  the two profiles are of different devices: /device:TPU:8 before, /device:TPU:0 now
where the time goes in v3:
time: 220 us; the launch traced here: 219 us
  waiting for transfers between devices  70.9 us (32%)
  starting transfers between devices  40.9 us (19%)
  blocking collectives  35.9 us (16%)
  matrix products  29.3 us (13%)
  Pallas kernels  18.8 us (9%)
  other arithmetic  12.3 us (6%)
  local copies, waits for them, and re-layouts  9.82 us (4%)
    ppermute x18, waiting for transfers between devices, swap(): return lax.ppermute(value, axis, [(i, i ^ mask) for i in range(size)])  31.6 us
    ppermute x9, waiting for transfers between devices, shift(): lax.ppermute(value, axis, [(i, (i + step) % size) for i in range(size)])  29.2 us
    all_gather x1, blocking collectives, small_body(): grad_y = lax.all_gather(grad_fetched, 'section', axis=0, tiled=True)  17 us
    dot_general x2, matrix products, contract_last(): lax.dot_general(left, right, (((1,), (1,)), ((), ())), preferred_element_...  16 us
    ppermute x18, starting transfers between devices, swap(): return lax.ppermute(value, axis, [(i, i ^ mask) for i in range(size)])  15.7 us
    ppermute x14, starting transfers between devices, send_home(): lax.ppermute(block, ('expert', 'dp'), [(i, i ^ code) for i in range(size)])  12.9 us
    ppermute x9, starting transfers between devices, shift(): lax.ppermute(value, axis, [(i, (i + step) % size) for i in range(size)])  12.3 us
    all_gather x1, blocking collectives, small_body(): all_ids = lax.all_gather(expert_ids.T, ('expert', 'dp'), axis=0)  12.2 us
  transfers between devices with their start and end apart: 41, of which 10 were waited for; matrix products, arithmetic and copies ran while one was open for 20% of the time, Pallas kernels for 9%

profile of v3, /device:TPU:0, one launch (start us, length us, event | category | flops | bytes accessed | tf_op | source)
XLA Modules:
  0.0 219.2 jit_solution(5773321634197920654)
XLA Ops:
  0.6 3.0 %collective-permute-start.1 = (bf16[128,2048]{1,0:T(8,128)(2,1)}, bf16[128,2048]{1,0:T(8,128)(2,1)S(1)}, u32[]{:S(2)}, u32[]{:S(2)}) collective-permute-start(bf16[128,2048]{1,0:T(8,128)(2,1)} %tokens_ref), channel_id=1, source_target_pairs={{0,4},{4,0},{1,5},{5,1},{2,6},{6,2},{3,7},{7,3},{8,12},{12,8},{9,1... | collective-permute-start | bytes 1572872 | tf_op jit(solution)/shard_map/ppermute | solution.py:38
  3.7 1.5 collective-permute-start
  5.9 0.8 copy.29
  6.6 1.4 convert_reduce_fusion
  8.9 12.2 %all-gather.1 = s32[8,2,128]{2,1,0:T(2,128)S(1)} all-gather(s32[1,2,128]{2,1,0:T(2,128)} %bitcast.117), channel_id=2, replica_groups=mesh['section'=4,'expert'=2,'dp'=4] {'expert','dp'}, dimensions={0}, use_global_device_ids=true | all-gather | bytes 9216 | tf_op jit(solution)/shard_map/all_gather | solution.py:417
  21.3 0.8 copy.32.gates_ref
  22.2 1.6 fusion.31
  24.6 0.9 constant_dynamic-slice_fusion.5
  25.9 1.7 collective-permute-start.7
  27.6 10.4 %collective-permute-done.2.refs_3_ = bf16[128,2048]{1,0:T(8,128)(2,1)S(1)} collective-permute-done((bf16[128,2048]{1,0:T(8,128)(2,1)S(1)}, bf16[128,2048]{1,0:T(8,128)(2,1)S(1)}, u32[]{:S(2)}, u32[]{:S(2)}) %collective-permute-start.2) | collective-permute-done | bytes 524320 | tf_op jit(solution)/shard_map/ppermute | solution.py:38
  38.6 1.0 copy-done.5
  39.6 1.3 dispatch.2
  41.0 3.2 %fusion.14 = f32[192,1024]{1,0:T(8,128)S(1)} fusion(bf16[192,2048]{1,0:T(8,128)(2,1)S(1)} %get-tuple-element.23, bf16[1,2048,1024]{2,1,0:T(8,128)(2,1)} %param.19), kind=kOutput, calls=%fused_computation.14 | convolution fusion | flops 805306368 | bytes 5767168 | tf_op jit(solution)/shard_map/dot_general | solution.py:450
  44.2 1.1 fusion.22
  45.4 1.5 collective-permute-start.5
  46.9 1.5 collective-permute-start.4
  48.4 1.0 fusion.12
  49.5 1.1 fusion.25
  50.6 2.5 %collective-permute-done.8.refs_1_ = bf16[128,2048]{1,0:T(8,128)(2,1)S(1)} collective-permute-done((bf16[128,2048]{1,0:T(8,128)(2,1)}, bf16[128,2048]{1,0:T(8,128)(2,1)S(1)}, u32[]{:S(2)}, u32[]{:S(2)}) %collective-permute-start.8) | collective-permute-done | bytes 524320 | tf_op jit(solution)/shard_map/ppermute | solution.py:38
  53.6 5.0 %collective-permute-done.7.key_other = bf16[1024,512]{1,0:T(8,128)(2,1)S(1)} collective-permute-done((bf16[1024,512]{1,0:T(8,128)(2,1)}, bf16[1024,512]{1,0:T(8,128)(2,1)S(1)}, u32[]{:S(2)}, u32[]{:S(2)}) %collective-permute-start.7) | collective-permute-done | bytes 1048608 | tf_op jit(solution)/shard_map/ppermute | solution.py:38
  58.8 2.7 %collective-permute-start.11 = (bf16[48,2048]{1,0:T(8,128)(2,1)S(1)}, bf16[48,2048]{1,0:T(8,128)(2,1)S(1)}, u32[]{:S(2)}, u32[]{:S(2)}) collective-permute-start(bf16[48,2048]{1,0:T(8,128)(2,1)S(1)} %get-tuple-element.53), channel_id=1, source_target_pairs={{0,5},{1,4},{2,7},{3,6},{4,1},{5,0},{6,3},{7,2},{8,13},{9,12},{10,... | collective-permute-start | bytes 589832 | tf_op jit(solution)/shard_map/ppermute | solution.py:203
  61.4 3.9 %collective-permute-done.4.refs_2_ = bf16[48,2048]{1,0:T(8,128)(2,1)S(1)} collective-permute-done((bf16[48,2048]{1,0:T(8,128)(2,1)S(1)}, bf16[48,2048]{1,0:T(8,128)(2,1)S(1)}, u32[]{:S(2)}, u32[]{:S(2)}) %collective-permute-start.4) | collective-permute-done | bytes 196640 | tf_op jit(solution)/shard_map/ppermute | solution.py:203
  65.4 17.0 %all_gather.15.refs_2_ = bf16[128,2048]{1,0:T(8,128)(2,1)} all-gather(bf16[32,2048]{1,0:T(8,128)(2,1)S(1)} %collective-permute-done.19), channel_id=1, replica_groups=mesh['section'=4,'expert'=2,'dp'=4] {'section'}, dimensions={0}, use_global_device_ids=true | all-gather | bytes 655360 | tf_op jit(solution)/shard_map/all_gather | solution.py:424
  82.4 2.8 %collective-permute-start.20 = (bf16[128,2048]{1,0:T(8,128)(2,1)}, bf16[128,2048]{1,0:T(8,128)(2,1)}, u32[]{:S(2)}, u32[]{:S(2)}) collective-permute-start(bf16[128,2048]{1,0:T(8,128)(2,1)} %all_gather.15.refs_2_), channel_id=1, source_target_pairs={{0,2},{1,3},{2,0},{3,1},{4,6},{5,7},{6,4},{7,5},{8,10},{9,11},{10,... | collective-permute-start | bytes 1572872 | tf_op jit(solution)/shard_map/ppermute | solution.py:38
  85.2 3.6 %combine.2 = (f32[128,512]{1,0:T(8,128)S(1)}, bf16[128,512]{1,0:T(8,128)(2,1)}, bf16[128,512]{1,0:T(8,128)(2,1)S(1)}, bf16[128,512]{1,0:T(8,128)(2,1)S(1)}) custom-call(s32[1]{0:T(128)} %bitcast.13.section_ref, s32[128,2]{1,0:T(8,128)S(1)} %multiply_add_fusion.position_ref, f32[128,2]{1,0:T(8,128)S(1)} %copy.32.gates_ref, ...), custom_call_target="tpu_custom_call" | custom-call | flops 402653184 | bytes 1572864 | tf_op jit(solution)/shard_map/combine/pallas_call | solution.py:243
  89.6 1.8 collective-permute-start.16
  91.4 2.5 %collective-permute-start.17 = (bf16[128,512]{1,0:T(8,128)(2,1)S(1)}, bf16[128,512]{1,0:T(8,128)(2,1)}, u32[]{:S(2)}, u32[]{:S(2)}) collective-permute-start(bf16[128,512]{1,0:T(8,128)(2,1)S(1)} %get-tuple-element.32), channel_id=1, source_target_pairs={{0,16},{8,24},{16,0},{24,8},{1,17},{9,25},{17,1},{25,9},{2,18},{10... | collective-permute-start | bytes 393224 | tf_op jit(solution)/shard_map/ppermute | solution.py:33
  93.9 1.4 fusion.33
  95.3 0.9 dynamic_slice.68
  96.3 1.9 collective-permute-done.16
  98.3 3.5 %collective-permute-done.17 = bf16[128,512]{1,0:T(8,128)(2,1)} collective-permute-done((bf16[128,512]{1,0:T(8,128)(2,1)S(1)}, bf16[128,512]{1,0:T(8,128)(2,1)}, u32[]{:S(2)}, u32[]{:S(2)}) %collective-permute-start.17) | collective-permute-done | bytes 131104 | tf_op jit(solution)/shard_map/ppermute | solution.py:33
  101.8 1.2 add_convert_fusion.2.refs_0_
  102.9 3.7 %collective-permute-start.24 = (bf16[128,512]{1,0:T(8,128)(2,1)S(1)}, bf16[128,512]{1,0:T(8,128)(2,1)S(1)}, u32[]{:S(2)}, u32[]{:S(2)}) collective-permute-start(bf16[128,512]{1,0:T(8,128)(2,1)S(1)} %add_convert_fusion.2.refs_0_), channel_id=1, source_target_pairs={{0,24},{8,0},{16,8},{24,16},{1,25},{9,1},{17,9},{25,17},{2,26},{10... | collective-permute-start | bytes 393224 | tf_op jit(solution)/shard_map/ppermute | solution.py:33
  107.3 6.7 %all_gather.14 = bf16[256,1024]{1,0:T(8,128)(2,1)S(1)} all-gather(bf16[64,1024]{1,0:T(8,128)(2,1)S(1)} %collective-permute-done.13), channel_id=1, replica_groups=mesh['section'=4,'expert'=2,'dp'=4] {'dp'}, dimensions={0}, use_global_device_ids=true | all-gather | bytes 655360 | tf_op jit(solution)/shard_map/all_gather | solution.py:482
  114.0 1.0 copy-done.7
  115.0 1.0 copy-done.9
  116.1 2.6 %dispatch.3 = (bf16[192,2048]{1,0:T(8,128)(2,1)S(1)}, bf16[192,2048]{1,0:T(8,128)(2,1)}) custom-call(s32[8,128]{1,0:T(8,128)S(1)} %fusion.34.code_ref, bf16[128,2048]{1,0:T(8,128)(2,1)S(1)} %copy-done.7, bf16[128,2048]{1,0:T(8,128)(2,1)S(1)} %copy-done.9, bf16[128,2048]{1,0:T(8,128)(2,1)} %all_gather.15.refs_2_, ...), custom_call_target="tpu_custom_call" | custom-call | flops 201326592 | bytes 3670016 | tf_op jit(solution)/shard_map/dispatch/pallas_call | solution.py:177
  118.7 1.0 copy-done.13
  120.1 1.1 convolution_convert_fusion
  121.2 8.1 %fusion.16 = bf16[192,2048]{1,0:T(8,128)(2,1)} fusion(bf16[1,2048,1024]{2,1,0:T(8,128)(2,1)} %param.19, f32[192,1024]{1,0:T(8,128)} %copy-done.16, bf16[192,2048]{1,0:T(8,128)(2,1)} %copy-done.13, bf16[1,1024,2048]{2,1,0:T(8,128)(2,1)} %param.20), kind=kOutput, calls=%fused_computation.18 | convolution fusion | flops 1614938112 | bytes 10747904 | tf_op jit(solution)/shard_map/dot_general | solution.py:26
  129.3 1.1 collective-permute-start.14
  130.4 7.8 %fusion.19 = bf16[192,2048]{1,0:T(8,128)(2,1)} fusion(bf16[1,2048,1024]{2,1,0:T(8,128)(2,1)} %param.19, f32[192,1024]{1,0:T(8,128)S(1)} %copy-done.18, bf16[192,2048]{1,0:T(8,128)(2,1)} %collective-permute-done.21, bf16[1,1024,2048]{2,1,0:T(8,128)(2,1)} %param.20), kind=kOutput, calls=%fused_computation.19 | convolution fusion | flops 1614938112 | bytes 10747904 | tf_op jit(solution)/shard_map/dot_general | solution.py:26
  138.3 1.0 copy-done.6
  139.4 2.3 %memory.1.near_ref = bf16[128,2048]{1,0:T(8,128)(2,1)} custom-call(s32[1]{0:T(128)} %bitcast.13.section_ref, bf16[128,2048]{1,0:T(8,128)(2,1)S(1)} %copy-done.6, f32[1,2048]{1,0:T(1,128)S(1)} %bitcast.115, bf16[128,512]{1,0:T(8,128)(2,1)S(1)} %add_convert_fusion.2.refs_0_, bf16[128,512]{1,0:T(8,128)(2,1)} %collective-permute-done.22.refs_1_, ...), custom_call_target="tpu_custom_call" | custom-call | tf_op jit(solution)/shard_map/memory/pallas_call | solution.py:279
  141.7 1.2 collective-permute-start.26
  142.9 2.3 %fusion.36 = f32[256,512]{1,0:T(8,128)} fusion(bf16[1,1024,512]{2,1,0:T(8,128)(2,1)S(1)} %copy-done, bf16[256,2048]{1,0:T(8,128)(2,1)} %fusion.33, s32[]{:T(128)S(6)} %select_n.121), kind=kOutput, calls=%fused_computation.39 | convolution fusion | flops 268435456 | bytes 2097156 | tf_op jit(solution)/shard_map/dot_general | solution.py:488
  145.2 0.9 collective-permute-start.27
  146.3 1.2 add_convert_fusion.1
  147.5 8.2 %collective-permute-done.26.near_ref = bf16[128,2048]{1,0:T(8,128)(2,1)} collective-permute-done((bf16[128,2048]{1,0:T(8,128)(2,1)}, bf16[128,2048]{1,0:T(8,128)(2,1)}, u32[]{:S(2)}, u32[]{:S(2)}) %collective-permute-start.26) | collective-permute-done | bytes 524320 | tf_op jit(solution)/shard_map/ppermute | solution.py:38
  155.7 1.5 pad_maximum_fusion
  157.3 3.6 %attend_sentence.2 = bf16[128,512]{1,0:T(8,128)(2,1)S(1)} custom-call(s32[3]{0:T(128)S(1)} %pad_add_fusion.1.place_ref, s32[2]{0:T(128)S(1)} %copy-done.12, bf16[128,512]{1,0:T(8,128)(2,1)S(1)} %get-tuple-element.72.query_ref, bf16[128,2048]{1,0:T(8,128)(2,1)} %memory.1.near_ref, bf16[128,2048]{1,0:T(8,128)(2,1)S(1)} %collective-permute-done.25.far_ref, ...), custom_call_target="tpu_custom_call" | custom-call | flops 1073741824 | bytes 5242880 | tf_op jit(solution)/shard_map/attend_sentence/pallas_call | solution.py:357
  161.1 2.8 %collective-permute-start.33 = (bf16[384,512]{1,0:T(8,128)(2,1)S(1)}, bf16[384,512]{1,0:T(8,128)(2,1)S(1)}, u32[]{:S(2)}, u32[]{:S(2)}) collective-permute-start(bf16[384,512]{1,0:T(8,128)(2,1)S(1)} %get-tuple-element.47), channel_id=1, source_target_pairs={{0,24},{8,0},{16,8},{24,16},{1,25},{9,1},{17,9},{25,17},{2,26},{10... | collective-permute-start | bytes 1179656 | tf_op jit(solution)/shard_map/ppermute | solution.py:33
  164.7 5.5 %collective-permute-done.27 = bf16[512,1024]{1,0:T(8,128)(2,1)} collective-permute-done((bf16[512,1024]{1,0:T(8,128)(2,1)}, bf16[512,1024]{1,0:T(8,128)(2,1)}, u32[]{:S(2)}, u32[]{:S(2)}) %collective-permute-start.27) | collective-permute-done | bytes 1048608 | tf_op jit(solution)/shard_map/ppermute | solution.py:38
  170.1 3.6 %attend_sentence.3 = bf16[128,512]{1,0:T(8,128)(2,1)S(1)} custom-call(s32[3]{0:T(128)S(1)} %pad_add_fusion.3.place_ref, s32[2]{0:T(128)S(1)} %copy-done.12, bf16[128,512]{1,0:T(8,128)(2,1)S(1)} %get-tuple-element.73.query_ref, bf16[128,2048]{1,0:T(8,128)(2,1)} %collective-permute-done.26.near_ref, bf16[128,2048]{1,0:T(8,128)(2,1)S(1)} %collective-permute-done.28.far_ref, ...), custom_call_target="tpu_custom_call" | custom-call | flops 1073741824 | bytes 5242880 | tf_op jit(solution)/shard_map/attend_sentence/pallas_call | solution.py:357
  173.8 1.3 fusion.66
  175.6 23.8 %collective-permute-done.32 = bf16[384,512]{1,0:T(8,128)(2,1)S(1)} collective-permute-done((bf16[384,512]{1,0:T(8,128)(2,1)S(1)}, bf16[384,512]{1,0:T(8,128)(2,1)S(1)}, u32[]{:S(2)}, u32[]{:S(2)}) %collective-permute-start.32) | collective-permute-done | bytes 393248 | tf_op jit(solution)/shard_map/ppermute | solution.py:33
  199.7 1.8 collective-permute-start.40
  202.7 1.3 fusion.69
  204.6 1.3 collective-permute-start.30
  206.0 2.0 collective-permute-start.36
  208.3 1.2 collective-permute-start.34
  209.6 6.1 %collective-permute-done.36.refs_3_ = bf16[48,512]{1,0:T(8,128)(2,1)S(1)} collective-permute-done((bf16[48,512]{1,0:T(8,128)(2,1)S(1)}, bf16[48,512]{1,0:T(8,128)(2,1)S(1)}, u32[]{:S(2)}, u32[]{:S(2)}) %collective-permute-start.36) | collective-permute-done | bytes 49184 | tf_op jit(solution)/shard_map/ppermute | solution.py:203
  215.7 1.6 combine.3
  217.4 1.8 fusion.98
  (120 shorter events, 10.4 us)
Async XLA Ops:
  0.6 119.4 %copy-start = (bf16[1,1024,512]{2,1,0:T(8,128)(2,1)S(1)}, bf16[1,1024,512]{2,1,0:T(8,128)(2,1)}, u32[]{:S(2)}) copy-start(bf16[1,1024,512]{2,1,0:T(8,128)(2,1)} %param.26) | copy-start | bytes 3145732
  0.6 23.2 %collective-permute-start.1 = (bf16[128,2048]{1,0:T(8,128)(2,1)}, bf16[128,2048]{1,0:T(8,128)(2,1)S(1)}, u32[]{:S(2)}, u32[]{:S(2)}) collective-permute-start(bf16[128,2048]{1,0:T(8,128)(2,1)} %tokens_ref), channel_id=1, source_target_pairs={{0,4},{4,0},{1,5},{5,1},{2,6},{6,2},{3,7},{7,3},{8,12},{12,8},{9,1... | collective-permute-start | bytes 1572872 | tf_op jit(solution)/shard_map/ppermute | solution.py:38
  3.7 34.9 %collective-permute-start = (bf16[128,2048]{1,0:T(8,128)(2,1)}, bf16[128,2048]{1,0:T(8,128)(2,1)S(1)}, u32[]{:S(2)}, u32[]{:S(2)}) collective-permute-start(bf16[128,2048]{1,0:T(8,128)(2,1)} %tokens_ref), channel_id=1, source_target_pairs={{0,2},{1,3},{2,0},{3,1},{4,6},{5,7},{6,4},{7,5},{8,10},{9,11},{10,... | collective-permute-start | bytes 1572872 | tf_op jit(solution)/shard_map/ppermute | solution.py:38
  23.8 14.2 %collective-permute-start.2 = (bf16[128,2048]{1,0:T(8,128)(2,1)S(1)}, bf16[128,2048]{1,0:T(8,128)(2,1)S(1)}, u32[]{:S(2)}, u32[]{:S(2)}) collective-permute-start(bf16[128,2048]{1,0:T(8,128)(2,1)S(1)} %collective-permute-done.1.refs_2_), channel_id=1, source_target_pairs={{0,2},{1,3},{2,0},{3,1},{4,6},{5,7},{6,4},{7,5},{8,10},{9,11},{10,... | collective-permute-start | bytes 1572872 | tf_op jit(solution)/shard_map/ppermute | solution.py:38
  25.5 33.3 %collective-permute-start.19 = (bf16[32,2048]{1,0:T(8,128)(2,1)S(1)}, bf16[32,2048]{1,0:T(8,128)(2,1)S(1)}, u32[]{:S(2)}, u32[]{:S(2)}) collective-permute-start(bf16[32,2048]{1,0:T(8,128)(2,1)S(1)} %constant_dynamic-slice_fusion.5), channel_id=1, source_target_pairs={{0,4},{4,0},{1,5},{5,1},{2,6},{6,2},{3,7},{7,3},{8,12},{12,8},{9,1... | collective-permute-start | bytes 393224 | tf_op jit(solution)/shard_map/ppermute | solution.py:38
  25.9 32.7 %collective-permute-start.7 = (bf16[1024,512]{1,0:T(8,128)(2,1)}, bf16[1024,512]{1,0:T(8,128)(2,1)S(1)}, u32[]{:S(2)}, u32[]{:S(2)}) collective-permute-start(bf16[1024,512]{1,0:T(8,128)(2,1)} %bitcast.109), channel_id=1, source_target_pairs={{0,4},{4,0},{1,5},{5,1},{2,6},{6,2},{3,7},{7,3},{8,12},{12,8},{9,1... | collective-permute-start | bytes 3145736 | tf_op jit(solution)/shard_map/ppermute | solution.py:38
  38.0 15.1 %collective-permute-start.8 = (bf16[128,2048]{1,0:T(8,128)(2,1)}, bf16[128,2048]{1,0:T(8,128)(2,1)S(1)}, u32[]{:S(2)}, u32[]{:S(2)}) collective-permute-start(bf16[128,2048]{1,0:T(8,128)(2,1)} %refs_0_.3), channel_id=1, source_target_pairs={{0,2},{1,3},{2,0},{3,1},{4,6},{5,7},{6,4},{7,5},{8,10},{9,11},{10,... | collective-permute-start | bytes 1572872 | tf_op jit(solution)/shard_map/ppermute | solution.py:38
  38.6 1.0 copy-start.5
  39.6 4.6 %copy-start.21 = (bf16[1,1024,2048]{2,1,0:T(8,128)(2,1)S(1)}, bf16[1,1024,2048]{2,1,0:T(8,128)(2,1)}, u32[]{:S(2)}) copy-start(bf16[1,1024,2048]{2,1,0:T(8,128)(2,1)} %param.20) | copy-start | bytes 12582916
  41.0 5.9 %collective-permute-start.6 = (bf16[192,2048]{1,0:T(8,128)(2,1)S(1)}, bf16[192,2048]{1,0:T(8,128)(2,1)S(1)}, u32[]{:S(2)}, u32[]{:S(2)}) collective-permute-start(bf16[192,2048]{1,0:T(8,128)(2,1)S(1)} %get-tuple-element.24), channel_id=1, source_target_pairs={{0,1},{1,0},{2,3},{3,2},{4,5},{5,4},{6,7},{7,6},{8,9},{9,8},{10,11... | collective-permute-start | bytes 2359304 | tf_op jit(solution)/shard_map/ppermute | solution.py:38
  44.2 5.2 %copy-start.16 = (f32[192,1024]{1,0:T(8,128)}, f32[192,1024]{1,0:T(8,128)S(1)}, u32[]{:S(2)}) copy-start(f32[192,1024]{1,0:T(8,128)S(1)} %fusion.14) | copy-start | bytes 2359300
  44.2 4.2 %copy-start.14 = (bf16[1,2048,1024]{2,1,0:T(8,128)(2,1)S(1)}, bf16[1,2048,1024]{2,1,0:T(8,128)(2,1)}, u32[]{:S(2)}) copy-start(bf16[1,2048,1024]{2,1,0:T(8,128)(2,1)} %param.19) | copy-start | bytes 12582916
  45.4 16.0 %collective-permute-start.5 = (bf16[48,2048]{1,0:T(8,128)(2,1)S(1)}, bf16[48,2048]{1,0:T(8,128)(2,1)S(1)}, u32[]{:S(2)}, u32[]{:S(2)}) collective-permute-start(bf16[48,2048]{1,0:T(8,128)(2,1)S(1)} %get-tuple-element.56), channel_id=1, source_target_pairs={{0,6},{1,7},{2,4},{3,5},{4,2},{5,3},{6,0},{7,1},{8,14},{9,15},{10,... | collective-permute-start | bytes 589832 | tf_op jit(solution)/shard_map/ppermute | solution.py:203
  46.9 18.5 %collective-permute-start.4 = (bf16[48,2048]{1,0:T(8,128)(2,1)S(1)}, bf16[48,2048]{1,0:T(8,128)(2,1)S(1)}, u32[]{:S(2)}, u32[]{:S(2)}) collective-permute-start(bf16[48,2048]{1,0:T(8,128)(2,1)S(1)} %get-tuple-element.57), channel_id=1, source_target_pairs={{0,4},{1,5},{2,6},{3,7},{4,0},{5,1},{6,2},{7,3},{8,12},{9,13},{10,... | collective-permute-start | bytes 589832 | tf_op jit(solution)/shard_map/ppermute | solution.py:203
  49.4 32.9 %copy-start.17 = (f32[192,1024]{1,0:T(8,128)}, f32[192,1024]{1,0:T(8,128)S(1)}, u32[]{:S(2)}) copy-start(f32[192,1024]{1,0:T(8,128)S(1)} %fusion.12) | copy-start | bytes 2359300
  49.4 44.5 %copy-start.15 = (bf16[1,256,2048]{2,1,0:T(8,128)(2,1)S(1)}, bf16[1,256,2048]{2,1,0:T(8,128)(2,1)}, u32[]{:S(2)}) copy-start(bf16[1,256,2048]{2,1,0:T(8,128)(2,1)} %param.22) | copy-start | bytes 3145732
  49.5 44.5 %copy-start.20 = (f32[1,2048]{1,0:T(1,128)S(1)}, f32[1,2048]{1,0:T(1,128)}, u32[]{:S(2)}) copy-start(f32[1,2048]{1,0:T(1,128)} %param.25) | copy-start | bytes 24580
  50.6 47.6 %copy-start.2 = (bf16[1,1024,512]{2,1,0:T(8,128)(2,1)S(1)}, bf16[1,1024,512]{2,1,0:T(8,128)(2,1)}, u32[]{:S(2)}) copy-start(bf16[1,1024,512]{2,1,0:T(8,128)(2,1)} %param.28) | copy-start | bytes 3145732
  53.1 35.8 %copy-start.8 = (bf16[128,2048]{1,0:T(8,128)(2,1)}, bf16[128,2048]{1,0:T(8,128)(2,1)S(1)}, u32[]{:S(2)}) copy-start(bf16[128,2048]{1,0:T(8,128)(2,1)S(1)} %collective-permute-done.8.refs_1_) | copy-start | bytes 1572868
  53.1 29.3 %collective-permute-start.3 = (bf16[48,2048]{1,0:T(8,128)(2,1)S(1)}, bf16[48,2048]{1,0:T(8,128)(2,1)S(1)}, u32[]{:S(2)}, u32[]{:S(2)}) collective-permute-start(bf16[48,2048]{1,0:T(8,128)(2,1)S(1)} %get-tuple-element.58), channel_id=1, source_target_pairs={{0,2},{1,3},{2,0},{3,1},{4,6},{5,7},{6,4},{7,5},{8,10},{9,11},{10,... | collective-permute-start | bytes 589832 | tf_op jit(solution)/shard_map/ppermute | solution.py:203
  58.6 60.1 %copy-start.3 = (bf16[1024,512]{1,0:T(8,128)(2,1)}, bf16[1024,512]{1,0:T(8,128)(2,1)S(1)}, u32[]{:S(2)}) copy-start(bf16[1024,512]{1,0:T(8,128)(2,1)S(1)} %collective-permute-done.7.key_other) | copy-start | bytes 3145732
  58.7 23.7 %collective-permute-start.12 = (bf16[48,2048]{1,0:T(8,128)(2,1)S(1)}, bf16[48,2048]{1,0:T(8,128)(2,1)S(1)}, u32[]{:S(2)}, u32[]{:S(2)}) collective-permute-start(bf16[48,2048]{1,0:T(8,128)(2,1)S(1)} %get-tuple-element.52), channel_id=1, source_target_pairs={{0,7},{1,6},{2,5},{3,4},{4,3},{5,2},{6,1},{7,0},{8,15},{9,14},{10,... | collective-permute-start | bytes 589832 | tf_op jit(solution)/shard_map/ppermute | solution.py:203
  58.8 23.6 %collective-permute-start.11 = (bf16[48,2048]{1,0:T(8,128)(2,1)S(1)}, bf16[48,2048]{1,0:T(8,128)(2,1)S(1)}, u32[]{:S(2)}, u32[]{:S(2)}) collective-permute-start(bf16[48,2048]{1,0:T(8,128)(2,1)S(1)} %get-tuple-element.53), channel_id=1, source_target_pairs={{0,5},{1,4},{2,7},{3,6},{4,1},{5,0},{6,3},{7,2},{8,13},{9,12},{10,... | collective-permute-start | bytes 589832 | tf_op jit(solution)/shard_map/ppermute | solution.py:203
  61.4 21.0 %collective-permute-start.10 = (bf16[48,2048]{1,0:T(8,128)(2,1)S(1)}, bf16[48,2048]{1,0:T(8,128)(2,1)S(1)}, u32[]{:S(2)}, u32[]{:S(2)}) collective-permute-start(bf16[48,2048]{1,0:T(8,128)(2,1)S(1)} %get-tuple-element.54), channel_id=1, source_target_pairs={{0,3},{1,2},{2,1},{3,0},{4,7},{5,6},{6,5},{7,4},{8,11},{9,10},{10,... | collective-permute-start | bytes 589832 | tf_op jit(solution)/shard_map/ppermute | solution.py:203
  65.4 17.0 %collective-permute-start.9 = (bf16[48,2048]{1,0:T(8,128)(2,1)S(1)}, bf16[48,2048]{1,0:T(8,128)(2,1)S(1)}, u32[]{:S(2)}, u32[]{:S(2)}) collective-permute-start(bf16[48,2048]{1,0:T(8,128)(2,1)S(1)} %get-tuple-element.55), channel_id=1, source_target_pairs={{0,1},{1,0},{2,3},{3,2},{4,5},{5,4},{6,7},{7,6},{8,9},{9,8},{10,11... | collective-permute-start | bytes 589832 | tf_op jit(solution)/shard_map/ppermute | solution.py:203
  82.4 31.6 %collective-permute-start.20 = (bf16[128,2048]{1,0:T(8,128)(2,1)}, bf16[128,2048]{1,0:T(8,128)(2,1)}, u32[]{:S(2)}, u32[]{:S(2)}) collective-permute-start(bf16[128,2048]{1,0:T(8,128)(2,1)} %all_gather.15.refs_2_), channel_id=1, source_target_pairs={{0,2},{1,3},{2,0},{3,1},{4,6},{5,7},{6,4},{7,5},{8,10},{9,11},{10,... | collective-permute-start | bytes 1572872 | tf_op jit(solution)/shard_map/ppermute | solution.py:38
  88.9 0.7 copy-start.10
  89.6 8.6 %collective-permute-start.16 = (bf16[128,512]{1,0:T(8,128)(2,1)}, bf16[128,512]{1,0:T(8,128)(2,1)}, u32[]{:S(2)}, u32[]{:S(2)}) collective-permute-start(bf16[128,512]{1,0:T(8,128)(2,1)} %get-tuple-element.31), channel_id=1, source_target_pairs={{0,8},{8,16},{16,24},{24,0},{1,9},{9,17},{17,25},{25,1},{2,10},{10... | collective-permute-start | bytes 393224 | tf_op jit(solution)/shard_map/ppermute | solution.py:33
  91.4 10.4 %collective-permute-start.17 = (bf16[128,512]{1,0:T(8,128)(2,1)S(1)}, bf16[128,512]{1,0:T(8,128)(2,1)}, u32[]{:S(2)}, u32[]{:S(2)}) collective-permute-start(bf16[128,512]{1,0:T(8,128)(2,1)S(1)} %get-tuple-element.32), channel_id=1, source_target_pairs={{0,16},{8,24},{16,0},{24,8},{1,17},{9,25},{17,1},{25,9},{2,18},{10... | collective-permute-start | bytes 393224 | tf_op jit(solution)/shard_map/ppermute | solution.py:33
  93.9 7.8 %collective-permute-start.18 = (bf16[128,512]{1,0:T(8,128)(2,1)S(1)}, bf16[128,512]{1,0:T(8,128)(2,1)}, u32[]{:S(2)}, u32[]{:S(2)}) collective-permute-start(bf16[128,512]{1,0:T(8,128)(2,1)S(1)} %get-tuple-element.33), channel_id=1, source_target_pairs={{0,24},{8,0},{16,8},{24,16},{1,25},{9,1},{17,9},{25,17},{2,26},{10... | collective-permute-start | bytes 393224 | tf_op jit(solution)/shard_map/ppermute | solution.py:33
  96.2 10.9 %collective-permute-start.13 = (bf16[64,1024]{1,0:T(8,128)(2,1)S(1)}, bf16[64,1024]{1,0:T(8,128)(2,1)S(1)}, u32[]{:S(2)}, u32[]{:S(2)}) collective-permute-start(bf16[64,1024]{1,0:T(8,128)(2,1)S(1)} %dynamic_slice.68), channel_id=1, source_target_pairs={{0,4},{4,0},{1,5},{5,1},{2,6},{6,2},{3,7},{7,3},{8,12},{12,8},{9,1... | collective-permute-start | bytes 393224 | tf_op jit(solution)/shard_map/ppermute | solution.py:38
  98.2 40.1 %collective-permute-start.15 = (bf16[1024,512]{1,0:T(8,128)(2,1)S(1)}, bf16[1024,512]{1,0:T(8,128)(2,1)}, u32[]{:S(2)}, u32[]{:S(2)}) collective-permute-start(bf16[1024,512]{1,0:T(8,128)(2,1)S(1)} %bitcast.112), channel_id=1, source_target_pairs={{0,4},{4,0},{1,5},{5,1},{2,6},{6,2},{3,7},{7,3},{8,12},{12,8},{9,1... | collective-permute-start | bytes 3145736 | tf_op jit(solution)/shard_map/ppermute | solution.py:38
  102.9 35.3 %collective-permute-start.24 = (bf16[128,512]{1,0:T(8,128)(2,1)S(1)}, bf16[128,512]{1,0:T(8,128)(2,1)S(1)}, u32[]{:S(2)}, u32[]{:S(2)}) collective-permute-start(bf16[128,512]{1,0:T(8,128)(2,1)S(1)} %add_convert_fusion.2.refs_0_), channel_id=1, source_target_pairs={{0,24},{8,0},{16,8},{24,16},{1,25},{9,1},{17,9},{25,17},{2,26},{10... | collective-permute-start | bytes 393224 | tf_op jit(solution)/shard_map/ppermute | solution.py:33
  106.7 31.6 %collective-permute-start.23 = (bf16[128,512]{1,0:T(8,128)(2,1)S(1)}, bf16[128,512]{1,0:T(8,128)(2,1)}, u32[]{:S(2)}, u32[]{:S(2)}) collective-permute-start(bf16[128,512]{1,0:T(8,128)(2,1)S(1)} %add_convert_fusion.2.refs_0_), channel_id=1, source_target_pairs={{0,16},{8,24},{16,0},{24,8},{1,17},{9,25},{17,1},{25,9},{2,18},{10... | collective-permute-start | bytes 393224 | tf_op jit(solution)/shard_map/ppermute | solution.py:33
  107.1 31.2 %collective-permute-start.22 = (bf16[128,512]{1,0:T(8,128)(2,1)S(1)}, bf16[128,512]{1,0:T(8,128)(2,1)}, u32[]{:S(2)}, u32[]{:S(2)}) collective-permute-start(bf16[128,512]{1,0:T(8,128)(2,1)S(1)} %add_convert_fusion.2.refs_0_), channel_id=1, source_target_pairs={{0,8},{8,16},{16,24},{24,0},{1,9},{9,17},{17,25},{25,1},{2,10},{10... | collective-permute-start | bytes 393224 | tf_op jit(solution)/shard_map/ppermute | solution.py:33
  114.0 1.0 copy-start.7
  115.0 1.0 copy-start.9
  118.7 1.0 copy-start.13
  119.7 9.6 %collective-permute-start.21 = (bf16[192,2048]{1,0:T(8,128)(2,1)}, bf16[192,2048]{1,0:T(8,128)(2,1)}, u32[]{:S(2)}, u32[]{:S(2)}) collective-permute-start(bf16[192,2048]{1,0:T(8,128)(2,1)} %get-tuple-element.38), channel_id=1, source_target_pairs={{0,1},{1,0},{2,3},{3,2},{4,5},{5,4},{6,7},{7,6},{8,9},{9,8},{10,11... | collective-permute-start | bytes 2359304 | tf_op jit(solution)/shard_map/ppermute | solution.py:38
  121.2 9.3 %copy-start.18 = (f32[192,1024]{1,0:T(8,128)S(1)}, f32[192,1024]{1,0:T(8,128)}, u32[]{:S(2)}) copy-start(f32[192,1024]{1,0:T(8,128)} %copy-done.17) | copy-start | bytes 2359300
  129.3 9.0 %copy-start.11 = (f32[2048]{0:T(1024)S(1)}, f32[2048]{0:T(1024)}, u32[]{:S(2)}) copy-start(f32[2048]{0:T(1024)} %param.21) | copy-start | bytes 24580
  129.3 16.9 %collective-permute-start.14 = (bf16[256,512]{1,0:T(8,128)(2,1)}, bf16[256,512]{1,0:T(8,128)(2,1)}, u32[]{:S(2)}, u32[]{:S(2)}) collective-permute-start(bf16[256,512]{1,0:T(8,128)(2,1)} %convolution_convert_fusion), channel_id=1, source_target_pairs={{0,4},{4,0},{1,5},{5,1},{2,6},{6,2},{3,7},{7,3},{8,12},{12,8},{9,1... | collective-permute-start | bytes 786440 | tf_op jit(solution)/shard_map/ppermute | solution.py:38
  138.3 1.0 copy-start.6
  139.3 18.0 %copy-start.1 = (bf16[1,1024,512]{2,1,0:T(8,128)(2,1)S(1)}, bf16[1,1024,512]{2,1,0:T(8,128)(2,1)}, u32[]{:S(2)}) copy-start(bf16[1,1024,512]{2,1,0:T(8,128)(2,1)} %param.27) | copy-start | bytes 3145732
  139.4 18.0 %copy-start.12 = (s32[2]{0:T(128)S(1)}, s32[2]{0:T(128)}, u32[]{:S(2)}) copy-start(s32[2]{0:T(128)} %lengths_ref.3) | copy-start | bytes 28
  141.7 14.0 %collective-permute-start.26 = (bf16[128,2048]{1,0:T(8,128)(2,1)}, bf16[128,2048]{1,0:T(8,128)(2,1)}, u32[]{:S(2)}, u32[]{:S(2)}) collective-permute-start(bf16[128,2048]{1,0:T(8,128)(2,1)} %memory.1.near_ref), channel_id=1, source_target_pairs={{0,2},{1,3},{2,0},{3,1},{4,6},{5,7},{6,4},{7,5},{8,10},{9,11},{10,... | collective-permute-start | bytes 1572872 | tf_op jit(solution)/shard_map/ppermute | solution.py:38
  145.2 25.0 %collective-permute-start.27 = (bf16[512,1024]{1,0:T(8,128)(2,1)}, bf16[512,1024]{1,0:T(8,128)(2,1)}, u32[]{:S(2)}, u32[]{:S(2)}) collective-permute-start(bf16[512,1024]{1,0:T(8,128)(2,1)} %bitcast.116), channel_id=1, source_target_pairs={{0,4},{4,0},{1,5},{5,1},{2,6},{6,2},{3,7},{7,3},{8,12},{12,8},{9,1... | collective-permute-start | bytes 3145736 | tf_op jit(solution)/shard_map/ppermute | solution.py:38
  146.2 11.2 %copy-start.4 = (bf16[1024,512]{1,0:T(8,128)(2,1)S(1)}, bf16[1024,512]{1,0:T(8,128)(2,1)}, u32[]{:S(2)}) copy-start(bf16[1024,512]{1,0:T(8,128)(2,1)} %copy-done.3) | copy-start | bytes 3145732
  146.2 11.1 %collective-permute-start.25 = (bf16[128,2048]{1,0:T(8,128)(2,1)}, bf16[128,2048]{1,0:T(8,128)(2,1)S(1)}, u32[]{:S(2)}, u32[]{:S(2)}) collective-permute-start(bf16[128,2048]{1,0:T(8,128)(2,1)} %memory.1.near_ref), channel_id=1, source_target_pairs={{0,1},{1,0},{2,3},{3,2},{4,5},{5,4},{6,7},{7,6},{8,9},{9,8},{10,11... | collective-permute-start | bytes 1572872 | tf_op jit(solution)/shard_map/ppermute | solution.py:38
  155.7 14.4 %collective-permute-start.28 = (bf16[128,2048]{1,0:T(8,128)(2,1)}, bf16[128,2048]{1,0:T(8,128)(2,1)S(1)}, u32[]{:S(2)}, u32[]{:S(2)}) collective-permute-start(bf16[128,2048]{1,0:T(8,128)(2,1)} %collective-permute-done.26.near_ref), channel_id=1, source_target_pairs={{0,1},{1,0},{2,3},{3,2},{4,5},{5,4},{6,7},{7,6},{8,9},{9,8},{10,11... | collective-permute-start | bytes 1572872 | tf_op jit(solution)/shard_map/ppermute | solution.py:38
  161.1 14.0 %copy-start.19 = (bf16[1,512,1024]{2,1,0:T(8,128)(2,1)S(1)}, bf16[1,512,1024]{2,1,0:T(8,128)(2,1)}, u32[]{:S(2)}) copy-start(bf16[1,512,1024]{2,1,0:T(8,128)(2,1)} %param.29) | copy-start | bytes 3145732
  161.1 14.5 %collective-permute-start.33 = (bf16[384,512]{1,0:T(8,128)(2,1)S(1)}, bf16[384,512]{1,0:T(8,128)(2,1)S(1)}, u32[]{:S(2)}, u32[]{:S(2)}) collective-permute-start(bf16[384,512]{1,0:T(8,128)(2,1)S(1)} %get-tuple-element.47), channel_id=1, source_target_pairs={{0,24},{8,0},{16,8},{24,16},{1,25},{9,1},{17,9},{25,17},{2,26},{10... | collective-permute-start | bytes 1179656 | tf_op jit(solution)/shard_map/ppermute | solution.py:33
  163.9 35.5 %collective-permute-start.32 = (bf16[384,512]{1,0:T(8,128)(2,1)S(1)}, bf16[384,512]{1,0:T(8,128)(2,1)S(1)}, u32[]{:S(2)}, u32[]{:S(2)}) collective-permute-start(bf16[384,512]{1,0:T(8,128)(2,1)S(1)} %get-tuple-element.48), channel_id=1, source_target_pairs={{0,16},{8,24},{16,0},{24,8},{1,17},{9,25},{17,1},{25,9},{2,18},{10... | collective-permute-start | bytes 1179656 | tf_op jit(solution)/shard_map/ppermute | solution.py:33
  164.7 34.8 %collective-permute-start.31 = (bf16[384,512]{1,0:T(8,128)(2,1)S(1)}, bf16[384,512]{1,0:T(8,128)(2,1)S(1)}, u32[]{:S(2)}, u32[]{:S(2)}) collective-permute-start(bf16[384,512]{1,0:T(8,128)(2,1)S(1)} %get-tuple-element.49), channel_id=1, source_target_pairs={{0,8},{8,16},{16,24},{24,0},{1,9},{9,17},{17,25},{25,1},{2,10},{10... | collective-permute-start | bytes 1179656 | tf_op jit(solution)/shard_map/ppermute | solution.py:33
  175.5 28.9 %collective-permute-start.29 = (bf16[2,256,512]{2,1,0:T(8,128)(2,1)S(1)}, bf16[2,256,512]{2,1,0:T(8,128)(2,1)S(1)}, u32[]{:S(2)}, u32[]{:S(2)}) collective-permute-start(bf16[2,256,512]{2,1,0:T(8,128)(2,1)S(1)} %pad_maximum_fusion.1), channel_id=1, source_target_pairs={{0,1},{1,0},{2,3},{3,2},{4,5},{5,4},{6,7},{7,6},{8,9},{9,8},{10,11... | collective-permute-start | bytes 1572872 | tf_op jit(solution)/shard_map/ppermute | solution.py:38
  199.7 9.9 %copy-start.22 = (s32[2]{0:T(128)S(1)}, s32[2]{0:T(128)}, u32[]{:S(2)}) copy-start(s32[2]{0:T(128)} %param.24) | copy-start | bytes 28
  199.7 6.3 %collective-permute-start.40 = (bf16[48,512]{1,0:T(8,128)(2,1)S(1)}, bf16[48,512]{1,0:T(8,128)(2,1)S(1)}, u32[]{:S(2)}, u32[]{:S(2)}) collective-permute-start(bf16[48,512]{1,0:T(8,128)(2,1)S(1)} %get-tuple-element.62), channel_id=1, source_target_pairs={{0,7},{1,6},{2,5},{3,4},{4,3},{5,2},{6,1},{7,0},{8,15},{9,14},{10,... | collective-permute-start | bytes 147464 | tf_op jit(solution)/shard_map/ppermute | solution.py:203
  201.5 6.5 %collective-permute-start.39 = (bf16[48,512]{1,0:T(8,128)(2,1)S(1)}, bf16[48,512]{1,0:T(8,128)(2,1)S(1)}, u32[]{:S(2)}, u32[]{:S(2)}) collective-permute-start(bf16[48,512]{1,0:T(8,128)(2,1)S(1)} %get-tuple-element.63), channel_id=1, source_target_pairs={{0,5},{1,4},{2,7},{3,6},{4,1},{5,0},{6,3},{7,2},{8,13},{9,12},{10,... | collective-permute-start | bytes 147464 | tf_op jit(solution)/shard_map/ppermute | solution.py:203
  202.2 6.2 %collective-permute-start.38 = (bf16[48,512]{1,0:T(8,128)(2,1)S(1)}, bf16[48,512]{1,0:T(8,128)(2,1)S(1)}, u32[]{:S(2)}, u32[]{:S(2)}) collective-permute-start(bf16[48,512]{1,0:T(8,128)(2,1)S(1)} %get-tuple-element.64), channel_id=1, source_target_pairs={{0,3},{1,2},{2,1},{3,0},{4,7},{5,6},{6,5},{7,4},{8,11},{9,10},{10,... | collective-permute-start | bytes 147464 | tf_op jit(solution)/shard_map/ppermute | solution.py:203
  204.6 12.7 %collective-permute-start.30 = (bf16[256,512]{1,0:T(8,128)(2,1)S(1)}, bf16[256,512]{1,0:T(8,128)(2,1)S(1)}, u32[]{:S(2)}, u32[]{:S(2)}) collective-permute-start(bf16[256,512]{1,0:T(8,128)(2,1)S(1)} %fusion.97), channel_id=1, source_target_pairs={{0,2},{1,3},{2,0},{3,1},{4,6},{5,7},{6,4},{7,5},{8,10},{9,11},{10,... | collective-permute-start | bytes 786440 | tf_op jit(solution)/shard_map/ppermute | solution.py:38
  205.9 3.7 %collective-permute-start.37 = (bf16[48,512]{1,0:T(8,128)(2,1)S(1)}, bf16[48,512]{1,0:T(8,128)(2,1)S(1)}, u32[]{:S(2)}, u32[]{:S(2)}) collective-permute-start(bf16[48,512]{1,0:T(8,128)(2,1)S(1)} %get-tuple-element.65), channel_id=1, source_target_pairs={{0,1},{1,0},{2,3},{3,2},{4,5},{5,4},{6,7},{7,6},{8,9},{9,8},{10,11... | collective-permute-start | bytes 147464 | tf_op jit(solution)/shard_map/ppermute | solution.py:203
  206.0 9.7 %collective-permute-start.36 = (bf16[48,512]{1,0:T(8,128)(2,1)S(1)}, bf16[48,512]{1,0:T(8,128)(2,1)S(1)}, u32[]{:S(2)}, u32[]{:S(2)}) collective-permute-start(bf16[48,512]{1,0:T(8,128)(2,1)S(1)} %get-tuple-element.66), channel_id=1, source_target_pairs={{0,6},{1,7},{2,4},{3,5},{4,2},{5,3},{6,0},{7,1},{8,14},{9,15},{10,... | collective-permute-start | bytes 147464 | tf_op jit(solution)/shard_map/ppermute | solution.py:203
  208.0 7.7 %collective-permute-start.35 = (bf16[48,512]{1,0:T(8,128)(2,1)S(1)}, bf16[48,512]{1,0:T(8,128)(2,1)S(1)}, u32[]{:S(2)}, u32[]{:S(2)}) collective-permute-start(bf16[48,512]{1,0:T(8,128)(2,1)S(1)} %get-tuple-element.67), channel_id=1, source_target_pairs={{0,4},{1,5},{2,6},{3,7},{4,0},{5,1},{6,2},{7,3},{8,12},{9,13},{10,... | collective-permute-start | bytes 147464 | tf_op jit(solution)/shard_map/ppermute | solution.py:203
  208.3 7.4 %collective-permute-start.34 = (bf16[48,512]{1,0:T(8,128)(2,1)S(1)}, bf16[48,512]{1,0:T(8,128)(2,1)S(1)}, u32[]{:S(2)}, u32[]{:S(2)}) collective-permute-start(bf16[48,512]{1,0:T(8,128)(2,1)S(1)} %get-tuple-element.68), channel_id=1, source_target_pairs={{0,2},{1,3},{2,0},{3,1},{4,6},{5,7},{6,4},{7,5},{8,10},{9,11},{10,... | collective-permute-start | bytes 147464 | tf_op jit(solution)/shard_map/ppermute | solution.py:203

commit v4 on v3

--- a/solution.py
+++ b/solution.py
@@ -1,4 +1,5 @@
 import functools
+import math
 
 import jax
 import jax.numpy as jnp
@@ -143,6 +144,9 @@
     return arrived.reshape(values.shape)
 
 
+SHORT = pl.CostEstimate(flops=1, bytes_accessed=1, transcendentals=0)
+
+
 def gate(value, *after):
     return lax.optimization_barrier((value,) + after)[0]
 
@@ -151,47 +155,62 @@
     return pltpu.VMEM(shape, dtype)
 
 
-def dispatch_kernel(capacity, count, code_ref, *refs):
+def dispatch_kernel(capacity, count, share, section_ref, code_ref, *refs):
     blocks, held, sems = refs[:count], refs[count + 2], refs[count + 3]
-    copies = [
-        pltpu.make_async_copy(block, held.at[place], sems.at[place])
-        for place, block in enumerate(blocks)
-    ]
-    for copy in copies:
-        copy.start()
-    for place, copy in enumerate(copies):
-        copy.wait()
-        for which, out_ref in enumerate(refs[count : count + 2]):
+    copies = []
+    for place, block in enumerate(blocks):
+        rows = block.shape[0]
+        if share and place >= count // 2:
+            pieces = rows // share
+            copies.append([])
+            for step in range(pieces):
+                owner = lax.rem(section_ref[0] - step + pieces, pieces)
+                there = held.at[place, pl.ds(pl.multiple_of(owner * share, share), share)]
+                here = block.at[pl.ds(step * share, share)]
+                copies[-1].append(pltpu.make_async_copy(here, there, sems.at[place, step]))
+        else:
+            copies.append([pltpu.make_async_copy(block, held.at[place], sems.at[place, 0])])
+    for group in copies:
+        for copy in group:
+            copy.start()
+    for place, group in enumerate(copies):
+        for copy in group:
+            copy.wait()
+        picks = []
+        for which in range(2):
             line = which * count + place
             code = code_ref[line : line + 1, :]
             slot = lax.broadcasted_iota(jnp.int32, (capacity, code.shape[1]), 0)
-            pick = jnp.where(slot == code, 1.0, 0.0).astype(jnp.bfloat16)
-            rows = jnp.dot(pick, held[place], preferred_element_type=jnp.float32)
-            out_ref[place * capacity : (place + 1) * capacity, :] = rows.astype(jnp.bfloat16)
-
-
-def dispatch(code, blocks, capacity):
+            picks.append(jnp.where(slot == code, 1.0, 0.0))
+        pick = jnp.concatenate(picks, axis=0).astype(jnp.bfloat16)
+        rows = jnp.dot(pick, held[place], preferred_element_type=jnp.float32).astype(jnp.bfloat16)
+        for which, out_ref in enumerate(refs[count : count + 2]):
+            out_ref[place * capacity : (place + 1) * capacity, :] = rows[
+                which * capacity : (which + 1) * capacity
+            ]
+
+
+def dispatch(section, code, blocks, capacity, share=0):
     rows, features = blocks[0].shape
     count = len(blocks)
     picked = jax.ShapeDtypeStruct((count * capacity, features), jnp.bfloat16)
     return pl.pallas_call(
-        functools.partial(dispatch_kernel, capacity, count),
+        functools.partial(dispatch_kernel, capacity, count, share),
         out_shape=(picked, picked),
-        in_specs=[pl.BlockSpec(memory_space=pltpu.VMEM)]
+        in_specs=[
+            pl.BlockSpec(memory_space=pltpu.SMEM),
+            pl.BlockSpec(memory_space=pltpu.VMEM),
+        ]
         + [pl.BlockSpec(memory_space=pl.ANY)] * count,
         out_specs=[pl.BlockSpec(memory_space=pltpu.VMEM)] * 2,
         scratch_shapes=[
             vmem((count, rows, features), jnp.bfloat16),
-            pltpu.SemaphoreType.DMA((count,)),
+            pltpu.SemaphoreType.DMA((count, 4)),
         ],
         compiler_params=pltpu.CompilerParams(vmem_limit_bytes=32 * 1024 * 1024),
-        cost_estimate=pl.CostEstimate(
-            flops=4 * count * capacity * rows * features,
-            bytes_accessed=2 * count * (rows + 2 * capacity) * features,
-            transcendentals=0,
-        ),
+        cost_estimate=SHORT,
         name="dispatch",
-    )(code, *blocks)
+    )(section, code, *blocks)
 
 
 def send_home(part, codes, capacity):
@@ -223,9 +242,10 @@
     ]
     for copy in copies:
         copy.wait()
-    first = jnp.dot(picks[0], held[...], preferred_element_type=jnp.float32)
-    second = jnp.dot(picks[1], held[...], preferred_element_type=jnp.float32)
-    total[...] = gates_ref[:, 0:1] * first + gates_ref[:, 1:2] * second
+    pick = jnp.concatenate(picks, axis=0)
+    rows = position.shape[0]
+    both = jnp.dot(pick, held[...], preferred_element_type=jnp.float32)
+    total[...] = gates_ref[:, 0:1] * both[:rows] + gates_ref[:, 1:2] * both[rows:]
     width = features // split
     for step, out_ref in enumerate(outs):
         owner = lax.rem(section_ref[0] + step, split)
@@ -252,17 +272,15 @@
             pltpu.SemaphoreType.DMA((count,)),
         ],
         compiler_params=pltpu.CompilerParams(vmem_limit_bytes=32 * 1024 * 1024),
-        cost_estimate=pl.CostEstimate(
-            flops=4 * rows * count * capacity * features,
-            bytes_accessed=2 * count * capacity * features,
-            transcendentals=0,
-        ),
+        cost_estimate=SHORT,
         name="combine",
     )(section, position, gates, *blocks)
 
 
 def memory_kernel(count, section_ref, tokens_ref, gain_ref, *refs):
-    slices, out_ref, mixed = refs[:count], refs[count], refs[count + 1]
+    slices, out_ref, mixed, held, sem = refs[:count], refs[count], *refs[count + 1 :]
+    fetch = pltpu.make_async_copy(tokens_ref, held, sem)
+    fetch.start()
     me = section_ref[0]
     width = slices[0].shape[1]
     for step, piece in enumerate(slices):
@@ -270,72 +288,74 @@
         mixed[:, pl.ds(pl.multiple_of(owner * width, width), width)] = piece[...].astype(
             jnp.float32
         )
-    values = tokens_ref[...].astype(jnp.float32) + mixed[...]
+    fetch.wait()
+    values = held[...].astype(jnp.float32) + mixed[...]
     out_ref[...] = normalize(values, gain_ref[...]).astype(jnp.bfloat16)
 
 
-def make_memory(tokens, slices, gain):
-    me = lax.axis_index("section").astype(jnp.int32).reshape(1)
+def make_memory(me, tokens, slices, gain):
     return pl.pallas_call(
         functools.partial(memory_kernel, len(slices)),
         out_shape=jax.ShapeDtypeStruct(tokens.shape, jnp.bfloat16),
-        in_specs=[pl.BlockSpec(memory_space=pltpu.SMEM)]
-        + [pl.BlockSpec(memory_space=pltpu.VMEM)] * (2 + len(slices)),
+        in_specs=[
+            pl.BlockSpec(memory_space=pltpu.SMEM),
+            pl.BlockSpec(memory_space=pl.ANY),
+        ]
+        + [pl.BlockSpec(memory_space=pltpu.VMEM)] * (1 + len(slices)),
         out_specs=pl.BlockSpec(memory_space=pltpu.VMEM),
-        scratch_shapes=[vmem(tokens.shape, jnp.float32)],
+        scratch_shapes=[
+            vmem(tokens.shape, jnp.float32),
+            vmem(tokens.shape, tokens.dtype),
+            pltpu.SemaphoreType.DMA,
+        ],
         compiler_params=pltpu.CompilerParams(vmem_limit_bytes=20 * 1024 * 1024),
+        cost_estimate=SHORT,
         name="memory",
     )(me, tokens, gain[None], *slices)
 
 
-def attend_kernel(
-    place_ref,
-    lengths_ref,
-    query_ref,
-    near_ref,
-    far_ref,
-    key_own,
-    key_other,
-    value_own,
-    value_other,
-    out_ref,
-    source,
-    key_weight,
-    value_weight,
-    keys,
-    values,
-    sems,
-):
+def attend_kernel(project, place_ref, lengths_ref, query_ref, *refs):
+    near_ref, far_ref, key_own, key_other, value_own, value_other = refs[:6]
     y, core, sentence = place_ref[0], place_ref[1], place_ref[2]
+    if project:
+        done_ref, out_own, out_other, sent_ref, kept_ref = refs[6:11]
+        source, key_weight, value_weight, keys, values, sems, out_weight, context = refs[11:]
+    else:
+        out_ref = refs[6]
+        source, key_weight, value_weight, keys, values, sems = refs[7:]
     rows = near_ref.shape[0]
     depth = key_own.shape[0]
-    moves = (
+    moves = [
         (near_ref, source.at[pl.ds(0, rows)]),
         (far_ref, source.at[pl.ds(rows, rows)]),
         (key_own, key_weight.at[y]),
         (key_other, key_weight.at[1 - y]),
         (value_own, value_weight.at[y]),
         (value_other, value_weight.at[1 - y]),
-    )
+    ]
+    if project:
+        moves += [(out_own, out_weight.at[y]), (out_other, out_weight.at[1 - y])]
     copies = [
         pltpu.make_async_copy(here, there, sems.at[i]) for i, (here, there) in enumerate(moves)
     ]
     for copy in copies:
         copy.start()
 
-    def project(weight, result):
+    def linear(weight, result):
         total = jnp.dot(source[:, :depth], weight[0], preferred_element_type=jnp.float32)
         total += jnp.dot(source[:, depth:], weight[1], preferred_element_type=jnp.float32)
         result[...] = total.astype(jnp.bfloat16)
 
     for copy in copies[:4]:
         copy.wait()
-    project(key_weight, keys)
-    for copy in copies[4:]:
+    linear(key_weight, keys)
+    for copy in copies[4:6]:
         copy.wait()
-    project(value_weight, values)
-
-    column = lax.broadcasted_iota(jnp.int32, (query_ref.shape[0], 2 * rows), 1)
+    linear(value_weight, values)
+
+    targets = query_ref.shape[0]
+    mine = pl.ds(pl.multiple_of(sentence * targets, targets), targets)
+    column = lax.broadcasted_iota(jnp.int32, (targets, 2 * rows), 1)
     position = jnp.where(column < rows, column + core * rows, column - core * rows)
     valid = position < lengths_ref[sentence]
     for head in range(query_ref.shape[1] // HEAD_DIM):
@@ -344,37 +364,140 @@
         scores = jnp.where(valid, scores, -1e30)
         weights = jnp.exp(scores - jnp.max(scores, axis=-1, keepdims=True))
         probs = (weights / jnp.sum(weights, axis=-1, keepdims=True)).astype(jnp.bfloat16)
-        context = jnp.dot(probs, values[:, span], preferred_element_type=jnp.float32)
-        out_ref[:, span] = context.astype(jnp.bfloat16)
-
-
-def attend_sentence(place, lengths, query, near, far, key_pair, value_pair):
+        result = jnp.dot(probs, values[:, span], preferred_element_type=jnp.float32)
+        if project:
+            context[mine, span] = result.astype(jnp.bfloat16)
+        else:
+            out_ref[:, span] = result.astype(jnp.bfloat16)
+
+    if project:
+        others = pl.ds(pl.multiple_of((1 - sentence) * targets, targets), targets)
+        context[others, :] = done_ref[...]
+        for copy in copies[6:]:
+            copy.wait()
+        columns = sent_ref.shape[2]
+        x = 1 - sentence
+        for which in range(2):
+            half = jnp.where(which == 0, x, 1 - x)
+            for out, side in ((sent_ref, 1 - core), (kept_ref, core)):
+                span = pl.ds(pl.multiple_of(side * columns, columns), columns)
+                part = jnp.dot(
+                    context[...], out_weight[half, :, span], preferred_element_type=jnp.float32
+                )
+                out[which] = part.astype(out.dtype)
+
+
+def attend_sentence(place, lengths, query, near, far, key_pair, value_pair, done=None, out_pair=()):
     rows, features = near.shape
     depth, width = key_pair[0].shape
+    project = done is not None
     hold = pl.BlockSpec(memory_space=pl.ANY)
     smem = pl.BlockSpec(memory_space=pltpu.SMEM)
     full = pl.BlockSpec(memory_space=pltpu.VMEM)
+    operands = [place, lengths, query, near, far, *key_pair, *value_pair]
+    in_specs = [smem, smem, full] + [hold] * 6
+    scratch = [
+        vmem((2 * rows, features), jnp.bfloat16),
+        vmem((2, depth, width), jnp.bfloat16),
+        vmem((2, depth, width), jnp.bfloat16),
+        vmem((2 * rows, width), jnp.bfloat16),
+        vmem((2 * rows, width), jnp.bfloat16),
+        pltpu.SemaphoreType.DMA((8,)),
+    ]
+    if project:
+        targets = 2 * query.shape[0]
+        columns = out_pair[0].shape[1] // 2
+        operands += [done, *out_pair]
+        in_specs += [full, hold, hold]
+        scratch += [
+            vmem((2,) + out_pair[0].shape, jnp.bfloat16),
+            vmem((targets, width), jnp.bfloat16),
+        ]
+        out_shape = (
+            jax.ShapeDtypeStruct((2, targets, columns), jnp.bfloat16),
+            jax.ShapeDtypeStruct((2, targets, columns), jnp.float32),
+        )
+        out_specs = [full, full]
+    else:
+        out_shape, out_specs = jax.ShapeDtypeStruct(query.shape, jnp.bfloat16), full
     return pl.pallas_call(
-        attend_kernel,
-        out_shape=jax.ShapeDtypeStruct(query.shape, jnp.bfloat16),
-        in_specs=[smem, smem, full] + [hold] * 6,
-        out_specs=full,
+        functools.partial(attend_kernel, project),
+        out_shape=out_shape,
+        in_specs=in_specs,
+        out_specs=out_specs,
+        scratch_shapes=scratch,
+        compiler_params=pltpu.CompilerParams(vmem_limit_bytes=32 * 1024 * 1024),
+        cost_estimate=SHORT,
+        name="attend_sentence",
+    )(*operands)
+
+
+def backward_kernel(split, section_ref, own_ref, core_ref, pre_own, pre_core, out_ref, in_ref, *refs):
+    outs = refs[:split]
+    grads, pre_act, weight_out, weight_in, slope, sems = refs[split:]
+    rows = own_ref.shape[0]
+    hidden, features = weight_out.shape
+    width = features // split
+    chunk = hidden // 4
+    moves = [
+        (own_ref, grads.at[pl.ds(0, rows)]),
+        (core_ref, grads.at[pl.ds(rows, rows)]),
+        (pre_own, pre_act.at[pl.ds(0, rows)]),
+        (pre_core, pre_act.at[pl.ds(rows, rows)]),
+    ]
+    for part in range(4):
+        span = pl.ds(part * chunk, chunk)
+        moves.append((out_ref.at[span], weight_out.at[span]))
+    moves.append((in_ref, weight_in))
+    copies = [
+        pltpu.make_async_copy(here, there, sems.at[i]) for i, (here, there) in enumerate(moves)
+    ]
+    for copy in copies:
+        copy.start()
+    for copy in copies[:4]:
+        copy.wait()
+    scale = (2.0 / math.pi) ** 0.5
+    for part in range(4):
+        copies[4 + part].wait()
+        span = slice(part * chunk, (part + 1) * chunk)
+        back = contract_last(grads[...], weight_out[span, :])
+        value = pre_act[:, span]
+        square = value * value
+        bent = jnp.tanh(scale * (value + 0.044715 * (square * value)))
+        inner = scale * (1.0 + 3.0 * 0.044715 * square)
+        rise = 0.5 * (1.0 + bent) + 0.5 * value * ((1.0 - bent * bent) * inner)
+        slope[:, span] = (back * rise).astype(jnp.bfloat16)
+    copies[8].wait()
+    for step in range(split):
+        owner = lax.rem(section_ref[0] + step, split)
+        start = pl.multiple_of(owner * width, width)
+        part = contract_last(slope[...], weight_in[pl.ds(start, width), :])
+        outs[step][...] = part.astype(outs[step].dtype)
+
+
+def expert_backward(section, grads_own, grads_core, pre_own, pre_core, weight_out, weight_in, split):
+    rows = 2 * grads_own.shape[0]
+    hidden, features = weight_out.shape
+    hold = pl.BlockSpec(memory_space=pl.ANY)
+    width = features // split
+    kinds = [jnp.float32] + [jnp.bfloat16] * (split - 1)
+    return pl.pallas_call(
+        functools.partial(backward_kernel, split),
+        out_shape=tuple(jax.ShapeDtypeStruct((rows, width), kind) for kind in kinds),
+        in_specs=[pl.BlockSpec(memory_space=pltpu.SMEM)] + [hold] * 6,
+        out_specs=[pl.BlockSpec(memory_space=pltpu.VMEM)] * split,
         scratch_shapes=[
-            vmem((2 * rows, features), jnp.bfloat16),
-            vmem((2, depth, width), jnp.bfloat16),
-            vmem((2, depth, width), jnp.bfloat16),
-            vmem((2 * rows, width), jnp.bfloat16),
-            vmem((2 * rows, width), jnp.bfloat16),
-            pltpu.SemaphoreType.DMA((6,)),
+            vmem((rows, features), jnp.bfloat16),
+            vmem((rows, hidden), jnp.float32),
+            vmem((hidden, features), jnp.bfloat16),
+            vmem((features, hidden), jnp.bfloat16),
+            vmem((rows, hidden), jnp.bfloat16),
+            pltpu.SemaphoreType.DMA((9,)),
         ],
-        compiler_params=pltpu.CompilerParams(vmem_limit_bytes=32 * 1024 * 1024),
-        cost_estimate=pl.CostEstimate(
-            flops=8 * rows * features * width,
-            bytes_accessed=4 * rows * features + 8 * depth * width,
-            transcendentals=query.shape[0] * 8 * rows,
-        ),
-        name="attend_sentence",
-    )(place, lengths, query, near, far, *key_pair, *value_pair)
+        compiler_params=pltpu.CompilerParams(vmem_limit_bytes=40 * 1024 * 1024),
+        cost_estimate=SHORT,
+        name="expert_backward",
+    )(section, grads_own, grads_core, pre_own, pre_core, weight_out, weight_in)
 
 
 def small_body(
@@ -411,24 +534,33 @@
     size = group_size
     near_codes = (0, 2, 4, 6)
     core_codes = (1, 3, 5, 7)
+    core, x = d % 2, d // 2
+    which_section = section.astype(jnp.int32).reshape(1)
 
     token_y = swap(tokens, "expert", 1)
     token_x = swap(tokens, "dp", 2)
-    all_ids = lax.all_gather(expert_ids.T, ("expert", "dp"), axis=0)
+    ids_y = jnp.stack([expert_ids.T, swap(expert_ids.T, "expert", 1)])
+    ids_x = swap(ids_y, "dp", 2)
     token_far = swap(token_y, "dp", 2)
 
     share = token_count // sections
     grad_share = lax.dynamic_slice_in_dim(out_grad, section * share, share, 0)
     grad_fetched = swap(gate(grad_share, token_y), "expert", 1)
     key_other = swap(gate(key_own, token_y), "expert", 1)
-    grad_y = lax.all_gather(grad_fetched, "section", axis=0, tiled=True)
+    states = dec_states[0]
+    normed = normalize(states.astype(jnp.float32), norm_gain[0]).astype(jnp.bfloat16)
+    quarter = normed.shape[0] // lax.axis_size("dp")
+    asked = lax.dynamic_slice(normed, (d * quarter, (1 - y) * half), (quarter, half))
+    asked_here = swap(gate(asked, grad_fetched), "expert", 1)
+    grad_y = jnp.concatenate(
+        [grad_fetched] + [shift(grad_fetched, "section", step) for step in range(1, sections)],
+        axis=0,
+    )
     grad_x = swap(gate(out_grad, token_far), "dp", 2)
 
     row = lax.broadcasted_iota(jnp.int32, (token_count, token_count), 0)
     column = lax.broadcasted_iota(jnp.int32, (token_count, token_count), 1)
-    ids = jnp.stack(
-        [lax.dynamic_index_in_dim(all_ids, here ^ code, 0, False) for code in near_codes]
-    )
+    ids = jnp.stack([ids_y[0], ids_x[0], ids_y[1], ids_x[1]])
     named_there = jnp.concatenate([(ids == here).any(axis=1), (ids == (here ^ 1)).any(axis=1)])
     before = jnp.dot(
         named_there.astype(jnp.bfloat16),
@@ -452,107 +584,79 @@
         part = jnp.dot(hidden, weight_out, preferred_element_type=jnp.float32)
         return pre_act, part.astype(jnp.bfloat16)
 
-    def backward(grads, pre_act):
-        back = contract_last(grads, weight_out)
-        slope = jax.vjp(jax.nn.gelu, pre_act)[1](back)[0].astype(jnp.bfloat16)
-        return contract_last(slope, weight_in).astype(jnp.bfloat16)
-
-    rows_own, rows_sent = dispatch(code, [tokens, token_x, token_y, token_far], capacity)
+    rows_own, rows_sent = dispatch(
+        which_section, code, [tokens, token_x, token_y, token_far], capacity
+    )
     rows_core = swap(rows_sent, "dp", 1)
     pre_own, part_own = forward(rows_own)
     pre_core, part_core = forward(rows_core)
     part_core = gate(part_core, key_other, grad_x)
     home = send_home(part_own, near_codes, capacity) + send_home(part_core, core_codes, capacity)
 
-    which_section = section.astype(jnp.int32).reshape(1)
-    cuts = combine(which_section, position, gate_weights, home, sections, jnp.float32)
+    asked_pair = jnp.concatenate([asked_here, swap(gate(asked_here, token_far), "dp", 2)], axis=0)
+    asked_rows = jnp.concatenate([asked_pair, swap(asked_pair, "dp", 1)], axis=0)
+    query_there = jnp.dot(asked_rows, query_own, preferred_element_type=jnp.float32)
+
+    held_gates = gate(gate_weights, query_there)
+    cuts = combine(which_section, position, held_gates, home, sections, jnp.float32)
     mixed_sum = cuts[0]
     for step in range(1, sections):
         mixed_sum = mixed_sum + shift(cuts[step], "section", step).astype(jnp.float32)
     mixed_slice = mixed_sum.astype(jnp.bfloat16)
     slices = [mixed_slice] + [shift(mixed_slice, "section", step) for step in range(1, sections)]
 
-    value_other = swap(gate(value_own, *home), "expert", 1)
-    grad_far = swap(gate(grad_y, *home), "dp", 2)
-    states = dec_states[0]
-    normed = normalize(states.astype(jnp.float32), norm_gain[0]).astype(jnp.bfloat16)
-    quarter = normed.shape[0] // lax.axis_size("dp")
-    asked = lax.dynamic_slice(normed, (d * quarter, (1 - y) * half), (quarter, half))
-    asked_here = swap(gate(asked, *home), "expert", 1)
-    asked_rows = lax.all_gather(asked_here, "dp", axis=0, tiled=True)
-    query_there = jnp.dot(asked_rows, query_own, preferred_element_type=jnp.float32)
-    query_other = swap(query_there.astype(jnp.bfloat16), "expert", 1)
+    value_other = swap(gate(value_own, cuts[0]), "expert", 1)
+    grad_far = swap(gate(grad_y, cuts[0]), "dp", 2)
+    query_back = swap(gate(query_there.astype(jnp.bfloat16), mixed_slice), "expert", 1)
     out_other = swap(gate(out_own, value_other), "expert", 1)
+
+    parts = []
+    for place in range(lax.axis_size("dp")):
+        code_here = d ^ place
+        at = (code_here >> 1) + 2 * (code_here & 1)
+        parts.append(lax.dynamic_slice_in_dim(query_back, at * quarter, quarter, 0))
     normed_own = lax.dynamic_slice_in_dim(normed, y * half, half, 1)
     query = (
         jnp.dot(normed_own, query_own, preferred_element_type=jnp.float32)
-        + query_other.astype(jnp.float32)
+        + jnp.concatenate(parts, axis=0).astype(jnp.float32)
     ).astype(jnp.bfloat16)
 
     grads_own, grads_sent = dispatch(
-        gate(code, mixed_slice), [out_grad, grad_x, grad_y, grad_far], capacity
+        which_section, gate(code, mixed_slice), [out_grad, grad_x, grad_y, grad_far], capacity, share
     )
     grads_core = swap(grads_sent, "dp", 1)
-    backward_own = backward(grads_own, pre_own)
-    backward_core = backward(grads_core, pre_core)
-    held_tokens = gate(tokens, value_other, backward_own, backward_core)
-    memory = make_memory(held_tokens, slices, final_gain)
-
-    core, x = d % 2, d // 2
+    backward_cuts = expert_backward(
+        which_section, grads_own, grads_core, pre_own, pre_core, weight_out, weight_in, sections
+    )
+    held_tokens = gate(tokens, value_other, backward_cuts[0])
+    memory = make_memory(which_section, held_tokens, slices, final_gain)
+    backward_arrived = [
+        shift(gate(backward_cuts[step], *slices), "section", step) for step in range(1, sections)
+    ]
+
     memory_x = swap(memory, "dp", 2)
     memory_core = swap(memory, "dp", 1)
-    memory_far = swap(memory_x, "dp", 1)
-
-    def sentence(which, near, far):
+
+    def sentence(which, near, far, *rest):
         place = jnp.stack([y, core, which]).astype(jnp.int32)
         rows_of = lax.dynamic_slice_in_dim(query, which * TGT_LEN, TGT_LEN, 0)
-        return attend_sentence(
-            place, src_lengths, rows_of, near, far, (key_own, key_other), (value_own, value_other)
-        )
+        pairs = (key_own, key_other), (value_own, value_other)
+        return attend_sentence(place, src_lengths, rows_of, near, far, *pairs, *rest)
 
     context_own = sentence(x, memory, memory_core)
-    context_other = sentence(1 - x, gate(memory_x, out_other), memory_far)
-
-    backward_part = jnp.concatenate([backward_own, backward_core], axis=0)
-    backward_part = gate(backward_part, context_own)
-    width = half * 2 // sections
-
-    def piece(owner):
-        return lax.dynamic_slice_in_dim(backward_part, owner * width, width, 1)
-
-    arrived = [
-        shift(piece(lax.rem(section + step, sections)), "section", step)
-        for step in range(1, sections)
-    ]
-    backward_sum = gate(piece(section), context_other).astype(jnp.float32)
-    for part in arrived:
+    memory_far = swap(gate(memory_x, context_own), "dp", 1)
+    sent, kept = sentence(1 - x, memory_x, memory_far, context_own, (out_own, out_other))
+
+    from_core = swap(sent, "dp", 1).astype(jnp.float32)
+    from_x = swap((kept[1] + from_core[1]).astype(jnp.bfloat16), "dp", 2)
+    attended = kept[0] + from_core[0] + from_x.astype(jnp.float32)
+    dec_out = add_residual(attended, states, tgt_lengths)
+
+    backward_sum = gate(backward_cuts[0], kept)
+    for part in backward_arrived:
         backward_sum = backward_sum + part.astype(jnp.float32)
-    backward_slice = backward_sum.astype(jnp.bfloat16)
-    grads_home = send_home(backward_slice, near_codes + core_codes, capacity)
+    grads_home = send_home(backward_sum.astype(jnp.bfloat16), near_codes + core_codes, capacity)
     (token_grad,) = combine(which_section, position, gate_weights, grads_home, 1, jnp.bfloat16)
-
-    context = jnp.concatenate(
-        [jnp.where(x == 0, context_own, context_other), jnp.where(x == 0, context_other, context_own)],
-        axis=0,
-    )
-    columns = feature_count // lax.axis_size("dp")
-
-    def project(weight, which):
-        part = lax.dynamic_slice_in_dim(weight, which * columns, columns, 1)
-        return jnp.dot(context, part, preferred_element_type=jnp.float32)
-
-    def by_x(which):
-        own, other = project(out_own, which), project(out_other, which)
-        first = y == 0
-        return jnp.stack([jnp.where(first, own, other), jnp.where(first, other, own)])
-
-    sent = by_x(1 - core).astype(jnp.bfloat16)
-    total = by_x(core) + swap(sent, "dp", 1).astype(jnp.float32)
-    last = lax.dynamic_index_in_dim(total, 1 - x, 0, False).astype(jnp.bfloat16)
-    attended = lax.dynamic_index_in_dim(total, x, 0, False) + swap(last, "dp", 2).astype(
-        jnp.float32
-    )
-    dec_out = add_residual(attended, states, tgt_lengths)
     return (dec_out[None], token_grad)
 
 

time: 220 us -> 205 us (0.932)
  blocking collectives: 35.9 us -> 0 us
  matrix products: 29.3 us -> 9.39 us
  local copies, waits for them, and re-layouts: 9.82 us -> 24.9 us
  starting transfers between devices: 40.9 us -> 54.8 us
  Pallas kernels: 18.8 us -> 27.3 us
  waiting for transfers between devices: 70.9 us -> 77 us
  other arithmetic: 12.3 us -> 9.93 us
    all_gather x3 -> x0, blocking collectives: 35.9 us -> none  [the longest x1 17 us: small_body(): grad_y = lax.all_gather(grad_fetched, 'section', axis=0, tiled=True)]
    dot_general x6 -> x0, matrix products: 19.3 us -> none  [the longest x2 16 us: contract_last(): lax.dot_general(left, right, (((1,), (1,)), ((), ())), preferred_element_...]
    ppermute x9 -> x12, waiting for transfers between devices: 29.2 us -> 48.5 us  [shift(): lax.ppermute(value, axis, [(i, (i + step) % size) for i in range(size)])]
    ppermute x18 -> x22, waiting for transfers between devices: 31.6 us -> 16.5 us  [swap(): return lax.ppermute(value, axis, [(i, i ^ mask) for i in range(size)])]
    unnamed x48 -> x85, local copies, waits for them, and re-layouts: 7.47 us -> 19.3 us
    pallas_call x4 -> x5, Pallas kernels: 11.1 us -> 20.3 us  [the longest x2 8.07 us: attend_sentence(): pl.pallas_call(functools.partial(attend_kernel, project), out_shape=out_s...]
    ppermute x9 -> x12, starting transfers between devices: 12.3 us -> 19.3 us  [shift(): lax.ppermute(value, axis, [(i, (i + step) % size) for i in range(size)])]
    ppermute x18 -> x22, starting transfers between devices: 15.7 us -> 22 us  [swap(): return lax.ppermute(value, axis, [(i, i ^ mask) for i in range(size)])]
  transfers between devices with their start and end apart: 41 -> 48, of which waited for: 10 -> 17; matrix products, arithmetic and copies ran while one was open for 20% -> 13% of each run, Pallas kernels for 9% -> 12%
where the time goes in v4:
time: 205 us
  waiting for transfers between devices  77 us (38%)
  starting transfers between devices  54.8 us (27%)
  Pallas kernels  27.3 us (13%)
  local copies, waits for them, and re-layouts  24.9 us (12%)
  other arithmetic  9.93 us (5%)
  matrix products  9.39 us (5%)
    ppermute x12, waiting for transfers between devices, shift(): lax.ppermute(value, axis, [(i, (i + step) % size) for i in range(size)])  48.5 us
    ppermute x22, starting transfers between devices, swap(): return lax.ppermute(value, axis, [(i, i ^ mask) for i in range(size)])  22 us
    unnamed x85, local copies, waits for them, and re-layouts  19.3 us
    ppermute x12, starting transfers between devices, shift(): lax.ppermute(value, axis, [(i, (i + step) % size) for i in range(size)])  19.3 us
    ppermute x22, waiting for transfers between devices, swap(): return lax.ppermute(value, axis, [(i, i ^ mask) for i in range(size)])  16.5 us
    ppermute x14, starting transfers between devices, send_home(): lax.ppermute(block, ('expert', 'dp'), [(i, i ^ code) for i in range(size)])  13.4 us
    ppermute x14, waiting for transfers between devices, send_home(): lax.ppermute(block, ('expert', 'dp'), [(i, i ^ code) for i in range(size)])  12.1 us
    pallas_call x2, Pallas kernels, attend_sentence(): pl.pallas_call(functools.partial(attend_kernel, project), out_shape=out_s...  8.07 us
  transfers between devices with their start and end apart: 48, of which 17 were waited for; matrix products, arithmetic and copies ran while one was open for 13% of the time, Pallas kernels for 12%

profile of v4, /device:TPU:0, one launch (start us, length us, event | category | flops | bytes accessed | tf_op | source)
XLA Modules:
  0.0 204.6 jit_solution(14679822305051706814)
XLA Ops:
  0.7 3.0 %collective-permute-start.8 = (bf16[128,2048]{1,0:T(8,128)(2,1)}, bf16[128,2048]{1,0:T(8,128)(2,1)S(1)}, u32[]{:S(2)}, u32[]{:S(2)}) collective-permute-start(bf16[128,2048]{1,0:T(8,128)(2,1)} %tokens_ref), channel_id=1, source_target_pairs={{0,2},{1,3},{2,0},{3,1},{4,6},{5,7},{6,4},{7,5},{8,10},{9,11},{10,... | collective-permute-start | bytes 1572872 | tf_op jit(solution)/shard_map/ppermute | solution.py:39
  3.7 1.5 collective-permute-start
  7.2 1.4 convert_reduce_fusion
  8.7 1.6 fusion.3
  11.3 2.6 %fusion.5 = bf16[256,2048]{1,0:T(8,128)(2,1)} fusion(bf16[1,256,2048]{2,1,0:T(8,128)(2,1)} %param.22, f32[2048]{0:T(1024)} %bitcast.85, f32[256]{0:T(256)S(1)} %add_rsqrt_fusion, f32[256]{0:T(256)S(1)} %broadcast_multiply_fusion), kind=kLoop, calls=%fused_computation.9 | loop fusion | flops 2621440 | bytes 2107392 | tf_op jit(solution)/shard_map/convert_element_type | solution.py:551
  13.9 3.5 %collective-permute-done.6 = s32[2,128]{1,0:T(2,128)S(1)} collective-permute-done((s32[2,128]{1,0:T(2,128)}, s32[2,128]{1,0:T(2,128)S(1)}, u32[]{:S(2)}, u32[]{:S(2)}) %collective-permute-start.6) | collective-permute-done | bytes 1056 | tf_op jit(solution)/shard_map/ppermute | solution.py:39
  19.6 1.7 collective-permute-start.1
  21.6 1.1 collective-permute-start.13
  23.6 2.6 %collective-permute-done.1 = bf16[32,2048]{1,0:T(8,128)(2,1)S(1)} collective-permute-done((bf16[32,2048]{1,0:T(8,128)(2,1)S(1)}, bf16[32,2048]{1,0:T(8,128)(2,1)S(1)}, u32[]{:S(2)}, u32[]{:S(2)}) %collective-permute-start.1) | collective-permute-done | bytes 131104 | tf_op jit(solution)/shard_map/ppermute | solution.py:39
  26.1 1.7 collective-permute-start.2
  27.8 1.6 collective-permute-start.24
  30.0 4.8 %collective-permute-done.24 = bf16[32,2048]{1,0:T(8,128)(2,1)S(1)} collective-permute-done((bf16[32,2048]{1,0:T(8,128)(2,1)S(1)}, bf16[32,2048]{1,0:T(8,128)(2,1)S(1)}, u32[]{:S(2)}, u32[]{:S(2)}) %collective-permute-start.24) | collective-permute-done | bytes 131104 | tf_op jit(solution)/shard_map/ppermute | solution.py:34
  34.8 2.9 %collective-permute-start.25 = (bf16[32,2048]{1,0:T(8,128)(2,1)S(1)}, bf16[32,2048]{1,0:T(8,128)(2,1)S(1)}, u32[]{:S(2)}, u32[]{:S(2)}) collective-permute-start(bf16[32,2048]{1,0:T(8,128)(2,1)S(1)} %collective-permute-done.1), channel_id=1, source_target_pairs={{0,16},{8,24},{16,0},{24,8},{1,17},{9,25},{17,1},{25,9},{2,18},{10... | collective-permute-start | bytes 393224 | tf_op jit(solution)/shard_map/ppermute | solution.py:34
  38.3 3.7 %collective-permute-done.25 = bf16[32,2048]{1,0:T(8,128)(2,1)S(1)} collective-permute-done((bf16[32,2048]{1,0:T(8,128)(2,1)S(1)}, bf16[32,2048]{1,0:T(8,128)(2,1)S(1)}, u32[]{:S(2)}, u32[]{:S(2)}) %collective-permute-start.25) | collective-permute-done | bytes 131104 | tf_op jit(solution)/shard_map/ppermute | solution.py:34
  43.4 3.7 %collective-permute-done.26 = bf16[32,2048]{1,0:T(8,128)(2,1)S(1)} collective-permute-done((bf16[32,2048]{1,0:T(8,128)(2,1)S(1)}, bf16[32,2048]{1,0:T(8,128)(2,1)S(1)}, u32[]{:S(2)}, u32[]{:S(2)}) %collective-permute-start.26) | collective-permute-done | bytes 131104 | tf_op jit(solution)/shard_map/ppermute | solution.py:34
  47.7 1.5 collective-permute-start.14
  49.2 1.8 dispatch.2
  51.7 3.2 %fusion.67.pre_own = f32[192,1024]{1,0:T(8,128)S(1)} fusion(bf16[192,2048]{1,0:T(8,128)(2,1)S(1)} %get-tuple-element.38, bf16[1,2048,1024]{2,1,0:T(8,128)(2,1)} %param.19), kind=kOutput, calls=%fused_computation.101 | convolution fusion | flops 805306368 | bytes 5767168 | tf_op jit(solution)/shard_map/dot_general | solution.py:582
  54.9 1.1 convolution_convert_fusion.1
  56.7 1.4 collective-permute-start.11
  58.2 2.2 %collective-permute-done.4 = bf16[64,1024]{1,0:T(8,128)(2,1)S(1)} collective-permute-done((bf16[64,1024]{1,0:T(8,128)(2,1)S(1)}, bf16[64,1024]{1,0:T(8,128)(2,1)S(1)}, u32[]{:S(2)}, u32[]{:S(2)}) %collective-permute-start.4) | collective-permute-done | bytes 131104 | tf_op jit(solution)/shard_map/ppermute | solution.py:39
  60.5 1.6 collective-permute-start.9
  63.1 1.1 convolution_convert_fusion
  66.8 2.0 collective-permute-start.18
  70.3 1.3 collective-permute-start.16
  71.9 1.1 fusion.7
  73.2 1.6 collective-permute-done.18.refs_7_
  74.7 4.7 %collective-permute-done.17.refs_6_ = bf16[48,2048]{1,0:T(8,128)(2,1)} collective-permute-done((bf16[48,2048]{1,0:T(8,128)(2,1)}, bf16[48,2048]{1,0:T(8,128)(2,1)}, u32[]{:S(2)}, u32[]{:S(2)}) %collective-permute-start.17) | collective-permute-done | bytes 196640 | tf_op jit(solution)/shard_map/ppermute | solution.py:222
  81.3 2.8 %combine.2 = (f32[128,512]{1,0:T(8,128)S(1)}, bf16[128,512]{1,0:T(8,128)(2,1)S(1)}, bf16[128,512]{1,0:T(8,128)(2,1)S(1)}, bf16[128,512]{1,0:T(8,128)(2,1)S(1)}) custom-call(s32[1]{0:T(128)} %bitcast.8.section_ref, s32[128,2]{1,0:T(8,128)S(1)} %multiply_add_fusion.position_ref, f32[128,2]{1,0:T(8,128)S(1)} %copy.32.gates_ref, ...), custom_call_target="tpu_custom_call" | custom-call | flops 1 | bytes 1 | tf_op jit(solution)/shard_map/combine/pallas_call | solution.py:263
  85.1 1.6 collective-permute-start.23
  86.7 1.1 collective-permute-start.19
  87.8 2.5 %collective-permute-start.20 = (bf16[128,512]{1,0:T(8,128)(2,1)S(1)}, bf16[128,512]{1,0:T(8,128)(2,1)S(1)}, u32[]{:S(2)}, u32[]{:S(2)}) collective-permute-start(bf16[128,512]{1,0:T(8,128)(2,1)S(1)} %get-tuple-element.45), channel_id=1, source_target_pairs={{0,16},{8,24},{16,0},{24,8},{1,17},{9,25},{17,1},{25,9},{2,18},{10... | collective-permute-start | bytes 393224 | tf_op jit(solution)/shard_map/ppermute | solution.py:34
  90.2 1.9 collective-permute-start.21
  92.1 2.8 %collective-permute-done.19 = bf16[128,512]{1,0:T(8,128)(2,1)S(1)} collective-permute-done((bf16[128,512]{1,0:T(8,128)(2,1)S(1)}, bf16[128,512]{1,0:T(8,128)(2,1)S(1)}, u32[]{:S(2)}, u32[]{:S(2)}) %collective-permute-start.19) | collective-permute-done | bytes 131104 | tf_op jit(solution)/shard_map/ppermute | solution.py:34
  94.9 4.2 %collective-permute-done.20 = bf16[128,512]{1,0:T(8,128)(2,1)S(1)} collective-permute-done((bf16[128,512]{1,0:T(8,128)(2,1)S(1)}, bf16[128,512]{1,0:T(8,128)(2,1)S(1)}, u32[]{:S(2)}, u32[]{:S(2)}) %collective-permute-start.20) | collective-permute-done | bytes 131104 | tf_op jit(solution)/shard_map/ppermute | solution.py:34
  99.2 1.0 copy-done.24
  100.3 3.1 %dispatch.3 = (bf16[192,2048]{1,0:T(8,128)(2,1)S(1)}, bf16[192,2048]{1,0:T(8,128)(2,1)}) custom-call(s32[1]{0:T(128)} %bitcast.8.section_ref, s32[8,128]{1,0:T(8,128)S(1)} %fusion.6.code_ref, bf16[128,2048]{1,0:T(8,128)(2,1)} %refs_0_.3, bf16[128,2048]{1,0:T(8,128)(2,1)S(1)} %copy-done.24, bf16[128,2048]{1,0:T(8,128)(2,1)} %constant_dynamic-update-slice_fusion.refs_2_, ...), custom_call_target="tpu_custom_call" | custom-call | flops 1 | bytes 1 | tf_op jit(solution)/shard_map/dispatch/pallas_call | solution.py:197
  105.2 3.9 %collective-permute-start.31 = (bf16[128,512]{1,0:T(8,128)(2,1)S(1)}, bf16[128,512]{1,0:T(8,128)(2,1)S(1)}, u32[]{:S(2)}, u32[]{:S(2)}) collective-permute-start(bf16[128,512]{1,0:T(8,128)(2,1)S(1)} %add_convert_fusion.2.refs_0_), channel_id=1, source_target_pairs={{0,24},{8,0},{16,8},{24,16},{1,25},{9,1},{17,9},{25,17},{2,26},{10... | collective-permute-start | bytes 393224 | tf_op jit(solution)/shard_map/ppermute | solution.py:34
  109.3 1.8 collective-permute-done.23.refs_5_
  112.3 2.5 %collective-permute-start.35 = (bf16[512,1024]{1,0:T(8,128)(2,1)}, bf16[512,1024]{1,0:T(8,128)(2,1)}, u32[]{:S(2)}, u32[]{:S(2)}) collective-permute-start(bf16[512,1024]{1,0:T(8,128)(2,1)} %bitcast.79), channel_id=1, source_target_pairs={{0,4},{4,0},{1,5},{5,1},{2,6},{6,2},{3,7},{7,3},{8,12},{12,8},{9,1... | collective-permute-start | bytes 3145736 | tf_op jit(solution)/shard_map/ppermute | solution.py:39
  114.8 2.2 %copy-done.2 = bf16[1,2048,1024]{2,1,0:T(8,128)(2,1)S(1)} copy-done((bf16[1,2048,1024]{2,1,0:T(8,128)(2,1)S(1)}, bf16[1,2048,1024]{2,1,0:T(8,128)(2,1)}, u32[]{:S(2)}) %copy-start.2) | copy-done | bytes 4194328
  117.0 2.2 %copy-done.4 = bf16[1,1024,2048]{2,1,0:T(8,128)(2,1)S(1)} copy-done((bf16[1,1024,2048]{2,1,0:T(8,128)(2,1)S(1)}, bf16[1,1024,2048]{2,1,0:T(8,128)(2,1)}, u32[]{:S(2)}) %copy-start.4) | copy-done | bytes 4194328
  119.2 1.1 copy-done.12
  120.3 1.1 copy-done.14
  121.4 1.1 copy-done.20
  122.6 7.3 %expert_backward.1 = (f32[384,512]{1,0:T(8,128)S(1)}, bf16[384,512]{1,0:T(8,128)(2,1)S(1)}, bf16[384,512]{1,0:T(8,128)(2,1)S(1)}, bf16[384,512]{1,0:T(8,128)(2,1)S(1)}) custom-call(s32[1]{0:T(128)} %bitcast.8.section_ref, bf16[192,2048]{1,0:T(8,128)(2,1)S(1)} %copy-done.20, bf16[192,2048]{1,0:T(8,128)(2,1)} %collective-permute-done.28.core_ref, ...), custom_call_target="tpu_custom_call" | custom-call | flops 1 | bytes 1 | tf_op jit(solution)/shard_map/expert_backward/pallas_call | solution.py:484
  130.7 2.6 %memory.1.refs_0_ = bf16[128,2048]{1,0:T(8,128)(2,1)} custom-call(s32[1]{0:T(128)} %bitcast.8.section_ref, bf16[128,2048]{1,0:T(8,128)(2,1)S(1)} %copy-done.16, f32[1,2048]{1,0:T(1,128)S(1)} %bitcast.81, bf16[128,512]{1,0:T(8,128)(2,1)S(1)} %add_convert_fusion.2.refs_0_, bf16[128,512]{1,0:T(8,128)(2,1)} %collective-permute-done.29.refs_1_, ...), custom_call_target="tpu_custom_call" | custom-call | flops 1 | bytes 1 | tf_op jit(solution)/shard_map/memory/pallas_call | solution.py:297
  133.4 1.5 collective-permute-start.32
  135.0 1.1 constant_dynamic-slice_fusion.5
  136.2 1.6 add_convert_fusion.1
  137.9 3.7 %attend_sentence.2.refs_6_ = bf16[128,512]{1,0:T(8,128)(2,1)S(1)} custom-call(s32[3]{0:T(128)S(1)} %pad_add_fusion.4.place_ref, s32[2]{0:T(128)S(1)} %copy-done.30, bf16[128,512]{1,0:T(8,128)(2,1)S(1)} %get-tuple-element.84.query_ref, bf16[128,2048]{1,0:T(8,128)(2,1)} %memory.1.refs_0_, bf16[128,2048]{1,0:T(8,128)(2,1)} %collective-permute-done.33.refs_1_, ...), custom_call_target="tpu_custom_call" | custom-call | flops 1 | bytes 1 | tf_op jit(solution)/shard_map/attend_sentence/pallas_call | solution.py:423
  141.7 6.4 %collective-permute-done.32.refs_0_ = bf16[128,2048]{1,0:T(8,128)(2,1)} collective-permute-done((bf16[128,2048]{1,0:T(8,128)(2,1)}, bf16[128,2048]{1,0:T(8,128)(2,1)}, u32[]{:S(2)}, u32[]{:S(2)}) %collective-permute-start.32) | collective-permute-done | bytes 524320 | tf_op jit(solution)/shard_map/ppermute | solution.py:39
  148.1 2.8 %collective-permute-start.40 = (bf16[384,512]{1,0:T(8,128)(2,1)S(1)}, bf16[384,512]{1,0:T(8,128)(2,1)S(1)}, u32[]{:S(2)}, u32[]{:S(2)}) collective-permute-start(bf16[384,512]{1,0:T(8,128)(2,1)S(1)} %copy-done.36), channel_id=1, source_target_pairs={{0,24},{8,0},{16,8},{24,16},{1,25},{9,1},{17,9},{25,17},{2,26},{10... | collective-permute-start | bytes 1179656 | tf_op jit(solution)/shard_map/ppermute | solution.py:34
  151.6 1.0 collective-permute-start.38
  152.7 4.3 %attend_sentence.3 = (bf16[2,256,512]{2,1,0:T(8,128)(2,1)S(1)}, f32[2,256,512]{2,1,0:T(8,128)S(1)}) custom-call(s32[3]{0:T(128)S(1)} %pad_add_fusion.2.place_ref, s32[2]{0:T(128)S(1)} %copy-done.30, bf16[128,512]{1,0:T(8,128)(2,1)S(1)} %get-tuple-element.85.query_ref, bf16[128,2048]{1,0:T(8,128)(2,1)} %collective-permute-done.32.refs_0_, ...), custom_call_target="tpu_custom_call" | custom-call | flops 1 | bytes 1 | tf_op jit(solution)/shard_map/attend_sentence/pallas_call | solution.py:423
  157.1 3.3 %collective-permute-done.40 = bf16[384,512]{1,0:T(8,128)(2,1)S(1)} collective-permute-done((bf16[384,512]{1,0:T(8,128)(2,1)S(1)}, bf16[384,512]{1,0:T(8,128)(2,1)S(1)}, u32[]{:S(2)}, u32[]{:S(2)}) %collective-permute-start.40) | collective-permute-done | bytes 393248 | tf_op jit(solution)/shard_map/ppermute | solution.py:34
  160.3 26.0 %collective-permute-done.39 = bf16[384,512]{1,0:T(8,128)(2,1)S(1)} collective-permute-done((bf16[384,512]{1,0:T(8,128)(2,1)S(1)}, bf16[384,512]{1,0:T(8,128)(2,1)S(1)}, u32[]{:S(2)}, u32[]{:S(2)}) %collective-permute-start.39) | collective-permute-done | bytes 393248 | tf_op jit(solution)/shard_map/ppermute | solution.py:34
  187.1 2.3 %collective-permute-start.46 = (bf16[48,512]{1,0:T(8,128)(2,1)S(1)}, bf16[48,512]{1,0:T(8,128)(2,1)S(1)}, u32[]{:S(2)}, u32[]{:S(2)}) collective-permute-start(bf16[48,512]{1,0:T(8,128)(2,1)S(1)} %get-tuple-element.77), channel_id=1, source_target_pairs={{0,5},{1,4},{2,7},{3,6},{4,1},{5,0},{6,3},{7,2},{8,13},{9,12},{10,... | collective-permute-start | bytes 147464 | tf_op jit(solution)/shard_map/ppermute | solution.py:222
  189.6 1.4 collective-permute-start.37
  191.7 1.0 collective-permute-start.43
  192.7 1.9 collective-permute-start.42
  195.3 4.7 %collective-permute-done.43.refs_3_ = bf16[48,512]{1,0:T(8,128)(2,1)S(1)} collective-permute-done((bf16[48,512]{1,0:T(8,128)(2,1)S(1)}, bf16[48,512]{1,0:T(8,128)(2,1)S(1)}, u32[]{:S(2)}, u32[]{:S(2)}) %collective-permute-start.43) | collective-permute-done | bytes 49184 | tf_op jit(solution)/shard_map/ppermute | solution.py:222
  201.0 1.6 combine.3
  202.6 2.0 fusion.49
  (163 shorter events, 27.8 us)
Async XLA Ops:
  0.6 71.3 %copy-start = (bf16[1,1024,512]{2,1,0:T(8,128)(2,1)S(1)}, bf16[1,1024,512]{2,1,0:T(8,128)(2,1)}, u32[]{:S(2)}) copy-start(bf16[1,1024,512]{2,1,0:T(8,128)(2,1)} %param.26) | copy-start | bytes 3145732
  0.6 48.6 %copy-start.15 = (bf16[128,2048]{1,0:T(8,128)(2,1)S(1)}, bf16[128,2048]{1,0:T(8,128)(2,1)}, u32[]{:S(2)}) copy-start(bf16[128,2048]{1,0:T(8,128)(2,1)} %tokens_ref) | copy-start | bytes 1572868
  0.7 16.7 %copy-start.37 = (s32[128,2]{0,1:T(2,128)S(1)}, s32[128,2]{0,1:T(2,128)}, u32[]{:S(2)}) copy-start(s32[128,2]{0,1:T(2,128)} %param.16) | copy-start | bytes 3076
  0.7 20.9 %copy-start.5 = (bf16[1,1024,512]{2,1,0:T(8,128)(2,1)S(1)}, bf16[1,1024,512]{2,1,0:T(8,128)(2,1)}, u32[]{:S(2)}) copy-start(bf16[1,1024,512]{2,1,0:T(8,128)(2,1)} %param.27) | copy-start | bytes 3145732
  0.7 48.5 %collective-permute-start.8 = (bf16[128,2048]{1,0:T(8,128)(2,1)}, bf16[128,2048]{1,0:T(8,128)(2,1)S(1)}, u32[]{:S(2)}, u32[]{:S(2)}) collective-permute-start(bf16[128,2048]{1,0:T(8,128)(2,1)} %tokens_ref), channel_id=1, source_target_pairs={{0,2},{1,3},{2,0},{3,1},{4,6},{5,7},{6,4},{7,5},{8,10},{9,11},{10,... | collective-permute-start | bytes 1572872 | tf_op jit(solution)/shard_map/ppermute | solution.py:39
  3.7 15.9 %collective-permute-start = (bf16[128,2048]{1,0:T(8,128)(2,1)}, bf16[128,2048]{1,0:T(8,128)(2,1)}, u32[]{:S(2)}, u32[]{:S(2)}) collective-permute-start(bf16[128,2048]{1,0:T(8,128)(2,1)} %tokens_ref), channel_id=1, source_target_pairs={{0,4},{4,0},{1,5},{5,1},{2,6},{6,2},{3,7},{7,3},{8,12},{12,8},{9,1... | collective-permute-start | bytes 1572872 | tf_op jit(solution)/shard_map/ppermute | solution.py:39
  5.2 12.2 %collective-permute-start.6 = (s32[2,128]{1,0:T(2,128)}, s32[2,128]{1,0:T(2,128)S(1)}, u32[]{:S(2)}, u32[]{:S(2)}) collective-permute-start(s32[2,128]{1,0:T(2,128)} %bitcast.82), channel_id=1, source_target_pairs={{0,4},{4,0},{1,5},{5,1},{2,6},{6,2},{3,7},{7,3},{8,12},{12,8},{9,1... | collective-permute-start | bytes 3080 | tf_op jit(solution)/shard_map/ppermute | solution.py:39
  17.4 4.0 %collective-permute-start.7 = (s32[2,2,128]{2,1,0:T(2,128)S(1)}, s32[2,2,128]{2,1,0:T(2,128)S(1)}, u32[]{:S(2)}, u32[]{:S(2)}) collective-permute-start(s32[2,2,128]{2,1,0:T(2,128)S(1)} %pad_add_fusion.1), channel_id=1, source_target_pairs={{0,2},{1,3},{2,0},{3,1},{4,6},{5,7},{6,4},{7,5},{8,10},{9,11},{10,... | collective-permute-start | bytes 6152 | tf_op jit(solution)/shard_map/ppermute | solution.py:39
  19.6 6.5 %collective-permute-start.1 = (bf16[32,2048]{1,0:T(8,128)(2,1)S(1)}, bf16[32,2048]{1,0:T(8,128)(2,1)S(1)}, u32[]{:S(2)}, u32[]{:S(2)}) collective-permute-start(bf16[32,2048]{1,0:T(8,128)(2,1)S(1)} %constant_dynamic-slice_fusion.6), channel_id=1, source_target_pairs={{0,4},{4,0},{1,5},{5,1},{2,6},{6,2},{3,7},{7,3},{8,12},{12,8},{9,1... | collective-permute-start | bytes 393224 | tf_op jit(solution)/shard_map/ppermute | solution.py:39
  21.6 43.4 %collective-permute-start.13 = (bf16[1024,512]{1,0:T(8,128)(2,1)S(1)}, bf16[1024,512]{1,0:T(8,128)(2,1)S(1)}, u32[]{:S(2)}, u32[]{:S(2)}) collective-permute-start(bf16[1024,512]{1,0:T(8,128)(2,1)S(1)} %bitcast.73), channel_id=1, source_target_pairs={{0,4},{4,0},{1,5},{5,1},{2,6},{6,2},{3,7},{7,3},{8,12},{12,8},{9,1... | collective-permute-start | bytes 3145736 | tf_op jit(solution)/shard_map/ppermute | solution.py:39
  22.7 25.0 %collective-permute-start.3 = (bf16[128,2048]{1,0:T(8,128)(2,1)}, bf16[128,2048]{1,0:T(8,128)(2,1)S(1)}, u32[]{:S(2)}, u32[]{:S(2)}) collective-permute-start(bf16[128,2048]{1,0:T(8,128)(2,1)} %collective-permute-done.refs_2_), channel_id=1, source_target_pairs={{0,2},{1,3},{2,0},{3,1},{4,6},{5,7},{6,4},{7,5},{8,10},{9,11},{10,... | collective-permute-start | bytes 1572872 | tf_op jit(solution)/shard_map/ppermute | solution.py:39
  26.1 24.9 %collective-permute-start.2 = (bf16[64,1024]{1,0:T(8,128)(2,1)S(1)}, bf16[64,1024]{1,0:T(8,128)(2,1)S(1)}, u32[]{:S(2)}, u32[]{:S(2)}) collective-permute-start(bf16[64,1024]{1,0:T(8,128)(2,1)S(1)} %dynamic_slice.32), channel_id=1, source_target_pairs={{0,4},{4,0},{1,5},{5,1},{2,6},{6,2},{3,7},{7,3},{8,12},{12,8},{9,1... | collective-permute-start | bytes 393224 | tf_op jit(solution)/shard_map/ppermute | solution.py:39
  27.8 7.0 %collective-permute-start.24 = (bf16[32,2048]{1,0:T(8,128)(2,1)S(1)}, bf16[32,2048]{1,0:T(8,128)(2,1)S(1)}, u32[]{:S(2)}, u32[]{:S(2)}) collective-permute-start(bf16[32,2048]{1,0:T(8,128)(2,1)S(1)} %collective-permute-done.1), channel_id=1, source_target_pairs={{0,8},{8,16},{16,24},{24,0},{1,9},{9,17},{17,25},{25,1},{2,10},{10... | collective-permute-start | bytes 393224 | tf_op jit(solution)/shard_map/ppermute | solution.py:34
  34.8 7.3 %collective-permute-start.25 = (bf16[32,2048]{1,0:T(8,128)(2,1)S(1)}, bf16[32,2048]{1,0:T(8,128)(2,1)S(1)}, u32[]{:S(2)}, u32[]{:S(2)}) collective-permute-start(bf16[32,2048]{1,0:T(8,128)(2,1)S(1)} %collective-permute-done.1), channel_id=1, source_target_pairs={{0,16},{8,24},{16,0},{24,8},{1,17},{9,25},{17,1},{25,9},{2,18},{10... | collective-permute-start | bytes 393224 | tf_op jit(solution)/shard_map/ppermute | solution.py:34
  38.3 16.5 %copy-start.3 = (bf16[1,1024,2048]{2,1,0:T(8,128)(2,1)S(1)}, bf16[1,1024,2048]{2,1,0:T(8,128)(2,1)}, u32[]{:S(2)}) copy-start(bf16[1,1024,2048]{2,1,0:T(8,128)(2,1)} %param.20) | copy-start | bytes 12582916
  42.1 5.0 %collective-permute-start.26 = (bf16[32,2048]{1,0:T(8,128)(2,1)S(1)}, bf16[32,2048]{1,0:T(8,128)(2,1)S(1)}, u32[]{:S(2)}, u32[]{:S(2)}) collective-permute-start(bf16[32,2048]{1,0:T(8,128)(2,1)S(1)} %collective-permute-done.1), channel_id=1, source_target_pairs={{0,24},{8,0},{16,8},{24,16},{1,25},{9,1},{17,9},{25,17},{2,26},{10... | collective-permute-start | bytes 393224 | tf_op jit(solution)/shard_map/ppermute | solution.py:34
  47.7 16.4 %collective-permute-start.14 = (bf16[128,2048]{1,0:T(8,128)(2,1)}, bf16[128,2048]{1,0:T(8,128)(2,1)S(1)}, u32[]{:S(2)}, u32[]{:S(2)}) collective-permute-start(bf16[128,2048]{1,0:T(8,128)(2,1)} %refs_0_.3), channel_id=1, source_target_pairs={{0,2},{1,3},{2,0},{3,1},{4,6},{5,7},{6,4},{7,5},{8,10},{9,11},{10,... | collective-permute-start | bytes 1572872 | tf_op jit(solution)/shard_map/ppermute | solution.py:39
  51.0 9.5 %collective-permute-start.12 = (bf16[192,2048]{1,0:T(8,128)(2,1)S(1)}, bf16[192,2048]{1,0:T(8,128)(2,1)S(1)}, u32[]{:S(2)}, u32[]{:S(2)}) collective-permute-start(bf16[192,2048]{1,0:T(8,128)(2,1)S(1)} %get-tuple-element.39), channel_id=1, source_target_pairs={{0,1},{1,0},{2,3},{3,2},{4,5},{5,4},{6,7},{7,6},{8,9},{9,8},{10,11... | collective-permute-start | bytes 2359304 | tf_op jit(solution)/shard_map/ppermute | solution.py:39
  51.1 9.3 %collective-permute-start.4 = (bf16[64,1024]{1,0:T(8,128)(2,1)S(1)}, bf16[64,1024]{1,0:T(8,128)(2,1)S(1)}, u32[]{:S(2)}, u32[]{:S(2)}) collective-permute-start(bf16[64,1024]{1,0:T(8,128)(2,1)S(1)} %collective-permute-done.2), channel_id=1, source_target_pairs={{0,2},{1,3},{2,0},{3,1},{4,6},{5,7},{6,4},{7,5},{8,10},{9,11},{10,... | collective-permute-start | bytes 393224 | tf_op jit(solution)/shard_map/ppermute | solution.py:39
  56.7 12.2 %collective-permute-start.11 = (bf16[48,2048]{1,0:T(8,128)(2,1)S(1)}, bf16[48,2048]{1,0:T(8,128)(2,1)S(1)}, u32[]{:S(2)}, u32[]{:S(2)}) collective-permute-start(bf16[48,2048]{1,0:T(8,128)(2,1)S(1)} %get-tuple-element.72), channel_id=1, source_target_pairs={{0,6},{1,7},{2,4},{3,5},{4,2},{5,3},{6,0},{7,1},{8,14},{9,15},{10,... | collective-permute-start | bytes 589832 | tf_op jit(solution)/shard_map/ppermute | solution.py:222
  60.4 9.2 %collective-permute-start.10 = (bf16[48,2048]{1,0:T(8,128)(2,1)S(1)}, bf16[48,2048]{1,0:T(8,128)(2,1)S(1)}, u32[]{:S(2)}, u32[]{:S(2)}) collective-permute-start(bf16[48,2048]{1,0:T(8,128)(2,1)S(1)} %get-tuple-element.73), channel_id=1, source_target_pairs={{0,4},{1,5},{2,6},{3,7},{4,0},{5,1},{6,2},{7,3},{8,12},{9,13},{10,... | collective-permute-start | bytes 589832 | tf_op jit(solution)/shard_map/ppermute | solution.py:222
  60.5 12.7 %collective-permute-start.9 = (bf16[48,2048]{1,0:T(8,128)(2,1)}, bf16[48,2048]{1,0:T(8,128)(2,1)}, u32[]{:S(2)}, u32[]{:S(2)}) collective-permute-start(bf16[48,2048]{1,0:T(8,128)(2,1)} %get-tuple-element.74), channel_id=1, source_target_pairs={{0,2},{1,3},{2,0},{3,1},{4,6},{5,7},{6,4},{7,5},{8,10},{9,11},{10,... | collective-permute-start | bytes 589832 | tf_op jit(solution)/shard_map/ppermute | solution.py:222
  63.0 10.0 %copy-start.38 = (f32[128,2]{0,1:T(2,128)S(1)}, f32[128,2]{0,1:T(2,128)}, u32[]{:S(2)}) copy-start(f32[128,2]{0,1:T(2,128)} %param.17) | copy-start | bytes 3076
  64.1 21.0 %copy-start.6 = (bf16[1,1024,512]{2,1,0:T(8,128)(2,1)S(1)}, bf16[1,1024,512]{2,1,0:T(8,128)(2,1)}, u32[]{:S(2)}) copy-start(bf16[1,1024,512]{2,1,0:T(8,128)(2,1)} %param.28) | copy-start | bytes 3145732
  65.0 6.6 %collective-permute-start.5 = (bf16[128,1024]{1,0:T(8,128)(2,1)S(1)}, bf16[128,1024]{1,0:T(8,128)(2,1)S(1)}, u32[]{:S(2)}, u32[]{:S(2)}) collective-permute-start(bf16[128,1024]{1,0:T(8,128)(2,1)S(1)} %pad_maximum_fusion), channel_id=1, source_target_pairs={{0,1},{1,0},{2,3},{3,2},{4,5},{5,4},{6,7},{7,6},{8,9},{9,8},{10,11... | collective-permute-start | bytes 786440 | tf_op jit(solution)/shard_map/ppermute | solution.py:39
  66.8 7.9 %collective-permute-start.18 = (bf16[48,2048]{1,0:T(8,128)(2,1)}, bf16[48,2048]{1,0:T(8,128)(2,1)}, u32[]{:S(2)}, u32[]{:S(2)}) collective-permute-start(bf16[48,2048]{1,0:T(8,128)(2,1)} %get-tuple-element.68), channel_id=1, source_target_pairs={{0,7},{1,6},{2,5},{3,4},{4,3},{5,2},{6,1},{7,0},{8,15},{9,14},{10,... | collective-permute-start | bytes 589832 | tf_op jit(solution)/shard_map/ppermute | solution.py:222
  69.6 9.9 %collective-permute-start.17 = (bf16[48,2048]{1,0:T(8,128)(2,1)}, bf16[48,2048]{1,0:T(8,128)(2,1)}, u32[]{:S(2)}, u32[]{:S(2)}) collective-permute-start(bf16[48,2048]{1,0:T(8,128)(2,1)} %get-tuple-element.69), channel_id=1, source_target_pairs={{0,5},{1,4},{2,7},{3,6},{4,1},{5,0},{6,3},{7,2},{8,13},{9,12},{10,... | collective-permute-start | bytes 589832 | tf_op jit(solution)/shard_map/ppermute | solution.py:222
  70.3 9.2 %collective-permute-start.16 = (bf16[48,2048]{1,0:T(8,128)(2,1)}, bf16[48,2048]{1,0:T(8,128)(2,1)}, u32[]{:S(2)}, u32[]{:S(2)}) collective-permute-start(bf16[48,2048]{1,0:T(8,128)(2,1)} %get-tuple-element.70), channel_id=1, source_target_pairs={{0,3},{1,2},{2,1},{3,0},{4,7},{5,6},{6,5},{7,4},{8,11},{9,10},{10,... | collective-permute-start | bytes 589832 | tf_op jit(solution)/shard_map/ppermute | solution.py:222
  71.6 7.9 %collective-permute-start.15 = (bf16[48,2048]{1,0:T(8,128)(2,1)}, bf16[48,2048]{1,0:T(8,128)(2,1)}, u32[]{:S(2)}, u32[]{:S(2)}) collective-permute-start(bf16[48,2048]{1,0:T(8,128)(2,1)} %get-tuple-element.71), channel_id=1, source_target_pairs={{0,1},{1,0},{2,3},{3,2},{4,5},{5,4},{6,7},{7,6},{8,9},{9,8},{10,11... | collective-permute-start | bytes 589832 | tf_op jit(solution)/shard_map/ppermute | solution.py:222
  84.2 15.1 %collective-permute-start.27 = (bf16[128,2048]{1,0:T(8,128)(2,1)}, bf16[128,2048]{1,0:T(8,128)(2,1)S(1)}, u32[]{:S(2)}, u32[]{:S(2)}) collective-permute-start(bf16[128,2048]{1,0:T(8,128)(2,1)} %constant_dynamic-update-slice_fusion.refs_2_), channel_id=1, source_target_pairs={{0,2},{1,3},{2,0},{3,1},{4,6},{5,7},{6,4},{7,5},{8,10},{9,11},{10,... | collective-permute-start | bytes 1572872 | tf_op jit(solution)/shard_map/ppermute | solution.py:39
  85.1 26.1 %collective-permute-start.23 = (bf16[1024,512]{1,0:T(8,128)(2,1)S(1)}, bf16[1024,512]{1,0:T(8,128)(2,1)S(1)}, u32[]{:S(2)}, u32[]{:S(2)}) collective-permute-start(bf16[1024,512]{1,0:T(8,128)(2,1)S(1)} %bitcast.76), channel_id=1, source_target_pairs={{0,4},{4,0},{1,5},{5,1},{2,6},{6,2},{3,7},{7,3},{8,12},{12,8},{9,1... | collective-permute-start | bytes 3145736 | tf_op jit(solution)/shard_map/ppermute | solution.py:39
  86.7 8.3 %collective-permute-start.19 = (bf16[128,512]{1,0:T(8,128)(2,1)S(1)}, bf16[128,512]{1,0:T(8,128)(2,1)S(1)}, u32[]{:S(2)}, u32[]{:S(2)}) collective-permute-start(bf16[128,512]{1,0:T(8,128)(2,1)S(1)} %get-tuple-element.44), channel_id=1, source_target_pairs={{0,8},{8,16},{16,24},{24,0},{1,9},{9,17},{17,25},{25,1},{2,10},{10... | collective-permute-start | bytes 393224 | tf_op jit(solution)/shard_map/ppermute | solution.py:34
  87.8 11.4 %collective-permute-start.20 = (bf16[128,512]{1,0:T(8,128)(2,1)S(1)}, bf16[128,512]{1,0:T(8,128)(2,1)S(1)}, u32[]{:S(2)}, u32[]{:S(2)}) collective-permute-start(bf16[128,512]{1,0:T(8,128)(2,1)S(1)} %get-tuple-element.45), channel_id=1, source_target_pairs={{0,16},{8,24},{16,0},{24,8},{1,17},{9,25},{17,1},{25,9},{2,18},{10... | collective-permute-start | bytes 393224 | tf_op jit(solution)/shard_map/ppermute | solution.py:34
  90.2 8.9 %collective-permute-start.21 = (bf16[128,512]{1,0:T(8,128)(2,1)S(1)}, bf16[128,512]{1,0:T(8,128)(2,1)S(1)}, u32[]{:S(2)}, u32[]{:S(2)}) collective-permute-start(bf16[128,512]{1,0:T(8,128)(2,1)S(1)} %get-tuple-element.46), channel_id=1, source_target_pairs={{0,24},{8,0},{16,8},{24,16},{1,25},{9,1},{17,9},{25,17},{2,26},{10... | collective-permute-start | bytes 393224 | tf_op jit(solution)/shard_map/ppermute | solution.py:34
  104.3 8.0 %collective-permute-start.28 = (bf16[192,2048]{1,0:T(8,128)(2,1)}, bf16[192,2048]{1,0:T(8,128)(2,1)}, u32[]{:S(2)}, u32[]{:S(2)}) collective-permute-start(bf16[192,2048]{1,0:T(8,128)(2,1)} %get-tuple-element.52), channel_id=1, source_target_pairs={{0,1},{1,0},{2,3},{3,2},{4,5},{5,4},{6,7},{7,6},{8,9},{9,8},{10,11... | collective-permute-start | bytes 2359304 | tf_op jit(solution)/shard_map/ppermute | solution.py:39
  104.3 30.8 %collective-permute-start.22 = (bf16[256,512]{1,0:T(8,128)(2,1)}, bf16[256,512]{1,0:T(8,128)(2,1)}, u32[]{:S(2)}, u32[]{:S(2)}) collective-permute-start(bf16[256,512]{1,0:T(8,128)(2,1)} %fusion.7), channel_id=1, source_target_pairs={{0,4},{4,0},{1,5},{5,1},{2,6},{6,2},{3,7},{7,3},{8,12},{12,8},{9,1... | collective-permute-start | bytes 786440 | tf_op jit(solution)/shard_map/ppermute | solution.py:39
  105.2 25.5 %collective-permute-start.31 = (bf16[128,512]{1,0:T(8,128)(2,1)S(1)}, bf16[128,512]{1,0:T(8,128)(2,1)S(1)}, u32[]{:S(2)}, u32[]{:S(2)}) collective-permute-start(bf16[128,512]{1,0:T(8,128)(2,1)S(1)} %add_convert_fusion.2.refs_0_), channel_id=1, source_target_pairs={{0,24},{8,0},{16,8},{24,16},{1,25},{9,1},{17,9},{25,17},{2,26},{10... | collective-permute-start | bytes 393224 | tf_op jit(solution)/shard_map/ppermute | solution.py:34
  109.1 21.6 %collective-permute-start.30 = (bf16[128,512]{1,0:T(8,128)(2,1)S(1)}, bf16[128,512]{1,0:T(8,128)(2,1)}, u32[]{:S(2)}, u32[]{:S(2)}) collective-permute-start(bf16[128,512]{1,0:T(8,128)(2,1)S(1)} %add_convert_fusion.2.refs_0_), channel_id=1, source_target_pairs={{0,16},{8,24},{16,0},{24,8},{1,17},{9,25},{17,1},{25,9},{2,18},{10... | collective-permute-start | bytes 393224 | tf_op jit(solution)/shard_map/ppermute | solution.py:34
  112.1 18.6 %collective-permute-start.29 = (bf16[128,512]{1,0:T(8,128)(2,1)S(1)}, bf16[128,512]{1,0:T(8,128)(2,1)}, u32[]{:S(2)}, u32[]{:S(2)}) collective-permute-start(bf16[128,512]{1,0:T(8,128)(2,1)S(1)} %add_convert_fusion.2.refs_0_), channel_id=1, source_target_pairs={{0,8},{8,16},{16,24},{24,0},{1,9},{9,17},{17,25},{25,1},{2,10},{10... | collective-permute-start | bytes 393224 | tf_op jit(solution)/shard_map/ppermute | solution.py:34
  112.3 40.3 %collective-permute-start.35 = (bf16[512,1024]{1,0:T(8,128)(2,1)}, bf16[512,1024]{1,0:T(8,128)(2,1)}, u32[]{:S(2)}, u32[]{:S(2)}) collective-permute-start(bf16[512,1024]{1,0:T(8,128)(2,1)} %bitcast.79), channel_id=1, source_target_pairs={{0,4},{4,0},{1,5},{5,1},{2,6},{6,2},{3,7},{7,3},{8,12},{12,8},{9,1... | collective-permute-start | bytes 3145736 | tf_op jit(solution)/shard_map/ppermute | solution.py:39
  122.6 8.2 %copy-start.16 = (bf16[128,2048]{1,0:T(8,128)(2,1)S(1)}, bf16[128,2048]{1,0:T(8,128)(2,1)}, u32[]{:S(2)}) copy-start(bf16[128,2048]{1,0:T(8,128)(2,1)} %tokens_ref) | copy-start | bytes 1572868
  122.6 8.2 %copy-start.29 = (f32[2048]{0:T(1024)S(1)}, f32[2048]{0:T(1024)}, u32[]{:S(2)}) copy-start(f32[2048]{0:T(1024)} %param.21) | copy-start | bytes 24580
  133.3 4.5 %collective-permute-start.33 = (bf16[128,2048]{1,0:T(8,128)(2,1)}, bf16[128,2048]{1,0:T(8,128)(2,1)}, u32[]{:S(2)}, u32[]{:S(2)}) collective-permute-start(bf16[128,2048]{1,0:T(8,128)(2,1)} %memory.1.refs_0_), channel_id=1, source_target_pairs={{0,1},{1,0},{2,3},{3,2},{4,5},{5,4},{6,7},{7,6},{8,9},{9,8},{10,11... | collective-permute-start | bytes 1572872 | tf_op jit(solution)/shard_map/ppermute | solution.py:39
  133.4 14.7 %collective-permute-start.32 = (bf16[128,2048]{1,0:T(8,128)(2,1)}, bf16[128,2048]{1,0:T(8,128)(2,1)}, u32[]{:S(2)}, u32[]{:S(2)}) collective-permute-start(bf16[128,2048]{1,0:T(8,128)(2,1)} %memory.1.refs_0_), channel_id=1, source_target_pairs={{0,2},{1,3},{2,0},{3,1},{4,6},{5,7},{6,4},{7,5},{8,10},{9,11},{10,... | collective-permute-start | bytes 1572872 | tf_op jit(solution)/shard_map/ppermute | solution.py:39
  136.2 11.9 %copy-start.36 = (bf16[384,512]{1,0:T(8,128)(2,1)S(1)}, bf16[384,512]{1,0:T(8,128)(2,1)}, u32[]{:S(2)}) copy-start(bf16[384,512]{1,0:T(8,128)(2,1)} %copy-done.35) | copy-start | bytes 1179652
  136.2 14.7 %copy-start.34 = (bf16[384,512]{1,0:T(8,128)(2,1)S(1)}, bf16[384,512]{1,0:T(8,128)(2,1)}, u32[]{:S(2)}) copy-start(bf16[384,512]{1,0:T(8,128)(2,1)} %copy-done.33) | copy-start | bytes 1179652
  136.2 15.4 %copy-start.32 = (bf16[384,512]{1,0:T(8,128)(2,1)S(1)}, bf16[384,512]{1,0:T(8,128)(2,1)}, u32[]{:S(2)}) copy-start(bf16[384,512]{1,0:T(8,128)(2,1)} %copy-done.31) | copy-start | bytes 1179652
  136.2 16.5 %copy-start.18 = (bf16[1,512,1024]{2,1,0:T(8,128)(2,1)S(1)}, bf16[1,512,1024]{2,1,0:T(8,128)(2,1)}, u32[]{:S(2)}) copy-start(bf16[1,512,1024]{2,1,0:T(8,128)(2,1)} %param.29) | copy-start | bytes 3145732
  141.7 44.7 %copy-start.22 = (f32[384,512]{1,0:T(8,128)S(1)}, f32[384,512]{1,0:T(8,128)}, u32[]{:S(2)}) copy-start(f32[384,512]{1,0:T(8,128)} %copy-done.21) | copy-start | bytes 2359300
  148.1 4.6 %collective-permute-start.34 = (bf16[128,2048]{1,0:T(8,128)(2,1)}, bf16[128,2048]{1,0:T(8,128)(2,1)S(1)}, u32[]{:S(2)}, u32[]{:S(2)}) collective-permute-start(bf16[128,2048]{1,0:T(8,128)(2,1)} %collective-permute-done.32.refs_0_), channel_id=1, source_target_pairs={{0,1},{1,0},{2,3},{3,2},{4,5},{5,4},{6,7},{7,6},{8,9},{9,8},{10,11... | collective-permute-start | bytes 1572872 | tf_op jit(solution)/shard_map/ppermute | solution.py:39
  148.1 12.3 %collective-permute-start.40 = (bf16[384,512]{1,0:T(8,128)(2,1)S(1)}, bf16[384,512]{1,0:T(8,128)(2,1)S(1)}, u32[]{:S(2)}, u32[]{:S(2)}) collective-permute-start(bf16[384,512]{1,0:T(8,128)(2,1)S(1)} %copy-done.36), channel_id=1, source_target_pairs={{0,24},{8,0},{16,8},{24,16},{1,25},{9,1},{17,9},{25,17},{2,26},{10... | collective-permute-start | bytes 1179656 | tf_op jit(solution)/shard_map/ppermute | solution.py:34
  150.8 35.5 %collective-permute-start.39 = (bf16[384,512]{1,0:T(8,128)(2,1)S(1)}, bf16[384,512]{1,0:T(8,128)(2,1)S(1)}, u32[]{:S(2)}, u32[]{:S(2)}) collective-permute-start(bf16[384,512]{1,0:T(8,128)(2,1)S(1)} %copy-done.34), channel_id=1, source_target_pairs={{0,16},{8,24},{16,0},{24,8},{1,17},{9,25},{17,1},{25,9},{2,18},{10... | collective-permute-start | bytes 1179656 | tf_op jit(solution)/shard_map/ppermute | solution.py:34
  151.6 34.8 %collective-permute-start.38 = (bf16[384,512]{1,0:T(8,128)(2,1)S(1)}, bf16[384,512]{1,0:T(8,128)(2,1)S(1)}, u32[]{:S(2)}, u32[]{:S(2)}) collective-permute-start(bf16[384,512]{1,0:T(8,128)(2,1)S(1)} %copy-done.32), channel_id=1, source_target_pairs={{0,8},{8,16},{16,24},{24,0},{1,9},{9,17},{17,25},{25,1},{2,10},{10... | collective-permute-start | bytes 1179656 | tf_op jit(solution)/shard_map/ppermute | solution.py:34
  157.0 32.5 %copy-start.17 = (f32[2,256,512]{2,1,0:T(8,128)}, f32[2,256,512]{2,1,0:T(8,128)S(1)}, u32[]{:S(2)}) copy-start(f32[2,256,512]{2,1,0:T(8,128)S(1)} %get-tuple-element.57) | copy-start | bytes 3145732
  157.0 38.2 %copy-start.39 = (s32[2]{0:T(128)S(1)}, s32[2]{0:T(128)}, u32[]{:S(2)}) copy-start(s32[2]{0:T(128)} %param.24) | copy-start | bytes 28
  157.0 32.4 %collective-permute-start.36 = (bf16[2,256,512]{2,1,0:T(8,128)(2,1)S(1)}, bf16[2,256,512]{2,1,0:T(8,128)(2,1)S(1)}, u32[]{:S(2)}, u32[]{:S(2)}) collective-permute-start(bf16[2,256,512]{2,1,0:T(8,128)(2,1)S(1)} %get-tuple-element.58), channel_id=1, source_target_pairs={{0,1},{1,0},{2,3},{3,2},{4,5},{5,4},{6,7},{7,6},{8,9},{9,8},{10,11... | collective-permute-start | bytes 1572872 | tf_op jit(solution)/shard_map/ppermute | solution.py:39
  186.6 5.0 %collective-permute-start.47 = (bf16[48,512]{1,0:T(8,128)(2,1)S(1)}, bf16[48,512]{1,0:T(8,128)(2,1)S(1)}, u32[]{:S(2)}, u32[]{:S(2)}) collective-permute-start(bf16[48,512]{1,0:T(8,128)(2,1)S(1)} %get-tuple-element.76), channel_id=1, source_target_pairs={{0,7},{1,6},{2,5},{3,4},{4,3},{5,2},{6,1},{7,0},{8,15},{9,14},{10,... | collective-permute-start | bytes 147464 | tf_op jit(solution)/shard_map/ppermute | solution.py:222
  187.1 5.6 %collective-permute-start.46 = (bf16[48,512]{1,0:T(8,128)(2,1)S(1)}, bf16[48,512]{1,0:T(8,128)(2,1)S(1)}, u32[]{:S(2)}, u32[]{:S(2)}) collective-permute-start(bf16[48,512]{1,0:T(8,128)(2,1)S(1)} %get-tuple-element.77), channel_id=1, source_target_pairs={{0,5},{1,4},{2,7},{3,6},{4,1},{5,0},{6,3},{7,2},{8,13},{9,12},{10,... | collective-permute-start | bytes 147464 | tf_op jit(solution)/shard_map/ppermute | solution.py:222
  189.4 5.2 %collective-permute-start.45 = (bf16[48,512]{1,0:T(8,128)(2,1)S(1)}, bf16[48,512]{1,0:T(8,128)(2,1)S(1)}, u32[]{:S(2)}, u32[]{:S(2)}) collective-permute-start(bf16[48,512]{1,0:T(8,128)(2,1)S(1)} %get-tuple-element.78), channel_id=1, source_target_pairs={{0,3},{1,2},{2,1},{3,0},{4,7},{5,6},{6,5},{7,4},{8,11},{9,10},{10,... | collective-permute-start | bytes 147464 | tf_op jit(solution)/shard_map/ppermute | solution.py:222
  189.6 13.0 %collective-permute-start.37 = (bf16[256,512]{1,0:T(8,128)(2,1)S(1)}, bf16[256,512]{1,0:T(8,128)(2,1)S(1)}, u32[]{:S(2)}, u32[]{:S(2)}) collective-permute-start(bf16[256,512]{1,0:T(8,128)(2,1)S(1)} %fusion.50), channel_id=1, source_target_pairs={{0,2},{1,3},{2,0},{3,1},{4,6},{5,7},{6,4},{7,5},{8,10},{9,11},{10,... | collective-permute-start | bytes 786440 | tf_op jit(solution)/shard_map/ppermute | solution.py:39
  191.0 4.3 %collective-permute-start.44 = (bf16[48,512]{1,0:T(8,128)(2,1)S(1)}, bf16[48,512]{1,0:T(8,128)(2,1)S(1)}, u32[]{:S(2)}, u32[]{:S(2)}) collective-permute-start(bf16[48,512]{1,0:T(8,128)(2,1)S(1)} %get-tuple-element.79), channel_id=1, source_target_pairs={{0,1},{1,0},{2,3},{3,2},{4,5},{5,4},{6,7},{7,6},{8,9},{9,8},{10,11... | collective-permute-start | bytes 147464 | tf_op jit(solution)/shard_map/ppermute | solution.py:222
  191.7 8.3 %collective-permute-start.43 = (bf16[48,512]{1,0:T(8,128)(2,1)S(1)}, bf16[48,512]{1,0:T(8,128)(2,1)S(1)}, u32[]{:S(2)}, u32[]{:S(2)}) collective-permute-start(bf16[48,512]{1,0:T(8,128)(2,1)S(1)} %get-tuple-element.80), channel_id=1, source_target_pairs={{0,6},{1,7},{2,4},{3,5},{4,2},{5,3},{6,0},{7,1},{8,14},{9,15},{10,... | collective-permute-start | bytes 147464 | tf_op jit(solution)/shard_map/ppermute | solution.py:222
  192.7 7.3 %collective-permute-start.42 = (bf16[48,512]{1,0:T(8,128)(2,1)S(1)}, bf16[48,512]{1,0:T(8,128)(2,1)S(1)}, u32[]{:S(2)}, u32[]{:S(2)}) collective-permute-start(bf16[48,512]{1,0:T(8,128)(2,1)S(1)} %get-tuple-element.81), channel_id=1, source_target_pairs={{0,4},{1,5},{2,6},{3,7},{4,0},{5,1},{6,2},{7,3},{8,12},{9,13},{10,... | collective-permute-start | bytes 147464 | tf_op jit(solution)/shard_map/ppermute | solution.py:222
  194.6 6.3 %collective-permute-start.41 = (bf16[48,512]{1,0:T(8,128)(2,1)S(1)}, bf16[48,512]{1,0:T(8,128)(2,1)S(1)}, u32[]{:S(2)}, u32[]{:S(2)}) collective-permute-start(bf16[48,512]{1,0:T(8,128)(2,1)S(1)} %get-tuple-element.82), channel_id=1, source_target_pairs={{0,2},{1,3},{2,0},{3,1},{4,6},{5,7},{6,4},{7,5},{8,10},{9,11},{10,... | collective-permute-start | bytes 147464 | tf_op jit(solution)/shard_map/ppermute | solution.py:222
  (24 other events, 55.2 us)

commit v5 on v4

--- a/solution.py
+++ b/solution.py
@@ -1,5 +1,4 @@
 import functools
-import math
 
 import jax
 import jax.numpy as jnp
@@ -155,27 +154,26 @@
     return pltpu.VMEM(shape, dtype)
 
 
-def dispatch_kernel(capacity, count, share, section_ref, code_ref, *refs):
-    blocks, held, sems = refs[:count], refs[count + 2], refs[count + 3]
+def dispatch_kernel(capacity, layout, section_ref, code_ref, *refs):
+    blocks = refs[:-4]
+    outs, held, sems = refs[-4:-2], refs[-2], refs[-1]
+    count, rows = held.shape[0], held.shape[1]
+    half = lax.rem(section_ref[0], 2)
     copies = []
-    for place, block in enumerate(blocks):
-        rows = block.shape[0]
-        if share and place >= count // 2:
-            pieces = rows // share
-            copies.append([])
-            for step in range(pieces):
-                owner = lax.rem(section_ref[0] - step + pieces, pieces)
-                there = held.at[place, pl.ds(pl.multiple_of(owner * share, share), share)]
-                here = block.at[pl.ds(step * share, share)]
-                copies[-1].append(pltpu.make_async_copy(here, there, sems.at[place, step]))
-        else:
-            copies.append([pltpu.make_async_copy(block, held.at[place], sems.at[place, 0])])
+    for place, pieces in enumerate(layout):
+        group = []
+        for i, (which, start, length, side) in enumerate(pieces):
+            there = held.at[place]
+            if side is not None:
+                offset = (half if side == 0 else 1 - half) * length
+                there = held.at[place, pl.ds(pl.multiple_of(offset, length), length)]
+            here = blocks[which].at[pl.ds(start, length)]
+            group.append(pltpu.make_async_copy(here, there, sems.at[place, i]))
+        copies.append(group)
     for group in copies:
         for copy in group:
             copy.start()
     for place, group in enumerate(copies):
-        for copy in group:
-            copy.wait()
         picks = []
         for which in range(2):
             line = which * count + place
@@ -183,31 +181,34 @@
             slot = lax.broadcasted_iota(jnp.int32, (capacity, code.shape[1]), 0)
             picks.append(jnp.where(slot == code, 1.0, 0.0))
         pick = jnp.concatenate(picks, axis=0).astype(jnp.bfloat16)
-        rows = jnp.dot(pick, held[place], preferred_element_type=jnp.float32).astype(jnp.bfloat16)
-        for which, out_ref in enumerate(refs[count : count + 2]):
-            out_ref[place * capacity : (place + 1) * capacity, :] = rows[
+        for copy in group:
+            copy.wait()
+        picked = jnp.dot(pick, held[place], preferred_element_type=jnp.float32)
+        picked = picked.astype(jnp.bfloat16)
+        for which, out_ref in enumerate(outs):
+            out_ref[place * capacity : (place + 1) * capacity, :] = picked[
                 which * capacity : (which + 1) * capacity
             ]
 
 
-def dispatch(section, code, blocks, capacity, share=0):
+def dispatch(section, code, blocks, layout, capacity):
     rows, features = blocks[0].shape
-    count = len(blocks)
+    count = len(layout)
     picked = jax.ShapeDtypeStruct((count * capacity, features), jnp.bfloat16)
     return pl.pallas_call(
-        functools.partial(dispatch_kernel, capacity, count, share),
+        functools.partial(dispatch_kernel, capacity, layout),
         out_shape=(picked, picked),
         in_specs=[
             pl.BlockSpec(memory_space=pltpu.SMEM),
             pl.BlockSpec(memory_space=pltpu.VMEM),
         ]
-        + [pl.BlockSpec(memory_space=pl.ANY)] * count,
+        + [pl.BlockSpec(memory_space=pltpu.HBM)] * len(blocks),
         out_specs=[pl.BlockSpec(memory_space=pltpu.VMEM)] * 2,
         scratch_shapes=[
             vmem((count, rows, features), jnp.bfloat16),
-            pltpu.SemaphoreType.DMA((count, 4)),
+            pltpu.SemaphoreType.DMA((count, 2)),
         ],
-        compiler_params=pltpu.CompilerParams(vmem_limit_bytes=32 * 1024 * 1024),
+        compiler_params=pltpu.CompilerParams(vmem_limit_bytes=10 * 1024 * 1024),
         cost_estimate=SHORT,
         name="dispatch",
     )(section, code, *blocks)
@@ -227,21 +228,15 @@
 def combine_kernel(count, split, section_ref, position_ref, gates_ref, *refs):
     blocks = refs[:count]
     outs = refs[count : count + split]
-    held, total, sems = refs[count + split :]
+    held, total = refs[count + split :]
     capacity, features = blocks[0].shape
-    copies = [
-        pltpu.make_async_copy(block, held.at[pl.ds(i * capacity, capacity)], sems.at[i])
-        for i, block in enumerate(blocks)
-    ]
-    for copy in copies:
-        copy.start()
     position = position_ref[...]
     slot = lax.broadcasted_iota(jnp.int32, (position.shape[0], count * capacity), 1)
     picks = [
         jnp.where(position[:, k : k + 1] == slot, 1.0, 0.0).astype(jnp.bfloat16) for k in range(2)
     ]
-    for copy in copies:
-        copy.wait()
+    for i, block in enumerate(blocks):
+        held[i * capacity : (i + 1) * capacity, :] = block[...]
     pick = jnp.concatenate(picks, axis=0)
     rows = position.shape[0]
     both = jnp.dot(pick, held[...], preferred_element_type=jnp.float32)
@@ -263,24 +258,20 @@
     return pl.pallas_call(
         functools.partial(combine_kernel, count, split),
         out_shape=tuple(jax.ShapeDtypeStruct((rows, width), kind) for kind in types),
-        in_specs=[pl.BlockSpec(memory_space=pltpu.SMEM), full, full]
-        + [pl.BlockSpec(memory_space=pl.ANY)] * count,
+        in_specs=[pl.BlockSpec(memory_space=pltpu.SMEM)] + [full] * (2 + count),
         out_specs=[full] * split,
         scratch_shapes=[
             vmem((count * capacity, features), jnp.bfloat16),
             vmem((rows, features), jnp.float32),
-            pltpu.SemaphoreType.DMA((count,)),
         ],
-        compiler_params=pltpu.CompilerParams(vmem_limit_bytes=32 * 1024 * 1024),
+        compiler_params=pltpu.CompilerParams(vmem_limit_bytes=14 * 1024 * 1024),
         cost_estimate=SHORT,
         name="combine",
     )(section, position, gates, *blocks)
 
 
 def memory_kernel(count, section_ref, tokens_ref, gain_ref, *refs):
-    slices, out_ref, mixed, held, sem = refs[:count], refs[count], *refs[count + 1 :]
-    fetch = pltpu.make_async_copy(tokens_ref, held, sem)
-    fetch.start()
+    slices, out_ref, mixed = refs[:count], refs[count], refs[count + 1]
     me = section_ref[0]
     width = slices[0].shape[1]
     for step, piece in enumerate(slices):
@@ -288,8 +279,7 @@
         mixed[:, pl.ds(pl.multiple_of(owner * width, width), width)] = piece[...].astype(
             jnp.float32
         )
-    fetch.wait()
-    values = held[...].astype(jnp.float32) + mixed[...]
+    values = tokens_ref[...].astype(jnp.float32) + mixed[...]
     out_ref[...] = normalize(values, gain_ref[...]).astype(jnp.bfloat16)
 
 
@@ -299,16 +289,11 @@
         out_shape=jax.ShapeDtypeStruct(tokens.shape, jnp.bfloat16),
         in_specs=[
             pl.BlockSpec(memory_space=pltpu.SMEM),
-            pl.BlockSpec(memory_space=pl.ANY),
         ]
-        + [pl.BlockSpec(memory_space=pltpu.VMEM)] * (1 + len(slices)),
+        + [pl.BlockSpec(memory_space=pltpu.VMEM)] * (2 + len(slices)),
         out_specs=pl.BlockSpec(memory_space=pltpu.VMEM),
-        scratch_shapes=[
-            vmem(tokens.shape, jnp.float32),
-            vmem(tokens.shape, tokens.dtype),
-            pltpu.SemaphoreType.DMA,
-        ],
-        compiler_params=pltpu.CompilerParams(vmem_limit_bytes=20 * 1024 * 1024),
+        scratch_shapes=[vmem(tokens.shape, jnp.float32)],
+        compiler_params=pltpu.CompilerParams(vmem_limit_bytes=8 * 1024 * 1024),
         cost_estimate=SHORT,
         name="memory",
     )(me, tokens, gain[None], *slices)
@@ -318,8 +303,8 @@
     near_ref, far_ref, key_own, key_other, value_own, value_other = refs[:6]
     y, core, sentence = place_ref[0], place_ref[1], place_ref[2]
     if project:
-        done_ref, out_own, out_other, sent_ref, kept_ref = refs[6:11]
-        source, key_weight, value_weight, keys, values, sems, out_weight, context = refs[11:]
+        done_ref, out_own, out_other, sent_ref, kept_mine, kept_other = refs[6:12]
+        source, key_weight, value_weight, keys, values, sems, out_weight, context = refs[12:]
     else:
         out_ref = refs[6]
         source, key_weight, value_weight, keys, values, sems = refs[7:]
@@ -379,19 +364,20 @@
         x = 1 - sentence
         for which in range(2):
             half = jnp.where(which == 0, x, 1 - x)
-            for out, side in ((sent_ref, 1 - core), (kept_ref, core)):
+            kept_ref = kept_mine if which == 0 else kept_other
+            for out, side in ((sent_ref.at[which], 1 - core), (kept_ref, core)):
                 span = pl.ds(pl.multiple_of(side * columns, columns), columns)
                 part = jnp.dot(
                     context[...], out_weight[half, :, span], preferred_element_type=jnp.float32
                 )
-                out[which] = part.astype(out.dtype)
+                out[...] = part.astype(out.dtype)
 
 
 def attend_sentence(place, lengths, query, near, far, key_pair, value_pair, done=None, out_pair=()):
     rows, features = near.shape
     depth, width = key_pair[0].shape
     project = done is not None
-    hold = pl.BlockSpec(memory_space=pl.ANY)
+    hold = pl.BlockSpec(memory_space=pltpu.HBM)
     smem = pl.BlockSpec(memory_space=pltpu.SMEM)
     full = pl.BlockSpec(memory_space=pltpu.VMEM)
     operands = [place, lengths, query, near, far, *key_pair, *value_pair]
@@ -415,9 +401,10 @@
         ]
         out_shape = (
             jax.ShapeDtypeStruct((2, targets, columns), jnp.bfloat16),
-            jax.ShapeDtypeStruct((2, targets, columns), jnp.float32),
+            jax.ShapeDtypeStruct((targets, columns), jnp.float32),
+            jax.ShapeDtypeStruct((targets, columns), jnp.float32),
         )
-        out_specs = [full, full]
+        out_specs = [full] * 3
     else:
         out_shape, out_specs = jax.ShapeDtypeStruct(query.shape, jnp.bfloat16), full
     return pl.pallas_call(
@@ -426,78 +413,77 @@
         in_specs=in_specs,
         out_specs=out_specs,
         scratch_shapes=scratch,
-        compiler_params=pltpu.CompilerParams(vmem_limit_bytes=32 * 1024 * 1024),
+        compiler_params=pltpu.CompilerParams(vmem_limit_bytes=56 * 1024 * 1024),
         cost_estimate=SHORT,
         name="attend_sentence",
     )(*operands)
 
 
-def backward_kernel(split, section_ref, own_ref, core_ref, pre_own, pre_core, out_ref, in_ref, *refs):
-    outs = refs[:split]
-    grads, pre_act, weight_out, weight_in, slope, sems = refs[split:]
+def backward_kernel(split, codes, place_ref, own_ref, core_ref, rise_own, rise_core, out_ref, in_ref, *refs):
+    sent_ref, kept_first, kept_second = refs[:3]
+    grads, rise, weight_out, weight_in, slope, sems = refs[3:]
     rows = own_ref.shape[0]
     hidden, features = weight_out.shape
     width = features // split
     chunk = hidden // 4
-    moves = [
-        (own_ref, grads.at[pl.ds(0, rows)]),
-        (core_ref, grads.at[pl.ds(rows, rows)]),
-        (pre_own, pre_act.at[pl.ds(0, rows)]),
-        (pre_core, pre_act.at[pl.ds(rows, rows)]),
-    ]
+    moves = []
     for part in range(4):
         span = pl.ds(part * chunk, chunk)
         moves.append((out_ref.at[span], weight_out.at[span]))
+    block = 2 * rows // len(codes)
+    for order, code in enumerate(codes):
+        source = place_ref[1] ^ code
+        there = pl.ds(pl.multiple_of(source * block, 16), block)
+        here = pl.ds(order * block % rows, block)
+        own = order * block < rows
+        moves.append(((own_ref if own else core_ref).at[here], grads.at[there]))
+        moves.append(((rise_own if own else rise_core).at[here], rise.at[there]))
     moves.append((in_ref, weight_in))
     copies = [
         pltpu.make_async_copy(here, there, sems.at[i]) for i, (here, there) in enumerate(moves)
     ]
     for copy in copies:
         copy.start()
-    for copy in copies[:4]:
+    for copy in copies[4:-1]:
         copy.wait()
-    scale = (2.0 / math.pi) ** 0.5
     for part in range(4):
-        copies[4 + part].wait()
+        copies[part].wait()
         span = slice(part * chunk, (part + 1) * chunk)
         back = contract_last(grads[...], weight_out[span, :])
-        value = pre_act[:, span]
-        square = value * value
-        bent = jnp.tanh(scale * (value + 0.044715 * (square * value)))
-        inner = scale * (1.0 + 3.0 * 0.044715 * square)
-        rise = 0.5 * (1.0 + bent) + 0.5 * value * ((1.0 - bent * bent) * inner)
-        slope[:, span] = (back * rise).astype(jnp.bfloat16)
-    copies[8].wait()
-    for step in range(split):
-        owner = lax.rem(section_ref[0] + step, split)
-        start = pl.multiple_of(owner * width, width)
+        slope[:, span] = (back * rise[:, span]).astype(jnp.bfloat16)
+    copies[-1].wait()
+    outs = (kept_first, sent_ref.at[0], kept_second, sent_ref.at[1])
+    for step, out_ref in enumerate(outs):
+        start = pl.multiple_of((place_ref[0] ^ step) * width, width)
         part = contract_last(slope[...], weight_in[pl.ds(start, width), :])
-        outs[step][...] = part.astype(outs[step].dtype)
-
-
-def expert_backward(section, grads_own, grads_core, pre_own, pre_core, weight_out, weight_in, split):
+        out_ref[...] = part.astype(out_ref.dtype)
+
+
+def expert_backward(
+    place, codes, grads_own, grads_core, rise_own, rise_core, weight_out, weight_in, split
+):
     rows = 2 * grads_own.shape[0]
     hidden, features = weight_out.shape
-    hold = pl.BlockSpec(memory_space=pl.ANY)
+    hold = pl.BlockSpec(memory_space=pltpu.HBM)
     width = features // split
-    kinds = [jnp.float32] + [jnp.bfloat16] * (split - 1)
+    kept = jax.ShapeDtypeStruct((rows, width), jnp.float32)
     return pl.pallas_call(
-        functools.partial(backward_kernel, split),
-        out_shape=tuple(jax.ShapeDtypeStruct((rows, width), kind) for kind in kinds),
+        functools.partial(backward_kernel, split, codes),
+        out_shape=(jax.ShapeDtypeStruct((2, rows, width), jnp.bfloat16), kept, kept),
         in_specs=[pl.BlockSpec(memory_space=pltpu.SMEM)] + [hold] * 6,
-        out_specs=[pl.BlockSpec(memory_space=pltpu.VMEM)] * split,
+        out_specs=[pl.BlockSpec(memory_space=pltpu.VMEM)] * 3,
         scratch_shapes=[
             vmem((rows, features), jnp.bfloat16),
             vmem((rows, hidden), jnp.float32),
             vmem((hidden, features), jnp.bfloat16),
             vmem((features, hidden), jnp.bfloat16),
             vmem((rows, hidden), jnp.bfloat16),
-            pltpu.SemaphoreType.DMA((9,)),
+            pltpu.SemaphoreType.DMA((5 + 2 * len(codes),)),
         ],
-        compiler_params=pltpu.CompilerParams(vmem_limit_bytes=40 * 1024 * 1024),
+        compiler_params=pltpu.CompilerParams(vmem_limit_bytes=56 * 1024 * 1024),
         cost_estimate=SHORT,
         name="expert_backward",
-    )(section, grads_own, grads_core, pre_own, pre_core, weight_out, weight_in)
+    )(place, grads_own, grads_core, rise_own, rise_core, weight_out, weight_in)
 
 
 def small_body(
@@ -543,20 +529,16 @@
     ids_x = swap(ids_y, "dp", 2)
     token_far = swap(token_y, "dp", 2)
 
-    share = token_count // sections
-    grad_share = lax.dynamic_slice_in_dim(out_grad, section * share, share, 0)
-    grad_fetched = swap(gate(grad_share, token_y), "expert", 1)
-    key_other = swap(gate(key_own, token_y), "expert", 1)
-    states = dec_states[0]
-    normed = normalize(states.astype(jnp.float32), norm_gain[0]).astype(jnp.bfloat16)
-    quarter = normed.shape[0] // lax.axis_size("dp")
-    asked = lax.dynamic_slice(normed, (d * quarter, (1 - y) * half), (quarter, half))
-    asked_here = swap(gate(asked, grad_fetched), "expert", 1)
-    grad_y = jnp.concatenate(
-        [grad_fetched] + [shift(grad_fetched, "section", step) for step in range(1, sections)],
-        axis=0,
-    )
-    grad_x = swap(gate(out_grad, token_far), "dp", 2)
+    side = lax.rem(section, 2)
+    share = token_count // 2
+    grad_half = lax.dynamic_slice_in_dim(out_grad, side * share, share, 0)
+    half_y = swap(gate(grad_half, token_y, token_x), "expert", 1)
+    key_other = swap(gate(key_own, token_y, token_x), "expert", 1)
+    other_y = swap(half_y, "section", 1)
+    half_x = swap(gate(grad_half, token_far), "dp", 2)
+    half_far = swap(gate(half_y, token_far), "dp", 2)
+    half_pair = jnp.concatenate([half_x, half_far], axis=0)
+    other_pair = swap(half_pair, "section", 1)
 
     row = lax.broadcasted_iota(jnp.int32, (token_count, token_count), 0)
     column = lax.broadcasted_iota(jnp.int32, (token_count, token_count), 1)
@@ -584,56 +566,70 @@
         part = jnp.dot(hidden, weight_out, preferred_element_type=jnp.float32)
         return pre_act, part.astype(jnp.bfloat16)
 
+    def slope_of(pre_act):
+        return jax.vjp(jax.nn.gelu, pre_act)[1](jnp.ones_like(pre_act))[0]
+
     rows_own, rows_sent = dispatch(
-        which_section, code, [tokens, token_x, token_y, token_far], capacity
+        which_section,
+        gate(code, other_y),
+        [tokens, token_x, token_y, token_far],
+        tuple(((place, 0, token_count, None),) for place in range(4)),
+        capacity,
     )
     rows_core = swap(rows_sent, "dp", 1)
     pre_own, part_own = forward(rows_own)
     pre_core, part_core = forward(rows_core)
-    part_core = gate(part_core, key_other, grad_x)
+    part_core = gate(part_core, key_other, half_pair)
+    rise_own, rise_core = slope_of(gate(pre_own, part_core)), slope_of(gate(pre_core, part_core))
     home = send_home(part_own, near_codes, capacity) + send_home(part_core, core_codes, capacity)
 
-    asked_pair = jnp.concatenate([asked_here, swap(gate(asked_here, token_far), "dp", 2)], axis=0)
-    asked_rows = jnp.concatenate([asked_pair, swap(asked_pair, "dp", 1)], axis=0)
-    query_there = jnp.dot(asked_rows, query_own, preferred_element_type=jnp.float32)
-
-    held_gates = gate(gate_weights, query_there)
+    grads_own, grads_sent = dispatch(
+        which_section,
+        code,
+        [out_grad, half_x, half_y, half_far, other_y, other_pair],
+        (
+            ((0, 0, token_count, None),),
+            ((1, 0, share, 0), (5, 0, share, 1)),
+            ((2, 0, share, 0), (4, 0, share, 1)),
+            ((3, 0, share, 0), (5, share, share, 1)),
+        ),
+        capacity,
+    )
+    grads_core = swap(grads_sent, "dp", 1)
+    held_gates = gate(gate_weights, grads_sent)
     cuts = combine(which_section, position, held_gates, home, sections, jnp.float32)
-    mixed_sum = cuts[0]
-    for step in range(1, sections):
-        mixed_sum = mixed_sum + shift(cuts[step], "section", step).astype(jnp.float32)
+    mixed_parts = [shift(cuts[step], "section", step) for step in range(1, sections)]
+    states = dec_states[0]
+    normed = normalize(states.astype(jnp.float32), norm_gain[0]).astype(jnp.bfloat16)
+    asked = lax.dynamic_slice_in_dim(normed, (1 - y) * half, half, 1)
+    asked_here = swap(gate(asked, cuts[0]), "expert", 1)
+    mixed_sum = gate(cuts[0], grads_core, asked_here)
+    for part in mixed_parts:
+        mixed_sum = mixed_sum + part.astype(jnp.float32)
     mixed_slice = mixed_sum.astype(jnp.bfloat16)
     slices = [mixed_slice] + [shift(mixed_slice, "section", step) for step in range(1, sections)]
 
-    value_other = swap(gate(value_own, cuts[0]), "expert", 1)
-    grad_far = swap(gate(grad_y, cuts[0]), "dp", 2)
-    query_back = swap(gate(query_there.astype(jnp.bfloat16), mixed_slice), "expert", 1)
+    value_other = swap(gate(value_own, *mixed_parts), "expert", 1)
+    query_there = jnp.dot(asked_here, query_own, preferred_element_type=jnp.float32)
+    query_back = swap(query_there.astype(jnp.bfloat16), "expert", 1)
     out_other = swap(gate(out_own, value_other), "expert", 1)
-
-    parts = []
-    for place in range(lax.axis_size("dp")):
-        code_here = d ^ place
-        at = (code_here >> 1) + 2 * (code_here & 1)
-        parts.append(lax.dynamic_slice_in_dim(query_back, at * quarter, quarter, 0))
     normed_own = lax.dynamic_slice_in_dim(normed, y * half, half, 1)
-    query = (
-        jnp.dot(normed_own, query_own, preferred_element_type=jnp.float32)
-        + jnp.concatenate(parts, axis=0).astype(jnp.float32)
-    ).astype(jnp.bfloat16)
-
-    grads_own, grads_sent = dispatch(
-        which_section, gate(code, mixed_slice), [out_grad, grad_x, grad_y, grad_far], capacity, share
-    )
-    grads_core = swap(grads_sent, "dp", 1)
-    backward_cuts = expert_backward(
-        which_section, grads_own, grads_core, pre_own, pre_core, weight_out, weight_in, sections
-    )
-    held_tokens = gate(tokens, value_other, backward_cuts[0])
+    query_here = jnp.dot(normed_own, query_own, preferred_element_type=jnp.float32)
+    query = (query_here + query_back.astype(jnp.float32)).astype(jnp.bfloat16)
+
+    sent_pair, kept_first, kept_second = expert_backward(
+        gate(jnp.stack([section, here]).astype(jnp.int32), slices[1]),
+        near_codes + core_codes,
+        grads_own,
+        grads_core,
+        rise_own,
+        rise_core,
+        weight_out,
+        weight_in,
+        sections,
+    )
+    held_tokens = gate(tokens, value_other, query_back, kept_first)
     memory = make_memory(which_section, held_tokens, slices, final_gain)
-    backward_arrived = [
-        shift(gate(backward_cuts[step], *slices), "section", step) for step in range(1, sections)
-    ]
-
     memory_x = swap(memory, "dp", 2)
     memory_core = swap(memory, "dp", 1)
 
@@ -644,19 +640,25 @@
         return attend_sentence(place, src_lengths, rows_of, near, far, *pairs, *rest)
 
     context_own = sentence(x, memory, memory_core)
+    from_pair = swap(sent_pair, "section", 1)
+    to_other = (kept_second + from_pair[1].astype(jnp.float32)).astype(jnp.bfloat16)
+    from_other = swap(to_other, "section", 2)
+    backward_sum = kept_first + from_pair[0].astype(jnp.float32) + from_other.astype(jnp.float32)
     memory_far = swap(gate(memory_x, context_own), "dp", 1)
-    sent, kept = sentence(1 - x, memory_x, memory_far, context_own, (out_own, out_other))
+    sent, kept_mine, kept_other = sentence(
+        1 - x, memory_x, memory_far, gate(context_own, to_other), (out_own, out_other)
+    )
 
     from_core = swap(sent, "dp", 1).astype(jnp.float32)
-    from_x = swap((kept[1] + from_core[1]).astype(jnp.bfloat16), "dp", 2)
-    attended = kept[0] + from_core[0] + from_x.astype(jnp.float32)
+    from_x = swap((gate(kept_other, from_other) + from_core[1]).astype(jnp.bfloat16), "dp", 2)
+    attended = kept_mine + from_core[0] + from_x.astype(jnp.float32)
     dec_out = add_residual(attended, states, tgt_lengths)
 
-    backward_sum = gate(backward_cuts[0], kept)
-    for part in backward_arrived:
-        backward_sum = backward_sum + part.astype(jnp.float32)
-    grads_home = send_home(backward_sum.astype(jnp.bfloat16), near_codes + core_codes, capacity)
-    (token_grad,) = combine(which_section, position, gate_weights, grads_home, 1, jnp.bfloat16)
+    grads_home = exchange(backward_sum.astype(jnp.bfloat16), group_size, capacity)
+    natural = expert_ids * capacity + rank
+    (token_grad,) = combine(
+        which_section, natural, gate_weights, [grads_home], 1, jnp.bfloat16
+    )
     return (dec_out[None], token_grad)
 
 
@@ -772,6 +774,6 @@
         P("section", "dp", "expert"),
     )
     out_specs = (P("section", "expert", "dp"), P(("expert", "dp"), "section"))
-    small = mesh.shape["expert"] == 2 and mesh.shape["dp"] == 4
+    small = (mesh.shape["section"], mesh.shape["expert"], mesh.shape["dp"]) == (4, 2, 4)
     chosen = small_body if small else body
     return jax.shard_map(chosen, mesh=mesh, in_specs=in_specs, out_specs=out_specs, check_vma=False)

time: 205 us -> 197 us (0.961)
  starting transfers between devices: 54.8 us -> 46.1 us
  other arithmetic: 9.93 us -> 18.6 us
  local copies, waits for them, and re-layouts: 24.9 us -> 17.6 us
    ppermute x22 -> x24, waiting for transfers between devices: 16.5 us -> 46.6 us  [swap(): return lax.ppermute(value, axis, [(i, i ^ mask) for i in range(size)])]
    ppermute x12 -> x6, waiting for transfers between devices: 48.5 us -> 24.1 us  [shift(): lax.ppermute(value, axis, [(i, (i + step) % size) for i in range(size)])]
    ppermute x14 -> x7, waiting for transfers between devices: 12.1 us -> 2.4 us  [send_home(): lax.ppermute(block, ('expert', 'dp'), [(i, i ^ code) for i in range(size)])]
    unnamed x85 -> x73, local copies, waits for them, and re-layouts: 19.3 us -> 9.99 us
    ppermute x12 -> x6, starting transfers between devices: 19.3 us -> 12.5 us  [shift(): lax.ppermute(value, axis, [(i, (i + step) % size) for i in range(size)])]
    ppermute x14 -> x7, starting transfers between devices: 13.4 us -> 6.98 us  [send_home(): lax.ppermute(block, ('expert', 'dp'), [(i, i ^ code) for i in range(size)])]
    pallas_call x2, Pallas kernels: 8.07 us -> 11.9 us  [attend_sentence(): pl.pallas_call(functools.partial(attend_kernel, project), out_shape=out_s...]
    all_to_all x0 -> x1, waiting for transfers between devices: none -> 3.63 us  [exchange(): lax.all_to_all(sent, ('expert', 'dp'), split_axis=0, concat_axis=0, tiled...]
  transfers between devices with their start and end apart: 48 -> 38, of which waited for: 17 -> 17; matrix products, arithmetic and copies ran while one was open for 13% -> 16% of each run, Pallas kernels for 12% -> 14%
where the time goes in v5:
time: 197 us; the launch traced here: 196 us
  waiting for transfers between devices  76.7 us (39%)
  starting transfers between devices  46.1 us (23%)
  Pallas kernels  28.8 us (15%)
  other arithmetic  18.6 us (9%)
  local copies, waits for them, and re-layouts  17.6 us (9%)
  matrix products  7.52 us (4%)
    ppermute x24, waiting for transfers between devices, swap(): return lax.ppermute(value, axis, [(i, i ^ mask) for i in range(size)])  46.6 us
    ppermute x6, waiting for transfers between devices, shift(): lax.ppermute(value, axis, [(i, (i + step) % size) for i in range(size)])  24.1 us
    ppermute x24, starting transfers between devices, swap(): return lax.ppermute(value, axis, [(i, i ^ mask) for i in range(size)])  23.2 us
    ppermute x6, starting transfers between devices, shift(): lax.ppermute(value, axis, [(i, (i + step) % size) for i in range(size)])  12.5 us
    pallas_call x2, Pallas kernels, attend_sentence(): pl.pallas_call(functools.partial(attend_kernel, project), out_shape=out_s...  11.9 us
    pallas_call x1, Pallas kernels, expert_backward(): pl.pallas_call(functools.partial(backward_kernel, split, codes), out_shap...  10.7 us
    unnamed x73, local copies, waits for them, and re-layouts  9.99 us
    ppermute x7, starting transfers between devices, send_home(): lax.ppermute(block, ('expert', 'dp'), [(i, i ^ code) for i in range(size)])  6.98 us
  transfers between devices with their start and end apart: 38, of which 17 were waited for; matrix products, arithmetic and copies ran while one was open for 16% of the time, Pallas kernels for 14%

profile of v5, /device:TPU:0, one launch (start us, length us, event | category | flops | bytes accessed | tf_op | source)
XLA Modules:
  0.0 196.5 jit_solution(14484073982884809059)
XLA Ops:
  0.7 3.0 %collective-permute-start.2 = (bf16[128,2048]{1,0:T(8,128)(2,1)}, bf16[128,2048]{1,0:T(8,128)(2,1)S(1)}, u32[]{:S(2)}, u32[]{:S(2)}) collective-permute-start(bf16[128,2048]{1,0:T(8,128)(2,1)} %tokens_ref), channel_id=1, source_target_pairs={{0,4},{4,0},{1,5},{5,1},{2,6},{6,2},{3,7},{7,3},{8,12},{12,8},{9,1... | collective-permute-start | bytes 1572872 | tf_op jit(solution)/shard_map/ppermute | solution.py:38
  3.7 1.5 collective-permute-start.5
  6.6 1.5 convert_reduce_fusion
  8.0 1.6 fusion.3
  9.7 1.7 constant_dynamic-slice_fusion.2
  11.3 2.6 %fusion.5 = bf16[256,2048]{1,0:T(8,128)(2,1)} fusion(bf16[1,256,2048]{2,1,0:T(8,128)(2,1)} %param.22, f32[2048]{0:T(1024)} %bitcast.104, f32[256]{0:T(256)S(1)} %add_rsqrt_fusion, f32[256]{0:T(256)S(1)} %broadcast_multiply_fusion.1), kind=kLoop, calls=%fused_computation.9 | loop fusion | flops 2621440 | bytes 2107392 | tf_op jit(solution)/shard_map/convert_element_type | solution.py:603
  13.9 1.9 collective-permute-done.2.refs_2_
  15.8 1.4 collective-permute-done.5.refs_1_
  17.7 1.6 collective-permute-start.3
  21.3 3.1 %collective-permute-done.6.refs_2_ = bf16[64,2048]{1,0:T(8,128)(2,1)S(1)} collective-permute-done((bf16[64,2048]{1,0:T(8,128)(2,1)}, bf16[64,2048]{1,0:T(8,128)(2,1)S(1)}, u32[]{:S(2)}, u32[]{:S(2)}) %collective-permute-start.6) | collective-permute-done | bytes 262176 | tf_op jit(solution)/shard_map/ppermute | solution.py:38
  24.4 1.6 collective-permute-start.8
  25.9 4.3 %collective-permute-done.1 = s32[2,2,128]{2,1,0:T(2,128)S(1)} collective-permute-done((s32[2,2,128]{2,1,0:T(2,128)S(1)}, s32[2,2,128]{2,1,0:T(2,128)S(1)}, u32[]{:S(2)}, u32[]{:S(2)}) %collective-permute-start.1) | collective-permute-done | bytes 2080 | tf_op jit(solution)/shard_map/ppermute | solution.py:38
  30.4 1.4 collective-permute-start.14
  32.6 1.5 collective-permute-start.7
  35.3 1.1 copy-done.6
  36.4 1.3 dispatch.3
  37.8 3.2 %fusion.75 = f32[192,1024]{1,0:T(8,128)S(1)} fusion(bf16[192,2048]{1,0:T(8,128)(2,1)S(1)} %get-tuple-element.40, bf16[1,2048,1024]{2,1,0:T(8,128)(2,1)} %param.19), kind=kOutput, calls=%fused_computation.113 | convolution fusion | flops 805306368 | bytes 5767168 | tf_op jit(solution)/shard_map/dot_general | solution.py:564
  41.1 1.1 convolution_convert_fusion.1
  42.9 1.5 collective-permute-start.10
  45.0 1.6 collective-permute-start.12
  46.6 1.6 collective-permute-start.9
  48.3 1.0 fusion.73
  49.3 1.1 convolution_convert_fusion
  50.4 9.3 %collective-permute-done.14.refs_3_ = bf16[1024,512]{1,0:T(8,128)(2,1)S(1)} collective-permute-done((bf16[1024,512]{1,0:T(8,128)(2,1)}, bf16[1024,512]{1,0:T(8,128)(2,1)S(1)}, u32[]{:S(2)}, u32[]{:S(2)}) %collective-permute-start.14) | collective-permute-done | bytes 1048608 | tf_op jit(solution)/shard_map/ppermute | solution.py:38
  59.7 1.0 fusion.86
  61.4 1.3 collective-permute-start.16
  64.3 1.1 collective-permute-start.18
  65.4 1.9 constant_dynamic-slice_fusion.3
  69.2 1.3 dispatch.2
  72.5 2.4 %collective-permute-done.17.refs_6_ = bf16[48,2048]{1,0:T(8,128)(2,1)} collective-permute-done((bf16[48,2048]{1,0:T(8,128)(2,1)}, bf16[48,2048]{1,0:T(8,128)(2,1)}, u32[]{:S(2)}, u32[]{:S(2)}) %collective-permute-start.17) | collective-permute-done | bytes 196640 | tf_op jit(solution)/shard_map/ppermute | solution.py:223
  76.8 2.2 %combine.2 = (f32[128,512]{1,0:T(8,128)S(1)}, bf16[128,512]{1,0:T(8,128)(2,1)S(1)}, bf16[128,512]{1,0:T(8,128)(2,1)S(1)}, bf16[128,512]{1,0:T(8,128)(2,1)S(1)}) custom-call(s32[1]{0:T(128)} %bitcast.8.section_ref, s32[128,2]{1,0:T(8,128)S(1)} %get-tuple-element.79.position_ref, f32[128,2]{1,0:T(8,128)S(1)} %copy.39.gates_ref, ...), custom_call_target="tpu_custom_call" | custom-call | flops 1 | bytes 1 | tf_op jit(solution)/shard_map/combine/pallas_call | solution.py:258
  79.0 1.4 collective-permute-start.19
  80.4 1.6 collective-permute-start.21
  82.0 2.6 %collective-permute-start.22 = (bf16[128,512]{1,0:T(8,128)(2,1)S(1)}, bf16[128,512]{1,0:T(8,128)(2,1)S(1)}, u32[]{:S(2)}, u32[]{:S(2)}) collective-permute-start(bf16[128,512]{1,0:T(8,128)(2,1)S(1)} %get-tuple-element.47), channel_id=1, source_target_pairs={{0,16},{8,24},{16,0},{24,8},{1,17},{9,25},{17,1},{25,9},{2,18},{10... | collective-permute-start | bytes 393224 | tf_op jit(solution)/shard_map/ppermute | solution.py:33
  84.6 1.3 collective-permute-start.23
  86.0 2.7 %collective-permute-done.21 = bf16[128,512]{1,0:T(8,128)(2,1)S(1)} collective-permute-done((bf16[128,512]{1,0:T(8,128)(2,1)S(1)}, bf16[128,512]{1,0:T(8,128)(2,1)S(1)}, u32[]{:S(2)}, u32[]{:S(2)}) %collective-permute-start.21) | collective-permute-done | bytes 131104 | tf_op jit(solution)/shard_map/ppermute | solution.py:33
  88.6 5.3 %collective-permute-done.22 = bf16[128,512]{1,0:T(8,128)(2,1)S(1)} collective-permute-done((bf16[128,512]{1,0:T(8,128)(2,1)S(1)}, bf16[128,512]{1,0:T(8,128)(2,1)S(1)}, u32[]{:S(2)}, u32[]{:S(2)}) %collective-permute-start.22) | collective-permute-done | bytes 131104 | tf_op jit(solution)/shard_map/ppermute | solution.py:33
  95.6 1.4 collective-permute-start.20
  97.1 3.5 %collective-permute-start.26 = (bf16[128,512]{1,0:T(8,128)(2,1)S(1)}, bf16[128,512]{1,0:T(8,128)(2,1)S(1)}, u32[]{:S(2)}, u32[]{:S(2)}) collective-permute-start(bf16[128,512]{1,0:T(8,128)(2,1)S(1)} %add_convert_fusion.1.refs_0_), channel_id=1, source_target_pairs={{0,8},{8,16},{16,24},{24,0},{1,9},{9,17},{17,25},{25,1},{2,10},{10... | collective-permute-start | bytes 393224 | tf_op jit(solution)/shard_map/ppermute | solution.py:33
  100.6 2.1 %fusion.15 = (f32[192,1024]{1,0:T(8,128)}, f32[192,1024]{1,0:T(8,128)}) fusion(f32[192,1024]{1,0:T(8,128)S(1)} %copy-done.23, f32[192,1024]{1,0:T(8,128)S(1)} %copy-done.25), kind=kLoop, calls=%fused_computation.28 | loop fusion | flops 6684672 | bytes 3145728 | tf_op jit(solution)/shard_map/transpose(jvp())/add_any | solution.py:570
  102.8 1.9 collective-permute-done.26.refs_1_
  104.7 10.7 %expert_backward.1 = (bf16[2,384,512]{2,1,0:T(8,128)(2,1)}, f32[384,512]{1,0:T(8,128)}, f32[384,512]{1,0:T(8,128)}) custom-call(s32[2]{0:T(128)} %pad_add_fusion.4.place_ref, bf16[192,2048]{1,0:T(8,128)(2,1)} %copy-done.4, bf16[192,2048]{1,0:T(8,128)(2,1)} %copy-done.26, f32[192,1024]{1,0:T(8,128)} %get-tuple-element.82.rise_own, ...), custom_call_target="tpu_custom_call" | custom-call | flops 1 | bytes 1 | tf_op jit(solution)/shard_map/expert_backward/pallas_call | solution.py:470
  115.4 1.0 collective-permute-start.32
  116.4 1.6 collective-permute-start.27
  118.0 1.8 collective-permute-start.28
  119.8 4.9 %collective-permute-done.20 = bf16[256,512]{1,0:T(8,128)(2,1)S(1)} collective-permute-done((bf16[256,512]{1,0:T(8,128)(2,1)S(1)}, bf16[256,512]{1,0:T(8,128)(2,1)S(1)}, u32[]{:S(2)}, u32[]{:S(2)}) %collective-permute-start.20) | collective-permute-done | bytes 262176 | tf_op jit(solution)/shard_map/ppermute | solution.py:38
  124.8 11.6 %collective-permute-done.27.refs_2_ = bf16[128,512]{1,0:T(8,128)(2,1)S(1)} collective-permute-done((bf16[128,512]{1,0:T(8,128)(2,1)S(1)}, bf16[128,512]{1,0:T(8,128)(2,1)S(1)}, u32[]{:S(2)}, u32[]{:S(2)}) %collective-permute-start.27) | collective-permute-done | bytes 131104 | tf_op jit(solution)/shard_map/ppermute | solution.py:33
  136.4 2.6 %collective-permute-done.28.refs_3_ = bf16[128,512]{1,0:T(8,128)(2,1)S(1)} collective-permute-done((bf16[128,512]{1,0:T(8,128)(2,1)S(1)}, bf16[128,512]{1,0:T(8,128)(2,1)S(1)}, u32[]{:S(2)}, u32[]{:S(2)}) %collective-permute-start.28) | collective-permute-done | bytes 131104 | tf_op jit(solution)/shard_map/ppermute | solution.py:33
  142.7 5.4 %attend_sentence.2.refs_6_ = bf16[128,512]{1,0:T(8,128)(2,1)} custom-call(s32[3]{0:T(128)} %pad_add_fusion.5.place_ref, s32[2]{0:T(128)} %lengths_ref.3, bf16[128,512]{1,0:T(8,128)(2,1)} %get-tuple-element.76.query_ref, bf16[128,2048]{1,0:T(8,128)(2,1)} %copy-done.2, bf16[128,2048]{1,0:T(8,128)(2,1)} %collective-permute-done.30.refs_1_, ...), custom_call_target="tpu_custom_call" | custom-call | flops 1 | bytes 1 | tf_op jit(solution)/shard_map/attend_sentence/pallas_call | solution.py:410
  148.1 5.9 %collective-permute-done.29.refs_0_ = bf16[128,2048]{1,0:T(8,128)(2,1)} collective-permute-done((bf16[128,2048]{1,0:T(8,128)(2,1)S(1)}, bf16[128,2048]{1,0:T(8,128)(2,1)}, u32[]{:S(2)}, u32[]{:S(2)}) %collective-permute-start.29) | collective-permute-done | bytes 524320 | tf_op jit(solution)/shard_map/ppermute | solution.py:38
  154.1 1.4 fusion.40
  155.4 1.2 collective-permute-start.35
  157.3 8.5 %collective-permute-done.33.refs_8_ = bf16[512,1024]{1,0:T(8,128)(2,1)} collective-permute-done((bf16[512,1024]{1,0:T(8,128)(2,1)}, bf16[512,1024]{1,0:T(8,128)(2,1)}, u32[]{:S(2)}, u32[]{:S(2)}) %collective-permute-start.33) | collective-permute-done | bytes 1048608 | tf_op jit(solution)/shard_map/ppermute | solution.py:38
  165.8 6.4 %attend_sentence.3 = (bf16[2,256,512]{2,1,0:T(8,128)(2,1)}, f32[256,512]{1,0:T(8,128)}, f32[256,512]{1,0:T(8,128)}) custom-call(s32[3]{0:T(128)} %pad_add_fusion.2.place_ref, s32[2]{0:T(128)} %lengths_ref.3, bf16[128,512]{1,0:T(8,128)(2,1)} %get-tuple-element.77.query_ref, bf16[128,2048]{1,0:T(8,128)(2,1)} %collective-permute-done.29.refs_0_, ...), custom_call_target="tpu_custom_call" | custom-call | flops 1 | bytes 1 | tf_op jit(solution)/shard_map/attend_sentence/pallas_call | solution.py:410
  172.3 4.0 %collective-permute-done.35 = bf16[384,512]{1,0:T(8,128)(2,1)S(1)} collective-permute-done((bf16[384,512]{1,0:T(8,128)(2,1)S(1)}, bf16[384,512]{1,0:T(8,128)(2,1)S(1)}, u32[]{:S(2)}, u32[]{:S(2)}) %collective-permute-start.35) | collective-permute-done | bytes 393248 | tf_op jit(solution)/shard_map/ppermute | solution.py:38
  176.3 1.9 fusion.39
  178.3 3.5 %all-to-all-start = ((bf16[8,48,512]{2,1,0:T(8,128)(2,1)}), bf16[8,48,512]{2,1,0:T(8,128)(2,1)S(1)}, u32[]{:S(2)}, u32[]{:S(2)}) async-start(bf16[8,48,512]{2,1,0:T(8,128)(2,1)} %bitcast.27), calls=%async_computation | async-start | bytes 786432 | tf_op jit(solution)/shard_map/all_to_all | solution.py:142
  181.7 1.2 convert_element_type.112
  182.9 1.8 fusion.42
  184.7 1.9 collective-permute-start.36
  186.8 3.6 %all-to-all-done = bf16[8,48,512]{2,1,0:T(8,128)(2,1)S(1)} async-done(((bf16[8,48,512]{2,1,0:T(8,128)(2,1)}), bf16[8,48,512]{2,1,0:T(8,128)(2,1)S(1)}, u32[]{:S(2)}, u32[]{:S(2)}) %all-to-all-start) | async-done | bytes 393248 | tf_op jit(solution)/shard_map/all_to_all | solution.py:142
  190.5 1.0 combine.3
  191.5 3.2 %collective-permute-done.36 = bf16[256,512]{1,0:T(8,128)(2,1)S(1)} collective-permute-done((bf16[256,512]{1,0:T(8,128)(2,1)}, bf16[256,512]{1,0:T(8,128)(2,1)S(1)}, u32[]{:S(2)}, u32[]{:S(2)}) %collective-permute-start.36) | collective-permute-done | bytes 262176 | tf_op jit(solution)/shard_map/ppermute | solution.py:38
  194.7 1.8 fusion.63
  (133 shorter events, 21.9 us)
Async XLA Ops:
  0.6 94.5 %copy-start = (bf16[1,1024,512]{2,1,0:T(8,128)(2,1)S(1)}, bf16[1,1024,512]{2,1,0:T(8,128)(2,1)}, u32[]{:S(2)}) copy-start(bf16[1,1024,512]{2,1,0:T(8,128)(2,1)} %param.26) | copy-start | bytes 3145732
  0.6 34.7 %copy-start.1 = (bf16[128,2048]{1,0:T(8,128)(2,1)S(1)}, bf16[128,2048]{1,0:T(8,128)(2,1)}, u32[]{:S(2)}) copy-start(bf16[128,2048]{1,0:T(8,128)(2,1)} %tokens_ref) | copy-start | bytes 1572868
  0.7 17.0 %copy-start.32 = (s32[128,2]{0,1:T(2,128)S(1)}, s32[128,2]{0,1:T(2,128)}, u32[]{:S(2)}) copy-start(s32[128,2]{0,1:T(2,128)} %param.16) | copy-start | bytes 3076
  0.7 15.2 %collective-permute-start.2 = (bf16[128,2048]{1,0:T(8,128)(2,1)}, bf16[128,2048]{1,0:T(8,128)(2,1)S(1)}, u32[]{:S(2)}, u32[]{:S(2)}) collective-permute-start(bf16[128,2048]{1,0:T(8,128)(2,1)} %tokens_ref), channel_id=1, source_target_pairs={{0,4},{4,0},{1,5},{5,1},{2,6},{6,2},{3,7},{7,3},{8,12},{12,8},{9,1... | collective-permute-start | bytes 1572872 | tf_op jit(solution)/shard_map/ppermute | solution.py:38
  3.7 13.6 %collective-permute-start.5 = (bf16[128,2048]{1,0:T(8,128)(2,1)}, bf16[128,2048]{1,0:T(8,128)(2,1)S(1)}, u32[]{:S(2)}, u32[]{:S(2)}) collective-permute-start(bf16[128,2048]{1,0:T(8,128)(2,1)} %tokens_ref), channel_id=1, source_target_pairs={{0,2},{1,3},{2,0},{3,1},{4,6},{5,7},{6,4},{7,5},{8,10},{9,11},{10,... | collective-permute-start | bytes 1572872 | tf_op jit(solution)/shard_map/ppermute | solution.py:38
  5.2 14.1 %collective-permute-start = (s32[2,128]{1,0:T(2,128)}, s32[2,128]{1,0:T(2,128)S(1)}, u32[]{:S(2)}, u32[]{:S(2)}) collective-permute-start(s32[2,128]{1,0:T(2,128)} %bitcast.101), channel_id=1, source_target_pairs={{0,4},{4,0},{1,5},{5,1},{2,6},{6,2},{3,7},{7,3},{8,12},{12,8},{9,1... | collective-permute-start | bytes 3080 | tf_op jit(solution)/shard_map/ppermute | solution.py:38
  17.3 7.1 %collective-permute-start.6 = (bf16[64,2048]{1,0:T(8,128)(2,1)}, bf16[64,2048]{1,0:T(8,128)(2,1)S(1)}, u32[]{:S(2)}, u32[]{:S(2)}) collective-permute-start(bf16[64,2048]{1,0:T(8,128)(2,1)} %constant_dynamic-slice_fusion.2), channel_id=1, source_target_pairs={{0,4},{4,0},{1,5},{5,1},{2,6},{6,2},{3,7},{7,3},{8,12},{12,8},{9,1... | collective-permute-start | bytes 786440 | tf_op jit(solution)/shard_map/ppermute | solution.py:38
  17.7 14.1 %collective-permute-start.3 = (bf16[128,2048]{1,0:T(8,128)(2,1)S(1)}, bf16[128,2048]{1,0:T(8,128)(2,1)S(1)}, u32[]{:S(2)}, u32[]{:S(2)}) collective-permute-start(bf16[128,2048]{1,0:T(8,128)(2,1)S(1)} %collective-permute-done.2.refs_2_), channel_id=1, source_target_pairs={{0,2},{1,3},{2,0},{3,1},{4,6},{5,7},{6,4},{7,5},{8,10},{9,11},{10,... | collective-permute-start | bytes 1572872 | tf_op jit(solution)/shard_map/ppermute | solution.py:38
  19.3 10.9 %collective-permute-start.1 = (s32[2,2,128]{2,1,0:T(2,128)S(1)}, s32[2,2,128]{2,1,0:T(2,128)S(1)}, u32[]{:S(2)}, u32[]{:S(2)}) collective-permute-start(s32[2,2,128]{2,1,0:T(2,128)S(1)} %pad_add_fusion.1), channel_id=1, source_target_pairs={{0,2},{1,3},{2,0},{3,1},{4,6},{5,7},{6,4},{7,5},{8,10},{9,11},{10,... | collective-permute-start | bytes 6152 | tf_op jit(solution)/shard_map/ppermute | solution.py:38
  24.4 10.9 %collective-permute-start.8 = (bf16[64,2048]{1,0:T(8,128)(2,1)S(1)}, bf16[64,2048]{1,0:T(8,128)(2,1)S(1)}, u32[]{:S(2)}, u32[]{:S(2)}) collective-permute-start(bf16[64,2048]{1,0:T(8,128)(2,1)S(1)} %collective-permute-done.6.refs_2_), channel_id=1, source_target_pairs={{0,8},{8,0},{16,24},{24,16},{1,9},{9,1},{17,25},{25,17},{2,10},{10... | collective-permute-start | bytes 786440 | tf_op jit(solution)/shard_map/ppermute | solution.py:38
  30.4 29.4 %collective-permute-start.14 = (bf16[1024,512]{1,0:T(8,128)(2,1)}, bf16[1024,512]{1,0:T(8,128)(2,1)S(1)}, u32[]{:S(2)}, u32[]{:S(2)}) collective-permute-start(bf16[1024,512]{1,0:T(8,128)(2,1)} %bitcast.95), channel_id=1, source_target_pairs={{0,4},{4,0},{1,5},{5,1},{2,6},{6,2},{3,7},{7,3},{8,12},{12,8},{9,1... | collective-permute-start | bytes 3145736 | tf_op jit(solution)/shard_map/ppermute | solution.py:38
  32.6 12.5 %collective-permute-start.7 = (bf16[64,2048]{1,0:T(8,128)(2,1)S(1)}, bf16[64,2048]{1,0:T(8,128)(2,1)S(1)}, u32[]{:S(2)}, u32[]{:S(2)}) collective-permute-start(bf16[64,2048]{1,0:T(8,128)(2,1)S(1)} %collective-permute-done.6.refs_2_), channel_id=1, source_target_pairs={{0,2},{1,3},{2,0},{3,1},{4,6},{5,7},{6,4},{7,5},{8,10},{9,11},{10,... | collective-permute-start | bytes 786440 | tf_op jit(solution)/shard_map/ppermute | solution.py:38
  34.8 9.6 %collective-permute-start.4 = (bf16[64,2048]{1,0:T(8,128)(2,1)}, bf16[64,2048]{1,0:T(8,128)(2,1)S(1)}, u32[]{:S(2)}, u32[]{:S(2)}) collective-permute-start(bf16[64,2048]{1,0:T(8,128)(2,1)} %constant_dynamic-slice_fusion.2), channel_id=1, source_target_pairs={{0,2},{1,3},{2,0},{3,1},{4,6},{5,7},{6,4},{7,5},{8,10},{9,11},{10,... | collective-permute-start | bytes 786440 | tf_op jit(solution)/shard_map/ppermute | solution.py:38
  35.3 2.4 %copy-start.9 = (bf16[64,2048]{1,0:T(8,128)(2,1)}, bf16[64,2048]{1,0:T(8,128)(2,1)S(1)}, u32[]{:S(2)}) copy-start(bf16[64,2048]{1,0:T(8,128)(2,1)S(1)} %collective-permute-done.8.refs_4_) | copy-start | bytes 786436
  35.3 1.1 copy-start.6
  36.4 4.6 %copy-start.19 = (bf16[1,1024,2048]{2,1,0:T(8,128)(2,1)S(1)}, bf16[1,1024,2048]{2,1,0:T(8,128)(2,1)}, u32[]{:S(2)}) copy-start(bf16[1,1024,2048]{2,1,0:T(8,128)(2,1)} %param.20) | copy-start | bytes 12582916
  37.7 8.9 %collective-permute-start.13 = (bf16[192,2048]{1,0:T(8,128)(2,1)S(1)}, bf16[192,2048]{1,0:T(8,128)(2,1)S(1)}, u32[]{:S(2)}, u32[]{:S(2)}) collective-permute-start(bf16[192,2048]{1,0:T(8,128)(2,1)S(1)} %get-tuple-element.41), channel_id=1, source_target_pairs={{0,1},{1,0},{2,3},{3,2},{4,5},{5,4},{6,7},{7,6},{8,9},{9,8},{10,11... | collective-permute-start | bytes 2359304 | tf_op jit(solution)/shard_map/ppermute | solution.py:38
  41.0 4.0 %copy-start.22 = (f32[192,1024]{1,0:T(8,128)}, f32[192,1024]{1,0:T(8,128)S(1)}, u32[]{:S(2)}) copy-start(f32[192,1024]{1,0:T(8,128)S(1)} %fusion.75) | copy-start | bytes 2359300
  41.0 7.2 %copy-start.17 = (bf16[1,2048,1024]{2,1,0:T(8,128)(2,1)S(1)}, bf16[1,2048,1024]{2,1,0:T(8,128)(2,1)}, u32[]{:S(2)}) copy-start(bf16[1,2048,1024]{2,1,0:T(8,128)(2,1)} %param.19) | copy-start | bytes 12582916
  42.9 17.8 %collective-permute-start.10 = (bf16[48,2048]{1,0:T(8,128)(2,1)S(1)}, bf16[48,2048]{1,0:T(8,128)(2,1)S(1)}, u32[]{:S(2)}, u32[]{:S(2)}) collective-permute-start(bf16[48,2048]{1,0:T(8,128)(2,1)S(1)} %get-tuple-element.74), channel_id=1, source_target_pairs={{0,2},{1,3},{2,0},{3,1},{4,6},{5,7},{6,4},{7,5},{8,10},{9,11},{10,... | collective-permute-start | bytes 589832 | tf_op jit(solution)/shard_map/ppermute | solution.py:223
  44.4 18.3 %collective-permute-start.11 = (bf16[48,2048]{1,0:T(8,128)(2,1)S(1)}, bf16[48,2048]{1,0:T(8,128)(2,1)S(1)}, u32[]{:S(2)}, u32[]{:S(2)}) collective-permute-start(bf16[48,2048]{1,0:T(8,128)(2,1)S(1)} %get-tuple-element.73), channel_id=1, source_target_pairs={{0,4},{1,5},{2,6},{3,7},{4,0},{5,1},{6,2},{7,3},{8,12},{9,13},{10,... | collective-permute-start | bytes 589832 | tf_op jit(solution)/shard_map/ppermute | solution.py:223
  45.0 27.5 %collective-permute-start.12 = (bf16[48,2048]{1,0:T(8,128)(2,1)}, bf16[48,2048]{1,0:T(8,128)(2,1)}, u32[]{:S(2)}, u32[]{:S(2)}) collective-permute-start(bf16[48,2048]{1,0:T(8,128)(2,1)} %get-tuple-element.72), channel_id=1, source_target_pairs={{0,6},{1,7},{2,4},{3,5},{4,2},{5,3},{6,0},{7,1},{8,14},{9,15},{10,... | collective-permute-start | bytes 589832 | tf_op jit(solution)/shard_map/ppermute | solution.py:223
  46.6 17.7 %collective-permute-start.9 = (bf16[128,2048]{1,0:T(8,128)(2,1)S(1)}, bf16[128,2048]{1,0:T(8,128)(2,1)S(1)}, u32[]{:S(2)}, u32[]{:S(2)}) collective-permute-start(bf16[128,2048]{1,0:T(8,128)(2,1)S(1)} %constant_dynamic-update-slice_fusion), channel_id=1, source_target_pairs={{0,8},{8,0},{16,24},{24,16},{1,9},{9,1},{17,25},{25,17},{2,10},{10... | collective-permute-start | bytes 1572872 | tf_op jit(solution)/shard_map/ppermute | solution.py:38
  49.3 16.1 %copy-start.24 = (f32[192,1024]{1,0:T(8,128)}, f32[192,1024]{1,0:T(8,128)S(1)}, u32[]{:S(2)}) copy-start(f32[192,1024]{1,0:T(8,128)S(1)} %fusion.73) | copy-start | bytes 2359300
  49.3 16.1 %copy-start.30 = (s32[128,2]{1,0:T(8,128)S(1)}, s32[128,2]{1,0:T(8,128)}, u32[]{:S(2)}) copy-start(s32[128,2]{1,0:T(8,128)} %copy.38) | copy-start | bytes 3076
  49.3 16.1 %copy-start.31 = (s32[128,2]{1,0:T(8,128)S(1)}, s32[128,2]{1,0:T(8,128)}, u32[]{:S(2)}) copy-start(s32[128,2]{1,0:T(8,128)} %copy.41) | copy-start | bytes 3076
  49.3 18.0 %copy-start.3 = (bf16[128,2048]{1,0:T(8,128)(2,1)S(1)}, bf16[128,2048]{1,0:T(8,128)(2,1)}, u32[]{:S(2)}) copy-start(bf16[128,2048]{1,0:T(8,128)(2,1)} %refs_0_.2) | copy-start | bytes 1572868
  49.3 23.1 %copy-start.33 = (f32[128,2]{0,1:T(2,128)S(1)}, f32[128,2]{0,1:T(2,128)}, u32[]{:S(2)}) copy-start(f32[128,2]{0,1:T(2,128)} %param.17) | copy-start | bytes 3076
  59.7 4.6 %copy-start.20 = (bf16[1024,512]{1,0:T(8,128)(2,1)}, bf16[1024,512]{1,0:T(8,128)(2,1)S(1)}, u32[]{:S(2)}) copy-start(bf16[1024,512]{1,0:T(8,128)(2,1)S(1)} %collective-permute-done.14.refs_3_) | copy-start | bytes 3145732
  60.7 11.8 %collective-permute-start.15 = (bf16[48,2048]{1,0:T(8,128)(2,1)}, bf16[48,2048]{1,0:T(8,128)(2,1)}, u32[]{:S(2)}, u32[]{:S(2)}) collective-permute-start(bf16[48,2048]{1,0:T(8,128)(2,1)} %get-tuple-element.71), channel_id=1, source_target_pairs={{0,1},{1,0},{2,3},{3,2},{4,5},{5,4},{6,7},{7,6},{8,9},{9,8},{10,11... | collective-permute-start | bytes 589832 | tf_op jit(solution)/shard_map/ppermute | solution.py:223
  61.4 11.1 %collective-permute-start.16 = (bf16[48,2048]{1,0:T(8,128)(2,1)}, bf16[48,2048]{1,0:T(8,128)(2,1)}, u32[]{:S(2)}, u32[]{:S(2)}) collective-permute-start(bf16[48,2048]{1,0:T(8,128)(2,1)} %get-tuple-element.70), channel_id=1, source_target_pairs={{0,3},{1,2},{2,1},{3,0},{4,7},{5,6},{6,5},{7,4},{8,11},{9,10},{10,... | collective-permute-start | bytes 589832 | tf_op jit(solution)/shard_map/ppermute | solution.py:223
  63.4 11.5 %collective-permute-start.17 = (bf16[48,2048]{1,0:T(8,128)(2,1)}, bf16[48,2048]{1,0:T(8,128)(2,1)}, u32[]{:S(2)}, u32[]{:S(2)}) collective-permute-start(bf16[48,2048]{1,0:T(8,128)(2,1)} %get-tuple-element.69), channel_id=1, source_target_pairs={{0,5},{1,4},{2,7},{3,6},{4,1},{5,0},{6,3},{7,2},{8,13},{9,12},{10,... | collective-permute-start | bytes 589832 | tf_op jit(solution)/shard_map/ppermute | solution.py:223
  64.3 10.6 %collective-permute-start.18 = (bf16[48,2048]{1,0:T(8,128)(2,1)}, bf16[48,2048]{1,0:T(8,128)(2,1)}, u32[]{:S(2)}, u32[]{:S(2)}) collective-permute-start(bf16[48,2048]{1,0:T(8,128)(2,1)} %get-tuple-element.68), channel_id=1, source_target_pairs={{0,7},{1,6},{2,5},{3,4},{4,3},{5,2},{6,1},{7,0},{8,15},{9,14},{10,... | collective-permute-start | bytes 589832 | tf_op jit(solution)/shard_map/ppermute | solution.py:223
  71.4 1.0 copy-start.16
  76.8 23.9 %copy-start.23 = (f32[192,1024]{1,0:T(8,128)S(1)}, f32[192,1024]{1,0:T(8,128)}, u32[]{:S(2)}) copy-start(f32[192,1024]{1,0:T(8,128)} %copy-done.22) | copy-start | bytes 2359300
  76.8 23.9 %copy-start.25 = (f32[192,1024]{1,0:T(8,128)S(1)}, f32[192,1024]{1,0:T(8,128)}, u32[]{:S(2)}) copy-start(f32[192,1024]{1,0:T(8,128)} %copy-done.24) | copy-start | bytes 2359300
  79.0 16.1 %collective-permute-start.19 = (bf16[256,1024]{1,0:T(8,128)(2,1)}, bf16[256,1024]{1,0:T(8,128)(2,1)S(1)}, u32[]{:S(2)}, u32[]{:S(2)}) collective-permute-start(bf16[256,1024]{1,0:T(8,128)(2,1)} %constant_dynamic-slice_fusion.3), channel_id=1, source_target_pairs={{0,4},{4,0},{1,5},{5,1},{2,6},{6,2},{3,7},{7,3},{8,12},{12,8},{9,1... | collective-permute-start | bytes 1572872 | tf_op jit(solution)/shard_map/ppermute | solution.py:38
  80.4 16.6 %collective-permute-start.25 = (bf16[192,2048]{1,0:T(8,128)(2,1)}, bf16[192,2048]{1,0:T(8,128)(2,1)S(1)}, u32[]{:S(2)}, u32[]{:S(2)}) collective-permute-start(bf16[192,2048]{1,0:T(8,128)(2,1)} %copy-done.16), channel_id=1, source_target_pairs={{0,1},{1,0},{2,3},{3,2},{4,5},{5,4},{6,7},{7,6},{8,9},{9,8},{10,11... | collective-permute-start | bytes 2359304 | tf_op jit(solution)/shard_map/ppermute | solution.py:38
  80.4 8.2 %collective-permute-start.21 = (bf16[128,512]{1,0:T(8,128)(2,1)S(1)}, bf16[128,512]{1,0:T(8,128)(2,1)S(1)}, u32[]{:S(2)}, u32[]{:S(2)}) collective-permute-start(bf16[128,512]{1,0:T(8,128)(2,1)S(1)} %get-tuple-element.46), channel_id=1, source_target_pairs={{0,8},{8,16},{16,24},{24,0},{1,9},{9,17},{17,25},{25,1},{2,10},{10... | collective-permute-start | bytes 393224 | tf_op jit(solution)/shard_map/ppermute | solution.py:33
  82.0 11.9 %collective-permute-start.22 = (bf16[128,512]{1,0:T(8,128)(2,1)S(1)}, bf16[128,512]{1,0:T(8,128)(2,1)S(1)}, u32[]{:S(2)}, u32[]{:S(2)}) collective-permute-start(bf16[128,512]{1,0:T(8,128)(2,1)S(1)} %get-tuple-element.47), channel_id=1, source_target_pairs={{0,16},{8,24},{16,0},{24,8},{1,17},{9,25},{17,1},{25,9},{2,18},{10... | collective-permute-start | bytes 393224 | tf_op jit(solution)/shard_map/ppermute | solution.py:33
  84.6 9.3 %collective-permute-start.23 = (bf16[128,512]{1,0:T(8,128)(2,1)S(1)}, bf16[128,512]{1,0:T(8,128)(2,1)S(1)}, u32[]{:S(2)}, u32[]{:S(2)}) collective-permute-start(bf16[128,512]{1,0:T(8,128)(2,1)S(1)} %get-tuple-element.48), channel_id=1, source_target_pairs={{0,24},{8,0},{16,8},{24,16},{1,25},{9,1},{17,9},{25,17},{2,26},{10... | collective-permute-start | bytes 393224 | tf_op jit(solution)/shard_map/ppermute | solution.py:33
  93.9 30.9 %collective-permute-start.24 = (bf16[1024,512]{1,0:T(8,128)(2,1)}, bf16[1024,512]{1,0:T(8,128)(2,1)S(1)}, u32[]{:S(2)}, u32[]{:S(2)}) collective-permute-start(bf16[1024,512]{1,0:T(8,128)(2,1)} %bitcast.98), channel_id=1, source_target_pairs={{0,4},{4,0},{1,5},{5,1},{2,6},{6,2},{3,7},{7,3},{8,12},{12,8},{9,1... | collective-permute-start | bytes 3145736 | tf_op jit(solution)/shard_map/ppermute | solution.py:38
  95.6 29.1 %collective-permute-start.20 = (bf16[256,512]{1,0:T(8,128)(2,1)S(1)}, bf16[256,512]{1,0:T(8,128)(2,1)S(1)}, u32[]{:S(2)}, u32[]{:S(2)}) collective-permute-start(bf16[256,512]{1,0:T(8,128)(2,1)S(1)} %convolution_convert_fusion.2), channel_id=1, source_target_pairs={{0,4},{4,0},{1,5},{5,1},{2,6},{6,2},{3,7},{7,3},{8,12},{12,8},{9,1... | collective-permute-start | bytes 786440 | tf_op jit(solution)/shard_map/ppermute | solution.py:38
  97.0 7.6 %copy-start.26 = (bf16[192,2048]{1,0:T(8,128)(2,1)}, bf16[192,2048]{1,0:T(8,128)(2,1)S(1)}, u32[]{:S(2)}) copy-start(bf16[192,2048]{1,0:T(8,128)(2,1)S(1)} %collective-permute-done.25.core_ref) | copy-start | bytes 2359300
  97.1 7.6 %collective-permute-start.26 = (bf16[128,512]{1,0:T(8,128)(2,1)S(1)}, bf16[128,512]{1,0:T(8,128)(2,1)S(1)}, u32[]{:S(2)}, u32[]{:S(2)}) collective-permute-start(bf16[128,512]{1,0:T(8,128)(2,1)S(1)} %add_convert_fusion.1.refs_0_), channel_id=1, source_target_pairs={{0,8},{8,16},{16,24},{24,0},{1,9},{9,17},{17,25},{25,1},{2,10},{10... | collective-permute-start | bytes 393224 | tf_op jit(solution)/shard_map/ppermute | solution.py:33
  104.7 34.4 %copy-start.15 = (f32[2048]{0:T(1024)S(1)}, f32[2048]{0:T(1024)}, u32[]{:S(2)}) copy-start(f32[2048]{0:T(1024)} %param.21) | copy-start | bytes 24580
  104.7 36.9 %copy-start.18 = (bf16[256,2048]{1,0:T(8,128)(2,1)S(1)}, bf16[256,2048]{1,0:T(8,128)(2,1)}, u32[]{:S(2)}) copy-start(bf16[256,2048]{1,0:T(8,128)(2,1)} %fusion.5) | copy-start | bytes 3145732
  115.4 38.7 %collective-permute-start.32 = (bf16[2,384,512]{2,1,0:T(8,128)(2,1)}, bf16[2,384,512]{2,1,0:T(8,128)(2,1)}, u32[]{:S(2)}, u32[]{:S(2)}) collective-permute-start(bf16[2,384,512]{2,1,0:T(8,128)(2,1)} %get-tuple-element.59), channel_id=1, source_target_pairs={{0,8},{8,0},{16,24},{24,16},{1,9},{9,1},{17,25},{25,17},{2,10},{10... | collective-permute-start | bytes 2359304 | tf_op jit(solution)/shard_map/ppermute | solution.py:38
  116.4 20.0 %collective-permute-start.27 = (bf16[128,512]{1,0:T(8,128)(2,1)S(1)}, bf16[128,512]{1,0:T(8,128)(2,1)S(1)}, u32[]{:S(2)}, u32[]{:S(2)}) collective-permute-start(bf16[128,512]{1,0:T(8,128)(2,1)S(1)} %add_convert_fusion.1.refs_0_), channel_id=1, source_target_pairs={{0,16},{8,24},{16,0},{24,8},{1,17},{9,25},{17,1},{25,9},{2,18},{10... | collective-permute-start | bytes 393224 | tf_op jit(solution)/shard_map/ppermute | solution.py:33
  118.0 21.0 %collective-permute-start.28 = (bf16[128,512]{1,0:T(8,128)(2,1)S(1)}, bf16[128,512]{1,0:T(8,128)(2,1)S(1)}, u32[]{:S(2)}, u32[]{:S(2)}) collective-permute-start(bf16[128,512]{1,0:T(8,128)(2,1)S(1)} %add_convert_fusion.1.refs_0_), channel_id=1, source_target_pairs={{0,24},{8,0},{16,8},{24,16},{1,25},{9,1},{17,9},{25,17},{2,26},{10... | collective-permute-start | bytes 393224 | tf_op jit(solution)/shard_map/ppermute | solution.py:33
  124.8 14.3 %copy-start.21 = (bf16[1024,512]{1,0:T(8,128)(2,1)}, bf16[1024,512]{1,0:T(8,128)(2,1)S(1)}, u32[]{:S(2)}) copy-start(bf16[1024,512]{1,0:T(8,128)(2,1)S(1)} %collective-permute-done.24.refs_5_) | copy-start | bytes 3145732
  139.5 3.2 %copy-start.2 = (bf16[128,2048]{1,0:T(8,128)(2,1)}, bf16[128,2048]{1,0:T(8,128)(2,1)S(1)}, u32[]{:S(2)}) copy-start(bf16[128,2048]{1,0:T(8,128)(2,1)S(1)} %memory.1.refs_0_) | copy-start | bytes 1572868
  139.5 3.2 %collective-permute-start.30 = (bf16[128,2048]{1,0:T(8,128)(2,1)S(1)}, bf16[128,2048]{1,0:T(8,128)(2,1)}, u32[]{:S(2)}, u32[]{:S(2)}) collective-permute-start(bf16[128,2048]{1,0:T(8,128)(2,1)S(1)} %memory.1.refs_0_), channel_id=1, source_target_pairs={{0,1},{1,0},{2,3},{3,2},{4,5},{5,4},{6,7},{7,6},{8,9},{9,8},{10,11... | collective-permute-start | bytes 1572872 | tf_op jit(solution)/shard_map/ppermute | solution.py:38
  139.6 14.4 %collective-permute-start.29 = (bf16[128,2048]{1,0:T(8,128)(2,1)S(1)}, bf16[128,2048]{1,0:T(8,128)(2,1)}, u32[]{:S(2)}, u32[]{:S(2)}) collective-permute-start(bf16[128,2048]{1,0:T(8,128)(2,1)S(1)} %memory.1.refs_0_), channel_id=1, source_target_pairs={{0,2},{1,3},{2,0},{3,1},{4,6},{5,7},{6,4},{7,5},{8,10},{9,11},{10,... | collective-permute-start | bytes 1572872 | tf_op jit(solution)/shard_map/ppermute | solution.py:38
  140.2 25.5 %collective-permute-start.33 = (bf16[512,1024]{1,0:T(8,128)(2,1)}, bf16[512,1024]{1,0:T(8,128)(2,1)}, u32[]{:S(2)}, u32[]{:S(2)}) collective-permute-start(bf16[512,1024]{1,0:T(8,128)(2,1)} %bitcast.22.refs_7_), channel_id=1, source_target_pairs={{0,4},{4,0},{1,5},{5,1},{2,6},{6,2},{3,7},{7,3},{8,12},{12,8},{9,1... | collective-permute-start | bytes 3145736 | tf_op jit(solution)/shard_map/ppermute | solution.py:38
  154.1 3.2 %collective-permute-start.31 = (bf16[128,2048]{1,0:T(8,128)(2,1)}, bf16[128,2048]{1,0:T(8,128)(2,1)S(1)}, u32[]{:S(2)}, u32[]{:S(2)}) collective-permute-start(bf16[128,2048]{1,0:T(8,128)(2,1)} %collective-permute-done.29.refs_0_), channel_id=1, source_target_pairs={{0,1},{1,0},{2,3},{3,2},{4,5},{5,4},{6,7},{7,6},{8,9},{9,8},{10,11... | collective-permute-start | bytes 1572872 | tf_op jit(solution)/shard_map/ppermute | solution.py:38
  155.4 20.9 %copy-start.27 = (f32[384,512]{1,0:T(8,128)S(1)}, f32[384,512]{1,0:T(8,128)}, u32[]{:S(2)}) copy-start(f32[384,512]{1,0:T(8,128)} %get-tuple-element.55) | copy-start | bytes 2359300
  155.4 20.9 %collective-permute-start.35 = (bf16[384,512]{1,0:T(8,128)(2,1)S(1)}, bf16[384,512]{1,0:T(8,128)(2,1)S(1)}, u32[]{:S(2)}, u32[]{:S(2)}) collective-permute-start(bf16[384,512]{1,0:T(8,128)(2,1)S(1)} %fusion.40), channel_id=1, source_target_pairs={{0,16},{8,24},{16,0},{24,8},{1,17},{9,25},{17,1},{25,9},{2,18},{10... | collective-permute-start | bytes 1179656 | tf_op jit(solution)/shard_map/ppermute | solution.py:38
  157.3 8.5 %copy-start.29 = (bf16[128,2048]{1,0:T(8,128)(2,1)}, bf16[128,2048]{1,0:T(8,128)(2,1)S(1)}, u32[]{:S(2)}) copy-start(bf16[128,2048]{1,0:T(8,128)(2,1)S(1)} %collective-permute-done.31.refs_1_) | copy-start | bytes 1572868
  172.2 14.6 %copy-start.34 = (s32[2]{0:T(128)S(1)}, s32[2]{0:T(128)}, u32[]{:S(2)}) copy-start(s32[2]{0:T(128)} %param.24) | copy-start | bytes 28
  172.2 22.5 %copy-start.28 = (f32[256,512]{1,0:T(8,128)S(1)}, f32[256,512]{1,0:T(8,128)}, u32[]{:S(2)}) copy-start(f32[256,512]{1,0:T(8,128)} %get-tuple-element.62) | copy-start | bytes 1572868
  172.2 9.5 %collective-permute-start.34 = (bf16[2,256,512]{2,1,0:T(8,128)(2,1)}, bf16[2,256,512]{2,1,0:T(8,128)(2,1)}, u32[]{:S(2)}, u32[]{:S(2)}) collective-permute-start(bf16[2,256,512]{2,1,0:T(8,128)(2,1)} %get-tuple-element.63), channel_id=1, source_target_pairs={{0,1},{1,0},{2,3},{3,2},{4,5},{5,4},{6,7},{7,6},{8,9},{9,8},{10,11... | collective-permute-start | bytes 1572872 | tf_op jit(solution)/shard_map/ppermute | solution.py:38
  178.3 12.2 %all-to-all-start = ((bf16[8,48,512]{2,1,0:T(8,128)(2,1)}), bf16[8,48,512]{2,1,0:T(8,128)(2,1)S(1)}, u32[]{:S(2)}, u32[]{:S(2)}) async-start(bf16[8,48,512]{2,1,0:T(8,128)(2,1)} %bitcast.27), calls=%async_computation | async-start | bytes 786432 | tf_op jit(solution)/shard_map/all_to_all | solution.py:142
  184.7 10.0 %collective-permute-start.36 = (bf16[256,512]{1,0:T(8,128)(2,1)}, bf16[256,512]{1,0:T(8,128)(2,1)S(1)}, u32[]{:S(2)}, u32[]{:S(2)}) collective-permute-start(bf16[256,512]{1,0:T(8,128)(2,1)} %fusion.42), channel_id=1, source_target_pairs={{0,2},{1,3},{2,0},{3,1},{4,6},{5,7},{6,4},{7,5},{8,10},{9,11},{10,... | collective-permute-start | bytes 786440 | tf_op jit(solution)/shard_map/ppermute | solution.py:38
  (9 other events, 7.6 us)

commit v6 on v5

--- a/solution.py
+++ b/solution.py
@@ -227,8 +227,7 @@
 
 def combine_kernel(count, split, section_ref, position_ref, gates_ref, *refs):
     blocks = refs[:count]
-    outs = refs[count : count + split]
-    held, total = refs[count + split :]
+    outs, (held, total) = refs[count:-2], refs[-2:]
     capacity, features = blocks[0].shape
     position = position_ref[...]
     slot = lax.broadcasted_iota(jnp.int32, (position.shape[0], count * capacity), 1)
@@ -241,25 +240,32 @@
     rows = position.shape[0]
     both = jnp.dot(pick, held[...], preferred_element_type=jnp.float32)
     total[...] = gates_ref[:, 0:1] * both[:rows] + gates_ref[:, 1:2] * both[rows:]
+    if split == 1:
+        outs[0][...] = total[...].astype(outs[0].dtype)
+        return
+    sent_ref, kept_first, kept_second = outs
     width = features // split
-    for step, out_ref in enumerate(outs):
-        owner = lax.rem(section_ref[0] + step, split)
-        start = pl.multiple_of(owner * width, width)
+    for step, out_ref in enumerate((kept_first, sent_ref.at[0], kept_second, sent_ref.at[1])):
+        start = pl.multiple_of((section_ref[0] ^ step) * width, width)
         out_ref[...] = total[:, pl.ds(start, width)].astype(out_ref.dtype)
 
 
-def combine(section, position, gates, blocks, split, kept):
+def combine(section, position, gates, blocks, split):
     capacity, features = blocks[0].shape
     rows = position.shape[0]
     count = len(blocks)
     width = features // split
-    types = [kept] + [jnp.bfloat16] * (split - 1)
+    kept = jax.ShapeDtypeStruct((rows, width), jnp.float32)
+    if split == 1:
+        out_shape = (jax.ShapeDtypeStruct((rows, width), jnp.bfloat16),)
+    else:
+        out_shape = (jax.ShapeDtypeStruct((2, rows, width), jnp.bfloat16), kept, kept)
     full = pl.BlockSpec(memory_space=pltpu.VMEM)
     return pl.pallas_call(
         functools.partial(combine_kernel, count, split),
-        out_shape=tuple(jax.ShapeDtypeStruct((rows, width), kind) for kind in types),
+        out_shape=out_shape,
         in_specs=[pl.BlockSpec(memory_space=pltpu.SMEM)] + [full] * (2 + count),
-        out_specs=[full] * split,
+        out_specs=[full] * len(out_shape),
         scratch_shapes=[
             vmem((count * capacity, features), jnp.bfloat16),
             vmem((rows, features), jnp.float32),
@@ -275,7 +281,7 @@
     me = section_ref[0]
     width = slices[0].shape[1]
     for step, piece in enumerate(slices):
-        owner = lax.rem(me - step + count, count)
+        owner = me ^ step
         mixed[:, pl.ds(pl.multiple_of(owner * width, width), width)] = piece[...].astype(
             jnp.float32
         )
@@ -525,15 +531,16 @@
 
     token_y = swap(tokens, "expert", 1)
     token_x = swap(tokens, "dp", 2)
-    ids_y = jnp.stack([expert_ids.T, swap(expert_ids.T, "expert", 1)])
-    ids_x = swap(ids_y, "dp", 2)
+    ids_own = expert_ids.T
+    ids_x, ids_y = swap(ids_own, "dp", 2), swap(ids_own, "expert", 1)
+    ids_far = swap(ids_x, "expert", 1)
     token_far = swap(token_y, "dp", 2)
 
     side = lax.rem(section, 2)
     share = token_count // 2
     grad_half = lax.dynamic_slice_in_dim(out_grad, side * share, share, 0)
-    half_y = swap(gate(grad_half, token_y, token_x), "expert", 1)
-    key_other = swap(gate(key_own, token_y, token_x), "expert", 1)
+    half_y = swap(gate(grad_half, token_y, ids_far), "expert", 1)
+    key_other = swap(gate(key_own, token_y), "expert", 1)
     other_y = swap(half_y, "section", 1)
     half_x = swap(gate(grad_half, token_far), "dp", 2)
     half_far = swap(gate(half_y, token_far), "dp", 2)
@@ -542,7 +549,7 @@
 
     row = lax.broadcasted_iota(jnp.int32, (token_count, token_count), 0)
     column = lax.broadcasted_iota(jnp.int32, (token_count, token_count), 1)
-    ids = jnp.stack([ids_y[0], ids_x[0], ids_y[1], ids_x[1]])
+    ids = jnp.stack([ids_own, ids_x, ids_y, ids_far])
     named_there = jnp.concatenate([(ids == here).any(axis=1), (ids == (here ^ 1)).any(axis=1)])
     before = jnp.dot(
         named_there.astype(jnp.bfloat16),
@@ -597,19 +604,21 @@
     )
     grads_core = swap(grads_sent, "dp", 1)
     held_gates = gate(gate_weights, grads_sent)
-    cuts = combine(which_section, position, held_gates, home, sections, jnp.float32)
-    mixed_parts = [shift(cuts[step], "section", step) for step in range(1, sections)]
+    sent_pair, first, second = combine(which_section, position, held_gates, home, sections)
+    from_pair = swap(sent_pair, "section", 1)
     states = dec_states[0]
     normed = normalize(states.astype(jnp.float32), norm_gain[0]).astype(jnp.bfloat16)
     asked = lax.dynamic_slice_in_dim(normed, (1 - y) * half, half, 1)
-    asked_here = swap(gate(asked, cuts[0]), "expert", 1)
-    mixed_sum = gate(cuts[0], grads_core, asked_here)
-    for part in mixed_parts:
-        mixed_sum = mixed_sum + part.astype(jnp.float32)
-    mixed_slice = mixed_sum.astype(jnp.bfloat16)
-    slices = [mixed_slice] + [shift(mixed_slice, "section", step) for step in range(1, sections)]
-
-    value_other = swap(gate(value_own, *mixed_parts), "expert", 1)
+    asked_here = swap(gate(asked, first), "expert", 1)
+    to_other = (second + from_pair[1].astype(jnp.float32)).astype(jnp.bfloat16)
+    from_other = swap(to_other, "section", 2)
+    mixed_sum = gate(first, grads_core) + from_pair[0].astype(jnp.float32)
+    mixed_slice = (mixed_sum + from_other.astype(jnp.float32)).astype(jnp.bfloat16)
+    mixed_near = swap(mixed_slice, "section", 1)
+    mixed_far = swap(jnp.stack([mixed_slice, mixed_near]), "section", 2)
+    slices = [mixed_slice, mixed_near, mixed_far[0], mixed_far[1]]
+
+    value_other = swap(gate(value_own, first), "expert", 1)
     query_there = jnp.dot(asked_here, query_own, preferred_element_type=jnp.float32)
     query_back = swap(query_there.astype(jnp.bfloat16), "expert", 1)
     out_other = swap(gate(out_own, value_other), "expert", 1)
@@ -617,8 +626,8 @@
     query_here = jnp.dot(normed_own, query_own, preferred_element_type=jnp.float32)
     query = (query_here + query_back.astype(jnp.float32)).astype(jnp.bfloat16)
 
-    sent_pair, kept_first, kept_second = expert_backward(
-        gate(jnp.stack([section, here]).astype(jnp.int32), slices[1]),
+    back_pair, back_first, back_second = expert_backward(
+        gate(jnp.stack([section, here]).astype(jnp.int32), mixed_near),
         near_codes + core_codes,
         grads_own,
         grads_core,
@@ -628,7 +637,7 @@
         weight_in,
         sections,
     )
-    held_tokens = gate(tokens, value_other, query_back, kept_first)
+    held_tokens = gate(tokens, value_other, query_back, back_first)
     memory = make_memory(which_section, held_tokens, slices, final_gain)
     memory_x = swap(memory, "dp", 2)
     memory_core = swap(memory, "dp", 1)
@@ -640,24 +649,26 @@
         return attend_sentence(place, src_lengths, rows_of, near, far, *pairs, *rest)
 
     context_own = sentence(x, memory, memory_core)
-    from_pair = swap(sent_pair, "section", 1)
-    to_other = (kept_second + from_pair[1].astype(jnp.float32)).astype(jnp.bfloat16)
-    from_other = swap(to_other, "section", 2)
-    backward_sum = kept_first + from_pair[0].astype(jnp.float32) + from_other.astype(jnp.float32)
+    back_from_pair = swap(back_pair, "section", 1)
+    back_to_other = (back_second + back_from_pair[1].astype(jnp.float32)).astype(jnp.bfloat16)
+    back_from_other = swap(back_to_other, "section", 2)
+    backward_sum = back_first + back_from_pair[0].astype(jnp.float32)
+    backward_sum = backward_sum + back_from_other.astype(jnp.float32)
     memory_far = swap(gate(memory_x, context_own), "dp", 1)
     sent, kept_mine, kept_other = sentence(
-        1 - x, memory_x, memory_far, gate(context_own, to_other), (out_own, out_other)
+        1 - x, memory_x, memory_far, gate(context_own, back_to_other), (out_own, out_other)
     )
 
     from_core = swap(sent, "dp", 1).astype(jnp.float32)
-    from_x = swap((gate(kept_other, from_other) + from_core[1]).astype(jnp.bfloat16), "dp", 2)
+    last = (kept_other + from_core[1]).astype(jnp.bfloat16)
+    from_x = swap(last, "dp", 2)
     attended = kept_mine + from_core[0] + from_x.astype(jnp.float32)
     dec_out = add_residual(attended, states, tgt_lengths)
 
-    grads_home = exchange(backward_sum.astype(jnp.bfloat16), group_size, capacity)
+    grads_home = exchange(gate(backward_sum.astype(jnp.bfloat16), last), group_size, capacity)
     natural = expert_ids * capacity + rank
     (token_grad,) = combine(
-        which_section, natural, gate_weights, [grads_home], 1, jnp.bfloat16
+        which_section, natural, gate_weights, [grads_home], 1
     )
     return (dec_out[None], token_grad)
 

time: 197 us -> 193 us (0.980)
  starting transfers between devices: 46.1 us -> 37 us
  waiting for transfers between devices: 76.7 us -> 82.8 us
  local copies, waits for them, and re-layouts: 17.6 us -> 13.8 us
  other arithmetic: 18.6 us -> 21.7 us
    ppermute x6 -> x0, waiting for transfers between devices: 24.1 us -> none  [shift(): lax.ppermute(value, axis, [(i, (i + step) % size) for i in range(size)])]
    ppermute x24 -> x29, waiting for transfers between devices: 46.6 us -> 70.4 us  [swap(): return lax.ppermute(value, axis, [(i, i ^ mask) for i in range(size)])]
    ppermute x6 -> x0, starting transfers between devices: 12.5 us -> none  [shift(): lax.ppermute(value, axis, [(i, (i + step) % size) for i in range(size)])]
    ppermute x24 -> x29, starting transfers between devices: 23.2 us -> 27.4 us  [swap(): return lax.ppermute(value, axis, [(i, i ^ mask) for i in range(size)])]
    ppermute x7, waiting for transfers between devices: 2.4 us -> 6.18 us  [send_home(): lax.ppermute(block, ('expert', 'dp'), [(i, i ^ code) for i in range(size)])]
    all_to_all x1, waiting for transfers between devices: 3.63 us -> 6.25 us  [exchange(): lax.all_to_all(sent, ('expert', 'dp'), split_axis=0, concat_axis=0, tiled...]
    convert_element_type x3 -> x4, other arithmetic: 3.25 us -> 4.81 us  [the longest x1 1.82 us: small_body(): last = (kept_other + from_core[1]).astype(jnp.bfloat16)]
    unnamed x73 -> x65, local copies, waits for them, and re-layouts: 9.99 us -> 8.93 us
  transfers between devices with their start and end apart: 38 -> 37, of which waited for: 17 -> 17; matrix products, arithmetic and copies ran while one was open for 16% -> 19% of each run, Pallas kernels for 14% -> 10%
where the time goes in v6:
time: 193 us; the launch traced here: 192 us
  waiting for transfers between devices  82.8 us (43%)
  starting transfers between devices  37 us (19%)
  Pallas kernels  27.7 us (14%)
  other arithmetic  21.7 us (11%)
  local copies, waits for them, and re-layouts  13.8 us (7%)
  matrix products  8.42 us (4%)
    ppermute x29, waiting for transfers between devices, swap(): return lax.ppermute(value, axis, [(i, i ^ mask) for i in range(size)])  70.4 us
    ppermute x29, starting transfers between devices, swap(): return lax.ppermute(value, axis, [(i, i ^ mask) for i in range(size)])  27.4 us
    pallas_call x2, Pallas kernels, attend_sentence(): pl.pallas_call(functools.partial(attend_kernel, project), out_shape=out_s...  12 us
    pallas_call x1, Pallas kernels, expert_backward(): pl.pallas_call(functools.partial(backward_kernel, split, codes), out_shap...  10.7 us
    unnamed x65, local copies, waits for them, and re-layouts  8.93 us
    all_to_all x1, waiting for transfers between devices, exchange(): lax.all_to_all(sent, ('expert', 'dp'), split_axis=0, concat_axis=0, tiled...  6.25 us
    ppermute x7, starting transfers between devices, send_home(): lax.ppermute(block, ('expert', 'dp'), [(i, i ^ code) for i in range(size)])  6.22 us
    ppermute x7, waiting for transfers between devices, send_home(): lax.ppermute(block, ('expert', 'dp'), [(i, i ^ code) for i in range(size)])  6.18 us
  transfers between devices with their start and end apart: 37, of which 17 were waited for; matrix products, arithmetic and copies ran while one was open for 19% of the time, Pallas kernels for 10%

profile of v6, /device:TPU:0, one launch (start us, length us, event | category | flops | bytes accessed | tf_op | source)
XLA Modules:
  0.0 192.5 jit_solution(6777147758130137949)
XLA Ops:
  0.6 3.0 %collective-permute-start = (s32[2,128]{1,0:T(2,128)}, s32[2,128]{1,0:T(2,128)S(1)}, u32[]{:S(2)}, u32[]{:S(2)}) collective-permute-start(s32[2,128]{1,0:T(2,128)} %bitcast.121), channel_id=1, source_target_pairs={{0,2},{1,3},{2,0},{3,1},{4,6},{5,7},{6,4},{7,5},{8,10},{9,11},{10,... | collective-permute-start | bytes 3080 | tf_op jit(solution)/shard_map/ppermute | solution.py:38
  3.6 1.5 collective-permute-start.1
  7.1 0.8 copy.36
  9.0 2.0 %collective-permute-start.2 = (s32[2,128]{1,0:T(2,128)S(1)}, s32[2,128]{1,0:T(2,128)S(1)}, u32[]{:S(2)}, u32[]{:S(2)}) collective-permute-start(s32[2,128]{1,0:T(2,128)S(1)} %collective-permute-done), channel_id=1, source_target_pairs={{0,4},{4,0},{1,5},{5,1},{2,6},{6,2},{3,7},{7,3},{8,12},{12,8},{9,1... | collective-permute-start | bytes 3080 | tf_op jit(solution)/shard_map/ppermute | solution.py:38
  11.1 1.0 constant_dynamic-slice_fusion.2
  12.1 6.5 %collective-permute-done.2 = s32[2,128]{1,0:T(2,128)S(1)} collective-permute-done((s32[2,128]{1,0:T(2,128)S(1)}, s32[2,128]{1,0:T(2,128)S(1)}, u32[]{:S(2)}, u32[]{:S(2)}) %collective-permute-start.2) | collective-permute-done | bytes 1056 | tf_op jit(solution)/shard_map/ppermute | solution.py:38
  19.1 1.4 convert_reduce_fusion
  20.9 4.2 %collective-permute-done.6.refs_2_ = bf16[64,2048]{1,0:T(8,128)(2,1)S(1)} collective-permute-done((bf16[64,2048]{1,0:T(8,128)(2,1)S(1)}, bf16[64,2048]{1,0:T(8,128)(2,1)S(1)}, u32[]{:S(2)}, u32[]{:S(2)}) %collective-permute-start.6) | collective-permute-done | bytes 262176 | tf_op jit(solution)/shard_map/ppermute | solution.py:38
  25.1 1.6 collective-permute-start.8
  26.7 2.2 %fusion.3 = f32[256]{0:T(256)} fusion(bf16[1,256,2048]{2,1,0:T(8,128)(2,1)} %param.22, f32[256]{0:T(256)S(1)} %broadcast_multiply_fusion.1), kind=kLoop, calls=%fused_computation.7 | loop fusion | flops 2096896 | bytes 1050624 | tf_op jit(solution)/shard_map/reduce_sum | solution.py:21
  30.2 2.4 %collective-permute-done.4.refs_3_ = bf16[128,2048]{1,0:T(8,128)(2,1)S(1)} collective-permute-done((bf16[128,2048]{1,0:T(8,128)(2,1)S(1)}, bf16[128,2048]{1,0:T(8,128)(2,1)S(1)}, u32[]{:S(2)}, u32[]{:S(2)}) %collective-permute-start.4) | collective-permute-done | bytes 524320 | tf_op jit(solution)/shard_map/ppermute | solution.py:38
  33.1 1.6 collective-permute-start.5
  34.7 1.0 copy-done.1
  35.7 1.3 dispatch.3
  37.1 3.2 %fusion.78 = f32[192,1024]{1,0:T(8,128)S(1)} fusion(bf16[192,2048]{1,0:T(8,128)(2,1)S(1)} %get-tuple-element.39, bf16[1,2048,1024]{2,1,0:T(8,128)(2,1)} %param.19), kind=kOutput, calls=%fused_computation.121 | convolution fusion | flops 805306368 | bytes 5767168 | tf_op jit(solution)/shard_map/dot_general | solution.py:571
  40.3 0.9 copy-done.17
  41.2 1.1 convolution_convert_fusion.1
  42.3 0.8 fusion.90
  43.7 1.5 collective-permute-start.12
  45.2 1.4 collective-permute-start.13
  46.7 1.6 collective-permute-start.9
  48.3 1.0 fusion.76
  49.3 1.1 convolution_convert_fusion
  50.4 8.0 %collective-permute-done.15.refs_3_ = bf16[1024,512]{1,0:T(8,128)(2,1)S(1)} collective-permute-done((bf16[1024,512]{1,0:T(8,128)(2,1)}, bf16[1024,512]{1,0:T(8,128)(2,1)S(1)}, u32[]{:S(2)}, u32[]{:S(2)}) %collective-permute-start.15) | collective-permute-done | bytes 1048608 | tf_op jit(solution)/shard_map/ppermute | solution.py:38
  58.4 1.0 fusion.89
  60.5 2.2 %collective-permute-start.19 = (bf16[48,2048]{1,0:T(8,128)(2,1)}, bf16[48,2048]{1,0:T(8,128)(2,1)S(1)}, u32[]{:S(2)}, u32[]{:S(2)}) collective-permute-start(bf16[48,2048]{1,0:T(8,128)(2,1)} %get-tuple-element.66), channel_id=1, source_target_pairs={{0,7},{1,6},{2,5},{3,4},{4,3},{5,2},{6,1},{7,0},{8,15},{9,14},{10,... | collective-permute-start | bytes 589832 | tf_op jit(solution)/shard_map/ppermute | solution.py:223
  62.7 1.5 dispatch.2
  64.3 0.9 copy-done.5
  65.1 0.9 copy-done.11
  66.3 5.6 %collective-permute-done.18.refs_6_ = bf16[48,2048]{1,0:T(8,128)(2,1)S(1)} collective-permute-done((bf16[48,2048]{1,0:T(8,128)(2,1)}, bf16[48,2048]{1,0:T(8,128)(2,1)S(1)}, u32[]{:S(2)}, u32[]{:S(2)}) %collective-permute-start.18) | collective-permute-done | bytes 196640 | tf_op jit(solution)/shard_map/ppermute | solution.py:223
  73.3 0.9 copy-done.7
  74.2 0.9 copy-done.9
  75.1 0.8 combine.2
  76.5 2.6 %fusion.5 = bf16[256,2048]{1,0:T(8,128)(2,1)} fusion(bf16[1,256,2048]{2,1,0:T(8,128)(2,1)} %param.22, f32[2048]{0:T(1024)S(1)} %bitcast.124, f32[256]{0:T(256)S(1)} %add_rsqrt_fusion, f32[256]{0:T(256)S(1)} %broadcast_multiply_fusion.1), kind=kLoop, calls=%fused_computation.9 | loop fusion | flops 2621440 | bytes 2107392 | tf_op jit(solution)/shard_map/convert_element_type | solution.py:610
  79.0 1.1 constant_dynamic-slice_fusion.3
  80.2 4.0 %collective-permute-done.24 = bf16[2,128,512]{2,1,0:T(8,128)(2,1)} collective-permute-done((bf16[2,128,512]{2,1,0:T(8,128)(2,1)S(1)}, bf16[2,128,512]{2,1,0:T(8,128)(2,1)}, u32[]{:S(2)}, u32[]{:S(2)}) %collective-permute-start.24) | collective-permute-done | bytes 262176 | tf_op jit(solution)/shard_map/ppermute | solution.py:38
  84.2 0.9 fusion.64
  85.2 2.6 %collective-permute-start.25 = (bf16[128,512]{1,0:T(8,128)(2,1)S(1)}, bf16[128,512]{1,0:T(8,128)(2,1)S(1)}, u32[]{:S(2)}, u32[]{:S(2)}) collective-permute-start(bf16[128,512]{1,0:T(8,128)(2,1)S(1)} %fusion.64), channel_id=1, source_target_pairs={{0,16},{8,24},{16,0},{24,8},{1,17},{9,25},{17,1},{25,9},{2,18},{10... | collective-permute-start | bytes 393224 | tf_op jit(solution)/shard_map/ppermute | solution.py:38
  88.8 4.4 %collective-permute-done.25 = bf16[128,512]{1,0:T(8,128)(2,1)S(1)} collective-permute-done((bf16[128,512]{1,0:T(8,128)(2,1)S(1)}, bf16[128,512]{1,0:T(8,128)(2,1)S(1)}, u32[]{:S(2)}, u32[]{:S(2)}) %collective-permute-start.25) | collective-permute-done | bytes 131104 | tf_op jit(solution)/shard_map/ppermute | solution.py:38
  93.2 0.9 fusion.66.refs_0_
  94.2 0.8 collective-permute-done.20
  95.5 0.8 collective-permute-start.21
  96.3 2.9 %collective-permute-done.26.refs_1_ = bf16[128,512]{1,0:T(8,128)(2,1)S(1)} collective-permute-done((bf16[128,512]{1,0:T(8,128)(2,1)S(1)}, bf16[128,512]{1,0:T(8,128)(2,1)S(1)}, u32[]{:S(2)}, u32[]{:S(2)}) %collective-permute-start.26) | collective-permute-done | bytes 131104 | tf_op jit(solution)/shard_map/ppermute | solution.py:38
  99.2 1.2 collective-permute-start.27
  100.4 2.1 %fusion.15 = (f32[192,1024]{1,0:T(8,128)}, f32[192,1024]{1,0:T(8,128)}) fusion(f32[192,1024]{1,0:T(8,128)S(1)} %copy-done.18, f32[192,1024]{1,0:T(8,128)S(1)} %copy-done.20), kind=kLoop, calls=%fused_computation.28 | loop fusion | flops 6684672 | bytes 3145728 | tf_op jit(solution)/shard_map/transpose(jvp())/add_any | solution.py:577
  102.5 10.7 %expert_backward.1 = (bf16[2,384,512]{2,1,0:T(8,128)(2,1)}, f32[384,512]{1,0:T(8,128)}, f32[384,512]{1,0:T(8,128)}) custom-call(s32[2]{0:T(128)} %pad_add_fusion.3.place_ref, bf16[192,2048]{1,0:T(8,128)(2,1)} %copy-done.5, bf16[192,2048]{1,0:T(8,128)(2,1)} %collective-permute-done.23.core_ref, f32[192,1024]{1,0:T(8,128)} %get-tuple-element.80.rise_own, ...), custom_call_target="tpu_custom_call" | custom-call | flops 1 | bytes 1 | tf_op jit(solution)/shard_map/expert_backward/pallas_call | solution.py:476
  113.3 2.1 %collective-permute-start.31 = (bf16[2,384,512]{2,1,0:T(8,128)(2,1)}, bf16[2,384,512]{2,1,0:T(8,128)(2,1)}, u32[]{:S(2)}, u32[]{:S(2)}) collective-permute-start(bf16[2,384,512]{2,1,0:T(8,128)(2,1)} %get-tuple-element.57), channel_id=1, source_target_pairs={{0,8},{8,0},{16,24},{24,16},{1,9},{9,1},{17,25},{25,17},{2,10},{10... | collective-permute-start | bytes 2359304 | tf_op jit(solution)/shard_map/ppermute | solution.py:38
  115.4 6.3 %collective-permute-done.21 = bf16[256,512]{1,0:T(8,128)(2,1)S(1)} collective-permute-done((bf16[256,512]{1,0:T(8,128)(2,1)S(1)}, bf16[256,512]{1,0:T(8,128)(2,1)S(1)}, u32[]{:S(2)}, u32[]{:S(2)}) %collective-permute-start.21) | collective-permute-done | bytes 262176 | tf_op jit(solution)/shard_map/ppermute | solution.py:38
  121.7 1.0 copy-done.16
  123.3 1.5 collective-permute-start.28
  125.9 1.4 add_convert_fusion
  128.0 5.4 %attend_sentence.2.refs_6_ = bf16[128,512]{1,0:T(8,128)(2,1)} custom-call(s32[3]{0:T(128)} %pad_add_fusion.4.place_ref, s32[2]{0:T(128)} %lengths_ref.3, bf16[128,512]{1,0:T(8,128)(2,1)} %get-tuple-element.74.query_ref, bf16[128,2048]{1,0:T(8,128)(2,1)} %copy-done.3, bf16[128,2048]{1,0:T(8,128)(2,1)} %collective-permute-done.29.refs_1_, ...), custom_call_target="tpu_custom_call" | custom-call | flops 1 | bytes 1 | tf_op jit(solution)/shard_map/attend_sentence/pallas_call | solution.py:416
  133.5 4.3 %collective-permute-done.28.refs_0_ = bf16[128,2048]{1,0:T(8,128)(2,1)} collective-permute-done((bf16[128,2048]{1,0:T(8,128)(2,1)S(1)}, bf16[128,2048]{1,0:T(8,128)(2,1)}, u32[]{:S(2)}, u32[]{:S(2)}) %collective-permute-start.28) | collective-permute-done | bytes 524320 | tf_op jit(solution)/shard_map/ppermute | solution.py:38
  138.3 1.1 fusion.40
  139.9 10.5 %collective-permute-done.32.refs_8_ = bf16[512,1024]{1,0:T(8,128)(2,1)} collective-permute-done((bf16[512,1024]{1,0:T(8,128)(2,1)}, bf16[512,1024]{1,0:T(8,128)(2,1)}, u32[]{:S(2)}, u32[]{:S(2)}) %collective-permute-start.32) | collective-permute-done | bytes 1048608 | tf_op jit(solution)/shard_map/ppermute | solution.py:38
  150.3 6.5 %attend_sentence.3 = (bf16[2,256,512]{2,1,0:T(8,128)(2,1)}, f32[256,512]{1,0:T(8,128)}, f32[256,512]{1,0:T(8,128)}) custom-call(s32[3]{0:T(128)} %pad_add_fusion.1.place_ref, s32[2]{0:T(128)} %lengths_ref.3, bf16[128,512]{1,0:T(8,128)(2,1)} %get-tuple-element.75.query_ref, bf16[128,2048]{1,0:T(8,128)(2,1)} %collective-permute-done.28.refs_0_, ...), custom_call_target="tpu_custom_call" | custom-call | flops 1 | bytes 1 | tf_op jit(solution)/shard_map/attend_sentence/pallas_call | solution.py:416
  157.0 2.7 %collective-permute-start.35 = (bf16[384,512]{1,0:T(8,128)(2,1)S(1)}, bf16[384,512]{1,0:T(8,128)(2,1)S(1)}, u32[]{:S(2)}, u32[]{:S(2)}) collective-permute-start(bf16[384,512]{1,0:T(8,128)(2,1)S(1)} %fusion.40), channel_id=1, source_target_pairs={{0,16},{8,24},{16,0},{24,8},{1,17},{9,25},{17,1},{25,9},{2,18},{10... | collective-permute-start | bytes 1179656 | tf_op jit(solution)/shard_map/ppermute | solution.py:38
  159.8 1.8 fusion.42
  162.3 15.5 %collective-permute-done.35 = bf16[384,512]{1,0:T(8,128)(2,1)S(1)} collective-permute-done((bf16[384,512]{1,0:T(8,128)(2,1)S(1)}, bf16[384,512]{1,0:T(8,128)(2,1)S(1)}, u32[]{:S(2)}, u32[]{:S(2)}) %collective-permute-start.35) | collective-permute-done | bytes 393248 | tf_op jit(solution)/shard_map/ppermute | solution.py:38
  177.8 1.9 fusion.39
  179.8 3.5 %all-to-all-start = ((bf16[8,48,512]{2,1,0:T(8,128)(2,1)}), bf16[8,48,512]{2,1,0:T(8,128)(2,1)S(1)}, u32[]{:S(2)}, u32[]{:S(2)}) async-start(bf16[8,48,512]{2,1,0:T(8,128)(2,1)} %bitcast.34), calls=%async_computation | async-start | bytes 786432 | tf_op jit(solution)/shard_map/all_to_all | solution.py:142
  183.4 1.8 fusion.63
  185.2 6.3 %all-to-all-done = bf16[8,48,512]{2,1,0:T(8,128)(2,1)S(1)} async-done(((bf16[8,48,512]{2,1,0:T(8,128)(2,1)}), bf16[8,48,512]{2,1,0:T(8,128)(2,1)S(1)}, u32[]{:S(2)}, u32[]{:S(2)}) %all-to-all-start) | async-done | bytes 393248 | tf_op jit(solution)/shard_map/all_to_all | solution.py:142
  191.5 1.0 combine.3
  (124 shorter events, 16.0 us)
Async XLA Ops:
  0.6 94.4 %copy-start = (bf16[1,1024,512]{2,1,0:T(8,128)(2,1)S(1)}, bf16[1,1024,512]{2,1,0:T(8,128)(2,1)}, u32[]{:S(2)}) copy-start(bf16[1,1024,512]{2,1,0:T(8,128)(2,1)} %param.26) | copy-start | bytes 3145732
  0.6 8.4 %collective-permute-start = (s32[2,128]{1,0:T(2,128)}, s32[2,128]{1,0:T(2,128)S(1)}, u32[]{:S(2)}, u32[]{:S(2)}) collective-permute-start(s32[2,128]{1,0:T(2,128)} %bitcast.121), channel_id=1, source_target_pairs={{0,2},{1,3},{2,0},{3,1},{4,6},{5,7},{6,4},{7,5},{8,10},{9,11},{10,... | collective-permute-start | bytes 3080 | tf_op jit(solution)/shard_map/ppermute | solution.py:38
  3.6 25.2 %collective-permute-start.1 = (s32[2,128]{1,0:T(2,128)}, s32[2,128]{1,0:T(2,128)S(1)}, u32[]{:S(2)}, u32[]{:S(2)}) collective-permute-start(s32[2,128]{1,0:T(2,128)} %bitcast.122), channel_id=1, source_target_pairs={{0,4},{4,0},{1,5},{5,1},{2,6},{6,2},{3,7},{7,3},{8,12},{12,8},{9,1... | collective-permute-start | bytes 3080 | tf_op jit(solution)/shard_map/ppermute | solution.py:38
  5.2 13.4 %collective-permute-start.3 = (bf16[128,2048]{1,0:T(8,128)(2,1)}, bf16[128,2048]{1,0:T(8,128)(2,1)S(1)}, u32[]{:S(2)}, u32[]{:S(2)}) collective-permute-start(bf16[128,2048]{1,0:T(8,128)(2,1)} %tokens_ref), channel_id=1, source_target_pairs={{0,4},{4,0},{1,5},{5,1},{2,6},{6,2},{3,7},{7,3},{8,12},{12,8},{9,1... | collective-permute-start | bytes 1572872 | tf_op jit(solution)/shard_map/ppermute | solution.py:38
  5.7 29.0 %collective-permute-start.10 = (bf16[128,2048]{1,0:T(8,128)(2,1)}, bf16[128,2048]{1,0:T(8,128)(2,1)S(1)}, u32[]{:S(2)}, u32[]{:S(2)}) collective-permute-start(bf16[128,2048]{1,0:T(8,128)(2,1)} %tokens_ref), channel_id=1, source_target_pairs={{0,2},{1,3},{2,0},{3,1},{4,6},{5,7},{6,4},{7,5},{8,10},{9,11},{10,... | collective-permute-start | bytes 1572872 | tf_op jit(solution)/shard_map/ppermute | solution.py:38
  9.0 9.5 %collective-permute-start.2 = (s32[2,128]{1,0:T(2,128)S(1)}, s32[2,128]{1,0:T(2,128)S(1)}, u32[]{:S(2)}, u32[]{:S(2)}) collective-permute-start(s32[2,128]{1,0:T(2,128)S(1)} %collective-permute-done), channel_id=1, source_target_pairs={{0,4},{4,0},{1,5},{5,1},{2,6},{6,2},{3,7},{7,3},{8,12},{12,8},{9,1... | collective-permute-start | bytes 3080 | tf_op jit(solution)/shard_map/ppermute | solution.py:38
  18.6 6.5 %collective-permute-start.6 = (bf16[64,2048]{1,0:T(8,128)(2,1)S(1)}, bf16[64,2048]{1,0:T(8,128)(2,1)S(1)}, u32[]{:S(2)}, u32[]{:S(2)}) collective-permute-start(bf16[64,2048]{1,0:T(8,128)(2,1)S(1)} %constant_dynamic-slice_fusion.2), channel_id=1, source_target_pairs={{0,4},{4,0},{1,5},{5,1},{2,6},{6,2},{3,7},{7,3},{8,12},{12,8},{9,1... | collective-permute-start | bytes 786440 | tf_op jit(solution)/shard_map/ppermute | solution.py:38
  20.5 12.2 %collective-permute-start.4 = (bf16[128,2048]{1,0:T(8,128)(2,1)S(1)}, bf16[128,2048]{1,0:T(8,128)(2,1)S(1)}, u32[]{:S(2)}, u32[]{:S(2)}) collective-permute-start(bf16[128,2048]{1,0:T(8,128)(2,1)S(1)} %collective-permute-done.3.refs_2_), channel_id=1, source_target_pairs={{0,2},{1,3},{2,0},{3,1},{4,6},{5,7},{6,4},{7,5},{8,10},{9,11},{10,... | collective-permute-start | bytes 1572872 | tf_op jit(solution)/shard_map/ppermute | solution.py:38
  25.1 9.6 %collective-permute-start.8 = (bf16[64,2048]{1,0:T(8,128)(2,1)S(1)}, bf16[64,2048]{1,0:T(8,128)(2,1)S(1)}, u32[]{:S(2)}, u32[]{:S(2)}) collective-permute-start(bf16[64,2048]{1,0:T(8,128)(2,1)S(1)} %collective-permute-done.6.refs_2_), channel_id=1, source_target_pairs={{0,8},{8,0},{16,24},{24,16},{1,9},{9,1},{17,25},{25,17},{2,10},{10... | collective-permute-start | bytes 786440 | tf_op jit(solution)/shard_map/ppermute | solution.py:38
  29.7 28.7 %collective-permute-start.15 = (bf16[1024,512]{1,0:T(8,128)(2,1)}, bf16[1024,512]{1,0:T(8,128)(2,1)S(1)}, u32[]{:S(2)}, u32[]{:S(2)}) collective-permute-start(bf16[1024,512]{1,0:T(8,128)(2,1)} %bitcast.115), channel_id=1, source_target_pairs={{0,4},{4,0},{1,5},{5,1},{2,6},{6,2},{3,7},{7,3},{8,12},{12,8},{9,1... | collective-permute-start | bytes 3145736 | tf_op jit(solution)/shard_map/ppermute | solution.py:38
  32.7 12.6 %collective-permute-start.7 = (bf16[64,2048]{1,0:T(8,128)(2,1)S(1)}, bf16[64,2048]{1,0:T(8,128)(2,1)S(1)}, u32[]{:S(2)}, u32[]{:S(2)}) collective-permute-start(bf16[64,2048]{1,0:T(8,128)(2,1)S(1)} %collective-permute-done.6.refs_2_), channel_id=1, source_target_pairs={{0,2},{1,3},{2,0},{3,1},{4,6},{5,7},{6,4},{7,5},{8,10},{9,11},{10,... | collective-permute-start | bytes 786440 | tf_op jit(solution)/shard_map/ppermute | solution.py:38
  33.1 10.5 %collective-permute-start.5 = (bf16[64,2048]{1,0:T(8,128)(2,1)S(1)}, bf16[64,2048]{1,0:T(8,128)(2,1)S(1)}, u32[]{:S(2)}, u32[]{:S(2)}) collective-permute-start(bf16[64,2048]{1,0:T(8,128)(2,1)S(1)} %constant_dynamic-slice_fusion.2), channel_id=1, source_target_pairs={{0,2},{1,3},{2,0},{3,1},{4,6},{5,7},{6,4},{7,5},{8,10},{9,11},{10,... | collective-permute-start | bytes 786440 | tf_op jit(solution)/shard_map/ppermute | solution.py:38
  34.7 1.0 copy-start.1
  35.7 5.5 %copy-start.14 = (bf16[1,1024,2048]{2,1,0:T(8,128)(2,1)S(1)}, bf16[1,1024,2048]{2,1,0:T(8,128)(2,1)}, u32[]{:S(2)}) copy-start(bf16[1,1024,2048]{2,1,0:T(8,128)(2,1)} %param.20) | copy-start | bytes 12582916
  37.0 9.6 %collective-permute-start.14 = (bf16[192,2048]{1,0:T(8,128)(2,1)S(1)}, bf16[192,2048]{1,0:T(8,128)(2,1)S(1)}, u32[]{:S(2)}, u32[]{:S(2)}) collective-permute-start(bf16[192,2048]{1,0:T(8,128)(2,1)S(1)} %get-tuple-element.40), channel_id=1, source_target_pairs={{0,1},{1,0},{2,3},{3,2},{4,5},{5,4},{6,7},{7,6},{8,9},{9,8},{10,11... | collective-permute-start | bytes 2359304 | tf_op jit(solution)/shard_map/ppermute | solution.py:38
  40.3 0.9 copy-start.17
  41.2 7.1 %copy-start.12 = (bf16[1,2048,1024]{2,1,0:T(8,128)(2,1)S(1)}, bf16[1,2048,1024]{2,1,0:T(8,128)(2,1)}, u32[]{:S(2)}) copy-start(bf16[1,2048,1024]{2,1,0:T(8,128)(2,1)} %param.19) | copy-start | bytes 12582916
  43.0 16.4 %collective-permute-start.11 = (bf16[48,2048]{1,0:T(8,128)(2,1)S(1)}, bf16[48,2048]{1,0:T(8,128)(2,1)S(1)}, u32[]{:S(2)}, u32[]{:S(2)}) collective-permute-start(bf16[48,2048]{1,0:T(8,128)(2,1)S(1)} %get-tuple-element.72), channel_id=1, source_target_pairs={{0,2},{1,3},{2,0},{3,1},{4,6},{5,7},{6,4},{7,5},{8,10},{9,11},{10,... | collective-permute-start | bytes 589832 | tf_op jit(solution)/shard_map/ppermute | solution.py:223
  43.7 16.9 %collective-permute-start.12 = (bf16[48,2048]{1,0:T(8,128)(2,1)S(1)}, bf16[48,2048]{1,0:T(8,128)(2,1)S(1)}, u32[]{:S(2)}, u32[]{:S(2)}) collective-permute-start(bf16[48,2048]{1,0:T(8,128)(2,1)S(1)} %get-tuple-element.71), channel_id=1, source_target_pairs={{0,4},{1,5},{2,6},{3,7},{4,0},{5,1},{6,2},{7,3},{8,12},{9,13},{10,... | collective-permute-start | bytes 589832 | tf_op jit(solution)/shard_map/ppermute | solution.py:223
  45.2 20.9 %collective-permute-start.13 = (bf16[48,2048]{1,0:T(8,128)(2,1)}, bf16[48,2048]{1,0:T(8,128)(2,1)S(1)}, u32[]{:S(2)}, u32[]{:S(2)}) collective-permute-start(bf16[48,2048]{1,0:T(8,128)(2,1)} %get-tuple-element.70), channel_id=1, source_target_pairs={{0,6},{1,7},{2,4},{3,5},{4,2},{5,3},{6,0},{7,1},{8,14},{9,15},{10,... | collective-permute-start | bytes 589832 | tf_op jit(solution)/shard_map/ppermute | solution.py:223
  46.7 13.9 %collective-permute-start.9 = (bf16[128,2048]{1,0:T(8,128)(2,1)S(1)}, bf16[128,2048]{1,0:T(8,128)(2,1)S(1)}, u32[]{:S(2)}, u32[]{:S(2)}) collective-permute-start(bf16[128,2048]{1,0:T(8,128)(2,1)S(1)} %constant_dynamic-update-slice_fusion), channel_id=1, source_target_pairs={{0,8},{8,0},{16,24},{24,16},{1,9},{9,1},{17,25},{25,17},{2,10},{10... | collective-permute-start | bytes 1572872 | tf_op jit(solution)/shard_map/ppermute | solution.py:38
  49.3 14.9 %copy-start.19 = (f32[192,1024]{1,0:T(8,128)}, f32[192,1024]{1,0:T(8,128)S(1)}, u32[]{:S(2)}) copy-start(f32[192,1024]{1,0:T(8,128)S(1)} %fusion.76) | copy-start | bytes 2359300
  49.3 13.4 %copy-start.29 = (f32[256]{0:T(256)S(1)}, f32[256]{0:T(256)}, u32[]{:S(2)}) copy-start(f32[256]{0:T(256)} %fusion.3) | copy-start | bytes 3076
  49.3 13.4 %copy-start.4 = (bf16[128,2048]{1,0:T(8,128)(2,1)S(1)}, bf16[128,2048]{1,0:T(8,128)(2,1)}, u32[]{:S(2)}) copy-start(bf16[128,2048]{1,0:T(8,128)(2,1)} %refs_0_.2) | copy-start | bytes 1572868
  49.3 16.7 %copy-start.27 = (f32[128,2]{0,1:T(2,128)S(1)}, f32[128,2]{0,1:T(2,128)}, u32[]{:S(2)}) copy-start(f32[128,2]{0,1:T(2,128)} %param.17) | copy-start | bytes 3076
  50.4 26.0 %copy-start.26 = (f32[1,2048]{1,0:T(1,128)S(1)}, f32[1,2048]{1,0:T(1,128)}, u32[]{:S(2)}) copy-start(f32[1,2048]{1,0:T(1,128)} %param.25) | copy-start | bytes 24580
  58.4 5.8 %copy-start.15 = (bf16[1024,512]{1,0:T(8,128)(2,1)}, bf16[1024,512]{1,0:T(8,128)(2,1)S(1)}, u32[]{:S(2)}) copy-start(bf16[1024,512]{1,0:T(8,128)(2,1)S(1)} %collective-permute-done.15.refs_3_) | copy-start | bytes 3145732
  59.4 6.8 %collective-permute-start.16 = (bf16[48,2048]{1,0:T(8,128)(2,1)}, bf16[48,2048]{1,0:T(8,128)(2,1)S(1)}, u32[]{:S(2)}, u32[]{:S(2)}) collective-permute-start(bf16[48,2048]{1,0:T(8,128)(2,1)} %get-tuple-element.69), channel_id=1, source_target_pairs={{0,1},{1,0},{2,3},{3,2},{4,5},{5,4},{6,7},{7,6},{8,9},{9,8},{10,11... | collective-permute-start | bytes 589832 | tf_op jit(solution)/shard_map/ppermute | solution.py:223
  59.4 6.9 %collective-permute-start.17 = (bf16[48,2048]{1,0:T(8,128)(2,1)}, bf16[48,2048]{1,0:T(8,128)(2,1)S(1)}, u32[]{:S(2)}, u32[]{:S(2)}) collective-permute-start(bf16[48,2048]{1,0:T(8,128)(2,1)} %get-tuple-element.68), channel_id=1, source_target_pairs={{0,3},{1,2},{2,1},{3,0},{4,7},{5,6},{6,5},{7,4},{8,11},{9,10},{10,... | collective-permute-start | bytes 589832 | tf_op jit(solution)/shard_map/ppermute | solution.py:223
  60.5 11.4 %collective-permute-start.18 = (bf16[48,2048]{1,0:T(8,128)(2,1)}, bf16[48,2048]{1,0:T(8,128)(2,1)S(1)}, u32[]{:S(2)}, u32[]{:S(2)}) collective-permute-start(bf16[48,2048]{1,0:T(8,128)(2,1)} %get-tuple-element.67), channel_id=1, source_target_pairs={{0,5},{1,4},{2,7},{3,6},{4,1},{5,0},{6,3},{7,2},{8,13},{9,12},{10,... | collective-permute-start | bytes 589832 | tf_op jit(solution)/shard_map/ppermute | solution.py:223
  60.5 12.0 %collective-permute-start.19 = (bf16[48,2048]{1,0:T(8,128)(2,1)}, bf16[48,2048]{1,0:T(8,128)(2,1)S(1)}, u32[]{:S(2)}, u32[]{:S(2)}) collective-permute-start(bf16[48,2048]{1,0:T(8,128)(2,1)} %get-tuple-element.66), channel_id=1, source_target_pairs={{0,7},{1,6},{2,5},{3,4},{4,3},{5,2},{6,1},{7,0},{8,15},{9,14},{10,... | collective-permute-start | bytes 589832 | tf_op jit(solution)/shard_map/ppermute | solution.py:223
  66.1 22.7 %collective-permute-start.23 = (bf16[192,2048]{1,0:T(8,128)(2,1)}, bf16[192,2048]{1,0:T(8,128)(2,1)}, u32[]{:S(2)}, u32[]{:S(2)}) collective-permute-start(bf16[192,2048]{1,0:T(8,128)(2,1)} %copy-done.11), channel_id=1, source_target_pairs={{0,1},{1,0},{2,3},{3,2},{4,5},{5,4},{6,7},{7,6},{8,9},{9,8},{10,11... | collective-permute-start | bytes 2359304 | tf_op jit(solution)/shard_map/ppermute | solution.py:38
  73.3 0.9 copy-start.7
  74.2 0.9 copy-start.9
  76.0 24.5 %copy-start.18 = (f32[192,1024]{1,0:T(8,128)S(1)}, f32[192,1024]{1,0:T(8,128)}, u32[]{:S(2)}) copy-start(f32[192,1024]{1,0:T(8,128)} %copy-done.17) | copy-start | bytes 2359300
  76.0 24.5 %copy-start.20 = (f32[192,1024]{1,0:T(8,128)S(1)}, f32[192,1024]{1,0:T(8,128)}, u32[]{:S(2)}) copy-start(f32[192,1024]{1,0:T(8,128)} %copy-done.19) | copy-start | bytes 2359300
  76.0 8.3 %collective-permute-start.24 = (bf16[2,128,512]{2,1,0:T(8,128)(2,1)S(1)}, bf16[2,128,512]{2,1,0:T(8,128)(2,1)}, u32[]{:S(2)}, u32[]{:S(2)}) collective-permute-start(bf16[2,128,512]{2,1,0:T(8,128)(2,1)S(1)} %get-tuple-element.47), channel_id=1, source_target_pairs={{0,8},{8,0},{16,24},{24,16},{1,9},{9,1},{17,25},{25,17},{2,10},{10... | collective-permute-start | bytes 786440 | tf_op jit(solution)/shard_map/ppermute | solution.py:38
  80.1 14.9 %collective-permute-start.20 = (bf16[256,1024]{1,0:T(8,128)(2,1)S(1)}, bf16[256,1024]{1,0:T(8,128)(2,1)S(1)}, u32[]{:S(2)}, u32[]{:S(2)}) collective-permute-start(bf16[256,1024]{1,0:T(8,128)(2,1)S(1)} %constant_dynamic-slice_fusion.3), channel_id=1, source_target_pairs={{0,4},{4,0},{1,5},{5,1},{2,6},{6,2},{3,7},{7,3},{8,12},{12,8},{9,1... | collective-permute-start | bytes 1572872 | tf_op jit(solution)/shard_map/ppermute | solution.py:38
  85.2 8.0 %collective-permute-start.25 = (bf16[128,512]{1,0:T(8,128)(2,1)S(1)}, bf16[128,512]{1,0:T(8,128)(2,1)S(1)}, u32[]{:S(2)}, u32[]{:S(2)}) collective-permute-start(bf16[128,512]{1,0:T(8,128)(2,1)S(1)} %fusion.64), channel_id=1, source_target_pairs={{0,16},{8,24},{16,0},{24,8},{1,17},{9,25},{17,1},{25,9},{2,18},{10... | collective-permute-start | bytes 393224 | tf_op jit(solution)/shard_map/ppermute | solution.py:38
  88.4 33.3 %collective-permute-start.22 = (bf16[1024,512]{1,0:T(8,128)(2,1)}, bf16[1024,512]{1,0:T(8,128)(2,1)S(1)}, u32[]{:S(2)}, u32[]{:S(2)}) collective-permute-start(bf16[1024,512]{1,0:T(8,128)(2,1)} %bitcast.118), channel_id=1, source_target_pairs={{0,4},{4,0},{1,5},{5,1},{2,6},{6,2},{3,7},{7,3},{8,12},{12,8},{9,1... | collective-permute-start | bytes 3145736 | tf_op jit(solution)/shard_map/ppermute | solution.py:38
  94.1 5.0 %collective-permute-start.26 = (bf16[128,512]{1,0:T(8,128)(2,1)S(1)}, bf16[128,512]{1,0:T(8,128)(2,1)S(1)}, u32[]{:S(2)}, u32[]{:S(2)}) collective-permute-start(bf16[128,512]{1,0:T(8,128)(2,1)S(1)} %fusion.66.refs_0_), channel_id=1, source_target_pairs={{0,8},{8,0},{16,24},{24,16},{1,9},{9,1},{17,25},{25,17},{2,10},{10... | collective-permute-start | bytes 393224 | tf_op jit(solution)/shard_map/ppermute | solution.py:38
  95.5 26.3 %collective-permute-start.21 = (bf16[256,512]{1,0:T(8,128)(2,1)S(1)}, bf16[256,512]{1,0:T(8,128)(2,1)S(1)}, u32[]{:S(2)}, u32[]{:S(2)}) collective-permute-start(bf16[256,512]{1,0:T(8,128)(2,1)S(1)} %convolution_convert_fusion.2), channel_id=1, source_target_pairs={{0,4},{4,0},{1,5},{5,1},{2,6},{6,2},{3,7},{7,3},{8,12},{12,8},{9,1... | collective-permute-start | bytes 786440 | tf_op jit(solution)/shard_map/ppermute | solution.py:38
  99.2 16.2 %collective-permute-start.27 = (bf16[2,128,512]{2,1,0:T(8,128)(2,1)S(1)}, bf16[2,128,512]{2,1,0:T(8,128)(2,1)S(1)}, u32[]{:S(2)}, u32[]{:S(2)}) collective-permute-start(bf16[2,128,512]{2,1,0:T(8,128)(2,1)S(1)} %pad_maximum_fusion), channel_id=1, source_target_pairs={{0,16},{8,24},{16,0},{24,8},{1,17},{9,25},{17,1},{25,9},{2,18},{10... | collective-permute-start | bytes 786440 | tf_op jit(solution)/shard_map/ppermute | solution.py:38
  102.5 20.2 %copy-start.2 = (bf16[128,2048]{1,0:T(8,128)(2,1)S(1)}, bf16[128,2048]{1,0:T(8,128)(2,1)}, u32[]{:S(2)}) copy-start(bf16[128,2048]{1,0:T(8,128)(2,1)} %tokens_ref) | copy-start | bytes 1572868
  102.5 20.2 %copy-start.10 = (f32[2048]{0:T(1024)S(1)}, f32[2048]{0:T(1024)}, u32[]{:S(2)}) copy-start(f32[2048]{0:T(1024)} %param.21) | copy-start | bytes 24580
  102.5 23.4 %copy-start.13 = (bf16[256,2048]{1,0:T(8,128)(2,1)S(1)}, bf16[256,2048]{1,0:T(8,128)(2,1)}, u32[]{:S(2)}) copy-start(bf16[256,2048]{1,0:T(8,128)(2,1)} %fusion.5) | copy-start | bytes 3145732
  113.3 25.0 %collective-permute-start.31 = (bf16[2,384,512]{2,1,0:T(8,128)(2,1)}, bf16[2,384,512]{2,1,0:T(8,128)(2,1)}, u32[]{:S(2)}, u32[]{:S(2)}) collective-permute-start(bf16[2,384,512]{2,1,0:T(8,128)(2,1)} %get-tuple-element.57), channel_id=1, source_target_pairs={{0,8},{8,0},{16,24},{24,16},{1,9},{9,1},{17,25},{25,17},{2,10},{10... | collective-permute-start | bytes 2359304 | tf_op jit(solution)/shard_map/ppermute | solution.py:38
  121.7 1.5 copy-start.25
  121.7 1.0 copy-start.16
  123.2 4.8 %copy-start.3 = (bf16[128,2048]{1,0:T(8,128)(2,1)}, bf16[128,2048]{1,0:T(8,128)(2,1)S(1)}, u32[]{:S(2)}) copy-start(bf16[128,2048]{1,0:T(8,128)(2,1)S(1)} %memory.1.refs_0_) | copy-start | bytes 1572868
  123.2 15.1 %copy-start.21 = (f32[384,512]{1,0:T(8,128)S(1)}, f32[384,512]{1,0:T(8,128)}, u32[]{:S(2)}) copy-start(f32[384,512]{1,0:T(8,128)} %get-tuple-element.56) | copy-start | bytes 2359300
  123.2 4.8 %collective-permute-start.29 = (bf16[128,2048]{1,0:T(8,128)(2,1)S(1)}, bf16[128,2048]{1,0:T(8,128)(2,1)}, u32[]{:S(2)}, u32[]{:S(2)}) collective-permute-start(bf16[128,2048]{1,0:T(8,128)(2,1)S(1)} %memory.1.refs_0_), channel_id=1, source_target_pairs={{0,1},{1,0},{2,3},{3,2},{4,5},{5,4},{6,7},{7,6},{8,9},{9,8},{10,11... | collective-permute-start | bytes 1572872 | tf_op jit(solution)/shard_map/ppermute | solution.py:38
  123.3 14.4 %collective-permute-start.28 = (bf16[128,2048]{1,0:T(8,128)(2,1)S(1)}, bf16[128,2048]{1,0:T(8,128)(2,1)}, u32[]{:S(2)}, u32[]{:S(2)}) collective-permute-start(bf16[128,2048]{1,0:T(8,128)(2,1)S(1)} %memory.1.refs_0_), channel_id=1, source_target_pairs={{0,2},{1,3},{2,0},{3,1},{4,6},{5,7},{6,4},{7,5},{8,10},{9,11},{10,... | collective-permute-start | bytes 1572872 | tf_op jit(solution)/shard_map/ppermute | solution.py:38
  124.8 25.5 %collective-permute-start.32 = (bf16[512,1024]{1,0:T(8,128)(2,1)}, bf16[512,1024]{1,0:T(8,128)(2,1)}, u32[]{:S(2)}, u32[]{:S(2)}) collective-permute-start(bf16[512,1024]{1,0:T(8,128)(2,1)} %bitcast.29.refs_7_), channel_id=1, source_target_pairs={{0,4},{4,0},{1,5},{5,1},{2,6},{6,2},{3,7},{7,3},{8,12},{12,8},{9,1... | collective-permute-start | bytes 3145736 | tf_op jit(solution)/shard_map/ppermute | solution.py:38
  137.7 2.1 %collective-permute-start.30 = (bf16[128,2048]{1,0:T(8,128)(2,1)}, bf16[128,2048]{1,0:T(8,128)(2,1)S(1)}, u32[]{:S(2)}, u32[]{:S(2)}) collective-permute-start(bf16[128,2048]{1,0:T(8,128)(2,1)} %collective-permute-done.28.refs_0_), channel_id=1, source_target_pairs={{0,1},{1,0},{2,3},{3,2},{4,5},{5,4},{6,7},{7,6},{8,9},{9,8},{10,11... | collective-permute-start | bytes 1572872 | tf_op jit(solution)/shard_map/ppermute | solution.py:38
  139.9 10.5 %copy-start.24 = (bf16[128,2048]{1,0:T(8,128)(2,1)}, bf16[128,2048]{1,0:T(8,128)(2,1)S(1)}, u32[]{:S(2)}) copy-start(bf16[128,2048]{1,0:T(8,128)(2,1)S(1)} %collective-permute-done.30.refs_1_) | copy-start | bytes 1572868
  150.3 27.5 %copy-start.22 = (f32[384,512]{1,0:T(8,128)S(1)}, f32[384,512]{1,0:T(8,128)}, u32[]{:S(2)}) copy-start(f32[384,512]{1,0:T(8,128)} %get-tuple-element.53) | copy-start | bytes 2359300
  156.9 26.3 %copy-start.30 = (s32[2]{0:T(128)S(1)}, s32[2]{0:T(128)}, u32[]{:S(2)}) copy-start(s32[2]{0:T(128)} %param.24) | copy-start | bytes 28
  156.9 26.4 %copy-start.28 = (f32[128,2]{0,1:T(2,128)S(1)}, f32[128,2]{0,1:T(2,128)}, u32[]{:S(2)}) copy-start(f32[128,2]{0,1:T(2,128)} %param.17) | copy-start | bytes 3076
  156.9 26.5 %copy-start.23 = (f32[256,512]{1,0:T(8,128)S(1)}, f32[256,512]{1,0:T(8,128)}, u32[]{:S(2)}) copy-start(f32[256,512]{1,0:T(8,128)} %get-tuple-element.60) | copy-start | bytes 1572868
  156.9 2.7 %collective-permute-start.33 = (bf16[2,256,512]{2,1,0:T(8,128)(2,1)}, bf16[2,256,512]{2,1,0:T(8,128)(2,1)S(1)}, u32[]{:S(2)}, u32[]{:S(2)}) collective-permute-start(bf16[2,256,512]{2,1,0:T(8,128)(2,1)} %get-tuple-element.61), channel_id=1, source_target_pairs={{0,1},{1,0},{2,3},{3,2},{4,5},{5,4},{6,7},{7,6},{8,9},{9,8},{10,11... | collective-permute-start | bytes 1572872 | tf_op jit(solution)/shard_map/ppermute | solution.py:38
  157.0 20.9 %collective-permute-start.35 = (bf16[384,512]{1,0:T(8,128)(2,1)S(1)}, bf16[384,512]{1,0:T(8,128)(2,1)S(1)}, u32[]{:S(2)}, u32[]{:S(2)}) collective-permute-start(bf16[384,512]{1,0:T(8,128)(2,1)S(1)} %fusion.40), channel_id=1, source_target_pairs={{0,16},{8,24},{16,0},{24,8},{1,17},{9,25},{17,1},{25,9},{2,18},{10... | collective-permute-start | bytes 1179656 | tf_op jit(solution)/shard_map/ppermute | solution.py:38
  161.6 21.8 %collective-permute-start.34 = (bf16[256,512]{1,0:T(8,128)(2,1)}, bf16[256,512]{1,0:T(8,128)(2,1)S(1)}, u32[]{:S(2)}, u32[]{:S(2)}) collective-permute-start(bf16[256,512]{1,0:T(8,128)(2,1)} %fusion.42), channel_id=1, source_target_pairs={{0,2},{1,3},{2,0},{3,1},{4,6},{5,7},{6,4},{7,5},{8,10},{9,11},{10,... | collective-permute-start | bytes 786440 | tf_op jit(solution)/shard_map/ppermute | solution.py:38
  179.8 11.7 %all-to-all-start = ((bf16[8,48,512]{2,1,0:T(8,128)(2,1)}), bf16[8,48,512]{2,1,0:T(8,128)(2,1)S(1)}, u32[]{:S(2)}, u32[]{:S(2)}) async-start(bf16[8,48,512]{2,1,0:T(8,128)(2,1)} %bitcast.34), calls=%async_computation | async-start | bytes 786432 | tf_op jit(solution)/shard_map/all_to_all | solution.py:142
  (4 other events, 3.1 us)

commit v7 on v6

--- a/solution.py
+++ b/solution.py
@@ -305,27 +305,42 @@
     )(me, tokens, gain[None], *slices)
 
 
-def attend_kernel(project, place_ref, lengths_ref, query_ref, *refs):
-    near_ref, far_ref, key_own, key_other, value_own, value_other = refs[:6]
+def normed_kernel(y_ref, states_ref, gain_ref, own_ref, other_ref):
+    values = normalize(states_ref[...].astype(jnp.float32), gain_ref[...]).astype(jnp.bfloat16)
+    width = own_ref.shape[1]
+    for out_ref, first in ((own_ref, y_ref[0] == 0), (other_ref, y_ref[0] == 1)):
+        out_ref[...] = jnp.where(first, values[:, :width], values[:, width:])
+
+
+def normed_halves(y, states, gain):
+    rows, features = states.shape
+    full = pl.BlockSpec(memory_space=pltpu.VMEM)
+    return pl.pallas_call(
+        normed_kernel,
+        out_shape=(jax.ShapeDtypeStruct((rows, features // 2), jnp.bfloat16),) * 2,
+        in_specs=[pl.BlockSpec(memory_space=pltpu.SMEM), full, full],
+        out_specs=[full] * 2,
+        compiler_params=pltpu.CompilerParams(vmem_limit_bytes=12 * 1024 * 1024),
+        cost_estimate=SHORT,
+        name="normed",
+    )(y.astype(jnp.int32).reshape(1), states, gain)
+
+
+def attend_kernel(place_ref, lengths_ref, query_ref, *refs):
+    near_ref, far_ref, key_own, key_top, key_low, value_own, value_other, out_ref = refs[:8]
+    source, key_weight, value_weight, keys, values, sems = refs[8:]
     y, core, sentence = place_ref[0], place_ref[1], place_ref[2]
-    if project:
-        done_ref, out_own, out_other, sent_ref, kept_mine, kept_other = refs[6:12]
-        source, key_weight, value_weight, keys, values, sems, out_weight, context = refs[12:]
-    else:
-        out_ref = refs[6]
-        source, key_weight, value_weight, keys, values, sems = refs[7:]
     rows = near_ref.shape[0]
     depth = key_own.shape[0]
     moves = [
         (near_ref, source.at[pl.ds(0, rows)]),
         (far_ref, source.at[pl.ds(rows, rows)]),
         (key_own, key_weight.at[y]),
-        (key_other, key_weight.at[1 - y]),
+        (key_top, key_weight.at[1 - y, pl.ds(0, depth // 2)]),
+        (key_low, key_weight.at[1 - y, pl.ds(depth // 2, depth // 2)]),
         (value_own, value_weight.at[y]),
         (value_other, value_weight.at[1 - y]),
     ]
-    if project:
-        moves += [(out_own, out_weight.at[y]), (out_other, out_weight.at[1 - y])]
     copies = [
         pltpu.make_async_copy(here, there, sems.at[i]) for i, (here, there) in enumerate(moves)
     ]
@@ -337,16 +352,14 @@
         total += jnp.dot(source[:, depth:], weight[1], preferred_element_type=jnp.float32)
         result[...] = total.astype(jnp.bfloat16)
 
-    for copy in copies[:4]:
+    for copy in copies[:5]:
         copy.wait()
     linear(key_weight, keys)
-    for copy in copies[4:6]:
+    for copy in copies[5:]:
         copy.wait()
     linear(value_weight, values)
 
-    targets = query_ref.shape[0]
-    mine = pl.ds(pl.multiple_of(sentence * targets, targets), targets)
-    column = lax.broadcasted_iota(jnp.int32, (targets, 2 * rows), 1)
+    column = lax.broadcasted_iota(jnp.int32, (query_ref.shape[0], 2 * rows), 1)
     position = jnp.where(column < rows, column + core * rows, column - core * rows)
     valid = position < lengths_ref[sentence]
     for head in range(query_ref.shape[1] // HEAD_DIM):
@@ -356,140 +369,167 @@
         weights = jnp.exp(scores - jnp.max(scores, axis=-1, keepdims=True))
         probs = (weights / jnp.sum(weights, axis=-1, keepdims=True)).astype(jnp.bfloat16)
         result = jnp.dot(probs, values[:, span], preferred_element_type=jnp.float32)
-        if project:
-            context[mine, span] = result.astype(jnp.bfloat16)
-        else:
-            out_ref[:, span] = result.astype(jnp.bfloat16)
-
-    if project:
-        others = pl.ds(pl.multiple_of((1 - sentence) * targets, targets), targets)
-        context[others, :] = done_ref[...]
-        for copy in copies[6:]:
-            copy.wait()
-        columns = sent_ref.shape[2]
-        x = 1 - sentence
-        for which in range(2):
-            half = jnp.where(which == 0, x, 1 - x)
-            kept_ref = kept_mine if which == 0 else kept_other
-            for out, side in ((sent_ref.at[which], 1 - core), (kept_ref, core)):
-                span = pl.ds(pl.multiple_of(side * columns, columns), columns)
-                part = jnp.dot(
-                    context[...], out_weight[half, :, span], preferred_element_type=jnp.float32
-                )
-                out[...] = part.astype(out.dtype)
-
-
-def attend_sentence(place, lengths, query, near, far, key_pair, value_pair, done=None, out_pair=()):
+        out_ref[:, span] = result.astype(jnp.bfloat16)
+
+
+def attend_sentence(place, lengths, query, near, far, key_parts, value_pair):
     rows, features = near.shape
-    depth, width = key_pair[0].shape
-    project = done is not None
+    depth, width = key_parts[0].shape
     hold = pl.BlockSpec(memory_space=pltpu.HBM)
     smem = pl.BlockSpec(memory_space=pltpu.SMEM)
     full = pl.BlockSpec(memory_space=pltpu.VMEM)
-    operands = [place, lengths, query, near, far, *key_pair, *value_pair]
-    in_specs = [smem, smem, full] + [hold] * 6
-    scratch = [
-        vmem((2 * rows, features), jnp.bfloat16),
-        vmem((2, depth, width), jnp.bfloat16),
-        vmem((2, depth, width), jnp.bfloat16),
-        vmem((2 * rows, width), jnp.bfloat16),
-        vmem((2 * rows, width), jnp.bfloat16),
-        pltpu.SemaphoreType.DMA((8,)),
-    ]
-    if project:
-        targets = 2 * query.shape[0]
-        columns = out_pair[0].shape[1] // 2
-        operands += [done, *out_pair]
-        in_specs += [full, hold, hold]
-        scratch += [
-            vmem((2,) + out_pair[0].shape, jnp.bfloat16),
-            vmem((targets, width), jnp.bfloat16),
-        ]
-        out_shape = (
-            jax.ShapeDtypeStruct((2, targets, columns), jnp.bfloat16),
-            jax.ShapeDtypeStruct((targets, columns), jnp.float32),
-            jax.ShapeDtypeStruct((targets, columns), jnp.float32),
-        )
-        out_specs = [full] * 3
-    else:
-        out_shape, out_specs = jax.ShapeDtypeStruct(query.shape, jnp.bfloat16), full
     return pl.pallas_call(
-        functools.partial(attend_kernel, project),
-        out_shape=out_shape,
-        in_specs=in_specs,
-        out_specs=out_specs,
-        scratch_shapes=scratch,
+        attend_kernel,
+        out_shape=jax.ShapeDtypeStruct(query.shape, jnp.bfloat16),
+        in_specs=[smem, smem, full] + [hold] * 7,
+        out_specs=full,
+        scratch_shapes=[
+            vmem((2 * rows, features), jnp.bfloat16),
+            vmem((2, depth, width), jnp.bfloat16),
+            vmem((2, depth, width), jnp.bfloat16),
+            vmem((2 * rows, width), jnp.bfloat16),
+            vmem((2 * rows, width), jnp.bfloat16),
+            pltpu.SemaphoreType.DMA((7,)),
+        ],
         compiler_params=pltpu.CompilerParams(vmem_limit_bytes=56 * 1024 * 1024),
         cost_estimate=SHORT,
         name="attend_sentence",
-    )(*operands)
-
-
-def backward_kernel(split, codes, place_ref, own_ref, core_ref, rise_own, rise_core, out_ref, in_ref, *refs):
-    sent_ref, kept_first, kept_second = refs[:3]
-    grads, rise, weight_out, weight_in, slope, sems = refs[3:]
+    )(place, lengths, query, near, far, *key_parts, *value_pair)
+
+
+def project_kernel(place_ref, mine_ref, done_ref, own_ref, other_ref, *refs):
+    sent, kept_mine, kept_other, context = refs
+    y, core, x = place_ref[0], place_ref[1], place_ref[2]
+    targets = mine_ref.shape[0]
+    for part, sentence in ((mine_ref, x), (done_ref, 1 - x)):
+        context[pl.ds(pl.multiple_of(sentence * targets, targets), targets), :] = part[...]
+    columns = kept_mine.shape[1]
+    outs = ((sent.at[0], kept_mine), (sent.at[1], kept_other))
+
+    def write(weight_ref, chosen):
+        for side, out_ref in zip((1 - core, core), chosen):
+            span = pl.ds(pl.multiple_of(side * columns, columns), columns)
+            part = jnp.dot(context[...], weight_ref[:, span], preferred_element_type=jnp.float32)
+            out_ref[...] = part.astype(out_ref.dtype)
+
+    @pl.when(x == y)
+    def _():
+        write(own_ref, outs[0])
+        write(other_ref, outs[1])
+
+    @pl.when(x != y)
+    def _():
+        write(other_ref, outs[0])
+        write(own_ref, outs[1])
+
+
+def project(place, mine, done, out_own, out_other):
+    targets, width = 2 * mine.shape[0], mine.shape[1]
+    columns = out_own.shape[1] // 2
+    full = pl.BlockSpec(memory_space=pltpu.VMEM)
+    kept = jax.ShapeDtypeStruct((targets, columns), jnp.float32)
+    return pl.pallas_call(
+        project_kernel,
+        out_shape=(jax.ShapeDtypeStruct((2, targets, columns), jnp.bfloat16), kept, kept),
+        in_specs=[pl.BlockSpec(memory_space=pltpu.SMEM)] + [full] * 4,
+        out_specs=[full] * 3,
+        scratch_shapes=[vmem((targets, width), jnp.bfloat16)],
+        compiler_params=pltpu.CompilerParams(vmem_limit_bytes=16 * 1024 * 1024),
+        cost_estimate=SHORT,
+        name="project",
+    )(place, mine, done, out_own, out_other)
+
+
+def slope_kernel(codes, here_ref, own_ref, core_ref, rise_own, rise_core, out_ref, slope, *refs):
+    grads, rise, weight_out, sems = refs
     rows = own_ref.shape[0]
-    hidden, features = weight_out.shape
-    width = features // split
+    hidden = weight_out.shape[0]
     chunk = hidden // 4
     moves = []
-    for part in range(4):
-        span = pl.ds(part * chunk, chunk)
-        moves.append((out_ref.at[span], weight_out.at[span]))
     block = 2 * rows // len(codes)
     for order, code in enumerate(codes):
-        source = place_ref[1] ^ code
+        source = here_ref[0] ^ code
         there = pl.ds(pl.multiple_of(source * block, 16), block)
         here = pl.ds(order * block % rows, block)
         own = order * block < rows
         moves.append(((own_ref if own else core_ref).at[here], grads.at[there]))
         moves.append(((rise_own if own else rise_core).at[here], rise.at[there]))
-    moves.append((in_ref, weight_in))
+    for part in range(4):
+        span = pl.ds(part * chunk, chunk)
+        moves.append((out_ref.at[span], weight_out.at[span]))
     copies = [
         pltpu.make_async_copy(here, there, sems.at[i]) for i, (here, there) in enumerate(moves)
     ]
     for copy in copies:
         copy.start()
-    for copy in copies[4:-1]:
+    for copy in copies[:-4]:
         copy.wait()
     for part in range(4):
-        copies[part].wait()
+        copies[part - 4].wait()
         span = slice(part * chunk, (part + 1) * chunk)
         back = contract_last(grads[...], weight_out[span, :])
         slope[:, span] = (back * rise[:, span]).astype(jnp.bfloat16)
-    copies[-1].wait()
-    outs = (kept_first, sent_ref.at[0], kept_second, sent_ref.at[1])
-    for step, out_ref in enumerate(outs):
-        start = pl.multiple_of((place_ref[0] ^ step) * width, width)
-        part = contract_last(slope[...], weight_in[pl.ds(start, width), :])
-        out_ref[...] = part.astype(out_ref.dtype)
-
-
-def expert_backward(
-    place, codes, grads_own, grads_core, rise_own, rise_core, weight_out, weight_in, split
-):
+
+
+def expert_slope(here, codes, grads_own, grads_core, rise_own, rise_core, weight_out):
     rows = 2 * grads_own.shape[0]
     hidden, features = weight_out.shape
     hold = pl.BlockSpec(memory_space=pltpu.HBM)
-    width = features // split
-    kept = jax.ShapeDtypeStruct((rows, width), jnp.float32)
     return pl.pallas_call(
-        functools.partial(backward_kernel, split, codes),
-        out_shape=(jax.ShapeDtypeStruct((2, rows, width), jnp.bfloat16), kept, kept),
-        in_specs=[pl.BlockSpec(memory_space=pltpu.SMEM)] + [hold] * 6,
-        out_specs=[pl.BlockSpec(memory_space=pltpu.VMEM)] * 3,
+        functools.partial(slope_kernel, codes),
+        out_shape=jax.ShapeDtypeStruct((rows, hidden), jnp.bfloat16),
+        in_specs=[pl.BlockSpec(memory_space=pltpu.SMEM)] + [hold] * 5,
+        out_specs=pl.BlockSpec(memory_space=pltpu.VMEM),
         scratch_shapes=[
             vmem((rows, features), jnp.bfloat16),
             vmem((rows, hidden), jnp.float32),
             vmem((hidden, features), jnp.bfloat16),
+            pltpu.SemaphoreType.DMA((4 + 2 * len(codes),)),
+        ],
+        compiler_params=pltpu.CompilerParams(vmem_limit_bytes=56 * 1024 * 1024),
+        cost_estimate=SHORT,
+        name="expert_slope",
+    )(here, grads_own, grads_core, rise_own, rise_core, weight_out)
+
+
+def backward_kernel(split, section_ref, slope_ref, in_ref, sent_ref, kept_first, kept_second, *refs):
+    weight_in, sems = refs
+    width = weight_in.shape[0] // split
+    outs = (sent_ref.at[0], sent_ref.at[1], kept_first, kept_second)
+    spans, copies = [], []
+    for i, step in enumerate((1, 3, 0, 2)):
+        start = pl.multiple_of((section_ref[0] ^ step) * width, width)
+        spans.append(pl.ds(start, width))
+        copies.append(
+            pltpu.make_async_copy(in_ref.at[spans[i]], weight_in.at[spans[i]], sems.at[i])
+        )
+    for copy in copies:
+        copy.start()
+    for copy, span, out_ref in zip(copies, spans, outs):
+        copy.wait()
+        part = contract_last(slope_ref[...], weight_in[span, :])
+        out_ref[...] = part.astype(out_ref.dtype)
+
+
+def expert_backward(section, slope, weight_in, split):
+    rows, hidden = slope.shape
+    features = weight_in.shape[0]
+    width = features // split
+    full = pl.BlockSpec(memory_space=pltpu.VMEM)
+    kept = jax.ShapeDtypeStruct((rows, width), jnp.float32)
+    return pl.pallas_call(
+        functools.partial(backward_kernel, split),
+        out_shape=(jax.ShapeDtypeStruct((2, rows, width), jnp.bfloat16), kept, kept),
+        in_specs=[pl.BlockSpec(memory_space=pltpu.SMEM), full, pl.BlockSpec(memory_space=pltpu.HBM)],
+        out_specs=[full] * 3,
+        scratch_shapes=[
             vmem((features, hidden), jnp.bfloat16),
-            vmem((rows, hidden), jnp.bfloat16),
-            pltpu.SemaphoreType.DMA((5 + 2 * len(codes),)),
+            pltpu.SemaphoreType.DMA((split,)),
         ],
         compiler_params=pltpu.CompilerParams(vmem_limit_bytes=56 * 1024 * 1024),
         cost_estimate=SHORT,
         name="expert_backward",
-    )(place, grads_own, grads_core, rise_own, rise_core, weight_out, weight_in)
+    )(section, slope, weight_in)
 
 
 def small_body(
@@ -540,7 +580,11 @@
     share = token_count // 2
     grad_half = lax.dynamic_slice_in_dim(out_grad, side * share, share, 0)
     half_y = swap(gate(grad_half, token_y, ids_far), "expert", 1)
-    key_other = swap(gate(key_own, token_y), "expert", 1)
+    depth = key_own.shape[0] // 2
+    key_top = swap(gate(key_own[:depth], token_y), "expert", 1)
+    key_low = swap(gate(key_own[depth:], key_top), "expert", 1)
+    states = dec_states[0]
+    normed_own, asked = normed_halves(y, states, norm_gain)
     other_y = swap(half_y, "section", 1)
     half_x = swap(gate(grad_half, token_far), "dp", 2)
     half_far = swap(gate(half_y, token_far), "dp", 2)
@@ -578,7 +622,7 @@
 
     rows_own, rows_sent = dispatch(
         which_section,
-        gate(code, other_y),
+        gate(code, key_top, asked),
         [tokens, token_x, token_y, token_far],
         tuple(((place, 0, token_count, None),) for place in range(4)),
         capacity,
@@ -586,13 +630,13 @@
     rows_core = swap(rows_sent, "dp", 1)
     pre_own, part_own = forward(rows_own)
     pre_core, part_core = forward(rows_core)
-    part_core = gate(part_core, key_other, half_pair)
+    part_core = gate(part_core, key_low, half_pair, other_y)
     rise_own, rise_core = slope_of(gate(pre_own, part_core)), slope_of(gate(pre_core, part_core))
     home = send_home(part_own, near_codes, capacity) + send_home(part_core, core_codes, capacity)
 
     grads_own, grads_sent = dispatch(
         which_section,
-        code,
+        gate(code, rise_own, rise_core),
         [out_grad, half_x, half_y, half_far, other_y, other_pair],
         (
             ((0, 0, token_count, None),),
@@ -606,58 +650,56 @@
     held_gates = gate(gate_weights, grads_sent)
     sent_pair, first, second = combine(which_section, position, held_gates, home, sections)
     from_pair = swap(sent_pair, "section", 1)
-    states = dec_states[0]
-    normed = normalize(states.astype(jnp.float32), norm_gain[0]).astype(jnp.bfloat16)
-    asked = lax.dynamic_slice_in_dim(normed, (1 - y) * half, half, 1)
     asked_here = swap(gate(asked, first), "expert", 1)
     to_other = (second + from_pair[1].astype(jnp.float32)).astype(jnp.bfloat16)
     from_other = swap(to_other, "section", 2)
-    mixed_sum = gate(first, grads_core) + from_pair[0].astype(jnp.float32)
-    mixed_slice = (mixed_sum + from_other.astype(jnp.float32)).astype(jnp.bfloat16)
-    mixed_near = swap(mixed_slice, "section", 1)
-    mixed_far = swap(jnp.stack([mixed_slice, mixed_near]), "section", 2)
-    slices = [mixed_slice, mixed_near, mixed_far[0], mixed_far[1]]
-
-    value_other = swap(gate(value_own, first), "expert", 1)
-    query_there = jnp.dot(asked_here, query_own, preferred_element_type=jnp.float32)
-    query_back = swap(query_there.astype(jnp.bfloat16), "expert", 1)
-    out_other = swap(gate(out_own, value_other), "expert", 1)
-    normed_own = lax.dynamic_slice_in_dim(normed, y * half, half, 1)
-    query_here = jnp.dot(normed_own, query_own, preferred_element_type=jnp.float32)
-    query = (query_here + query_back.astype(jnp.float32)).astype(jnp.bfloat16)
-
-    back_pair, back_first, back_second = expert_backward(
-        gate(jnp.stack([section, here]).astype(jnp.int32), mixed_near),
+    slope = expert_slope(
+        gate(here.astype(jnp.int32).reshape(1), to_other),
         near_codes + core_codes,
         grads_own,
         grads_core,
         rise_own,
         rise_core,
         weight_out,
-        weight_in,
-        sections,
     )
-    held_tokens = gate(tokens, value_other, query_back, back_first)
-    memory = make_memory(which_section, held_tokens, slices, final_gain)
+    mixed_sum = gate(first, slope) + from_pair[0].astype(jnp.float32)
+    mixed_slice = (mixed_sum + from_other.astype(jnp.float32)).astype(jnp.bfloat16)
+    mixed_near = swap(mixed_slice, "section", 1)
+    back_pair, back_first, back_second = expert_backward(
+        gate(which_section, mixed_slice), slope, weight_in, sections
+    )
+    mixed_far = swap(jnp.stack([mixed_slice, gate(mixed_near, back_first)]), "section", 2)
+    slices = [mixed_slice, mixed_near, mixed_far[0], mixed_far[1]]
+
+    value_other = swap(gate(value_own, first), "expert", 1)
+    query_there = jnp.dot(asked_here, query_own, preferred_element_type=jnp.float32)
+    query_back = swap(query_there.astype(jnp.bfloat16), "expert", 1)
+    out_other = swap(gate(out_own, value_other), "expert", 1)
+    query_here = jnp.dot(normed_own, query_own, preferred_element_type=jnp.float32)
+    query = (query_here + query_back.astype(jnp.float32)).astype(jnp.bfloat16)
+
+    memory = make_memory(which_section, tokens, slices, final_gain)
     memory_x = swap(memory, "dp", 2)
     memory_core = swap(memory, "dp", 1)
 
-    def sentence(which, near, far, *rest):
-        place = jnp.stack([y, core, which]).astype(jnp.int32)
+    def sentence(which, near, far, *after):
+        place = gate(jnp.stack([y, core, which]).astype(jnp.int32), *after)
         rows_of = lax.dynamic_slice_in_dim(query, which * TGT_LEN, TGT_LEN, 0)
-        pairs = (key_own, key_other), (value_own, value_other)
-        return attend_sentence(place, src_lengths, rows_of, near, far, *pairs, *rest)
-
-    context_own = sentence(x, memory, memory_core)
+        parts = (key_own, key_top, key_low), (value_own, value_other)
+        return attend_sentence(place, src_lengths, rows_of, near, far, *parts)
+
     back_from_pair = swap(back_pair, "section", 1)
     back_to_other = (back_second + back_from_pair[1].astype(jnp.float32)).astype(jnp.bfloat16)
-    back_from_other = swap(back_to_other, "section", 2)
+    part = back_to_other.shape[0] // 2
+    back_top = swap(back_to_other[:part], "section", 2)
+    back_low = swap(gate(back_to_other[part:], back_top), "section", 2)
     backward_sum = back_first + back_from_pair[0].astype(jnp.float32)
-    backward_sum = backward_sum + back_from_other.astype(jnp.float32)
-    memory_far = swap(gate(memory_x, context_own), "dp", 1)
-    sent, kept_mine, kept_other = sentence(
-        1 - x, memory_x, memory_far, gate(context_own, back_to_other), (out_own, out_other)
-    )
+    backward_sum = backward_sum + jnp.concatenate([back_top, back_low], axis=0).astype(jnp.float32)
+    context_own = sentence(x, memory, memory_core, back_top)
+    memory_far = swap(memory_x, "dp", 1)
+    context_other = sentence(1 - x, memory_x, memory_far)
+    place = gate(jnp.stack([y, core, x]).astype(jnp.int32), back_low)
+    sent, kept_mine, kept_other = project(place, context_own, context_other, out_own, out_other)
 
     from_core = swap(sent, "dp", 1).astype(jnp.float32)
     last = (kept_other + from_core[1]).astype(jnp.bfloat16)

time: 193 us -> 191 us (0.990)
  other arithmetic: 21.7 us -> 12.1 us
  waiting for transfers between devices: 82.8 us -> 76.6 us
  Pallas kernels: 27.7 us -> 33.4 us
  local copies, waits for them, and re-layouts: 13.8 us -> 17.9 us
  starting transfers between devices: 37 us -> 40.5 us
    pallas_call x3 -> x6, Pallas kernels: 22.7 us -> 27.5 us  [the longest x2 10.9 us: attend_sentence(): pl.pallas_call(attend_kernel, out_shape=jax.ShapeDtypeStruct(query.shape,...]
    ppermute x29 -> x31, waiting for transfers between devices: 70.4 us -> 65.7 us  [swap(): return lax.ppermute(value, axis, [(i, i ^ mask) for i in range(size)])]
    reduce_sum x2 -> x0, other arithmetic: 3.65 us -> none  [the longest x1 2.2 us: normalize(): spread = jnp.mean(centred * centred, axis=-1, keepdims=True)]
    ppermute x29 -> x31, starting transfers between devices: 27.4 us -> 30.7 us  [swap(): return lax.ppermute(value, axis, [(i, i ^ mask) for i in range(size)])]
    slice x0 -> x2, local copies, waits for them, and re-layouts: none -> 3.13 us  [the longest x1 2.26 us: small_body(): key_low = swap(gate(key_own[depth:], key_top), 'expert', 1)]
    all_to_all x1, waiting for transfers between devices: 6.25 us -> 4.18 us  [exchange(): lax.all_to_all(sent, ('expert', 'dp'), split_axis=0, concat_axis=0, tiled...]
    unnamed x65 -> x67, local copies, waits for them, and re-layouts: 8.93 us -> 10.3 us
  transfers between devices with their start and end apart: 37 -> 39, of which waited for: 17 -> 14; matrix products, arithmetic and copies ran while one was open for 19% -> 15% of each run, Pallas kernels for 10% -> 16%
where the time goes in v7:
time: 191 us
  waiting for transfers between devices  76.6 us (40%)
  starting transfers between devices  40.5 us (21%)
  Pallas kernels  33.4 us (17%)
  local copies, waits for them, and re-layouts  17.9 us (9%)
  other arithmetic  12.1 us (6%)
  matrix products  9 us (5%)
    ppermute x31, waiting for transfers between devices, swap(): return lax.ppermute(value, axis, [(i, i ^ mask) for i in range(size)])  65.7 us
    ppermute x31, starting transfers between devices, swap(): return lax.ppermute(value, axis, [(i, i ^ mask) for i in range(size)])  30.7 us
    pallas_call x2, Pallas kernels, attend_sentence(): pl.pallas_call(attend_kernel, out_shape=jax.ShapeDtypeStruct(query.shape,...  10.9 us
    unnamed x67, local copies, waits for them, and re-layouts  10.3 us
    pallas_call x1, Pallas kernels, expert_slope(): pl.pallas_call(functools.partial(slope_kernel, codes), out_shape=jax.Shap...  7.34 us
    ppermute x7, waiting for transfers between devices, send_home(): lax.ppermute(block, ('expert', 'dp'), [(i, i ^ code) for i in range(size)])  6.72 us
    ppermute x7, starting transfers between devices, send_home(): lax.ppermute(block, ('expert', 'dp'), [(i, i ^ code) for i in range(size)])  6.39 us
    pallas_call x1, Pallas kernels, expert_backward(): pl.pallas_call(functools.partial(backward_kernel, split), out_shape=(jax....  5.72 us
  transfers between devices with their start and end apart: 39, of which 14 were waited for; matrix products, arithmetic and copies ran while one was open for 15% of the time, Pallas kernels for 16%

profile of v7, /device:TPU:0, one launch (start us, length us, event | category | flops | bytes accessed | tf_op | source)
XLA Modules:
  0.0 190.6 jit_solution(12895646589810213580)
XLA Ops:
  0.7 3.0 %collective-permute-start = (s32[2,128]{1,0:T(2,128)}, s32[2,128]{1,0:T(2,128)S(1)}, u32[]{:S(2)}, u32[]{:S(2)}) collective-permute-start(s32[2,128]{1,0:T(2,128)} %bitcast.112), channel_id=1, source_target_pairs={{0,2},{1,3},{2,0},{3,1},{4,6},{5,7},{6,4},{7,5},{8,10},{9,11},{10,... | collective-permute-start | bytes 3080 | tf_op jit(solution)/shard_map/ppermute | solution.py:38
  3.7 1.5 collective-permute-start.1
  5.8 1.7 constant_dynamic-slice_fusion.2
  7.4 2.3 %slice_bitcast_fusion.2 = (bf16[512,512]{1,0:T(8,128)(2,1)}, bf16[512,512]{1,0:T(8,128)(2,1)}) fusion(bf16[1,1024,512]{2,1,0:T(8,128)(2,1)} %param.27), kind=kLoop, calls=%fused_computation.58 | loop fusion | bytes 2097152 | tf_op jit(solution)/shard_map/slice | solution.py:585
  10.4 2.0 %collective-permute-start.2 = (s32[2,128]{1,0:T(2,128)S(1)}, s32[2,128]{1,0:T(2,128)S(1)}, u32[]{:S(2)}, u32[]{:S(2)}) collective-permute-start(s32[2,128]{1,0:T(2,128)S(1)} %collective-permute-done), channel_id=1, source_target_pairs={{0,4},{4,0},{1,5},{5,1},{2,6},{6,2},{3,7},{7,3},{8,12},{12,8},{9,1... | collective-permute-start | bytes 3080 | tf_op jit(solution)/shard_map/ppermute | solution.py:38
  12.4 6.2 %collective-permute-done.3.refs_2_ = bf16[128,2048]{1,0:T(8,128)(2,1)S(1)} collective-permute-done((bf16[128,2048]{1,0:T(8,128)(2,1)}, bf16[128,2048]{1,0:T(8,128)(2,1)S(1)}, u32[]{:S(2)}, u32[]{:S(2)}) %collective-permute-start.3) | collective-permute-done | bytes 524320 | tf_op jit(solution)/shard_map/ppermute | solution.py:38
  19.5 1.7 collective-permute-start.10
  22.6 1.2 copy-done.3
  24.5 1.6 normed.1
  26.1 0.8 copy-done.9
  26.9 0.8 copy.36
  28.6 0.9 compare_reduce_fusion.1
  29.6 7.0 %collective-permute-done.10.refs_2_ = bf16[64,2048]{1,0:T(8,128)(2,1)S(1)} collective-permute-done((bf16[64,2048]{1,0:T(8,128)(2,1)}, bf16[64,2048]{1,0:T(8,128)(2,1)S(1)}, u32[]{:S(2)}, u32[]{:S(2)}) %collective-permute-start.10) | collective-permute-done | bytes 262176 | tf_op jit(solution)/shard_map/ppermute | solution.py:38
  36.5 1.6 collective-permute-start.12
  38.6 1.5 collective-permute-start.9
  40.1 1.3 dispatch.2
  42.1 3.2 %fusion.66 = f32[192,1024]{1,0:T(8,128)S(1)} fusion(bf16[192,2048]{1,0:T(8,128)(2,1)S(1)} %get-tuple-element.42, bf16[1,2048,1024]{2,1,0:T(8,128)(2,1)} %param.19), kind=kOutput, calls=%fused_computation.109 | convolution fusion | flops 805306368 | bytes 5767168 | tf_op jit(solution)/shard_map/dot_general | solution.py:615
  45.3 1.1 convolution_convert_fusion
  46.5 2.6 %collective-permute-done.9.refs_1_ = bf16[64,2048]{1,0:T(8,128)(2,1)S(1)} collective-permute-done((bf16[64,2048]{1,0:T(8,128)(2,1)}, bf16[64,2048]{1,0:T(8,128)(2,1)S(1)}, u32[]{:S(2)}, u32[]{:S(2)}) %collective-permute-start.9) | collective-permute-done | bytes 262176 | tf_op jit(solution)/shard_map/ppermute | solution.py:38
  50.2 2.5 %collective-permute-start.16 = (bf16[48,2048]{1,0:T(8,128)(2,1)S(1)}, bf16[48,2048]{1,0:T(8,128)(2,1)S(1)}, u32[]{:S(2)}, u32[]{:S(2)}) collective-permute-start(bf16[48,2048]{1,0:T(8,128)(2,1)S(1)} %get-tuple-element.84), channel_id=1, source_target_pairs={{0,6},{1,7},{2,4},{3,5},{4,2},{5,3},{6,0},{7,1},{8,14},{9,15},{10,... | collective-permute-start | bytes 589832 | tf_op jit(solution)/shard_map/ppermute | solution.py:223
  52.8 1.0 fusion.64
  53.8 1.1 convolution_convert_fusion.1
  55.4 5.3 %collective-permute-done.8.refs_4_ = bf16[512,512]{1,0:T(8,128)(2,1)S(1)} collective-permute-done((bf16[512,512]{1,0:T(8,128)(2,1)}, bf16[512,512]{1,0:T(8,128)(2,1)S(1)}, u32[]{:S(2)}, u32[]{:S(2)}) %collective-permute-start.8) | collective-permute-done | bytes 524320 | tf_op jit(solution)/shard_map/ppermute | solution.py:38
  60.7 1.0 fusion.77
  61.7 2.1 %fusion.9 = (f32[192,1024]{1,0:T(8,128)}, f32[192,1024]{1,0:T(8,128)}) fusion(f32[192,1024]{1,0:T(8,128)S(1)} %fusion.66, f32[192,1024]{1,0:T(8,128)S(1)} %fusion.64), kind=kLoop, calls=%fused_computation.20 | loop fusion | flops 6684672 | bytes 3145728 | tf_op jit(solution)/shard_map/transpose(jvp())/add_any | solution.py:621
  63.8 1.8 collective-permute-done.13.refs_5_
  65.6 2.4 %dispatch.3 = (bf16[192,2048]{1,0:T(8,128)(2,1)S(1)}, bf16[192,2048]{1,0:T(8,128)(2,1)}) custom-call(s32[1]{0:T(128)} %bitcast.5.section_ref, s32[8,128]{1,0:T(8,128)S(1)} %fusion.code_ref, bf16[128,2048]{1,0:T(8,128)(2,1)S(1)} %copy-done.4, bf16[64,2048]{1,0:T(8,128)(2,1)S(1)} %collective-permute-done.9.refs_1_, ...), custom_call_target="tpu_custom_call" | custom-call | flops 1 | bytes 1 | tf_op jit(solution)/shard_map/dispatch/pallas_call | solution.py:198
  68.0 0.9 copy-done.6
  68.8 1.8 collective-permute-start.19
  70.6 1.0 collective-permute-start.20
  73.0 6.7 %collective-permute-done.19.refs_6_ = bf16[48,2048]{1,0:T(8,128)(2,1)S(1)} collective-permute-done((bf16[48,2048]{1,0:T(8,128)(2,1)}, bf16[48,2048]{1,0:T(8,128)(2,1)S(1)}, u32[]{:S(2)}, u32[]{:S(2)}) %collective-permute-start.19) | collective-permute-done | bytes 196640 | tf_op jit(solution)/shard_map/ppermute | solution.py:223
  81.1 0.9 copy-done.12
  82.0 0.9 copy-done.14
  82.9 0.9 copy-done.16
  83.9 0.8 combine.2
  85.1 8.5 %collective-permute-done.21 = bf16[2,128,512]{2,1,0:T(8,128)(2,1)S(1)} collective-permute-done((bf16[2,128,512]{2,1,0:T(8,128)(2,1)S(1)}, bf16[2,128,512]{2,1,0:T(8,128)(2,1)S(1)}, u32[]{:S(2)}, u32[]{:S(2)}) %collective-permute-start.21) | collective-permute-done | bytes 262176 | tf_op jit(solution)/shard_map/ppermute | solution.py:38
  93.6 2.6 %collective-permute-start.23 = (bf16[128,512]{1,0:T(8,128)(2,1)S(1)}, bf16[128,512]{1,0:T(8,128)(2,1)S(1)}, u32[]{:S(2)}, u32[]{:S(2)}) collective-permute-start(bf16[128,512]{1,0:T(8,128)(2,1)S(1)} %fusion.55), channel_id=1, source_target_pairs={{0,16},{8,24},{16,0},{24,8},{1,17},{9,25},{17,1},{25,9},{2,18},{10... | collective-permute-start | bytes 393224 | tf_op jit(solution)/shard_map/ppermute | solution.py:38
  96.2 1.5 collective-permute-start.32
  97.7 7.3 %expert_slope.1.slope_ref = bf16[384,1024]{1,0:T(8,128)(2,1)} custom-call(s32[1]{0:T(128)} %bitcast.17.here_ref, bf16[192,2048]{1,0:T(8,128)(2,1)} %copy-done.6, bf16[192,2048]{1,0:T(8,128)(2,1)} %collective-permute-done.22.core_ref, f32[192,1024]{1,0:T(8,128)} %get-tuple-element.96.rise_own, f32[192,1024]{1,0:T(8,128)} %get-tuple-element.97.rise_core, ...), custom_call_target="tpu_custom_call" | custom-call | flops 1 | bytes 1 | tf_op jit(solution)/shard_map/expert_slope/pallas_call | solution.py:478
  106.2 5.7 %expert_backward.1 = (bf16[2,384,512]{2,1,0:T(8,128)(2,1)}, f32[384,512]{1,0:T(8,128)}, f32[384,512]{1,0:T(8,128)}) custom-call(s32[1]{0:T(128)} %bitcast.5.section_ref, bf16[384,1024]{1,0:T(8,128)(2,1)} %expert_slope.1.slope_ref, bf16[2048,1024]{1,0:T(8,128)(2,1)} %bitcast.105), custom_call_target="tpu_custom_call" | custom-call | flops 1 | bytes 1 | tf_op jit(solution)/shard_map/expert_backward/pallas_call | solution.py:520
  112.0 1.6 collective-permute-start.24
  114.1 1.3 fusion.2
  115.3 19.8 %collective-permute-done.30 = bf16[2,128,512]{2,1,0:T(8,128)(2,1)S(1)} collective-permute-done((bf16[2,128,512]{2,1,0:T(8,128)(2,1)S(1)}, bf16[2,128,512]{2,1,0:T(8,128)(2,1)S(1)}, u32[]{:S(2)}, u32[]{:S(2)}) %collective-permute-start.30) | collective-permute-done | bytes 262176 | tf_op jit(solution)/shard_map/ppermute | solution.py:38
  135.6 1.5 collective-permute-start.33
  137.1 1.1 convolution_convert_fusion.2
  138.8 1.6 collective-permute-start.35
  140.5 0.9 fusion.79
  141.4 3.4 %collective-permute-start.25 = (bf16[192,512]{1,0:T(8,128)(2,1)}, bf16[192,512]{1,0:T(8,128)(2,1)}, u32[]{:S(2)}, u32[]{:S(2)}) collective-permute-start(bf16[192,512]{1,0:T(8,128)(2,1)} %get-tuple-element.88), channel_id=1, source_target_pairs={{0,16},{8,24},{16,0},{24,8},{1,17},{9,25},{17,1},{25,9},{2,18},{10... | collective-permute-start | bytes 589832 | tf_op jit(solution)/shard_map/ppermute | solution.py:38
  144.8 2.6 %collective-permute-done.33.refs_0_ = bf16[128,2048]{1,0:T(8,128)(2,1)} collective-permute-done((bf16[128,2048]{1,0:T(8,128)(2,1)S(1)}, bf16[128,2048]{1,0:T(8,128)(2,1)}, u32[]{:S(2)}, u32[]{:S(2)}) %collective-permute-start.33) | collective-permute-done | bytes 524320 | tf_op jit(solution)/shard_map/ppermute | solution.py:38
  148.6 5.9 %collective-permute-done.25 = bf16[192,512]{1,0:T(8,128)(2,1)} collective-permute-done((bf16[192,512]{1,0:T(8,128)(2,1)}, bf16[192,512]{1,0:T(8,128)(2,1)}, u32[]{:S(2)}, u32[]{:S(2)}) %collective-permute-start.25) | collective-permute-done | bytes 196640 | tf_op jit(solution)/shard_map/ppermute | solution.py:38
  154.5 1.0 add_convert_fusion
  156.3 5.4 %attend_sentence.2.mine_ref = bf16[128,512]{1,0:T(8,128)(2,1)} custom-call(s32[3]{0:T(128)} %pad_add_fusion.1.place_ref, s32[2]{0:T(128)} %lengths_ref.3, bf16[128,512]{1,0:T(8,128)(2,1)} %get-tuple-element.91.query_ref, bf16[128,2048]{1,0:T(8,128)(2,1)} %copy-done.2, bf16[128,2048]{1,0:T(8,128)(2,1)} %collective-permute-done.31.refs_1_, ...), custom_call_target="tpu_custom_call" | custom-call | flops 1 | bytes 1 | tf_op jit(solution)/shard_map/attend_sentence/pallas_call | solution.py:381
  161.7 2.0 %collective-permute-done.26 = bf16[192,512]{1,0:T(8,128)(2,1)S(1)} collective-permute-done((bf16[192,512]{1,0:T(8,128)(2,1)S(1)}, bf16[192,512]{1,0:T(8,128)(2,1)S(1)}, u32[]{:S(2)}, u32[]{:S(2)}) %collective-permute-start.26) | collective-permute-done | bytes 196640 | tf_op jit(solution)/shard_map/ppermute | solution.py:38
  163.7 5.5 %attend_sentence.3.done_ref = bf16[128,512]{1,0:T(8,128)(2,1)} custom-call(s32[3]{0:T(128)} %pad_add_fusion.3.place_ref, s32[2]{0:T(128)} %lengths_ref.3, bf16[128,512]{1,0:T(8,128)(2,1)} %get-tuple-element.90.query_ref, bf16[128,2048]{1,0:T(8,128)(2,1)} %collective-permute-done.33.refs_0_, bf16[128,2048]{1,0:T(8,128)(2,1)} %collective-permute-done.34.refs_1_, ...), custom_call_target="tpu_custom_call" | custom-call | flops 1 | bytes 1 | tf_op jit(solution)/shard_map/attend_sentence/pallas_call | solution.py:381
  169.3 0.9 copy-done.8
  170.2 2.0 %project.1 = (bf16[2,256,512]{2,1,0:T(8,128)(2,1)S(1)}, f32[256,512]{1,0:T(8,128)S(1)}, f32[256,512]{1,0:T(8,128)S(1)}) custom-call(s32[3]{0:T(128)S(1)} %copy-done.19, bf16[128,512]{1,0:T(8,128)(2,1)S(1)} %copy-done.7, bf16[128,512]{1,0:T(8,128)(2,1)S(1)} %copy-done.8, bf16[512,1024]{1,0:T(8,128)(2,1)S(1)} %bitcast.102, ...), custom_call_target="tpu_custom_call" | custom-call | flops 1 | bytes 1 | tf_op jit(solution)/shard_map/project/pallas_call | solution.py:431
  172.2 1.9 collective-permute-done.36
  175.0 1.0 collective-permute-start.37
  176.0 1.8 fusion.33
  177.8 3.5 %all-to-all-start = ((bf16[8,48,512]{2,1,0:T(8,128)(2,1)}), bf16[8,48,512]{2,1,0:T(8,128)(2,1)S(1)}, u32[]{:S(2)}, u32[]{:S(2)}) async-start(bf16[8,48,512]{2,1,0:T(8,128)(2,1)} %bitcast.35), calls=%async_computation | async-start | bytes 786432 | tf_op jit(solution)/shard_map/all_to_all | solution.py:142
  181.5 2.1 %collective-permute-done.37 = bf16[256,512]{1,0:T(8,128)(2,1)S(1)} collective-permute-done((bf16[256,512]{1,0:T(8,128)(2,1)}, bf16[256,512]{1,0:T(8,128)(2,1)S(1)}, u32[]{:S(2)}, u32[]{:S(2)}) %collective-permute-start.37) | collective-permute-done | bytes 262176 | tf_op jit(solution)/shard_map/ppermute | solution.py:38
  183.6 1.8 fusion.52
  185.4 4.2 %all-to-all-done = bf16[8,48,512]{2,1,0:T(8,128)(2,1)S(1)} async-done(((bf16[8,48,512]{2,1,0:T(8,128)(2,1)}), bf16[8,48,512]{2,1,0:T(8,128)(2,1)S(1)}, u32[]{:S(2)}, u32[]{:S(2)}) %all-to-all-start) | async-done | bytes 393248 | tf_op jit(solution)/shard_map/all_to_all | solution.py:142
  189.6 1.0 combine.3
  (129 shorter events, 17.3 us)
Async XLA Ops:
  0.6 113.4 %copy-start = (bf16[1,1024,512]{2,1,0:T(8,128)(2,1)S(1)}, bf16[1,1024,512]{2,1,0:T(8,128)(2,1)}, u32[]{:S(2)}) copy-start(bf16[1,1024,512]{2,1,0:T(8,128)(2,1)} %param.26) | copy-start | bytes 3145732
  0.6 39.5 %copy-start.1 = (bf16[128,2048]{1,0:T(8,128)(2,1)S(1)}, bf16[128,2048]{1,0:T(8,128)(2,1)}, u32[]{:S(2)}) copy-start(bf16[128,2048]{1,0:T(8,128)(2,1)} %tokens_ref.1) | copy-start | bytes 1572868
  0.7 9.7 %collective-permute-start = (s32[2,128]{1,0:T(2,128)}, s32[2,128]{1,0:T(2,128)S(1)}, u32[]{:S(2)}, u32[]{:S(2)}) collective-permute-start(s32[2,128]{1,0:T(2,128)} %bitcast.112), channel_id=1, source_target_pairs={{0,2},{1,3},{2,0},{3,1},{4,6},{5,7},{6,4},{7,5},{8,10},{9,11},{10,... | collective-permute-start | bytes 3080 | tf_op jit(solution)/shard_map/ppermute | solution.py:38
  3.7 24.9 %collective-permute-start.1 = (s32[2,128]{1,0:T(2,128)}, s32[2,128]{1,0:T(2,128)S(1)}, u32[]{:S(2)}, u32[]{:S(2)}) collective-permute-start(s32[2,128]{1,0:T(2,128)} %bitcast.113), channel_id=1, source_target_pairs={{0,4},{4,0},{1,5},{5,1},{2,6},{6,2},{3,7},{7,3},{8,12},{12,8},{9,1... | collective-permute-start | bytes 3080 | tf_op jit(solution)/shard_map/ppermute | solution.py:38
  5.2 13.3 %collective-permute-start.3 = (bf16[128,2048]{1,0:T(8,128)(2,1)}, bf16[128,2048]{1,0:T(8,128)(2,1)S(1)}, u32[]{:S(2)}, u32[]{:S(2)}) collective-permute-start(bf16[128,2048]{1,0:T(8,128)(2,1)} %tokens_ref.1), channel_id=1, source_target_pairs={{0,4},{4,0},{1,5},{5,1},{2,6},{6,2},{3,7},{7,3},{8,12},{12,8},{9,1... | collective-permute-start | bytes 1572872 | tf_op jit(solution)/shard_map/ppermute | solution.py:38
  5.7 34.4 %collective-permute-start.5 = (bf16[128,2048]{1,0:T(8,128)(2,1)}, bf16[128,2048]{1,0:T(8,128)(2,1)S(1)}, u32[]{:S(2)}, u32[]{:S(2)}) collective-permute-start(bf16[128,2048]{1,0:T(8,128)(2,1)} %tokens_ref.1), channel_id=1, source_target_pairs={{0,2},{1,3},{2,0},{3,1},{4,6},{5,7},{6,4},{7,5},{8,10},{9,11},{10,... | collective-permute-start | bytes 1572872 | tf_op jit(solution)/shard_map/ppermute | solution.py:38
  10.4 9.1 %collective-permute-start.2 = (s32[2,128]{1,0:T(2,128)S(1)}, s32[2,128]{1,0:T(2,128)S(1)}, u32[]{:S(2)}, u32[]{:S(2)}) collective-permute-start(s32[2,128]{1,0:T(2,128)S(1)} %collective-permute-done), channel_id=1, source_target_pairs={{0,4},{4,0},{1,5},{5,1},{2,6},{6,2},{3,7},{7,3},{8,12},{12,8},{9,1... | collective-permute-start | bytes 3080 | tf_op jit(solution)/shard_map/ppermute | solution.py:38
  18.5 21.6 %collective-permute-start.4 = (bf16[512,512]{1,0:T(8,128)(2,1)}, bf16[512,512]{1,0:T(8,128)(2,1)}, u32[]{:S(2)}, u32[]{:S(2)}) collective-permute-start(bf16[512,512]{1,0:T(8,128)(2,1)} %get-tuple-element.39), channel_id=1, source_target_pairs={{0,4},{4,0},{1,5},{5,1},{2,6},{6,2},{3,7},{7,3},{8,12},{12,8},{9,1... | collective-permute-start | bytes 1572872 | tf_op jit(solution)/shard_map/ppermute | solution.py:38
  19.0 19.1 %collective-permute-start.6 = (bf16[128,2048]{1,0:T(8,128)(2,1)S(1)}, bf16[128,2048]{1,0:T(8,128)(2,1)S(1)}, u32[]{:S(2)}, u32[]{:S(2)}) collective-permute-start(bf16[128,2048]{1,0:T(8,128)(2,1)S(1)} %collective-permute-done.3.refs_2_), channel_id=1, source_target_pairs={{0,2},{1,3},{2,0},{3,1},{4,6},{5,7},{6,4},{7,5},{8,10},{9,11},{10,... | collective-permute-start | bytes 1572872 | tf_op jit(solution)/shard_map/ppermute | solution.py:38
  19.5 6.6 %copy-start.30 = (s32[2,128]{1,0:T(2,128)}, s32[2,128]{1,0:T(2,128)S(1)}, u32[]{:S(2)}) copy-start(s32[2,128]{1,0:T(2,128)S(1)} %collective-permute-done.2) | copy-start | bytes 3076
  19.5 17.0 %collective-permute-start.10 = (bf16[64,2048]{1,0:T(8,128)(2,1)}, bf16[64,2048]{1,0:T(8,128)(2,1)S(1)}, u32[]{:S(2)}, u32[]{:S(2)}) collective-permute-start(bf16[64,2048]{1,0:T(8,128)(2,1)} %constant_dynamic-slice_fusion.2), channel_id=1, source_target_pairs={{0,4},{4,0},{1,5},{5,1},{2,6},{6,2},{3,7},{7,3},{8,12},{12,8},{9,1... | collective-permute-start | bytes 786440 | tf_op jit(solution)/shard_map/ppermute | solution.py:38
  22.6 1.2 copy-start.3
  28.6 16.7 %copy-start.21 = (bf16[1,1024,2048]{2,1,0:T(8,128)(2,1)S(1)}, bf16[1,1024,2048]{2,1,0:T(8,128)(2,1)}, u32[]{:S(2)}) copy-start(bf16[1,1024,2048]{2,1,0:T(8,128)(2,1)} %param.20) | copy-start | bytes 12582916
  36.5 18.4 %collective-permute-start.12 = (bf16[64,2048]{1,0:T(8,128)(2,1)S(1)}, bf16[64,2048]{1,0:T(8,128)(2,1)S(1)}, u32[]{:S(2)}, u32[]{:S(2)}) collective-permute-start(bf16[64,2048]{1,0:T(8,128)(2,1)S(1)} %collective-permute-done.10.refs_2_), channel_id=1, source_target_pairs={{0,8},{8,0},{16,24},{24,16},{1,9},{9,1},{17,25},{25,17},{2,10},{10... | collective-permute-start | bytes 786440 | tf_op jit(solution)/shard_map/ppermute | solution.py:38
  38.1 11.5 %collective-permute-start.11 = (bf16[64,2048]{1,0:T(8,128)(2,1)S(1)}, bf16[64,2048]{1,0:T(8,128)(2,1)S(1)}, u32[]{:S(2)}, u32[]{:S(2)}) collective-permute-start(bf16[64,2048]{1,0:T(8,128)(2,1)S(1)} %collective-permute-done.10.refs_2_), channel_id=1, source_target_pairs={{0,2},{1,3},{2,0},{3,1},{4,6},{5,7},{6,4},{7,5},{8,10},{9,11},{10,... | collective-permute-start | bytes 786440 | tf_op jit(solution)/shard_map/ppermute | solution.py:38
  38.6 10.4 %collective-permute-start.9 = (bf16[64,2048]{1,0:T(8,128)(2,1)}, bf16[64,2048]{1,0:T(8,128)(2,1)S(1)}, u32[]{:S(2)}, u32[]{:S(2)}) collective-permute-start(bf16[64,2048]{1,0:T(8,128)(2,1)} %constant_dynamic-slice_fusion.2), channel_id=1, source_target_pairs={{0,2},{1,3},{2,0},{3,1},{4,6},{5,7},{6,4},{7,5},{8,10},{9,11},{10,... | collective-permute-start | bytes 786440 | tf_op jit(solution)/shard_map/ppermute | solution.py:38
  41.4 8.8 %collective-permute-start.7 = (bf16[192,2048]{1,0:T(8,128)(2,1)S(1)}, bf16[192,2048]{1,0:T(8,128)(2,1)S(1)}, u32[]{:S(2)}, u32[]{:S(2)}) collective-permute-start(bf16[192,2048]{1,0:T(8,128)(2,1)S(1)} %get-tuple-element.43), channel_id=1, source_target_pairs={{0,1},{1,0},{2,3},{3,2},{4,5},{5,4},{6,7},{7,6},{8,9},{9,8},{10,11... | collective-permute-start | bytes 2359304 | tf_op jit(solution)/shard_map/ppermute | solution.py:38
  41.5 19.2 %collective-permute-start.8 = (bf16[512,512]{1,0:T(8,128)(2,1)}, bf16[512,512]{1,0:T(8,128)(2,1)S(1)}, u32[]{:S(2)}, u32[]{:S(2)}) collective-permute-start(bf16[512,512]{1,0:T(8,128)(2,1)} %get-tuple-element.44), channel_id=1, source_target_pairs={{0,4},{4,0},{1,5},{5,1},{2,6},{6,2},{3,7},{7,3},{8,12},{12,8},{9,1... | collective-permute-start | bytes 1572872 | tf_op jit(solution)/shard_map/ppermute | solution.py:38
  45.3 7.5 %copy-start.20 = (bf16[1,2048,1024]{2,1,0:T(8,128)(2,1)S(1)}, bf16[1,2048,1024]{2,1,0:T(8,128)(2,1)}, u32[]{:S(2)}) copy-start(bf16[1,2048,1024]{2,1,0:T(8,128)(2,1)} %param.19) | copy-start | bytes 12582916
  49.1 19.8 %collective-permute-start.14 = (bf16[48,2048]{1,0:T(8,128)(2,1)S(1)}, bf16[48,2048]{1,0:T(8,128)(2,1)S(1)}, u32[]{:S(2)}, u32[]{:S(2)}) collective-permute-start(bf16[48,2048]{1,0:T(8,128)(2,1)S(1)} %get-tuple-element.86), channel_id=1, source_target_pairs={{0,2},{1,3},{2,0},{3,1},{4,6},{5,7},{6,4},{7,5},{8,10},{9,11},{10,... | collective-permute-start | bytes 589832 | tf_op jit(solution)/shard_map/ppermute | solution.py:223
  49.6 21.0 %collective-permute-start.15 = (bf16[48,2048]{1,0:T(8,128)(2,1)S(1)}, bf16[48,2048]{1,0:T(8,128)(2,1)S(1)}, u32[]{:S(2)}, u32[]{:S(2)}) collective-permute-start(bf16[48,2048]{1,0:T(8,128)(2,1)S(1)} %get-tuple-element.85), channel_id=1, source_target_pairs={{0,4},{1,5},{2,6},{3,7},{4,0},{5,1},{6,2},{7,3},{8,12},{9,13},{10,... | collective-permute-start | bytes 589832 | tf_op jit(solution)/shard_map/ppermute | solution.py:223
  50.2 21.4 %collective-permute-start.16 = (bf16[48,2048]{1,0:T(8,128)(2,1)S(1)}, bf16[48,2048]{1,0:T(8,128)(2,1)S(1)}, u32[]{:S(2)}, u32[]{:S(2)}) collective-permute-start(bf16[48,2048]{1,0:T(8,128)(2,1)S(1)} %get-tuple-element.84), channel_id=1, source_target_pairs={{0,6},{1,7},{2,4},{3,5},{4,2},{5,3},{6,0},{7,1},{8,14},{9,15},{10,... | collective-permute-start | bytes 589832 | tf_op jit(solution)/shard_map/ppermute | solution.py:223
  53.8 11.8 %copy-start.4 = (bf16[128,2048]{1,0:T(8,128)(2,1)S(1)}, bf16[128,2048]{1,0:T(8,128)(2,1)}, u32[]{:S(2)}) copy-start(bf16[128,2048]{1,0:T(8,128)(2,1)} %refs_0_.3) | copy-start | bytes 1572868
  54.9 17.3 %copy-start.28 = (s32[128,2]{1,0:T(8,128)S(1)}, s32[128,2]{1,0:T(8,128)}, u32[]{:S(2)}) copy-start(s32[128,2]{1,0:T(8,128)} %copy.41) | copy-start | bytes 3076
  54.9 17.3 %copy-start.29 = (f32[128,2]{0,1:T(2,128)S(1)}, f32[128,2]{0,1:T(2,128)}, u32[]{:S(2)}) copy-start(f32[128,2]{0,1:T(2,128)} %param.17) | copy-start | bytes 3076
  54.9 10.7 %collective-permute-start.13 = (bf16[128,2048]{1,0:T(8,128)(2,1)S(1)}, bf16[128,2048]{1,0:T(8,128)(2,1)S(1)}, u32[]{:S(2)}, u32[]{:S(2)}) collective-permute-start(bf16[128,2048]{1,0:T(8,128)(2,1)S(1)} %constant_dynamic-update-slice_fusion), channel_id=1, source_target_pairs={{0,8},{8,0},{16,24},{24,16},{1,9},{9,1},{17,25},{25,17},{2,10},{10... | collective-permute-start | bytes 1572872 | tf_op jit(solution)/shard_map/ppermute | solution.py:38
  60.7 11.5 %copy-start.22 = (bf16[512,512]{1,0:T(8,128)(2,1)}, bf16[512,512]{1,0:T(8,128)(2,1)S(1)}, u32[]{:S(2)}) copy-start(bf16[512,512]{1,0:T(8,128)(2,1)S(1)} %collective-permute-done.8.refs_4_) | copy-start | bytes 1572868
  63.8 8.6 %collective-permute-start.17 = (bf16[48,2048]{1,0:T(8,128)(2,1)}, bf16[48,2048]{1,0:T(8,128)(2,1)S(1)}, u32[]{:S(2)}, u32[]{:S(2)}) collective-permute-start(bf16[48,2048]{1,0:T(8,128)(2,1)} %get-tuple-element.83), channel_id=1, source_target_pairs={{0,1},{1,0},{2,3},{3,2},{4,5},{5,4},{6,7},{7,6},{8,9},{9,8},{10,11... | collective-permute-start | bytes 589832 | tf_op jit(solution)/shard_map/ppermute | solution.py:223
  65.6 6.8 %collective-permute-start.18 = (bf16[48,2048]{1,0:T(8,128)(2,1)}, bf16[48,2048]{1,0:T(8,128)(2,1)S(1)}, u32[]{:S(2)}, u32[]{:S(2)}) collective-permute-start(bf16[48,2048]{1,0:T(8,128)(2,1)} %get-tuple-element.82), channel_id=1, source_target_pairs={{0,3},{1,2},{2,1},{3,0},{4,7},{5,6},{6,5},{7,4},{8,11},{9,10},{10,... | collective-permute-start | bytes 589832 | tf_op jit(solution)/shard_map/ppermute | solution.py:223
  68.8 10.9 %collective-permute-start.19 = (bf16[48,2048]{1,0:T(8,128)(2,1)}, bf16[48,2048]{1,0:T(8,128)(2,1)S(1)}, u32[]{:S(2)}, u32[]{:S(2)}) collective-permute-start(bf16[48,2048]{1,0:T(8,128)(2,1)} %get-tuple-element.81), channel_id=1, source_target_pairs={{0,5},{1,4},{2,7},{3,6},{4,1},{5,0},{6,3},{7,2},{8,13},{9,12},{10,... | collective-permute-start | bytes 589832 | tf_op jit(solution)/shard_map/ppermute | solution.py:223
  70.6 9.8 %collective-permute-start.20 = (bf16[48,2048]{1,0:T(8,128)(2,1)}, bf16[48,2048]{1,0:T(8,128)(2,1)S(1)}, u32[]{:S(2)}, u32[]{:S(2)}) collective-permute-start(bf16[48,2048]{1,0:T(8,128)(2,1)} %get-tuple-element.80), channel_id=1, source_target_pairs={{0,7},{1,6},{2,5},{3,4},{4,3},{5,2},{6,1},{7,0},{8,15},{9,14},{10,... | collective-permute-start | bytes 589832 | tf_op jit(solution)/shard_map/ppermute | solution.py:223
  71.6 26.1 %collective-permute-start.22 = (bf16[192,2048]{1,0:T(8,128)(2,1)}, bf16[192,2048]{1,0:T(8,128)(2,1)}, u32[]{:S(2)}, u32[]{:S(2)}) collective-permute-start(bf16[192,2048]{1,0:T(8,128)(2,1)} %get-tuple-element.52), channel_id=1, source_target_pairs={{0,1},{1,0},{2,3},{3,2},{4,5},{5,4},{6,7},{7,6},{8,9},{9,8},{10,11... | collective-permute-start | bytes 2359304 | tf_op jit(solution)/shard_map/ppermute | solution.py:38
  81.1 0.9 copy-start.12
  82.0 0.9 copy-start.14
  82.9 0.9 copy-start.16
  84.7 8.9 %collective-permute-start.21 = (bf16[2,128,512]{2,1,0:T(8,128)(2,1)S(1)}, bf16[2,128,512]{2,1,0:T(8,128)(2,1)S(1)}, u32[]{:S(2)}, u32[]{:S(2)}) collective-permute-start(bf16[2,128,512]{2,1,0:T(8,128)(2,1)S(1)} %get-tuple-element.56), channel_id=1, source_target_pairs={{0,8},{8,0},{16,24},{24,16},{1,9},{9,1},{17,25},{25,17},{2,10},{10... | collective-permute-start | bytes 786440 | tf_op jit(solution)/shard_map/ppermute | solution.py:38
  93.6 11.5 %collective-permute-start.23 = (bf16[128,512]{1,0:T(8,128)(2,1)S(1)}, bf16[128,512]{1,0:T(8,128)(2,1)S(1)}, u32[]{:S(2)}, u32[]{:S(2)}) collective-permute-start(bf16[128,512]{1,0:T(8,128)(2,1)S(1)} %fusion.55), channel_id=1, source_target_pairs={{0,16},{8,24},{16,0},{24,8},{1,17},{9,25},{17,1},{25,9},{2,18},{10... | collective-permute-start | bytes 393224 | tf_op jit(solution)/shard_map/ppermute | solution.py:38
  96.2 42.6 %collective-permute-start.32 = (bf16[1024,512]{1,0:T(8,128)(2,1)}, bf16[1024,512]{1,0:T(8,128)(2,1)}, u32[]{:S(2)}, u32[]{:S(2)}) collective-permute-start(bf16[1024,512]{1,0:T(8,128)(2,1)} %bitcast.109), channel_id=1, source_target_pairs={{0,4},{4,0},{1,5},{5,1},{2,6},{6,2},{3,7},{7,3},{8,12},{12,8},{9,1... | collective-permute-start | bytes 3145736 | tf_op jit(solution)/shard_map/ppermute | solution.py:38
  105.1 9.0 %copy-start.10 = (bf16[256,1024]{1,0:T(8,128)(2,1)S(1)}, bf16[256,1024]{1,0:T(8,128)(2,1)}, u32[]{:S(2)}) copy-start(bf16[256,1024]{1,0:T(8,128)(2,1)} %copy-done.9) | copy-start | bytes 1572868
  105.2 30.0 %copy-start.18 = (f32[2048]{0:T(1024)S(1)}, f32[2048]{0:T(1024)}, u32[]{:S(2)}) copy-start(f32[2048]{0:T(1024)} %param.21) | copy-start | bytes 24580
  105.2 8.4 %collective-permute-start.29 = (bf16[128,512]{1,0:T(8,128)(2,1)S(1)}, bf16[128,512]{1,0:T(8,128)(2,1)S(1)}, u32[]{:S(2)}, u32[]{:S(2)}) collective-permute-start(bf16[128,512]{1,0:T(8,128)(2,1)S(1)} %fusion.54.refs_0_), channel_id=1, source_target_pairs={{0,8},{8,0},{16,24},{24,16},{1,9},{9,1},{17,25},{25,17},{2,10},{10... | collective-permute-start | bytes 393224 | tf_op jit(solution)/shard_map/ppermute | solution.py:38
  105.7 31.5 %collective-permute-start.27 = (bf16[256,1024]{1,0:T(8,128)(2,1)}, bf16[256,1024]{1,0:T(8,128)(2,1)S(1)}, u32[]{:S(2)}, u32[]{:S(2)}) collective-permute-start(bf16[256,1024]{1,0:T(8,128)(2,1)} %get-tuple-element.67), channel_id=1, source_target_pairs={{0,4},{4,0},{1,5},{5,1},{2,6},{6,2},{3,7},{7,3},{8,12},{12,8},{9,1... | collective-permute-start | bytes 1572872 | tf_op jit(solution)/shard_map/ppermute | solution.py:38
  111.9 26.9 %copy-start.5 = (bf16[1,512,1024]{2,1,0:T(8,128)(2,1)S(1)}, bf16[1,512,1024]{2,1,0:T(8,128)(2,1)}, u32[]{:S(2)}) copy-start(bf16[1,512,1024]{2,1,0:T(8,128)(2,1)} %param.29) | copy-start | bytes 3145732
  112.0 28.4 %copy-start.24 = (f32[384,512]{1,0:T(8,128)S(1)}, f32[384,512]{1,0:T(8,128)}, u32[]{:S(2)}) copy-start(f32[384,512]{1,0:T(8,128)} %get-tuple-element.61) | copy-start | bytes 2359300
  112.0 28.4 %collective-permute-start.24 = (bf16[2,384,512]{2,1,0:T(8,128)(2,1)}, bf16[2,384,512]{2,1,0:T(8,128)(2,1)S(1)}, u32[]{:S(2)}, u32[]{:S(2)}) collective-permute-start(bf16[2,384,512]{2,1,0:T(8,128)(2,1)} %get-tuple-element.62), channel_id=1, source_target_pairs={{0,8},{8,0},{16,24},{24,16},{1,9},{9,1},{17,25},{25,17},{2,10},{10... | collective-permute-start | bytes 2359304 | tf_op jit(solution)/shard_map/ppermute | solution.py:38
  113.6 21.5 %collective-permute-start.30 = (bf16[2,128,512]{2,1,0:T(8,128)(2,1)S(1)}, bf16[2,128,512]{2,1,0:T(8,128)(2,1)S(1)}, u32[]{:S(2)}, u32[]{:S(2)}) collective-permute-start(bf16[2,128,512]{2,1,0:T(8,128)(2,1)S(1)} %pad_maximum_fusion), channel_id=1, source_target_pairs={{0,16},{8,24},{16,0},{24,8},{1,17},{9,25},{17,1},{25,9},{2,18},{10... | collective-permute-start | bytes 786440 | tf_op jit(solution)/shard_map/ppermute | solution.py:38
  135.6 20.7 %copy-start.2 = (bf16[128,2048]{1,0:T(8,128)(2,1)}, bf16[128,2048]{1,0:T(8,128)(2,1)S(1)}, u32[]{:S(2)}) copy-start(bf16[128,2048]{1,0:T(8,128)(2,1)S(1)} %memory.1.refs_0_) | copy-start | bytes 1572868
  135.6 18.9 %copy-start.23 = (f32[256,512]{1,0:T(8,128)S(1)}, f32[256,512]{1,0:T(8,128)}, u32[]{:S(2)}) copy-start(f32[256,512]{1,0:T(8,128)} %fusion.2) | copy-start | bytes 1572868
  135.6 11.8 %collective-permute-start.33 = (bf16[128,2048]{1,0:T(8,128)(2,1)S(1)}, bf16[128,2048]{1,0:T(8,128)(2,1)}, u32[]{:S(2)}, u32[]{:S(2)}) collective-permute-start(bf16[128,2048]{1,0:T(8,128)(2,1)S(1)} %memory.1.refs_0_), channel_id=1, source_target_pairs={{0,2},{1,3},{2,0},{3,1},{4,6},{5,7},{6,4},{7,5},{8,10},{9,11},{10,... | collective-permute-start | bytes 1572872 | tf_op jit(solution)/shard_map/ppermute | solution.py:38
  138.3 16.2 %collective-permute-start.28 = (bf16[256,512]{1,0:T(8,128)(2,1)}, bf16[256,512]{1,0:T(8,128)(2,1)}, u32[]{:S(2)}, u32[]{:S(2)}) collective-permute-start(bf16[256,512]{1,0:T(8,128)(2,1)} %convolution_convert_fusion.2), channel_id=1, source_target_pairs={{0,4},{4,0},{1,5},{5,1},{2,6},{6,2},{3,7},{7,3},{8,12},{12,8},{9,1... | collective-permute-start | bytes 786440 | tf_op jit(solution)/shard_map/ppermute | solution.py:38
  138.8 17.4 %collective-permute-start.31 = (bf16[128,2048]{1,0:T(8,128)(2,1)S(1)}, bf16[128,2048]{1,0:T(8,128)(2,1)}, u32[]{:S(2)}, u32[]{:S(2)}) collective-permute-start(bf16[128,2048]{1,0:T(8,128)(2,1)S(1)} %memory.1.refs_0_), channel_id=1, source_target_pairs={{0,1},{1,0},{2,3},{3,2},{4,5},{5,4},{6,7},{7,6},{8,9},{9,8},{10,11... | collective-permute-start | bytes 1572872 | tf_op jit(solution)/shard_map/ppermute | solution.py:38
  138.8 30.4 %collective-permute-start.35 = (bf16[512,1024]{1,0:T(8,128)(2,1)S(1)}, bf16[512,1024]{1,0:T(8,128)(2,1)}, u32[]{:S(2)}, u32[]{:S(2)}) collective-permute-start(bf16[512,1024]{1,0:T(8,128)(2,1)S(1)} %bitcast.101), channel_id=1, source_target_pairs={{0,4},{4,0},{1,5},{5,1},{2,6},{6,2},{3,7},{7,3},{8,12},{12,8},{9,1... | collective-permute-start | bytes 3145736 | tf_op jit(solution)/shard_map/ppermute | solution.py:38
  140.4 7.0 %copy-start.26 = (bf16[2,384,512]{2,1,0:T(8,128)(2,1)}, bf16[2,384,512]{2,1,0:T(8,128)(2,1)S(1)}, u32[]{:S(2)}) copy-start(bf16[2,384,512]{2,1,0:T(8,128)(2,1)S(1)} %collective-permute-done.24) | copy-start | bytes 2359300
  141.4 13.1 %collective-permute-start.25 = (bf16[192,512]{1,0:T(8,128)(2,1)}, bf16[192,512]{1,0:T(8,128)(2,1)}, u32[]{:S(2)}, u32[]{:S(2)}) collective-permute-start(bf16[192,512]{1,0:T(8,128)(2,1)} %get-tuple-element.88), channel_id=1, source_target_pairs={{0,16},{8,24},{16,0},{24,8},{1,17},{9,25},{17,1},{25,9},{2,18},{10... | collective-permute-start | bytes 589832 | tf_op jit(solution)/shard_map/ppermute | solution.py:38
  147.4 16.3 %collective-permute-start.34 = (bf16[128,2048]{1,0:T(8,128)(2,1)}, bf16[128,2048]{1,0:T(8,128)(2,1)}, u32[]{:S(2)}, u32[]{:S(2)}) collective-permute-start(bf16[128,2048]{1,0:T(8,128)(2,1)} %collective-permute-done.33.refs_0_), channel_id=1, source_target_pairs={{0,1},{1,0},{2,3},{3,2},{4,5},{5,4},{6,7},{7,6},{8,9},{9,8},{10,11... | collective-permute-start | bytes 1572872 | tf_op jit(solution)/shard_map/ppermute | solution.py:38
  154.5 9.2 %collective-permute-start.26 = (bf16[192,512]{1,0:T(8,128)(2,1)S(1)}, bf16[192,512]{1,0:T(8,128)(2,1)S(1)}, u32[]{:S(2)}, u32[]{:S(2)}) collective-permute-start(bf16[192,512]{1,0:T(8,128)(2,1)S(1)} %get-tuple-element.63), channel_id=1, source_target_pairs={{0,16},{8,24},{16,0},{24,8},{1,17},{9,25},{17,1},{25,9},{2,18},{10... | collective-permute-start | bytes 589832 | tf_op jit(solution)/shard_map/ppermute | solution.py:38
  156.3 13.0 %copy-start.19 = (s32[3]{0:T(128)S(1)}, s32[3]{0:T(128)}, u32[]{:S(2)}) copy-start(s32[3]{0:T(128)} %pad_add_fusion.1.place_ref) | copy-start | bytes 40
  161.7 7.6 %copy-start.7 = (bf16[128,512]{1,0:T(8,128)(2,1)S(1)}, bf16[128,512]{1,0:T(8,128)(2,1)}, u32[]{:S(2)}) copy-start(bf16[128,512]{1,0:T(8,128)(2,1)} %attend_sentence.2.mine_ref) | copy-start | bytes 393220
  163.7 12.3 %copy-start.25 = (f32[384,512]{1,0:T(8,128)S(1)}, f32[384,512]{1,0:T(8,128)}, u32[]{:S(2)}) copy-start(f32[384,512]{1,0:T(8,128)} %get-tuple-element.68) | copy-start | bytes 2359300
  163.7 12.3 %copy-start.27 = (bf16[2,384,512]{2,1,0:T(8,128)(2,1)S(1)}, bf16[2,384,512]{2,1,0:T(8,128)(2,1)}, u32[]{:S(2)}) copy-start(bf16[2,384,512]{2,1,0:T(8,128)(2,1)} %copy-done.26) | copy-start | bytes 2359300
  170.2 11.1 %copy-start.31 = (s32[2]{0:T(128)S(1)}, s32[2]{0:T(128)}, u32[]{:S(2)}) copy-start(s32[2]{0:T(128)} %param.24) | copy-start | bytes 28
  172.1 2.0 %collective-permute-start.36 = (bf16[2,256,512]{2,1,0:T(8,128)(2,1)S(1)}, bf16[2,256,512]{2,1,0:T(8,128)(2,1)S(1)}, u32[]{:S(2)}, u32[]{:S(2)}) collective-permute-start(bf16[2,256,512]{2,1,0:T(8,128)(2,1)S(1)} %get-tuple-element.73), channel_id=1, source_target_pairs={{0,1},{1,0},{2,3},{3,2},{4,5},{5,4},{6,7},{7,6},{8,9},{9,8},{10,11... | collective-permute-start | bytes 1572872 | tf_op jit(solution)/shard_map/ppermute | solution.py:38
  175.0 8.6 %collective-permute-start.37 = (bf16[256,512]{1,0:T(8,128)(2,1)}, bf16[256,512]{1,0:T(8,128)(2,1)S(1)}, u32[]{:S(2)}, u32[]{:S(2)}) collective-permute-start(bf16[256,512]{1,0:T(8,128)(2,1)} %fusion.36), channel_id=1, source_target_pairs={{0,2},{1,3},{2,0},{3,1},{4,6},{5,7},{6,4},{7,5},{8,10},{9,11},{10,... | collective-permute-start | bytes 786440 | tf_op jit(solution)/shard_map/ppermute | solution.py:38
  177.8 11.7 %all-to-all-start = ((bf16[8,48,512]{2,1,0:T(8,128)(2,1)}), bf16[8,48,512]{2,1,0:T(8,128)(2,1)S(1)}, u32[]{:S(2)}, u32[]{:S(2)}) async-start(bf16[8,48,512]{2,1,0:T(8,128)(2,1)} %bitcast.35), calls=%async_computation | async-start | bytes 786432 | tf_op jit(solution)/shard_map/all_to_all | solution.py:142
  (7 other events, 5.4 us)

commit v8 on v7

--- a/solution.py
+++ b/solution.py
@@ -327,8 +327,8 @@
 
 
 def attend_kernel(place_ref, lengths_ref, query_ref, *refs):
-    near_ref, far_ref, key_own, key_top, key_low, value_own, value_other, out_ref = refs[:8]
-    source, key_weight, value_weight, keys, values, sems = refs[8:]
+    near_ref, far_ref, key_own, key_other, value_own, value_other, out_ref = refs[:7]
+    source, key_weight, value_weight, keys, values, sems = refs[7:]
     y, core, sentence = place_ref[0], place_ref[1], place_ref[2]
     rows = near_ref.shape[0]
     depth = key_own.shape[0]
@@ -336,8 +336,7 @@
         (near_ref, source.at[pl.ds(0, rows)]),
         (far_ref, source.at[pl.ds(rows, rows)]),
         (key_own, key_weight.at[y]),
-        (key_top, key_weight.at[1 - y, pl.ds(0, depth // 2)]),
-        (key_low, key_weight.at[1 - y, pl.ds(depth // 2, depth // 2)]),
+        (key_other, key_weight.at[1 - y]),
         (value_own, value_weight.at[y]),
         (value_other, value_weight.at[1 - y]),
     ]
@@ -352,10 +351,10 @@
         total += jnp.dot(source[:, depth:], weight[1], preferred_element_type=jnp.float32)
         result[...] = total.astype(jnp.bfloat16)
 
-    for copy in copies[:5]:
+    for copy in copies[:4]:
         copy.wait()
     linear(key_weight, keys)
-    for copy in copies[5:]:
+    for copy in copies[4:]:
         copy.wait()
     linear(value_weight, values)
 
@@ -381,7 +380,7 @@
     return pl.pallas_call(
         attend_kernel,
         out_shape=jax.ShapeDtypeStruct(query.shape, jnp.bfloat16),
-        in_specs=[smem, smem, full] + [hold] * 7,
+        in_specs=[smem, smem, full] + [hold] * 6,
         out_specs=full,
         scratch_shapes=[
             vmem((2 * rows, features), jnp.bfloat16),
@@ -389,7 +388,7 @@
             vmem((2, depth, width), jnp.bfloat16),
             vmem((2 * rows, width), jnp.bfloat16),
             vmem((2 * rows, width), jnp.bfloat16),
-            pltpu.SemaphoreType.DMA((7,)),
+            pltpu.SemaphoreType.DMA((6,)),
         ],
         compiler_params=pltpu.CompilerParams(vmem_limit_bytes=56 * 1024 * 1024),
         cost_estimate=SHORT,
@@ -580,9 +579,7 @@
     share = token_count // 2
     grad_half = lax.dynamic_slice_in_dim(out_grad, side * share, share, 0)
     half_y = swap(gate(grad_half, token_y, ids_far), "expert", 1)
-    depth = key_own.shape[0] // 2
-    key_top = swap(gate(key_own[:depth], token_y), "expert", 1)
-    key_low = swap(gate(key_own[depth:], key_top), "expert", 1)
+    key_other = swap(gate(key_own, half_y), "expert", 1)
     states = dec_states[0]
     normed_own, asked = normed_halves(y, states, norm_gain)
     other_y = swap(half_y, "section", 1)
@@ -622,7 +619,7 @@
 
     rows_own, rows_sent = dispatch(
         which_section,
-        gate(code, key_top, asked),
+        gate(code, asked),
         [tokens, token_x, token_y, token_far],
         tuple(((place, 0, token_count, None),) for place in range(4)),
         capacity,
@@ -630,13 +627,13 @@
     rows_core = swap(rows_sent, "dp", 1)
     pre_own, part_own = forward(rows_own)
     pre_core, part_core = forward(rows_core)
-    part_core = gate(part_core, key_low, half_pair, other_y)
+    part_core = gate(part_core, key_other)
     rise_own, rise_core = slope_of(gate(pre_own, part_core)), slope_of(gate(pre_core, part_core))
     home = send_home(part_own, near_codes, capacity) + send_home(part_core, core_codes, capacity)
 
     grads_own, grads_sent = dispatch(
         which_section,
-        gate(code, rise_own, rise_core),
+        gate(code, home[2], rise_own, rise_core),
         [out_grad, half_x, half_y, half_far, other_y, other_pair],
         (
             ((0, 0, token_count, None),),
@@ -646,10 +643,10 @@
         ),
         capacity,
     )
-    grads_core = swap(grads_sent, "dp", 1)
     held_gates = gate(gate_weights, grads_sent)
     sent_pair, first, second = combine(which_section, position, held_gates, home, sections)
     from_pair = swap(sent_pair, "section", 1)
+    grads_core = swap(grads_sent, "dp", 1)
     asked_here = swap(gate(asked, first), "expert", 1)
     to_other = (second + from_pair[1].astype(jnp.float32)).astype(jnp.bfloat16)
     from_other = swap(to_other, "section", 2)
@@ -666,26 +663,26 @@
     mixed_slice = (mixed_sum + from_other.astype(jnp.float32)).astype(jnp.bfloat16)
     mixed_near = swap(mixed_slice, "section", 1)
     back_pair, back_first, back_second = expert_backward(
-        gate(which_section, mixed_slice), slope, weight_in, sections
+        gate(which_section, mixed_near), slope, weight_in, sections
     )
-    mixed_far = swap(jnp.stack([mixed_slice, gate(mixed_near, back_first)]), "section", 2)
+    mixed_far = swap(jnp.stack([mixed_slice, mixed_near]), "section", 2)
     slices = [mixed_slice, mixed_near, mixed_far[0], mixed_far[1]]
 
     value_other = swap(gate(value_own, first), "expert", 1)
     query_there = jnp.dot(asked_here, query_own, preferred_element_type=jnp.float32)
     query_back = swap(query_there.astype(jnp.bfloat16), "expert", 1)
-    out_other = swap(gate(out_own, value_other), "expert", 1)
+    out_other = swap(gate(out_own, value_other, query_back), "expert", 1)
     query_here = jnp.dot(normed_own, query_own, preferred_element_type=jnp.float32)
     query = (query_here + query_back.astype(jnp.float32)).astype(jnp.bfloat16)
 
-    memory = make_memory(which_section, tokens, slices, final_gain)
+    memory = make_memory(which_section, gate(tokens, value_other, query_back), slices, final_gain)
     memory_x = swap(memory, "dp", 2)
     memory_core = swap(memory, "dp", 1)
 
     def sentence(which, near, far, *after):
         place = gate(jnp.stack([y, core, which]).astype(jnp.int32), *after)
         rows_of = lax.dynamic_slice_in_dim(query, which * TGT_LEN, TGT_LEN, 0)
-        parts = (key_own, key_top, key_low), (value_own, value_other)
+        parts = (key_own, key_other), (value_own, value_other)
         return attend_sentence(place, src_lengths, rows_of, near, far, *parts)
 
     back_from_pair = swap(back_pair, "section", 1)
@@ -695,19 +692,19 @@
     back_low = swap(gate(back_to_other[part:], back_top), "section", 2)
     backward_sum = back_first + back_from_pair[0].astype(jnp.float32)
     backward_sum = backward_sum + jnp.concatenate([back_top, back_low], axis=0).astype(jnp.float32)
-    context_own = sentence(x, memory, memory_core, back_top)
-    memory_far = swap(memory_x, "dp", 1)
+    context_own = sentence(x, memory, memory_core)
+    memory_far = swap(gate(memory_x, context_own), "dp", 1)
     context_other = sentence(1 - x, memory_x, memory_far)
-    place = gate(jnp.stack([y, core, x]).astype(jnp.int32), back_low)
+    place = gate(jnp.stack([y, core, x]).astype(jnp.int32), back_top)
     sent, kept_mine, kept_other = project(place, context_own, context_other, out_own, out_other)
 
     from_core = swap(sent, "dp", 1).astype(jnp.float32)
-    last = (kept_other + from_core[1]).astype(jnp.bfloat16)
+    last = (gate(kept_other, back_low) + from_core[1]).astype(jnp.bfloat16)
     from_x = swap(last, "dp", 2)
     attended = kept_mine + from_core[0] + from_x.astype(jnp.float32)
     dec_out = add_residual(attended, states, tgt_lengths)
 
-    grads_home = exchange(gate(backward_sum.astype(jnp.bfloat16), last), group_size, capacity)
+    grads_home = exchange(gate(backward_sum.astype(jnp.bfloat16), sent), group_size, capacity)
     natural = expert_ids * capacity + rank
     (token_grad,) = combine(
         which_section, natural, gate_weights, [grads_home], 1

time: 191 us -> 202 us (1.058)
  waiting for transfers between devices: 76.6 us -> 91 us
  local copies, waits for them, and re-layouts: 17.9 us -> 14.2 us
  other arithmetic: 12.1 us -> 14.2 us
    ppermute x31 -> x30, waiting for transfers between devices: 65.7 us -> 80.6 us  [swap(): return lax.ppermute(value, axis, [(i, i ^ mask) for i in range(size)])]
    slice x2 -> x1, local copies, waits for them, and re-layouts: 3.13 us -> 0.03 us  [small_body(): back_low = swap(gate(back_to_other[part:], back_top), 'section', 2)]
    ppermute x31 -> x30, starting transfers between devices: 30.7 us -> 29.9 us  [swap(): return lax.ppermute(value, axis, [(i, i ^ mask) for i in range(size)])]
    unnamed x67 -> x58, local copies, waits for them, and re-layouts: 10.3 us -> 9.88 us
  transfers between devices with their start and end apart: 39 -> 38, of which waited for: 14 -> 19; matrix products, arithmetic and copies ran while one was open for 15% -> 12% of each run, Pallas kernels for 16% -> 15%
where the time goes in v8:
time: 202 us; the launch traced here: 201 us
  waiting for transfers between devices  91 us (45%)
  starting transfers between devices  40.3 us (20%)
  Pallas kernels  32.6 us (16%)
  local copies, waits for them, and re-layouts  14.2 us (7%)
  other arithmetic  14.2 us (7%)
  matrix products  7.47 us (4%)
    ppermute x30, waiting for transfers between devices, swap(): return lax.ppermute(value, axis, [(i, i ^ mask) for i in range(size)])  80.6 us
    ppermute x30, starting transfers between devices, swap(): return lax.ppermute(value, axis, [(i, i ^ mask) for i in range(size)])  29.9 us
    pallas_call x2, Pallas kernels, attend_sentence(): pl.pallas_call(attend_kernel, out_shape=jax.ShapeDtypeStruct(query.shape,...  10.8 us
    unnamed x58, local copies, waits for them, and re-layouts  9.88 us
    pallas_call x1, Pallas kernels, expert_slope(): pl.pallas_call(functools.partial(slope_kernel, codes), out_shape=jax.Shap...  7.35 us
    ppermute x7, starting transfers between devices, send_home(): lax.ppermute(block, ('expert', 'dp'), [(i, i ^ code) for i in range(size)])  6.94 us
    ppermute x7, waiting for transfers between devices, send_home(): lax.ppermute(block, ('expert', 'dp'), [(i, i ^ code) for i in range(size)])  6.77 us
    pallas_call x1, Pallas kernels, expert_backward(): pl.pallas_call(functools.partial(backward_kernel, split), out_shape=(jax....  5.71 us
  transfers between devices with their start and end apart: 38, of which 19 were waited for; matrix products, arithmetic and copies ran while one was open for 12% of the time, Pallas kernels for 15%

profile of v8, /device:TPU:0, one launch (start us, length us, event | category | flops | bytes accessed | tf_op | source)
XLA Modules:
  0.0 200.8 jit_solution(7293056589929900029)
XLA Ops:
  0.6 3.0 %collective-permute-start.4 = (bf16[128,2048]{1,0:T(8,128)(2,1)}, bf16[128,2048]{1,0:T(8,128)(2,1)S(1)}, u32[]{:S(2)}, u32[]{:S(2)}) collective-permute-start(bf16[128,2048]{1,0:T(8,128)(2,1)} %tokens_ref), channel_id=1, source_target_pairs={{0,4},{4,0},{1,5},{5,1},{2,6},{6,2},{3,7},{7,3},{8,12},{12,8},{9,1... | collective-permute-start | bytes 1572872 | tf_op jit(solution)/shard_map/ppermute | solution.py:38
  3.7 1.5 collective-permute-start
  5.8 1.7 constant_dynamic-slice_fusion.2
  8.1 1.9 collective-permute-start.2
  10.1 5.7 %collective-permute-done.4.refs_2_ = bf16[128,2048]{1,0:T(8,128)(2,1)S(1)} collective-permute-done((bf16[128,2048]{1,0:T(8,128)(2,1)}, bf16[128,2048]{1,0:T(8,128)(2,1)S(1)}, u32[]{:S(2)}, u32[]{:S(2)}) %collective-permute-start.4) | collective-permute-done | bytes 524320 | tf_op jit(solution)/shard_map/ppermute | solution.py:38
  15.8 1.7 collective-permute-start.5
  17.7 1.5 collective-permute-start.8
  20.6 1.2 copy-done.4
  24.1 0.8 copy.36
  27.1 1.6 collective-permute-start.12
  28.7 1.3 collective-permute-done.5.refs_3_
  29.9 1.0 copy-done.1
  31.0 1.3 dispatch.2
  32.8 1.6 collective-permute-start.10
  34.4 3.2 %fusion.66 = f32[192,1024]{1,0:T(8,128)S(1)} fusion(bf16[192,2048]{1,0:T(8,128)(2,1)S(1)} %get-tuple-element.41, bf16[1,2048,1024]{2,1,0:T(8,128)(2,1)} %param.19), kind=kOutput, calls=%fused_computation.106 | convolution fusion | flops 805306368 | bytes 5767168 | tf_op jit(solution)/shard_map/dot_general | solution.py:612
  37.7 1.1 convolution_convert_fusion.1
  38.8 2.7 %collective-permute-done.11.refs_3_ = bf16[64,2048]{1,0:T(8,128)(2,1)S(1)} collective-permute-done((bf16[64,2048]{1,0:T(8,128)(2,1)S(1)}, bf16[64,2048]{1,0:T(8,128)(2,1)S(1)}, u32[]{:S(2)}, u32[]{:S(2)}) %collective-permute-start.11) | collective-permute-done | bytes 262176 | tf_op jit(solution)/shard_map/ppermute | solution.py:38
  41.5 1.5 collective-permute-start.6
  43.0 3.6 %collective-permute-done.10.refs_1_ = bf16[64,2048]{1,0:T(8,128)(2,1)S(1)} collective-permute-done((bf16[64,2048]{1,0:T(8,128)(2,1)}, bf16[64,2048]{1,0:T(8,128)(2,1)S(1)}, u32[]{:S(2)}, u32[]{:S(2)}) %collective-permute-start.10) | collective-permute-done | bytes 262176 | tf_op jit(solution)/shard_map/ppermute | solution.py:38
  47.1 2.7 %collective-permute-start.15 = (bf16[48,2048]{1,0:T(8,128)(2,1)S(1)}, bf16[48,2048]{1,0:T(8,128)(2,1)S(1)}, u32[]{:S(2)}, u32[]{:S(2)}) collective-permute-start(bf16[48,2048]{1,0:T(8,128)(2,1)S(1)} %get-tuple-element.82), channel_id=1, source_target_pairs={{0,6},{1,7},{2,4},{3,5},{4,2},{5,3},{6,0},{7,1},{8,14},{9,15},{10,... | collective-permute-start | bytes 589832 | tf_op jit(solution)/shard_map/ppermute | solution.py:223
  49.8 1.0 fusion.64
  50.8 1.1 convolution_convert_fusion
  52.3 1.6 collective-permute-start.13
  53.9 0.9 fusion.77
  54.8 2.1 %fusion.9 = (f32[192,1024]{1,0:T(8,128)}, f32[192,1024]{1,0:T(8,128)}) fusion(f32[192,1024]{1,0:T(8,128)S(1)} %fusion.66, f32[192,1024]{1,0:T(8,128)S(1)} %fusion.64), kind=kLoop, calls=%fused_computation.20 | loop fusion | flops 6684672 | bytes 3145728 | tf_op jit(solution)/shard_map/transpose(jvp())/add_any | solution.py:618
  56.9 1.8 collective-permute-done.6.refs_2_
  59.3 5.6 %collective-permute-done.13.refs_5_ = bf16[128,2048]{1,0:T(8,128)(2,1)S(1)} collective-permute-done((bf16[128,2048]{1,0:T(8,128)(2,1)S(1)}, bf16[128,2048]{1,0:T(8,128)(2,1)S(1)}, u32[]{:S(2)}, u32[]{:S(2)}) %collective-permute-start.13) | collective-permute-done | bytes 524320 | tf_op jit(solution)/shard_map/ppermute | solution.py:38
  64.9 2.4 %dispatch.3 = (bf16[192,2048]{1,0:T(8,128)(2,1)S(1)}, bf16[192,2048]{1,0:T(8,128)(2,1)}) custom-call(s32[1]{0:T(128)} %bitcast.5.section_ref, s32[8,128]{1,0:T(8,128)S(1)} %fusion.code_ref, bf16[128,2048]{1,0:T(8,128)(2,1)S(1)} %copy-done.5, bf16[64,2048]{1,0:T(8,128)(2,1)S(1)} %collective-permute-done.10.refs_1_, ...), custom_call_target="tpu_custom_call" | custom-call | flops 1 | bytes 1 | tf_op jit(solution)/shard_map/dispatch/pallas_call | solution.py:198
  67.3 0.9 copy-done.7
  68.2 1.7 collective-permute-start.19
  70.1 1.3 collective-permute-done.18.refs_6_
  72.1 3.7 %collective-permute-done.19.refs_7_ = bf16[48,2048]{1,0:T(8,128)(2,1)S(1)} collective-permute-done((bf16[48,2048]{1,0:T(8,128)(2,1)}, bf16[48,2048]{1,0:T(8,128)(2,1)S(1)}, u32[]{:S(2)}, u32[]{:S(2)}) %collective-permute-start.19) | collective-permute-done | bytes 196640 | tf_op jit(solution)/shard_map/ppermute | solution.py:223
  75.7 0.9 copy-done.12
  76.7 0.8 combine.2
  77.5 1.7 collective-permute-start.20
  79.1 7.2 %collective-permute-done.20 = bf16[2,128,512]{2,1,0:T(8,128)(2,1)S(1)} collective-permute-done((bf16[2,128,512]{2,1,0:T(8,128)(2,1)S(1)}, bf16[2,128,512]{2,1,0:T(8,128)(2,1)S(1)}, u32[]{:S(2)}, u32[]{:S(2)}) %collective-permute-start.20) | collective-permute-done | bytes 262176 | tf_op jit(solution)/shard_map/ppermute | solution.py:38
  86.4 2.6 %collective-permute-start.22 = (bf16[128,512]{1,0:T(8,128)(2,1)S(1)}, bf16[128,512]{1,0:T(8,128)(2,1)S(1)}, u32[]{:S(2)}, u32[]{:S(2)}) collective-permute-start(bf16[128,512]{1,0:T(8,128)(2,1)S(1)} %fusion.55), channel_id=1, source_target_pairs={{0,16},{8,24},{16,0},{24,8},{1,17},{9,25},{17,1},{25,9},{2,18},{10... | collective-permute-start | bytes 393224 | tf_op jit(solution)/shard_map/ppermute | solution.py:38
  89.0 2.0 %collective-permute-start.28 = (bf16[1024,512]{1,0:T(8,128)(2,1)}, bf16[1024,512]{1,0:T(8,128)(2,1)S(1)}, u32[]{:S(2)}, u32[]{:S(2)}) collective-permute-start(bf16[1024,512]{1,0:T(8,128)(2,1)} %bitcast.108), channel_id=1, source_target_pairs={{0,4},{4,0},{1,5},{5,1},{2,6},{6,2},{3,7},{7,3},{8,12},{12,8},{9,1... | collective-permute-start | bytes 3145736 | tf_op jit(solution)/shard_map/ppermute | solution.py:38
  91.1 7.3 %expert_slope.1.slope_ref = bf16[384,1024]{1,0:T(8,128)(2,1)} custom-call(s32[1]{0:T(128)} %bitcast.16.here_ref, bf16[192,2048]{1,0:T(8,128)(2,1)} %copy-done.7, bf16[192,2048]{1,0:T(8,128)(2,1)} %collective-permute-done.21.core_ref, f32[192,1024]{1,0:T(8,128)} %get-tuple-element.94.rise_own, f32[192,1024]{1,0:T(8,128)} %get-tuple-element.95.rise_core, ...), custom_call_target="tpu_custom_call" | custom-call | flops 1 | bytes 1 | tf_op jit(solution)/shard_map/expert_slope/pallas_call | solution.py:477
  98.5 1.7 collective-permute-start.23
  100.2 3.4 %collective-permute-done.23.refs_1_ = bf16[128,512]{1,0:T(8,128)(2,1)S(1)} collective-permute-done((bf16[128,512]{1,0:T(8,128)(2,1)S(1)}, bf16[128,512]{1,0:T(8,128)(2,1)S(1)}, u32[]{:S(2)}, u32[]{:S(2)}) %collective-permute-start.23) | collective-permute-done | bytes 131104 | tf_op jit(solution)/shard_map/ppermute | solution.py:38
  104.6 5.7 %expert_backward.1 = (bf16[2,384,512]{2,1,0:T(8,128)(2,1)}, f32[384,512]{1,0:T(8,128)}, f32[384,512]{1,0:T(8,128)}) custom-call(s32[1]{0:T(128)} %bitcast.5.section_ref, bf16[384,1024]{1,0:T(8,128)(2,1)} %expert_slope.1.slope_ref, bf16[2048,1024]{1,0:T(8,128)(2,1)} %bitcast.103), custom_call_target="tpu_custom_call" | custom-call | flops 1 | bytes 1 | tf_op jit(solution)/shard_map/expert_backward/pallas_call | solution.py:519
  110.3 1.7 collective-permute-start.24
  112.0 4.6 %collective-permute-done.29 = bf16[2,128,512]{2,1,0:T(8,128)(2,1)S(1)} collective-permute-done((bf16[2,128,512]{2,1,0:T(8,128)(2,1)S(1)}, bf16[2,128,512]{2,1,0:T(8,128)(2,1)S(1)}, u32[]{:S(2)}, u32[]{:S(2)}) %collective-permute-start.29) | collective-permute-done | bytes 262176 | tf_op jit(solution)/shard_map/ppermute | solution.py:38
  116.7 14.1 %collective-permute-done.27 = bf16[256,512]{1,0:T(8,128)(2,1)S(1)} collective-permute-done((bf16[256,512]{1,0:T(8,128)(2,1)S(1)}, bf16[256,512]{1,0:T(8,128)(2,1)S(1)}, u32[]{:S(2)}, u32[]{:S(2)}) %collective-permute-start.27) | collective-permute-done | bytes 262176 | tf_op jit(solution)/shard_map/ppermute | solution.py:38
  130.7 1.0 copy-done.20
  135.2 5.4 %attend_sentence.2.mine_ref = bf16[128,512]{1,0:T(8,128)(2,1)} custom-call(s32[3]{0:T(128)} %pad_add_fusion.1.place_ref, s32[2]{0:T(128)} %lengths_ref.3, bf16[128,512]{1,0:T(8,128)(2,1)} %get-tuple-element.89.query_ref, bf16[128,2048]{1,0:T(8,128)(2,1)} %copy-done.3, bf16[128,2048]{1,0:T(8,128)(2,1)} %collective-permute-done.30.refs_1_, ...), custom_call_target="tpu_custom_call" | custom-call | flops 1 | bytes 1 | tf_op jit(solution)/shard_map/attend_sentence/pallas_call | solution.py:380
  140.6 6.1 %collective-permute-done.31.refs_0_ = bf16[128,2048]{1,0:T(8,128)(2,1)} collective-permute-done((bf16[128,2048]{1,0:T(8,128)(2,1)S(1)}, bf16[128,2048]{1,0:T(8,128)(2,1)}, u32[]{:S(2)}, u32[]{:S(2)}) %collective-permute-start.31) | collective-permute-done | bytes 524320 | tf_op jit(solution)/shard_map/ppermute | solution.py:38
  146.7 1.1 fusion.34
  148.9 11.4 %collective-permute-done.25 = bf16[192,512]{1,0:T(8,128)(2,1)S(1)} collective-permute-done((bf16[192,512]{1,0:T(8,128)(2,1)S(1)}, bf16[192,512]{1,0:T(8,128)(2,1)S(1)}, u32[]{:S(2)}, u32[]{:S(2)}) %collective-permute-start.25) | collective-permute-done | bytes 196640 | tf_op jit(solution)/shard_map/ppermute | solution.py:38
  160.3 0.8 copy-done.23
  161.1 5.4 %attend_sentence.3.done_ref = bf16[128,512]{1,0:T(8,128)(2,1)} custom-call(s32[3]{0:T(128)} %pad_add_fusion.3.place_ref, s32[2]{0:T(128)} %lengths_ref.3, bf16[128,512]{1,0:T(8,128)(2,1)} %get-tuple-element.88.query_ref, bf16[128,2048]{1,0:T(8,128)(2,1)} %collective-permute-done.31.refs_0_, bf16[128,2048]{1,0:T(8,128)(2,1)} %copy-done.23, ...), custom_call_target="tpu_custom_call" | custom-call | flops 1 | bytes 1 | tf_op jit(solution)/shard_map/attend_sentence/pallas_call | solution.py:380
  166.6 0.9 copy-done.9
  167.5 2.1 %project.1 = (bf16[2,256,512]{2,1,0:T(8,128)(2,1)}, f32[256,512]{1,0:T(8,128)S(1)}, f32[256,512]{1,0:T(8,128)S(1)}) custom-call(s32[3]{0:T(128)S(1)} %copy-done.15, bf16[128,512]{1,0:T(8,128)(2,1)S(1)} %copy-done.8, bf16[128,512]{1,0:T(8,128)(2,1)S(1)} %copy-done.9, bf16[512,1024]{1,0:T(8,128)(2,1)S(1)} %bitcast.100, ...), custom_call_target="tpu_custom_call" | custom-call | flops 1 | bytes 1 | tf_op jit(solution)/shard_map/project/pallas_call | solution.py:430
  169.6 11.0 %collective-permute-done.35 = bf16[192,512]{1,0:T(8,128)(2,1)S(1)} collective-permute-done((bf16[192,512]{1,0:T(8,128)(2,1)S(1)}, bf16[192,512]{1,0:T(8,128)(2,1)S(1)}, u32[]{:S(2)}, u32[]{:S(2)}) %collective-permute-start.35) | collective-permute-done | bytes 196640 | tf_op jit(solution)/shard_map/ppermute | solution.py:38
  180.6 1.9 fusion.33
  182.6 3.5 %all-to-all-start = ((bf16[8,48,512]{2,1,0:T(8,128)(2,1)}), bf16[8,48,512]{2,1,0:T(8,128)(2,1)S(1)}, u32[]{:S(2)}, u32[]{:S(2)}) async-start(bf16[8,48,512]{2,1,0:T(8,128)(2,1)} %bitcast.33), calls=%async_computation | async-start | bytes 786432 | tf_op jit(solution)/shard_map/all_to_all | solution.py:142
  186.0 1.2 convert_element_type.112
  187.2 1.8 fusion.36
  189.0 1.9 collective-permute-start.36
  191.1 3.6 %all-to-all-done = bf16[8,48,512]{2,1,0:T(8,128)(2,1)S(1)} async-done(((bf16[8,48,512]{2,1,0:T(8,128)(2,1)}), bf16[8,48,512]{2,1,0:T(8,128)(2,1)S(1)}, u32[]{:S(2)}, u32[]{:S(2)}) %all-to-all-start) | async-done | bytes 393248 | tf_op jit(solution)/shard_map/all_to_all | solution.py:142
  194.8 1.0 combine.3
  195.8 3.2 %collective-permute-done.36 = bf16[256,512]{1,0:T(8,128)(2,1)S(1)} collective-permute-done((bf16[256,512]{1,0:T(8,128)(2,1)}, bf16[256,512]{1,0:T(8,128)(2,1)S(1)}, u32[]{:S(2)}, u32[]{:S(2)}) %collective-permute-start.36) | collective-permute-done | bytes 262176 | tf_op jit(solution)/shard_map/ppermute | solution.py:38
  199.0 1.8 fusion.52
  (116 shorter events, 16.2 us)
Async XLA Ops:
  0.6 103.5 %copy-start = (bf16[1,1024,512]{2,1,0:T(8,128)(2,1)S(1)}, bf16[1,1024,512]{2,1,0:T(8,128)(2,1)}, u32[]{:S(2)}) copy-start(bf16[1,1024,512]{2,1,0:T(8,128)(2,1)} %param.26) | copy-start | bytes 3145732
  0.6 15.2 %collective-permute-start.4 = (bf16[128,2048]{1,0:T(8,128)(2,1)}, bf16[128,2048]{1,0:T(8,128)(2,1)S(1)}, u32[]{:S(2)}, u32[]{:S(2)}) collective-permute-start(bf16[128,2048]{1,0:T(8,128)(2,1)} %tokens_ref), channel_id=1, source_target_pairs={{0,4},{4,0},{1,5},{5,1},{2,6},{6,2},{3,7},{7,3},{8,12},{12,8},{9,1... | collective-permute-start | bytes 1572872 | tf_op jit(solution)/shard_map/ppermute | solution.py:38
  3.7 4.5 %collective-permute-start = (s32[2,128]{1,0:T(2,128)}, s32[2,128]{1,0:T(2,128)S(1)}, u32[]{:S(2)}, u32[]{:S(2)}) collective-permute-start(s32[2,128]{1,0:T(2,128)} %bitcast.111), channel_id=1, source_target_pairs={{0,2},{1,3},{2,0},{3,1},{4,6},{5,7},{6,4},{7,5},{8,10},{9,11},{10,... | collective-permute-start | bytes 3080 | tf_op jit(solution)/shard_map/ppermute | solution.py:38
  5.2 20.6 %collective-permute-start.1 = (s32[2,128]{1,0:T(2,128)}, s32[2,128]{1,0:T(2,128)S(1)}, u32[]{:S(2)}, u32[]{:S(2)}) collective-permute-start(s32[2,128]{1,0:T(2,128)} %bitcast.112), channel_id=1, source_target_pairs={{0,4},{4,0},{1,5},{5,1},{2,6},{6,2},{3,7},{7,3},{8,12},{12,8},{9,1... | collective-permute-start | bytes 3080 | tf_op jit(solution)/shard_map/ppermute | solution.py:38
  5.7 23.0 %collective-permute-start.3 = (bf16[128,2048]{1,0:T(8,128)(2,1)}, bf16[128,2048]{1,0:T(8,128)(2,1)S(1)}, u32[]{:S(2)}, u32[]{:S(2)}) collective-permute-start(bf16[128,2048]{1,0:T(8,128)(2,1)} %tokens_ref), channel_id=1, source_target_pairs={{0,2},{1,3},{2,0},{3,1},{4,6},{5,7},{6,4},{7,5},{8,10},{9,11},{10,... | collective-permute-start | bytes 1572872 | tf_op jit(solution)/shard_map/ppermute | solution.py:38
  8.1 9.5 %collective-permute-start.2 = (s32[2,128]{1,0:T(2,128)S(1)}, s32[2,128]{1,0:T(2,128)S(1)}, u32[]{:S(2)}, u32[]{:S(2)}) collective-permute-start(s32[2,128]{1,0:T(2,128)S(1)} %collective-permute-done), channel_id=1, source_target_pairs={{0,4},{4,0},{1,5},{5,1},{2,6},{6,2},{3,7},{7,3},{8,12},{12,8},{9,1... | collective-permute-start | bytes 3080 | tf_op jit(solution)/shard_map/ppermute | solution.py:38
  15.8 14.1 %collective-permute-start.5 = (bf16[128,2048]{1,0:T(8,128)(2,1)S(1)}, bf16[128,2048]{1,0:T(8,128)(2,1)S(1)}, u32[]{:S(2)}, u32[]{:S(2)}) collective-permute-start(bf16[128,2048]{1,0:T(8,128)(2,1)S(1)} %collective-permute-done.4.refs_2_), channel_id=1, source_target_pairs={{0,2},{1,3},{2,0},{3,1},{4,6},{5,7},{6,4},{7,5},{8,10},{9,11},{10,... | collective-permute-start | bytes 1572872 | tf_op jit(solution)/shard_map/ppermute | solution.py:38
  17.7 5.6 %copy-start.26 = (s32[2,128]{1,0:T(2,128)}, s32[2,128]{1,0:T(2,128)S(1)}, u32[]{:S(2)}) copy-start(s32[2,128]{1,0:T(2,128)S(1)} %collective-permute-done.2) | copy-start | bytes 3076
  17.7 8.9 %collective-permute-start.8 = (bf16[64,2048]{1,0:T(8,128)(2,1)}, bf16[64,2048]{1,0:T(8,128)(2,1)S(1)}, u32[]{:S(2)}, u32[]{:S(2)}) collective-permute-start(bf16[64,2048]{1,0:T(8,128)(2,1)} %constant_dynamic-slice_fusion.2), channel_id=1, source_target_pairs={{0,4},{4,0},{1,5},{5,1},{2,6},{6,2},{3,7},{7,3},{8,12},{12,8},{9,1... | collective-permute-start | bytes 786440 | tf_op jit(solution)/shard_map/ppermute | solution.py:38
  20.6 1.2 copy-start.4
  23.3 0.8 copy-start.16
  26.6 25.8 %collective-permute-start.9 = (bf16[1024,512]{1,0:T(8,128)(2,1)}, bf16[1024,512]{1,0:T(8,128)(2,1)S(1)}, u32[]{:S(2)}, u32[]{:S(2)}) collective-permute-start(bf16[1024,512]{1,0:T(8,128)(2,1)} %bitcast.105), channel_id=1, source_target_pairs={{0,4},{4,0},{1,5},{5,1},{2,6},{6,2},{3,7},{7,3},{8,12},{12,8},{9,1... | collective-permute-start | bytes 3145736 | tf_op jit(solution)/shard_map/ppermute | solution.py:38
  27.1 31.6 %collective-permute-start.12 = (bf16[64,2048]{1,0:T(8,128)(2,1)S(1)}, bf16[64,2048]{1,0:T(8,128)(2,1)S(1)}, u32[]{:S(2)}, u32[]{:S(2)}) collective-permute-start(bf16[64,2048]{1,0:T(8,128)(2,1)S(1)} %collective-permute-done.8.refs_2_), channel_id=1, source_target_pairs={{0,8},{8,0},{16,24},{24,16},{1,9},{9,1},{17,25},{25,17},{2,10},{10... | collective-permute-start | bytes 786440 | tf_op jit(solution)/shard_map/ppermute | solution.py:38
  29.9 1.0 copy-start.1
  31.0 6.7 %copy-start.18 = (bf16[1,1024,2048]{2,1,0:T(8,128)(2,1)S(1)}, bf16[1,1024,2048]{2,1,0:T(8,128)(2,1)}, u32[]{:S(2)}) copy-start(bf16[1,1024,2048]{2,1,0:T(8,128)(2,1)} %param.20) | copy-start | bytes 12582916
  32.3 14.9 %collective-permute-start.7 = (bf16[192,2048]{1,0:T(8,128)(2,1)S(1)}, bf16[192,2048]{1,0:T(8,128)(2,1)S(1)}, u32[]{:S(2)}, u32[]{:S(2)}) collective-permute-start(bf16[192,2048]{1,0:T(8,128)(2,1)S(1)} %get-tuple-element.42), channel_id=1, source_target_pairs={{0,1},{1,0},{2,3},{3,2},{4,5},{5,4},{6,7},{7,6},{8,9},{9,8},{10,11... | collective-permute-start | bytes 2359304 | tf_op jit(solution)/shard_map/ppermute | solution.py:38
  32.3 9.2 %collective-permute-start.11 = (bf16[64,2048]{1,0:T(8,128)(2,1)S(1)}, bf16[64,2048]{1,0:T(8,128)(2,1)S(1)}, u32[]{:S(2)}, u32[]{:S(2)}) collective-permute-start(bf16[64,2048]{1,0:T(8,128)(2,1)S(1)} %collective-permute-done.8.refs_2_), channel_id=1, source_target_pairs={{0,2},{1,3},{2,0},{3,1},{4,6},{5,7},{6,4},{7,5},{8,10},{9,11},{10,... | collective-permute-start | bytes 786440 | tf_op jit(solution)/shard_map/ppermute | solution.py:38
  32.8 13.9 %collective-permute-start.10 = (bf16[64,2048]{1,0:T(8,128)(2,1)}, bf16[64,2048]{1,0:T(8,128)(2,1)S(1)}, u32[]{:S(2)}, u32[]{:S(2)}) collective-permute-start(bf16[64,2048]{1,0:T(8,128)(2,1)} %constant_dynamic-slice_fusion.2), channel_id=1, source_target_pairs={{0,2},{1,3},{2,0},{3,1},{4,6},{5,7},{6,4},{7,5},{8,10},{9,11},{10,... | collective-permute-start | bytes 786440 | tf_op jit(solution)/shard_map/ppermute | solution.py:38
  37.6 12.1 %copy-start.17 = (bf16[1,2048,1024]{2,1,0:T(8,128)(2,1)S(1)}, bf16[1,2048,1024]{2,1,0:T(8,128)(2,1)}, u32[]{:S(2)}) copy-start(bf16[1,2048,1024]{2,1,0:T(8,128)(2,1)} %param.19) | copy-start | bytes 12582916
  41.5 17.1 %collective-permute-start.6 = (bf16[48,2048]{1,0:T(8,128)(2,1)S(1)}, bf16[48,2048]{1,0:T(8,128)(2,1)S(1)}, u32[]{:S(2)}, u32[]{:S(2)}) collective-permute-start(bf16[48,2048]{1,0:T(8,128)(2,1)S(1)} %get-tuple-element.85), channel_id=1, source_target_pairs={{0,4},{1,5},{2,6},{3,7},{4,0},{5,1},{6,2},{7,3},{8,12},{9,13},{10,... | collective-permute-start | bytes 589832 | tf_op jit(solution)/shard_map/ppermute | solution.py:223
  46.7 21.5 %collective-permute-start.14 = (bf16[48,2048]{1,0:T(8,128)(2,1)S(1)}, bf16[48,2048]{1,0:T(8,128)(2,1)S(1)}, u32[]{:S(2)}, u32[]{:S(2)}) collective-permute-start(bf16[48,2048]{1,0:T(8,128)(2,1)S(1)} %get-tuple-element.83), channel_id=1, source_target_pairs={{0,2},{1,3},{2,0},{3,1},{4,6},{5,7},{6,4},{7,5},{8,10},{9,11},{10,... | collective-permute-start | bytes 589832 | tf_op jit(solution)/shard_map/ppermute | solution.py:223
  47.1 22.8 %collective-permute-start.15 = (bf16[48,2048]{1,0:T(8,128)(2,1)S(1)}, bf16[48,2048]{1,0:T(8,128)(2,1)S(1)}, u32[]{:S(2)}, u32[]{:S(2)}) collective-permute-start(bf16[48,2048]{1,0:T(8,128)(2,1)S(1)} %get-tuple-element.82), channel_id=1, source_target_pairs={{0,6},{1,7},{2,4},{3,5},{4,2},{5,3},{6,0},{7,1},{8,14},{9,15},{10,... | collective-permute-start | bytes 589832 | tf_op jit(solution)/shard_map/ppermute | solution.py:223
  50.8 14.1 %copy-start.5 = (bf16[128,2048]{1,0:T(8,128)(2,1)S(1)}, bf16[128,2048]{1,0:T(8,128)(2,1)}, u32[]{:S(2)}) copy-start(bf16[128,2048]{1,0:T(8,128)(2,1)} %refs_0_.3) | copy-start | bytes 1572868
  51.9 18.0 %copy-start.24 = (s32[128,2]{1,0:T(8,128)S(1)}, s32[128,2]{1,0:T(8,128)}, u32[]{:S(2)}) copy-start(s32[128,2]{1,0:T(8,128)} %copy.41) | copy-start | bytes 3076
  51.9 18.1 %copy-start.25 = (f32[128,2]{0,1:T(2,128)S(1)}, f32[128,2]{0,1:T(2,128)}, u32[]{:S(2)}) copy-start(f32[128,2]{0,1:T(2,128)} %param.17) | copy-start | bytes 3076
  52.3 17.6 %copy-start.19 = (bf16[1024,512]{1,0:T(8,128)(2,1)}, bf16[1024,512]{1,0:T(8,128)(2,1)S(1)}, u32[]{:S(2)}) copy-start(bf16[1024,512]{1,0:T(8,128)(2,1)S(1)} %collective-permute-done.9.refs_3_) | copy-start | bytes 3145732
  52.3 12.6 %collective-permute-start.13 = (bf16[128,2048]{1,0:T(8,128)(2,1)S(1)}, bf16[128,2048]{1,0:T(8,128)(2,1)S(1)}, u32[]{:S(2)}, u32[]{:S(2)}) collective-permute-start(bf16[128,2048]{1,0:T(8,128)(2,1)S(1)} %pad_maximum_fusion), channel_id=1, source_target_pairs={{0,8},{8,0},{16,24},{24,16},{1,9},{9,1},{17,25},{25,17},{2,10},{10... | collective-permute-start | bytes 1572872 | tf_op jit(solution)/shard_map/ppermute | solution.py:38
  58.7 11.4 %collective-permute-start.16 = (bf16[48,2048]{1,0:T(8,128)(2,1)}, bf16[48,2048]{1,0:T(8,128)(2,1)S(1)}, u32[]{:S(2)}, u32[]{:S(2)}) collective-permute-start(bf16[48,2048]{1,0:T(8,128)(2,1)} %get-tuple-element.81), channel_id=1, source_target_pairs={{0,1},{1,0},{2,3},{3,2},{4,5},{5,4},{6,7},{7,6},{8,9},{9,8},{10,11... | collective-permute-start | bytes 589832 | tf_op jit(solution)/shard_map/ppermute | solution.py:223
  58.7 11.4 %collective-permute-start.17 = (bf16[48,2048]{1,0:T(8,128)(2,1)}, bf16[48,2048]{1,0:T(8,128)(2,1)S(1)}, u32[]{:S(2)}, u32[]{:S(2)}) collective-permute-start(bf16[48,2048]{1,0:T(8,128)(2,1)} %get-tuple-element.80), channel_id=1, source_target_pairs={{0,3},{1,2},{2,1},{3,0},{4,7},{5,6},{6,5},{7,4},{8,11},{9,10},{10,... | collective-permute-start | bytes 589832 | tf_op jit(solution)/shard_map/ppermute | solution.py:223
  64.9 6.5 %collective-permute-start.18 = (bf16[48,2048]{1,0:T(8,128)(2,1)}, bf16[48,2048]{1,0:T(8,128)(2,1)S(1)}, u32[]{:S(2)}, u32[]{:S(2)}) collective-permute-start(bf16[48,2048]{1,0:T(8,128)(2,1)} %get-tuple-element.79), channel_id=1, source_target_pairs={{0,5},{1,4},{2,7},{3,6},{4,1},{5,0},{6,3},{7,2},{8,13},{9,12},{10,... | collective-permute-start | bytes 589832 | tf_op jit(solution)/shard_map/ppermute | solution.py:223
  67.3 0.9 copy-start.7
  68.2 7.5 %collective-permute-start.19 = (bf16[48,2048]{1,0:T(8,128)(2,1)}, bf16[48,2048]{1,0:T(8,128)(2,1)S(1)}, u32[]{:S(2)}, u32[]{:S(2)}) collective-permute-start(bf16[48,2048]{1,0:T(8,128)(2,1)} %get-tuple-element.78), channel_id=1, source_target_pairs={{0,7},{1,6},{2,5},{3,4},{4,3},{5,2},{6,1},{7,0},{8,15},{9,14},{10,... | collective-permute-start | bytes 589832 | tf_op jit(solution)/shard_map/ppermute | solution.py:223
  69.9 21.2 %collective-permute-start.21 = (bf16[192,2048]{1,0:T(8,128)(2,1)}, bf16[192,2048]{1,0:T(8,128)(2,1)}, u32[]{:S(2)}, u32[]{:S(2)}) collective-permute-start(bf16[192,2048]{1,0:T(8,128)(2,1)} %get-tuple-element.51), channel_id=1, source_target_pairs={{0,1},{1,0},{2,3},{3,2},{4,5},{5,4},{6,7},{7,6},{8,9},{9,8},{10,11... | collective-permute-start | bytes 2359304 | tf_op jit(solution)/shard_map/ppermute | solution.py:38
  75.7 0.9 copy-start.12
  77.5 8.9 %collective-permute-start.20 = (bf16[2,128,512]{2,1,0:T(8,128)(2,1)S(1)}, bf16[2,128,512]{2,1,0:T(8,128)(2,1)S(1)}, u32[]{:S(2)}, u32[]{:S(2)}) collective-permute-start(bf16[2,128,512]{2,1,0:T(8,128)(2,1)S(1)} %get-tuple-element.55), channel_id=1, source_target_pairs={{0,8},{8,0},{16,24},{24,16},{1,9},{9,1},{17,25},{25,17},{2,10},{10... | collective-permute-start | bytes 786440 | tf_op jit(solution)/shard_map/ppermute | solution.py:38
  86.4 12.1 %collective-permute-start.22 = (bf16[128,512]{1,0:T(8,128)(2,1)S(1)}, bf16[128,512]{1,0:T(8,128)(2,1)S(1)}, u32[]{:S(2)}, u32[]{:S(2)}) collective-permute-start(bf16[128,512]{1,0:T(8,128)(2,1)S(1)} %fusion.55), channel_id=1, source_target_pairs={{0,16},{8,24},{16,0},{24,8},{1,17},{9,25},{17,1},{25,9},{2,18},{10... | collective-permute-start | bytes 393224 | tf_op jit(solution)/shard_map/ppermute | solution.py:38
  89.0 15.1 %collective-permute-start.26 = (bf16[256,1024]{1,0:T(8,128)(2,1)}, bf16[256,1024]{1,0:T(8,128)(2,1)S(1)}, u32[]{:S(2)}, u32[]{:S(2)}) collective-permute-start(bf16[256,1024]{1,0:T(8,128)(2,1)} %copy-done.16), channel_id=1, source_target_pairs={{0,4},{4,0},{1,5},{5,1},{2,6},{6,2},{3,7},{7,3},{8,12},{12,8},{9,1... | collective-permute-start | bytes 1572872 | tf_op jit(solution)/shard_map/ppermute | solution.py:38
  89.0 41.7 %collective-permute-start.28 = (bf16[1024,512]{1,0:T(8,128)(2,1)}, bf16[1024,512]{1,0:T(8,128)(2,1)S(1)}, u32[]{:S(2)}, u32[]{:S(2)}) collective-permute-start(bf16[1024,512]{1,0:T(8,128)(2,1)} %bitcast.108), channel_id=1, source_target_pairs={{0,4},{4,0},{1,5},{5,1},{2,6},{6,2},{3,7},{7,3},{8,12},{12,8},{9,1... | collective-permute-start | bytes 3145736 | tf_op jit(solution)/shard_map/ppermute | solution.py:38
  98.4 33.3 %copy-start.2 = (bf16[128,2048]{1,0:T(8,128)(2,1)S(1)}, bf16[128,2048]{1,0:T(8,128)(2,1)}, u32[]{:S(2)}) copy-start(bf16[128,2048]{1,0:T(8,128)(2,1)} %tokens_ref) | copy-start | bytes 1572868
  98.4 33.3 %copy-start.14 = (f32[2048]{0:T(1024)S(1)}, f32[2048]{0:T(1024)}, u32[]{:S(2)}) copy-start(f32[2048]{0:T(1024)} %param.21) | copy-start | bytes 24580
  98.5 5.0 %collective-permute-start.23 = (bf16[128,512]{1,0:T(8,128)(2,1)S(1)}, bf16[128,512]{1,0:T(8,128)(2,1)S(1)}, u32[]{:S(2)}, u32[]{:S(2)}) collective-permute-start(bf16[128,512]{1,0:T(8,128)(2,1)S(1)} %fusion.54.refs_0_), channel_id=1, source_target_pairs={{0,8},{8,0},{16,24},{24,16},{1,9},{9,1},{17,25},{25,17},{2,10},{10... | collective-permute-start | bytes 393224 | tf_op jit(solution)/shard_map/ppermute | solution.py:38
  103.6 29.8 %copy-start.6 = (bf16[1,512,1024]{2,1,0:T(8,128)(2,1)S(1)}, bf16[1,512,1024]{2,1,0:T(8,128)(2,1)}, u32[]{:S(2)}) copy-start(bf16[1,512,1024]{2,1,0:T(8,128)(2,1)} %param.29) | copy-start | bytes 3145732
  103.6 13.1 %collective-permute-start.29 = (bf16[2,128,512]{2,1,0:T(8,128)(2,1)S(1)}, bf16[2,128,512]{2,1,0:T(8,128)(2,1)S(1)}, u32[]{:S(2)}, u32[]{:S(2)}) collective-permute-start(bf16[2,128,512]{2,1,0:T(8,128)(2,1)S(1)} %pad_maximum_fusion.1), channel_id=1, source_target_pairs={{0,16},{8,24},{16,0},{24,8},{1,17},{9,25},{17,1},{25,9},{2,18},{10... | collective-permute-start | bytes 786440 | tf_op jit(solution)/shard_map/ppermute | solution.py:38
  104.5 26.2 %collective-permute-start.27 = (bf16[256,512]{1,0:T(8,128)(2,1)S(1)}, bf16[256,512]{1,0:T(8,128)(2,1)S(1)}, u32[]{:S(2)}, u32[]{:S(2)}) collective-permute-start(bf16[256,512]{1,0:T(8,128)(2,1)S(1)} %convolution_convert_fusion.2), channel_id=1, source_target_pairs={{0,4},{4,0},{1,5},{5,1},{2,6},{6,2},{3,7},{7,3},{8,12},{12,8},{9,1... | collective-permute-start | bytes 786440 | tf_op jit(solution)/shard_map/ppermute | solution.py:38
  110.3 36.4 %collective-permute-start.24 = (bf16[2,384,512]{2,1,0:T(8,128)(2,1)}, bf16[2,384,512]{2,1,0:T(8,128)(2,1)}, u32[]{:S(2)}, u32[]{:S(2)}) collective-permute-start(bf16[2,384,512]{2,1,0:T(8,128)(2,1)} %get-tuple-element.61), channel_id=1, source_target_pairs={{0,8},{8,0},{16,24},{24,16},{1,9},{9,1},{17,25},{25,17},{2,10},{10... | collective-permute-start | bytes 2359304 | tf_op jit(solution)/shard_map/ppermute | solution.py:38
  130.7 1.0 copy-start.20
  132.1 3.0 %copy-start.3 = (bf16[128,2048]{1,0:T(8,128)(2,1)}, bf16[128,2048]{1,0:T(8,128)(2,1)S(1)}, u32[]{:S(2)}) copy-start(bf16[128,2048]{1,0:T(8,128)(2,1)S(1)} %memory.1.refs_0_) | copy-start | bytes 1572868
  132.2 3.0 %collective-permute-start.30 = (bf16[128,2048]{1,0:T(8,128)(2,1)S(1)}, bf16[128,2048]{1,0:T(8,128)(2,1)}, u32[]{:S(2)}, u32[]{:S(2)}) collective-permute-start(bf16[128,2048]{1,0:T(8,128)(2,1)S(1)} %memory.1.refs_0_), channel_id=1, source_target_pairs={{0,1},{1,0},{2,3},{3,2},{4,5},{5,4},{6,7},{7,6},{8,9},{9,8},{10,11... | collective-permute-start | bytes 1572872 | tf_op jit(solution)/shard_map/ppermute | solution.py:38
  132.2 14.4 %collective-permute-start.31 = (bf16[128,2048]{1,0:T(8,128)(2,1)S(1)}, bf16[128,2048]{1,0:T(8,128)(2,1)}, u32[]{:S(2)}, u32[]{:S(2)}) collective-permute-start(bf16[128,2048]{1,0:T(8,128)(2,1)S(1)} %memory.1.refs_0_), channel_id=1, source_target_pairs={{0,2},{1,3},{2,0},{3,1},{4,6},{5,7},{6,4},{7,5},{8,10},{9,11},{10,... | collective-permute-start | bytes 1572872 | tf_op jit(solution)/shard_map/ppermute | solution.py:38
  133.4 13.3 %copy-start.21 = (f32[384,512]{1,0:T(8,128)S(1)}, f32[384,512]{1,0:T(8,128)}, u32[]{:S(2)}) copy-start(f32[384,512]{1,0:T(8,128)} %get-tuple-element.60) | copy-start | bytes 2359300
  133.4 33.2 %collective-permute-start.33 = (bf16[512,1024]{1,0:T(8,128)(2,1)S(1)}, bf16[512,1024]{1,0:T(8,128)(2,1)S(1)}, u32[]{:S(2)}, u32[]{:S(2)}) collective-permute-start(bf16[512,1024]{1,0:T(8,128)(2,1)S(1)} %bitcast.99), channel_id=1, source_target_pairs={{0,4},{4,0},{1,5},{5,1},{2,6},{6,2},{3,7},{7,3},{8,12},{12,8},{9,1... | collective-permute-start | bytes 3145736 | tf_op jit(solution)/shard_map/ppermute | solution.py:38
  140.6 26.0 %copy-start.8 = (bf16[128,512]{1,0:T(8,128)(2,1)S(1)}, bf16[128,512]{1,0:T(8,128)(2,1)}, u32[]{:S(2)}) copy-start(bf16[128,512]{1,0:T(8,128)(2,1)} %attend_sentence.2.mine_ref) | copy-start | bytes 393220
  140.6 26.0 %copy-start.15 = (s32[3]{0:T(128)S(1)}, s32[3]{0:T(128)}, u32[]{:S(2)}) copy-start(s32[3]{0:T(128)} %pad_add_fusion.1.place_ref) | copy-start | bytes 40
  146.7 13.7 %collective-permute-start.32 = (bf16[128,2048]{1,0:T(8,128)(2,1)}, bf16[128,2048]{1,0:T(8,128)(2,1)S(1)}, u32[]{:S(2)}, u32[]{:S(2)}) collective-permute-start(bf16[128,2048]{1,0:T(8,128)(2,1)} %collective-permute-done.31.refs_0_), channel_id=1, source_target_pairs={{0,1},{1,0},{2,3},{3,2},{4,5},{5,4},{6,7},{7,6},{8,9},{9,8},{10,11... | collective-permute-start | bytes 1572872 | tf_op jit(solution)/shard_map/ppermute | solution.py:38
  147.8 32.8 %copy-start.22 = (f32[384,512]{1,0:T(8,128)S(1)}, f32[384,512]{1,0:T(8,128)}, u32[]{:S(2)}) copy-start(f32[384,512]{1,0:T(8,128)} %get-tuple-element.74) | copy-start | bytes 2359300
  147.9 12.5 %collective-permute-start.25 = (bf16[192,512]{1,0:T(8,128)(2,1)S(1)}, bf16[192,512]{1,0:T(8,128)(2,1)S(1)}, u32[]{:S(2)}, u32[]{:S(2)}) collective-permute-start(bf16[192,512]{1,0:T(8,128)(2,1)S(1)} %get-tuple-element.87), channel_id=1, source_target_pairs={{0,16},{8,24},{16,0},{24,8},{1,17},{9,25},{17,1},{25,9},{2,18},{10... | collective-permute-start | bytes 589832 | tf_op jit(solution)/shard_map/ppermute | solution.py:38
  160.3 0.8 copy-start.23
  166.6 0.9 copy-start.9
  167.5 23.6 %copy-start.27 = (s32[2]{0:T(128)S(1)}, s32[2]{0:T(128)}, u32[]{:S(2)}) copy-start(s32[2]{0:T(128)} %param.24) | copy-start | bytes 28
  169.6 13.0 %copy-start.10 = (f32[256,512]{1,0:T(8,128)}, f32[256,512]{1,0:T(8,128)S(1)}, u32[]{:S(2)}) copy-start(f32[256,512]{1,0:T(8,128)S(1)} %get-tuple-element.73) | copy-start | bytes 1572868
  169.6 16.5 %collective-permute-start.34 = (bf16[2,256,512]{2,1,0:T(8,128)(2,1)}, bf16[2,256,512]{2,1,0:T(8,128)(2,1)}, u32[]{:S(2)}, u32[]{:S(2)}) collective-permute-start(bf16[2,256,512]{2,1,0:T(8,128)(2,1)} %get-tuple-element.70), channel_id=1, source_target_pairs={{0,1},{1,0},{2,3},{3,2},{4,5},{5,4},{6,7},{7,6},{8,9},{9,8},{10,11... | collective-permute-start | bytes 1572872 | tf_op jit(solution)/shard_map/ppermute | solution.py:38
  169.6 11.0 %collective-permute-start.35 = (bf16[192,512]{1,0:T(8,128)(2,1)S(1)}, bf16[192,512]{1,0:T(8,128)(2,1)S(1)}, u32[]{:S(2)}, u32[]{:S(2)}) collective-permute-start(bf16[192,512]{1,0:T(8,128)(2,1)S(1)} %get-tuple-element.72), channel_id=1, source_target_pairs={{0,16},{8,24},{16,0},{24,8},{1,17},{9,25},{17,1},{25,9},{2,18},{10... | collective-permute-start | bytes 589832 | tf_op jit(solution)/shard_map/ppermute | solution.py:38
  182.6 12.2 %all-to-all-start = ((bf16[8,48,512]{2,1,0:T(8,128)(2,1)}), bf16[8,48,512]{2,1,0:T(8,128)(2,1)S(1)}, u32[]{:S(2)}, u32[]{:S(2)}) async-start(bf16[8,48,512]{2,1,0:T(8,128)(2,1)} %bitcast.33), calls=%async_computation | async-start | bytes 786432 | tf_op jit(solution)/shard_map/all_to_all | solution.py:142
  189.0 10.0 %collective-permute-start.36 = (bf16[256,512]{1,0:T(8,128)(2,1)}, bf16[256,512]{1,0:T(8,128)(2,1)S(1)}, u32[]{:S(2)}, u32[]{:S(2)}) collective-permute-start(bf16[256,512]{1,0:T(8,128)(2,1)} %fusion.36), channel_id=1, source_target_pairs={{0,2},{1,3},{2,0},{3,1},{4,6},{5,7},{6,4},{7,5},{8,10},{9,11},{10,... | collective-permute-start | bytes 786440 | tf_op jit(solution)/shard_map/ppermute | solution.py:38
  (2 other events, 1.4 us)

commit v9 on v8

--- a/solution.py
+++ b/solution.py
@@ -397,13 +397,13 @@
 
 
 def project_kernel(place_ref, mine_ref, done_ref, own_ref, other_ref, *refs):
-    sent, kept_mine, kept_other, context = refs
+    sent_mine, sent_other, kept_mine, kept_other, context = refs
     y, core, x = place_ref[0], place_ref[1], place_ref[2]
     targets = mine_ref.shape[0]
     for part, sentence in ((mine_ref, x), (done_ref, 1 - x)):
         context[pl.ds(pl.multiple_of(sentence * targets, targets), targets), :] = part[...]
     columns = kept_mine.shape[1]
-    outs = ((sent.at[0], kept_mine), (sent.at[1], kept_other))
+    outs = ((sent_mine, kept_mine), (sent_other, kept_other))
 
     def write(weight_ref, chosen):
         for side, out_ref in zip((1 - core, core), chosen):
@@ -426,12 +426,13 @@
     targets, width = 2 * mine.shape[0], mine.shape[1]
     columns = out_own.shape[1] // 2
     full = pl.BlockSpec(memory_space=pltpu.VMEM)
+    sent = jax.ShapeDtypeStruct((targets, columns), jnp.bfloat16)
     kept = jax.ShapeDtypeStruct((targets, columns), jnp.float32)
     return pl.pallas_call(
         project_kernel,
-        out_shape=(jax.ShapeDtypeStruct((2, targets, columns), jnp.bfloat16), kept, kept),
+        out_shape=(sent, sent, kept, kept),
         in_specs=[pl.BlockSpec(memory_space=pltpu.SMEM)] + [full] * 4,
-        out_specs=[full] * 3,
+        out_specs=[full] * 4,
         scratch_shapes=[vmem((targets, width), jnp.bfloat16)],
         compiler_params=pltpu.CompilerParams(vmem_limit_bytes=16 * 1024 * 1024),
         cost_estimate=SHORT,
@@ -579,9 +580,11 @@
     share = token_count // 2
     grad_half = lax.dynamic_slice_in_dim(out_grad, side * share, share, 0)
     half_y = swap(gate(grad_half, token_y, ids_far), "expert", 1)
-    key_other = swap(gate(key_own, half_y), "expert", 1)
     states = dec_states[0]
     normed_own, asked = normed_halves(y, states, norm_gain)
+    asked_here = swap(gate(asked, half_y), "expert", 1)
+    query_there = jnp.dot(asked_here, query_own, preferred_element_type=jnp.float32)
+    query_back = swap(query_there.astype(jnp.bfloat16), "expert", 1)
     other_y = swap(half_y, "section", 1)
     half_x = swap(gate(grad_half, token_far), "dp", 2)
     half_far = swap(gate(half_y, token_far), "dp", 2)
@@ -608,9 +611,9 @@
     codes_of = expert_ids ^ here
     position = ((codes_of >> 1) + 4 * (codes_of & 1)) * capacity + rank
 
-    def forward(rows):
+    def forward(rows, after):
         pre_act = jnp.dot(rows, weight_in, preferred_element_type=jnp.float32)
-        hidden = jax.nn.gelu(pre_act).astype(jnp.bfloat16)
+        hidden = jax.nn.gelu(gate(pre_act, after)).astype(jnp.bfloat16)
         part = jnp.dot(hidden, weight_out, preferred_element_type=jnp.float32)
         return pre_act, part.astype(jnp.bfloat16)
 
@@ -619,18 +622,17 @@
 
     rows_own, rows_sent = dispatch(
         which_section,
-        gate(code, asked),
+        code,
         [tokens, token_x, token_y, token_far],
         tuple(((place, 0, token_count, None),) for place in range(4)),
         capacity,
     )
     rows_core = swap(rows_sent, "dp", 1)
-    pre_own, part_own = forward(rows_own)
-    pre_core, part_core = forward(rows_core)
-    part_core = gate(part_core, key_other)
-    rise_own, rise_core = slope_of(gate(pre_own, part_core)), slope_of(gate(pre_core, part_core))
+    pre_own, part_own = forward(rows_own, rows_core)
+    pre_core, part_core = forward(gate(rows_core, asked_here), half_pair)
     home = send_home(part_own, near_codes, capacity) + send_home(part_core, core_codes, capacity)
 
+    rise_own, rise_core = slope_of(gate(pre_own, home[1])), slope_of(gate(pre_core, home[1]))
     grads_own, grads_sent = dispatch(
         which_section,
         gate(code, home[2], rise_own, rise_core),
@@ -643,11 +645,10 @@
         ),
         capacity,
     )
-    held_gates = gate(gate_weights, grads_sent)
+    held_gates = gate(gate_weights, grads_sent, query_back)
     sent_pair, first, second = combine(which_section, position, held_gates, home, sections)
     from_pair = swap(sent_pair, "section", 1)
     grads_core = swap(grads_sent, "dp", 1)
-    asked_here = swap(gate(asked, first), "expert", 1)
     to_other = (second + from_pair[1].astype(jnp.float32)).astype(jnp.bfloat16)
     from_other = swap(to_other, "section", 2)
     slope = expert_slope(
@@ -661,21 +662,21 @@
     )
     mixed_sum = gate(first, slope) + from_pair[0].astype(jnp.float32)
     mixed_slice = (mixed_sum + from_other.astype(jnp.float32)).astype(jnp.bfloat16)
+    key_other = swap(gate(key_own, first), "expert", 1)
     mixed_near = swap(mixed_slice, "section", 1)
     back_pair, back_first, back_second = expert_backward(
         gate(which_section, mixed_near), slope, weight_in, sections
     )
-    mixed_far = swap(jnp.stack([mixed_slice, mixed_near]), "section", 2)
+    mixed_far = swap(jnp.stack([mixed_slice, gate(mixed_near, key_other)]), "section", 2)
     slices = [mixed_slice, mixed_near, mixed_far[0], mixed_far[1]]
 
-    value_other = swap(gate(value_own, first), "expert", 1)
-    query_there = jnp.dot(asked_here, query_own, preferred_element_type=jnp.float32)
-    query_back = swap(query_there.astype(jnp.bfloat16), "expert", 1)
-    out_other = swap(gate(out_own, value_other, query_back), "expert", 1)
+    value_other = swap(gate(value_own, mixed_slice), "expert", 1)
+
     query_here = jnp.dot(normed_own, query_own, preferred_element_type=jnp.float32)
     query = (query_here + query_back.astype(jnp.float32)).astype(jnp.bfloat16)
 
-    memory = make_memory(which_section, gate(tokens, value_other, query_back), slices, final_gain)
+    memory = make_memory(which_section, gate(tokens, value_other), slices, final_gain)
+    out_other = swap(gate(out_own, memory), "expert", 1)
     memory_x = swap(memory, "dp", 2)
     memory_core = swap(memory, "dp", 1)
 
@@ -687,24 +688,25 @@
 
     back_from_pair = swap(back_pair, "section", 1)
     back_to_other = (back_second + back_from_pair[1].astype(jnp.float32)).astype(jnp.bfloat16)
-    part = back_to_other.shape[0] // 2
-    back_top = swap(back_to_other[:part], "section", 2)
-    back_low = swap(gate(back_to_other[part:], back_top), "section", 2)
+    back_from_other = swap(back_to_other, "section", 2)
     backward_sum = back_first + back_from_pair[0].astype(jnp.float32)
-    backward_sum = backward_sum + jnp.concatenate([back_top, back_low], axis=0).astype(jnp.float32)
+    backward_sum = backward_sum + back_from_other.astype(jnp.float32)
     context_own = sentence(x, memory, memory_core)
     memory_far = swap(gate(memory_x, context_own), "dp", 1)
     context_other = sentence(1 - x, memory_x, memory_far)
-    place = gate(jnp.stack([y, core, x]).astype(jnp.int32), back_top)
-    sent, kept_mine, kept_other = project(place, context_own, context_other, out_own, out_other)
-
-    from_core = swap(sent, "dp", 1).astype(jnp.float32)
-    last = (gate(kept_other, back_low) + from_core[1]).astype(jnp.bfloat16)
-    from_x = swap(last, "dp", 2)
-    attended = kept_mine + from_core[0] + from_x.astype(jnp.float32)
+    place = jnp.stack([y, core, x]).astype(jnp.int32)
+    sent_mine, sent_other, kept_mine, kept_other = project(
+        place, context_own, context_other, out_own, out_other
+    )
+
+    core_other = swap(sent_other, "dp", 1)
+    core_mine = swap(sent_mine, "dp", 1)
+    last = gate(kept_other, back_from_other) + core_other.astype(jnp.float32)
+    from_x = swap(last.astype(jnp.bfloat16), "dp", 2)
+    attended = kept_mine + core_mine.astype(jnp.float32) + from_x.astype(jnp.float32)
     dec_out = add_residual(attended, states, tgt_lengths)
 
-    grads_home = exchange(gate(backward_sum.astype(jnp.bfloat16), sent), group_size, capacity)
+    grads_home = exchange(gate(backward_sum.astype(jnp.bfloat16), last), group_size, capacity)
     natural = expert_ids * capacity + rank
     (token_grad,) = combine(
         which_section, natural, gate_weights, [grads_home], 1

time: 202 us -> 177 us (0.88)
  waiting for transfers between devices: 91 us -> 65.1 us
  starting transfers between devices: 40.3 us -> 45.7 us
  local copies, waits for them, and re-layouts: 14.2 us -> 11.8 us
  other arithmetic: 14.2 us -> 11.9 us
    ppermute x30, waiting for transfers between devices: 80.6 us -> 50.2 us  [swap(): return lax.ppermute(value, axis, [(i, i ^ mask) for i in range(size)])]
    ppermute x30, starting transfers between devices: 29.9 us -> 35.4 us  [swap(): return lax.ppermute(value, axis, [(i, i ^ mask) for i in range(size)])]
    convert_element_type x2 -> x0, other arithmetic: 2.98 us -> none  [the longest x1 1.82 us: small_body(): last = (gate(kept_other, back_low) + from_core[1]).astype(jnp.bfloat16)]
    unnamed x58 -> x59, local copies, waits for them, and re-layouts: 9.88 us -> 7.41 us
    ppermute x7, waiting for transfers between devices: 6.77 us -> 9.22 us  [send_home(): lax.ppermute(block, ('expert', 'dp'), [(i, i ^ code) for i in range(size)])]
  transfers between devices with their start and end apart: 38 -> 38, of which waited for: 19 -> 18; matrix products, arithmetic and copies ran while one was open for 12% -> 14% of each run, Pallas kernels for 15% -> 18%
where the time goes in v9:
time: 177 us; the launch traced here: 176 us
  waiting for transfers between devices  65.1 us (37%)
  starting transfers between devices  45.7 us (26%)
  Pallas kernels  32.7 us (18%)
  other arithmetic  11.9 us (7%)
  local copies, waits for them, and re-layouts  11.8 us (7%)
  matrix products  7.67 us (4%)
    ppermute x30, waiting for transfers between devices, swap(): return lax.ppermute(value, axis, [(i, i ^ mask) for i in range(size)])  50.2 us
    ppermute x30, starting transfers between devices, swap(): return lax.ppermute(value, axis, [(i, i ^ mask) for i in range(size)])  35.4 us
    pallas_call x2, Pallas kernels, attend_sentence(): pl.pallas_call(attend_kernel, out_shape=jax.ShapeDtypeStruct(query.shape,...  10.9 us
    ppermute x7, waiting for transfers between devices, send_home(): lax.ppermute(block, ('expert', 'dp'), [(i, i ^ code) for i in range(size)])  9.22 us
    pallas_call x1, Pallas kernels, expert_slope(): pl.pallas_call(functools.partial(slope_kernel, codes), out_shape=jax.Shap...  7.41 us
    unnamed x59, local copies, waits for them, and re-layouts  7.41 us
    ppermute x7, starting transfers between devices, send_home(): lax.ppermute(block, ('expert', 'dp'), [(i, i ^ code) for i in range(size)])  6.88 us
    pallas_call x1, Pallas kernels, expert_backward(): pl.pallas_call(functools.partial(backward_kernel, split), out_shape=(jax....  5.76 us
  transfers between devices with their start and end apart: 38, of which 18 were waited for; matrix products, arithmetic and copies ran while one was open for 14% of the time, Pallas kernels for 18%

profile of v9, /device:TPU:0, one launch (start us, length us, event | category | flops | bytes accessed | tf_op | source)
XLA Modules:
  0.0 175.9 jit_solution(7410199523531444141)
XLA Ops:
  0.6 3.0 %collective-permute-start = (bf16[128,2048]{1,0:T(8,128)(2,1)}, bf16[128,2048]{1,0:T(8,128)(2,1)S(1)}, u32[]{:S(2)}, u32[]{:S(2)}) collective-permute-start(bf16[128,2048]{1,0:T(8,128)(2,1)} %tokens_ref), channel_id=1, source_target_pairs={{0,4},{4,0},{1,5},{5,1},{2,6},{6,2},{3,7},{7,3},{8,12},{12,8},{9,1... | collective-permute-start | bytes 1572872 | tf_op jit(solution)/shard_map/ppermute | solution.py:38
  3.8 1.9 %collective-permute-start.1 = (s32[2,128]{1,0:T(2,128)}, s32[2,128]{1,0:T(2,128)S(1)}, u32[]{:S(2)}, u32[]{:S(2)}) collective-permute-start(s32[2,128]{1,0:T(2,128)} %bitcast.92), channel_id=1, source_target_pairs={{0,2},{1,3},{2,0},{3,1},{4,6},{5,7},{6,4},{7,5},{8,10},{9,11},{10,... | collective-permute-start | bytes 3080 | tf_op jit(solution)/shard_map/ppermute | solution.py:38
  5.8 1.7 constant_dynamic-slice_fusion.2
  8.1 1.9 %collective-permute-start.2 = (s32[2,128]{1,0:T(2,128)S(1)}, s32[2,128]{1,0:T(2,128)S(1)}, u32[]{:S(2)}, u32[]{:S(2)}) collective-permute-start(s32[2,128]{1,0:T(2,128)S(1)} %collective-permute-done.1), channel_id=1, source_target_pairs={{0,4},{4,0},{1,5},{5,1},{2,6},{6,2},{3,7},{7,3},{8,12},{12,8},{9,1... | collective-permute-start | bytes 3080 | tf_op jit(solution)/shard_map/ppermute | solution.py:38
  10.1 5.7 %collective-permute-done.refs_2_ = bf16[128,2048]{1,0:T(8,128)(2,1)S(1)} collective-permute-done((bf16[128,2048]{1,0:T(8,128)(2,1)}, bf16[128,2048]{1,0:T(8,128)(2,1)S(1)}, u32[]{:S(2)}, u32[]{:S(2)}) %collective-permute-start) | collective-permute-done | bytes 524320 | tf_op jit(solution)/shard_map/ppermute | solution.py:38
  15.8 1.7 collective-permute-start.8
  17.7 1.5 collective-permute-start.3
  20.6 1.2 copy-done.4
  27.1 1.6 collective-permute-start.14
  28.7 1.3 collective-permute-done.8.refs_3_
  30.3 1.6 collective-permute-start.13
  32.0 1.0 copy-done.1
  33.0 1.3 dispatch.2
  34.4 3.4 %fusion.60 = f32[192,1024]{1,0:T(8,128)S(1)} fusion(bf16[192,2048]{1,0:T(8,128)(2,1)S(1)} %get-tuple-element.44, bf16[1,2048,1024]{2,1,0:T(8,128)(2,1)} %param.19), kind=kOutput, calls=%fused_computation.101 | convolution fusion | flops 805306368 | bytes 5767168 | tf_op jit(solution)/shard_map/dot_general | solution.py:615
  37.8 1.7 collective-permute-done.12.refs_1_
  39.4 3.7 %collective-permute-done.13.refs_3_ = bf16[64,2048]{1,0:T(8,128)(2,1)S(1)} collective-permute-done((bf16[64,2048]{1,0:T(8,128)(2,1)S(1)}, bf16[64,2048]{1,0:T(8,128)(2,1)S(1)}, u32[]{:S(2)}, u32[]{:S(2)}) %collective-permute-start.13) | collective-permute-done | bytes 262176 | tf_op jit(solution)/shard_map/ppermute | solution.py:38
  43.2 1.5 collective-permute-start.15
  45.2 1.6 collective-permute-start.5
  46.8 1.1 convolution_convert_fusion.1
  48.2 1.7 collective-permute-start.11
  50.0 1.0 fusion.58
  51.0 1.1 convolution_convert_fusion
  52.1 0.9 fusion.71
  53.0 3.6 %collective-permute-done.11.refs_1_ = bf16[48,2048]{1,0:T(8,128)(2,1)S(1)} collective-permute-done((bf16[48,2048]{1,0:T(8,128)(2,1)S(1)}, bf16[48,2048]{1,0:T(8,128)(2,1)S(1)}, u32[]{:S(2)}, u32[]{:S(2)}) %collective-permute-start.11) | collective-permute-done | bytes 196640 | tf_op jit(solution)/shard_map/ppermute | solution.py:223
  56.6 1.5 collective-permute-start.10
  58.1 1.4 fusion.9.rise_own
  59.5 1.4 fusion.15.rise_core
  60.9 1.4 collective-permute-done.10.refs_2_
  62.3 1.6 collective-permute-start.19
  63.8 1.2 collective-permute-start.18
  65.1 2.3 %dispatch.3 = (bf16[192,2048]{1,0:T(8,128)(2,1)S(1)}, bf16[192,2048]{1,0:T(8,128)(2,1)}) custom-call(s32[1]{0:T(128)} %bitcast.8.section_ref, s32[8,128]{1,0:T(8,128)S(1)} %fusion.code_ref, bf16[128,2048]{1,0:T(8,128)(2,1)S(1)} %copy-done.5, bf16[64,2048]{1,0:T(8,128)(2,1)S(1)} %collective-permute-done.12.refs_1_, ...), custom_call_target="tpu_custom_call" | custom-call | flops 1 | bytes 1 | tf_op jit(solution)/shard_map/dispatch/pallas_call | solution.py:198
  67.4 0.9 copy-done.7
  69.2 1.1 collective-permute-done.20.refs_7_
  70.3 3.1 %collective-permute-done.19.refs_6_ = bf16[48,2048]{1,0:T(8,128)(2,1)S(1)} collective-permute-done((bf16[48,2048]{1,0:T(8,128)(2,1)}, bf16[48,2048]{1,0:T(8,128)(2,1)S(1)}, u32[]{:S(2)}, u32[]{:S(2)}) %collective-permute-start.19) | collective-permute-done | bytes 196640 | tf_op jit(solution)/shard_map/ppermute | solution.py:223
  73.3 0.8 combine.2
  74.7 0.9 collective-permute-start.26
  75.6 7.0 %collective-permute-done.21 = bf16[2,128,512]{2,1,0:T(8,128)(2,1)S(1)} collective-permute-done((bf16[2,128,512]{2,1,0:T(8,128)(2,1)S(1)}, bf16[2,128,512]{2,1,0:T(8,128)(2,1)S(1)}, u32[]{:S(2)}, u32[]{:S(2)}) %collective-permute-start.21) | collective-permute-done | bytes 262176 | tf_op jit(solution)/shard_map/ppermute | solution.py:38
  82.6 2.7 %collective-permute-start.23 = (bf16[128,512]{1,0:T(8,128)(2,1)S(1)}, bf16[128,512]{1,0:T(8,128)(2,1)S(1)}, u32[]{:S(2)}, u32[]{:S(2)}) collective-permute-start(bf16[128,512]{1,0:T(8,128)(2,1)S(1)} %fusion.49), channel_id=1, source_target_pairs={{0,16},{8,24},{16,0},{24,8},{1,17},{9,25},{17,1},{25,9},{2,18},{10... | collective-permute-start | bytes 393224 | tf_op jit(solution)/shard_map/ppermute | solution.py:38
  85.3 7.4 %expert_slope.1.slope_ref = bf16[384,1024]{1,0:T(8,128)(2,1)} custom-call(s32[1]{0:T(128)} %bitcast.17.here_ref, bf16[192,2048]{1,0:T(8,128)(2,1)} %copy-done.7, bf16[192,2048]{1,0:T(8,128)(2,1)} %collective-permute-done.22.core_ref, f32[192,1024]{1,0:T(8,128)} %fusion.9.rise_own, f32[192,1024]{1,0:T(8,128)} %fusion.15.rise_core, bf16[1024,2048]{1,0:T(8,128)(2,1)} %bitcast.84), custom_call_target="tpu_custom_call" | custom-call | flops 1 | bytes 1 | tf_op jit(solution)/shard_map/expert_slope/pallas_call | solution.py:478
  92.8 0.9 collective-permute-start.24
  94.2 4.5 %collective-permute-done.25.refs_1_ = bf16[128,512]{1,0:T(8,128)(2,1)S(1)} collective-permute-done((bf16[128,512]{1,0:T(8,128)(2,1)S(1)}, bf16[128,512]{1,0:T(8,128)(2,1)S(1)}, u32[]{:S(2)}, u32[]{:S(2)}) %collective-permute-start.25) | collective-permute-done | bytes 131104 | tf_op jit(solution)/shard_map/ppermute | solution.py:38
  98.7 2.2 %collective-permute-done.26.refs_3_ = bf16[1024,512]{1,0:T(8,128)(2,1)S(1)} collective-permute-done((bf16[1024,512]{1,0:T(8,128)(2,1)}, bf16[1024,512]{1,0:T(8,128)(2,1)S(1)}, u32[]{:S(2)}, u32[]{:S(2)}) %collective-permute-start.26) | collective-permute-done | bytes 1048608 | tf_op jit(solution)/shard_map/ppermute | solution.py:38
  101.0 2.7 %collective-permute-start.27 = (bf16[2,128,512]{2,1,0:T(8,128)(2,1)S(1)}, bf16[2,128,512]{2,1,0:T(8,128)(2,1)S(1)}, u32[]{:S(2)}, u32[]{:S(2)}) collective-permute-start(bf16[2,128,512]{2,1,0:T(8,128)(2,1)S(1)} %pad_maximum_fusion), channel_id=1, source_target_pairs={{0,16},{8,24},{16,0},{24,8},{1,17},{9,25},{17,1},{25,9},{2,18},{10... | collective-permute-start | bytes 786440 | tf_op jit(solution)/shard_map/ppermute | solution.py:38
  103.6 5.8 %expert_backward.1 = (bf16[2,384,512]{2,1,0:T(8,128)(2,1)}, f32[384,512]{1,0:T(8,128)}, f32[384,512]{1,0:T(8,128)}) custom-call(s32[1]{0:T(128)} %bitcast.8.section_ref, bf16[384,1024]{1,0:T(8,128)(2,1)} %expert_slope.1.slope_ref, bf16[2048,1024]{1,0:T(8,128)(2,1)} %bitcast.83), custom_call_target="tpu_custom_call" | custom-call | flops 1 | bytes 1 | tf_op jit(solution)/shard_map/expert_backward/pallas_call | solution.py:520
  109.4 1.6 collective-permute-start.33
  111.1 2.7 %collective-permute-done.27 = bf16[2,128,512]{2,1,0:T(8,128)(2,1)S(1)} collective-permute-done((bf16[2,128,512]{2,1,0:T(8,128)(2,1)S(1)}, bf16[2,128,512]{2,1,0:T(8,128)(2,1)S(1)}, u32[]{:S(2)}, u32[]{:S(2)}) %collective-permute-start.27) | collective-permute-done | bytes 262176 | tf_op jit(solution)/shard_map/ppermute | solution.py:38
  113.7 8.6 %collective-permute-done.24.refs_5_ = bf16[1024,512]{1,0:T(8,128)(2,1)S(1)} collective-permute-done((bf16[1024,512]{1,0:T(8,128)(2,1)S(1)}, bf16[1024,512]{1,0:T(8,128)(2,1)S(1)}, u32[]{:S(2)}, u32[]{:S(2)}) %collective-permute-start.24) | collective-permute-done | bytes 1048608 | tf_op jit(solution)/shard_map/ppermute | solution.py:38
  122.8 1.8 %collective-permute-start.29 = (bf16[128,2048]{1,0:T(8,128)(2,1)S(1)}, bf16[128,2048]{1,0:T(8,128)(2,1)}, u32[]{:S(2)}, u32[]{:S(2)}) collective-permute-start(bf16[128,2048]{1,0:T(8,128)(2,1)S(1)} %memory.1.refs_0_), channel_id=1, source_target_pairs={{0,2},{1,3},{2,0},{3,1},{4,6},{5,7},{6,4},{7,5},{8,10},{9,11},{10,... | collective-permute-start | bytes 1572872 | tf_op jit(solution)/shard_map/ppermute | solution.py:38
  124.6 1.0 collective-permute-start.31
  127.5 5.4 %attend_sentence.2.mine_ref = bf16[128,512]{1,0:T(8,128)(2,1)} custom-call(s32[3]{0:T(128)} %pad_add_fusion.1.place_ref, s32[2]{0:T(128)} %lengths_ref.3, bf16[128,512]{1,0:T(8,128)(2,1)} %get-tuple-element.89.query_ref, bf16[128,2048]{1,0:T(8,128)(2,1)} %copy-done.3, bf16[128,2048]{1,0:T(8,128)(2,1)} %collective-permute-done.28.refs_1_, ...), custom_call_target="tpu_custom_call" | custom-call | flops 1 | bytes 1 | tf_op jit(solution)/shard_map/attend_sentence/pallas_call | solution.py:380
  132.9 4.4 %collective-permute-done.29.refs_0_ = bf16[128,2048]{1,0:T(8,128)(2,1)} collective-permute-done((bf16[128,2048]{1,0:T(8,128)(2,1)S(1)}, bf16[128,2048]{1,0:T(8,128)(2,1)}, u32[]{:S(2)}, u32[]{:S(2)}) %collective-permute-start.29) | collective-permute-done | bytes 524320 | tf_op jit(solution)/shard_map/ppermute | solution.py:38
  137.3 1.1 fusion.34
  138.4 2.7 %collective-permute-start.34 = (bf16[384,512]{1,0:T(8,128)(2,1)S(1)}, bf16[384,512]{1,0:T(8,128)(2,1)S(1)}, u32[]{:S(2)}, u32[]{:S(2)}) collective-permute-start(bf16[384,512]{1,0:T(8,128)(2,1)S(1)} %fusion.34), channel_id=1, source_target_pairs={{0,16},{8,24},{16,0},{24,8},{1,17},{9,25},{17,1},{25,9},{2,18},{10... | collective-permute-start | bytes 1179656 | tf_op jit(solution)/shard_map/ppermute | solution.py:38
  142.5 5.5 %attend_sentence.3.done_ref = bf16[128,512]{1,0:T(8,128)(2,1)} custom-call(s32[3]{0:T(128)} %pad_add_fusion.3.place_ref, s32[2]{0:T(128)} %lengths_ref.3, bf16[128,512]{1,0:T(8,128)(2,1)} %get-tuple-element.88.query_ref, bf16[128,2048]{1,0:T(8,128)(2,1)} %collective-permute-done.29.refs_0_, bf16[128,2048]{1,0:T(8,128)(2,1)} %copy-done.21, ...), custom_call_target="tpu_custom_call" | custom-call | flops 1 | bytes 1 | tf_op jit(solution)/shard_map/attend_sentence/pallas_call | solution.py:380
  148.0 2.0 %collective-permute-done.31.other_ref = bf16[512,1024]{1,0:T(8,128)(2,1)} collective-permute-done((bf16[512,1024]{1,0:T(8,128)(2,1)S(1)}, bf16[512,1024]{1,0:T(8,128)(2,1)}, u32[]{:S(2)}, u32[]{:S(2)}) %collective-permute-start.31) | collective-permute-done | bytes 1048608 | tf_op jit(solution)/shard_map/ppermute | solution.py:38
  150.0 0.9 copy-done.9
  150.9 2.0 %project.1 = (bf16[256,512]{1,0:T(8,128)(2,1)S(1)}, bf16[256,512]{1,0:T(8,128)(2,1)S(1)}, f32[256,512]{1,0:T(8,128)S(1)}, f32[256,512]{1,0:T(8,128)S(1)}) custom-call(s32[3]{0:T(128)S(1)} %copy-done.12, bf16[128,512]{1,0:T(8,128)(2,1)S(1)} %copy-done.8, bf16[128,512]{1,0:T(8,128)(2,1)S(1)} %copy-done.9, bf16[512,1024]{1,0:T(8,128)(2,1)S(1)} %bitcast.80, ...), custom_call_target="tpu_custom_call" | custom-call | flops 1 | bytes 1 | tf_op jit(solution)/shard_map/project/pallas_call | solution.py:431
  153.5 5.8 %collective-permute-done.34 = bf16[384,512]{1,0:T(8,128)(2,1)S(1)} collective-permute-done((bf16[384,512]{1,0:T(8,128)(2,1)S(1)}, bf16[384,512]{1,0:T(8,128)(2,1)S(1)}, u32[]{:S(2)}, u32[]{:S(2)}) %collective-permute-start.34) | collective-permute-done | bytes 393248 | tf_op jit(solution)/shard_map/ppermute | solution.py:38
  159.4 1.8 %collective-permute-start.36 = (bf16[256,512]{1,0:T(8,128)(2,1)S(1)}, bf16[256,512]{1,0:T(8,128)(2,1)S(1)}, u32[]{:S(2)}, u32[]{:S(2)}) collective-permute-start(bf16[256,512]{1,0:T(8,128)(2,1)S(1)} %convert_add_fusion.3), channel_id=1, source_target_pairs={{0,2},{1,3},{2,0},{3,1},{4,6},{5,7},{6,4},{7,5},{8,10},{9,11},{10,... | collective-permute-start | bytes 786440 | tf_op jit(solution)/shard_map/ppermute | solution.py:38
  161.2 1.9 %fusion.33 = bf16[384,512]{1,0:T(8,128)(2,1)} fusion(f32[384,512]{1,0:T(8,128)S(1)} %copy-done.20, bf16[384,512]{1,0:T(8,128)(2,1)S(1)} %collective-permute-done.34, bf16[2,384,512]{2,1,0:T(8,128)(2,1)} %collective-permute-done.33), kind=kLoop, calls=%fused_computation.45 | loop fusion | flops 983040 | bytes 1966080 | tf_op jit(solution)/shard_map/convert_element_type | solution.py:709
  163.2 3.5 %all-to-all-start = ((bf16[8,48,512]{2,1,0:T(8,128)(2,1)}), bf16[8,48,512]{2,1,0:T(8,128)(2,1)S(1)}, u32[]{:S(2)}, u32[]{:S(2)}) async-start(bf16[8,48,512]{2,1,0:T(8,128)(2,1)} %bitcast.31), calls=%async_computation | async-start | bytes 786432 | tf_op jit(solution)/shard_map/all_to_all | solution.py:142
  167.4 1.8 %fusion.46 = bf16[1,256,512]{2,1,0:T(8,128)(2,1)} fusion(bf16[256,512]{1,0:T(8,128)(2,1)S(1)} %collective-permute-done.36, f32[256,512]{1,0:T(8,128)S(1)} %get-tuple-element.68, bf16[256,512]{1,0:T(8,128)(2,1)S(1)} %collective-permute-done.32, bf16[1,256,2048]{2,1,0:T(8,128)(2,1)} %param.22, s32[]{:T(128)S(6)} %select_n.35, ...), kind=kLoop, calls=%fused_computation.62 | loop fusion | flops 1048576 | bytes 1573124 | tf_op jit(solution)/shard_map/broadcast_in_dim | solution.py:714
  169.2 5.7 %all-to-all-done = bf16[8,48,512]{2,1,0:T(8,128)(2,1)S(1)} async-done(((bf16[8,48,512]{2,1,0:T(8,128)(2,1)}), bf16[8,48,512]{2,1,0:T(8,128)(2,1)S(1)}, u32[]{:S(2)}, u32[]{:S(2)}) %all-to-all-start) | async-done | bytes 393248 | tf_op jit(solution)/shard_map/all_to_all | solution.py:142
  174.9 1.0 combine.3
  (116 shorter events, 16.1 us)
Async XLA Ops:
  0.6 44.1 %copy-start = (bf16[1,1024,512]{2,1,0:T(8,128)(2,1)S(1)}, bf16[1,1024,512]{2,1,0:T(8,128)(2,1)}, u32[]{:S(2)}) copy-start(bf16[1,1024,512]{2,1,0:T(8,128)(2,1)} %param.26) | copy-start | bytes 3145732
  0.6 15.2 %collective-permute-start = (bf16[128,2048]{1,0:T(8,128)(2,1)}, bf16[128,2048]{1,0:T(8,128)(2,1)S(1)}, u32[]{:S(2)}, u32[]{:S(2)}) collective-permute-start(bf16[128,2048]{1,0:T(8,128)(2,1)} %tokens_ref), channel_id=1, source_target_pairs={{0,4},{4,0},{1,5},{5,1},{2,6},{6,2},{3,7},{7,3},{8,12},{12,8},{9,1... | collective-permute-start | bytes 1572872 | tf_op jit(solution)/shard_map/ppermute | solution.py:38
  3.7 22.1 %collective-permute-start.6 = (s32[2,128]{1,0:T(2,128)}, s32[2,128]{1,0:T(2,128)S(1)}, u32[]{:S(2)}, u32[]{:S(2)}) collective-permute-start(s32[2,128]{1,0:T(2,128)} %bitcast.91), channel_id=1, source_target_pairs={{0,4},{4,0},{1,5},{5,1},{2,6},{6,2},{3,7},{7,3},{8,12},{12,8},{9,1... | collective-permute-start | bytes 3080 | tf_op jit(solution)/shard_map/ppermute | solution.py:38
  3.8 4.4 %collective-permute-start.1 = (s32[2,128]{1,0:T(2,128)}, s32[2,128]{1,0:T(2,128)S(1)}, u32[]{:S(2)}, u32[]{:S(2)}) collective-permute-start(s32[2,128]{1,0:T(2,128)} %bitcast.92), channel_id=1, source_target_pairs={{0,2},{1,3},{2,0},{3,1},{4,6},{5,7},{6,4},{7,5},{8,10},{9,11},{10,... | collective-permute-start | bytes 3080 | tf_op jit(solution)/shard_map/ppermute | solution.py:38
  5.7 26.3 %collective-permute-start.7 = (bf16[128,2048]{1,0:T(8,128)(2,1)}, bf16[128,2048]{1,0:T(8,128)(2,1)S(1)}, u32[]{:S(2)}, u32[]{:S(2)}) collective-permute-start(bf16[128,2048]{1,0:T(8,128)(2,1)} %tokens_ref), channel_id=1, source_target_pairs={{0,2},{1,3},{2,0},{3,1},{4,6},{5,7},{6,4},{7,5},{8,10},{9,11},{10,... | collective-permute-start | bytes 1572872 | tf_op jit(solution)/shard_map/ppermute | solution.py:38
  8.1 9.5 %collective-permute-start.2 = (s32[2,128]{1,0:T(2,128)S(1)}, s32[2,128]{1,0:T(2,128)S(1)}, u32[]{:S(2)}, u32[]{:S(2)}) collective-permute-start(s32[2,128]{1,0:T(2,128)S(1)} %collective-permute-done.1), channel_id=1, source_target_pairs={{0,4},{4,0},{1,5},{5,1},{2,6},{6,2},{3,7},{7,3},{8,12},{12,8},{9,1... | collective-permute-start | bytes 3080 | tf_op jit(solution)/shard_map/ppermute | solution.py:38
  15.8 14.1 %collective-permute-start.8 = (bf16[128,2048]{1,0:T(8,128)(2,1)S(1)}, bf16[128,2048]{1,0:T(8,128)(2,1)S(1)}, u32[]{:S(2)}, u32[]{:S(2)}) collective-permute-start(bf16[128,2048]{1,0:T(8,128)(2,1)S(1)} %collective-permute-done.refs_2_), channel_id=1, source_target_pairs={{0,2},{1,3},{2,0},{3,1},{4,6},{5,7},{6,4},{7,5},{8,10},{9,11},{10,... | collective-permute-start | bytes 1572872 | tf_op jit(solution)/shard_map/ppermute | solution.py:38
  17.7 2.9 %copy-start.26 = (s32[2,128]{1,0:T(2,128)}, s32[2,128]{1,0:T(2,128)S(1)}, u32[]{:S(2)}) copy-start(s32[2,128]{1,0:T(2,128)S(1)} %collective-permute-done.2) | copy-start | bytes 3076
  17.7 8.9 %collective-permute-start.3 = (bf16[64,2048]{1,0:T(8,128)(2,1)}, bf16[64,2048]{1,0:T(8,128)(2,1)S(1)}, u32[]{:S(2)}, u32[]{:S(2)}) collective-permute-start(bf16[64,2048]{1,0:T(8,128)(2,1)} %constant_dynamic-slice_fusion.2), channel_id=1, source_target_pairs={{0,4},{4,0},{1,5},{5,1},{2,6},{6,2},{3,7},{7,3},{8,12},{12,8},{9,1... | collective-permute-start | bytes 786440 | tf_op jit(solution)/shard_map/ppermute | solution.py:38
  20.6 1.2 copy-start.4
  23.3 0.8 copy-start.13
  26.6 18.1 %collective-permute-start.4 = (bf16[256,1024]{1,0:T(8,128)(2,1)}, bf16[256,1024]{1,0:T(8,128)(2,1)S(1)}, u32[]{:S(2)}, u32[]{:S(2)}) collective-permute-start(bf16[256,1024]{1,0:T(8,128)(2,1)} %copy-done.13), channel_id=1, source_target_pairs={{0,4},{4,0},{1,5},{5,1},{2,6},{6,2},{3,7},{7,3},{8,12},{12,8},{9,1... | collective-permute-start | bytes 1572872 | tf_op jit(solution)/shard_map/ppermute | solution.py:38
  27.1 35.2 %collective-permute-start.14 = (bf16[64,2048]{1,0:T(8,128)(2,1)S(1)}, bf16[64,2048]{1,0:T(8,128)(2,1)S(1)}, u32[]{:S(2)}, u32[]{:S(2)}) collective-permute-start(bf16[64,2048]{1,0:T(8,128)(2,1)S(1)} %collective-permute-done.3.refs_2_), channel_id=1, source_target_pairs={{0,8},{8,0},{16,24},{24,16},{1,9},{9,1},{17,25},{25,17},{2,10},{10... | collective-permute-start | bytes 786440 | tf_op jit(solution)/shard_map/ppermute | solution.py:38
  30.0 9.5 %collective-permute-start.12 = (bf16[64,2048]{1,0:T(8,128)(2,1)}, bf16[64,2048]{1,0:T(8,128)(2,1)S(1)}, u32[]{:S(2)}, u32[]{:S(2)}) collective-permute-start(bf16[64,2048]{1,0:T(8,128)(2,1)} %constant_dynamic-slice_fusion.2), channel_id=1, source_target_pairs={{0,2},{1,3},{2,0},{3,1},{4,6},{5,7},{6,4},{7,5},{8,10},{9,11},{10,... | collective-permute-start | bytes 786440 | tf_op jit(solution)/shard_map/ppermute | solution.py:38
  30.3 12.8 %collective-permute-start.13 = (bf16[64,2048]{1,0:T(8,128)(2,1)S(1)}, bf16[64,2048]{1,0:T(8,128)(2,1)S(1)}, u32[]{:S(2)}, u32[]{:S(2)}) collective-permute-start(bf16[64,2048]{1,0:T(8,128)(2,1)S(1)} %collective-permute-done.3.refs_2_), channel_id=1, source_target_pairs={{0,2},{1,3},{2,0},{3,1},{4,6},{5,7},{6,4},{7,5},{8,10},{9,11},{10,... | collective-permute-start | bytes 786440 | tf_op jit(solution)/shard_map/ppermute | solution.py:38
  32.0 1.0 copy-start.1
  34.3 12.5 %collective-permute-start.9 = (bf16[192,2048]{1,0:T(8,128)(2,1)S(1)}, bf16[192,2048]{1,0:T(8,128)(2,1)S(1)}, u32[]{:S(2)}, u32[]{:S(2)}) collective-permute-start(bf16[192,2048]{1,0:T(8,128)(2,1)S(1)} %get-tuple-element.45), channel_id=1, source_target_pairs={{0,1},{1,0},{2,3},{3,2},{4,5},{5,4},{6,7},{7,6},{8,9},{9,8},{10,11... | collective-permute-start | bytes 2359304 | tf_op jit(solution)/shard_map/ppermute | solution.py:38
  34.4 12.4 %copy-start.15 = (bf16[1,1024,2048]{2,1,0:T(8,128)(2,1)S(1)}, bf16[1,1024,2048]{2,1,0:T(8,128)(2,1)}, u32[]{:S(2)}) copy-start(bf16[1,1024,2048]{2,1,0:T(8,128)(2,1)} %param.20) | copy-start | bytes 12582916
  43.2 20.7 %collective-permute-start.15 = (bf16[128,2048]{1,0:T(8,128)(2,1)S(1)}, bf16[128,2048]{1,0:T(8,128)(2,1)S(1)}, u32[]{:S(2)}, u32[]{:S(2)}) collective-permute-start(bf16[128,2048]{1,0:T(8,128)(2,1)S(1)} %constant_dynamic-update-slice_fusion), channel_id=1, source_target_pairs={{0,8},{8,0},{16,24},{24,16},{1,9},{9,1},{17,25},{25,17},{2,10},{10... | collective-permute-start | bytes 1572872 | tf_op jit(solution)/shard_map/ppermute | solution.py:38
  45.2 4.8 %copy-start.14 = (bf16[1,2048,1024]{2,1,0:T(8,128)(2,1)S(1)}, bf16[1,2048,1024]{2,1,0:T(8,128)(2,1)}, u32[]{:S(2)}) copy-start(bf16[1,2048,1024]{2,1,0:T(8,128)(2,1)} %param.19) | copy-start | bytes 12582916
  45.2 23.1 %collective-permute-start.5 = (bf16[256,512]{1,0:T(8,128)(2,1)S(1)}, bf16[256,512]{1,0:T(8,128)(2,1)S(1)}, u32[]{:S(2)}, u32[]{:S(2)}) collective-permute-start(bf16[256,512]{1,0:T(8,128)(2,1)S(1)} %convolution_convert_fusion.2), channel_id=1, source_target_pairs={{0,4},{4,0},{1,5},{5,1},{2,6},{6,2},{3,7},{7,3},{8,12},{12,8},{9,1... | collective-permute-start | bytes 786440 | tf_op jit(solution)/shard_map/ppermute | solution.py:38
  47.9 20.9 %collective-permute-start.16 = (bf16[48,2048]{1,0:T(8,128)(2,1)S(1)}, bf16[48,2048]{1,0:T(8,128)(2,1)S(1)}, u32[]{:S(2)}, u32[]{:S(2)}) collective-permute-start(bf16[48,2048]{1,0:T(8,128)(2,1)S(1)} %get-tuple-element.84), channel_id=1, source_target_pairs={{0,6},{1,7},{2,4},{3,5},{4,2},{5,3},{6,0},{7,1},{8,14},{9,15},{10,... | collective-permute-start | bytes 589832 | tf_op jit(solution)/shard_map/ppermute | solution.py:223
  48.2 8.4 %collective-permute-start.11 = (bf16[48,2048]{1,0:T(8,128)(2,1)S(1)}, bf16[48,2048]{1,0:T(8,128)(2,1)S(1)}, u32[]{:S(2)}, u32[]{:S(2)}) collective-permute-start(bf16[48,2048]{1,0:T(8,128)(2,1)S(1)} %get-tuple-element.86), channel_id=1, source_target_pairs={{0,2},{1,3},{2,0},{3,1},{4,6},{5,7},{6,4},{7,5},{8,10},{9,11},{10,... | collective-permute-start | bytes 589832 | tf_op jit(solution)/shard_map/ppermute | solution.py:223
  51.0 14.1 %copy-start.5 = (bf16[128,2048]{1,0:T(8,128)(2,1)S(1)}, bf16[128,2048]{1,0:T(8,128)(2,1)}, u32[]{:S(2)}) copy-start(bf16[128,2048]{1,0:T(8,128)(2,1)} %refs_0_.3) | copy-start | bytes 1572868
  52.1 16.9 %copy-start.22 = (s32[128,2]{1,0:T(8,128)S(1)}, s32[128,2]{1,0:T(8,128)}, u32[]{:S(2)}) copy-start(s32[128,2]{1,0:T(8,128)} %copy.41) | copy-start | bytes 3076
  52.1 16.9 %copy-start.25 = (f32[128,2]{0,1:T(2,128)S(1)}, f32[128,2]{0,1:T(2,128)}, u32[]{:S(2)}) copy-start(f32[128,2]{0,1:T(2,128)} %param.17) | copy-start | bytes 3076
  56.6 5.7 %collective-permute-start.10 = (bf16[48,2048]{1,0:T(8,128)(2,1)S(1)}, bf16[48,2048]{1,0:T(8,128)(2,1)S(1)}, u32[]{:S(2)}, u32[]{:S(2)}) collective-permute-start(bf16[48,2048]{1,0:T(8,128)(2,1)S(1)} %get-tuple-element.87), channel_id=1, source_target_pairs={{0,4},{1,5},{2,6},{3,7},{4,0},{5,1},{6,2},{7,3},{8,12},{9,13},{10,... | collective-permute-start | bytes 589832 | tf_op jit(solution)/shard_map/ppermute | solution.py:223
  62.3 8.0 %collective-permute-start.20 = (bf16[48,2048]{1,0:T(8,128)(2,1)}, bf16[48,2048]{1,0:T(8,128)(2,1)S(1)}, u32[]{:S(2)}, u32[]{:S(2)}) collective-permute-start(bf16[48,2048]{1,0:T(8,128)(2,1)} %get-tuple-element.80), channel_id=1, source_target_pairs={{0,7},{1,6},{2,5},{3,4},{4,3},{5,2},{6,1},{7,0},{8,15},{9,14},{10,... | collective-permute-start | bytes 589832 | tf_op jit(solution)/shard_map/ppermute | solution.py:223
  62.3 11.1 %collective-permute-start.19 = (bf16[48,2048]{1,0:T(8,128)(2,1)}, bf16[48,2048]{1,0:T(8,128)(2,1)S(1)}, u32[]{:S(2)}, u32[]{:S(2)}) collective-permute-start(bf16[48,2048]{1,0:T(8,128)(2,1)} %get-tuple-element.81), channel_id=1, source_target_pairs={{0,5},{1,4},{2,7},{3,6},{4,1},{5,0},{6,3},{7,2},{8,13},{9,12},{10,... | collective-permute-start | bytes 589832 | tf_op jit(solution)/shard_map/ppermute | solution.py:223
  63.8 9.5 %collective-permute-start.18 = (bf16[48,2048]{1,0:T(8,128)(2,1)}, bf16[48,2048]{1,0:T(8,128)(2,1)S(1)}, u32[]{:S(2)}, u32[]{:S(2)}) collective-permute-start(bf16[48,2048]{1,0:T(8,128)(2,1)} %get-tuple-element.82), channel_id=1, source_target_pairs={{0,3},{1,2},{2,1},{3,0},{4,7},{5,6},{6,5},{7,4},{8,11},{9,10},{10,... | collective-permute-start | bytes 589832 | tf_op jit(solution)/shard_map/ppermute | solution.py:223
  67.4 0.9 copy-start.7
  68.3 5.0 %collective-permute-start.17 = (bf16[48,2048]{1,0:T(8,128)(2,1)}, bf16[48,2048]{1,0:T(8,128)(2,1)S(1)}, u32[]{:S(2)}, u32[]{:S(2)}) collective-permute-start(bf16[48,2048]{1,0:T(8,128)(2,1)} %get-tuple-element.83), channel_id=1, source_target_pairs={{0,1},{1,0},{2,3},{3,2},{4,5},{5,4},{6,7},{7,6},{8,9},{9,8},{10,11... | collective-permute-start | bytes 589832 | tf_op jit(solution)/shard_map/ppermute | solution.py:223
  68.9 16.4 %collective-permute-start.22 = (bf16[192,2048]{1,0:T(8,128)(2,1)}, bf16[192,2048]{1,0:T(8,128)(2,1)}, u32[]{:S(2)}, u32[]{:S(2)}) collective-permute-start(bf16[192,2048]{1,0:T(8,128)(2,1)} %get-tuple-element.53), channel_id=1, source_target_pairs={{0,1},{1,0},{2,3},{3,2},{4,5},{5,4},{6,7},{7,6},{8,9},{9,8},{10,11... | collective-permute-start | bytes 2359304 | tf_op jit(solution)/shard_map/ppermute | solution.py:38
  74.2 8.4 %collective-permute-start.21 = (bf16[2,128,512]{2,1,0:T(8,128)(2,1)S(1)}, bf16[2,128,512]{2,1,0:T(8,128)(2,1)S(1)}, u32[]{:S(2)}, u32[]{:S(2)}) collective-permute-start(bf16[2,128,512]{2,1,0:T(8,128)(2,1)S(1)} %get-tuple-element.58), channel_id=1, source_target_pairs={{0,8},{8,0},{16,24},{24,16},{1,9},{9,1},{17,25},{25,17},{2,10},{10... | collective-permute-start | bytes 786440 | tf_op jit(solution)/shard_map/ppermute | solution.py:38
  74.7 26.3 %collective-permute-start.26 = (bf16[1024,512]{1,0:T(8,128)(2,1)}, bf16[1024,512]{1,0:T(8,128)(2,1)S(1)}, u32[]{:S(2)}, u32[]{:S(2)}) collective-permute-start(bf16[1024,512]{1,0:T(8,128)(2,1)} %bitcast.85), channel_id=1, source_target_pairs={{0,4},{4,0},{1,5},{5,1},{2,6},{6,2},{3,7},{7,3},{8,12},{12,8},{9,1... | collective-permute-start | bytes 3145736 | tf_op jit(solution)/shard_map/ppermute | solution.py:38
  82.6 10.1 %collective-permute-start.23 = (bf16[128,512]{1,0:T(8,128)(2,1)S(1)}, bf16[128,512]{1,0:T(8,128)(2,1)S(1)}, u32[]{:S(2)}, u32[]{:S(2)}) collective-permute-start(bf16[128,512]{1,0:T(8,128)(2,1)S(1)} %fusion.49), channel_id=1, source_target_pairs={{0,16},{8,24},{16,0},{24,8},{1,17},{9,25},{17,1},{25,9},{2,18},{10... | collective-permute-start | bytes 393224 | tf_op jit(solution)/shard_map/ppermute | solution.py:38
  85.3 7.5 %copy-start.16 = (bf16[1,1024,512]{2,1,0:T(8,128)(2,1)S(1)}, bf16[1,1024,512]{2,1,0:T(8,128)(2,1)}, u32[]{:S(2)}) copy-start(bf16[1,1024,512]{2,1,0:T(8,128)(2,1)} %param.28) | copy-start | bytes 3145732
  92.7 29.6 %copy-start.2 = (bf16[128,2048]{1,0:T(8,128)(2,1)S(1)}, bf16[128,2048]{1,0:T(8,128)(2,1)}, u32[]{:S(2)}) copy-start(bf16[128,2048]{1,0:T(8,128)(2,1)} %tokens_ref) | copy-start | bytes 1572868
  92.7 29.6 %copy-start.11 = (f32[2048]{0:T(1024)S(1)}, f32[2048]{0:T(1024)}, u32[]{:S(2)}) copy-start(f32[2048]{0:T(1024)} %param.21) | copy-start | bytes 24580
  92.7 31.9 %copy-start.6 = (bf16[1,512,1024]{2,1,0:T(8,128)(2,1)S(1)}, bf16[1,512,1024]{2,1,0:T(8,128)(2,1)}, u32[]{:S(2)}) copy-start(bf16[1,512,1024]{2,1,0:T(8,128)(2,1)} %param.29) | copy-start | bytes 3145732
  92.7 33.6 %copy-start.24 = (bf16[256,512]{1,0:T(8,128)(2,1)S(1)}, bf16[256,512]{1,0:T(8,128)(2,1)}, u32[]{:S(2)}) copy-start(bf16[256,512]{1,0:T(8,128)(2,1)} %copy-done.23) | copy-start | bytes 786436
  92.8 29.5 %collective-permute-start.24 = (bf16[1024,512]{1,0:T(8,128)(2,1)S(1)}, bf16[1024,512]{1,0:T(8,128)(2,1)S(1)}, u32[]{:S(2)}, u32[]{:S(2)}) collective-permute-start(bf16[1024,512]{1,0:T(8,128)(2,1)S(1)} %bitcast.90), channel_id=1, source_target_pairs={{0,4},{4,0},{1,5},{5,1},{2,6},{6,2},{3,7},{7,3},{8,12},{12,8},{9,1... | collective-permute-start | bytes 3145736 | tf_op jit(solution)/shard_map/ppermute | solution.py:38
  93.7 5.0 %collective-permute-start.25 = (bf16[128,512]{1,0:T(8,128)(2,1)S(1)}, bf16[128,512]{1,0:T(8,128)(2,1)S(1)}, u32[]{:S(2)}, u32[]{:S(2)}) collective-permute-start(bf16[128,512]{1,0:T(8,128)(2,1)S(1)} %fusion.48.refs_0_), channel_id=1, source_target_pairs={{0,8},{8,0},{16,24},{24,16},{1,9},{9,1},{17,25},{25,17},{2,10},{10... | collective-permute-start | bytes 393224 | tf_op jit(solution)/shard_map/ppermute | solution.py:38
  101.0 23.7 %copy-start.17 = (bf16[1024,512]{1,0:T(8,128)(2,1)}, bf16[1024,512]{1,0:T(8,128)(2,1)S(1)}, u32[]{:S(2)}) copy-start(bf16[1024,512]{1,0:T(8,128)(2,1)S(1)} %collective-permute-done.26.refs_3_) | copy-start | bytes 3145732
  101.0 12.7 %collective-permute-start.27 = (bf16[2,128,512]{2,1,0:T(8,128)(2,1)S(1)}, bf16[2,128,512]{2,1,0:T(8,128)(2,1)S(1)}, u32[]{:S(2)}, u32[]{:S(2)}) collective-permute-start(bf16[2,128,512]{2,1,0:T(8,128)(2,1)S(1)} %pad_maximum_fusion), channel_id=1, source_target_pairs={{0,16},{8,24},{16,0},{24,8},{1,17},{9,25},{17,1},{25,9},{2,18},{10... | collective-permute-start | bytes 786440 | tf_op jit(solution)/shard_map/ppermute | solution.py:38
  109.4 27.9 %collective-permute-start.33 = (bf16[2,384,512]{2,1,0:T(8,128)(2,1)}, bf16[2,384,512]{2,1,0:T(8,128)(2,1)}, u32[]{:S(2)}, u32[]{:S(2)}) collective-permute-start(bf16[2,384,512]{2,1,0:T(8,128)(2,1)} %get-tuple-element.73), channel_id=1, source_target_pairs={{0,8},{8,0},{16,24},{24,16},{1,9},{9,1},{17,25},{25,17},{2,10},{10... | collective-permute-start | bytes 2359304 | tf_op jit(solution)/shard_map/ppermute | solution.py:38
  122.3 2.3 %copy-start.18 = (bf16[1024,512]{1,0:T(8,128)(2,1)}, bf16[1024,512]{1,0:T(8,128)(2,1)S(1)}, u32[]{:S(2)}) copy-start(bf16[1024,512]{1,0:T(8,128)(2,1)S(1)} %collective-permute-done.24.refs_5_) | copy-start | bytes 3145732
  122.7 4.7 %copy-start.3 = (bf16[128,2048]{1,0:T(8,128)(2,1)}, bf16[128,2048]{1,0:T(8,128)(2,1)S(1)}, u32[]{:S(2)}) copy-start(bf16[128,2048]{1,0:T(8,128)(2,1)S(1)} %memory.1.refs_0_) | copy-start | bytes 1572868
  122.7 4.7 %collective-permute-start.28 = (bf16[128,2048]{1,0:T(8,128)(2,1)S(1)}, bf16[128,2048]{1,0:T(8,128)(2,1)}, u32[]{:S(2)}, u32[]{:S(2)}) collective-permute-start(bf16[128,2048]{1,0:T(8,128)(2,1)S(1)} %memory.1.refs_0_), channel_id=1, source_target_pairs={{0,1},{1,0},{2,3},{3,2},{4,5},{5,4},{6,7},{7,6},{8,9},{9,8},{10,11... | collective-permute-start | bytes 1572872 | tf_op jit(solution)/shard_map/ppermute | solution.py:38
  122.8 14.4 %collective-permute-start.29 = (bf16[128,2048]{1,0:T(8,128)(2,1)S(1)}, bf16[128,2048]{1,0:T(8,128)(2,1)}, u32[]{:S(2)}, u32[]{:S(2)}) collective-permute-start(bf16[128,2048]{1,0:T(8,128)(2,1)S(1)} %memory.1.refs_0_), channel_id=1, source_target_pairs={{0,2},{1,3},{2,0},{3,1},{4,6},{5,7},{6,4},{7,5},{8,10},{9,11},{10,... | collective-permute-start | bytes 1572872 | tf_op jit(solution)/shard_map/ppermute | solution.py:38
  124.6 25.4 %collective-permute-start.31 = (bf16[512,1024]{1,0:T(8,128)(2,1)S(1)}, bf16[512,1024]{1,0:T(8,128)(2,1)}, u32[]{:S(2)}, u32[]{:S(2)}) collective-permute-start(bf16[512,1024]{1,0:T(8,128)(2,1)S(1)} %bitcast.79), channel_id=1, source_target_pairs={{0,4},{4,0},{1,5},{5,1},{2,6},{6,2},{3,7},{7,3},{8,12},{12,8},{9,1... | collective-permute-start | bytes 3145736 | tf_op jit(solution)/shard_map/ppermute | solution.py:38
  126.3 11.0 %copy-start.19 = (f32[384,512]{1,0:T(8,128)S(1)}, f32[384,512]{1,0:T(8,128)}, u32[]{:S(2)}) copy-start(f32[384,512]{1,0:T(8,128)} %get-tuple-element.72) | copy-start | bytes 2359300
  132.9 17.1 %copy-start.8 = (bf16[128,512]{1,0:T(8,128)(2,1)S(1)}, bf16[128,512]{1,0:T(8,128)(2,1)}, u32[]{:S(2)}) copy-start(bf16[128,512]{1,0:T(8,128)(2,1)} %attend_sentence.2.mine_ref) | copy-start | bytes 393220
  132.9 17.1 %copy-start.12 = (s32[3]{0:T(128)S(1)}, s32[3]{0:T(128)}, u32[]{:S(2)}) copy-start(s32[3]{0:T(128)} %pad_add_fusion.1.place_ref) | copy-start | bytes 40
  137.3 4.4 %collective-permute-start.30 = (bf16[128,2048]{1,0:T(8,128)(2,1)}, bf16[128,2048]{1,0:T(8,128)(2,1)S(1)}, u32[]{:S(2)}, u32[]{:S(2)}) collective-permute-start(bf16[128,2048]{1,0:T(8,128)(2,1)} %collective-permute-done.29.refs_0_), channel_id=1, source_target_pairs={{0,1},{1,0},{2,3},{3,2},{4,5},{5,4},{6,7},{7,6},{8,9},{9,8},{10,11... | collective-permute-start | bytes 1572872 | tf_op jit(solution)/shard_map/ppermute | solution.py:38
  138.4 20.9 %collective-permute-start.34 = (bf16[384,512]{1,0:T(8,128)(2,1)S(1)}, bf16[384,512]{1,0:T(8,128)(2,1)S(1)}, u32[]{:S(2)}, u32[]{:S(2)}) collective-permute-start(bf16[384,512]{1,0:T(8,128)(2,1)S(1)} %fusion.34), channel_id=1, source_target_pairs={{0,16},{8,24},{16,0},{24,8},{1,17},{9,25},{17,1},{25,9},{2,18},{10... | collective-permute-start | bytes 1179656 | tf_op jit(solution)/shard_map/ppermute | solution.py:38
  141.7 0.8 copy-start.21
  142.5 18.7 %copy-start.20 = (f32[384,512]{1,0:T(8,128)S(1)}, f32[384,512]{1,0:T(8,128)}, u32[]{:S(2)}) copy-start(f32[384,512]{1,0:T(8,128)} %get-tuple-element.76) | copy-start | bytes 2359300
  150.0 0.9 copy-start.9
  150.9 15.7 %copy-start.27 = (s32[2]{0:T(128)S(1)}, s32[2]{0:T(128)}, u32[]{:S(2)}) copy-start(s32[2]{0:T(128)} %param.24) | copy-start | bytes 28
  152.9 6.4 %collective-permute-start.35 = (bf16[256,512]{1,0:T(8,128)(2,1)S(1)}, bf16[256,512]{1,0:T(8,128)(2,1)S(1)}, u32[]{:S(2)}, u32[]{:S(2)}) collective-permute-start(bf16[256,512]{1,0:T(8,128)(2,1)S(1)} %get-tuple-element.75), channel_id=1, source_target_pairs={{0,1},{1,0},{2,3},{3,2},{4,5},{5,4},{6,7},{7,6},{8,9},{9,8},{10,11... | collective-permute-start | bytes 786440 | tf_op jit(solution)/shard_map/ppermute | solution.py:38
  153.0 13.8 %collective-permute-start.32 = (bf16[256,512]{1,0:T(8,128)(2,1)S(1)}, bf16[256,512]{1,0:T(8,128)(2,1)S(1)}, u32[]{:S(2)}, u32[]{:S(2)}) collective-permute-start(bf16[256,512]{1,0:T(8,128)(2,1)S(1)} %get-tuple-element.69), channel_id=1, source_target_pairs={{0,1},{1,0},{2,3},{3,2},{4,5},{5,4},{6,7},{7,6},{8,9},{9,8},{10,11... | collective-permute-start | bytes 786440 | tf_op jit(solution)/shard_map/ppermute | solution.py:38
  159.4 8.0 %collective-permute-start.36 = (bf16[256,512]{1,0:T(8,128)(2,1)S(1)}, bf16[256,512]{1,0:T(8,128)(2,1)S(1)}, u32[]{:S(2)}, u32[]{:S(2)}) collective-permute-start(bf16[256,512]{1,0:T(8,128)(2,1)S(1)} %convert_add_fusion.3), channel_id=1, source_target_pairs={{0,2},{1,3},{2,0},{3,1},{4,6},{5,7},{6,4},{7,5},{8,10},{9,11},{10,... | collective-permute-start | bytes 786440 | tf_op jit(solution)/shard_map/ppermute | solution.py:38
  163.2 11.7 %all-to-all-start = ((bf16[8,48,512]{2,1,0:T(8,128)(2,1)}), bf16[8,48,512]{2,1,0:T(8,128)(2,1)S(1)}, u32[]{:S(2)}, u32[]{:S(2)}) async-start(bf16[8,48,512]{2,1,0:T(8,128)(2,1)} %bitcast.31), calls=%async_computation | async-start | bytes 786432 | tf_op jit(solution)/shard_map/all_to_all | solution.py:142
  (2 other events, 1.4 us)

commit v10 on v9

--- a/solution.py
+++ b/solution.py
@@ -586,10 +586,9 @@
     query_there = jnp.dot(asked_here, query_own, preferred_element_type=jnp.float32)
     query_back = swap(query_there.astype(jnp.bfloat16), "expert", 1)
     other_y = swap(half_y, "section", 1)
+    grad_y = jnp.concatenate([half_y, other_y], axis=0)
     half_x = swap(gate(grad_half, token_far), "dp", 2)
-    half_far = swap(gate(half_y, token_far), "dp", 2)
-    half_pair = jnp.concatenate([half_x, half_far], axis=0)
-    other_pair = swap(half_pair, "section", 1)
+    other_x = swap(half_x, "section", 1)
 
     row = lax.broadcasted_iota(jnp.int32, (token_count, token_count), 0)
     column = lax.broadcasted_iota(jnp.int32, (token_count, token_count), 1)
@@ -611,9 +610,9 @@
     codes_of = expert_ids ^ here
     position = ((codes_of >> 1) + 4 * (codes_of & 1)) * capacity + rank
 
-    def forward(rows, after):
+    def forward(rows, *after):
         pre_act = jnp.dot(rows, weight_in, preferred_element_type=jnp.float32)
-        hidden = jax.nn.gelu(gate(pre_act, after)).astype(jnp.bfloat16)
+        hidden = jax.nn.gelu(gate(pre_act, *after)).astype(jnp.bfloat16)
         part = jnp.dot(hidden, weight_out, preferred_element_type=jnp.float32)
         return pre_act, part.astype(jnp.bfloat16)
 
@@ -628,31 +627,37 @@
         capacity,
     )
     rows_core = swap(rows_sent, "dp", 1)
-    pre_own, part_own = forward(rows_own, rows_core)
-    pre_core, part_core = forward(gate(rows_core, asked_here), half_pair)
+    pre_own, part_own = forward(rows_own, rows_core, half_x)
+    pre_core, part_core = forward(rows_core, asked_here)
     home = send_home(part_own, near_codes, capacity) + send_home(part_core, core_codes, capacity)
 
     rise_own, rise_core = slope_of(gate(pre_own, home[1])), slope_of(gate(pre_core, home[1]))
+    held_gates = gate(gate_weights, rise_own, rise_core, query_back, other_x, other_y)
+    sent_pair, first, second = combine(which_section, position, held_gates, home, sections)
+    from_pair = swap(sent_pair, "section", 1)
+    grad_far = swap(gate(grad_y, first), "dp", 2)
     grads_own, grads_sent = dispatch(
         which_section,
-        gate(code, home[2], rise_own, rise_core),
-        [out_grad, half_x, half_y, half_far, other_y, other_pair],
+        code,
+        [out_grad, half_x, other_x, grad_y, grad_far],
         (
             ((0, 0, token_count, None),),
-            ((1, 0, share, 0), (5, 0, share, 1)),
-            ((2, 0, share, 0), (4, 0, share, 1)),
-            ((3, 0, share, 0), (5, share, share, 1)),
+            ((1, 0, share, 0), (2, 0, share, 1)),
+            ((3, 0, share, 0), (3, share, share, 1)),
+            ((4, 0, share, 0), (4, share, share, 1)),
         ),
         capacity,
     )
-    held_gates = gate(gate_weights, grads_sent, query_back)
-    sent_pair, first, second = combine(which_section, position, held_gates, home, sections)
-    from_pair = swap(sent_pair, "section", 1)
+    grads_core = swap(grads_sent, "dp", 1)
     grads_core = swap(grads_sent, "dp", 1)
     to_other = (second + from_pair[1].astype(jnp.float32)).astype(jnp.bfloat16)
     from_other = swap(to_other, "section", 2)
+    mixed_sum = gate(first, grads_sent) + from_pair[0].astype(jnp.float32)
+    mixed_slice = (mixed_sum + from_other.astype(jnp.float32)).astype(jnp.bfloat16)
+    key_other = swap(gate(key_own, first), "expert", 1)
+    mixed_near = swap(mixed_slice, "section", 1)
     slope = expert_slope(
-        gate(here.astype(jnp.int32).reshape(1), to_other),
+        gate(here.astype(jnp.int32).reshape(1), mixed_near),
         near_codes + core_codes,
         grads_own,
         grads_core,
@@ -660,12 +665,8 @@
         rise_core,
         weight_out,
     )
-    mixed_sum = gate(first, slope) + from_pair[0].astype(jnp.float32)
-    mixed_slice = (mixed_sum + from_other.astype(jnp.float32)).astype(jnp.bfloat16)
-    key_other = swap(gate(key_own, first), "expert", 1)
-    mixed_near = swap(mixed_slice, "section", 1)
     back_pair, back_first, back_second = expert_backward(
-        gate(which_section, mixed_near), slope, weight_in, sections
+        which_section, slope, weight_in, sections
     )
     mixed_far = swap(jnp.stack([mixed_slice, gate(mixed_near, key_other)]), "section", 2)
     slices = [mixed_slice, mixed_near, mixed_far[0], mixed_far[1]]
@@ -675,7 +676,7 @@
     query_here = jnp.dot(normed_own, query_own, preferred_element_type=jnp.float32)
     query = (query_here + query_back.astype(jnp.float32)).astype(jnp.bfloat16)
 
-    memory = make_memory(which_section, gate(tokens, value_other), slices, final_gain)
+    memory = make_memory(which_section, tokens, slices, final_gain)
     out_other = swap(gate(out_own, memory), "expert", 1)
     memory_x = swap(memory, "dp", 2)
     memory_core = swap(memory, "dp", 1)

time: 177 us -> 172 us (0.972)
  starting transfers between devices: 45.7 us -> 39 us
  local copies, waits for them, and re-layouts: 11.8 us -> 15.9 us
    ppermute x30, starting transfers between devices: 35.4 us -> 26.3 us  [swap(): return lax.ppermute(value, axis, [(i, i ^ mask) for i in range(size)])]
    unnamed x59 -> x63, local copies, waits for them, and re-layouts: 7.41 us -> 11.2 us
    ppermute x7, starting transfers between devices: 6.88 us -> 9.31 us  [send_home(): lax.ppermute(block, ('expert', 'dp'), [(i, i ^ code) for i in range(size)])]
  transfers between devices with their start and end apart: 38 -> 38, of which waited for: 18 -> 19; matrix products, arithmetic and copies ran while one was open for 14% -> 15% of each run, Pallas kernels for 18% -> 17%
where the time goes in v10:
time: 172 us
  waiting for transfers between devices  63.8 us (37%)
  starting transfers between devices  39 us (23%)
  Pallas kernels  33 us (19%)
  local copies, waits for them, and re-layouts  15.9 us (9%)
  other arithmetic  11.1 us (6%)
  matrix products  7.53 us (4%)
    ppermute x30, waiting for transfers between devices, swap(): return lax.ppermute(value, axis, [(i, i ^ mask) for i in range(size)])  50.1 us
    ppermute x30, starting transfers between devices, swap(): return lax.ppermute(value, axis, [(i, i ^ mask) for i in range(size)])  26.3 us
    unnamed x63, local copies, waits for them, and re-layouts  11.2 us
    pallas_call x2, Pallas kernels, attend_sentence(): pl.pallas_call(attend_kernel, out_shape=jax.ShapeDtypeStruct(query.shape,...  10.9 us
    ppermute x7, starting transfers between devices, send_home(): lax.ppermute(block, ('expert', 'dp'), [(i, i ^ code) for i in range(size)])  9.31 us
    ppermute x7, waiting for transfers between devices, send_home(): lax.ppermute(block, ('expert', 'dp'), [(i, i ^ code) for i in range(size)])  7.74 us
    pallas_call x1, Pallas kernels, expert_slope(): pl.pallas_call(functools.partial(slope_kernel, codes), out_shape=jax.Shap...  7.35 us
    all_to_all x1, waiting for transfers between devices, exchange(): lax.all_to_all(sent, ('expert', 'dp'), split_axis=0, concat_axis=0, tiled...  5.96 us
  transfers between devices with their start and end apart: 38, of which 19 were waited for; matrix products, arithmetic and copies ran while one was open for 15% of the time, Pallas kernels for 17%

profile of v10, /device:TPU:0, one launch (start us, length us, event | category | flops | bytes accessed | tf_op | source)
XLA Modules:
  0.0 171.5 jit_solution(16735860075596735519)
XLA Ops:
  0.6 3.0 %collective-permute-start.1 = (s32[2,128]{1,0:T(2,128)}, s32[2,128]{1,0:T(2,128)S(1)}, u32[]{:S(2)}, u32[]{:S(2)}) collective-permute-start(s32[2,128]{1,0:T(2,128)} %bitcast.88), channel_id=1, source_target_pairs={{0,2},{1,3},{2,0},{3,1},{4,6},{5,7},{6,4},{7,5},{8,10},{9,11},{10,... | collective-permute-start | bytes 3080 | tf_op jit(solution)/shard_map/ppermute | solution.py:38
  3.6 1.5 collective-permute-start.6
  6.6 1.0 constant_dynamic-slice_fusion.2
  7.6 10.9 %collective-permute-done.refs_2_ = bf16[128,2048]{1,0:T(8,128)(2,1)S(1)} collective-permute-done((bf16[128,2048]{1,0:T(8,128)(2,1)}, bf16[128,2048]{1,0:T(8,128)(2,1)S(1)}, u32[]{:S(2)}, u32[]{:S(2)}) %collective-permute-start) | collective-permute-done | bytes 524320 | tf_op jit(solution)/shard_map/ppermute | solution.py:38
  20.7 0.8 copy.36
  21.8 1.5 collective-permute-done.2
  23.7 1.2 copy-done.4
  25.6 0.8 normed.1
  26.3 0.8 copy-done.17
  28.0 2.8 %collective-permute-done.3 = bf16[64,2048]{1,0:T(8,128)(2,1)} collective-permute-done((bf16[64,2048]{1,0:T(8,128)(2,1)S(1)}, bf16[64,2048]{1,0:T(8,128)(2,1)}, u32[]{:S(2)}, u32[]{:S(2)}) %collective-permute-start.3) | collective-permute-done | bytes 262176 | tf_op jit(solution)/shard_map/ppermute | solution.py:38
  30.8 1.6 collective-permute-start.13
  32.4 1.0 copy-done.1
  33.4 1.3 dispatch.2
  34.8 1.1 constant_dynamic-update-slice_fusion.1
  35.9 1.6 collective-permute-start.10
  37.5 3.2 %fusion.60 = f32[192,1024]{1,0:T(8,128)S(1)} fusion(bf16[192,2048]{1,0:T(8,128)(2,1)S(1)} %get-tuple-element.40, bf16[1,2048,1024]{2,1,0:T(8,128)(2,1)} %param.19), kind=kOutput, calls=%fused_computation.101 | convolution fusion | flops 805306368 | bytes 5767168 | tf_op jit(solution)/shard_map/dot_general | solution.py:614
  41.3 1.9 %collective-permute-start.5 = (bf16[256,512]{1,0:T(8,128)(2,1)S(1)}, bf16[256,512]{1,0:T(8,128)(2,1)S(1)}, u32[]{:S(2)}, u32[]{:S(2)}) collective-permute-start(bf16[256,512]{1,0:T(8,128)(2,1)S(1)} %convolution_convert_fusion.2), channel_id=1, source_target_pairs={{0,4},{4,0},{1,5},{5,1},{2,6},{6,2},{3,7},{7,3},{8,12},{12,8},{9,1... | collective-permute-start | bytes 786440 | tf_op jit(solution)/shard_map/ppermute | solution.py:38
  43.3 1.3 collective-permute-done.10.refs_1_
  45.0 1.1 convolution_convert_fusion.1
  46.8 1.5 collective-permute-start.11
  48.3 2.0 %collective-permute-start.14 = (bf16[48,2048]{1,0:T(8,128)(2,1)S(1)}, bf16[48,2048]{1,0:T(8,128)(2,1)S(1)}, u32[]{:S(2)}, u32[]{:S(2)}) collective-permute-start(bf16[48,2048]{1,0:T(8,128)(2,1)S(1)} %get-tuple-element.77), channel_id=1, source_target_pairs={{0,4},{1,5},{2,6},{3,7},{4,0},{5,1},{6,2},{7,3},{8,12},{9,13},{10,... | collective-permute-start | bytes 589832 | tf_op jit(solution)/shard_map/ppermute | solution.py:223
  50.4 1.0 fusion.58
  51.4 1.1 convolution_convert_fusion
  52.5 0.9 fusion.71
  53.4 2.5 %collective-permute-start.15 = (bf16[48,2048]{1,0:T(8,128)(2,1)}, bf16[48,2048]{1,0:T(8,128)(2,1)}, u32[]{:S(2)}, u32[]{:S(2)}) collective-permute-start(bf16[48,2048]{1,0:T(8,128)(2,1)} %get-tuple-element.76), channel_id=1, source_target_pairs={{0,6},{1,7},{2,4},{3,5},{4,2},{5,3},{6,0},{7,1},{8,14},{9,15},{10,... | collective-permute-start | bytes 589832 | tf_op jit(solution)/shard_map/ppermute | solution.py:223
  56.7 2.5 %collective-permute-start.19 = (bf16[48,2048]{1,0:T(8,128)(2,1)}, bf16[48,2048]{1,0:T(8,128)(2,1)}, u32[]{:S(2)}, u32[]{:S(2)}) collective-permute-start(bf16[48,2048]{1,0:T(8,128)(2,1)} %get-tuple-element.72), channel_id=1, source_target_pairs={{0,7},{1,6},{2,5},{3,4},{4,3},{5,2},{6,1},{7,0},{8,15},{9,14},{10,... | collective-permute-start | bytes 589832 | tf_op jit(solution)/shard_map/ppermute | solution.py:223
  59.2 2.1 %fusion.9 = (f32[192,1024]{1,0:T(8,128)}, f32[192,1024]{1,0:T(8,128)}) fusion(f32[192,1024]{1,0:T(8,128)S(1)} %fusion.60, f32[192,1024]{1,0:T(8,128)S(1)} %fusion.58), kind=kLoop, calls=%fused_computation.20 | loop fusion | flops 6684672 | bytes 3145728 | tf_op jit(solution)/shard_map/transpose(jvp())/add_any | solution.py:620
  61.9 3.7 %collective-permute-done.17.refs_5_ = bf16[48,2048]{1,0:T(8,128)(2,1)} collective-permute-done((bf16[48,2048]{1,0:T(8,128)(2,1)}, bf16[48,2048]{1,0:T(8,128)(2,1)}, u32[]{:S(2)}, u32[]{:S(2)}) %collective-permute-start.17) | collective-permute-done | bytes 196640 | tf_op jit(solution)/shard_map/ppermute | solution.py:223
  65.6 3.5 %collective-permute-done.18.refs_6_ = bf16[48,2048]{1,0:T(8,128)(2,1)} collective-permute-done((bf16[48,2048]{1,0:T(8,128)(2,1)}, bf16[48,2048]{1,0:T(8,128)(2,1)}, u32[]{:S(2)}, u32[]{:S(2)}) %collective-permute-start.18) | collective-permute-done | bytes 196640 | tf_op jit(solution)/shard_map/ppermute | solution.py:223
  69.2 0.9 copy-done.11
  70.1 0.9 copy-done.13
  71.0 2.1 %combine.2 = (bf16[2,128,512]{2,1,0:T(8,128)(2,1)S(1)}, f32[128,512]{1,0:T(8,128)S(1)}, f32[128,512]{1,0:T(8,128)S(1)}) custom-call(s32[1]{0:T(128)} %bitcast.8.section_ref, s32[128,2]{1,0:T(8,128)S(1)} %get-tuple-element.85.position_ref, f32[128,2]{1,0:T(8,128)S(1)} %copy.39.gates_ref, bf16[48,2048]{1,0:T(8,128)(2,1)S(1)} %get-tuple-element.78.refs_0_, ...), custom_call_target="tpu_custom_call" | custom-call | flops 1 | bytes 1 | tf_op jit(solution)/shard_map/combine/pallas_call | solution.py:264
  73.1 1.6 collective-permute-start.21
  74.8 1.0 constant_dynamic-update-slice_fusion.refs_3_
  75.7 1.3 collective-permute-start.20
  77.1 4.5 %collective-permute-done.21 = bf16[2,128,512]{2,1,0:T(8,128)(2,1)S(1)} collective-permute-done((bf16[2,128,512]{2,1,0:T(8,128)(2,1)S(1)}, bf16[2,128,512]{2,1,0:T(8,128)(2,1)S(1)}, u32[]{:S(2)}, u32[]{:S(2)}) %collective-permute-start.21) | collective-permute-done | bytes 262176 | tf_op jit(solution)/shard_map/ppermute | solution.py:38
  81.6 2.7 %collective-permute-start.22 = (bf16[128,512]{1,0:T(8,128)(2,1)S(1)}, bf16[128,512]{1,0:T(8,128)(2,1)S(1)}, u32[]{:S(2)}, u32[]{:S(2)}) collective-permute-start(bf16[128,512]{1,0:T(8,128)(2,1)S(1)} %fusion.47), channel_id=1, source_target_pairs={{0,16},{8,24},{16,0},{24,8},{1,17},{9,25},{17,1},{25,9},{2,18},{10... | collective-permute-start | bytes 393224 | tf_op jit(solution)/shard_map/ppermute | solution.py:38
  84.2 5.8 %collective-permute-done.20.refs_4_ = bf16[128,2048]{1,0:T(8,128)(2,1)S(1)} collective-permute-done((bf16[128,2048]{1,0:T(8,128)(2,1)S(1)}, bf16[128,2048]{1,0:T(8,128)(2,1)S(1)}, u32[]{:S(2)}, u32[]{:S(2)}) %collective-permute-start.20) | collective-permute-done | bytes 524320 | tf_op jit(solution)/shard_map/ppermute | solution.py:38
  90.0 1.5 dispatch.3
  91.4 0.9 copy-done.7
  92.9 1.3 collective-permute-start.27
  94.2 4.2 %collective-permute-done.23.refs_1_ = bf16[128,512]{1,0:T(8,128)(2,1)S(1)} collective-permute-done((bf16[128,512]{1,0:T(8,128)(2,1)S(1)}, bf16[128,512]{1,0:T(8,128)(2,1)S(1)}, u32[]{:S(2)}, u32[]{:S(2)}) %collective-permute-start.23) | collective-permute-done | bytes 131104 | tf_op jit(solution)/shard_map/ppermute | solution.py:38
  98.4 2.7 %collective-permute-done.24.refs_3_ = bf16[1024,512]{1,0:T(8,128)(2,1)S(1)} collective-permute-done((bf16[1024,512]{1,0:T(8,128)(2,1)}, bf16[1024,512]{1,0:T(8,128)(2,1)S(1)}, u32[]{:S(2)}, u32[]{:S(2)}) %collective-permute-start.24) | collective-permute-done | bytes 1048608 | tf_op jit(solution)/shard_map/ppermute | solution.py:38
  101.1 2.7 %collective-permute-start.25 = (bf16[2,128,512]{2,1,0:T(8,128)(2,1)S(1)}, bf16[2,128,512]{2,1,0:T(8,128)(2,1)S(1)}, u32[]{:S(2)}, u32[]{:S(2)}) collective-permute-start(bf16[2,128,512]{2,1,0:T(8,128)(2,1)S(1)} %pad_maximum_fusion), channel_id=1, source_target_pairs={{0,16},{8,24},{16,0},{24,8},{1,17},{9,25},{17,1},{25,9},{2,18},{10... | collective-permute-start | bytes 786440 | tf_op jit(solution)/shard_map/ppermute | solution.py:38
  103.7 0.9 copy-done.21
  104.6 7.3 %expert_slope.1.slope_ref = bf16[384,1024]{1,0:T(8,128)(2,1)} custom-call(s32[1]{0:T(128)} %bitcast.27.here_ref, bf16[192,2048]{1,0:T(8,128)(2,1)} %copy-done.7, bf16[192,2048]{1,0:T(8,128)(2,1)} %copy-done.21, f32[192,1024]{1,0:T(8,128)} %get-tuple-element.86.rise_own, f32[192,1024]{1,0:T(8,128)} %get-tuple-element.87.rise_core, bf16[1024,2048]{1,0:T(8,128)(2,1)} %bitcast.84), custom_call_target="tpu_custom_call" | custom-call | flops 1 | bytes 1 | tf_op jit(solution)/shard_map/expert_slope/pallas_call | solution.py:478
  112.0 5.8 %expert_backward.1 = (bf16[2,384,512]{2,1,0:T(8,128)(2,1)}, f32[384,512]{1,0:T(8,128)}, f32[384,512]{1,0:T(8,128)}) custom-call(s32[1]{0:T(128)} %bitcast.8.section_ref, bf16[384,1024]{1,0:T(8,128)(2,1)} %expert_slope.1.slope_ref, bf16[2048,1024]{1,0:T(8,128)(2,1)} %bitcast.83), custom_call_target="tpu_custom_call" | custom-call | flops 1 | bytes 1 | tf_op jit(solution)/shard_map/expert_backward/pallas_call | solution.py:520
  119.0 1.3 collective-permute-start.28
  122.5 5.4 %attend_sentence.2.mine_ref = bf16[128,512]{1,0:T(8,128)(2,1)} custom-call(s32[3]{0:T(128)} %pad_add_fusion.1.place_ref, s32[2]{0:T(128)} %lengths_ref.3, bf16[128,512]{1,0:T(8,128)(2,1)} %get-tuple-element.81.query_ref, bf16[128,2048]{1,0:T(8,128)(2,1)} %copy-done.3, bf16[128,2048]{1,0:T(8,128)(2,1)} %collective-permute-done.26.refs_1_, ...), custom_call_target="tpu_custom_call" | custom-call | flops 1 | bytes 1 | tf_op jit(solution)/shard_map/attend_sentence/pallas_call | solution.py:380
  127.9 5.5 %collective-permute-done.28.refs_0_ = bf16[128,2048]{1,0:T(8,128)(2,1)} collective-permute-done((bf16[128,2048]{1,0:T(8,128)(2,1)S(1)}, bf16[128,2048]{1,0:T(8,128)(2,1)}, u32[]{:S(2)}, u32[]{:S(2)}) %collective-permute-start.28) | collective-permute-done | bytes 524320 | tf_op jit(solution)/shard_map/ppermute | solution.py:38
  133.4 1.8 %collective-permute-done.33 = bf16[2,384,512]{2,1,0:T(8,128)(2,1)} collective-permute-done((bf16[2,384,512]{2,1,0:T(8,128)(2,1)}, bf16[2,384,512]{2,1,0:T(8,128)(2,1)}, u32[]{:S(2)}, u32[]{:S(2)}) %collective-permute-start.33) | collective-permute-done | bytes 786464 | tf_op jit(solution)/shard_map/ppermute | solution.py:38
  135.2 1.1 fusion.34
  137.6 0.8 copy-done.24
  138.3 5.5 %attend_sentence.3.done_ref = bf16[128,512]{1,0:T(8,128)(2,1)} custom-call(s32[3]{0:T(128)} %pad_add_fusion.3.place_ref, s32[2]{0:T(128)} %lengths_ref.3, bf16[128,512]{1,0:T(8,128)(2,1)} %get-tuple-element.80.query_ref, bf16[128,2048]{1,0:T(8,128)(2,1)} %collective-permute-done.28.refs_0_, bf16[128,2048]{1,0:T(8,128)(2,1)} %copy-done.24, ...), custom_call_target="tpu_custom_call" | custom-call | flops 1 | bytes 1 | tf_op jit(solution)/shard_map/attend_sentence/pallas_call | solution.py:380
  143.8 1.8 %collective-permute-done.30.other_ref = bf16[512,1024]{1,0:T(8,128)(2,1)} collective-permute-done((bf16[512,1024]{1,0:T(8,128)(2,1)S(1)}, bf16[512,1024]{1,0:T(8,128)(2,1)}, u32[]{:S(2)}, u32[]{:S(2)}) %collective-permute-start.30) | collective-permute-done | bytes 1048608 | tf_op jit(solution)/shard_map/ppermute | solution.py:38
  145.6 0.9 copy-done.9
  146.5 2.0 %project.1 = (bf16[256,512]{1,0:T(8,128)(2,1)S(1)}, bf16[256,512]{1,0:T(8,128)(2,1)S(1)}, f32[256,512]{1,0:T(8,128)S(1)}, f32[256,512]{1,0:T(8,128)S(1)}) custom-call(s32[3]{0:T(128)S(1)} %copy-done.16, bf16[128,512]{1,0:T(8,128)(2,1)S(1)} %copy-done.8, bf16[128,512]{1,0:T(8,128)(2,1)S(1)} %copy-done.9, bf16[512,1024]{1,0:T(8,128)(2,1)S(1)} %bitcast.80, ...), custom_call_target="tpu_custom_call" | custom-call | flops 1 | bytes 1 | tf_op jit(solution)/shard_map/project/pallas_call | solution.py:431
  149.1 6.4 %collective-permute-done.34 = bf16[384,512]{1,0:T(8,128)(2,1)S(1)} collective-permute-done((bf16[384,512]{1,0:T(8,128)(2,1)S(1)}, bf16[384,512]{1,0:T(8,128)(2,1)S(1)}, u32[]{:S(2)}, u32[]{:S(2)}) %collective-permute-start.34) | collective-permute-done | bytes 393248 | tf_op jit(solution)/shard_map/ppermute | solution.py:38
  155.5 1.3 collective-permute-start.36
  156.9 1.9 %fusion.33 = bf16[384,512]{1,0:T(8,128)(2,1)} fusion(f32[384,512]{1,0:T(8,128)S(1)} %copy-done.23, bf16[384,512]{1,0:T(8,128)(2,1)S(1)} %collective-permute-done.34, bf16[2,384,512]{2,1,0:T(8,128)(2,1)} %collective-permute-done.33), kind=kLoop, calls=%fused_computation.45 | loop fusion | flops 983040 | bytes 1966080 | tf_op jit(solution)/shard_map/convert_element_type | solution.py:710
  158.8 3.5 %all-to-all-start = ((bf16[8,48,512]{2,1,0:T(8,128)(2,1)}), bf16[8,48,512]{2,1,0:T(8,128)(2,1)S(1)}, u32[]{:S(2)}, u32[]{:S(2)}) async-start(bf16[8,48,512]{2,1,0:T(8,128)(2,1)} %bitcast.31), calls=%async_computation | async-start | bytes 786432 | tf_op jit(solution)/shard_map/all_to_all | solution.py:142
  162.7 1.8 %fusion.46 = bf16[1,256,512]{2,1,0:T(8,128)(2,1)} fusion(bf16[256,512]{1,0:T(8,128)(2,1)S(1)} %collective-permute-done.36, f32[256,512]{1,0:T(8,128)S(1)} %get-tuple-element.59, bf16[256,512]{1,0:T(8,128)(2,1)S(1)} %collective-permute-done.31, bf16[1,256,2048]{2,1,0:T(8,128)(2,1)} %param.22, s32[]{:T(128)S(6)} %select_n.35, ...), kind=kLoop, calls=%fused_computation.62 | loop fusion | flops 1048576 | bytes 1573124 | tf_op jit(solution)/shard_map/broadcast_in_dim | solution.py:715
  164.5 6.0 %all-to-all-done = bf16[8,48,512]{2,1,0:T(8,128)(2,1)S(1)} async-done(((bf16[8,48,512]{2,1,0:T(8,128)(2,1)}), bf16[8,48,512]{2,1,0:T(8,128)(2,1)S(1)}, u32[]{:S(2)}, u32[]{:S(2)}) %all-to-all-start) | async-done | bytes 393248 | tf_op jit(solution)/shard_map/all_to_all | solution.py:142
  170.5 1.0 combine.3
  (119 shorter events, 15.4 us)
Async XLA Ops:
  0.6 40.3 %copy-start = (bf16[1,1024,512]{2,1,0:T(8,128)(2,1)S(1)}, bf16[1,1024,512]{2,1,0:T(8,128)(2,1)}, u32[]{:S(2)}) copy-start(bf16[1,1024,512]{2,1,0:T(8,128)(2,1)} %param.26) | copy-start | bytes 3145732
  0.6 19.1 %collective-permute-start.1 = (s32[2,128]{1,0:T(2,128)}, s32[2,128]{1,0:T(2,128)S(1)}, u32[]{:S(2)}, u32[]{:S(2)}) collective-permute-start(s32[2,128]{1,0:T(2,128)} %bitcast.88), channel_id=1, source_target_pairs={{0,2},{1,3},{2,0},{3,1},{4,6},{5,7},{6,4},{7,5},{8,10},{9,11},{10,... | collective-permute-start | bytes 3080 | tf_op jit(solution)/shard_map/ppermute | solution.py:38
  3.6 23.5 %collective-permute-start.6 = (s32[2,128]{1,0:T(2,128)}, s32[2,128]{1,0:T(2,128)S(1)}, u32[]{:S(2)}, u32[]{:S(2)}) collective-permute-start(s32[2,128]{1,0:T(2,128)} %bitcast.89), channel_id=1, source_target_pairs={{0,4},{4,0},{1,5},{5,1},{2,6},{6,2},{3,7},{7,3},{8,12},{12,8},{9,1... | collective-permute-start | bytes 3080 | tf_op jit(solution)/shard_map/ppermute | solution.py:38
  5.2 13.3 %collective-permute-start = (bf16[128,2048]{1,0:T(8,128)(2,1)}, bf16[128,2048]{1,0:T(8,128)(2,1)S(1)}, u32[]{:S(2)}, u32[]{:S(2)}) collective-permute-start(bf16[128,2048]{1,0:T(8,128)(2,1)} %tokens_ref.1), channel_id=1, source_target_pairs={{0,4},{4,0},{1,5},{5,1},{2,6},{6,2},{3,7},{7,3},{8,12},{12,8},{9,1... | collective-permute-start | bytes 1572872 | tf_op jit(solution)/shard_map/ppermute | solution.py:38
  5.7 26.7 %collective-permute-start.7 = (bf16[128,2048]{1,0:T(8,128)(2,1)}, bf16[128,2048]{1,0:T(8,128)(2,1)S(1)}, u32[]{:S(2)}, u32[]{:S(2)}) collective-permute-start(bf16[128,2048]{1,0:T(8,128)(2,1)} %tokens_ref.1), channel_id=1, source_target_pairs={{0,2},{1,3},{2,0},{3,1},{4,6},{5,7},{6,4},{7,5},{8,10},{9,11},{10,... | collective-permute-start | bytes 1572872 | tf_op jit(solution)/shard_map/ppermute | solution.py:38
  18.5 13.9 %collective-permute-start.8 = (bf16[128,2048]{1,0:T(8,128)(2,1)S(1)}, bf16[128,2048]{1,0:T(8,128)(2,1)S(1)}, u32[]{:S(2)}, u32[]{:S(2)}) collective-permute-start(bf16[128,2048]{1,0:T(8,128)(2,1)S(1)} %collective-permute-done.refs_2_), channel_id=1, source_target_pairs={{0,2},{1,3},{2,0},{3,1},{4,6},{5,7},{6,4},{7,5},{8,10},{9,11},{10,... | collective-permute-start | bytes 1572872 | tf_op jit(solution)/shard_map/ppermute | solution.py:38
  19.7 3.6 %collective-permute-start.2 = (s32[2,128]{1,0:T(2,128)S(1)}, s32[2,128]{1,0:T(2,128)S(1)}, u32[]{:S(2)}, u32[]{:S(2)}) collective-permute-start(s32[2,128]{1,0:T(2,128)S(1)} %collective-permute-done.1), channel_id=1, source_target_pairs={{0,4},{4,0},{1,5},{5,1},{2,6},{6,2},{3,7},{7,3},{8,12},{12,8},{9,1... | collective-permute-start | bytes 3080 | tf_op jit(solution)/shard_map/ppermute | solution.py:38
  23.3 7.5 %collective-permute-start.3 = (bf16[64,2048]{1,0:T(8,128)(2,1)S(1)}, bf16[64,2048]{1,0:T(8,128)(2,1)}, u32[]{:S(2)}, u32[]{:S(2)}) collective-permute-start(bf16[64,2048]{1,0:T(8,128)(2,1)S(1)} %constant_dynamic-slice_fusion.2), channel_id=1, source_target_pairs={{0,4},{4,0},{1,5},{5,1},{2,6},{6,2},{3,7},{7,3},{8,12},{12,8},{9,1... | collective-permute-start | bytes 786440 | tf_op jit(solution)/shard_map/ppermute | solution.py:38
  23.6 1.2 copy-start.4
  30.8 10.1 %collective-permute-start.4 = (bf16[256,1024]{1,0:T(8,128)(2,1)}, bf16[256,1024]{1,0:T(8,128)(2,1)S(1)}, u32[]{:S(2)}, u32[]{:S(2)}) collective-permute-start(bf16[256,1024]{1,0:T(8,128)(2,1)} %copy-done.17), channel_id=1, source_target_pairs={{0,4},{4,0},{1,5},{5,1},{2,6},{6,2},{3,7},{7,3},{8,12},{12,8},{9,1... | collective-permute-start | bytes 1572872 | tf_op jit(solution)/shard_map/ppermute | solution.py:38
  30.8 25.1 %collective-permute-start.13 = (bf16[64,2048]{1,0:T(8,128)(2,1)}, bf16[64,2048]{1,0:T(8,128)(2,1)S(1)}, u32[]{:S(2)}, u32[]{:S(2)}) collective-permute-start(bf16[64,2048]{1,0:T(8,128)(2,1)} %collective-permute-done.3), channel_id=1, source_target_pairs={{0,8},{8,0},{16,24},{24,16},{1,9},{9,1},{17,25},{25,17},{2,10},{10... | collective-permute-start | bytes 786440 | tf_op jit(solution)/shard_map/ppermute | solution.py:38
  32.4 1.0 copy-start.1
  34.7 10.3 %copy-start.19 = (bf16[1,1024,2048]{2,1,0:T(8,128)(2,1)S(1)}, bf16[1,1024,2048]{2,1,0:T(8,128)(2,1)}, u32[]{:S(2)}) copy-start(bf16[1,1024,2048]{2,1,0:T(8,128)(2,1)} %param.20) | copy-start | bytes 12582916
  34.7 10.3 %collective-permute-start.9 = (bf16[192,2048]{1,0:T(8,128)(2,1)S(1)}, bf16[192,2048]{1,0:T(8,128)(2,1)S(1)}, u32[]{:S(2)}, u32[]{:S(2)}) collective-permute-start(bf16[192,2048]{1,0:T(8,128)(2,1)S(1)} %get-tuple-element.41), channel_id=1, source_target_pairs={{0,1},{1,0},{2,3},{3,2},{4,5},{5,4},{6,7},{7,6},{8,9},{9,8},{10,11... | collective-permute-start | bytes 2359304 | tf_op jit(solution)/shard_map/ppermute | solution.py:38
  35.9 8.6 %collective-permute-start.10 = (bf16[64,2048]{1,0:T(8,128)(2,1)S(1)}, bf16[64,2048]{1,0:T(8,128)(2,1)S(1)}, u32[]{:S(2)}, u32[]{:S(2)}) collective-permute-start(bf16[64,2048]{1,0:T(8,128)(2,1)S(1)} %constant_dynamic-slice_fusion.2), channel_id=1, source_target_pairs={{0,2},{1,3},{2,0},{3,1},{4,6},{5,7},{6,4},{7,5},{8,10},{9,11},{10,... | collective-permute-start | bytes 786440 | tf_op jit(solution)/shard_map/ppermute | solution.py:38
  41.3 9.0 %copy-start.18 = (bf16[1,2048,1024]{2,1,0:T(8,128)(2,1)S(1)}, bf16[1,2048,1024]{2,1,0:T(8,128)(2,1)}, u32[]{:S(2)}) copy-start(bf16[1,2048,1024]{2,1,0:T(8,128)(2,1)} %param.19) | copy-start | bytes 12582916
  41.3 14.5 %collective-permute-start.5 = (bf16[256,512]{1,0:T(8,128)(2,1)S(1)}, bf16[256,512]{1,0:T(8,128)(2,1)S(1)}, u32[]{:S(2)}, u32[]{:S(2)}) collective-permute-start(bf16[256,512]{1,0:T(8,128)(2,1)S(1)} %convolution_convert_fusion.2), channel_id=1, source_target_pairs={{0,4},{4,0},{1,5},{5,1},{2,6},{6,2},{3,7},{7,3},{8,12},{12,8},{9,1... | collective-permute-start | bytes 786440 | tf_op jit(solution)/shard_map/ppermute | solution.py:38
  44.5 12.0 %collective-permute-start.12 = (bf16[64,2048]{1,0:T(8,128)(2,1)S(1)}, bf16[64,2048]{1,0:T(8,128)(2,1)S(1)}, u32[]{:S(2)}, u32[]{:S(2)}) collective-permute-start(bf16[64,2048]{1,0:T(8,128)(2,1)S(1)} %collective-permute-done.10.refs_1_), channel_id=1, source_target_pairs={{0,8},{8,0},{16,24},{24,16},{1,9},{9,1},{17,25},{25,17},{2,10},{10... | collective-permute-start | bytes 786440 | tf_op jit(solution)/shard_map/ppermute | solution.py:38
  46.8 6.6 %collective-permute-start.11 = (bf16[48,2048]{1,0:T(8,128)(2,1)S(1)}, bf16[48,2048]{1,0:T(8,128)(2,1)S(1)}, u32[]{:S(2)}, u32[]{:S(2)}) collective-permute-start(bf16[48,2048]{1,0:T(8,128)(2,1)S(1)} %get-tuple-element.79), channel_id=1, source_target_pairs={{0,2},{1,3},{2,0},{3,1},{4,6},{5,7},{6,4},{7,5},{8,10},{9,11},{10,... | collective-permute-start | bytes 589832 | tf_op jit(solution)/shard_map/ppermute | solution.py:223
  48.3 8.4 %collective-permute-start.14 = (bf16[48,2048]{1,0:T(8,128)(2,1)S(1)}, bf16[48,2048]{1,0:T(8,128)(2,1)S(1)}, u32[]{:S(2)}, u32[]{:S(2)}) collective-permute-start(bf16[48,2048]{1,0:T(8,128)(2,1)S(1)} %get-tuple-element.77), channel_id=1, source_target_pairs={{0,4},{1,5},{2,6},{3,7},{4,0},{5,1},{6,2},{7,3},{8,12},{9,13},{10,... | collective-permute-start | bytes 589832 | tf_op jit(solution)/shard_map/ppermute | solution.py:223
  51.4 10.0 %copy-start.28 = (f32[128,2]{0,1:T(2,128)S(1)}, f32[128,2]{0,1:T(2,128)}, u32[]{:S(2)}) copy-start(f32[128,2]{0,1:T(2,128)} %param.17) | copy-start | bytes 3076
  52.5 37.5 %copy-start.5 = (bf16[128,2048]{1,0:T(8,128)(2,1)S(1)}, bf16[128,2048]{1,0:T(8,128)(2,1)}, u32[]{:S(2)}) copy-start(bf16[128,2048]{1,0:T(8,128)(2,1)} %refs_0_.3) | copy-start | bytes 1572868
  53.4 7.9 %copy-start.10 = (bf16[48,2048]{1,0:T(8,128)(2,1)}, bf16[48,2048]{1,0:T(8,128)(2,1)S(1)}, u32[]{:S(2)}) copy-start(bf16[48,2048]{1,0:T(8,128)(2,1)S(1)} %collective-permute-done.11.refs_1_) | copy-start | bytes 589828
  53.4 8.5 %collective-permute-start.15 = (bf16[48,2048]{1,0:T(8,128)(2,1)}, bf16[48,2048]{1,0:T(8,128)(2,1)}, u32[]{:S(2)}, u32[]{:S(2)}) collective-permute-start(bf16[48,2048]{1,0:T(8,128)(2,1)} %get-tuple-element.76), channel_id=1, source_target_pairs={{0,6},{1,7},{2,4},{3,5},{4,2},{5,3},{6,0},{7,1},{8,14},{9,15},{10,... | collective-permute-start | bytes 589832 | tf_op jit(solution)/shard_map/ppermute | solution.py:223
  55.9 5.4 %copy-start.25 = (bf16[64,2048]{1,0:T(8,128)(2,1)}, bf16[64,2048]{1,0:T(8,128)(2,1)S(1)}, u32[]{:S(2)}) copy-start(bf16[64,2048]{1,0:T(8,128)(2,1)S(1)} %collective-permute-done.13) | copy-start | bytes 786436
  55.9 6.1 %collective-permute-start.16 = (bf16[48,2048]{1,0:T(8,128)(2,1)}, bf16[48,2048]{1,0:T(8,128)(2,1)}, u32[]{:S(2)}, u32[]{:S(2)}) collective-permute-start(bf16[48,2048]{1,0:T(8,128)(2,1)} %get-tuple-element.75), channel_id=1, source_target_pairs={{0,1},{1,0},{2,3},{3,2},{4,5},{5,4},{6,7},{7,6},{8,9},{9,8},{10,11... | collective-permute-start | bytes 589832 | tf_op jit(solution)/shard_map/ppermute | solution.py:223
  55.9 5.4 %copy-start.26 = (bf16[256,512]{1,0:T(8,128)(2,1)}, bf16[256,512]{1,0:T(8,128)(2,1)S(1)}, u32[]{:S(2)}) copy-start(bf16[256,512]{1,0:T(8,128)(2,1)S(1)} %collective-permute-done.5) | copy-start | bytes 786436
  55.9 9.7 %collective-permute-start.17 = (bf16[48,2048]{1,0:T(8,128)(2,1)}, bf16[48,2048]{1,0:T(8,128)(2,1)}, u32[]{:S(2)}, u32[]{:S(2)}) collective-permute-start(bf16[48,2048]{1,0:T(8,128)(2,1)} %get-tuple-element.74), channel_id=1, source_target_pairs={{0,3},{1,2},{2,1},{3,0},{4,7},{5,6},{6,5},{7,4},{8,11},{9,10},{10,... | collective-permute-start | bytes 589832 | tf_op jit(solution)/shard_map/ppermute | solution.py:223
  56.5 12.6 %collective-permute-start.18 = (bf16[48,2048]{1,0:T(8,128)(2,1)}, bf16[48,2048]{1,0:T(8,128)(2,1)}, u32[]{:S(2)}, u32[]{:S(2)}) collective-permute-start(bf16[48,2048]{1,0:T(8,128)(2,1)} %get-tuple-element.73), channel_id=1, source_target_pairs={{0,5},{1,4},{2,7},{3,6},{4,1},{5,0},{6,3},{7,2},{8,13},{9,12},{10,... | collective-permute-start | bytes 589832 | tf_op jit(solution)/shard_map/ppermute | solution.py:223
  56.7 4.6 %copy-start.12 = (bf16[48,2048]{1,0:T(8,128)(2,1)}, bf16[48,2048]{1,0:T(8,128)(2,1)S(1)}, u32[]{:S(2)}) copy-start(bf16[48,2048]{1,0:T(8,128)(2,1)S(1)} %collective-permute-done.14.refs_2_) | copy-start | bytes 589828
  56.7 12.5 %collective-permute-start.19 = (bf16[48,2048]{1,0:T(8,128)(2,1)}, bf16[48,2048]{1,0:T(8,128)(2,1)}, u32[]{:S(2)}, u32[]{:S(2)}) collective-permute-start(bf16[48,2048]{1,0:T(8,128)(2,1)} %get-tuple-element.72), channel_id=1, source_target_pairs={{0,7},{1,6},{2,5},{3,4},{4,3},{5,2},{6,1},{7,0},{8,15},{9,14},{10,... | collective-permute-start | bytes 589832 | tf_op jit(solution)/shard_map/ppermute | solution.py:223
  69.2 0.9 copy-start.11
  70.1 0.9 copy-start.13
  73.1 8.4 %collective-permute-start.21 = (bf16[2,128,512]{2,1,0:T(8,128)(2,1)S(1)}, bf16[2,128,512]{2,1,0:T(8,128)(2,1)S(1)}, u32[]{:S(2)}, u32[]{:S(2)}) collective-permute-start(bf16[2,128,512]{2,1,0:T(8,128)(2,1)S(1)} %get-tuple-element.52), channel_id=1, source_target_pairs={{0,8},{8,0},{16,24},{24,16},{1,9},{9,1},{17,25},{25,17},{2,10},{10... | collective-permute-start | bytes 786440 | tf_op jit(solution)/shard_map/ppermute | solution.py:38
  74.8 26.3 %collective-permute-start.24 = (bf16[1024,512]{1,0:T(8,128)(2,1)}, bf16[1024,512]{1,0:T(8,128)(2,1)S(1)}, u32[]{:S(2)}, u32[]{:S(2)}) collective-permute-start(bf16[1024,512]{1,0:T(8,128)(2,1)} %bitcast.85), channel_id=1, source_target_pairs={{0,4},{4,0},{1,5},{5,1},{2,6},{6,2},{3,7},{7,3},{8,12},{12,8},{9,1... | collective-permute-start | bytes 3145736 | tf_op jit(solution)/shard_map/ppermute | solution.py:38
  75.7 14.2 %collective-permute-start.20 = (bf16[128,2048]{1,0:T(8,128)(2,1)S(1)}, bf16[128,2048]{1,0:T(8,128)(2,1)S(1)}, u32[]{:S(2)}, u32[]{:S(2)}) collective-permute-start(bf16[128,2048]{1,0:T(8,128)(2,1)S(1)} %constant_dynamic-update-slice_fusion.refs_3_), channel_id=1, source_target_pairs={{0,2},{1,3},{2,0},{3,1},{4,6},{5,7},{6,4},{7,5},{8,10},{9,11},{10,... | collective-permute-start | bytes 1572872 | tf_op jit(solution)/shard_map/ppermute | solution.py:38
  81.6 10.8 %collective-permute-start.22 = (bf16[128,512]{1,0:T(8,128)(2,1)S(1)}, bf16[128,512]{1,0:T(8,128)(2,1)S(1)}, u32[]{:S(2)}, u32[]{:S(2)}) collective-permute-start(bf16[128,512]{1,0:T(8,128)(2,1)S(1)} %fusion.47), channel_id=1, source_target_pairs={{0,16},{8,24},{16,0},{24,8},{1,17},{9,25},{17,1},{25,9},{2,18},{10... | collective-permute-start | bytes 393224 | tf_op jit(solution)/shard_map/ppermute | solution.py:38
  92.3 11.4 %collective-permute-start.32 = (bf16[192,2048]{1,0:T(8,128)(2,1)S(1)}, bf16[192,2048]{1,0:T(8,128)(2,1)S(1)}, u32[]{:S(2)}, u32[]{:S(2)}) collective-permute-start(bf16[192,2048]{1,0:T(8,128)(2,1)S(1)} %get-tuple-element.50), channel_id=1, source_target_pairs={{0,1},{1,0},{2,3},{3,2},{4,5},{5,4},{6,7},{7,6},{8,9},{9,8},{10,11... | collective-permute-start | bytes 2359304 | tf_op jit(solution)/shard_map/ppermute | solution.py:38
  92.4 6.0 %collective-permute-start.23 = (bf16[128,512]{1,0:T(8,128)(2,1)S(1)}, bf16[128,512]{1,0:T(8,128)(2,1)S(1)}, u32[]{:S(2)}, u32[]{:S(2)}) collective-permute-start(bf16[128,512]{1,0:T(8,128)(2,1)S(1)} %fusion.49.refs_0_), channel_id=1, source_target_pairs={{0,8},{8,0},{16,24},{24,16},{1,9},{9,1},{17,25},{25,17},{2,10},{10... | collective-permute-start | bytes 393224 | tf_op jit(solution)/shard_map/ppermute | solution.py:38
  92.9 29.6 %collective-permute-start.27 = (bf16[1024,512]{1,0:T(8,128)(2,1)}, bf16[1024,512]{1,0:T(8,128)(2,1)}, u32[]{:S(2)}, u32[]{:S(2)}) collective-permute-start(bf16[1024,512]{1,0:T(8,128)(2,1)} %bitcast.24.refs_4_), channel_id=1, source_target_pairs={{0,4},{4,0},{1,5},{5,1},{2,6},{6,2},{3,7},{7,3},{8,12},{12,8},{9,1... | collective-permute-start | bytes 3145736 | tf_op jit(solution)/shard_map/ppermute | solution.py:38
  101.0 11.0 %copy-start.20 = (bf16[1024,512]{1,0:T(8,128)(2,1)}, bf16[1024,512]{1,0:T(8,128)(2,1)S(1)}, u32[]{:S(2)}) copy-start(bf16[1024,512]{1,0:T(8,128)(2,1)S(1)} %collective-permute-done.24.refs_3_) | copy-start | bytes 3145732
  101.1 17.3 %collective-permute-start.25 = (bf16[2,128,512]{2,1,0:T(8,128)(2,1)S(1)}, bf16[2,128,512]{2,1,0:T(8,128)(2,1)S(1)}, u32[]{:S(2)}, u32[]{:S(2)}) collective-permute-start(bf16[2,128,512]{2,1,0:T(8,128)(2,1)S(1)} %pad_maximum_fusion), channel_id=1, source_target_pairs={{0,16},{8,24},{16,0},{24,8},{1,17},{9,25},{17,1},{25,9},{2,18},{10... | collective-permute-start | bytes 786440 | tf_op jit(solution)/shard_map/ppermute | solution.py:38
  103.7 0.9 copy-start.21
  112.0 6.4 %copy-start.2 = (bf16[128,2048]{1,0:T(8,128)(2,1)S(1)}, bf16[128,2048]{1,0:T(8,128)(2,1)}, u32[]{:S(2)}) copy-start(bf16[128,2048]{1,0:T(8,128)(2,1)} %tokens_ref.1) | copy-start | bytes 1572868
  112.0 6.4 %copy-start.15 = (f32[2048]{0:T(1024)S(1)}, f32[2048]{0:T(1024)}, u32[]{:S(2)}) copy-start(f32[2048]{0:T(1024)} %param.21) | copy-start | bytes 24580
  112.0 8.3 %copy-start.6 = (bf16[1,512,1024]{2,1,0:T(8,128)(2,1)S(1)}, bf16[1,512,1024]{2,1,0:T(8,128)(2,1)}, u32[]{:S(2)}) copy-start(bf16[1,512,1024]{2,1,0:T(8,128)(2,1)} %param.29) | copy-start | bytes 3145732
  112.0 8.8 %copy-start.27 = (bf16[256,512]{1,0:T(8,128)(2,1)S(1)}, bf16[256,512]{1,0:T(8,128)(2,1)}, u32[]{:S(2)}) copy-start(bf16[256,512]{1,0:T(8,128)(2,1)} %copy-done.26) | copy-start | bytes 786436
  117.9 17.3 %collective-permute-start.33 = (bf16[2,384,512]{2,1,0:T(8,128)(2,1)}, bf16[2,384,512]{2,1,0:T(8,128)(2,1)}, u32[]{:S(2)}, u32[]{:S(2)}) collective-permute-start(bf16[2,384,512]{2,1,0:T(8,128)(2,1)} %get-tuple-element.65), channel_id=1, source_target_pairs={{0,8},{8,0},{16,24},{24,16},{1,9},{9,1},{17,25},{25,17},{2,10},{10... | collective-permute-start | bytes 2359304 | tf_op jit(solution)/shard_map/ppermute | solution.py:38
  118.9 3.6 %copy-start.3 = (bf16[128,2048]{1,0:T(8,128)(2,1)}, bf16[128,2048]{1,0:T(8,128)(2,1)S(1)}, u32[]{:S(2)}) copy-start(bf16[128,2048]{1,0:T(8,128)(2,1)S(1)} %memory.1.refs_0_) | copy-start | bytes 1572868
  118.9 3.6 %collective-permute-start.26 = (bf16[128,2048]{1,0:T(8,128)(2,1)S(1)}, bf16[128,2048]{1,0:T(8,128)(2,1)}, u32[]{:S(2)}, u32[]{:S(2)}) collective-permute-start(bf16[128,2048]{1,0:T(8,128)(2,1)S(1)} %memory.1.refs_0_), channel_id=1, source_target_pairs={{0,1},{1,0},{2,3},{3,2},{4,5},{5,4},{6,7},{7,6},{8,9},{9,8},{10,11... | collective-permute-start | bytes 1572872 | tf_op jit(solution)/shard_map/ppermute | solution.py:38
  119.0 14.4 %collective-permute-start.28 = (bf16[128,2048]{1,0:T(8,128)(2,1)S(1)}, bf16[128,2048]{1,0:T(8,128)(2,1)}, u32[]{:S(2)}, u32[]{:S(2)}) collective-permute-start(bf16[128,2048]{1,0:T(8,128)(2,1)S(1)} %memory.1.refs_0_), channel_id=1, source_target_pairs={{0,2},{1,3},{2,0},{3,1},{4,6},{5,7},{6,4},{7,5},{8,10},{9,11},{10,... | collective-permute-start | bytes 1572872 | tf_op jit(solution)/shard_map/ppermute | solution.py:38
  120.3 25.3 %collective-permute-start.30 = (bf16[512,1024]{1,0:T(8,128)(2,1)S(1)}, bf16[512,1024]{1,0:T(8,128)(2,1)}, u32[]{:S(2)}, u32[]{:S(2)}) collective-permute-start(bf16[512,1024]{1,0:T(8,128)(2,1)S(1)} %bitcast.79), channel_id=1, source_target_pairs={{0,4},{4,0},{1,5},{5,1},{2,6},{6,2},{3,7},{7,3},{8,12},{12,8},{9,1... | collective-permute-start | bytes 3145736 | tf_op jit(solution)/shard_map/ppermute | solution.py:38
  120.9 14.4 %copy-start.22 = (f32[384,512]{1,0:T(8,128)S(1)}, f32[384,512]{1,0:T(8,128)}, u32[]{:S(2)}) copy-start(f32[384,512]{1,0:T(8,128)} %get-tuple-element.64) | copy-start | bytes 2359300
  127.9 17.7 %copy-start.8 = (bf16[128,512]{1,0:T(8,128)(2,1)S(1)}, bf16[128,512]{1,0:T(8,128)(2,1)}, u32[]{:S(2)}) copy-start(bf16[128,512]{1,0:T(8,128)(2,1)} %attend_sentence.2.mine_ref) | copy-start | bytes 393220
  127.9 17.7 %copy-start.16 = (s32[3]{0:T(128)S(1)}, s32[3]{0:T(128)}, u32[]{:S(2)}) copy-start(s32[3]{0:T(128)} %pad_add_fusion.1.place_ref) | copy-start | bytes 40
  133.4 4.1 %collective-permute-start.29 = (bf16[128,2048]{1,0:T(8,128)(2,1)}, bf16[128,2048]{1,0:T(8,128)(2,1)S(1)}, u32[]{:S(2)}, u32[]{:S(2)}) collective-permute-start(bf16[128,2048]{1,0:T(8,128)(2,1)} %collective-permute-done.28.refs_0_), channel_id=1, source_target_pairs={{0,1},{1,0},{2,3},{3,2},{4,5},{5,4},{6,7},{7,6},{8,9},{9,8},{10,11... | collective-permute-start | bytes 1572872 | tf_op jit(solution)/shard_map/ppermute | solution.py:38
  136.4 19.1 %collective-permute-start.34 = (bf16[384,512]{1,0:T(8,128)(2,1)S(1)}, bf16[384,512]{1,0:T(8,128)(2,1)S(1)}, u32[]{:S(2)}, u32[]{:S(2)}) collective-permute-start(bf16[384,512]{1,0:T(8,128)(2,1)S(1)} %fusion.34), channel_id=1, source_target_pairs={{0,16},{8,24},{16,0},{24,8},{1,17},{9,25},{17,1},{25,9},{2,18},{10... | collective-permute-start | bytes 1179656 | tf_op jit(solution)/shard_map/ppermute | solution.py:38
  138.3 18.5 %copy-start.23 = (f32[384,512]{1,0:T(8,128)S(1)}, f32[384,512]{1,0:T(8,128)}, u32[]{:S(2)}) copy-start(f32[384,512]{1,0:T(8,128)} %get-tuple-element.68) | copy-start | bytes 2359300
  145.6 0.9 copy-start.9
  146.5 15.7 %copy-start.29 = (s32[2]{0:T(128)S(1)}, s32[2]{0:T(128)}, u32[]{:S(2)}) copy-start(s32[2]{0:T(128)} %param.24) | copy-start | bytes 28
  148.5 7.0 %collective-permute-start.35 = (bf16[256,512]{1,0:T(8,128)(2,1)S(1)}, bf16[256,512]{1,0:T(8,128)(2,1)S(1)}, u32[]{:S(2)}, u32[]{:S(2)}) collective-permute-start(bf16[256,512]{1,0:T(8,128)(2,1)S(1)} %get-tuple-element.67), channel_id=1, source_target_pairs={{0,1},{1,0},{2,3},{3,2},{4,5},{5,4},{6,7},{7,6},{8,9},{9,8},{10,11... | collective-permute-start | bytes 786440 | tf_op jit(solution)/shard_map/ppermute | solution.py:38
  148.6 13.9 %collective-permute-start.31 = (bf16[256,512]{1,0:T(8,128)(2,1)S(1)}, bf16[256,512]{1,0:T(8,128)(2,1)S(1)}, u32[]{:S(2)}, u32[]{:S(2)}) collective-permute-start(bf16[256,512]{1,0:T(8,128)(2,1)S(1)} %get-tuple-element.60), channel_id=1, source_target_pairs={{0,1},{1,0},{2,3},{3,2},{4,5},{5,4},{6,7},{7,6},{8,9},{9,8},{10,11... | collective-permute-start | bytes 786440 | tf_op jit(solution)/shard_map/ppermute | solution.py:38
  155.5 7.2 %collective-permute-start.36 = (bf16[256,512]{1,0:T(8,128)(2,1)S(1)}, bf16[256,512]{1,0:T(8,128)(2,1)S(1)}, u32[]{:S(2)}, u32[]{:S(2)}) collective-permute-start(bf16[256,512]{1,0:T(8,128)(2,1)S(1)} %convert_add_fusion.3), channel_id=1, source_target_pairs={{0,2},{1,3},{2,0},{3,1},{4,6},{5,7},{6,4},{7,5},{8,10},{9,11},{10,... | collective-permute-start | bytes 786440 | tf_op jit(solution)/shard_map/ppermute | solution.py:38
  158.8 11.7 %all-to-all-start = ((bf16[8,48,512]{2,1,0:T(8,128)(2,1)}), bf16[8,48,512]{2,1,0:T(8,128)(2,1)S(1)}, u32[]{:S(2)}, u32[]{:S(2)}) async-start(bf16[8,48,512]{2,1,0:T(8,128)(2,1)} %bitcast.31), calls=%async_computation | async-start | bytes 786432 | tf_op jit(solution)/shard_map/all_to_all | solution.py:142
  (4 other events, 3.2 us)

commit v11 on v10

--- a/solution.py
+++ b/solution.py
@@ -571,27 +571,33 @@
 
     token_y = swap(tokens, "expert", 1)
     token_x = swap(tokens, "dp", 2)
-    ids_own = expert_ids.T
+    row = lax.broadcasted_iota(jnp.int32, (token_count, token_count), 0)
+    column = lax.broadcasted_iota(jnp.int32, (token_count, token_count), 1)
+    named = expert_ids[:, :, None] == jnp.arange(size, dtype=jnp.int32)[None, None, :]
+    either = (named[:, 0] | named[:, 1]).astype(jnp.bfloat16)
+    earlier = jnp.dot(
+        (column < row).astype(jnp.bfloat16), either, preferred_element_type=jnp.float32
+    ).astype(jnp.int32)
+    rank = jnp.sum(jnp.where(named, earlier[:, None, :], 0), axis=2)
+    codes_of = expert_ids ^ here
+    position = ((codes_of >> 1) + 4 * (codes_of & 1)) * capacity + rank
+
+    states = dec_states[0]
+    normed_own, asked = normed_halves(y, states, norm_gain)
+    ids_own = gate(expert_ids, asked).T
     ids_x, ids_y = swap(ids_own, "dp", 2), swap(ids_own, "expert", 1)
     ids_far = swap(ids_x, "expert", 1)
-    token_far = swap(token_y, "dp", 2)
+    token_far = swap(gate(token_y, ids_x, ids_y, asked), "dp", 2)
 
     side = lax.rem(section, 2)
     share = token_count // 2
     grad_half = lax.dynamic_slice_in_dim(out_grad, side * share, share, 0)
-    half_y = swap(gate(grad_half, token_y, ids_far), "expert", 1)
-    states = dec_states[0]
-    normed_own, asked = normed_halves(y, states, norm_gain)
-    asked_here = swap(gate(asked, half_y), "expert", 1)
+    asked_here = swap(gate(asked, token_y), "expert", 1)
+    half_y = swap(gate(grad_half, asked_here), "expert", 1)
+    other_y = swap(half_y, "section", 1)
     query_there = jnp.dot(asked_here, query_own, preferred_element_type=jnp.float32)
     query_back = swap(query_there.astype(jnp.bfloat16), "expert", 1)
-    other_y = swap(half_y, "section", 1)
-    grad_y = jnp.concatenate([half_y, other_y], axis=0)
-    half_x = swap(gate(grad_half, token_far), "dp", 2)
-    other_x = swap(half_x, "section", 1)
-
-    row = lax.broadcasted_iota(jnp.int32, (token_count, token_count), 0)
-    column = lax.broadcasted_iota(jnp.int32, (token_count, token_count), 1)
+
     ids = jnp.stack([ids_own, ids_x, ids_y, ids_far])
     named_there = jnp.concatenate([(ids == here).any(axis=1), (ids == (here ^ 1)).any(axis=1)])
     before = jnp.dot(
@@ -601,15 +607,6 @@
     ).astype(jnp.int32)
     code = jnp.where(named_there, before, -1)
 
-    named = expert_ids[:, :, None] == jnp.arange(size, dtype=jnp.int32)[None, None, :]
-    either = (named[:, 0] | named[:, 1]).astype(jnp.bfloat16)
-    earlier = jnp.dot(
-        (column < row).astype(jnp.bfloat16), either, preferred_element_type=jnp.float32
-    ).astype(jnp.int32)
-    rank = jnp.sum(jnp.where(named, earlier[:, None, :], 0), axis=2)
-    codes_of = expert_ids ^ here
-    position = ((codes_of >> 1) + 4 * (codes_of & 1)) * capacity + rank
-
     def forward(rows, *after):
         pre_act = jnp.dot(rows, weight_in, preferred_element_type=jnp.float32)
         hidden = jax.nn.gelu(gate(pre_act, *after)).astype(jnp.bfloat16)
@@ -621,43 +618,46 @@
 
     rows_own, rows_sent = dispatch(
         which_section,
-        code,
+        gate(code, asked),
         [tokens, token_x, token_y, token_far],
         tuple(((place, 0, token_count, None),) for place in range(4)),
         capacity,
     )
     rows_core = swap(rows_sent, "dp", 1)
-    pre_own, part_own = forward(rows_own, rows_core, half_x)
-    pre_core, part_core = forward(rows_core, asked_here)
+    pre_own, part_own = forward(rows_own)
+    pre_core, part_core = forward(gate(rows_core, part_own))
+    part_core = gate(part_core, query_back)
     home = send_home(part_own, near_codes, capacity) + send_home(part_core, core_codes, capacity)
+    grad_y = jnp.concatenate([gate(half_y, home[4]), other_y], axis=0)
 
     rise_own, rise_core = slope_of(gate(pre_own, home[1])), slope_of(gate(pre_core, home[1]))
-    held_gates = gate(gate_weights, rise_own, rise_core, query_back, other_x, other_y)
+    held_gates = gate(gate_weights, rise_own, rise_core, grad_y)
     sent_pair, first, second = combine(which_section, position, held_gates, home, sections)
     from_pair = swap(sent_pair, "section", 1)
+    grad_x = swap(gate(out_grad, home[5]), "dp", 2)
     grad_far = swap(gate(grad_y, first), "dp", 2)
-    grads_own, grads_sent = dispatch(
-        which_section,
-        code,
-        [out_grad, half_x, other_x, grad_y, grad_far],
-        (
-            ((0, 0, token_count, None),),
-            ((1, 0, share, 0), (2, 0, share, 1)),
-            ((3, 0, share, 0), (3, share, share, 1)),
-            ((4, 0, share, 0), (4, share, share, 1)),
-        ),
-        capacity,
-    )
-    grads_core = swap(grads_sent, "dp", 1)
-    grads_core = swap(grads_sent, "dp", 1)
     to_other = (second + from_pair[1].astype(jnp.float32)).astype(jnp.bfloat16)
     from_other = swap(to_other, "section", 2)
-    mixed_sum = gate(first, grads_sent) + from_pair[0].astype(jnp.float32)
+    mixed_sum = first + from_pair[0].astype(jnp.float32)
     mixed_slice = (mixed_sum + from_other.astype(jnp.float32)).astype(jnp.bfloat16)
     key_other = swap(gate(key_own, first), "expert", 1)
     mixed_near = swap(mixed_slice, "section", 1)
+    grads_own, grads_sent = dispatch(
+        which_section,
+        gate(code, mixed_near),
+        [out_grad, grad_x, grad_y, grad_far],
+        (
+            ((0, 0, token_count, None),),
+            ((1, 0, token_count, None),),
+            ((2, 0, share, 0), (2, share, share, 1)),
+            ((3, 0, share, 0), (3, share, share, 1)),
+        ),
+        capacity,
+    )
+    grads_core = swap(grads_sent, "dp", 1)
+    grads_core = swap(grads_sent, "dp", 1)
     slope = expert_slope(
-        gate(here.astype(jnp.int32).reshape(1), mixed_near),
+        here.astype(jnp.int32).reshape(1),
         near_codes + core_codes,
         grads_own,
         grads_core,
@@ -665,13 +665,13 @@
         rise_core,
         weight_out,
     )
+    mixed_far = swap(jnp.stack([mixed_slice, gate(mixed_near, key_other)]), "section", 2)
     back_pair, back_first, back_second = expert_backward(
         which_section, slope, weight_in, sections
     )
-    mixed_far = swap(jnp.stack([mixed_slice, gate(mixed_near, key_other)]), "section", 2)
     slices = [mixed_slice, mixed_near, mixed_far[0], mixed_far[1]]
 
-    value_other = swap(gate(value_own, mixed_slice), "expert", 1)
+    value_other = swap(gate(value_own, mixed_near), "expert", 1)
 
     query_here = jnp.dot(normed_own, query_own, preferred_element_type=jnp.float32)
     query = (query_here + query_back.astype(jnp.float32)).astype(jnp.bfloat16)

time: 172 us -> 183 us (1.064)
  waiting for transfers between devices: 63.8 us -> 73.3 us
    ppermute x30 -> x29, waiting for transfers between devices: 50.1 us -> 57.8 us  [swap(): return lax.ppermute(value, axis, [(i, i ^ mask) for i in range(size)])]
    ppermute x7, starting transfers between devices: 9.31 us -> 5.92 us  [send_home(): lax.ppermute(block, ('expert', 'dp'), [(i, i ^ code) for i in range(size)])]
    ppermute x30 -> x29, starting transfers between devices: 26.3 us -> 29.5 us  [swap(): return lax.ppermute(value, axis, [(i, i ^ mask) for i in range(size)])]
    ppermute x7, waiting for transfers between devices: 7.74 us -> 10.8 us  [send_home(): lax.ppermute(block, ('expert', 'dp'), [(i, i ^ code) for i in range(size)])]
    unnamed x63 -> x61, local copies, waits for them, and re-layouts: 11.2 us -> 11.5 us
  transfers between devices with their start and end apart: 38 -> 37, of which waited for: 19 -> 16; matrix products, arithmetic and copies ran while one was open for 15% -> 14% of each run, Pallas kernels for 17% -> 16%
where the time goes in v11:
time: 183 us; the launch traced here: 182 us
  waiting for transfers between devices  73.3 us (40%)
  starting transfers between devices  38.8 us (21%)
  Pallas kernels  33 us (18%)
  local copies, waits for them, and re-layouts  16 us (9%)
  other arithmetic  11.2 us (6%)
  matrix products  8.56 us (5%)
    ppermute x29, waiting for transfers between devices, swap(): return lax.ppermute(value, axis, [(i, i ^ mask) for i in range(size)])  57.8 us
    ppermute x29, starting transfers between devices, swap(): return lax.ppermute(value, axis, [(i, i ^ mask) for i in range(size)])  29.5 us
    unnamed x61, local copies, waits for them, and re-layouts  11.5 us
    pallas_call x2, Pallas kernels, attend_sentence(): pl.pallas_call(attend_kernel, out_shape=jax.ShapeDtypeStruct(query.shape,...  10.9 us
    ppermute x7, waiting for transfers between devices, send_home(): lax.ppermute(block, ('expert', 'dp'), [(i, i ^ code) for i in range(size)])  10.8 us
    pallas_call x1, Pallas kernels, expert_slope(): pl.pallas_call(functools.partial(slope_kernel, codes), out_shape=jax.Shap...  7.34 us
    ppermute x7, starting transfers between devices, send_home(): lax.ppermute(block, ('expert', 'dp'), [(i, i ^ code) for i in range(size)])  5.92 us
    pallas_call x1, Pallas kernels, expert_backward(): pl.pallas_call(functools.partial(backward_kernel, split), out_shape=(jax....  5.83 us
  transfers between devices with their start and end apart: 37, of which 16 were waited for; matrix products, arithmetic and copies ran while one was open for 14% of the time, Pallas kernels for 16%

profile of v11, /device:TPU:0, one launch (start us, length us, event | category | flops | bytes accessed | tf_op | source)
XLA Modules:
  0.0 181.9 jit_solution(10681705408532736133)
XLA Ops:
  0.7 1.3 copy-done.4
  4.2 2.9 %collective-permute-start.3 = (s32[2,128]{1,0:T(2,128)}, s32[2,128]{1,0:T(2,128)S(1)}, u32[]{:S(2)}, u32[]{:S(2)}) collective-permute-start(s32[2,128]{1,0:T(2,128)} %bitcast.88), channel_id=1, source_target_pairs={{0,2},{1,3},{2,0},{3,1},{4,6},{5,7},{6,4},{7,5},{8,10},{9,11},{10,... | collective-permute-start | bytes 3080 | tf_op jit(solution)/shard_map/ppermute | solution.py:38
  7.2 1.5 collective-permute-start.4
  12.5 9.5 %collective-permute-done.refs_2_ = bf16[128,2048]{1,0:T(8,128)(2,1)S(1)} collective-permute-done((bf16[128,2048]{1,0:T(8,128)(2,1)}, bf16[128,2048]{1,0:T(8,128)(2,1)S(1)}, u32[]{:S(2)}, u32[]{:S(2)}) %collective-permute-start) | collective-permute-done | bytes 524320 | tf_op jit(solution)/shard_map/ppermute | solution.py:38
  22.9 1.7 collective-permute-start.1
  24.6 1.7 constant_dynamic-slice_fusion.1
  27.2 7.0 %collective-permute-done.7.refs_3_ = bf16[128,2048]{1,0:T(8,128)(2,1)S(1)} collective-permute-done((bf16[128,2048]{1,0:T(8,128)(2,1)S(1)}, bf16[128,2048]{1,0:T(8,128)(2,1)S(1)}, u32[]{:S(2)}, u32[]{:S(2)}) %collective-permute-start.7) | collective-permute-done | bytes 524320 | tf_op jit(solution)/shard_map/ppermute | solution.py:38
  34.2 1.0 copy-done.1
  35.2 1.3 dispatch.2
  36.5 3.2 %fusion.60 = f32[192,1024]{1,0:T(8,128)S(1)} fusion(bf16[192,2048]{1,0:T(8,128)(2,1)S(1)} %get-tuple-element.45, bf16[1,2048,1024]{2,1,0:T(8,128)(2,1)} %param.19), kind=kOutput, calls=%fused_computation.101 | convolution fusion | flops 805306368 | bytes 5767168 | tf_op jit(solution)/shard_map/dot_general | solution.py:611
  39.8 0.8 collective-permute-start.10
  40.7 1.1 convolution_convert_fusion.1
  41.8 0.8 fusion.72
  43.1 1.5 convolution_convert_fusion.2
  44.6 1.3 collective-permute-start.2
  46.7 2.9 %collective-permute-done.8.refs_1_ = bf16[48,2048]{1,0:T(8,128)(2,1)S(1)} collective-permute-done((bf16[48,2048]{1,0:T(8,128)(2,1)S(1)}, bf16[48,2048]{1,0:T(8,128)(2,1)S(1)}, u32[]{:S(2)}, u32[]{:S(2)}) %collective-permute-start.8) | collective-permute-done | bytes 196640 | tf_op jit(solution)/shard_map/ppermute | solution.py:223
  49.5 1.2 collective-permute-start.14
  50.7 1.6 collective-permute-start.12
  52.4 1.0 fusion.58
  53.4 1.1 convolution_convert_fusion
  54.5 4.6 %collective-permute-done.2 = bf16[256,512]{1,0:T(8,128)(2,1)S(1)} collective-permute-done((bf16[256,512]{1,0:T(8,128)(2,1)S(1)}, bf16[256,512]{1,0:T(8,128)(2,1)S(1)}, u32[]{:S(2)}, u32[]{:S(2)}) %collective-permute-start.2) | collective-permute-done | bytes 262176 | tf_op jit(solution)/shard_map/ppermute | solution.py:38
  59.0 0.9 fusion.71
  60.6 2.1 %fusion.9 = (f32[192,1024]{1,0:T(8,128)}, f32[192,1024]{1,0:T(8,128)}) fusion(f32[192,1024]{1,0:T(8,128)S(1)} %fusion.60, f32[192,1024]{1,0:T(8,128)S(1)} %fusion.58), kind=kLoop, calls=%fused_computation.20 | loop fusion | flops 6684672 | bytes 3145728 | tf_op jit(solution)/shard_map/transpose(jvp())/add_any | solution.py:617
  63.3 0.9 collective-permute-start.16
  64.2 1.9 %collective-permute-start.17 = (bf16[48,2048]{1,0:T(8,128)(2,1)}, bf16[48,2048]{1,0:T(8,128)(2,1)}, u32[]{:S(2)}, u32[]{:S(2)}) collective-permute-start(bf16[48,2048]{1,0:T(8,128)(2,1)} %get-tuple-element.78), channel_id=1, source_target_pairs={{0,7},{1,6},{2,5},{3,4},{4,3},{5,2},{6,1},{7,0},{8,15},{9,14},{10,... | collective-permute-start | bytes 589832 | tf_op jit(solution)/shard_map/ppermute | solution.py:223
  66.9 7.9 %collective-permute-done.16.refs_6_ = bf16[48,2048]{1,0:T(8,128)(2,1)} collective-permute-done((bf16[48,2048]{1,0:T(8,128)(2,1)}, bf16[48,2048]{1,0:T(8,128)(2,1)}, u32[]{:S(2)}, u32[]{:S(2)}) %collective-permute-start.16) | collective-permute-done | bytes 196640 | tf_op jit(solution)/shard_map/ppermute | solution.py:223
  74.9 0.9 copy-done.11
  75.8 0.9 copy-done.13
  76.7 2.0 %combine.2 = (bf16[2,128,512]{2,1,0:T(8,128)(2,1)S(1)}, f32[128,512]{1,0:T(8,128)S(1)}, f32[128,512]{1,0:T(8,128)S(1)}) custom-call(s32[1]{0:T(128)} %bitcast.7.section_ref, s32[128,2]{1,0:T(8,128)S(1)} %get-tuple-element.91.position_ref, f32[128,2]{1,0:T(8,128)S(1)} %copy.39.gates_ref, bf16[48,2048]{1,0:T(8,128)(2,1)S(1)} %get-tuple-element.84.refs_0_, ...), custom_call_target="tpu_custom_call" | custom-call | flops 1 | bytes 1 | tf_op jit(solution)/shard_map/combine/pallas_call | solution.py:264
  78.8 1.7 collective-permute-start.18
  80.4 1.5 collective-permute-start.30
  82.5 1.3 collective-permute-start.21
  83.7 3.5 %collective-permute-done.18 = bf16[2,128,512]{2,1,0:T(8,128)(2,1)S(1)} collective-permute-done((bf16[2,128,512]{2,1,0:T(8,128)(2,1)S(1)}, bf16[2,128,512]{2,1,0:T(8,128)(2,1)S(1)}, u32[]{:S(2)}, u32[]{:S(2)}) %collective-permute-start.18) | collective-permute-done | bytes 262176 | tf_op jit(solution)/shard_map/ppermute | solution.py:38
  87.2 2.7 %collective-permute-start.19 = (bf16[128,512]{1,0:T(8,128)(2,1)S(1)}, bf16[128,512]{1,0:T(8,128)(2,1)S(1)}, u32[]{:S(2)}, u32[]{:S(2)}) collective-permute-start(bf16[128,512]{1,0:T(8,128)(2,1)S(1)} %fusion.47), channel_id=1, source_target_pairs={{0,16},{8,24},{16,0},{24,8},{1,17},{9,25},{17,1},{25,9},{2,18},{10... | collective-permute-start | bytes 393224 | tf_op jit(solution)/shard_map/ppermute | solution.py:38
  89.9 5.8 %collective-permute-done.19 = bf16[128,512]{1,0:T(8,128)(2,1)S(1)} collective-permute-done((bf16[128,512]{1,0:T(8,128)(2,1)S(1)}, bf16[128,512]{1,0:T(8,128)(2,1)S(1)}, u32[]{:S(2)}, u32[]{:S(2)}) %collective-permute-start.19) | collective-permute-done | bytes 131104 | tf_op jit(solution)/shard_map/ppermute | solution.py:38
  96.5 4.3 %collective-permute-done.20.refs_1_ = bf16[128,512]{1,0:T(8,128)(2,1)S(1)} collective-permute-done((bf16[128,512]{1,0:T(8,128)(2,1)S(1)}, bf16[128,512]{1,0:T(8,128)(2,1)S(1)}, u32[]{:S(2)}, u32[]{:S(2)}) %collective-permute-start.20) | collective-permute-done | bytes 131104 | tf_op jit(solution)/shard_map/ppermute | solution.py:38
  100.8 4.6 %collective-permute-done.29.refs_1_ = bf16[128,2048]{1,0:T(8,128)(2,1)S(1)} collective-permute-done((bf16[128,2048]{1,0:T(8,128)(2,1)S(1)}, bf16[128,2048]{1,0:T(8,128)(2,1)S(1)}, u32[]{:S(2)}, u32[]{:S(2)}) %collective-permute-start.29) | collective-permute-done | bytes 524320 | tf_op jit(solution)/shard_map/ppermute | solution.py:38
  105.3 1.4 dispatch.3
  106.8 0.9 copy-done.7
  107.7 1.3 collective-permute-start.24
  109.0 2.7 %collective-permute-start.22 = (bf16[2,128,512]{2,1,0:T(8,128)(2,1)S(1)}, bf16[2,128,512]{2,1,0:T(8,128)(2,1)S(1)}, u32[]{:S(2)}, u32[]{:S(2)}) collective-permute-start(bf16[2,128,512]{2,1,0:T(8,128)(2,1)S(1)} %pad_maximum_fusion), channel_id=1, source_target_pairs={{0,16},{8,24},{16,0},{24,8},{1,17},{9,25},{17,1},{25,9},{2,18},{10... | collective-permute-start | bytes 786440 | tf_op jit(solution)/shard_map/ppermute | solution.py:38
  111.6 0.9 copy-done.21
  112.5 7.3 %expert_slope.1.slope_ref = bf16[384,1024]{1,0:T(8,128)(2,1)} custom-call(s32[1]{0:T(128)} %bitcast.27.here_ref, bf16[192,2048]{1,0:T(8,128)(2,1)} %copy-done.7, bf16[192,2048]{1,0:T(8,128)(2,1)} %copy-done.21, f32[192,1024]{1,0:T(8,128)} %get-tuple-element.92.rise_own, f32[192,1024]{1,0:T(8,128)} %get-tuple-element.93.rise_core, bf16[1024,2048]{1,0:T(8,128)(2,1)} %bitcast.84), custom_call_target="tpu_custom_call" | custom-call | flops 1 | bytes 1 | tf_op jit(solution)/shard_map/expert_slope/pallas_call | solution.py:478
  119.9 5.8 %expert_backward.1 = (bf16[2,384,512]{2,1,0:T(8,128)(2,1)}, f32[384,512]{1,0:T(8,128)}, f32[384,512]{1,0:T(8,128)}) custom-call(s32[1]{0:T(128)} %bitcast.7.section_ref, bf16[384,1024]{1,0:T(8,128)(2,1)} %expert_slope.1.slope_ref, bf16[2048,1024]{1,0:T(8,128)(2,1)} %bitcast.83), custom_call_target="tpu_custom_call" | custom-call | flops 1 | bytes 1 | tf_op jit(solution)/shard_map/expert_backward/pallas_call | solution.py:520
  126.8 1.1 collective-permute-start.25
  127.9 1.2 collective-permute-start.27
  131.0 3.0 %collective-permute-done.24.refs_5_ = bf16[1024,512]{1,0:T(8,128)(2,1)} collective-permute-done((bf16[1024,512]{1,0:T(8,128)(2,1)}, bf16[1024,512]{1,0:T(8,128)(2,1)}, u32[]{:S(2)}, u32[]{:S(2)}) %collective-permute-start.24) | collective-permute-done | bytes 1048608 | tf_op jit(solution)/shard_map/ppermute | solution.py:38
  134.0 5.4 %attend_sentence.2.mine_ref = bf16[128,512]{1,0:T(8,128)(2,1)} custom-call(s32[3]{0:T(128)} %pad_add_fusion.1.place_ref, s32[2]{0:T(128)} %lengths_ref.3, bf16[128,512]{1,0:T(8,128)(2,1)} %get-tuple-element.87.query_ref, bf16[128,2048]{1,0:T(8,128)(2,1)} %copy-done.3, bf16[128,2048]{1,0:T(8,128)(2,1)} %collective-permute-done.23.refs_1_, ...), custom_call_target="tpu_custom_call" | custom-call | flops 1 | bytes 1 | tf_op jit(solution)/shard_map/attend_sentence/pallas_call | solution.py:380
  139.4 1.9 %collective-permute-done.25.refs_0_ = bf16[128,2048]{1,0:T(8,128)(2,1)} collective-permute-done((bf16[128,2048]{1,0:T(8,128)(2,1)S(1)}, bf16[128,2048]{1,0:T(8,128)(2,1)}, u32[]{:S(2)}, u32[]{:S(2)}) %collective-permute-start.25) | collective-permute-done | bytes 524320 | tf_op jit(solution)/shard_map/ppermute | solution.py:38
  141.3 4.3 %collective-permute-done.32 = bf16[2,384,512]{2,1,0:T(8,128)(2,1)} collective-permute-done((bf16[2,384,512]{2,1,0:T(8,128)(2,1)}, bf16[2,384,512]{2,1,0:T(8,128)(2,1)}, u32[]{:S(2)}, u32[]{:S(2)}) %collective-permute-start.32) | collective-permute-done | bytes 786464 | tf_op jit(solution)/shard_map/ppermute | solution.py:38
  145.6 1.1 fusion.34
  146.7 1.2 collective-permute-start.33
  149.2 5.5 %attend_sentence.3.done_ref = bf16[128,512]{1,0:T(8,128)(2,1)} custom-call(s32[3]{0:T(128)} %pad_add_fusion.3.place_ref, s32[2]{0:T(128)} %lengths_ref.3, bf16[128,512]{1,0:T(8,128)(2,1)} %get-tuple-element.86.query_ref, bf16[128,2048]{1,0:T(8,128)(2,1)} %collective-permute-done.25.refs_0_, bf16[128,2048]{1,0:T(8,128)(2,1)} %copy-done.24, ...), custom_call_target="tpu_custom_call" | custom-call | flops 1 | bytes 1 | tf_op jit(solution)/shard_map/attend_sentence/pallas_call | solution.py:380
  154.7 1.3 collective-permute-done.27.other_ref
  156.1 0.9 copy-done.9
  157.0 2.0 %project.1 = (bf16[256,512]{1,0:T(8,128)(2,1)S(1)}, bf16[256,512]{1,0:T(8,128)(2,1)S(1)}, f32[256,512]{1,0:T(8,128)S(1)}, f32[256,512]{1,0:T(8,128)S(1)}) custom-call(s32[3]{0:T(128)S(1)} %copy-done.16, bf16[128,512]{1,0:T(8,128)(2,1)S(1)} %copy-done.8, bf16[128,512]{1,0:T(8,128)(2,1)S(1)} %copy-done.9, bf16[512,1024]{1,0:T(8,128)(2,1)S(1)} %bitcast.80, ...), custom_call_target="tpu_custom_call" | custom-call | flops 1 | bytes 1 | tf_op jit(solution)/shard_map/project/pallas_call | solution.py:431
  159.5 6.6 %collective-permute-done.33 = bf16[384,512]{1,0:T(8,128)(2,1)S(1)} collective-permute-done((bf16[384,512]{1,0:T(8,128)(2,1)S(1)}, bf16[384,512]{1,0:T(8,128)(2,1)S(1)}, u32[]{:S(2)}, u32[]{:S(2)}) %collective-permute-start.33) | collective-permute-done | bytes 393248 | tf_op jit(solution)/shard_map/ppermute | solution.py:38
  166.2 1.1 collective-permute-start.35
  167.2 2.0 %fusion.33 = bf16[384,512]{1,0:T(8,128)(2,1)} fusion(f32[384,512]{1,0:T(8,128)S(1)} %copy-done.23, bf16[384,512]{1,0:T(8,128)(2,1)S(1)} %collective-permute-done.33, bf16[2,384,512]{2,1,0:T(8,128)(2,1)} %collective-permute-done.32), kind=kLoop, calls=%fused_computation.45 | loop fusion | flops 983040 | bytes 1966080 | tf_op jit(solution)/shard_map/convert_element_type | solution.py:710
  169.2 3.5 %all-to-all-start = ((bf16[8,48,512]{2,1,0:T(8,128)(2,1)}), bf16[8,48,512]{2,1,0:T(8,128)(2,1)S(1)}, u32[]{:S(2)}, u32[]{:S(2)}) async-start(bf16[8,48,512]{2,1,0:T(8,128)(2,1)} %bitcast.31), calls=%async_computation | async-start | bytes 786432 | tf_op jit(solution)/shard_map/all_to_all | solution.py:142
  172.9 1.6 collective-permute-done.35
  174.4 1.8 fusion.46
  176.2 4.7 %all-to-all-done = bf16[8,48,512]{2,1,0:T(8,128)(2,1)S(1)} async-done(((bf16[8,48,512]{2,1,0:T(8,128)(2,1)}), bf16[8,48,512]{2,1,0:T(8,128)(2,1)S(1)}, u32[]{:S(2)}, u32[]{:S(2)}) %all-to-all-start) | async-done | bytes 393248 | tf_op jit(solution)/shard_map/all_to_all | solution.py:142
  180.9 1.0 combine.3
  (115 shorter events, 17.9 us)
Async XLA Ops:
  0.6 42.5 %copy-start = (bf16[1,1024,512]{2,1,0:T(8,128)(2,1)S(1)}, bf16[1,1024,512]{2,1,0:T(8,128)(2,1)}, u32[]{:S(2)}) copy-start(bf16[1,1024,512]{2,1,0:T(8,128)(2,1)} %param.26) | copy-start | bytes 3145732
  0.7 1.3 copy-start.4
  2.0 0.7 copy-start.14
  3.4 0.8 copy-start.17
  4.2 8.3 %collective-permute-start.3 = (s32[2,128]{1,0:T(2,128)}, s32[2,128]{1,0:T(2,128)S(1)}, u32[]{:S(2)}, u32[]{:S(2)}) collective-permute-start(s32[2,128]{1,0:T(2,128)} %bitcast.88), channel_id=1, source_target_pairs={{0,2},{1,3},{2,0},{3,1},{4,6},{5,7},{6,4},{7,5},{8,10},{9,11},{10,... | collective-permute-start | bytes 3080 | tf_op jit(solution)/shard_map/ppermute | solution.py:38
  7.2 5.3 %collective-permute-start.4 = (s32[2,128]{1,0:T(2,128)}, s32[2,128]{1,0:T(2,128)S(1)}, u32[]{:S(2)}, u32[]{:S(2)}) collective-permute-start(s32[2,128]{1,0:T(2,128)} %bitcast.89), channel_id=1, source_target_pairs={{0,4},{4,0},{1,5},{5,1},{2,6},{6,2},{3,7},{7,3},{8,12},{12,8},{9,1... | collective-permute-start | bytes 3080 | tf_op jit(solution)/shard_map/ppermute | solution.py:38
  8.7 13.3 %collective-permute-start = (bf16[128,2048]{1,0:T(8,128)(2,1)}, bf16[128,2048]{1,0:T(8,128)(2,1)S(1)}, u32[]{:S(2)}, u32[]{:S(2)}) collective-permute-start(bf16[128,2048]{1,0:T(8,128)(2,1)} %tokens_ref.1), channel_id=1, source_target_pairs={{0,4},{4,0},{1,5},{5,1},{2,6},{6,2},{3,7},{7,3},{8,12},{12,8},{9,1... | collective-permute-start | bytes 1572872 | tf_op jit(solution)/shard_map/ppermute | solution.py:38
  9.2 18.0 %collective-permute-start.6 = (bf16[128,2048]{1,0:T(8,128)(2,1)}, bf16[128,2048]{1,0:T(8,128)(2,1)S(1)}, u32[]{:S(2)}, u32[]{:S(2)}) collective-permute-start(bf16[128,2048]{1,0:T(8,128)(2,1)} %tokens_ref.1), channel_id=1, source_target_pairs={{0,2},{1,3},{2,0},{3,1},{4,6},{5,7},{6,4},{7,5},{8,10},{9,11},{10,... | collective-permute-start | bytes 1572872 | tf_op jit(solution)/shard_map/ppermute | solution.py:38
  22.0 12.2 %collective-permute-start.7 = (bf16[128,2048]{1,0:T(8,128)(2,1)S(1)}, bf16[128,2048]{1,0:T(8,128)(2,1)S(1)}, u32[]{:S(2)}, u32[]{:S(2)}) collective-permute-start(bf16[128,2048]{1,0:T(8,128)(2,1)S(1)} %collective-permute-done.refs_2_), channel_id=1, source_target_pairs={{0,2},{1,3},{2,0},{3,1},{4,6},{5,7},{6,4},{7,5},{8,10},{9,11},{10,... | collective-permute-start | bytes 1572872 | tf_op jit(solution)/shard_map/ppermute | solution.py:38
  22.6 3.8 %collective-permute-start.5 = (s32[2,128]{1,0:T(2,128)S(1)}, s32[2,128]{1,0:T(2,128)S(1)}, u32[]{:S(2)}, u32[]{:S(2)}) collective-permute-start(s32[2,128]{1,0:T(2,128)S(1)} %collective-permute-done.3), channel_id=1, source_target_pairs={{0,4},{4,0},{1,5},{5,1},{2,6},{6,2},{3,7},{7,3},{8,12},{12,8},{9,1... | collective-permute-start | bytes 3080 | tf_op jit(solution)/shard_map/ppermute | solution.py:38
  22.9 16.9 %collective-permute-start.1 = (bf16[256,1024]{1,0:T(8,128)(2,1)}, bf16[256,1024]{1,0:T(8,128)(2,1)}, u32[]{:S(2)}, u32[]{:S(2)}) collective-permute-start(bf16[256,1024]{1,0:T(8,128)(2,1)} %copy-done.17), channel_id=1, source_target_pairs={{0,4},{4,0},{1,5},{5,1},{2,6},{6,2},{3,7},{7,3},{8,12},{12,8},{9,1... | collective-permute-start | bytes 1572872 | tf_op jit(solution)/shard_map/ppermute | solution.py:38
  34.2 1.0 copy-start.1
  35.2 5.4 %copy-start.19 = (bf16[1,1024,2048]{2,1,0:T(8,128)(2,1)S(1)}, bf16[1,1024,2048]{2,1,0:T(8,128)(2,1)}, u32[]{:S(2)}) copy-start(bf16[1,1024,2048]{2,1,0:T(8,128)(2,1)} %param.20) | copy-start | bytes 12582916
  39.7 12.6 %copy-start.18 = (bf16[1,2048,1024]{2,1,0:T(8,128)(2,1)S(1)}, bf16[1,2048,1024]{2,1,0:T(8,128)(2,1)}, u32[]{:S(2)}) copy-start(bf16[1,2048,1024]{2,1,0:T(8,128)(2,1)} %param.19) | copy-start | bytes 12582916
  39.7 12.6 %collective-permute-start.9 = (bf16[192,2048]{1,0:T(8,128)(2,1)S(1)}, bf16[192,2048]{1,0:T(8,128)(2,1)S(1)}, u32[]{:S(2)}, u32[]{:S(2)}) collective-permute-start(bf16[192,2048]{1,0:T(8,128)(2,1)S(1)} %get-tuple-element.47), channel_id=1, source_target_pairs={{0,1},{1,0},{2,3},{3,2},{4,5},{5,4},{6,7},{7,6},{8,9},{9,8},{10,11... | collective-permute-start | bytes 2359304 | tf_op jit(solution)/shard_map/ppermute | solution.py:38
  39.8 10.9 %collective-permute-start.10 = (bf16[64,2048]{1,0:T(8,128)(2,1)}, bf16[64,2048]{1,0:T(8,128)(2,1)S(1)}, u32[]{:S(2)}, u32[]{:S(2)}) collective-permute-start(bf16[64,2048]{1,0:T(8,128)(2,1)} %constant_dynamic-slice_fusion.1), channel_id=1, source_target_pairs={{0,4},{4,0},{1,5},{5,1},{2,6},{6,2},{3,7},{7,3},{8,12},{12,8},{9,1... | collective-permute-start | bytes 786440 | tf_op jit(solution)/shard_map/ppermute | solution.py:38
  42.6 7.0 %collective-permute-start.8 = (bf16[48,2048]{1,0:T(8,128)(2,1)S(1)}, bf16[48,2048]{1,0:T(8,128)(2,1)S(1)}, u32[]{:S(2)}, u32[]{:S(2)}) collective-permute-start(bf16[48,2048]{1,0:T(8,128)(2,1)S(1)} %get-tuple-element.85), channel_id=1, source_target_pairs={{0,2},{1,3},{2,0},{3,1},{4,6},{5,7},{6,4},{7,5},{8,10},{9,11},{10,... | collective-permute-start | bytes 589832 | tf_op jit(solution)/shard_map/ppermute | solution.py:223
  44.6 14.4 %collective-permute-start.2 = (bf16[256,512]{1,0:T(8,128)(2,1)S(1)}, bf16[256,512]{1,0:T(8,128)(2,1)S(1)}, u32[]{:S(2)}, u32[]{:S(2)}) collective-permute-start(bf16[256,512]{1,0:T(8,128)(2,1)S(1)} %convolution_convert_fusion.2), channel_id=1, source_target_pairs={{0,4},{4,0},{1,5},{5,1},{2,6},{6,2},{3,7},{7,3},{8,12},{12,8},{9,1... | collective-permute-start | bytes 786440 | tf_op jit(solution)/shard_map/ppermute | solution.py:38
  45.9 20.4 %collective-permute-start.13 = (bf16[48,2048]{1,0:T(8,128)(2,1)}, bf16[48,2048]{1,0:T(8,128)(2,1)S(1)}, u32[]{:S(2)}, u32[]{:S(2)}) collective-permute-start(bf16[48,2048]{1,0:T(8,128)(2,1)} %get-tuple-element.83), channel_id=1, source_target_pairs={{0,4},{1,5},{2,6},{3,7},{4,0},{5,1},{6,2},{7,3},{8,12},{9,13},{10,... | collective-permute-start | bytes 589832 | tf_op jit(solution)/shard_map/ppermute | solution.py:223
  49.5 17.4 %collective-permute-start.14 = (bf16[48,2048]{1,0:T(8,128)(2,1)}, bf16[48,2048]{1,0:T(8,128)(2,1)}, u32[]{:S(2)}, u32[]{:S(2)}) collective-permute-start(bf16[48,2048]{1,0:T(8,128)(2,1)} %get-tuple-element.82), channel_id=1, source_target_pairs={{0,6},{1,7},{2,4},{3,5},{4,2},{5,3},{6,0},{7,1},{8,14},{9,15},{10,... | collective-permute-start | bytes 589832 | tf_op jit(solution)/shard_map/ppermute | solution.py:223
  50.7 13.5 %collective-permute-start.12 = (bf16[64,2048]{1,0:T(8,128)(2,1)S(1)}, bf16[64,2048]{1,0:T(8,128)(2,1)S(1)}, u32[]{:S(2)}, u32[]{:S(2)}) collective-permute-start(bf16[64,2048]{1,0:T(8,128)(2,1)S(1)} %collective-permute-done.10), channel_id=1, source_target_pairs={{0,8},{8,0},{16,24},{24,16},{1,9},{9,1},{17,25},{25,17},{2,10},{10... | collective-permute-start | bytes 786440 | tf_op jit(solution)/shard_map/ppermute | solution.py:38
  54.5 11.7 %copy-start.27 = (f32[128,2]{0,1:T(2,128)S(1)}, f32[128,2]{0,1:T(2,128)}, u32[]{:S(2)}) copy-start(f32[128,2]{0,1:T(2,128)} %param.17) | copy-start | bytes 3076
  54.5 27.5 %copy-start.5 = (bf16[128,2048]{1,0:T(8,128)(2,1)S(1)}, bf16[128,2048]{1,0:T(8,128)(2,1)}, u32[]{:S(2)}) copy-start(bf16[128,2048]{1,0:T(8,128)(2,1)} %refs_0_.3) | copy-start | bytes 1572868
  59.0 4.3 %copy-start.25 = (bf16[256,512]{1,0:T(8,128)(2,1)}, bf16[256,512]{1,0:T(8,128)(2,1)S(1)}, u32[]{:S(2)}) copy-start(bf16[256,512]{1,0:T(8,128)(2,1)S(1)} %collective-permute-done.2) | copy-start | bytes 786436
  59.9 2.7 %collective-permute-start.11 = (bf16[48,2048]{1,0:T(8,128)(2,1)S(1)}, bf16[48,2048]{1,0:T(8,128)(2,1)S(1)}, u32[]{:S(2)}, u32[]{:S(2)}) collective-permute-start(bf16[48,2048]{1,0:T(8,128)(2,1)S(1)} %get-tuple-element.81), channel_id=1, source_target_pairs={{0,1},{1,0},{2,3},{3,2},{4,5},{5,4},{6,7},{7,6},{8,9},{9,8},{10,11... | collective-permute-start | bytes 589832 | tf_op jit(solution)/shard_map/ppermute | solution.py:223
  59.9 7.0 %collective-permute-start.15 = (bf16[48,2048]{1,0:T(8,128)(2,1)}, bf16[48,2048]{1,0:T(8,128)(2,1)}, u32[]{:S(2)}, u32[]{:S(2)}) collective-permute-start(bf16[48,2048]{1,0:T(8,128)(2,1)} %get-tuple-element.80), channel_id=1, source_target_pairs={{0,3},{1,2},{2,1},{3,0},{4,7},{5,6},{6,5},{7,4},{8,11},{9,10},{10,... | collective-permute-start | bytes 589832 | tf_op jit(solution)/shard_map/ppermute | solution.py:223
  63.3 11.5 %collective-permute-start.16 = (bf16[48,2048]{1,0:T(8,128)(2,1)}, bf16[48,2048]{1,0:T(8,128)(2,1)}, u32[]{:S(2)}, u32[]{:S(2)}) collective-permute-start(bf16[48,2048]{1,0:T(8,128)(2,1)} %get-tuple-element.79), channel_id=1, source_target_pairs={{0,5},{1,4},{2,7},{3,6},{4,1},{5,0},{6,3},{7,2},{8,13},{9,12},{10,... | collective-permute-start | bytes 589832 | tf_op jit(solution)/shard_map/ppermute | solution.py:223
  64.2 10.6 %collective-permute-start.17 = (bf16[48,2048]{1,0:T(8,128)(2,1)}, bf16[48,2048]{1,0:T(8,128)(2,1)}, u32[]{:S(2)}, u32[]{:S(2)}) collective-permute-start(bf16[48,2048]{1,0:T(8,128)(2,1)} %get-tuple-element.78), channel_id=1, source_target_pairs={{0,7},{1,6},{2,5},{3,4},{4,3},{5,2},{6,1},{7,0},{8,15},{9,14},{10,... | collective-permute-start | bytes 589832 | tf_op jit(solution)/shard_map/ppermute | solution.py:223
  74.9 0.9 copy-start.11
  75.8 0.9 copy-start.13
  78.8 8.4 %collective-permute-start.18 = (bf16[2,128,512]{2,1,0:T(8,128)(2,1)S(1)}, bf16[2,128,512]{2,1,0:T(8,128)(2,1)S(1)}, u32[]{:S(2)}, u32[]{:S(2)}) collective-permute-start(bf16[2,128,512]{2,1,0:T(8,128)(2,1)S(1)} %get-tuple-element.55), channel_id=1, source_target_pairs={{0,8},{8,0},{16,24},{24,16},{1,9},{9,1},{17,25},{25,17},{2,10},{10... | collective-permute-start | bytes 786440 | tf_op jit(solution)/shard_map/ppermute | solution.py:38
  80.4 20.3 %collective-permute-start.30 = (bf16[128,2048]{1,0:T(8,128)(2,1)S(1)}, bf16[128,2048]{1,0:T(8,128)(2,1)S(1)}, u32[]{:S(2)}, u32[]{:S(2)}) collective-permute-start(bf16[128,2048]{1,0:T(8,128)(2,1)S(1)} %constant_dynamic-update-slice_fusion.refs_2_), channel_id=1, source_target_pairs={{0,2},{1,3},{2,0},{3,1},{4,6},{5,7},{6,4},{7,5},{8,10},{9,11},{10,... | collective-permute-start | bytes 1572872 | tf_op jit(solution)/shard_map/ppermute | solution.py:38
  81.9 23.4 %collective-permute-start.29 = (bf16[128,2048]{1,0:T(8,128)(2,1)S(1)}, bf16[128,2048]{1,0:T(8,128)(2,1)S(1)}, u32[]{:S(2)}, u32[]{:S(2)}) collective-permute-start(bf16[128,2048]{1,0:T(8,128)(2,1)S(1)} %copy-done.5), channel_id=1, source_target_pairs={{0,2},{1,3},{2,0},{3,1},{4,6},{5,7},{6,4},{7,5},{8,10},{9,11},{10,... | collective-permute-start | bytes 1572872 | tf_op jit(solution)/shard_map/ppermute | solution.py:38
  82.5 26.5 %collective-permute-start.21 = (bf16[1024,512]{1,0:T(8,128)(2,1)}, bf16[1024,512]{1,0:T(8,128)(2,1)S(1)}, u32[]{:S(2)}, u32[]{:S(2)}) collective-permute-start(bf16[1024,512]{1,0:T(8,128)(2,1)} %bitcast.85), channel_id=1, source_target_pairs={{0,4},{4,0},{1,5},{5,1},{2,6},{6,2},{3,7},{7,3},{8,12},{12,8},{9,1... | collective-permute-start | bytes 3145736 | tf_op jit(solution)/shard_map/ppermute | solution.py:38
  87.2 8.5 %collective-permute-start.19 = (bf16[128,512]{1,0:T(8,128)(2,1)S(1)}, bf16[128,512]{1,0:T(8,128)(2,1)S(1)}, u32[]{:S(2)}, u32[]{:S(2)}) collective-permute-start(bf16[128,512]{1,0:T(8,128)(2,1)S(1)} %fusion.47), channel_id=1, source_target_pairs={{0,16},{8,24},{16,0},{24,8},{1,17},{9,25},{17,1},{25,9},{2,18},{10... | collective-permute-start | bytes 393224 | tf_op jit(solution)/shard_map/ppermute | solution.py:38
  95.7 5.0 %collective-permute-start.20 = (bf16[128,512]{1,0:T(8,128)(2,1)S(1)}, bf16[128,512]{1,0:T(8,128)(2,1)S(1)}, u32[]{:S(2)}, u32[]{:S(2)}) collective-permute-start(bf16[128,512]{1,0:T(8,128)(2,1)S(1)} %fusion.49.refs_0_), channel_id=1, source_target_pairs={{0,8},{8,0},{16,24},{24,16},{1,9},{9,1},{17,25},{25,17},{2,10},{10... | collective-permute-start | bytes 393224 | tf_op jit(solution)/shard_map/ppermute | solution.py:38
  106.8 0.9 copy-start.7
  107.7 4.0 %collective-permute-start.31 = (bf16[192,2048]{1,0:T(8,128)(2,1)S(1)}, bf16[192,2048]{1,0:T(8,128)(2,1)S(1)}, u32[]{:S(2)}, u32[]{:S(2)}) collective-permute-start(bf16[192,2048]{1,0:T(8,128)(2,1)S(1)} %get-tuple-element.69), channel_id=1, source_target_pairs={{0,1},{1,0},{2,3},{3,2},{4,5},{5,4},{6,7},{7,6},{8,9},{9,8},{10,11... | collective-permute-start | bytes 2359304 | tf_op jit(solution)/shard_map/ppermute | solution.py:38
  107.7 26.3 %collective-permute-start.24 = (bf16[1024,512]{1,0:T(8,128)(2,1)}, bf16[1024,512]{1,0:T(8,128)(2,1)}, u32[]{:S(2)}, u32[]{:S(2)}) collective-permute-start(bf16[1024,512]{1,0:T(8,128)(2,1)} %bitcast.24.refs_4_), channel_id=1, source_target_pairs={{0,4},{4,0},{1,5},{5,1},{2,6},{6,2},{3,7},{7,3},{8,12},{12,8},{9,1... | collective-permute-start | bytes 3145736 | tf_op jit(solution)/shard_map/ppermute | solution.py:38
  109.0 10.9 %copy-start.20 = (bf16[1024,512]{1,0:T(8,128)(2,1)}, bf16[1024,512]{1,0:T(8,128)(2,1)S(1)}, u32[]{:S(2)}) copy-start(bf16[1024,512]{1,0:T(8,128)(2,1)S(1)} %collective-permute-done.21.refs_3_) | copy-start | bytes 3145732
  109.0 17.3 %collective-permute-start.22 = (bf16[2,128,512]{2,1,0:T(8,128)(2,1)S(1)}, bf16[2,128,512]{2,1,0:T(8,128)(2,1)S(1)}, u32[]{:S(2)}, u32[]{:S(2)}) collective-permute-start(bf16[2,128,512]{2,1,0:T(8,128)(2,1)S(1)} %pad_maximum_fusion), channel_id=1, source_target_pairs={{0,16},{8,24},{16,0},{24,8},{1,17},{9,25},{17,1},{25,9},{2,18},{10... | collective-permute-start | bytes 786440 | tf_op jit(solution)/shard_map/ppermute | solution.py:38
  111.6 0.9 copy-start.21
  119.9 6.4 %copy-start.2 = (bf16[128,2048]{1,0:T(8,128)(2,1)S(1)}, bf16[128,2048]{1,0:T(8,128)(2,1)}, u32[]{:S(2)}) copy-start(bf16[128,2048]{1,0:T(8,128)(2,1)} %tokens_ref.1) | copy-start | bytes 1572868
  119.9 6.4 %copy-start.15 = (f32[2048]{0:T(1024)S(1)}, f32[2048]{0:T(1024)}, u32[]{:S(2)}) copy-start(f32[2048]{0:T(1024)} %param.21) | copy-start | bytes 24580
  119.9 8.0 %copy-start.6 = (bf16[1,512,1024]{2,1,0:T(8,128)(2,1)S(1)}, bf16[1,512,1024]{2,1,0:T(8,128)(2,1)}, u32[]{:S(2)}) copy-start(bf16[1,512,1024]{2,1,0:T(8,128)(2,1)} %param.29) | copy-start | bytes 3145732
  119.9 9.9 %copy-start.26 = (bf16[256,512]{1,0:T(8,128)(2,1)S(1)}, bf16[256,512]{1,0:T(8,128)(2,1)}, u32[]{:S(2)}) copy-start(bf16[256,512]{1,0:T(8,128)(2,1)} %copy-done.25) | copy-start | bytes 786436
  125.8 19.8 %collective-permute-start.32 = (bf16[2,384,512]{2,1,0:T(8,128)(2,1)}, bf16[2,384,512]{2,1,0:T(8,128)(2,1)}, u32[]{:S(2)}, u32[]{:S(2)}) collective-permute-start(bf16[2,384,512]{2,1,0:T(8,128)(2,1)} %get-tuple-element.71), channel_id=1, source_target_pairs={{0,8},{8,0},{16,24},{24,16},{1,9},{9,1},{17,25},{25,17},{2,10},{10... | collective-permute-start | bytes 2359304 | tf_op jit(solution)/shard_map/ppermute | solution.py:38
  126.8 7.2 %copy-start.3 = (bf16[128,2048]{1,0:T(8,128)(2,1)}, bf16[128,2048]{1,0:T(8,128)(2,1)S(1)}, u32[]{:S(2)}) copy-start(bf16[128,2048]{1,0:T(8,128)(2,1)S(1)} %memory.1.refs_0_) | copy-start | bytes 1572868
  126.8 7.2 %collective-permute-start.23 = (bf16[128,2048]{1,0:T(8,128)(2,1)S(1)}, bf16[128,2048]{1,0:T(8,128)(2,1)}, u32[]{:S(2)}, u32[]{:S(2)}) collective-permute-start(bf16[128,2048]{1,0:T(8,128)(2,1)S(1)} %memory.1.refs_0_), channel_id=1, source_target_pairs={{0,1},{1,0},{2,3},{3,2},{4,5},{5,4},{6,7},{7,6},{8,9},{9,8},{10,11... | collective-permute-start | bytes 1572872 | tf_op jit(solution)/shard_map/ppermute | solution.py:38
  126.8 14.4 %collective-permute-start.25 = (bf16[128,2048]{1,0:T(8,128)(2,1)S(1)}, bf16[128,2048]{1,0:T(8,128)(2,1)}, u32[]{:S(2)}, u32[]{:S(2)}) collective-permute-start(bf16[128,2048]{1,0:T(8,128)(2,1)S(1)} %memory.1.refs_0_), channel_id=1, source_target_pairs={{0,2},{1,3},{2,0},{3,1},{4,6},{5,7},{6,4},{7,5},{8,10},{9,11},{10,... | collective-permute-start | bytes 1572872 | tf_op jit(solution)/shard_map/ppermute | solution.py:38
  127.9 28.1 %collective-permute-start.27 = (bf16[512,1024]{1,0:T(8,128)(2,1)S(1)}, bf16[512,1024]{1,0:T(8,128)(2,1)}, u32[]{:S(2)}, u32[]{:S(2)}) collective-permute-start(bf16[512,1024]{1,0:T(8,128)(2,1)S(1)} %bitcast.79), channel_id=1, source_target_pairs={{0,4},{4,0},{1,5},{5,1},{2,6},{6,2},{3,7},{7,3},{8,12},{12,8},{9,1... | collective-permute-start | bytes 3145736 | tf_op jit(solution)/shard_map/ppermute | solution.py:38
  129.8 15.7 %copy-start.22 = (f32[384,512]{1,0:T(8,128)S(1)}, f32[384,512]{1,0:T(8,128)}, u32[]{:S(2)}) copy-start(f32[384,512]{1,0:T(8,128)} %get-tuple-element.70) | copy-start | bytes 2359300
  139.4 16.7 %copy-start.8 = (bf16[128,512]{1,0:T(8,128)(2,1)S(1)}, bf16[128,512]{1,0:T(8,128)(2,1)}, u32[]{:S(2)}) copy-start(bf16[128,512]{1,0:T(8,128)(2,1)} %attend_sentence.2.mine_ref) | copy-start | bytes 393220
  139.4 16.7 %copy-start.16 = (s32[3]{0:T(128)S(1)}, s32[3]{0:T(128)}, u32[]{:S(2)}) copy-start(s32[3]{0:T(128)} %pad_add_fusion.1.place_ref) | copy-start | bytes 40
  141.3 7.1 %collective-permute-start.26 = (bf16[128,2048]{1,0:T(8,128)(2,1)}, bf16[128,2048]{1,0:T(8,128)(2,1)S(1)}, u32[]{:S(2)}, u32[]{:S(2)}) collective-permute-start(bf16[128,2048]{1,0:T(8,128)(2,1)} %collective-permute-done.25.refs_0_), channel_id=1, source_target_pairs={{0,1},{1,0},{2,3},{3,2},{4,5},{5,4},{6,7},{7,6},{8,9},{9,8},{10,11... | collective-permute-start | bytes 1572872 | tf_op jit(solution)/shard_map/ppermute | solution.py:38
  146.7 19.4 %collective-permute-start.33 = (bf16[384,512]{1,0:T(8,128)(2,1)S(1)}, bf16[384,512]{1,0:T(8,128)(2,1)S(1)}, u32[]{:S(2)}, u32[]{:S(2)}) collective-permute-start(bf16[384,512]{1,0:T(8,128)(2,1)S(1)} %fusion.34), channel_id=1, source_target_pairs={{0,16},{8,24},{16,0},{24,8},{1,17},{9,25},{17,1},{25,9},{2,18},{10... | collective-permute-start | bytes 1179656 | tf_op jit(solution)/shard_map/ppermute | solution.py:38
  148.4 0.8 copy-start.24
  149.2 18.0 %copy-start.23 = (f32[384,512]{1,0:T(8,128)S(1)}, f32[384,512]{1,0:T(8,128)}, u32[]{:S(2)}) copy-start(f32[384,512]{1,0:T(8,128)} %get-tuple-element.74) | copy-start | bytes 2359300
  156.1 0.9 copy-start.9
  157.0 15.7 %copy-start.28 = (s32[2]{0:T(128)S(1)}, s32[2]{0:T(128)}, u32[]{:S(2)}) copy-start(s32[2]{0:T(128)} %param.24) | copy-start | bytes 28
  158.9 7.1 %collective-permute-start.34 = (bf16[256,512]{1,0:T(8,128)(2,1)S(1)}, bf16[256,512]{1,0:T(8,128)(2,1)S(1)}, u32[]{:S(2)}, u32[]{:S(2)}) collective-permute-start(bf16[256,512]{1,0:T(8,128)(2,1)S(1)} %get-tuple-element.73), channel_id=1, source_target_pairs={{0,1},{1,0},{2,3},{3,2},{4,5},{5,4},{6,7},{7,6},{8,9},{9,8},{10,11... | collective-permute-start | bytes 786440 | tf_op jit(solution)/shard_map/ppermute | solution.py:38
  159.0 13.8 %collective-permute-start.28 = (bf16[256,512]{1,0:T(8,128)(2,1)S(1)}, bf16[256,512]{1,0:T(8,128)(2,1)S(1)}, u32[]{:S(2)}, u32[]{:S(2)}) collective-permute-start(bf16[256,512]{1,0:T(8,128)(2,1)S(1)} %get-tuple-element.63), channel_id=1, source_target_pairs={{0,1},{1,0},{2,3},{3,2},{4,5},{5,4},{6,7},{7,6},{8,9},{9,8},{10,11... | collective-permute-start | bytes 786440 | tf_op jit(solution)/shard_map/ppermute | solution.py:38
  166.2 8.3 %collective-permute-start.35 = (bf16[256,512]{1,0:T(8,128)(2,1)S(1)}, bf16[256,512]{1,0:T(8,128)(2,1)S(1)}, u32[]{:S(2)}, u32[]{:S(2)}) collective-permute-start(bf16[256,512]{1,0:T(8,128)(2,1)S(1)} %convert_add_fusion.3), channel_id=1, source_target_pairs={{0,2},{1,3},{2,0},{3,1},{4,6},{5,7},{6,4},{7,5},{8,10},{9,11},{10,... | collective-permute-start | bytes 786440 | tf_op jit(solution)/shard_map/ppermute | solution.py:38
  169.2 11.7 %all-to-all-start = ((bf16[8,48,512]{2,1,0:T(8,128)(2,1)}), bf16[8,48,512]{2,1,0:T(8,128)(2,1)S(1)}, u32[]{:S(2)}, u32[]{:S(2)}) async-start(bf16[8,48,512]{2,1,0:T(8,128)(2,1)} %bitcast.31), calls=%async_computation | async-start | bytes 786432 | tf_op jit(solution)/shard_map/all_to_all | solution.py:142
  (2 other events, 1.4 us)

commit v12 on v11

--- a/solution.py
+++ b/solution.py
@@ -582,21 +582,20 @@
     codes_of = expert_ids ^ here
     position = ((codes_of >> 1) + 4 * (codes_of & 1)) * capacity + rank
 
-    states = dec_states[0]
-    normed_own, asked = normed_halves(y, states, norm_gain)
-    ids_own = gate(expert_ids, asked).T
+    ids_own = expert_ids.T
     ids_x, ids_y = swap(ids_own, "dp", 2), swap(ids_own, "expert", 1)
     ids_far = swap(ids_x, "expert", 1)
-    token_far = swap(gate(token_y, ids_x, ids_y, asked), "dp", 2)
+    token_far = swap(gate(token_y, ids_x, ids_y), "dp", 2)
 
     side = lax.rem(section, 2)
     share = token_count // 2
     grad_half = lax.dynamic_slice_in_dim(out_grad, side * share, share, 0)
-    asked_here = swap(gate(asked, token_y), "expert", 1)
-    half_y = swap(gate(grad_half, asked_here), "expert", 1)
+    half_y = swap(gate(grad_half, token_y), "expert", 1)
+    states = dec_states[0]
+    normed_own, asked = normed_halves(y, states, norm_gain)
+    asked_here = swap(gate(asked, half_y), "expert", 1)
+    query_there = jnp.dot(asked_here, query_own, preferred_element_type=jnp.float32)
     other_y = swap(half_y, "section", 1)
-    query_there = jnp.dot(asked_here, query_own, preferred_element_type=jnp.float32)
-    query_back = swap(query_there.astype(jnp.bfloat16), "expert", 1)
 
     ids = jnp.stack([ids_own, ids_x, ids_y, ids_far])
     named_there = jnp.concatenate([(ids == here).any(axis=1), (ids == (here ^ 1)).any(axis=1)])
@@ -624,14 +623,14 @@
         capacity,
     )
     rows_core = swap(rows_sent, "dp", 1)
-    pre_own, part_own = forward(rows_own)
+    pre_own, part_own = forward(rows_own, other_y)
     pre_core, part_core = forward(gate(rows_core, part_own))
-    part_core = gate(part_core, query_back)
     home = send_home(part_own, near_codes, capacity) + send_home(part_core, core_codes, capacity)
     grad_y = jnp.concatenate([gate(half_y, home[4]), other_y], axis=0)
+    query_back = swap(gate(query_there.astype(jnp.bfloat16), home[5], home[6]), "expert", 1)
 
     rise_own, rise_core = slope_of(gate(pre_own, home[1])), slope_of(gate(pre_core, home[1]))
-    held_gates = gate(gate_weights, rise_own, rise_core, grad_y)
+    held_gates = gate(gate_weights, rise_own, rise_core, query_there, grad_y)
     sent_pair, first, second = combine(which_section, position, held_gates, home, sections)
     from_pair = swap(sent_pair, "section", 1)
     grad_x = swap(gate(out_grad, home[5]), "dp", 2)
@@ -665,10 +664,10 @@
         rise_core,
         weight_out,
     )
-    mixed_far = swap(jnp.stack([mixed_slice, gate(mixed_near, key_other)]), "section", 2)
     back_pair, back_first, back_second = expert_backward(
         which_section, slope, weight_in, sections
     )
+    mixed_far = swap(jnp.stack([mixed_slice, gate(mixed_near, key_other)]), "section", 2)
     slices = [mixed_slice, mixed_near, mixed_far[0], mixed_far[1]]
 
     value_other = swap(gate(value_own, mixed_near), "expert", 1)
@@ -676,7 +675,7 @@
     query_here = jnp.dot(normed_own, query_own, preferred_element_type=jnp.float32)
     query = (query_here + query_back.astype(jnp.float32)).astype(jnp.bfloat16)
 
-    memory = make_memory(which_section, tokens, slices, final_gain)
+    memory = make_memory(which_section, gate(tokens, query_back), slices, final_gain)
     out_other = swap(gate(out_own, memory), "expert", 1)
     memory_x = swap(memory, "dp", 2)
     memory_core = swap(memory, "dp", 1)

time: 183 us -> 173 us (0.945)
  waiting for transfers between devices: 73.3 us -> 60.7 us
  starting transfers between devices: 38.8 us -> 42.6 us
    ppermute x29, waiting for transfers between devices: 57.8 us -> 46.1 us  [swap(): return lax.ppermute(value, axis, [(i, i ^ mask) for i in range(size)])]
    ppermute x29, starting transfers between devices: 29.5 us -> 32.2 us  [swap(): return lax.ppermute(value, axis, [(i, i ^ mask) for i in range(size)])]
    unnamed x61 -> x59, local copies, waits for them, and re-layouts: 11.5 us -> 10.8 us
  transfers between devices with their start and end apart: 37 -> 37, of which waited for: 16 -> 15; matrix products, arithmetic and copies ran while one was open for 14% -> 15% of each run, Pallas kernels for 16% -> 17%
where the time goes in v12:
time: 173 us
  waiting for transfers between devices  60.7 us (35%)
  starting transfers between devices  42.6 us (25%)
  Pallas kernels  33 us (19%)
  local copies, waits for them, and re-layouts  15.8 us (9%)
  other arithmetic  11.2 us (6%)
  matrix products  8.25 us (5%)
    ppermute x29, waiting for transfers between devices, swap(): return lax.ppermute(value, axis, [(i, i ^ mask) for i in range(size)])  46.1 us
    ppermute x29, starting transfers between devices, swap(): return lax.ppermute(value, axis, [(i, i ^ mask) for i in range(size)])  32.2 us
    pallas_call x2, Pallas kernels, attend_sentence(): pl.pallas_call(attend_kernel, out_shape=jax.ShapeDtypeStruct(query.shape,...  10.9 us
    unnamed x59, local copies, waits for them, and re-layouts  10.8 us
    ppermute x7, waiting for transfers between devices, send_home(): lax.ppermute(block, ('expert', 'dp'), [(i, i ^ code) for i in range(size)])  9.08 us
    pallas_call x1, Pallas kernels, expert_slope(): pl.pallas_call(functools.partial(slope_kernel, codes), out_shape=jax.Shap...  7.34 us
    ppermute x7, starting transfers between devices, send_home(): lax.ppermute(block, ('expert', 'dp'), [(i, i ^ code) for i in range(size)])  6.88 us
    pallas_call x1, Pallas kernels, expert_backward(): pl.pallas_call(functools.partial(backward_kernel, split), out_shape=(jax....  5.84 us
  transfers between devices with their start and end apart: 37, of which 15 were waited for; matrix products, arithmetic and copies ran while one was open for 15% of the time, Pallas kernels for 17%

profile of v12, /device:TPU:0, one launch (start us, length us, event | category | flops | bytes accessed | tf_op | source)
XLA Modules:
  0.0 172.6 jit_solution(5789531636921790046)
XLA Ops:
  0.6 3.0 %collective-permute-start = (bf16[128,2048]{1,0:T(8,128)(2,1)}, bf16[128,2048]{1,0:T(8,128)(2,1)S(1)}, u32[]{:S(2)}, u32[]{:S(2)}) collective-permute-start(bf16[128,2048]{1,0:T(8,128)(2,1)} %tokens_ref), channel_id=1, source_target_pairs={{0,4},{4,0},{1,5},{5,1},{2,6},{6,2},{3,7},{7,3},{8,12},{12,8},{9,1... | collective-permute-start | bytes 1572872 | tf_op jit(solution)/shard_map/ppermute | solution.py:38
  3.7 1.5 collective-permute-start.3
  5.8 1.0 constant_dynamic-slice_fusion.2
  7.5 8.4 %collective-permute-done.4 = s32[2,128]{1,0:T(2,128)S(1)} collective-permute-done((s32[2,128]{1,0:T(2,128)}, s32[2,128]{1,0:T(2,128)S(1)}, u32[]{:S(2)}, u32[]{:S(2)}) %collective-permute-start.4) | collective-permute-done | bytes 1056 | tf_op jit(solution)/shard_map/ppermute | solution.py:38
  15.9 1.7 collective-permute-start.7
  17.7 1.5 collective-permute-start.1
  21.1 1.2 copy-done.4
  23.8 0.8 copy-done.15
  27.7 1.5 collective-permute-start.2
  29.3 1.6 collective-permute-start.9
  30.9 1.0 copy-done.1
  31.9 1.3 dispatch.2
  33.2 3.2 %fusion.61 = f32[192,1024]{1,0:T(8,128)S(1)} fusion(bf16[192,2048]{1,0:T(8,128)(2,1)S(1)} %get-tuple-element.47, bf16[1,2048,1024]{2,1,0:T(8,128)(2,1)} %param.19), kind=kOutput, calls=%fused_computation.101 | convolution fusion | flops 805306368 | bytes 5767168 | tf_op jit(solution)/shard_map/dot_general | solution.py:610
  36.5 1.1 convolution_convert_fusion.1
  37.6 0.8 fusion.73
  39.7 2.3 %collective-permute-start.16 = (bf16[48,2048]{1,0:T(8,128)(2,1)}, bf16[48,2048]{1,0:T(8,128)(2,1)}, u32[]{:S(2)}, u32[]{:S(2)}) collective-permute-start(bf16[48,2048]{1,0:T(8,128)(2,1)} %get-tuple-element.84), channel_id=1, source_target_pairs={{0,6},{1,7},{2,4},{3,5},{4,2},{5,3},{6,0},{7,1},{8,14},{9,15},{10,... | collective-permute-start | bytes 589832 | tf_op jit(solution)/shard_map/ppermute | solution.py:223
  42.0 4.1 %collective-permute-done.13.refs_1_ = bf16[48,2048]{1,0:T(8,128)(2,1)S(1)} collective-permute-done((bf16[48,2048]{1,0:T(8,128)(2,1)S(1)}, bf16[48,2048]{1,0:T(8,128)(2,1)S(1)}, u32[]{:S(2)}, u32[]{:S(2)}) %collective-permute-start.13) | collective-permute-done | bytes 196640 | tf_op jit(solution)/shard_map/ppermute | solution.py:223
  46.1 1.2 fusion.1
  47.3 1.0 fusion.59
  48.3 1.1 convolution_convert_fusion
  49.4 0.8 fusion.72
  51.1 2.1 %fusion.10 = (f32[192,1024]{1,0:T(8,128)}, f32[192,1024]{1,0:T(8,128)}) fusion(f32[192,1024]{1,0:T(8,128)S(1)} %fusion.61, f32[192,1024]{1,0:T(8,128)S(1)} %fusion.59), kind=kLoop, calls=%fused_computation.20 | loop fusion | flops 6684672 | bytes 3145728 | tf_op jit(solution)/shard_map/transpose(jvp())/add_any | solution.py:616
  53.9 2.5 %collective-permute-start.17 = (bf16[48,2048]{1,0:T(8,128)(2,1)}, bf16[48,2048]{1,0:T(8,128)(2,1)}, u32[]{:S(2)}, u32[]{:S(2)}) collective-permute-start(bf16[48,2048]{1,0:T(8,128)(2,1)} %get-tuple-element.80), channel_id=1, source_target_pairs={{0,7},{1,6},{2,5},{3,4},{4,3},{5,2},{6,1},{7,0},{8,15},{9,14},{10,... | collective-permute-start | bytes 589832 | tf_op jit(solution)/shard_map/ppermute | solution.py:223
  56.3 1.0 constant_dynamic-update-slice_fusion.1
  57.5 5.0 %collective-permute-done.11.refs_6_ = bf16[48,2048]{1,0:T(8,128)(2,1)} collective-permute-done((bf16[48,2048]{1,0:T(8,128)(2,1)}, bf16[48,2048]{1,0:T(8,128)(2,1)}, u32[]{:S(2)}, u32[]{:S(2)}) %collective-permute-start.11) | collective-permute-done | bytes 196640 | tf_op jit(solution)/shard_map/ppermute | solution.py:223
  62.5 0.9 copy-done.11
  63.4 2.1 %combine.2 = (bf16[2,128,512]{2,1,0:T(8,128)(2,1)S(1)}, f32[128,512]{1,0:T(8,128)S(1)}, f32[128,512]{1,0:T(8,128)S(1)}) custom-call(s32[1]{0:T(128)} %bitcast.7.section_ref, s32[128,2]{1,0:T(8,128)S(1)} %get-tuple-element.93.position_ref, f32[128,2]{1,0:T(8,128)S(1)} %copy.39.gates_ref, bf16[48,2048]{1,0:T(8,128)(2,1)S(1)} %get-tuple-element.86.refs_0_, ...), custom_call_target="tpu_custom_call" | custom-call | flops 1 | bytes 1 | tf_op jit(solution)/shard_map/combine/pallas_call | solution.py:264
  65.5 0.8 collective-permute-start.18
  66.3 1.5 collective-permute-start.30
  68.3 0.9 collective-permute-start.21
  69.2 4.6 %collective-permute-done.18 = bf16[2,128,512]{2,1,0:T(8,128)(2,1)S(1)} collective-permute-done((bf16[2,128,512]{2,1,0:T(8,128)(2,1)S(1)}, bf16[2,128,512]{2,1,0:T(8,128)(2,1)S(1)}, u32[]{:S(2)}, u32[]{:S(2)}) %collective-permute-start.18) | collective-permute-done | bytes 262176 | tf_op jit(solution)/shard_map/ppermute | solution.py:38
  73.9 2.7 %collective-permute-start.19 = (bf16[128,512]{1,0:T(8,128)(2,1)S(1)}, bf16[128,512]{1,0:T(8,128)(2,1)S(1)}, u32[]{:S(2)}, u32[]{:S(2)}) collective-permute-start(bf16[128,512]{1,0:T(8,128)(2,1)S(1)} %fusion.48), channel_id=1, source_target_pairs={{0,16},{8,24},{16,0},{24,8},{1,17},{9,25},{17,1},{25,9},{2,18},{10... | collective-permute-start | bytes 393224 | tf_op jit(solution)/shard_map/ppermute | solution.py:38
  76.5 5.8 %collective-permute-done.19 = bf16[128,512]{1,0:T(8,128)(2,1)S(1)} collective-permute-done((bf16[128,512]{1,0:T(8,128)(2,1)S(1)}, bf16[128,512]{1,0:T(8,128)(2,1)S(1)}, u32[]{:S(2)}, u32[]{:S(2)}) %collective-permute-start.19) | collective-permute-done | bytes 131104 | tf_op jit(solution)/shard_map/ppermute | solution.py:38
  83.1 4.3 %collective-permute-done.20.refs_1_ = bf16[128,512]{1,0:T(8,128)(2,1)S(1)} collective-permute-done((bf16[128,512]{1,0:T(8,128)(2,1)S(1)}, bf16[128,512]{1,0:T(8,128)(2,1)S(1)}, u32[]{:S(2)}, u32[]{:S(2)}) %collective-permute-start.20) | collective-permute-done | bytes 131104 | tf_op jit(solution)/shard_map/ppermute | solution.py:38
  87.4 4.1 %collective-permute-done.29.refs_1_ = bf16[128,2048]{1,0:T(8,128)(2,1)S(1)} collective-permute-done((bf16[128,2048]{1,0:T(8,128)(2,1)S(1)}, bf16[128,2048]{1,0:T(8,128)(2,1)S(1)}, u32[]{:S(2)}, u32[]{:S(2)}) %collective-permute-start.29) | collective-permute-done | bytes 524320 | tf_op jit(solution)/shard_map/ppermute | solution.py:38
  91.6 1.4 dispatch.3
  93.0 0.9 copy-done.7
  93.9 0.9 collective-permute-start.12
  94.9 1.1 collective-permute-start.24
  96.0 2.7 %collective-permute-start.22 = (bf16[2,128,512]{2,1,0:T(8,128)(2,1)S(1)}, bf16[2,128,512]{2,1,0:T(8,128)(2,1)S(1)}, u32[]{:S(2)}, u32[]{:S(2)}) collective-permute-start(bf16[2,128,512]{2,1,0:T(8,128)(2,1)S(1)} %pad_maximum_fusion), channel_id=1, source_target_pairs={{0,16},{8,24},{16,0},{24,8},{1,17},{9,25},{17,1},{25,9},{2,18},{10... | collective-permute-start | bytes 786440 | tf_op jit(solution)/shard_map/ppermute | solution.py:38
  98.6 4.4 %collective-permute-done.12 = bf16[256,512]{1,0:T(8,128)(2,1)S(1)} collective-permute-done((bf16[256,512]{1,0:T(8,128)(2,1)S(1)}, bf16[256,512]{1,0:T(8,128)(2,1)S(1)}, u32[]{:S(2)}, u32[]{:S(2)}) %collective-permute-start.12) | collective-permute-done | bytes 262176 | tf_op jit(solution)/shard_map/ppermute | solution.py:38
  103.0 0.9 copy-done.19
  103.9 7.3 %expert_slope.1.slope_ref = bf16[384,1024]{1,0:T(8,128)(2,1)} custom-call(s32[1]{0:T(128)} %bitcast.27.here_ref, bf16[192,2048]{1,0:T(8,128)(2,1)} %copy-done.7, bf16[192,2048]{1,0:T(8,128)(2,1)} %copy-done.19, f32[192,1024]{1,0:T(8,128)} %get-tuple-element.94.rise_own, f32[192,1024]{1,0:T(8,128)} %get-tuple-element.95.rise_core, bf16[1024,2048]{1,0:T(8,128)(2,1)} %bitcast.84), custom_call_target="tpu_custom_call" | custom-call | flops 1 | bytes 1 | tf_op jit(solution)/shard_map/expert_slope/pallas_call | solution.py:478
  111.3 5.8 %expert_backward.1 = (bf16[2,384,512]{2,1,0:T(8,128)(2,1)}, f32[384,512]{1,0:T(8,128)}, f32[384,512]{1,0:T(8,128)}) custom-call(s32[1]{0:T(128)} %bitcast.7.section_ref, bf16[384,1024]{1,0:T(8,128)(2,1)} %expert_slope.1.slope_ref, bf16[2048,1024]{1,0:T(8,128)(2,1)} %bitcast.83), custom_call_target="tpu_custom_call" | custom-call | flops 1 | bytes 1 | tf_op jit(solution)/shard_map/expert_backward/pallas_call | solution.py:520
  117.2 1.0 collective-permute-start.32
  118.7 1.6 collective-permute-start.25
  120.3 1.0 collective-permute-start.27
  123.0 2.6 %collective-permute-done.24.refs_5_ = bf16[1024,512]{1,0:T(8,128)(2,1)} collective-permute-done((bf16[1024,512]{1,0:T(8,128)(2,1)}, bf16[1024,512]{1,0:T(8,128)(2,1)}, u32[]{:S(2)}, u32[]{:S(2)}) %collective-permute-start.24) | collective-permute-done | bytes 1048608 | tf_op jit(solution)/shard_map/ppermute | solution.py:38
  125.6 5.4 %attend_sentence.2.mine_ref = bf16[128,512]{1,0:T(8,128)(2,1)} custom-call(s32[3]{0:T(128)} %pad_add_fusion.1.place_ref, s32[2]{0:T(128)} %lengths_ref.3, bf16[128,512]{1,0:T(8,128)(2,1)} %get-tuple-element.89.query_ref, bf16[128,2048]{1,0:T(8,128)(2,1)} %copy-done.3, bf16[128,2048]{1,0:T(8,128)(2,1)} %collective-permute-done.23.refs_1_, ...), custom_call_target="tpu_custom_call" | custom-call | flops 1 | bytes 1 | tf_op jit(solution)/shard_map/attend_sentence/pallas_call | solution.py:380
  131.0 2.1 %collective-permute-done.25.refs_0_ = bf16[128,2048]{1,0:T(8,128)(2,1)} collective-permute-done((bf16[128,2048]{1,0:T(8,128)(2,1)S(1)}, bf16[128,2048]{1,0:T(8,128)(2,1)}, u32[]{:S(2)}, u32[]{:S(2)}) %collective-permute-start.25) | collective-permute-done | bytes 524320 | tf_op jit(solution)/shard_map/ppermute | solution.py:38
  133.1 3.2 %collective-permute-done.32 = bf16[2,384,512]{2,1,0:T(8,128)(2,1)} collective-permute-done((bf16[2,384,512]{2,1,0:T(8,128)(2,1)}, bf16[2,384,512]{2,1,0:T(8,128)(2,1)}, u32[]{:S(2)}, u32[]{:S(2)}) %collective-permute-start.32) | collective-permute-done | bytes 786464 | tf_op jit(solution)/shard_map/ppermute | solution.py:38
  136.3 1.1 fusion.35
  137.5 2.7 %collective-permute-start.33 = (bf16[384,512]{1,0:T(8,128)(2,1)S(1)}, bf16[384,512]{1,0:T(8,128)(2,1)S(1)}, u32[]{:S(2)}, u32[]{:S(2)}) collective-permute-start(bf16[384,512]{1,0:T(8,128)(2,1)S(1)} %fusion.35), channel_id=1, source_target_pairs={{0,16},{8,24},{16,0},{24,8},{1,17},{9,25},{17,1},{25,9},{2,18},{10... | collective-permute-start | bytes 1179656 | tf_op jit(solution)/shard_map/ppermute | solution.py:38
  140.7 0.8 copy-done.22
  141.5 5.5 %attend_sentence.3.done_ref = bf16[128,512]{1,0:T(8,128)(2,1)} custom-call(s32[3]{0:T(128)} %pad_add_fusion.3.place_ref, s32[2]{0:T(128)} %lengths_ref.3, bf16[128,512]{1,0:T(8,128)(2,1)} %get-tuple-element.88.query_ref, bf16[128,2048]{1,0:T(8,128)(2,1)} %collective-permute-done.25.refs_0_, bf16[128,2048]{1,0:T(8,128)(2,1)} %copy-done.22, ...), custom_call_target="tpu_custom_call" | custom-call | flops 1 | bytes 1 | tf_op jit(solution)/shard_map/attend_sentence/pallas_call | solution.py:380
  147.7 0.9 copy-done.9
  148.6 2.0 %project.1 = (bf16[256,512]{1,0:T(8,128)(2,1)S(1)}, bf16[256,512]{1,0:T(8,128)(2,1)S(1)}, f32[256,512]{1,0:T(8,128)S(1)}, f32[256,512]{1,0:T(8,128)S(1)}) custom-call(s32[3]{0:T(128)S(1)} %copy-done.14, bf16[128,512]{1,0:T(8,128)(2,1)S(1)} %copy-done.8, bf16[128,512]{1,0:T(8,128)(2,1)S(1)} %copy-done.9, bf16[512,1024]{1,0:T(8,128)(2,1)S(1)} %bitcast.80, ...), custom_call_target="tpu_custom_call" | custom-call | flops 1 | bytes 1 | tf_op jit(solution)/shard_map/project/pallas_call | solution.py:431
  151.1 5.2 %collective-permute-done.33 = bf16[384,512]{1,0:T(8,128)(2,1)S(1)} collective-permute-done((bf16[384,512]{1,0:T(8,128)(2,1)S(1)}, bf16[384,512]{1,0:T(8,128)(2,1)S(1)}, u32[]{:S(2)}, u32[]{:S(2)}) %collective-permute-start.33) | collective-permute-done | bytes 393248 | tf_op jit(solution)/shard_map/ppermute | solution.py:38
  156.4 1.6 collective-permute-start.35
  158.0 1.9 %fusion.34 = bf16[384,512]{1,0:T(8,128)(2,1)} fusion(f32[384,512]{1,0:T(8,128)S(1)} %copy-done.21, bf16[384,512]{1,0:T(8,128)(2,1)S(1)} %collective-permute-done.33, bf16[2,384,512]{2,1,0:T(8,128)(2,1)} %collective-permute-done.32), kind=kLoop, calls=%fused_computation.45 | loop fusion | flops 983040 | bytes 1966080 | tf_op jit(solution)/shard_map/convert_element_type | solution.py:709
  159.9 3.5 %all-to-all-start = ((bf16[8,48,512]{2,1,0:T(8,128)(2,1)}), bf16[8,48,512]{2,1,0:T(8,128)(2,1)S(1)}, u32[]{:S(2)}, u32[]{:S(2)}) async-start(bf16[8,48,512]{2,1,0:T(8,128)(2,1)} %bitcast.31), calls=%async_computation | async-start | bytes 786432 | tf_op jit(solution)/shard_map/all_to_all | solution.py:142
  164.3 1.8 %fusion.47 = bf16[1,256,512]{2,1,0:T(8,128)(2,1)} fusion(bf16[256,512]{1,0:T(8,128)(2,1)S(1)} %collective-permute-done.35, f32[256,512]{1,0:T(8,128)S(1)} %get-tuple-element.64, bf16[256,512]{1,0:T(8,128)(2,1)S(1)} %collective-permute-done.28, bf16[1,256,2048]{2,1,0:T(8,128)(2,1)} %param.22, s32[]{:T(128)S(6)} %select_n.35, ...), kind=kLoop, calls=%fused_computation.62 | loop fusion | flops 1048576 | bytes 1573124 | tf_op jit(solution)/shard_map/broadcast_in_dim | solution.py:714
  166.1 5.5 %all-to-all-done = bf16[8,48,512]{2,1,0:T(8,128)(2,1)S(1)} async-done(((bf16[8,48,512]{2,1,0:T(8,128)(2,1)}), bf16[8,48,512]{2,1,0:T(8,128)(2,1)S(1)}, u32[]{:S(2)}, u32[]{:S(2)}) %all-to-all-start) | async-done | bytes 393248 | tf_op jit(solution)/shard_map/all_to_all | solution.py:142
  171.6 1.0 combine.3
  (113 shorter events, 17.5 us)
Async XLA Ops:
  0.6 45.5 %copy-start = (bf16[1,1024,512]{2,1,0:T(8,128)(2,1)S(1)}, bf16[1,1024,512]{2,1,0:T(8,128)(2,1)}, u32[]{:S(2)}) copy-start(bf16[1,1024,512]{2,1,0:T(8,128)(2,1)} %param.26) | copy-start | bytes 3145732
  0.6 15.2 %collective-permute-start = (bf16[128,2048]{1,0:T(8,128)(2,1)}, bf16[128,2048]{1,0:T(8,128)(2,1)S(1)}, u32[]{:S(2)}, u32[]{:S(2)}) collective-permute-start(bf16[128,2048]{1,0:T(8,128)(2,1)} %tokens_ref), channel_id=1, source_target_pairs={{0,4},{4,0},{1,5},{5,1},{2,6},{6,2},{3,7},{7,3},{8,12},{12,8},{9,1... | collective-permute-start | bytes 1572872 | tf_op jit(solution)/shard_map/ppermute | solution.py:38
  3.7 3.8 %collective-permute-start.3 = (s32[2,128]{1,0:T(2,128)}, s32[2,128]{1,0:T(2,128)S(1)}, u32[]{:S(2)}, u32[]{:S(2)}) collective-permute-start(s32[2,128]{1,0:T(2,128)} %bitcast.88), channel_id=1, source_target_pairs={{0,2},{1,3},{2,0},{3,1},{4,6},{5,7},{6,4},{7,5},{8,10},{9,11},{10,... | collective-permute-start | bytes 3080 | tf_op jit(solution)/shard_map/ppermute | solution.py:38
  5.2 10.7 %collective-permute-start.4 = (s32[2,128]{1,0:T(2,128)}, s32[2,128]{1,0:T(2,128)S(1)}, u32[]{:S(2)}, u32[]{:S(2)}) collective-permute-start(s32[2,128]{1,0:T(2,128)} %bitcast.89), channel_id=1, source_target_pairs={{0,4},{4,0},{1,5},{5,1},{2,6},{6,2},{3,7},{7,3},{8,12},{12,8},{9,1... | collective-permute-start | bytes 3080 | tf_op jit(solution)/shard_map/ppermute | solution.py:38
  5.7 25.2 %collective-permute-start.6 = (bf16[128,2048]{1,0:T(8,128)(2,1)}, bf16[128,2048]{1,0:T(8,128)(2,1)S(1)}, u32[]{:S(2)}, u32[]{:S(2)}) collective-permute-start(bf16[128,2048]{1,0:T(8,128)(2,1)} %tokens_ref), channel_id=1, source_target_pairs={{0,2},{1,3},{2,0},{3,1},{4,6},{5,7},{6,4},{7,5},{8,10},{9,11},{10,... | collective-permute-start | bytes 1572872 | tf_op jit(solution)/shard_map/ppermute | solution.py:38
  15.9 15.0 %collective-permute-start.7 = (bf16[128,2048]{1,0:T(8,128)(2,1)S(1)}, bf16[128,2048]{1,0:T(8,128)(2,1)S(1)}, u32[]{:S(2)}, u32[]{:S(2)}) collective-permute-start(bf16[128,2048]{1,0:T(8,128)(2,1)S(1)} %collective-permute-done.refs_2_), channel_id=1, source_target_pairs={{0,2},{1,3},{2,0},{3,1},{4,6},{5,7},{6,4},{7,5},{8,10},{9,11},{10,... | collective-permute-start | bytes 1572872 | tf_op jit(solution)/shard_map/ppermute | solution.py:38
  17.7 10.0 %collective-permute-start.1 = (bf16[64,2048]{1,0:T(8,128)(2,1)S(1)}, bf16[64,2048]{1,0:T(8,128)(2,1)}, u32[]{:S(2)}, u32[]{:S(2)}) collective-permute-start(bf16[64,2048]{1,0:T(8,128)(2,1)S(1)} %constant_dynamic-slice_fusion.2), channel_id=1, source_target_pairs={{0,4},{4,0},{1,5},{5,1},{2,6},{6,2},{3,7},{7,3},{8,12},{12,8},{9,1... | collective-permute-start | bytes 786440 | tf_op jit(solution)/shard_map/ppermute | solution.py:38
  19.9 7.0 %collective-permute-start.5 = (s32[2,128]{1,0:T(2,128)S(1)}, s32[2,128]{1,0:T(2,128)S(1)}, u32[]{:S(2)}, u32[]{:S(2)}) collective-permute-start(s32[2,128]{1,0:T(2,128)S(1)} %collective-permute-done.3), channel_id=1, source_target_pairs={{0,4},{4,0},{1,5},{5,1},{2,6},{6,2},{3,7},{7,3},{8,12},{12,8},{9,1... | collective-permute-start | bytes 3080 | tf_op jit(solution)/shard_map/ppermute | solution.py:38
  21.1 1.2 copy-start.4
  22.4 0.7 copy-start.12
  23.8 0.8 copy-start.15
  27.7 18.4 %collective-permute-start.2 = (bf16[256,1024]{1,0:T(8,128)(2,1)}, bf16[256,1024]{1,0:T(8,128)(2,1)S(1)}, u32[]{:S(2)}, u32[]{:S(2)}) collective-permute-start(bf16[256,1024]{1,0:T(8,128)(2,1)} %copy-done.15), channel_id=1, source_target_pairs={{0,4},{4,0},{1,5},{5,1},{2,6},{6,2},{3,7},{7,3},{8,12},{12,8},{9,1... | collective-permute-start | bytes 1572872 | tf_op jit(solution)/shard_map/ppermute | solution.py:38
  29.3 7.1 %collective-permute-start.9 = (bf16[64,2048]{1,0:T(8,128)(2,1)}, bf16[64,2048]{1,0:T(8,128)(2,1)S(1)}, u32[]{:S(2)}, u32[]{:S(2)}) collective-permute-start(bf16[64,2048]{1,0:T(8,128)(2,1)} %collective-permute-done.1), channel_id=1, source_target_pairs={{0,8},{8,0},{16,24},{24,16},{1,9},{9,1},{17,25},{25,17},{2,10},{10... | collective-permute-start | bytes 786440 | tf_op jit(solution)/shard_map/ppermute | solution.py:38
  30.9 1.0 copy-start.1
  31.9 4.6 %copy-start.17 = (bf16[1,1024,2048]{2,1,0:T(8,128)(2,1)S(1)}, bf16[1,1024,2048]{2,1,0:T(8,128)(2,1)}, u32[]{:S(2)}) copy-start(bf16[1,1024,2048]{2,1,0:T(8,128)(2,1)} %param.20) | copy-start | bytes 12582916
  36.4 2.6 %copy-start.24 = (s32[128,2]{1,0:T(8,128)S(1)}, s32[128,2]{1,0:T(8,128)}, u32[]{:S(2)}) copy-start(s32[128,2]{1,0:T(8,128)} %copy.38) | copy-start | bytes 3076
  36.4 2.6 %copy-start.25 = (s32[128,2]{1,0:T(8,128)S(1)}, s32[128,2]{1,0:T(8,128)}, u32[]{:S(2)}) copy-start(s32[128,2]{1,0:T(8,128)} %copy.41) | copy-start | bytes 3076
  36.4 10.9 %copy-start.16 = (bf16[1,2048,1024]{2,1,0:T(8,128)(2,1)S(1)}, bf16[1,2048,1024]{2,1,0:T(8,128)(2,1)}, u32[]{:S(2)}) copy-start(bf16[1,2048,1024]{2,1,0:T(8,128)(2,1)} %param.19) | copy-start | bytes 12582916
  36.4 10.9 %collective-permute-start.8 = (bf16[192,2048]{1,0:T(8,128)(2,1)S(1)}, bf16[192,2048]{1,0:T(8,128)(2,1)S(1)}, u32[]{:S(2)}, u32[]{:S(2)}) collective-permute-start(bf16[192,2048]{1,0:T(8,128)(2,1)S(1)} %get-tuple-element.46), channel_id=1, source_target_pairs={{0,1},{1,0},{2,3},{3,2},{4,5},{5,4},{6,7},{7,6},{8,9},{9,8},{10,11... | collective-permute-start | bytes 2359304 | tf_op jit(solution)/shard_map/ppermute | solution.py:38
  38.4 7.7 %collective-permute-start.13 = (bf16[48,2048]{1,0:T(8,128)(2,1)S(1)}, bf16[48,2048]{1,0:T(8,128)(2,1)S(1)}, u32[]{:S(2)}, u32[]{:S(2)}) collective-permute-start(bf16[48,2048]{1,0:T(8,128)(2,1)S(1)} %get-tuple-element.87), channel_id=1, source_target_pairs={{0,2},{1,3},{2,0},{3,1},{4,6},{5,7},{6,4},{7,5},{8,10},{9,11},{10,... | collective-permute-start | bytes 589832 | tf_op jit(solution)/shard_map/ppermute | solution.py:223
  39.0 18.5 %collective-permute-start.15 = (bf16[48,2048]{1,0:T(8,128)(2,1)}, bf16[48,2048]{1,0:T(8,128)(2,1)S(1)}, u32[]{:S(2)}, u32[]{:S(2)}) collective-permute-start(bf16[48,2048]{1,0:T(8,128)(2,1)} %get-tuple-element.85), channel_id=1, source_target_pairs={{0,4},{1,5},{2,6},{3,7},{4,0},{5,1},{6,2},{7,3},{8,12},{9,13},{10,... | collective-permute-start | bytes 589832 | tf_op jit(solution)/shard_map/ppermute | solution.py:223
  39.7 17.8 %collective-permute-start.16 = (bf16[48,2048]{1,0:T(8,128)(2,1)}, bf16[48,2048]{1,0:T(8,128)(2,1)}, u32[]{:S(2)}, u32[]{:S(2)}) collective-permute-start(bf16[48,2048]{1,0:T(8,128)(2,1)} %get-tuple-element.84), channel_id=1, source_target_pairs={{0,6},{1,7},{2,4},{3,5},{4,2},{5,3},{6,0},{7,1},{8,14},{9,15},{10,... | collective-permute-start | bytes 589832 | tf_op jit(solution)/shard_map/ppermute | solution.py:223
  49.4 8.0 %copy-start.26 = (f32[128,2]{0,1:T(2,128)S(1)}, f32[128,2]{0,1:T(2,128)}, u32[]{:S(2)}) copy-start(f32[128,2]{0,1:T(2,128)} %param.17) | copy-start | bytes 3076
  49.4 18.4 %copy-start.5 = (bf16[128,2048]{1,0:T(8,128)(2,1)S(1)}, bf16[128,2048]{1,0:T(8,128)(2,1)}, u32[]{:S(2)}) copy-start(bf16[128,2048]{1,0:T(8,128)(2,1)} %refs_0_.3) | copy-start | bytes 1572868
  50.3 2.9 %collective-permute-start.14 = (bf16[48,2048]{1,0:T(8,128)(2,1)S(1)}, bf16[48,2048]{1,0:T(8,128)(2,1)S(1)}, u32[]{:S(2)}, u32[]{:S(2)}) collective-permute-start(bf16[48,2048]{1,0:T(8,128)(2,1)S(1)} %get-tuple-element.81), channel_id=1, source_target_pairs={{0,1},{1,0},{2,3},{3,2},{4,5},{5,4},{6,7},{7,6},{8,9},{9,8},{10,11... | collective-permute-start | bytes 589832 | tf_op jit(solution)/shard_map/ppermute | solution.py:223
  50.3 7.2 %collective-permute-start.10 = (bf16[48,2048]{1,0:T(8,128)(2,1)}, bf16[48,2048]{1,0:T(8,128)(2,1)}, u32[]{:S(2)}, u32[]{:S(2)}) collective-permute-start(bf16[48,2048]{1,0:T(8,128)(2,1)} %get-tuple-element.83), channel_id=1, source_target_pairs={{0,3},{1,2},{2,1},{3,0},{4,7},{5,6},{6,5},{7,4},{8,11},{9,10},{10,... | collective-permute-start | bytes 589832 | tf_op jit(solution)/shard_map/ppermute | solution.py:223
  50.9 11.5 %collective-permute-start.11 = (bf16[48,2048]{1,0:T(8,128)(2,1)}, bf16[48,2048]{1,0:T(8,128)(2,1)}, u32[]{:S(2)}, u32[]{:S(2)}) collective-permute-start(bf16[48,2048]{1,0:T(8,128)(2,1)} %get-tuple-element.82), channel_id=1, source_target_pairs={{0,5},{1,4},{2,7},{3,6},{4,1},{5,0},{6,3},{7,2},{8,13},{9,12},{10,... | collective-permute-start | bytes 589832 | tf_op jit(solution)/shard_map/ppermute | solution.py:223
  53.9 8.6 %collective-permute-start.17 = (bf16[48,2048]{1,0:T(8,128)(2,1)}, bf16[48,2048]{1,0:T(8,128)(2,1)}, u32[]{:S(2)}, u32[]{:S(2)}) collective-permute-start(bf16[48,2048]{1,0:T(8,128)(2,1)} %get-tuple-element.80), channel_id=1, source_target_pairs={{0,7},{1,6},{2,5},{3,4},{4,3},{5,2},{6,1},{7,0},{8,15},{9,14},{10,... | collective-permute-start | bytes 589832 | tf_op jit(solution)/shard_map/ppermute | solution.py:223
  62.5 0.9 copy-start.11
  63.4 30.5 %copy-start.23 = (bf16[256,512]{1,0:T(8,128)(2,1)S(1)}, bf16[256,512]{1,0:T(8,128)(2,1)}, u32[]{:S(2)}) copy-start(bf16[256,512]{1,0:T(8,128)(2,1)} %fusion.1) | copy-start | bytes 786436
  65.5 8.4 %collective-permute-start.18 = (bf16[2,128,512]{2,1,0:T(8,128)(2,1)S(1)}, bf16[2,128,512]{2,1,0:T(8,128)(2,1)S(1)}, u32[]{:S(2)}, u32[]{:S(2)}) collective-permute-start(bf16[2,128,512]{2,1,0:T(8,128)(2,1)S(1)} %get-tuple-element.57), channel_id=1, source_target_pairs={{0,8},{8,0},{16,24},{24,16},{1,9},{9,1},{17,25},{25,17},{2,10},{10... | collective-permute-start | bytes 786440 | tf_op jit(solution)/shard_map/ppermute | solution.py:38
  66.3 21.1 %collective-permute-start.30 = (bf16[128,2048]{1,0:T(8,128)(2,1)S(1)}, bf16[128,2048]{1,0:T(8,128)(2,1)S(1)}, u32[]{:S(2)}, u32[]{:S(2)}) collective-permute-start(bf16[128,2048]{1,0:T(8,128)(2,1)S(1)} %constant_dynamic-update-slice_fusion.refs_2_), channel_id=1, source_target_pairs={{0,2},{1,3},{2,0},{3,1},{4,6},{5,7},{6,4},{7,5},{8,10},{9,11},{10,... | collective-permute-start | bytes 1572872 | tf_op jit(solution)/shard_map/ppermute | solution.py:38
  67.8 23.8 %collective-permute-start.29 = (bf16[128,2048]{1,0:T(8,128)(2,1)S(1)}, bf16[128,2048]{1,0:T(8,128)(2,1)S(1)}, u32[]{:S(2)}, u32[]{:S(2)}) collective-permute-start(bf16[128,2048]{1,0:T(8,128)(2,1)S(1)} %copy-done.5), channel_id=1, source_target_pairs={{0,2},{1,3},{2,0},{3,1},{4,6},{5,7},{6,4},{7,5},{8,10},{9,11},{10,... | collective-permute-start | bytes 1572872 | tf_op jit(solution)/shard_map/ppermute | solution.py:38
  68.3 27.6 %collective-permute-start.21 = (bf16[1024,512]{1,0:T(8,128)(2,1)}, bf16[1024,512]{1,0:T(8,128)(2,1)S(1)}, u32[]{:S(2)}, u32[]{:S(2)}) collective-permute-start(bf16[1024,512]{1,0:T(8,128)(2,1)} %bitcast.85), channel_id=1, source_target_pairs={{0,4},{4,0},{1,5},{5,1},{2,6},{6,2},{3,7},{7,3},{8,12},{12,8},{9,1... | collective-permute-start | bytes 3145736 | tf_op jit(solution)/shard_map/ppermute | solution.py:38
  73.9 8.5 %collective-permute-start.19 = (bf16[128,512]{1,0:T(8,128)(2,1)S(1)}, bf16[128,512]{1,0:T(8,128)(2,1)S(1)}, u32[]{:S(2)}, u32[]{:S(2)}) collective-permute-start(bf16[128,512]{1,0:T(8,128)(2,1)S(1)} %fusion.48), channel_id=1, source_target_pairs={{0,16},{8,24},{16,0},{24,8},{1,17},{9,25},{17,1},{25,9},{2,18},{10... | collective-permute-start | bytes 393224 | tf_op jit(solution)/shard_map/ppermute | solution.py:38
  82.4 5.0 %collective-permute-start.20 = (bf16[128,512]{1,0:T(8,128)(2,1)S(1)}, bf16[128,512]{1,0:T(8,128)(2,1)S(1)}, u32[]{:S(2)}, u32[]{:S(2)}) collective-permute-start(bf16[128,512]{1,0:T(8,128)(2,1)S(1)} %fusion.50.refs_0_), channel_id=1, source_target_pairs={{0,8},{8,0},{16,24},{24,16},{1,9},{9,1},{17,25},{25,17},{2,10},{10... | collective-permute-start | bytes 393224 | tf_op jit(solution)/shard_map/ppermute | solution.py:38
  93.0 0.9 copy-start.7
  93.9 9.1 %collective-permute-start.31 = (bf16[192,2048]{1,0:T(8,128)(2,1)S(1)}, bf16[192,2048]{1,0:T(8,128)(2,1)S(1)}, u32[]{:S(2)}, u32[]{:S(2)}) collective-permute-start(bf16[192,2048]{1,0:T(8,128)(2,1)S(1)} %get-tuple-element.71), channel_id=1, source_target_pairs={{0,1},{1,0},{2,3},{3,2},{4,5},{5,4},{6,7},{7,6},{8,9},{9,8},{10,11... | collective-permute-start | bytes 2359304 | tf_op jit(solution)/shard_map/ppermute | solution.py:38
  93.9 9.1 %collective-permute-start.12 = (bf16[256,512]{1,0:T(8,128)(2,1)S(1)}, bf16[256,512]{1,0:T(8,128)(2,1)S(1)}, u32[]{:S(2)}, u32[]{:S(2)}) collective-permute-start(bf16[256,512]{1,0:T(8,128)(2,1)S(1)} %copy-done.23), channel_id=1, source_target_pairs={{0,4},{4,0},{1,5},{5,1},{2,6},{6,2},{3,7},{7,3},{8,12},{12,8},{9,1... | collective-permute-start | bytes 786440 | tf_op jit(solution)/shard_map/ppermute | solution.py:38
  94.9 30.7 %collective-permute-start.24 = (bf16[1024,512]{1,0:T(8,128)(2,1)}, bf16[1024,512]{1,0:T(8,128)(2,1)}, u32[]{:S(2)}, u32[]{:S(2)}) collective-permute-start(bf16[1024,512]{1,0:T(8,128)(2,1)} %bitcast.24.refs_4_), channel_id=1, source_target_pairs={{0,4},{4,0},{1,5},{5,1},{2,6},{6,2},{3,7},{7,3},{8,12},{12,8},{9,1... | collective-permute-start | bytes 3145736 | tf_op jit(solution)/shard_map/ppermute | solution.py:38
  95.9 15.3 %copy-start.18 = (bf16[1024,512]{1,0:T(8,128)(2,1)}, bf16[1024,512]{1,0:T(8,128)(2,1)S(1)}, u32[]{:S(2)}) copy-start(bf16[1024,512]{1,0:T(8,128)(2,1)S(1)} %collective-permute-done.21.refs_3_) | copy-start | bytes 3145732
  96.0 22.2 %collective-permute-start.22 = (bf16[2,128,512]{2,1,0:T(8,128)(2,1)S(1)}, bf16[2,128,512]{2,1,0:T(8,128)(2,1)S(1)}, u32[]{:S(2)}, u32[]{:S(2)}) collective-permute-start(bf16[2,128,512]{2,1,0:T(8,128)(2,1)S(1)} %pad_maximum_fusion), channel_id=1, source_target_pairs={{0,16},{8,24},{16,0},{24,8},{1,17},{9,25},{17,1},{25,9},{2,18},{10... | collective-permute-start | bytes 786440 | tf_op jit(solution)/shard_map/ppermute | solution.py:38
  103.0 0.9 copy-start.19
  111.3 6.9 %copy-start.2 = (bf16[128,2048]{1,0:T(8,128)(2,1)S(1)}, bf16[128,2048]{1,0:T(8,128)(2,1)}, u32[]{:S(2)}) copy-start(bf16[128,2048]{1,0:T(8,128)(2,1)} %tokens_ref) | copy-start | bytes 1572868
  111.3 6.9 %copy-start.13 = (f32[2048]{0:T(1024)S(1)}, f32[2048]{0:T(1024)}, u32[]{:S(2)}) copy-start(f32[2048]{0:T(1024)} %param.21) | copy-start | bytes 24580
  111.3 8.9 %copy-start.6 = (bf16[1,512,1024]{2,1,0:T(8,128)(2,1)S(1)}, bf16[1,512,1024]{2,1,0:T(8,128)(2,1)}, u32[]{:S(2)}) copy-start(bf16[1,512,1024]{2,1,0:T(8,128)(2,1)} %param.29) | copy-start | bytes 3145732
  117.2 19.2 %collective-permute-start.32 = (bf16[2,384,512]{2,1,0:T(8,128)(2,1)}, bf16[2,384,512]{2,1,0:T(8,128)(2,1)}, u32[]{:S(2)}, u32[]{:S(2)}) collective-permute-start(bf16[2,384,512]{2,1,0:T(8,128)(2,1)} %get-tuple-element.73), channel_id=1, source_target_pairs={{0,8},{8,0},{16,24},{24,16},{1,9},{9,1},{17,25},{25,17},{2,10},{10... | collective-permute-start | bytes 2359304 | tf_op jit(solution)/shard_map/ppermute | solution.py:38
  118.6 7.0 %copy-start.3 = (bf16[128,2048]{1,0:T(8,128)(2,1)}, bf16[128,2048]{1,0:T(8,128)(2,1)S(1)}, u32[]{:S(2)}) copy-start(bf16[128,2048]{1,0:T(8,128)(2,1)S(1)} %memory.1.refs_0_) | copy-start | bytes 1572868
  118.6 7.0 %collective-permute-start.23 = (bf16[128,2048]{1,0:T(8,128)(2,1)S(1)}, bf16[128,2048]{1,0:T(8,128)(2,1)}, u32[]{:S(2)}, u32[]{:S(2)}) collective-permute-start(bf16[128,2048]{1,0:T(8,128)(2,1)S(1)} %memory.1.refs_0_), channel_id=1, source_target_pairs={{0,1},{1,0},{2,3},{3,2},{4,5},{5,4},{6,7},{7,6},{8,9},{9,8},{10,11... | collective-permute-start | bytes 1572872 | tf_op jit(solution)/shard_map/ppermute | solution.py:38
  118.7 14.4 %collective-permute-start.25 = (bf16[128,2048]{1,0:T(8,128)(2,1)S(1)}, bf16[128,2048]{1,0:T(8,128)(2,1)}, u32[]{:S(2)}, u32[]{:S(2)}) collective-permute-start(bf16[128,2048]{1,0:T(8,128)(2,1)S(1)} %memory.1.refs_0_), channel_id=1, source_target_pairs={{0,2},{1,3},{2,0},{3,1},{4,6},{5,7},{6,4},{7,5},{8,10},{9,11},{10,... | collective-permute-start | bytes 1572872 | tf_op jit(solution)/shard_map/ppermute | solution.py:38
  120.3 27.4 %collective-permute-start.27 = (bf16[512,1024]{1,0:T(8,128)(2,1)S(1)}, bf16[512,1024]{1,0:T(8,128)(2,1)}, u32[]{:S(2)}, u32[]{:S(2)}) collective-permute-start(bf16[512,1024]{1,0:T(8,128)(2,1)S(1)} %bitcast.79), channel_id=1, source_target_pairs={{0,4},{4,0},{1,5},{5,1},{2,6},{6,2},{3,7},{7,3},{8,12},{12,8},{9,1... | collective-permute-start | bytes 3145736 | tf_op jit(solution)/shard_map/ppermute | solution.py:38
  121.8 14.5 %copy-start.20 = (f32[384,512]{1,0:T(8,128)S(1)}, f32[384,512]{1,0:T(8,128)}, u32[]{:S(2)}) copy-start(f32[384,512]{1,0:T(8,128)} %get-tuple-element.72) | copy-start | bytes 2359300
  131.0 16.7 %copy-start.8 = (bf16[128,512]{1,0:T(8,128)(2,1)S(1)}, bf16[128,512]{1,0:T(8,128)(2,1)}, u32[]{:S(2)}) copy-start(bf16[128,512]{1,0:T(8,128)(2,1)} %attend_sentence.2.mine_ref) | copy-start | bytes 393220
  131.0 16.6 %copy-start.14 = (s32[3]{0:T(128)S(1)}, s32[3]{0:T(128)}, u32[]{:S(2)}) copy-start(s32[3]{0:T(128)} %pad_add_fusion.1.place_ref) | copy-start | bytes 40
  133.1 7.6 %collective-permute-start.26 = (bf16[128,2048]{1,0:T(8,128)(2,1)}, bf16[128,2048]{1,0:T(8,128)(2,1)S(1)}, u32[]{:S(2)}, u32[]{:S(2)}) collective-permute-start(bf16[128,2048]{1,0:T(8,128)(2,1)} %collective-permute-done.25.refs_0_), channel_id=1, source_target_pairs={{0,1},{1,0},{2,3},{3,2},{4,5},{5,4},{6,7},{7,6},{8,9},{9,8},{10,11... | collective-permute-start | bytes 1572872 | tf_op jit(solution)/shard_map/ppermute | solution.py:38
  137.5 18.8 %collective-permute-start.33 = (bf16[384,512]{1,0:T(8,128)(2,1)S(1)}, bf16[384,512]{1,0:T(8,128)(2,1)S(1)}, u32[]{:S(2)}, u32[]{:S(2)}) collective-permute-start(bf16[384,512]{1,0:T(8,128)(2,1)S(1)} %fusion.35), channel_id=1, source_target_pairs={{0,16},{8,24},{16,0},{24,8},{1,17},{9,25},{17,1},{25,9},{2,18},{10... | collective-permute-start | bytes 1179656 | tf_op jit(solution)/shard_map/ppermute | solution.py:38
  140.7 0.8 copy-start.22
  141.5 16.4 %copy-start.21 = (f32[384,512]{1,0:T(8,128)S(1)}, f32[384,512]{1,0:T(8,128)}, u32[]{:S(2)}) copy-start(f32[384,512]{1,0:T(8,128)} %get-tuple-element.76) | copy-start | bytes 2359300
  147.7 0.9 copy-start.9
  148.6 14.8 %copy-start.27 = (s32[2]{0:T(128)S(1)}, s32[2]{0:T(128)}, u32[]{:S(2)}) copy-start(s32[2]{0:T(128)} %param.24) | copy-start | bytes 28
  150.6 5.7 %collective-permute-start.34 = (bf16[256,512]{1,0:T(8,128)(2,1)S(1)}, bf16[256,512]{1,0:T(8,128)(2,1)S(1)}, u32[]{:S(2)}, u32[]{:S(2)}) collective-permute-start(bf16[256,512]{1,0:T(8,128)(2,1)S(1)} %get-tuple-element.75), channel_id=1, source_target_pairs={{0,1},{1,0},{2,3},{3,2},{4,5},{5,4},{6,7},{7,6},{8,9},{9,8},{10,11... | collective-permute-start | bytes 786440 | tf_op jit(solution)/shard_map/ppermute | solution.py:38
  150.6 12.9 %collective-permute-start.28 = (bf16[256,512]{1,0:T(8,128)(2,1)S(1)}, bf16[256,512]{1,0:T(8,128)(2,1)S(1)}, u32[]{:S(2)}, u32[]{:S(2)}) collective-permute-start(bf16[256,512]{1,0:T(8,128)(2,1)S(1)} %get-tuple-element.65), channel_id=1, source_target_pairs={{0,1},{1,0},{2,3},{3,2},{4,5},{5,4},{6,7},{7,6},{8,9},{9,8},{10,11... | collective-permute-start | bytes 786440 | tf_op jit(solution)/shard_map/ppermute | solution.py:38
  156.4 7.9 %collective-permute-start.35 = (bf16[256,512]{1,0:T(8,128)(2,1)S(1)}, bf16[256,512]{1,0:T(8,128)(2,1)S(1)}, u32[]{:S(2)}, u32[]{:S(2)}) collective-permute-start(bf16[256,512]{1,0:T(8,128)(2,1)S(1)} %convert_add_fusion.3), channel_id=1, source_target_pairs={{0,2},{1,3},{2,0},{3,1},{4,6},{5,7},{6,4},{7,5},{8,10},{9,11},{10,... | collective-permute-start | bytes 786440 | tf_op jit(solution)/shard_map/ppermute | solution.py:38
  159.9 11.7 %all-to-all-start = ((bf16[8,48,512]{2,1,0:T(8,128)(2,1)}), bf16[8,48,512]{2,1,0:T(8,128)(2,1)S(1)}, u32[]{:S(2)}, u32[]{:S(2)}) async-start(bf16[8,48,512]{2,1,0:T(8,128)(2,1)} %bitcast.31), calls=%async_computation | async-start | bytes 786432 | tf_op jit(solution)/shard_map/all_to_all | solution.py:142
  (1 other events, 0.7 us)

commit v13 on v12

--- a/solution.py
+++ b/solution.py
@@ -596,6 +596,7 @@
     asked_here = swap(gate(asked, half_y), "expert", 1)
     query_there = jnp.dot(asked_here, query_own, preferred_element_type=jnp.float32)
     other_y = swap(half_y, "section", 1)
+    half_x = swap(gate(grad_half, token_far), "dp", 2)
 
     ids = jnp.stack([ids_own, ids_x, ids_y, ids_far])
     named_there = jnp.concatenate([(ids == here).any(axis=1), (ids == (here ^ 1)).any(axis=1)])
@@ -623,40 +624,40 @@
         capacity,
     )
     rows_core = swap(rows_sent, "dp", 1)
-    pre_own, part_own = forward(rows_own, other_y)
+    pre_own, part_own = forward(rows_own, other_y, half_x)
     pre_core, part_core = forward(gate(rows_core, part_own))
     home = send_home(part_own, near_codes, capacity) + send_home(part_core, core_codes, capacity)
+    other_x = swap(gate(half_x, home[1], home[2], home[3]), "section", 1)
     grad_y = jnp.concatenate([gate(half_y, home[4]), other_y], axis=0)
     query_back = swap(gate(query_there.astype(jnp.bfloat16), home[5], home[6]), "expert", 1)
 
-    rise_own, rise_core = slope_of(gate(pre_own, home[1])), slope_of(gate(pre_core, home[1]))
-    held_gates = gate(gate_weights, rise_own, rise_core, query_there, grad_y)
+    rise_own, rise_core = slope_of(gate(pre_own, home[5])), slope_of(gate(pre_core, home[5]))
+    held_gates = gate(gate_weights, rise_own, rise_core, query_there, grad_y, other_x)
     sent_pair, first, second = combine(which_section, position, held_gates, home, sections)
     from_pair = swap(sent_pair, "section", 1)
-    grad_x = swap(gate(out_grad, home[5]), "dp", 2)
     grad_far = swap(gate(grad_y, first), "dp", 2)
     to_other = (second + from_pair[1].astype(jnp.float32)).astype(jnp.bfloat16)
     from_other = swap(to_other, "section", 2)
-    mixed_sum = first + from_pair[0].astype(jnp.float32)
+    grads_own, grads_sent = dispatch(
+        which_section,
+        gate(code, to_other),
+        [out_grad, half_x, other_x, grad_y, grad_far],
+        (
+            ((0, 0, token_count, None),),
+            ((1, 0, share, 0), (2, 0, share, 1)),
+            ((3, 0, share, 0), (3, share, share, 1)),
+            ((4, 0, share, 0), (4, share, share, 1)),
+        ),
+        capacity,
+    )
+    grads_core = swap(grads_sent, "dp", 1)
+    grads_core = swap(grads_sent, "dp", 1)
+    mixed_sum = gate(first, query_back, grads_sent) + from_pair[0].astype(jnp.float32)
     mixed_slice = (mixed_sum + from_other.astype(jnp.float32)).astype(jnp.bfloat16)
     key_other = swap(gate(key_own, first), "expert", 1)
     mixed_near = swap(mixed_slice, "section", 1)
-    grads_own, grads_sent = dispatch(
-        which_section,
-        gate(code, mixed_near),
-        [out_grad, grad_x, grad_y, grad_far],
-        (
-            ((0, 0, token_count, None),),
-            ((1, 0, token_count, None),),
-            ((2, 0, share, 0), (2, share, share, 1)),
-            ((3, 0, share, 0), (3, share, share, 1)),
-        ),
-        capacity,
-    )
-    grads_core = swap(grads_sent, "dp", 1)
-    grads_core = swap(grads_sent, "dp", 1)
     slope = expert_slope(
-        here.astype(jnp.int32).reshape(1),
+        gate(here.astype(jnp.int32).reshape(1), mixed_near, key_other),
         near_codes + core_codes,
         grads_own,
         grads_core,
@@ -667,7 +668,7 @@
     back_pair, back_first, back_second = expert_backward(
         which_section, slope, weight_in, sections
     )
-    mixed_far = swap(jnp.stack([mixed_slice, gate(mixed_near, key_other)]), "section", 2)
+    mixed_far = swap(jnp.stack([mixed_slice, mixed_near]), "section", 2)
     slices = [mixed_slice, mixed_near, mixed_far[0], mixed_far[1]]
 
     value_other = swap(gate(value_own, mixed_near), "expert", 1)
@@ -675,7 +676,7 @@
     query_here = jnp.dot(normed_own, query_own, preferred_element_type=jnp.float32)
     query = (query_here + query_back.astype(jnp.float32)).astype(jnp.bfloat16)
 
-    memory = make_memory(which_section, gate(tokens, query_back), slices, final_gain)
+    memory = make_memory(which_section, tokens, slices, final_gain)
     out_other = swap(gate(out_own, memory), "expert", 1)
     memory_x = swap(memory, "dp", 2)
     memory_core = swap(memory, "dp", 1)

time: 173 us -> 174 us (level)
  local copies, waits for them, and re-layouts: 15.8 us -> 21 us
  waiting for transfers between devices: 60.7 us -> 56.3 us
    unnamed x59 -> x73, local copies, waits for them, and re-layouts: 10.8 us -> 17.3 us
    ppermute x7, waiting for transfers between devices: 9.08 us -> 6.48 us  [send_home(): lax.ppermute(block, ('expert', 'dp'), [(i, i ^ code) for i in range(size)])]
    ppermute x29 -> x30, waiting for transfers between devices: 46.1 us -> 44.4 us  [swap(): return lax.ppermute(value, axis, [(i, i ^ mask) for i in range(size)])]
    ppermute x29 -> x30, starting transfers between devices: 32.2 us -> 32.6 us  [swap(): return lax.ppermute(value, axis, [(i, i ^ mask) for i in range(size)])]
  transfers between devices with their start and end apart: 37 -> 38, of which waited for: 15 -> 15; matrix products, arithmetic and copies ran while one was open for 15% -> 14% of each run, Pallas kernels for 17% -> 17%
where the time goes in v13:
time: 174 us; the launch traced here: 173 us
  waiting for transfers between devices  56.3 us (32%)
  starting transfers between devices  42.6 us (24%)
  Pallas kernels  32.8 us (19%)
  local copies, waits for them, and re-layouts  21 us (12%)
  other arithmetic  11.1 us (6%)
  matrix products  8.25 us (5%)
    ppermute x30, waiting for transfers between devices, swap(): return lax.ppermute(value, axis, [(i, i ^ mask) for i in range(size)])  44.4 us
    ppermute x30, starting transfers between devices, swap(): return lax.ppermute(value, axis, [(i, i ^ mask) for i in range(size)])  32.6 us
    unnamed x73, local copies, waits for them, and re-layouts  17.3 us
    pallas_call x2, Pallas kernels, attend_sentence(): pl.pallas_call(attend_kernel, out_shape=jax.ShapeDtypeStruct(query.shape,...  10.9 us
    pallas_call x1, Pallas kernels, expert_slope(): pl.pallas_call(functools.partial(slope_kernel, codes), out_shape=jax.Shap...  7.36 us
    ppermute x7, starting transfers between devices, send_home(): lax.ppermute(block, ('expert', 'dp'), [(i, i ^ code) for i in range(size)])  6.57 us
    ppermute x7, waiting for transfers between devices, send_home(): lax.ppermute(block, ('expert', 'dp'), [(i, i ^ code) for i in range(size)])  6.48 us
    pallas_call x1, Pallas kernels, expert_backward(): pl.pallas_call(functools.partial(backward_kernel, split), out_shape=(jax....  5.83 us
  transfers between devices with their start and end apart: 38, of which 15 were waited for; matrix products, arithmetic and copies ran while one was open for 14% of the time, Pallas kernels for 17%

profile of v13, /device:TPU:0, one launch (start us, length us, event | category | flops | bytes accessed | tf_op | source)
XLA Modules:
  0.0 173.2 jit_solution(9661931791109743637)
XLA Ops:
  0.6 3.0 %collective-permute-start.3 = (s32[2,128]{1,0:T(2,128)}, s32[2,128]{1,0:T(2,128)S(1)}, u32[]{:S(2)}, u32[]{:S(2)}) collective-permute-start(s32[2,128]{1,0:T(2,128)} %bitcast.88), channel_id=1, source_target_pairs={{0,2},{1,3},{2,0},{3,1},{4,6},{5,7},{6,4},{7,5},{8,10},{9,11},{10,... | collective-permute-start | bytes 3080 | tf_op jit(solution)/shard_map/ppermute | solution.py:38
  3.6 1.5 collective-permute-start.4
  9.0 9.5 %collective-permute-done.refs_2_ = bf16[128,2048]{1,0:T(8,128)(2,1)S(1)} collective-permute-done((bf16[128,2048]{1,0:T(8,128)(2,1)}, bf16[128,2048]{1,0:T(8,128)(2,1)S(1)}, u32[]{:S(2)}, u32[]{:S(2)}) %collective-permute-start) | collective-permute-done | bytes 524320 | tf_op jit(solution)/shard_map/ppermute | solution.py:38
  19.0 1.7 constant_dynamic-slice_fusion.2
  21.0 1.7 collective-permute-start.1
  22.8 1.2 copy-done.4
  27.7 1.9 %collective-permute-start.2 = (bf16[256,1024]{1,0:T(8,128)(2,1)}, bf16[256,1024]{1,0:T(8,128)(2,1)S(1)}, u32[]{:S(2)}, u32[]{:S(2)}) collective-permute-start(bf16[256,1024]{1,0:T(8,128)(2,1)} %copy-done.23), channel_id=1, source_target_pairs={{0,4},{4,0},{1,5},{5,1},{2,6},{6,2},{3,7},{7,3},{8,12},{12,8},{9,1... | collective-permute-start | bytes 1572872 | tf_op jit(solution)/shard_map/ppermute | solution.py:38
  29.6 1.6 collective-permute-start.9
  31.2 1.5 collective-permute-start.10
  32.7 1.0 copy-done.1
  33.7 1.3 dispatch.2
  35.1 3.2 %fusion.61 = f32[192,1024]{1,0:T(8,128)S(1)} fusion(bf16[192,2048]{1,0:T(8,128)(2,1)S(1)} %get-tuple-element.48, bf16[1,2048,1024]{2,1,0:T(8,128)(2,1)} %param.19), kind=kOutput, calls=%fused_computation.101 | convolution fusion | flops 805306368 | bytes 5767168 | tf_op jit(solution)/shard_map/dot_general | solution.py:611
  38.3 1.1 convolution_convert_fusion.1
  39.5 1.0 collective-permute-start.15
  41.0 2.0 %collective-permute-start.17 = (bf16[48,2048]{1,0:T(8,128)(2,1)S(1)}, bf16[48,2048]{1,0:T(8,128)(2,1)S(1)}, u32[]{:S(2)}, u32[]{:S(2)}) collective-permute-start(bf16[48,2048]{1,0:T(8,128)(2,1)S(1)} %get-tuple-element.87), channel_id=1, source_target_pairs={{0,6},{1,7},{2,4},{3,5},{4,2},{5,3},{6,0},{7,1},{8,14},{9,15},{10,... | collective-permute-start | bytes 589832 | tf_op jit(solution)/shard_map/ppermute | solution.py:223
  43.0 1.0 fusion.59
  44.0 1.1 convolution_convert_fusion
  46.0 1.0 collective-permute-start.11
  47.1 1.2 fusion.1
  48.9 2.3 %collective-permute-done.16.refs_2_ = bf16[48,2048]{1,0:T(8,128)(2,1)S(1)} collective-permute-done((bf16[48,2048]{1,0:T(8,128)(2,1)S(1)}, bf16[48,2048]{1,0:T(8,128)(2,1)S(1)}, u32[]{:S(2)}, u32[]{:S(2)}) %collective-permute-start.16) | collective-permute-done | bytes 196640 | tf_op jit(solution)/shard_map/ppermute | solution.py:223
  52.6 1.2 collective-permute-start.18
  53.8 2.0 %collective-permute-start.19 = (bf16[48,2048]{1,0:T(8,128)(2,1)}, bf16[48,2048]{1,0:T(8,128)(2,1)}, u32[]{:S(2)}, u32[]{:S(2)}) collective-permute-start(bf16[48,2048]{1,0:T(8,128)(2,1)} %get-tuple-element.82), channel_id=1, source_target_pairs={{0,7},{1,6},{2,5},{3,4},{4,3},{5,2},{6,1},{7,0},{8,15},{9,14},{10,... | collective-permute-start | bytes 589832 | tf_op jit(solution)/shard_map/ppermute | solution.py:223
  57.1 2.1 %fusion.10 = (f32[192,1024]{1,0:T(8,128)}, f32[192,1024]{1,0:T(8,128)}) fusion(f32[192,1024]{1,0:T(8,128)S(1)} %fusion.61, f32[192,1024]{1,0:T(8,128)S(1)} %fusion.59), kind=kLoop, calls=%fused_computation.20 | loop fusion | flops 6684672 | bytes 3145728 | tf_op jit(solution)/shard_map/transpose(jvp())/add_any | solution.py:617
  59.2 1.0 constant_dynamic-update-slice_fusion.1
  60.3 4.2 %collective-permute-done.12.refs_6_ = bf16[48,2048]{1,0:T(8,128)(2,1)} collective-permute-done((bf16[48,2048]{1,0:T(8,128)(2,1)}, bf16[48,2048]{1,0:T(8,128)(2,1)}, u32[]{:S(2)}, u32[]{:S(2)}) %collective-permute-start.12) | collective-permute-done | bytes 196640 | tf_op jit(solution)/shard_map/ppermute | solution.py:223
  64.5 0.9 copy-done.11
  65.5 0.9 copy-done.13
  66.4 0.9 copy-done.15
  67.3 0.9 copy-done.17
  68.2 0.9 copy-done.19
  69.2 1.8 %combine.2 = (bf16[2,128,512]{2,1,0:T(8,128)(2,1)S(1)}, f32[128,512]{1,0:T(8,128)S(1)}, f32[128,512]{1,0:T(8,128)S(1)}) custom-call(s32[1]{0:T(128)} %bitcast.7.section_ref, s32[128,2]{1,0:T(8,128)S(1)} %get-tuple-element.95.position_ref, f32[128,2]{1,0:T(8,128)S(1)} %copy.39.gates_ref, bf16[48,2048]{1,0:T(8,128)(2,1)S(1)} %get-tuple-element.86.refs_0_, ...), custom_call_target="tpu_custom_call" | custom-call | flops 1 | bytes 1 | tf_op jit(solution)/shard_map/combine/pallas_call | solution.py:264
  71.0 1.4 collective-permute-start.20
  72.5 1.0 collective-permute-start.21
  73.5 1.3 collective-permute-start.13
  75.5 3.2 %collective-permute-done.20 = bf16[2,128,512]{2,1,0:T(8,128)(2,1)S(1)} collective-permute-done((bf16[2,128,512]{2,1,0:T(8,128)(2,1)S(1)}, bf16[2,128,512]{2,1,0:T(8,128)(2,1)S(1)}, u32[]{:S(2)}, u32[]{:S(2)}) %collective-permute-start.20) | collective-permute-done | bytes 262176 | tf_op jit(solution)/shard_map/ppermute | solution.py:38
  78.7 2.7 %collective-permute-start.22 = (bf16[128,512]{1,0:T(8,128)(2,1)S(1)}, bf16[128,512]{1,0:T(8,128)(2,1)S(1)}, u32[]{:S(2)}, u32[]{:S(2)}) collective-permute-start(bf16[128,512]{1,0:T(8,128)(2,1)S(1)} %fusion.50), channel_id=1, source_target_pairs={{0,16},{8,24},{16,0},{24,8},{1,17},{9,25},{17,1},{25,9},{2,18},{10... | collective-permute-start | bytes 393224 | tf_op jit(solution)/shard_map/ppermute | solution.py:38
  81.4 4.4 %collective-permute-done.21.refs_4_ = bf16[128,2048]{1,0:T(8,128)(2,1)S(1)} collective-permute-done((bf16[128,2048]{1,0:T(8,128)(2,1)S(1)}, bf16[128,2048]{1,0:T(8,128)(2,1)S(1)}, u32[]{:S(2)}, u32[]{:S(2)}) %collective-permute-start.21) | collective-permute-done | bytes 524320 | tf_op jit(solution)/shard_map/ppermute | solution.py:38
  85.8 1.5 dispatch.3
  87.3 0.9 copy-done.7
  88.6 5.5 %collective-permute-done.23.refs_1_ = bf16[128,512]{1,0:T(8,128)(2,1)S(1)} collective-permute-done((bf16[128,512]{1,0:T(8,128)(2,1)S(1)}, bf16[128,512]{1,0:T(8,128)(2,1)S(1)}, u32[]{:S(2)}, u32[]{:S(2)}) %collective-permute-start.23) | collective-permute-done | bytes 131104 | tf_op jit(solution)/shard_map/ppermute | solution.py:38
  94.2 0.9 collective-permute-start.27
  95.2 2.7 %collective-permute-start.24 = (bf16[2,128,512]{2,1,0:T(8,128)(2,1)S(1)}, bf16[2,128,512]{2,1,0:T(8,128)(2,1)S(1)}, u32[]{:S(2)}, u32[]{:S(2)}) collective-permute-start(bf16[2,128,512]{2,1,0:T(8,128)(2,1)S(1)} %pad_maximum_fusion), channel_id=1, source_target_pairs={{0,16},{8,24},{16,0},{24,8},{1,17},{9,25},{17,1},{25,9},{2,18},{10... | collective-permute-start | bytes 786440 | tf_op jit(solution)/shard_map/ppermute | solution.py:38
  97.8 7.6 %collective-permute-done.26.refs_3_ = bf16[1024,512]{1,0:T(8,128)(2,1)S(1)} collective-permute-done((bf16[1024,512]{1,0:T(8,128)(2,1)}, bf16[1024,512]{1,0:T(8,128)(2,1)S(1)}, u32[]{:S(2)}, u32[]{:S(2)}) %collective-permute-start.26) | collective-permute-done | bytes 1048608 | tf_op jit(solution)/shard_map/ppermute | solution.py:38
  105.4 0.9 copy-done.27
  106.3 7.4 %expert_slope.1.slope_ref = bf16[384,1024]{1,0:T(8,128)(2,1)} custom-call(s32[1]{0:T(128)} %bitcast.27.here_ref, bf16[192,2048]{1,0:T(8,128)(2,1)} %copy-done.7, bf16[192,2048]{1,0:T(8,128)(2,1)} %copy-done.27, f32[192,1024]{1,0:T(8,128)} %get-tuple-element.96.rise_own, f32[192,1024]{1,0:T(8,128)} %get-tuple-element.97.rise_core, bf16[1024,2048]{1,0:T(8,128)(2,1)} %bitcast.84), custom_call_target="tpu_custom_call" | custom-call | flops 1 | bytes 1 | tf_op jit(solution)/shard_map/expert_slope/pallas_call | solution.py:478
  113.8 5.8 %expert_backward.1 = (bf16[2,384,512]{2,1,0:T(8,128)(2,1)}, f32[384,512]{1,0:T(8,128)}, f32[384,512]{1,0:T(8,128)}) custom-call(s32[1]{0:T(128)} %bitcast.7.section_ref, bf16[384,1024]{1,0:T(8,128)(2,1)} %expert_slope.1.slope_ref, bf16[2048,1024]{1,0:T(8,128)(2,1)} %bitcast.83), custom_call_target="tpu_custom_call" | custom-call | flops 1 | bytes 1 | tf_op jit(solution)/shard_map/expert_backward/pallas_call | solution.py:520
  120.8 1.1 collective-permute-start.28
  121.9 1.3 collective-permute-start.30
  125.0 2.3 %collective-permute-done.27.refs_5_ = bf16[1024,512]{1,0:T(8,128)(2,1)} collective-permute-done((bf16[1024,512]{1,0:T(8,128)(2,1)}, bf16[1024,512]{1,0:T(8,128)(2,1)}, u32[]{:S(2)}, u32[]{:S(2)}) %collective-permute-start.27) | collective-permute-done | bytes 1048608 | tf_op jit(solution)/shard_map/ppermute | solution.py:38
  127.3 5.4 %attend_sentence.2.mine_ref = bf16[128,512]{1,0:T(8,128)(2,1)} custom-call(s32[3]{0:T(128)} %pad_add_fusion.1.place_ref, s32[2]{0:T(128)} %lengths_ref.3, bf16[128,512]{1,0:T(8,128)(2,1)} %get-tuple-element.91.query_ref, bf16[128,2048]{1,0:T(8,128)(2,1)} %copy-done.3, bf16[128,2048]{1,0:T(8,128)(2,1)} %collective-permute-done.25.refs_1_, ...), custom_call_target="tpu_custom_call" | custom-call | flops 1 | bytes 1 | tf_op jit(solution)/shard_map/attend_sentence/pallas_call | solution.py:380
  132.8 2.5 %collective-permute-done.28.refs_0_ = bf16[128,2048]{1,0:T(8,128)(2,1)} collective-permute-done((bf16[128,2048]{1,0:T(8,128)(2,1)S(1)}, bf16[128,2048]{1,0:T(8,128)(2,1)}, u32[]{:S(2)}, u32[]{:S(2)}) %collective-permute-start.28) | collective-permute-done | bytes 524320 | tf_op jit(solution)/shard_map/ppermute | solution.py:38
  135.7 1.1 fusion.35
  136.9 2.7 %collective-permute-start.34 = (bf16[384,512]{1,0:T(8,128)(2,1)S(1)}, bf16[384,512]{1,0:T(8,128)(2,1)S(1)}, u32[]{:S(2)}, u32[]{:S(2)}) collective-permute-start(bf16[384,512]{1,0:T(8,128)(2,1)S(1)} %fusion.35), channel_id=1, source_target_pairs={{0,16},{8,24},{16,0},{24,8},{1,17},{9,25},{17,1},{25,9},{2,18},{10... | collective-permute-start | bytes 1179656 | tf_op jit(solution)/shard_map/ppermute | solution.py:38
  140.9 5.5 %attend_sentence.3.done_ref = bf16[128,512]{1,0:T(8,128)(2,1)} custom-call(s32[3]{0:T(128)} %pad_add_fusion.3.place_ref, s32[2]{0:T(128)} %lengths_ref.3, bf16[128,512]{1,0:T(8,128)(2,1)} %get-tuple-element.90.query_ref, bf16[128,2048]{1,0:T(8,128)(2,1)} %collective-permute-done.28.refs_0_, bf16[128,2048]{1,0:T(8,128)(2,1)} %copy-done.30, ...), custom_call_target="tpu_custom_call" | custom-call | flops 1 | bytes 1 | tf_op jit(solution)/shard_map/attend_sentence/pallas_call | solution.py:380
  146.4 2.1 %collective-permute-done.30.other_ref = bf16[512,1024]{1,0:T(8,128)(2,1)} collective-permute-done((bf16[512,1024]{1,0:T(8,128)(2,1)S(1)}, bf16[512,1024]{1,0:T(8,128)(2,1)}, u32[]{:S(2)}, u32[]{:S(2)}) %collective-permute-start.30) | collective-permute-done | bytes 1048608 | tf_op jit(solution)/shard_map/ppermute | solution.py:38
  148.6 0.9 copy-done.9
  149.5 2.0 %project.1 = (bf16[256,512]{1,0:T(8,128)(2,1)S(1)}, bf16[256,512]{1,0:T(8,128)(2,1)S(1)}, f32[256,512]{1,0:T(8,128)S(1)}, f32[256,512]{1,0:T(8,128)S(1)}) custom-call(s32[3]{0:T(128)S(1)} %copy-done.22, bf16[128,512]{1,0:T(8,128)(2,1)S(1)} %copy-done.8, bf16[128,512]{1,0:T(8,128)(2,1)S(1)} %copy-done.9, bf16[512,1024]{1,0:T(8,128)(2,1)S(1)} %bitcast.80, ...), custom_call_target="tpu_custom_call" | custom-call | flops 1 | bytes 1 | tf_op jit(solution)/shard_map/project/pallas_call | solution.py:431
  152.0 5.3 %collective-permute-done.34 = bf16[384,512]{1,0:T(8,128)(2,1)S(1)} collective-permute-done((bf16[384,512]{1,0:T(8,128)(2,1)S(1)}, bf16[384,512]{1,0:T(8,128)(2,1)S(1)}, u32[]{:S(2)}, u32[]{:S(2)}) %collective-permute-start.34) | collective-permute-done | bytes 393248 | tf_op jit(solution)/shard_map/ppermute | solution.py:38
  157.4 1.1 collective-permute-start.36
  158.5 1.9 %fusion.34 = bf16[384,512]{1,0:T(8,128)(2,1)} fusion(f32[384,512]{1,0:T(8,128)S(1)} %copy-done.29, bf16[384,512]{1,0:T(8,128)(2,1)S(1)} %collective-permute-done.34, bf16[2,384,512]{2,1,0:T(8,128)(2,1)} %collective-permute-done.33), kind=kLoop, calls=%fused_computation.45 | loop fusion | flops 983040 | bytes 1966080 | tf_op jit(solution)/shard_map/convert_element_type | solution.py:710
  160.4 3.5 %all-to-all-start = ((bf16[8,48,512]{2,1,0:T(8,128)(2,1)}), bf16[8,48,512]{2,1,0:T(8,128)(2,1)S(1)}, u32[]{:S(2)}, u32[]{:S(2)}) async-start(bf16[8,48,512]{2,1,0:T(8,128)(2,1)} %bitcast.31), calls=%async_computation | async-start | bytes 786432 | tf_op jit(solution)/shard_map/all_to_all | solution.py:142
  164.9 1.8 %fusion.47 = bf16[1,256,512]{2,1,0:T(8,128)(2,1)} fusion(bf16[256,512]{1,0:T(8,128)(2,1)S(1)} %collective-permute-done.36, f32[256,512]{1,0:T(8,128)S(1)} %get-tuple-element.69, bf16[256,512]{1,0:T(8,128)(2,1)S(1)} %collective-permute-done.31, bf16[1,256,2048]{2,1,0:T(8,128)(2,1)} %param.22, s32[]{:T(128)S(6)} %select_n.35, ...), kind=kLoop, calls=%fused_computation.62 | loop fusion | flops 1048576 | bytes 1573124 | tf_op jit(solution)/shard_map/broadcast_in_dim | solution.py:715
  166.7 5.4 %all-to-all-done = bf16[8,48,512]{2,1,0:T(8,128)(2,1)S(1)} async-done(((bf16[8,48,512]{2,1,0:T(8,128)(2,1)}), bf16[8,48,512]{2,1,0:T(8,128)(2,1)S(1)}, u32[]{:S(2)}, u32[]{:S(2)}) %all-to-all-start) | async-done | bytes 393248 | tf_op jit(solution)/shard_map/all_to_all | solution.py:142
  172.2 1.0 combine.3
  (129 shorter events, 21.3 us)
Async XLA Ops:
  0.6 46.4 %copy-start = (bf16[1,1024,512]{2,1,0:T(8,128)(2,1)S(1)}, bf16[1,1024,512]{2,1,0:T(8,128)(2,1)}, u32[]{:S(2)}) copy-start(bf16[1,1024,512]{2,1,0:T(8,128)(2,1)} %param.26) | copy-start | bytes 3145732
  0.6 8.3 %collective-permute-start.3 = (s32[2,128]{1,0:T(2,128)}, s32[2,128]{1,0:T(2,128)S(1)}, u32[]{:S(2)}, u32[]{:S(2)}) collective-permute-start(s32[2,128]{1,0:T(2,128)} %bitcast.88), channel_id=1, source_target_pairs={{0,2},{1,3},{2,0},{3,1},{4,6},{5,7},{6,4},{7,5},{8,10},{9,11},{10,... | collective-permute-start | bytes 3080 | tf_op jit(solution)/shard_map/ppermute | solution.py:38
  3.6 5.4 %collective-permute-start.4 = (s32[2,128]{1,0:T(2,128)}, s32[2,128]{1,0:T(2,128)S(1)}, u32[]{:S(2)}, u32[]{:S(2)}) collective-permute-start(s32[2,128]{1,0:T(2,128)} %bitcast.89), channel_id=1, source_target_pairs={{0,4},{4,0},{1,5},{5,1},{2,6},{6,2},{3,7},{7,3},{8,12},{12,8},{9,1... | collective-permute-start | bytes 3080 | tf_op jit(solution)/shard_map/ppermute | solution.py:38
  5.2 13.3 %collective-permute-start = (bf16[128,2048]{1,0:T(8,128)(2,1)}, bf16[128,2048]{1,0:T(8,128)(2,1)S(1)}, u32[]{:S(2)}, u32[]{:S(2)}) collective-permute-start(bf16[128,2048]{1,0:T(8,128)(2,1)} %tokens_ref.1), channel_id=1, source_target_pairs={{0,4},{4,0},{1,5},{5,1},{2,6},{6,2},{3,7},{7,3},{8,12},{12,8},{9,1... | collective-permute-start | bytes 1572872 | tf_op jit(solution)/shard_map/ppermute | solution.py:38
  5.7 27.0 %collective-permute-start.6 = (bf16[128,2048]{1,0:T(8,128)(2,1)}, bf16[128,2048]{1,0:T(8,128)(2,1)S(1)}, u32[]{:S(2)}, u32[]{:S(2)}) collective-permute-start(bf16[128,2048]{1,0:T(8,128)(2,1)} %tokens_ref.1), channel_id=1, source_target_pairs={{0,2},{1,3},{2,0},{3,1},{4,6},{5,7},{6,4},{7,5},{8,10},{9,11},{10,... | collective-permute-start | bytes 1572872 | tf_op jit(solution)/shard_map/ppermute | solution.py:38
  18.5 12.7 %collective-permute-start.7 = (bf16[128,2048]{1,0:T(8,128)(2,1)S(1)}, bf16[128,2048]{1,0:T(8,128)(2,1)S(1)}, u32[]{:S(2)}, u32[]{:S(2)}) collective-permute-start(bf16[128,2048]{1,0:T(8,128)(2,1)S(1)} %collective-permute-done.refs_2_), channel_id=1, source_target_pairs={{0,2},{1,3},{2,0},{3,1},{4,6},{5,7},{6,4},{7,5},{8,10},{9,11},{10,... | collective-permute-start | bytes 1572872 | tf_op jit(solution)/shard_map/ppermute | solution.py:38
  20.7 5.6 %collective-permute-start.5 = (s32[2,128]{1,0:T(2,128)S(1)}, s32[2,128]{1,0:T(2,128)S(1)}, u32[]{:S(2)}, u32[]{:S(2)}) collective-permute-start(s32[2,128]{1,0:T(2,128)S(1)} %collective-permute-done.3), channel_id=1, source_target_pairs={{0,4},{4,0},{1,5},{5,1},{2,6},{6,2},{3,7},{7,3},{8,12},{12,8},{9,1... | collective-permute-start | bytes 3080 | tf_op jit(solution)/shard_map/ppermute | solution.py:38
  21.0 6.7 %collective-permute-start.1 = (bf16[64,2048]{1,0:T(8,128)(2,1)}, bf16[64,2048]{1,0:T(8,128)(2,1)}, u32[]{:S(2)}, u32[]{:S(2)}) collective-permute-start(bf16[64,2048]{1,0:T(8,128)(2,1)} %constant_dynamic-slice_fusion.2), channel_id=1, source_target_pairs={{0,4},{4,0},{1,5},{5,1},{2,6},{6,2},{3,7},{7,3},{8,12},{12,8},{9,1... | collective-permute-start | bytes 786440 | tf_op jit(solution)/shard_map/ppermute | solution.py:38
  22.7 1.2 copy-start.4
  27.7 18.3 %collective-permute-start.2 = (bf16[256,1024]{1,0:T(8,128)(2,1)}, bf16[256,1024]{1,0:T(8,128)(2,1)S(1)}, u32[]{:S(2)}, u32[]{:S(2)}) collective-permute-start(bf16[256,1024]{1,0:T(8,128)(2,1)} %copy-done.23), channel_id=1, source_target_pairs={{0,4},{4,0},{1,5},{5,1},{2,6},{6,2},{3,7},{7,3},{8,12},{12,8},{9,1... | collective-permute-start | bytes 1572872 | tf_op jit(solution)/shard_map/ppermute | solution.py:38
  29.6 8.7 %collective-permute-start.9 = (bf16[64,2048]{1,0:T(8,128)(2,1)}, bf16[64,2048]{1,0:T(8,128)(2,1)S(1)}, u32[]{:S(2)}, u32[]{:S(2)}) collective-permute-start(bf16[64,2048]{1,0:T(8,128)(2,1)} %collective-permute-done.1), channel_id=1, source_target_pairs={{0,8},{8,0},{16,24},{24,16},{1,9},{9,1},{17,25},{25,17},{2,10},{10... | collective-permute-start | bytes 786440 | tf_op jit(solution)/shard_map/ppermute | solution.py:38
  31.2 7.1 %collective-permute-start.10 = (bf16[64,2048]{1,0:T(8,128)(2,1)}, bf16[64,2048]{1,0:T(8,128)(2,1)S(1)}, u32[]{:S(2)}, u32[]{:S(2)}) collective-permute-start(bf16[64,2048]{1,0:T(8,128)(2,1)} %constant_dynamic-slice_fusion.2), channel_id=1, source_target_pairs={{0,2},{1,3},{2,0},{3,1},{4,6},{5,7},{6,4},{7,5},{8,10},{9,11},{10,... | collective-permute-start | bytes 786440 | tf_op jit(solution)/shard_map/ppermute | solution.py:38
  32.7 1.0 copy-start.1
  33.7 4.6 %copy-start.25 = (bf16[1,1024,2048]{2,1,0:T(8,128)(2,1)S(1)}, bf16[1,1024,2048]{2,1,0:T(8,128)(2,1)}, u32[]{:S(2)}) copy-start(bf16[1,1024,2048]{2,1,0:T(8,128)(2,1)} %param.20) | copy-start | bytes 12582916
  35.0 8.1 %collective-permute-start.8 = (bf16[192,2048]{1,0:T(8,128)(2,1)S(1)}, bf16[192,2048]{1,0:T(8,128)(2,1)S(1)}, u32[]{:S(2)}, u32[]{:S(2)}) collective-permute-start(bf16[192,2048]{1,0:T(8,128)(2,1)S(1)} %get-tuple-element.47), channel_id=1, source_target_pairs={{0,1},{1,0},{2,3},{3,2},{4,5},{5,4},{6,7},{7,6},{8,9},{9,8},{10,11... | collective-permute-start | bytes 2359304 | tf_op jit(solution)/shard_map/ppermute | solution.py:38
  38.3 4.8 %copy-start.24 = (bf16[1,2048,1024]{2,1,0:T(8,128)(2,1)S(1)}, bf16[1,2048,1024]{2,1,0:T(8,128)(2,1)}, u32[]{:S(2)}) copy-start(bf16[1,2048,1024]{2,1,0:T(8,128)(2,1)} %param.19) | copy-start | bytes 12582916
  39.5 8.7 %collective-permute-start.15 = (bf16[48,2048]{1,0:T(8,128)(2,1)S(1)}, bf16[48,2048]{1,0:T(8,128)(2,1)S(1)}, u32[]{:S(2)}, u32[]{:S(2)}) collective-permute-start(bf16[48,2048]{1,0:T(8,128)(2,1)S(1)} %get-tuple-element.89), channel_id=1, source_target_pairs={{0,2},{1,3},{2,0},{3,1},{4,6},{5,7},{6,4},{7,5},{8,10},{9,11},{10,... | collective-permute-start | bytes 589832 | tf_op jit(solution)/shard_map/ppermute | solution.py:223
  40.5 10.7 %collective-permute-start.16 = (bf16[48,2048]{1,0:T(8,128)(2,1)S(1)}, bf16[48,2048]{1,0:T(8,128)(2,1)S(1)}, u32[]{:S(2)}, u32[]{:S(2)}) collective-permute-start(bf16[48,2048]{1,0:T(8,128)(2,1)S(1)} %get-tuple-element.88), channel_id=1, source_target_pairs={{0,4},{1,5},{2,6},{3,7},{4,0},{5,1},{6,2},{7,3},{8,12},{9,13},{10,... | collective-permute-start | bytes 589832 | tf_op jit(solution)/shard_map/ppermute | solution.py:223
  41.0 10.9 %collective-permute-start.17 = (bf16[48,2048]{1,0:T(8,128)(2,1)S(1)}, bf16[48,2048]{1,0:T(8,128)(2,1)S(1)}, u32[]{:S(2)}, u32[]{:S(2)}) collective-permute-start(bf16[48,2048]{1,0:T(8,128)(2,1)S(1)} %get-tuple-element.87), channel_id=1, source_target_pairs={{0,6},{1,7},{2,4},{3,5},{4,2},{5,3},{6,0},{7,1},{8,14},{9,15},{10,... | collective-permute-start | bytes 589832 | tf_op jit(solution)/shard_map/ppermute | solution.py:223
  45.1 15.1 %copy-start.33 = (f32[128,2]{0,1:T(2,128)S(1)}, f32[128,2]{0,1:T(2,128)}, u32[]{:S(2)}) copy-start(f32[128,2]{0,1:T(2,128)} %param.17) | copy-start | bytes 3076
  46.0 39.8 %copy-start.5 = (bf16[128,2048]{1,0:T(8,128)(2,1)S(1)}, bf16[128,2048]{1,0:T(8,128)(2,1)}, u32[]{:S(2)}) copy-start(bf16[128,2048]{1,0:T(8,128)(2,1)} %refs_0_.3) | copy-start | bytes 1572868
  46.0 9.8 %collective-permute-start.14 = (bf16[48,2048]{1,0:T(8,128)(2,1)S(1)}, bf16[48,2048]{1,0:T(8,128)(2,1)S(1)}, u32[]{:S(2)}, u32[]{:S(2)}) collective-permute-start(bf16[48,2048]{1,0:T(8,128)(2,1)S(1)} %get-tuple-element.83), channel_id=1, source_target_pairs={{0,1},{1,0},{2,3},{3,2},{4,5},{5,4},{6,7},{7,6},{8,9},{9,8},{10,11... | collective-permute-start | bytes 589832 | tf_op jit(solution)/shard_map/ppermute | solution.py:223
  46.0 10.4 %collective-permute-start.11 = (bf16[48,2048]{1,0:T(8,128)(2,1)S(1)}, bf16[48,2048]{1,0:T(8,128)(2,1)S(1)}, u32[]{:S(2)}, u32[]{:S(2)}) collective-permute-start(bf16[48,2048]{1,0:T(8,128)(2,1)S(1)} %get-tuple-element.85), channel_id=1, source_target_pairs={{0,3},{1,2},{2,1},{3,0},{4,7},{5,6},{6,5},{7,4},{8,11},{9,10},{10,... | collective-permute-start | bytes 589832 | tf_op jit(solution)/shard_map/ppermute | solution.py:223
  52.6 7.7 %collective-permute-start.18 = (bf16[64,2048]{1,0:T(8,128)(2,1)S(1)}, bf16[64,2048]{1,0:T(8,128)(2,1)S(1)}, u32[]{:S(2)}, u32[]{:S(2)}) collective-permute-start(bf16[64,2048]{1,0:T(8,128)(2,1)S(1)} %collective-permute-done.10.refs_1_), channel_id=1, source_target_pairs={{0,8},{8,0},{16,24},{24,16},{1,9},{9,1},{17,25},{25,17},{2,10},{10... | collective-permute-start | bytes 786440 | tf_op jit(solution)/shard_map/ppermute | solution.py:38
  53.8 10.7 %collective-permute-start.12 = (bf16[48,2048]{1,0:T(8,128)(2,1)}, bf16[48,2048]{1,0:T(8,128)(2,1)}, u32[]{:S(2)}, u32[]{:S(2)}) collective-permute-start(bf16[48,2048]{1,0:T(8,128)(2,1)} %get-tuple-element.84), channel_id=1, source_target_pairs={{0,5},{1,4},{2,7},{3,6},{4,1},{5,0},{6,3},{7,2},{8,13},{9,12},{10,... | collective-permute-start | bytes 589832 | tf_op jit(solution)/shard_map/ppermute | solution.py:223
  53.8 10.7 %collective-permute-start.19 = (bf16[48,2048]{1,0:T(8,128)(2,1)}, bf16[48,2048]{1,0:T(8,128)(2,1)}, u32[]{:S(2)}, u32[]{:S(2)}) collective-permute-start(bf16[48,2048]{1,0:T(8,128)(2,1)} %get-tuple-element.82), channel_id=1, source_target_pairs={{0,7},{1,6},{2,5},{3,4},{4,3},{5,2},{6,1},{7,0},{8,15},{9,14},{10,... | collective-permute-start | bytes 589832 | tf_op jit(solution)/shard_map/ppermute | solution.py:223
  64.5 0.9 copy-start.11
  65.4 0.9 copy-start.13
  66.4 0.9 copy-start.15
  67.3 0.9 copy-start.17
  68.2 0.9 copy-start.19
  71.0 7.7 %collective-permute-start.20 = (bf16[2,128,512]{2,1,0:T(8,128)(2,1)S(1)}, bf16[2,128,512]{2,1,0:T(8,128)(2,1)S(1)}, u32[]{:S(2)}, u32[]{:S(2)}) collective-permute-start(bf16[2,128,512]{2,1,0:T(8,128)(2,1)S(1)} %get-tuple-element.60), channel_id=1, source_target_pairs={{0,8},{8,0},{16,24},{24,16},{1,9},{9,1},{17,25},{25,17},{2,10},{10... | collective-permute-start | bytes 786440 | tf_op jit(solution)/shard_map/ppermute | solution.py:38
  72.5 13.3 %collective-permute-start.21 = (bf16[128,2048]{1,0:T(8,128)(2,1)S(1)}, bf16[128,2048]{1,0:T(8,128)(2,1)S(1)}, u32[]{:S(2)}, u32[]{:S(2)}) collective-permute-start(bf16[128,2048]{1,0:T(8,128)(2,1)S(1)} %constant_dynamic-update-slice_fusion.refs_3_), channel_id=1, source_target_pairs={{0,2},{1,3},{2,0},{3,1},{4,6},{5,7},{6,4},{7,5},{8,10},{9,11},{10,... | collective-permute-start | bytes 1572872 | tf_op jit(solution)/shard_map/ppermute | solution.py:38
  73.5 14.7 %collective-permute-start.13 = (bf16[256,512]{1,0:T(8,128)(2,1)}, bf16[256,512]{1,0:T(8,128)(2,1)S(1)}, u32[]{:S(2)}, u32[]{:S(2)}) collective-permute-start(bf16[256,512]{1,0:T(8,128)(2,1)} %fusion.1), channel_id=1, source_target_pairs={{0,4},{4,0},{1,5},{5,1},{2,6},{6,2},{3,7},{7,3},{8,12},{12,8},{9,1... | collective-permute-start | bytes 786440 | tf_op jit(solution)/shard_map/ppermute | solution.py:38
  74.8 30.6 %collective-permute-start.26 = (bf16[1024,512]{1,0:T(8,128)(2,1)}, bf16[1024,512]{1,0:T(8,128)(2,1)S(1)}, u32[]{:S(2)}, u32[]{:S(2)}) collective-permute-start(bf16[1024,512]{1,0:T(8,128)(2,1)} %bitcast.85), channel_id=1, source_target_pairs={{0,4},{4,0},{1,5},{5,1},{2,6},{6,2},{3,7},{7,3},{8,12},{12,8},{9,1... | collective-permute-start | bytes 3145736 | tf_op jit(solution)/shard_map/ppermute | solution.py:38
  78.7 9.4 %collective-permute-start.22 = (bf16[128,512]{1,0:T(8,128)(2,1)S(1)}, bf16[128,512]{1,0:T(8,128)(2,1)S(1)}, u32[]{:S(2)}, u32[]{:S(2)}) collective-permute-start(bf16[128,512]{1,0:T(8,128)(2,1)S(1)} %fusion.50), channel_id=1, source_target_pairs={{0,16},{8,24},{16,0},{24,8},{1,17},{9,25},{17,1},{25,9},{2,18},{10... | collective-permute-start | bytes 393224 | tf_op jit(solution)/shard_map/ppermute | solution.py:38
  88.2 17.3 %collective-permute-start.32 = (bf16[192,2048]{1,0:T(8,128)(2,1)S(1)}, bf16[192,2048]{1,0:T(8,128)(2,1)S(1)}, u32[]{:S(2)}, u32[]{:S(2)}) collective-permute-start(bf16[192,2048]{1,0:T(8,128)(2,1)S(1)} %get-tuple-element.63), channel_id=1, source_target_pairs={{0,1},{1,0},{2,3},{3,2},{4,5},{5,4},{6,7},{7,6},{8,9},{9,8},{10,11... | collective-permute-start | bytes 2359304 | tf_op jit(solution)/shard_map/ppermute | solution.py:38
  88.2 25.5 %copy-start.31 = (bf16[256,512]{1,0:T(8,128)(2,1)}, bf16[256,512]{1,0:T(8,128)(2,1)S(1)}, u32[]{:S(2)}) copy-start(bf16[256,512]{1,0:T(8,128)(2,1)S(1)} %collective-permute-done.13) | copy-start | bytes 786436
  88.2 6.0 %collective-permute-start.23 = (bf16[128,512]{1,0:T(8,128)(2,1)S(1)}, bf16[128,512]{1,0:T(8,128)(2,1)S(1)}, u32[]{:S(2)}, u32[]{:S(2)}) collective-permute-start(bf16[128,512]{1,0:T(8,128)(2,1)S(1)} %fusion.49.refs_0_), channel_id=1, source_target_pairs={{0,8},{8,0},{16,24},{24,16},{1,9},{9,1},{17,25},{25,17},{2,10},{10... | collective-permute-start | bytes 393224 | tf_op jit(solution)/shard_map/ppermute | solution.py:38
  94.2 33.1 %collective-permute-start.27 = (bf16[1024,512]{1,0:T(8,128)(2,1)}, bf16[1024,512]{1,0:T(8,128)(2,1)}, u32[]{:S(2)}, u32[]{:S(2)}) collective-permute-start(bf16[1024,512]{1,0:T(8,128)(2,1)} %bitcast.24.refs_4_), channel_id=1, source_target_pairs={{0,4},{4,0},{1,5},{5,1},{2,6},{6,2},{3,7},{7,3},{8,12},{12,8},{9,1... | collective-permute-start | bytes 3145736 | tf_op jit(solution)/shard_map/ppermute | solution.py:38
  95.2 25.1 %collective-permute-start.24 = (bf16[2,128,512]{2,1,0:T(8,128)(2,1)S(1)}, bf16[2,128,512]{2,1,0:T(8,128)(2,1)S(1)}, u32[]{:S(2)}, u32[]{:S(2)}) collective-permute-start(bf16[2,128,512]{2,1,0:T(8,128)(2,1)S(1)} %pad_maximum_fusion), channel_id=1, source_target_pairs={{0,16},{8,24},{16,0},{24,8},{1,17},{9,25},{17,1},{25,9},{2,18},{10... | collective-permute-start | bytes 786440 | tf_op jit(solution)/shard_map/ppermute | solution.py:38
  105.4 14.2 %copy-start.26 = (bf16[1024,512]{1,0:T(8,128)(2,1)}, bf16[1024,512]{1,0:T(8,128)(2,1)S(1)}, u32[]{:S(2)}) copy-start(bf16[1024,512]{1,0:T(8,128)(2,1)S(1)} %collective-permute-done.26.refs_3_) | copy-start | bytes 3145732
  105.4 0.9 copy-start.27
  113.7 6.6 %copy-start.2 = (bf16[128,2048]{1,0:T(8,128)(2,1)S(1)}, bf16[128,2048]{1,0:T(8,128)(2,1)}, u32[]{:S(2)}) copy-start(bf16[128,2048]{1,0:T(8,128)(2,1)} %tokens_ref.1) | copy-start | bytes 1572868
  113.7 6.6 %copy-start.21 = (f32[2048]{0:T(1024)S(1)}, f32[2048]{0:T(1024)}, u32[]{:S(2)}) copy-start(f32[2048]{0:T(1024)} %param.21) | copy-start | bytes 24580
  113.7 8.2 %copy-start.6 = (bf16[1,512,1024]{2,1,0:T(8,128)(2,1)S(1)}, bf16[1,512,1024]{2,1,0:T(8,128)(2,1)}, u32[]{:S(2)}) copy-start(bf16[1,512,1024]{2,1,0:T(8,128)(2,1)} %param.29) | copy-start | bytes 3145732
  113.7 10.1 %copy-start.32 = (bf16[256,512]{1,0:T(8,128)(2,1)S(1)}, bf16[256,512]{1,0:T(8,128)(2,1)}, u32[]{:S(2)}) copy-start(bf16[256,512]{1,0:T(8,128)(2,1)} %copy-done.31) | copy-start | bytes 786436
  119.6 16.1 %collective-permute-start.33 = (bf16[2,384,512]{2,1,0:T(8,128)(2,1)}, bf16[2,384,512]{2,1,0:T(8,128)(2,1)}, u32[]{:S(2)}, u32[]{:S(2)}) collective-permute-start(bf16[2,384,512]{2,1,0:T(8,128)(2,1)} %get-tuple-element.75), channel_id=1, source_target_pairs={{0,8},{8,0},{16,24},{24,16},{1,9},{9,1},{17,25},{25,17},{2,10},{10... | collective-permute-start | bytes 2359304 | tf_op jit(solution)/shard_map/ppermute | solution.py:38
  120.7 6.6 %copy-start.3 = (bf16[128,2048]{1,0:T(8,128)(2,1)}, bf16[128,2048]{1,0:T(8,128)(2,1)S(1)}, u32[]{:S(2)}) copy-start(bf16[128,2048]{1,0:T(8,128)(2,1)S(1)} %memory.1.refs_0_) | copy-start | bytes 1572868
  120.8 4.3 %collective-permute-start.25 = (bf16[128,2048]{1,0:T(8,128)(2,1)S(1)}, bf16[128,2048]{1,0:T(8,128)(2,1)}, u32[]{:S(2)}, u32[]{:S(2)}) collective-permute-start(bf16[128,2048]{1,0:T(8,128)(2,1)S(1)} %memory.1.refs_0_), channel_id=1, source_target_pairs={{0,1},{1,0},{2,3},{3,2},{4,5},{5,4},{6,7},{7,6},{8,9},{9,8},{10,11... | collective-permute-start | bytes 1572872 | tf_op jit(solution)/shard_map/ppermute | solution.py:38
  120.8 14.4 %collective-permute-start.28 = (bf16[128,2048]{1,0:T(8,128)(2,1)S(1)}, bf16[128,2048]{1,0:T(8,128)(2,1)}, u32[]{:S(2)}, u32[]{:S(2)}) collective-permute-start(bf16[128,2048]{1,0:T(8,128)(2,1)S(1)} %memory.1.refs_0_), channel_id=1, source_target_pairs={{0,2},{1,3},{2,0},{3,1},{4,6},{5,7},{6,4},{7,5},{8,10},{9,11},{10,... | collective-permute-start | bytes 1572872 | tf_op jit(solution)/shard_map/ppermute | solution.py:38
  121.9 26.6 %collective-permute-start.30 = (bf16[512,1024]{1,0:T(8,128)(2,1)S(1)}, bf16[512,1024]{1,0:T(8,128)(2,1)}, u32[]{:S(2)}, u32[]{:S(2)}) collective-permute-start(bf16[512,1024]{1,0:T(8,128)(2,1)S(1)} %bitcast.79), channel_id=1, source_target_pairs={{0,4},{4,0},{1,5},{5,1},{2,6},{6,2},{3,7},{7,3},{8,12},{12,8},{9,1... | collective-permute-start | bytes 3145736 | tf_op jit(solution)/shard_map/ppermute | solution.py:38
  123.8 11.9 %copy-start.28 = (f32[384,512]{1,0:T(8,128)S(1)}, f32[384,512]{1,0:T(8,128)}, u32[]{:S(2)}) copy-start(f32[384,512]{1,0:T(8,128)} %get-tuple-element.74) | copy-start | bytes 2359300
  132.7 15.8 %copy-start.8 = (bf16[128,512]{1,0:T(8,128)(2,1)S(1)}, bf16[128,512]{1,0:T(8,128)(2,1)}, u32[]{:S(2)}) copy-start(bf16[128,512]{1,0:T(8,128)(2,1)} %attend_sentence.2.mine_ref) | copy-start | bytes 393220
  132.8 15.8 %copy-start.22 = (s32[3]{0:T(128)S(1)}, s32[3]{0:T(128)}, u32[]{:S(2)}) copy-start(s32[3]{0:T(128)} %pad_add_fusion.1.place_ref) | copy-start | bytes 40
  135.3 4.8 %collective-permute-start.29 = (bf16[128,2048]{1,0:T(8,128)(2,1)}, bf16[128,2048]{1,0:T(8,128)(2,1)S(1)}, u32[]{:S(2)}, u32[]{:S(2)}) collective-permute-start(bf16[128,2048]{1,0:T(8,128)(2,1)} %collective-permute-done.28.refs_0_), channel_id=1, source_target_pairs={{0,1},{1,0},{2,3},{3,2},{4,5},{5,4},{6,7},{7,6},{8,9},{9,8},{10,11... | collective-permute-start | bytes 1572872 | tf_op jit(solution)/shard_map/ppermute | solution.py:38
  136.9 20.5 %collective-permute-start.34 = (bf16[384,512]{1,0:T(8,128)(2,1)S(1)}, bf16[384,512]{1,0:T(8,128)(2,1)S(1)}, u32[]{:S(2)}, u32[]{:S(2)}) collective-permute-start(bf16[384,512]{1,0:T(8,128)(2,1)S(1)} %fusion.35), channel_id=1, source_target_pairs={{0,16},{8,24},{16,0},{24,8},{1,17},{9,25},{17,1},{25,9},{2,18},{10... | collective-permute-start | bytes 1179656 | tf_op jit(solution)/shard_map/ppermute | solution.py:38
  140.9 17.6 %copy-start.29 = (f32[384,512]{1,0:T(8,128)S(1)}, f32[384,512]{1,0:T(8,128)}, u32[]{:S(2)}) copy-start(f32[384,512]{1,0:T(8,128)} %get-tuple-element.78) | copy-start | bytes 2359300
  148.6 0.9 copy-start.9
  149.5 14.4 %copy-start.34 = (s32[2]{0:T(128)S(1)}, s32[2]{0:T(128)}, u32[]{:S(2)}) copy-start(s32[2]{0:T(128)} %param.24) | copy-start | bytes 28
  151.5 5.9 %collective-permute-start.35 = (bf16[256,512]{1,0:T(8,128)(2,1)S(1)}, bf16[256,512]{1,0:T(8,128)(2,1)S(1)}, u32[]{:S(2)}, u32[]{:S(2)}) collective-permute-start(bf16[256,512]{1,0:T(8,128)(2,1)S(1)} %get-tuple-element.77), channel_id=1, source_target_pairs={{0,1},{1,0},{2,3},{3,2},{4,5},{5,4},{6,7},{7,6},{8,9},{9,8},{10,11... | collective-permute-start | bytes 786440 | tf_op jit(solution)/shard_map/ppermute | solution.py:38
  151.5 12.6 %collective-permute-start.31 = (bf16[256,512]{1,0:T(8,128)(2,1)S(1)}, bf16[256,512]{1,0:T(8,128)(2,1)S(1)}, u32[]{:S(2)}, u32[]{:S(2)}) collective-permute-start(bf16[256,512]{1,0:T(8,128)(2,1)S(1)} %get-tuple-element.70), channel_id=1, source_target_pairs={{0,1},{1,0},{2,3},{3,2},{4,5},{5,4},{6,7},{7,6},{8,9},{9,8},{10,11... | collective-permute-start | bytes 786440 | tf_op jit(solution)/shard_map/ppermute | solution.py:38
  157.4 7.5 %collective-permute-start.36 = (bf16[256,512]{1,0:T(8,128)(2,1)S(1)}, bf16[256,512]{1,0:T(8,128)(2,1)S(1)}, u32[]{:S(2)}, u32[]{:S(2)}) collective-permute-start(bf16[256,512]{1,0:T(8,128)(2,1)S(1)} %convert_add_fusion.3), channel_id=1, source_target_pairs={{0,2},{1,3},{2,0},{3,1},{4,6},{5,7},{6,4},{7,5},{8,10},{9,11},{10,... | collective-permute-start | bytes 786440 | tf_op jit(solution)/shard_map/ppermute | solution.py:38
  160.4 11.7 %all-to-all-start = ((bf16[8,48,512]{2,1,0:T(8,128)(2,1)}), bf16[8,48,512]{2,1,0:T(8,128)(2,1)S(1)}, u32[]{:S(2)}, u32[]{:S(2)}) async-start(bf16[8,48,512]{2,1,0:T(8,128)(2,1)} %bitcast.31), calls=%async_computation | async-start | bytes 786432 | tf_op jit(solution)/shard_map/all_to_all | solution.py:142
  (9 other events, 6.7 us)

commit v14 on v13

--- a/solution.py
+++ b/solution.py
@@ -227,15 +227,21 @@
 
 def combine_kernel(count, split, section_ref, position_ref, gates_ref, *refs):
     blocks = refs[:count]
-    outs, (held, total) = refs[count:-2], refs[-2:]
+    outs, (held, total, sems) = refs[count:-3], refs[-3:]
     capacity, features = blocks[0].shape
+    copies = [
+        pltpu.make_async_copy(block, held.at[pl.ds(i * capacity, capacity)], sems.at[i])
+        for i, block in enumerate(blocks)
+    ]
+    for copy in copies:
+        copy.start()
     position = position_ref[...]
     slot = lax.broadcasted_iota(jnp.int32, (position.shape[0], count * capacity), 1)
     picks = [
         jnp.where(position[:, k : k + 1] == slot, 1.0, 0.0).astype(jnp.bfloat16) for k in range(2)
     ]
-    for i, block in enumerate(blocks):
-        held[i * capacity : (i + 1) * capacity, :] = block[...]
+    for copy in copies:
+        copy.wait()
     pick = jnp.concatenate(picks, axis=0)
     rows = position.shape[0]
     both = jnp.dot(pick, held[...], preferred_element_type=jnp.float32)
@@ -264,13 +270,15 @@
     return pl.pallas_call(
         functools.partial(combine_kernel, count, split),
         out_shape=out_shape,
-        in_specs=[pl.BlockSpec(memory_space=pltpu.SMEM)] + [full] * (2 + count),
+        in_specs=[pl.BlockSpec(memory_space=pltpu.SMEM), full, full]
+        + [pl.BlockSpec(memory_space=pltpu.HBM)] * count,
         out_specs=[full] * len(out_shape),
         scratch_shapes=[
             vmem((count * capacity, features), jnp.bfloat16),
             vmem((rows, features), jnp.float32),
+            pltpu.SemaphoreType.DMA((count,)),
         ],
-        compiler_params=pltpu.CompilerParams(vmem_limit_bytes=14 * 1024 * 1024),
+        compiler_params=pltpu.CompilerParams(vmem_limit_bytes=56 * 1024 * 1024),
         cost_estimate=SHORT,
         name="combine",
     )(section, position, gates, *blocks)
@@ -573,19 +581,20 @@
     token_x = swap(tokens, "dp", 2)
     row = lax.broadcasted_iota(jnp.int32, (token_count, token_count), 0)
     column = lax.broadcasted_iota(jnp.int32, (token_count, token_count), 1)
-    named = expert_ids[:, :, None] == jnp.arange(size, dtype=jnp.int32)[None, None, :]
+    ids_own = expert_ids.T
+    ids_x, ids_y = swap(ids_own, "dp", 2), swap(ids_own, "expert", 1)
+    ids_far = swap(ids_x, "expert", 1)
+    token_far = swap(gate(token_y, ids_x, ids_y, token_x), "dp", 2)
+
+    later_ids = gate(expert_ids, token_far)
+    named = later_ids[:, :, None] == jnp.arange(size, dtype=jnp.int32)[None, None, :]
     either = (named[:, 0] | named[:, 1]).astype(jnp.bfloat16)
     earlier = jnp.dot(
         (column < row).astype(jnp.bfloat16), either, preferred_element_type=jnp.float32
     ).astype(jnp.int32)
     rank = jnp.sum(jnp.where(named, earlier[:, None, :], 0), axis=2)
-    codes_of = expert_ids ^ here
+    codes_of = later_ids ^ here
     position = ((codes_of >> 1) + 4 * (codes_of & 1)) * capacity + rank
-
-    ids_own = expert_ids.T
-    ids_x, ids_y = swap(ids_own, "dp", 2), swap(ids_own, "expert", 1)
-    ids_far = swap(ids_x, "expert", 1)
-    token_far = swap(gate(token_y, ids_x, ids_y), "dp", 2)
 
     side = lax.rem(section, 2)
     share = token_count // 2
@@ -657,7 +666,7 @@
     key_other = swap(gate(key_own, first), "expert", 1)
     mixed_near = swap(mixed_slice, "section", 1)
     slope = expert_slope(
-        gate(here.astype(jnp.int32).reshape(1), mixed_near, key_other),
+        gate(here.astype(jnp.int32).reshape(1), mixed_near),
         near_codes + core_codes,
         grads_own,
         grads_core,
@@ -676,7 +685,7 @@
     query_here = jnp.dot(normed_own, query_own, preferred_element_type=jnp.float32)
     query = (query_here + query_back.astype(jnp.float32)).astype(jnp.bfloat16)
 
-    memory = make_memory(which_section, tokens, slices, final_gain)
+    memory = make_memory(which_section, gate(tokens, key_other), slices, final_gain)
     out_other = swap(gate(out_own, memory), "expert", 1)
     memory_x = swap(memory, "dp", 2)
     memory_core = swap(memory, "dp", 1)
@@ -708,7 +717,7 @@
     dec_out = add_residual(attended, states, tgt_lengths)
 
     grads_home = exchange(gate(backward_sum.astype(jnp.bfloat16), last), group_size, capacity)
-    natural = expert_ids * capacity + rank
+    natural = later_ids * capacity + rank
     (token_grad,) = combine(
         which_section, natural, gate_weights, [grads_home], 1
     )

time: 174 us -> 183 us (1.052)
  local copies, waits for them, and re-layouts: 21 us -> 15.1 us
  waiting for transfers between devices: 56.3 us -> 61.7 us
  Pallas kernels: 32.8 us -> 37.7 us
  matrix products: 8.25 us -> 13 us
  starting transfers between devices: 42.6 us -> 40.4 us
  other arithmetic: 11.1 us -> 13.1 us
    unnamed x73 -> x60, local copies, waits for them, and re-layouts: 17.3 us -> 9.78 us
    ppermute x30, waiting for transfers between devices: 44.4 us -> 50.3 us  [swap(): return lax.ppermute(value, axis, [(i, i ^ mask) for i in range(size)])]
    pallas_call x2, Pallas kernels: 2.84 us -> 6.89 us  [combine(): pl.pallas_call(functools.partial(combine_kernel, count, split), out_shape...]
    dot_general x2, matrix products: 2.18 us -> 4.75 us  [forward(): part = jnp.dot(hidden, weight_out, preferred_element_type=jnp.float32)]
    ppermute x30, starting transfers between devices: 32.6 us -> 30 us  [swap(): return lax.ppermute(value, axis, [(i, i ^ mask) for i in range(size)])]
  transfers between devices with their start and end apart: 38 -> 38, of which waited for: 15 -> 17; matrix products, arithmetic and copies ran while one was open for 14% -> 18% of each run, Pallas kernels for 17% -> 17%
where the time goes in v14:
time: 183 us; the launch traced here: 182 us
  waiting for transfers between devices  61.7 us (34%)
  starting transfers between devices  40.4 us (22%)
  Pallas kernels  37.7 us (21%)
  local copies, waits for them, and re-layouts  15.1 us (8%)
  other arithmetic  13.1 us (7%)
  matrix products  13 us (7%)
    ppermute x30, waiting for transfers between devices, swap(): return lax.ppermute(value, axis, [(i, i ^ mask) for i in range(size)])  50.3 us
    ppermute x30, starting transfers between devices, swap(): return lax.ppermute(value, axis, [(i, i ^ mask) for i in range(size)])  30 us
    pallas_call x2, Pallas kernels, attend_sentence(): pl.pallas_call(attend_kernel, out_shape=jax.ShapeDtypeStruct(query.shape,...  10.9 us
    unnamed x60, local copies, waits for them, and re-layouts  9.78 us
    pallas_call x1, Pallas kernels, expert_slope(): pl.pallas_call(functools.partial(slope_kernel, codes), out_shape=jax.Shap...  7.35 us
    ppermute x7, starting transfers between devices, send_home(): lax.ppermute(block, ('expert', 'dp'), [(i, i ^ code) for i in range(size)])  6.92 us
    pallas_call x2, Pallas kernels, combine(): pl.pallas_call(functools.partial(combine_kernel, count, split), out_shape...  6.89 us
    ppermute x7, waiting for transfers between devices, send_home(): lax.ppermute(block, ('expert', 'dp'), [(i, i ^ code) for i in range(size)])  6.2 us
  transfers between devices with their start and end apart: 38, of which 17 were waited for; matrix products, arithmetic and copies ran while one was open for 18% of the time, Pallas kernels for 17%

profile of v14, /device:TPU:0, one launch (start us, length us, event | category | flops | bytes accessed | tf_op | source)
XLA Modules:
  0.0 182.2 jit_solution(15227261448975725150)
XLA Ops:
  0.6 3.0 %collective-permute-start.6 = (bf16[128,2048]{1,0:T(8,128)(2,1)}, bf16[128,2048]{1,0:T(8,128)(2,1)S(1)}, u32[]{:S(2)}, u32[]{:S(2)}) collective-permute-start(bf16[128,2048]{1,0:T(8,128)(2,1)} %tokens_ref), channel_id=1, source_target_pairs={{0,2},{1,3},{2,0},{3,1},{4,6},{5,7},{6,4},{7,5},{8,10},{9,11},{10,... | collective-permute-start | bytes 1572872 | tf_op jit(solution)/shard_map/ppermute | solution.py:38
  3.6 1.5 collective-permute-start
  5.8 10.1 %collective-permute-done.3 = s32[2,128]{1,0:T(2,128)S(1)} collective-permute-done((s32[2,128]{1,0:T(2,128)}, s32[2,128]{1,0:T(2,128)S(1)}, u32[]{:S(2)}, u32[]{:S(2)}) %collective-permute-start.3) | collective-permute-done | bytes 1056 | tf_op jit(solution)/shard_map/ppermute | solution.py:38
  15.8 1.5 collective-permute-done.4
  17.7 1.0 constant_dynamic-slice_fusion.2
  18.7 1.7 collective-permute-start.1
  20.8 1.2 copy-done.4
  24.3 1.5 collective-permute-done.5
  26.6 1.5 collective-permute-start.2
  28.0 1.6 collective-permute-start.9
  31.2 1.3 collective-permute-start.10
  32.5 1.0 copy-done.1
  33.6 2.2 %dispatch.2 = (bf16[192,2048]{1,0:T(8,128)(2,1)S(1)}, bf16[192,2048]{1,0:T(8,128)(2,1)}) custom-call(s32[1]{0:T(128)} %bitcast.7.section_ref, s32[8,128]{1,0:T(8,128)S(1)} %fusion.code_ref, bf16[128,2048]{1,0:T(8,128)(2,1)S(1)} %copy-done.1, bf16[128,2048]{1,0:T(8,128)(2,1)S(1)} %collective-permute-done.6.refs_1_, ...), custom_call_target="tpu_custom_call" | custom-call | flops 1 | bytes 1 | tf_op jit(solution)/shard_map/dispatch/pallas_call | solution.py:198
  35.8 3.2 %fusion.61 = f32[192,1024]{1,0:T(8,128)S(1)} fusion(bf16[192,2048]{1,0:T(8,128)(2,1)S(1)} %get-tuple-element.50, bf16[1,2048,1024]{2,1,0:T(8,128)(2,1)} %param.19), kind=kOutput, calls=%fused_computation.101 | convolution fusion | flops 805306368 | bytes 5767168 | tf_op jit(solution)/shard_map/dot_general | solution.py:620
  40.1 3.7 %convolution_convert_fusion.1 = bf16[192,2048]{1,0:T(8,128)(2,1)S(1)} fusion(f32[192,1024]{1,0:T(8,128)S(1)} %fusion.61, bf16[1,1024,2048]{2,1,0:T(8,128)(2,1)} %param.20), kind=kOutput, calls=%fused_computation.1 | convolution fusion | flops 807469056 | bytes 5767168 | tf_op jit(solution)/shard_map/dot_general | solution.py:622
  44.5 1.7 collective-permute-start.17
  46.7 1.2 collective-permute-start.15
  48.0 2.2 %fusion.59 = f32[192,1024]{1,0:T(8,128)S(1)} fusion(bf16[192,2048]{1,0:T(8,128)(2,1)} %collective-permute-done.8, bf16[1,2048,1024]{2,1,0:T(8,128)(2,1)S(1)} %copy-done.14), kind=kOutput, calls=%fused_computation.99 | convolution fusion | flops 805306368 | bytes 5767168 | tf_op jit(solution)/shard_map/dot_general | solution.py:620
  50.2 1.1 convolution_convert_fusion
  51.3 0.8 fusion.72
  52.1 0.9 collective-permute-start.11
  53.0 2.2 %fusion.1 = bf16[256,512]{1,0:T(8,128)(2,1)} fusion(bf16[256,1024]{1,0:T(8,128)(2,1)} %collective-permute-done.2, bf16[1,1024,512]{2,1,0:T(8,128)(2,1)S(1)} %copy-done), kind=kOutput, calls=%fused_computation.11 | convolution fusion | flops 268435456 | bytes 1835008 | tf_op jit(solution)/shard_map/dot_general | solution.py:606
  55.2 1.7 collective-permute-done.16.refs_2_
  56.9 1.5 collective-permute-start.18
  58.6 2.3 %collective-permute-start.12 = (bf16[48,2048]{1,0:T(8,128)(2,1)}, bf16[48,2048]{1,0:T(8,128)(2,1)}, u32[]{:S(2)}, u32[]{:S(2)}) collective-permute-start(bf16[48,2048]{1,0:T(8,128)(2,1)} %get-tuple-element.88), channel_id=1, source_target_pairs={{0,5},{1,4},{2,7},{3,6},{4,1},{5,0},{6,3},{7,2},{8,13},{9,12},{10,... | collective-permute-start | bytes 589832 | tf_op jit(solution)/shard_map/ppermute | solution.py:223
  61.0 2.1 %fusion.10 = (f32[192,1024]{1,0:T(8,128)}, f32[192,1024]{1,0:T(8,128)}) fusion(f32[192,1024]{1,0:T(8,128)S(1)} %fusion.61, f32[192,1024]{1,0:T(8,128)S(1)} %fusion.59), kind=kLoop, calls=%fused_computation.20 | loop fusion | flops 6684672 | bytes 3145728 | tf_op jit(solution)/shard_map/transpose(jvp())/add_any | solution.py:626
  63.0 1.0 constant_dynamic-update-slice_fusion.1
  64.0 1.0 constant_dynamic-update-slice_fusion.refs_3_
  66.5 4.0 %collective-permute-done.12.refs_6_ = bf16[48,2048]{1,0:T(8,128)(2,1)} collective-permute-done((bf16[48,2048]{1,0:T(8,128)(2,1)}, bf16[48,2048]{1,0:T(8,128)(2,1)}, u32[]{:S(2)}, u32[]{:S(2)}) %collective-permute-start.12) | collective-permute-done | bytes 196640 | tf_op jit(solution)/shard_map/ppermute | solution.py:223
  70.6 4.1 %combine.2 = (bf16[2,128,512]{2,1,0:T(8,128)(2,1)}, f32[128,512]{1,0:T(8,128)}, f32[128,512]{1,0:T(8,128)}) custom-call(s32[1]{0:T(128)} %bitcast.7.section_ref, s32[128,2]{1,0:T(8,128)} %get-tuple-element.99.position_ref, f32[128,2]{1,0:T(8,128)} %copy.39.gates_ref, bf16[48,2048]{1,0:T(8,128)(2,1)} %get-tuple-element.90.refs_0_, ...), custom_call_target="tpu_custom_call" | custom-call | flops 1 | bytes 1 | tf_op jit(solution)/shard_map/combine/pallas_call | solution.py:270
  74.6 1.0 collective-permute-start.21
  75.7 0.8 collective-permute-start.22
  76.5 1.0 collective-permute-start.13
  77.5 5.8 %collective-permute-done.21 = bf16[2,128,512]{2,1,0:T(8,128)(2,1)S(1)} collective-permute-done((bf16[2,128,512]{2,1,0:T(8,128)(2,1)}, bf16[2,128,512]{2,1,0:T(8,128)(2,1)S(1)}, u32[]{:S(2)}, u32[]{:S(2)}) %collective-permute-start.21) | collective-permute-done | bytes 262176 | tf_op jit(solution)/shard_map/ppermute | solution.py:38
  83.2 1.0 fusion.50
  84.2 2.7 %collective-permute-start.23 = (bf16[128,512]{1,0:T(8,128)(2,1)S(1)}, bf16[128,512]{1,0:T(8,128)(2,1)S(1)}, u32[]{:S(2)}, u32[]{:S(2)}) collective-permute-start(bf16[128,512]{1,0:T(8,128)(2,1)S(1)} %fusion.50), channel_id=1, source_target_pairs={{0,16},{8,24},{16,0},{24,8},{1,17},{9,25},{17,1},{25,9},{2,18},{10... | collective-permute-start | bytes 393224 | tf_op jit(solution)/shard_map/ppermute | solution.py:38
  86.9 1.2 collective-permute-start.20
  88.1 1.3 collective-permute-done.22.refs_4_
  89.3 1.5 dispatch.3
  90.8 0.9 copy-done.7
  91.7 1.0 collective-permute-done.23
  92.7 1.0 fusion.49.refs_0_
  94.0 4.8 %collective-permute-done.24.refs_1_ = bf16[128,512]{1,0:T(8,128)(2,1)S(1)} collective-permute-done((bf16[128,512]{1,0:T(8,128)(2,1)S(1)}, bf16[128,512]{1,0:T(8,128)(2,1)S(1)}, u32[]{:S(2)}, u32[]{:S(2)}) %collective-permute-start.24) | collective-permute-done | bytes 131104 | tf_op jit(solution)/shard_map/ppermute | solution.py:38
  98.7 1.4 collective-permute-start.27
  100.1 1.9 %collective-permute-start.25 = (bf16[2,128,512]{2,1,0:T(8,128)(2,1)S(1)}, bf16[2,128,512]{2,1,0:T(8,128)(2,1)S(1)}, u32[]{:S(2)}, u32[]{:S(2)}) collective-permute-start(bf16[2,128,512]{2,1,0:T(8,128)(2,1)S(1)} %pad_maximum_fusion), channel_id=1, source_target_pairs={{0,16},{8,24},{16,0},{24,8},{1,17},{9,25},{17,1},{25,9},{2,18},{10... | collective-permute-start | bytes 786440 | tf_op jit(solution)/shard_map/ppermute | solution.py:38
  102.1 0.9 copy-done.18
  103.0 7.4 %expert_slope.1.slope_ref = bf16[384,1024]{1,0:T(8,128)(2,1)} custom-call(s32[1]{0:T(128)} %bitcast.27.here_ref, bf16[192,2048]{1,0:T(8,128)(2,1)} %copy-done.7, bf16[192,2048]{1,0:T(8,128)(2,1)} %copy-done.18, f32[192,1024]{1,0:T(8,128)} %get-tuple-element.100.rise_own, f32[192,1024]{1,0:T(8,128)} %get-tuple-element.101.rise_core, bf16[1024,2048]{1,0:T(8,128)(2,1)} %bitcast.83), custom_call_target="tpu_custom_call" | custom-call | flops 1 | bytes 1 | tf_op jit(solution)/shard_map/expert_slope/pallas_call | solution.py:486
  110.4 5.8 %expert_backward.1 = (bf16[2,384,512]{2,1,0:T(8,128)(2,1)}, f32[384,512]{1,0:T(8,128)}, f32[384,512]{1,0:T(8,128)}) custom-call(s32[1]{0:T(128)} %bitcast.7.section_ref, bf16[384,1024]{1,0:T(8,128)(2,1)} %expert_slope.1.slope_ref, bf16[2048,1024]{1,0:T(8,128)(2,1)} %bitcast.82), custom_call_target="tpu_custom_call" | custom-call | flops 1 | bytes 1 | tf_op jit(solution)/shard_map/expert_backward/pallas_call | solution.py:528
  116.2 1.6 collective-permute-start.33
  119.2 1.5 collective-permute-start.30
  122.4 13.3 %collective-permute-done.27.refs_5_ = bf16[1024,512]{1,0:T(8,128)(2,1)} collective-permute-done((bf16[1024,512]{1,0:T(8,128)(2,1)}, bf16[1024,512]{1,0:T(8,128)(2,1)}, u32[]{:S(2)}, u32[]{:S(2)}) %collective-permute-start.27) | collective-permute-done | bytes 1048608 | tf_op jit(solution)/shard_map/ppermute | solution.py:38
  135.8 5.4 %attend_sentence.2.mine_ref = bf16[128,512]{1,0:T(8,128)(2,1)} custom-call(s32[3]{0:T(128)} %pad_add_fusion.1.place_ref, s32[2]{0:T(128)} %lengths_ref.3, bf16[128,512]{1,0:T(8,128)(2,1)} %get-tuple-element.95.query_ref, bf16[128,2048]{1,0:T(8,128)(2,1)} %copy-done.3, bf16[128,2048]{1,0:T(8,128)(2,1)} %collective-permute-done.26.refs_1_, ...), custom_call_target="tpu_custom_call" | custom-call | flops 1 | bytes 1 | tf_op jit(solution)/shard_map/attend_sentence/pallas_call | solution.py:388
  141.3 1.1 fusion.35
  144.2 5.5 %attend_sentence.3.done_ref = bf16[128,512]{1,0:T(8,128)(2,1)} custom-call(s32[3]{0:T(128)} %pad_add_fusion.3.place_ref, s32[2]{0:T(128)} %lengths_ref.3, bf16[128,512]{1,0:T(8,128)(2,1)} %get-tuple-element.94.query_ref, bf16[128,2048]{1,0:T(8,128)(2,1)} %collective-permute-done.28.refs_0_, bf16[128,2048]{1,0:T(8,128)(2,1)} %copy-done.21, ...), custom_call_target="tpu_custom_call" | custom-call | flops 1 | bytes 1 | tf_op jit(solution)/shard_map/attend_sentence/pallas_call | solution.py:388
  149.7 6.5 %collective-permute-done.30.other_ref = bf16[512,1024]{1,0:T(8,128)(2,1)} collective-permute-done((bf16[512,1024]{1,0:T(8,128)(2,1)S(1)}, bf16[512,1024]{1,0:T(8,128)(2,1)}, u32[]{:S(2)}, u32[]{:S(2)}) %collective-permute-start.30) | collective-permute-done | bytes 1048608 | tf_op jit(solution)/shard_map/ppermute | solution.py:38
  156.2 0.9 copy-done.9
  157.1 2.0 %project.1 = (bf16[256,512]{1,0:T(8,128)(2,1)S(1)}, bf16[256,512]{1,0:T(8,128)(2,1)S(1)}, f32[256,512]{1,0:T(8,128)S(1)}, f32[256,512]{1,0:T(8,128)S(1)}) custom-call(s32[3]{0:T(128)S(1)} %copy-done.12, bf16[128,512]{1,0:T(8,128)(2,1)S(1)} %copy-done.8, bf16[128,512]{1,0:T(8,128)(2,1)S(1)} %copy-done.9, bf16[512,1024]{1,0:T(8,128)(2,1)S(1)} %bitcast.79, ...), custom_call_target="tpu_custom_call" | custom-call | flops 1 | bytes 1 | tf_op jit(solution)/shard_map/project/pallas_call | solution.py:439
  159.7 3.7 %collective-permute-done.34 = bf16[384,512]{1,0:T(8,128)(2,1)S(1)} collective-permute-done((bf16[384,512]{1,0:T(8,128)(2,1)S(1)}, bf16[384,512]{1,0:T(8,128)(2,1)S(1)}, u32[]{:S(2)}, u32[]{:S(2)}) %collective-permute-start.34) | collective-permute-done | bytes 393248 | tf_op jit(solution)/shard_map/ppermute | solution.py:38
  163.4 1.3 collective-permute-start.36
  164.7 1.9 %fusion.34 = bf16[384,512]{1,0:T(8,128)(2,1)} fusion(f32[384,512]{1,0:T(8,128)S(1)} %copy-done.20, bf16[384,512]{1,0:T(8,128)(2,1)S(1)} %collective-permute-done.34, bf16[2,384,512]{2,1,0:T(8,128)(2,1)} %collective-permute-done.33), kind=kLoop, calls=%fused_computation.45 | loop fusion | flops 983040 | bytes 1966080 | tf_op jit(solution)/shard_map/convert_element_type | solution.py:719
  166.7 3.5 %all-to-all-start = ((bf16[8,48,512]{2,1,0:T(8,128)(2,1)}), bf16[8,48,512]{2,1,0:T(8,128)(2,1)S(1)}, u32[]{:S(2)}, u32[]{:S(2)}) async-start(bf16[8,48,512]{2,1,0:T(8,128)(2,1)} %bitcast.31), calls=%async_computation | async-start | bytes 786432 | tf_op jit(solution)/shard_map/all_to_all | solution.py:142
  171.4 1.8 fusion.47
  173.2 5.2 %all-to-all-done = bf16[8,48,512]{2,1,0:T(8,128)(2,1)S(1)} async-done(((bf16[8,48,512]{2,1,0:T(8,128)(2,1)}), bf16[8,48,512]{2,1,0:T(8,128)(2,1)S(1)}, u32[]{:S(2)}, u32[]{:S(2)}) %all-to-all-start) | async-done | bytes 393248 | tf_op jit(solution)/shard_map/all_to_all | solution.py:142
  179.2 2.8 %combine.3 = bf16[128,512]{1,0:T(8,128)(2,1)} custom-call(s32[1]{0:T(128)} %bitcast.7.section_ref, s32[128,2]{1,0:T(8,128)} %get-tuple-element.98.position_ref, f32[128,2]{1,0:T(8,128)} %copy.43.gates_ref, bf16[384,512]{1,0:T(8,128)(2,1)} %bitcast.87), custom_call_target="tpu_custom_call" | custom-call | flops 1 | bytes 1 | tf_op jit(solution)/shard_map/combine/pallas_call | solution.py:270
  (117 shorter events, 18.2 us)
Async XLA Ops:
  0.6 52.4 %copy-start = (bf16[1,1024,512]{2,1,0:T(8,128)(2,1)S(1)}, bf16[1,1024,512]{2,1,0:T(8,128)(2,1)}, u32[]{:S(2)}) copy-start(bf16[1,1024,512]{2,1,0:T(8,128)(2,1)} %param.26) | copy-start | bytes 3145732
  0.6 16.7 %collective-permute-start.6 = (bf16[128,2048]{1,0:T(8,128)(2,1)}, bf16[128,2048]{1,0:T(8,128)(2,1)S(1)}, u32[]{:S(2)}, u32[]{:S(2)}) collective-permute-start(bf16[128,2048]{1,0:T(8,128)(2,1)} %tokens_ref), channel_id=1, source_target_pairs={{0,2},{1,3},{2,0},{3,1},{4,6},{5,7},{6,4},{7,5},{8,10},{9,11},{10,... | collective-permute-start | bytes 1572872 | tf_op jit(solution)/shard_map/ppermute | solution.py:38
  3.6 13.7 %collective-permute-start = (bf16[128,2048]{1,0:T(8,128)(2,1)}, bf16[128,2048]{1,0:T(8,128)(2,1)S(1)}, u32[]{:S(2)}, u32[]{:S(2)}) collective-permute-start(bf16[128,2048]{1,0:T(8,128)(2,1)} %tokens_ref), channel_id=1, source_target_pairs={{0,4},{4,0},{1,5},{5,1},{2,6},{6,2},{3,7},{7,3},{8,12},{12,8},{9,1... | collective-permute-start | bytes 1572872 | tf_op jit(solution)/shard_map/ppermute | solution.py:38
  5.2 10.7 %collective-permute-start.3 = (s32[2,128]{1,0:T(2,128)}, s32[2,128]{1,0:T(2,128)S(1)}, u32[]{:S(2)}, u32[]{:S(2)}) collective-permute-start(s32[2,128]{1,0:T(2,128)} %bitcast.88), channel_id=1, source_target_pairs={{0,2},{1,3},{2,0},{3,1},{4,6},{5,7},{6,4},{7,5},{8,10},{9,11},{10,... | collective-permute-start | bytes 3080 | tf_op jit(solution)/shard_map/ppermute | solution.py:38
  5.7 11.6 %collective-permute-start.4 = (s32[2,128]{1,0:T(2,128)}, s32[2,128]{1,0:T(2,128)S(1)}, u32[]{:S(2)}, u32[]{:S(2)}) collective-permute-start(s32[2,128]{1,0:T(2,128)} %bitcast.89), channel_id=1, source_target_pairs={{0,4},{4,0},{1,5},{5,1},{2,6},{6,2},{3,7},{7,3},{8,12},{12,8},{9,1... | collective-permute-start | bytes 3080 | tf_op jit(solution)/shard_map/ppermute | solution.py:38
  17.3 12.4 %collective-permute-start.7 = (bf16[128,2048]{1,0:T(8,128)(2,1)S(1)}, bf16[128,2048]{1,0:T(8,128)(2,1)S(1)}, u32[]{:S(2)}, u32[]{:S(2)}) collective-permute-start(bf16[128,2048]{1,0:T(8,128)(2,1)S(1)} %collective-permute-done.refs_2_), channel_id=1, source_target_pairs={{0,2},{1,3},{2,0},{3,1},{4,6},{5,7},{6,4},{7,5},{8,10},{9,11},{10,... | collective-permute-start | bytes 1572872 | tf_op jit(solution)/shard_map/ppermute | solution.py:38
  18.7 12.4 %copy-start.22 = (bf16[64,2048]{1,0:T(8,128)(2,1)}, bf16[64,2048]{1,0:T(8,128)(2,1)S(1)}, u32[]{:S(2)}) copy-start(bf16[64,2048]{1,0:T(8,128)(2,1)S(1)} %constant_dynamic-slice_fusion.2) | copy-start | bytes 786436
  18.7 7.9 %collective-permute-start.1 = (bf16[64,2048]{1,0:T(8,128)(2,1)S(1)}, bf16[64,2048]{1,0:T(8,128)(2,1)}, u32[]{:S(2)}, u32[]{:S(2)}) collective-permute-start(bf16[64,2048]{1,0:T(8,128)(2,1)S(1)} %constant_dynamic-slice_fusion.2), channel_id=1, source_target_pairs={{0,4},{4,0},{1,5},{5,1},{2,6},{6,2},{3,7},{7,3},{8,12},{12,8},{9,1... | collective-permute-start | bytes 786440 | tf_op jit(solution)/shard_map/ppermute | solution.py:38
  20.4 5.3 %collective-permute-start.5 = (s32[2,128]{1,0:T(2,128)S(1)}, s32[2,128]{1,0:T(2,128)S(1)}, u32[]{:S(2)}, u32[]{:S(2)}) collective-permute-start(s32[2,128]{1,0:T(2,128)S(1)} %collective-permute-done.3), channel_id=1, source_target_pairs={{0,4},{4,0},{1,5},{5,1},{2,6},{6,2},{3,7},{7,3},{8,12},{12,8},{9,1... | collective-permute-start | bytes 3080 | tf_op jit(solution)/shard_map/ppermute | solution.py:38
  20.8 1.2 copy-start.4
  23.5 0.8 copy-start.13
  24.3 14.8 %copy-start.26 = (s32[128,2]{0,1:T(2,128)S(1)}, s32[128,2]{0,1:T(2,128)}, u32[]{:S(2)}) copy-start(s32[128,2]{0,1:T(2,128)} %param.16) | copy-start | bytes 3076
  26.6 25.5 %collective-permute-start.2 = (bf16[256,1024]{1,0:T(8,128)(2,1)}, bf16[256,1024]{1,0:T(8,128)(2,1)}, u32[]{:S(2)}, u32[]{:S(2)}) collective-permute-start(bf16[256,1024]{1,0:T(8,128)(2,1)} %copy-done.13), channel_id=1, source_target_pairs={{0,4},{4,0},{1,5},{5,1},{2,6},{6,2},{3,7},{7,3},{8,12},{12,8},{9,1... | collective-permute-start | bytes 1572872 | tf_op jit(solution)/shard_map/ppermute | solution.py:38
  28.0 12.0 %collective-permute-start.9 = (bf16[64,2048]{1,0:T(8,128)(2,1)}, bf16[64,2048]{1,0:T(8,128)(2,1)}, u32[]{:S(2)}, u32[]{:S(2)}) collective-permute-start(bf16[64,2048]{1,0:T(8,128)(2,1)} %collective-permute-done.1), channel_id=1, source_target_pairs={{0,8},{8,0},{16,24},{24,16},{1,9},{9,1},{17,25},{25,17},{2,10},{10... | collective-permute-start | bytes 786440 | tf_op jit(solution)/shard_map/ppermute | solution.py:38
  31.2 8.8 %collective-permute-start.10 = (bf16[64,2048]{1,0:T(8,128)(2,1)}, bf16[64,2048]{1,0:T(8,128)(2,1)S(1)}, u32[]{:S(2)}, u32[]{:S(2)}) collective-permute-start(bf16[64,2048]{1,0:T(8,128)(2,1)} %copy-done.22), channel_id=1, source_target_pairs={{0,2},{1,3},{2,0},{3,1},{4,6},{5,7},{6,4},{7,5},{8,10},{9,11},{10,... | collective-permute-start | bytes 786440 | tf_op jit(solution)/shard_map/ppermute | solution.py:38
  32.5 1.0 copy-start.1
  35.7 12.3 %collective-permute-start.8 = (bf16[192,2048]{1,0:T(8,128)(2,1)}, bf16[192,2048]{1,0:T(8,128)(2,1)}, u32[]{:S(2)}, u32[]{:S(2)}) collective-permute-start(bf16[192,2048]{1,0:T(8,128)(2,1)} %get-tuple-element.49), channel_id=1, source_target_pairs={{0,1},{1,0},{2,3},{3,2},{4,5},{5,4},{6,7},{7,6},{8,9},{9,8},{10,11... | collective-permute-start | bytes 2359304 | tf_op jit(solution)/shard_map/ppermute | solution.py:38
  39.4 8.6 %copy-start.14 = (bf16[1,2048,1024]{2,1,0:T(8,128)(2,1)S(1)}, bf16[1,2048,1024]{2,1,0:T(8,128)(2,1)}, u32[]{:S(2)}) copy-start(bf16[1,2048,1024]{2,1,0:T(8,128)(2,1)} %param.19) | copy-start | bytes 12582916
  43.7 6.4 %copy-start.15 = (bf16[1,1024,2048]{2,1,0:T(8,128)(2,1)S(1)}, bf16[1,1024,2048]{2,1,0:T(8,128)(2,1)}, u32[]{:S(2)}) copy-start(bf16[1,1024,2048]{2,1,0:T(8,128)(2,1)} %param.20) | copy-start | bytes 12582916
  44.5 10.7 %collective-permute-start.17 = (bf16[48,2048]{1,0:T(8,128)(2,1)S(1)}, bf16[48,2048]{1,0:T(8,128)(2,1)S(1)}, u32[]{:S(2)}, u32[]{:S(2)}) collective-permute-start(bf16[48,2048]{1,0:T(8,128)(2,1)S(1)} %get-tuple-element.91), channel_id=1, source_target_pairs={{0,6},{1,7},{2,4},{3,5},{4,2},{5,3},{6,0},{7,1},{8,14},{9,15},{10,... | collective-permute-start | bytes 589832 | tf_op jit(solution)/shard_map/ppermute | solution.py:223
  46.2 10.7 %collective-permute-start.16 = (bf16[48,2048]{1,0:T(8,128)(2,1)S(1)}, bf16[48,2048]{1,0:T(8,128)(2,1)S(1)}, u32[]{:S(2)}, u32[]{:S(2)}) collective-permute-start(bf16[48,2048]{1,0:T(8,128)(2,1)S(1)} %get-tuple-element.92), channel_id=1, source_target_pairs={{0,4},{1,5},{2,6},{3,7},{4,0},{5,1},{6,2},{7,3},{8,12},{9,13},{10,... | collective-permute-start | bytes 589832 | tf_op jit(solution)/shard_map/ppermute | solution.py:223
  46.7 10.2 %collective-permute-start.15 = (bf16[48,2048]{1,0:T(8,128)(2,1)S(1)}, bf16[48,2048]{1,0:T(8,128)(2,1)S(1)}, u32[]{:S(2)}, u32[]{:S(2)}) collective-permute-start(bf16[48,2048]{1,0:T(8,128)(2,1)S(1)} %get-tuple-element.93), channel_id=1, source_target_pairs={{0,2},{1,3},{2,0},{3,1},{4,6},{5,7},{6,4},{7,5},{8,10},{9,11},{10,... | collective-permute-start | bytes 589832 | tf_op jit(solution)/shard_map/ppermute | solution.py:223
  51.3 14.1 %copy-start.27 = (f32[128,2]{0,1:T(2,128)S(1)}, f32[128,2]{0,1:T(2,128)}, u32[]{:S(2)}) copy-start(f32[128,2]{0,1:T(2,128)} %param.17) | copy-start | bytes 3076
  52.1 37.2 %copy-start.5 = (bf16[128,2048]{1,0:T(8,128)(2,1)S(1)}, bf16[128,2048]{1,0:T(8,128)(2,1)}, u32[]{:S(2)}) copy-start(bf16[128,2048]{1,0:T(8,128)(2,1)} %refs_0_.3) | copy-start | bytes 1572868
  52.1 8.9 %collective-permute-start.14 = (bf16[48,2048]{1,0:T(8,128)(2,1)S(1)}, bf16[48,2048]{1,0:T(8,128)(2,1)}, u32[]{:S(2)}, u32[]{:S(2)}) collective-permute-start(bf16[48,2048]{1,0:T(8,128)(2,1)S(1)} %get-tuple-element.87), channel_id=1, source_target_pairs={{0,1},{1,0},{2,3},{3,2},{4,5},{5,4},{6,7},{7,6},{8,9},{9,8},{10,11... | collective-permute-start | bytes 589832 | tf_op jit(solution)/shard_map/ppermute | solution.py:223
  52.1 8.8 %collective-permute-start.11 = (bf16[48,2048]{1,0:T(8,128)(2,1)S(1)}, bf16[48,2048]{1,0:T(8,128)(2,1)}, u32[]{:S(2)}, u32[]{:S(2)}) collective-permute-start(bf16[48,2048]{1,0:T(8,128)(2,1)S(1)} %get-tuple-element.89), channel_id=1, source_target_pairs={{0,3},{1,2},{2,1},{3,0},{4,7},{5,6},{6,5},{7,4},{8,11},{9,10},{10,... | collective-permute-start | bytes 589832 | tf_op jit(solution)/shard_map/ppermute | solution.py:223
  55.2 10.1 %copy-start.23 = (bf16[48,2048]{1,0:T(8,128)(2,1)}, bf16[48,2048]{1,0:T(8,128)(2,1)S(1)}, u32[]{:S(2)}) copy-start(bf16[48,2048]{1,0:T(8,128)(2,1)S(1)} %collective-permute-done.17.refs_3_) | copy-start | bytes 589828
  56.9 8.4 %copy-start.24 = (bf16[48,2048]{1,0:T(8,128)(2,1)}, bf16[48,2048]{1,0:T(8,128)(2,1)S(1)}, u32[]{:S(2)}) copy-start(bf16[48,2048]{1,0:T(8,128)(2,1)S(1)} %collective-permute-done.16.refs_2_) | copy-start | bytes 589828
  56.9 8.4 %copy-start.25 = (bf16[48,2048]{1,0:T(8,128)(2,1)}, bf16[48,2048]{1,0:T(8,128)(2,1)S(1)}, u32[]{:S(2)}) copy-start(bf16[48,2048]{1,0:T(8,128)(2,1)S(1)} %collective-permute-done.15.refs_1_) | copy-start | bytes 589828
  56.9 8.4 %collective-permute-start.18 = (bf16[64,2048]{1,0:T(8,128)(2,1)S(1)}, bf16[64,2048]{1,0:T(8,128)(2,1)S(1)}, u32[]{:S(2)}, u32[]{:S(2)}) collective-permute-start(bf16[64,2048]{1,0:T(8,128)(2,1)S(1)} %collective-permute-done.10.refs_1_), channel_id=1, source_target_pairs={{0,8},{8,0},{16,24},{24,16},{1,9},{9,1},{17,25},{25,17},{2,10},{10... | collective-permute-start | bytes 786440 | tf_op jit(solution)/shard_map/ppermute | solution.py:38
  58.4 8.1 %collective-permute-start.19 = (bf16[48,2048]{1,0:T(8,128)(2,1)}, bf16[48,2048]{1,0:T(8,128)(2,1)}, u32[]{:S(2)}, u32[]{:S(2)}) collective-permute-start(bf16[48,2048]{1,0:T(8,128)(2,1)} %get-tuple-element.86), channel_id=1, source_target_pairs={{0,7},{1,6},{2,5},{3,4},{4,3},{5,2},{6,1},{7,0},{8,15},{9,14},{10,... | collective-permute-start | bytes 589832 | tf_op jit(solution)/shard_map/ppermute | solution.py:223
  58.6 11.9 %collective-permute-start.12 = (bf16[48,2048]{1,0:T(8,128)(2,1)}, bf16[48,2048]{1,0:T(8,128)(2,1)}, u32[]{:S(2)}, u32[]{:S(2)}) collective-permute-start(bf16[48,2048]{1,0:T(8,128)(2,1)} %get-tuple-element.88), channel_id=1, source_target_pairs={{0,5},{1,4},{2,7},{3,6},{4,1},{5,0},{6,3},{7,2},{8,13},{9,12},{10,... | collective-permute-start | bytes 589832 | tf_op jit(solution)/shard_map/ppermute | solution.py:223
  74.6 8.6 %collective-permute-start.21 = (bf16[2,128,512]{2,1,0:T(8,128)(2,1)}, bf16[2,128,512]{2,1,0:T(8,128)(2,1)S(1)}, u32[]{:S(2)}, u32[]{:S(2)}) collective-permute-start(bf16[2,128,512]{2,1,0:T(8,128)(2,1)} %get-tuple-element.65), channel_id=1, source_target_pairs={{0,8},{8,0},{16,24},{24,16},{1,9},{9,1},{17,25},{25,17},{2,10},{10... | collective-permute-start | bytes 786440 | tf_op jit(solution)/shard_map/ppermute | solution.py:38
  75.7 13.7 %collective-permute-start.22 = (bf16[128,2048]{1,0:T(8,128)(2,1)S(1)}, bf16[128,2048]{1,0:T(8,128)(2,1)S(1)}, u32[]{:S(2)}, u32[]{:S(2)}) collective-permute-start(bf16[128,2048]{1,0:T(8,128)(2,1)S(1)} %constant_dynamic-update-slice_fusion.refs_3_), channel_id=1, source_target_pairs={{0,2},{1,3},{2,0},{3,1},{4,6},{5,7},{6,4},{7,5},{8,10},{9,11},{10,... | collective-permute-start | bytes 1572872 | tf_op jit(solution)/shard_map/ppermute | solution.py:38
  76.5 15.2 %collective-permute-start.13 = (bf16[256,512]{1,0:T(8,128)(2,1)}, bf16[256,512]{1,0:T(8,128)(2,1)S(1)}, u32[]{:S(2)}, u32[]{:S(2)}) collective-permute-start(bf16[256,512]{1,0:T(8,128)(2,1)} %fusion.1), channel_id=1, source_target_pairs={{0,4},{4,0},{1,5},{5,1},{2,6},{6,2},{3,7},{7,3},{8,12},{12,8},{9,1... | collective-permute-start | bytes 786440 | tf_op jit(solution)/shard_map/ppermute | solution.py:38
  84.2 8.5 %collective-permute-start.23 = (bf16[128,512]{1,0:T(8,128)(2,1)S(1)}, bf16[128,512]{1,0:T(8,128)(2,1)S(1)}, u32[]{:S(2)}, u32[]{:S(2)}) collective-permute-start(bf16[128,512]{1,0:T(8,128)(2,1)S(1)} %fusion.50), channel_id=1, source_target_pairs={{0,16},{8,24},{16,0},{24,8},{1,17},{9,25},{17,1},{25,9},{2,18},{10... | collective-permute-start | bytes 393224 | tf_op jit(solution)/shard_map/ppermute | solution.py:38
  86.9 30.9 %collective-permute-start.20 = (bf16[1024,512]{1,0:T(8,128)(2,1)}, bf16[1024,512]{1,0:T(8,128)(2,1)S(1)}, u32[]{:S(2)}, u32[]{:S(2)}) collective-permute-start(bf16[1024,512]{1,0:T(8,128)(2,1)} %bitcast.84), channel_id=1, source_target_pairs={{0,4},{4,0},{1,5},{5,1},{2,6},{6,2},{3,7},{7,3},{8,12},{12,8},{9,1... | collective-permute-start | bytes 3145736 | tf_op jit(solution)/shard_map/ppermute | solution.py:38
  90.8 0.9 copy-start.7
  91.7 10.4 %collective-permute-start.32 = (bf16[192,2048]{1,0:T(8,128)(2,1)S(1)}, bf16[192,2048]{1,0:T(8,128)(2,1)S(1)}, u32[]{:S(2)}, u32[]{:S(2)}) collective-permute-start(bf16[192,2048]{1,0:T(8,128)(2,1)S(1)} %get-tuple-element.68), channel_id=1, source_target_pairs={{0,1},{1,0},{2,3},{3,2},{4,5},{5,4},{6,7},{7,6},{8,9},{9,8},{10,11... | collective-permute-start | bytes 2359304 | tf_op jit(solution)/shard_map/ppermute | solution.py:38
  93.7 5.0 %collective-permute-start.24 = (bf16[128,512]{1,0:T(8,128)(2,1)S(1)}, bf16[128,512]{1,0:T(8,128)(2,1)S(1)}, u32[]{:S(2)}, u32[]{:S(2)}) collective-permute-start(bf16[128,512]{1,0:T(8,128)(2,1)S(1)} %fusion.49.refs_0_), channel_id=1, source_target_pairs={{0,8},{8,0},{16,24},{24,16},{1,9},{9,1},{17,25},{25,17},{2,10},{10... | collective-permute-start | bytes 393224 | tf_op jit(solution)/shard_map/ppermute | solution.py:38
  98.7 37.1 %collective-permute-start.27 = (bf16[1024,512]{1,0:T(8,128)(2,1)}, bf16[1024,512]{1,0:T(8,128)(2,1)}, u32[]{:S(2)}, u32[]{:S(2)}) collective-permute-start(bf16[1024,512]{1,0:T(8,128)(2,1)} %bitcast.24.refs_4_), channel_id=1, source_target_pairs={{0,4},{4,0},{1,5},{5,1},{2,6},{6,2},{3,7},{7,3},{8,12},{12,8},{9,1... | collective-permute-start | bytes 3145736 | tf_op jit(solution)/shard_map/ppermute | solution.py:38
  100.1 17.6 %collective-permute-start.25 = (bf16[2,128,512]{2,1,0:T(8,128)(2,1)S(1)}, bf16[2,128,512]{2,1,0:T(8,128)(2,1)S(1)}, u32[]{:S(2)}, u32[]{:S(2)}) collective-permute-start(bf16[2,128,512]{2,1,0:T(8,128)(2,1)S(1)} %pad_maximum_fusion), channel_id=1, source_target_pairs={{0,16},{8,24},{16,0},{24,8},{1,17},{9,25},{17,1},{25,9},{2,18},{10... | collective-permute-start | bytes 786440 | tf_op jit(solution)/shard_map/ppermute | solution.py:38
  102.1 0.9 copy-start.18
  110.3 7.5 %copy-start.2 = (bf16[128,2048]{1,0:T(8,128)(2,1)S(1)}, bf16[128,2048]{1,0:T(8,128)(2,1)}, u32[]{:S(2)}) copy-start(bf16[128,2048]{1,0:T(8,128)(2,1)} %tokens_ref) | copy-start | bytes 1572868
  110.4 7.5 %copy-start.11 = (f32[2048]{0:T(1024)S(1)}, f32[2048]{0:T(1024)}, u32[]{:S(2)}) copy-start(f32[2048]{0:T(1024)} %param.21) | copy-start | bytes 24580
  110.4 8.8 %copy-start.6 = (bf16[1,512,1024]{2,1,0:T(8,128)(2,1)S(1)}, bf16[1,512,1024]{2,1,0:T(8,128)(2,1)}, u32[]{:S(2)}) copy-start(bf16[1,512,1024]{2,1,0:T(8,128)(2,1)} %param.29) | copy-start | bytes 3145732
  116.2 25.1 %collective-permute-start.33 = (bf16[2,384,512]{2,1,0:T(8,128)(2,1)}, bf16[2,384,512]{2,1,0:T(8,128)(2,1)}, u32[]{:S(2)}, u32[]{:S(2)}) collective-permute-start(bf16[2,384,512]{2,1,0:T(8,128)(2,1)} %get-tuple-element.79), channel_id=1, source_target_pairs={{0,8},{8,0},{16,24},{24,16},{1,9},{9,1},{17,25},{25,17},{2,10},{10... | collective-permute-start | bytes 2359304 | tf_op jit(solution)/shard_map/ppermute | solution.py:38
  117.8 1.4 copy-start.16
  118.3 17.5 %copy-start.3 = (bf16[128,2048]{1,0:T(8,128)(2,1)}, bf16[128,2048]{1,0:T(8,128)(2,1)S(1)}, u32[]{:S(2)}) copy-start(bf16[128,2048]{1,0:T(8,128)(2,1)S(1)} %memory.1.refs_0_) | copy-start | bytes 1572868
  118.3 4.1 %collective-permute-start.26 = (bf16[128,2048]{1,0:T(8,128)(2,1)S(1)}, bf16[128,2048]{1,0:T(8,128)(2,1)}, u32[]{:S(2)}, u32[]{:S(2)}) collective-permute-start(bf16[128,2048]{1,0:T(8,128)(2,1)S(1)} %memory.1.refs_0_), channel_id=1, source_target_pairs={{0,1},{1,0},{2,3},{3,2},{4,5},{5,4},{6,7},{7,6},{8,9},{9,8},{10,11... | collective-permute-start | bytes 1572872 | tf_op jit(solution)/shard_map/ppermute | solution.py:38
  118.4 22.8 %collective-permute-start.28 = (bf16[128,2048]{1,0:T(8,128)(2,1)S(1)}, bf16[128,2048]{1,0:T(8,128)(2,1)}, u32[]{:S(2)}, u32[]{:S(2)}) collective-permute-start(bf16[128,2048]{1,0:T(8,128)(2,1)S(1)} %memory.1.refs_0_), channel_id=1, source_target_pairs={{0,2},{1,3},{2,0},{3,1},{4,6},{5,7},{6,4},{7,5},{8,10},{9,11},{10,... | collective-permute-start | bytes 1572872 | tf_op jit(solution)/shard_map/ppermute | solution.py:38
  119.2 37.0 %collective-permute-start.30 = (bf16[512,1024]{1,0:T(8,128)(2,1)S(1)}, bf16[512,1024]{1,0:T(8,128)(2,1)}, u32[]{:S(2)}, u32[]{:S(2)}) collective-permute-start(bf16[512,1024]{1,0:T(8,128)(2,1)S(1)} %bitcast.78), channel_id=1, source_target_pairs={{0,4},{4,0},{1,5},{5,1},{2,6},{6,2},{3,7},{7,3},{8,12},{12,8},{9,1... | collective-permute-start | bytes 3145736 | tf_op jit(solution)/shard_map/ppermute | solution.py:38
  121.3 20.1 %copy-start.19 = (f32[384,512]{1,0:T(8,128)S(1)}, f32[384,512]{1,0:T(8,128)}, u32[]{:S(2)}) copy-start(f32[384,512]{1,0:T(8,128)} %get-tuple-element.78) | copy-start | bytes 2359300
  141.2 15.0 %copy-start.8 = (bf16[128,512]{1,0:T(8,128)(2,1)S(1)}, bf16[128,512]{1,0:T(8,128)(2,1)}, u32[]{:S(2)}) copy-start(bf16[128,512]{1,0:T(8,128)(2,1)} %attend_sentence.2.mine_ref) | copy-start | bytes 393220
  141.2 15.0 %copy-start.12 = (s32[3]{0:T(128)S(1)}, s32[3]{0:T(128)}, u32[]{:S(2)}) copy-start(s32[3]{0:T(128)} %pad_add_fusion.1.place_ref) | copy-start | bytes 40
  141.2 2.2 %collective-permute-start.29 = (bf16[128,2048]{1,0:T(8,128)(2,1)}, bf16[128,2048]{1,0:T(8,128)(2,1)S(1)}, u32[]{:S(2)}, u32[]{:S(2)}) collective-permute-start(bf16[128,2048]{1,0:T(8,128)(2,1)} %collective-permute-done.28.refs_0_), channel_id=1, source_target_pairs={{0,1},{1,0},{2,3},{3,2},{4,5},{5,4},{6,7},{7,6},{8,9},{9,8},{10,11... | collective-permute-start | bytes 1572872 | tf_op jit(solution)/shard_map/ppermute | solution.py:38
  142.5 20.9 %collective-permute-start.34 = (bf16[384,512]{1,0:T(8,128)(2,1)S(1)}, bf16[384,512]{1,0:T(8,128)(2,1)S(1)}, u32[]{:S(2)}, u32[]{:S(2)}) collective-permute-start(bf16[384,512]{1,0:T(8,128)(2,1)S(1)} %fusion.35), channel_id=1, source_target_pairs={{0,16},{8,24},{16,0},{24,8},{1,17},{9,25},{17,1},{25,9},{2,18},{10... | collective-permute-start | bytes 1179656 | tf_op jit(solution)/shard_map/ppermute | solution.py:38
  144.2 20.5 %copy-start.20 = (f32[384,512]{1,0:T(8,128)S(1)}, f32[384,512]{1,0:T(8,128)}, u32[]{:S(2)}) copy-start(f32[384,512]{1,0:T(8,128)} %get-tuple-element.82) | copy-start | bytes 2359300
  156.2 0.9 copy-start.9
  157.1 13.0 %copy-start.28 = (s32[2]{0:T(128)S(1)}, s32[2]{0:T(128)}, u32[]{:S(2)}) copy-start(s32[2]{0:T(128)} %param.24) | copy-start | bytes 28
  159.1 4.2 %collective-permute-start.35 = (bf16[256,512]{1,0:T(8,128)(2,1)S(1)}, bf16[256,512]{1,0:T(8,128)(2,1)S(1)}, u32[]{:S(2)}, u32[]{:S(2)}) collective-permute-start(bf16[256,512]{1,0:T(8,128)(2,1)S(1)} %get-tuple-element.81), channel_id=1, source_target_pairs={{0,1},{1,0},{2,3},{3,2},{4,5},{5,4},{6,7},{7,6},{8,9},{9,8},{10,11... | collective-permute-start | bytes 786440 | tf_op jit(solution)/shard_map/ppermute | solution.py:38
  159.2 11.8 %collective-permute-start.31 = (bf16[256,512]{1,0:T(8,128)(2,1)S(1)}, bf16[256,512]{1,0:T(8,128)(2,1)S(1)}, u32[]{:S(2)}, u32[]{:S(2)}) collective-permute-start(bf16[256,512]{1,0:T(8,128)(2,1)S(1)} %get-tuple-element.74), channel_id=1, source_target_pairs={{0,1},{1,0},{2,3},{3,2},{4,5},{5,4},{6,7},{7,6},{8,9},{9,8},{10,11... | collective-permute-start | bytes 786440 | tf_op jit(solution)/shard_map/ppermute | solution.py:38
  163.4 8.0 %collective-permute-start.36 = (bf16[256,512]{1,0:T(8,128)(2,1)S(1)}, bf16[256,512]{1,0:T(8,128)(2,1)S(1)}, u32[]{:S(2)}, u32[]{:S(2)}) collective-permute-start(bf16[256,512]{1,0:T(8,128)(2,1)S(1)} %convert_add_fusion.3), channel_id=1, source_target_pairs={{0,2},{1,3},{2,0},{3,1},{4,6},{5,7},{6,4},{7,5},{8,10},{9,11},{10,... | collective-permute-start | bytes 786440 | tf_op jit(solution)/shard_map/ppermute | solution.py:38
  166.7 11.7 %all-to-all-start = ((bf16[8,48,512]{2,1,0:T(8,128)(2,1)}), bf16[8,48,512]{2,1,0:T(8,128)(2,1)S(1)}, u32[]{:S(2)}, u32[]{:S(2)}) async-start(bf16[8,48,512]{2,1,0:T(8,128)(2,1)} %bitcast.31), calls=%async_computation | async-start | bytes 786432 | tf_op jit(solution)/shard_map/all_to_all | solution.py:142
  (3 other events, 2.2 us)

commit v15 on v13

--- a/solution.py
+++ b/solution.py
@@ -585,12 +585,12 @@
     ids_own = expert_ids.T
     ids_x, ids_y = swap(ids_own, "dp", 2), swap(ids_own, "expert", 1)
     ids_far = swap(ids_x, "expert", 1)
-    token_far = swap(gate(token_y, ids_x, ids_y), "dp", 2)
+    token_far = swap(gate(token_y, ids_x), "dp", 2)
 
     side = lax.rem(section, 2)
     share = token_count // 2
     grad_half = lax.dynamic_slice_in_dim(out_grad, side * share, share, 0)
-    half_y = swap(gate(grad_half, token_y), "expert", 1)
+    half_y = swap(gate(grad_half, token_y, token_x), "expert", 1)
     states = dec_states[0]
     normed_own, asked = normed_halves(y, states, norm_gain)
     asked_here = swap(gate(asked, half_y), "expert", 1)
@@ -657,7 +657,7 @@
     key_other = swap(gate(key_own, first), "expert", 1)
     mixed_near = swap(mixed_slice, "section", 1)
     slope = expert_slope(
-        gate(here.astype(jnp.int32).reshape(1), mixed_near, key_other),
+        gate(here.astype(jnp.int32).reshape(1), mixed_near),
         near_codes + core_codes,
         grads_own,
         grads_core,
@@ -666,7 +666,7 @@
         weight_out,
     )
     back_pair, back_first, back_second = expert_backward(
-        which_section, slope, weight_in, sections
+        gate(which_section, key_other), slope, weight_in, sections
     )
     mixed_far = swap(jnp.stack([mixed_slice, mixed_near]), "section", 2)
     slices = [mixed_slice, mixed_near, mixed_far[0], mixed_far[1]]

time: 174 us -> 176 us (1.011)
  waiting for transfers between devices: 56.3 us -> 59.5 us
    ppermute x30, waiting for transfers between devices: 44.4 us -> 46.4 us  [swap(): return lax.ppermute(value, axis, [(i, i ^ mask) for i in range(size)])]
  transfers between devices with their start and end apart: 38 -> 38, of which waited for: 15 -> 17; matrix products, arithmetic and copies ran while one was open for 14% -> 14% of each run, Pallas kernels for 17% -> 17%
where the time goes in v15:
time: 176 us; the launch traced here: 175 us
  waiting for transfers between devices  59.5 us (34%)
  starting transfers between devices  41.5 us (24%)
  Pallas kernels  32.8 us (19%)
  local copies, waits for them, and re-layouts  21 us (12%)
  other arithmetic  11.1 us (6%)
  matrix products  8.25 us (5%)
    ppermute x30, waiting for transfers between devices, swap(): return lax.ppermute(value, axis, [(i, i ^ mask) for i in range(size)])  46.4 us
    ppermute x30, starting transfers between devices, swap(): return lax.ppermute(value, axis, [(i, i ^ mask) for i in range(size)])  31.3 us
    unnamed x73, local copies, waits for them, and re-layouts  17.3 us
    pallas_call x2, Pallas kernels, attend_sentence(): pl.pallas_call(attend_kernel, out_shape=jax.ShapeDtypeStruct(query.shape,...  10.9 us
    pallas_call x1, Pallas kernels, expert_slope(): pl.pallas_call(functools.partial(slope_kernel, codes), out_shape=jax.Shap...  7.36 us
    ppermute x7, waiting for transfers between devices, send_home(): lax.ppermute(block, ('expert', 'dp'), [(i, i ^ code) for i in range(size)])  6.89 us
    ppermute x7, starting transfers between devices, send_home(): lax.ppermute(block, ('expert', 'dp'), [(i, i ^ code) for i in range(size)])  6.73 us
    all_to_all x1, waiting for transfers between devices, exchange(): lax.all_to_all(sent, ('expert', 'dp'), split_axis=0, concat_axis=0, tiled...  6.25 us
  transfers between devices with their start and end apart: 38, of which 17 were waited for; matrix products, arithmetic and copies ran while one was open for 14% of the time, Pallas kernels for 17%

profile of v15, /device:TPU:0, one launch (start us, length us, event | category | flops | bytes accessed | tf_op | source)
XLA Modules:
  0.0 175.2 jit_solution(2438994027581699464)
XLA Ops:
  0.6 3.0 %collective-permute-start.4 = (s32[2,128]{1,0:T(2,128)}, s32[2,128]{1,0:T(2,128)S(1)}, u32[]{:S(2)}, u32[]{:S(2)}) collective-permute-start(s32[2,128]{1,0:T(2,128)} %bitcast.88), channel_id=1, source_target_pairs={{0,2},{1,3},{2,0},{3,1},{4,6},{5,7},{6,4},{7,5},{8,10},{9,11},{10,... | collective-permute-start | bytes 3080 | tf_op jit(solution)/shard_map/ppermute | solution.py:38
  3.6 1.5 collective-permute-start.5
  9.0 9.7 %collective-permute-done.refs_2_ = bf16[128,2048]{1,0:T(8,128)(2,1)S(1)} collective-permute-done((bf16[128,2048]{1,0:T(8,128)(2,1)}, bf16[128,2048]{1,0:T(8,128)(2,1)S(1)}, u32[]{:S(2)}, u32[]{:S(2)}) %collective-permute-start) | collective-permute-done | bytes 524320 | tf_op jit(solution)/shard_map/ppermute | solution.py:38
  18.7 1.5 collective-permute-start.7
  20.2 1.7 constant_dynamic-slice_fusion.2
  22.4 1.5 collective-permute-start.2
  24.0 1.2 copy-done.4
  28.3 1.2 collective-permute-done.2
  29.6 1.5 collective-permute-start.3
  31.1 1.6 collective-permute-start.9
  33.2 1.0 copy-done.1
  34.2 1.3 dispatch.2
  35.6 3.2 %fusion.61 = f32[192,1024]{1,0:T(8,128)S(1)} fusion(bf16[192,2048]{1,0:T(8,128)(2,1)S(1)} %get-tuple-element.49, bf16[1,2048,1024]{2,1,0:T(8,128)(2,1)} %param.19), kind=kOutput, calls=%fused_computation.101 | convolution fusion | flops 805306368 | bytes 5767168 | tf_op jit(solution)/shard_map/dot_general | solution.py:611
  39.2 1.1 convolution_convert_fusion.1
  40.4 1.1 collective-permute-start.17
  41.5 1.5 collective-permute-start.16
  43.0 0.9 collective-permute-start.15
  44.0 1.0 fusion.59
  45.0 1.1 convolution_convert_fusion
  46.9 1.2 collective-permute-start.11
  48.1 1.2 fusion.1
  50.0 2.5 %collective-permute-done.16.refs_2_ = bf16[48,2048]{1,0:T(8,128)(2,1)S(1)} collective-permute-done((bf16[48,2048]{1,0:T(8,128)(2,1)S(1)}, bf16[48,2048]{1,0:T(8,128)(2,1)S(1)}, u32[]{:S(2)}, u32[]{:S(2)}) %collective-permute-start.16) | collective-permute-done | bytes 196640 | tf_op jit(solution)/shard_map/ppermute | solution.py:223
  55.1 1.2 collective-permute-start.12
  57.7 2.1 %fusion.10 = (f32[192,1024]{1,0:T(8,128)}, f32[192,1024]{1,0:T(8,128)}) fusion(f32[192,1024]{1,0:T(8,128)S(1)} %fusion.61, f32[192,1024]{1,0:T(8,128)S(1)} %fusion.59), kind=kLoop, calls=%fused_computation.20 | loop fusion | flops 6684672 | bytes 3145728 | tf_op jit(solution)/shard_map/transpose(jvp())/add_any | solution.py:617
  59.8 1.0 constant_dynamic-update-slice_fusion.1
  60.8 1.3 collective-permute-done.18.refs_2_
  62.8 3.8 %collective-permute-done.12.refs_6_ = bf16[48,2048]{1,0:T(8,128)(2,1)} collective-permute-done((bf16[48,2048]{1,0:T(8,128)(2,1)}, bf16[48,2048]{1,0:T(8,128)(2,1)}, u32[]{:S(2)}, u32[]{:S(2)}) %collective-permute-start.12) | collective-permute-done | bytes 196640 | tf_op jit(solution)/shard_map/ppermute | solution.py:223
  66.6 0.9 copy-done.11
  67.5 0.9 copy-done.13
  68.5 0.9 copy-done.15
  69.4 0.9 copy-done.17
  70.3 0.9 copy-done.19
  71.2 1.8 %combine.2 = (bf16[2,128,512]{2,1,0:T(8,128)(2,1)S(1)}, f32[128,512]{1,0:T(8,128)S(1)}, f32[128,512]{1,0:T(8,128)S(1)}) custom-call(s32[1]{0:T(128)} %bitcast.7.section_ref, s32[128,2]{1,0:T(8,128)S(1)} %get-tuple-element.97.position_ref, f32[128,2]{1,0:T(8,128)S(1)} %copy.39.gates_ref, bf16[48,2048]{1,0:T(8,128)(2,1)S(1)} %get-tuple-element.88.refs_0_, ...), custom_call_target="tpu_custom_call" | custom-call | flops 1 | bytes 1 | tf_op jit(solution)/shard_map/combine/pallas_call | solution.py:264
  73.1 1.7 collective-permute-start.20
  74.9 2.0 %collective-permute-start.13 = (bf16[256,512]{1,0:T(8,128)(2,1)}, bf16[256,512]{1,0:T(8,128)(2,1)S(1)}, u32[]{:S(2)}, u32[]{:S(2)}) collective-permute-start(bf16[256,512]{1,0:T(8,128)(2,1)} %fusion.1), channel_id=1, source_target_pairs={{0,4},{4,0},{1,5},{5,1},{2,6},{6,2},{3,7},{7,3},{8,12},{12,8},{9,1... | collective-permute-start | bytes 786440 | tf_op jit(solution)/shard_map/ppermute | solution.py:38
  77.0 4.5 %collective-permute-done.20 = bf16[2,128,512]{2,1,0:T(8,128)(2,1)S(1)} collective-permute-done((bf16[2,128,512]{2,1,0:T(8,128)(2,1)S(1)}, bf16[2,128,512]{2,1,0:T(8,128)(2,1)S(1)}, u32[]{:S(2)}, u32[]{:S(2)}) %collective-permute-start.20) | collective-permute-done | bytes 262176 | tf_op jit(solution)/shard_map/ppermute | solution.py:38
  81.5 2.7 %collective-permute-start.22 = (bf16[128,512]{1,0:T(8,128)(2,1)S(1)}, bf16[128,512]{1,0:T(8,128)(2,1)S(1)}, u32[]{:S(2)}, u32[]{:S(2)}) collective-permute-start(bf16[128,512]{1,0:T(8,128)(2,1)S(1)} %fusion.50), channel_id=1, source_target_pairs={{0,16},{8,24},{16,0},{24,8},{1,17},{9,25},{17,1},{25,9},{2,18},{10... | collective-permute-start | bytes 393224 | tf_op jit(solution)/shard_map/ppermute | solution.py:38
  84.2 4.3 %collective-permute-done.21.refs_4_ = bf16[128,2048]{1,0:T(8,128)(2,1)S(1)} collective-permute-done((bf16[128,2048]{1,0:T(8,128)(2,1)S(1)}, bf16[128,2048]{1,0:T(8,128)(2,1)S(1)}, u32[]{:S(2)}, u32[]{:S(2)}) %collective-permute-start.21) | collective-permute-done | bytes 524320 | tf_op jit(solution)/shard_map/ppermute | solution.py:38
  88.5 1.5 dispatch.3
  89.9 0.9 copy-done.7
  91.4 5.5 %collective-permute-done.23.refs_1_ = bf16[128,512]{1,0:T(8,128)(2,1)S(1)} collective-permute-done((bf16[128,512]{1,0:T(8,128)(2,1)S(1)}, bf16[128,512]{1,0:T(8,128)(2,1)S(1)}, u32[]{:S(2)}, u32[]{:S(2)}) %collective-permute-start.23) | collective-permute-done | bytes 131104 | tf_op jit(solution)/shard_map/ppermute | solution.py:38
  97.5 2.7 %collective-permute-start.24 = (bf16[2,128,512]{2,1,0:T(8,128)(2,1)S(1)}, bf16[2,128,512]{2,1,0:T(8,128)(2,1)S(1)}, u32[]{:S(2)}, u32[]{:S(2)}) collective-permute-start(bf16[2,128,512]{2,1,0:T(8,128)(2,1)S(1)} %pad_maximum_fusion), channel_id=1, source_target_pairs={{0,16},{8,24},{16,0},{24,8},{1,17},{9,25},{17,1},{25,9},{2,18},{10... | collective-permute-start | bytes 786440 | tf_op jit(solution)/shard_map/ppermute | solution.py:38
  100.2 6.7 %collective-permute-done.26.refs_3_ = bf16[1024,512]{1,0:T(8,128)(2,1)S(1)} collective-permute-done((bf16[1024,512]{1,0:T(8,128)(2,1)}, bf16[1024,512]{1,0:T(8,128)(2,1)S(1)}, u32[]{:S(2)}, u32[]{:S(2)}) %collective-permute-start.26) | collective-permute-done | bytes 1048608 | tf_op jit(solution)/shard_map/ppermute | solution.py:38
  106.8 0.9 copy-done.27
  107.7 7.4 %expert_slope.1.slope_ref = bf16[384,1024]{1,0:T(8,128)(2,1)} custom-call(s32[1]{0:T(128)} %bitcast.27.here_ref, bf16[192,2048]{1,0:T(8,128)(2,1)} %copy-done.7, bf16[192,2048]{1,0:T(8,128)(2,1)} %copy-done.27, f32[192,1024]{1,0:T(8,128)} %get-tuple-element.98.rise_own, f32[192,1024]{1,0:T(8,128)} %get-tuple-element.99.rise_core, bf16[1024,2048]{1,0:T(8,128)(2,1)} %bitcast.84), custom_call_target="tpu_custom_call" | custom-call | flops 1 | bytes 1 | tf_op jit(solution)/shard_map/expert_slope/pallas_call | solution.py:478
  115.2 5.8 %expert_backward.1 = (bf16[2,384,512]{2,1,0:T(8,128)(2,1)}, f32[384,512]{1,0:T(8,128)}, f32[384,512]{1,0:T(8,128)}) custom-call(s32[1]{0:T(128)} %bitcast.7.section_ref, bf16[384,1024]{1,0:T(8,128)(2,1)} %expert_slope.1.slope_ref, bf16[2048,1024]{1,0:T(8,128)(2,1)} %bitcast.83), custom_call_target="tpu_custom_call" | custom-call | flops 1 | bytes 1 | tf_op jit(solution)/shard_map/expert_backward/pallas_call | solution.py:520
  122.3 1.8 %collective-permute-start.28 = (bf16[128,2048]{1,0:T(8,128)(2,1)S(1)}, bf16[128,2048]{1,0:T(8,128)(2,1)}, u32[]{:S(2)}, u32[]{:S(2)}) collective-permute-start(bf16[128,2048]{1,0:T(8,128)(2,1)S(1)} %memory.1.refs_0_), channel_id=1, source_target_pairs={{0,2},{1,3},{2,0},{3,1},{4,6},{5,7},{6,4},{7,5},{8,10},{9,11},{10,... | collective-permute-start | bytes 1572872 | tf_op jit(solution)/shard_map/ppermute | solution.py:38
  126.5 2.9 %collective-permute-done.27.refs_5_ = bf16[1024,512]{1,0:T(8,128)(2,1)} collective-permute-done((bf16[1024,512]{1,0:T(8,128)(2,1)}, bf16[1024,512]{1,0:T(8,128)(2,1)}, u32[]{:S(2)}, u32[]{:S(2)}) %collective-permute-start.27) | collective-permute-done | bytes 1048608 | tf_op jit(solution)/shard_map/ppermute | solution.py:38
  129.4 5.4 %attend_sentence.2.mine_ref = bf16[128,512]{1,0:T(8,128)(2,1)} custom-call(s32[3]{0:T(128)} %pad_add_fusion.1.place_ref, s32[2]{0:T(128)} %lengths_ref.3, bf16[128,512]{1,0:T(8,128)(2,1)} %get-tuple-element.93.query_ref, bf16[128,2048]{1,0:T(8,128)(2,1)} %copy-done.3, bf16[128,2048]{1,0:T(8,128)(2,1)} %collective-permute-done.25.refs_1_, ...), custom_call_target="tpu_custom_call" | custom-call | flops 1 | bytes 1 | tf_op jit(solution)/shard_map/attend_sentence/pallas_call | solution.py:380
  134.9 1.8 %collective-permute-done.28.refs_0_ = bf16[128,2048]{1,0:T(8,128)(2,1)} collective-permute-done((bf16[128,2048]{1,0:T(8,128)(2,1)S(1)}, bf16[128,2048]{1,0:T(8,128)(2,1)}, u32[]{:S(2)}, u32[]{:S(2)}) %collective-permute-start.28) | collective-permute-done | bytes 524320 | tf_op jit(solution)/shard_map/ppermute | solution.py:38
  136.7 1.8 %collective-permute-done.33 = bf16[2,384,512]{2,1,0:T(8,128)(2,1)} collective-permute-done((bf16[2,384,512]{2,1,0:T(8,128)(2,1)}, bf16[2,384,512]{2,1,0:T(8,128)(2,1)}, u32[]{:S(2)}, u32[]{:S(2)}) %collective-permute-start.33) | collective-permute-done | bytes 786464 | tf_op jit(solution)/shard_map/ppermute | solution.py:38
  138.5 1.1 fusion.35
  139.6 2.7 %collective-permute-start.34 = (bf16[384,512]{1,0:T(8,128)(2,1)S(1)}, bf16[384,512]{1,0:T(8,128)(2,1)S(1)}, u32[]{:S(2)}, u32[]{:S(2)}) collective-permute-start(bf16[384,512]{1,0:T(8,128)(2,1)S(1)} %fusion.35), channel_id=1, source_target_pairs={{0,16},{8,24},{16,0},{24,8},{1,17},{9,25},{17,1},{25,9},{2,18},{10... | collective-permute-start | bytes 1179656 | tf_op jit(solution)/shard_map/ppermute | solution.py:38
  143.7 5.5 %attend_sentence.3.done_ref = bf16[128,512]{1,0:T(8,128)(2,1)} custom-call(s32[3]{0:T(128)} %pad_add_fusion.3.place_ref, s32[2]{0:T(128)} %lengths_ref.3, bf16[128,512]{1,0:T(8,128)(2,1)} %get-tuple-element.92.query_ref, bf16[128,2048]{1,0:T(8,128)(2,1)} %collective-permute-done.28.refs_0_, bf16[128,2048]{1,0:T(8,128)(2,1)} %copy-done.30, ...), custom_call_target="tpu_custom_call" | custom-call | flops 1 | bytes 1 | tf_op jit(solution)/shard_map/attend_sentence/pallas_call | solution.py:380
  149.2 1.5 collective-permute-done.30.other_ref
  150.7 0.9 copy-done.9
  151.6 2.0 %project.1 = (bf16[256,512]{1,0:T(8,128)(2,1)S(1)}, bf16[256,512]{1,0:T(8,128)(2,1)S(1)}, f32[256,512]{1,0:T(8,128)S(1)}, f32[256,512]{1,0:T(8,128)S(1)}) custom-call(s32[3]{0:T(128)S(1)} %copy-done.22, bf16[128,512]{1,0:T(8,128)(2,1)S(1)} %copy-done.8, bf16[128,512]{1,0:T(8,128)(2,1)S(1)} %copy-done.9, bf16[512,1024]{1,0:T(8,128)(2,1)S(1)} %bitcast.80, ...), custom_call_target="tpu_custom_call" | custom-call | flops 1 | bytes 1 | tf_op jit(solution)/shard_map/project/pallas_call | solution.py:431
  154.1 4.6 %collective-permute-done.34 = bf16[384,512]{1,0:T(8,128)(2,1)S(1)} collective-permute-done((bf16[384,512]{1,0:T(8,128)(2,1)S(1)}, bf16[384,512]{1,0:T(8,128)(2,1)S(1)}, u32[]{:S(2)}, u32[]{:S(2)}) %collective-permute-start.34) | collective-permute-done | bytes 393248 | tf_op jit(solution)/shard_map/ppermute | solution.py:38
  158.8 1.8 %collective-permute-start.36 = (bf16[256,512]{1,0:T(8,128)(2,1)S(1)}, bf16[256,512]{1,0:T(8,128)(2,1)S(1)}, u32[]{:S(2)}, u32[]{:S(2)}) collective-permute-start(bf16[256,512]{1,0:T(8,128)(2,1)S(1)} %convert_add_fusion.3), channel_id=1, source_target_pairs={{0,2},{1,3},{2,0},{3,1},{4,6},{5,7},{6,4},{7,5},{8,10},{9,11},{10,... | collective-permute-start | bytes 786440 | tf_op jit(solution)/shard_map/ppermute | solution.py:38
  160.6 1.9 %fusion.34 = bf16[384,512]{1,0:T(8,128)(2,1)} fusion(f32[384,512]{1,0:T(8,128)S(1)} %copy-done.29, bf16[384,512]{1,0:T(8,128)(2,1)S(1)} %collective-permute-done.34, bf16[2,384,512]{2,1,0:T(8,128)(2,1)} %collective-permute-done.33), kind=kLoop, calls=%fused_computation.45 | loop fusion | flops 983040 | bytes 1966080 | tf_op jit(solution)/shard_map/convert_element_type | solution.py:710
  162.5 3.5 %all-to-all-start = ((bf16[8,48,512]{2,1,0:T(8,128)(2,1)}), bf16[8,48,512]{2,1,0:T(8,128)(2,1)S(1)}, u32[]{:S(2)}, u32[]{:S(2)}) async-start(bf16[8,48,512]{2,1,0:T(8,128)(2,1)} %bitcast.31), calls=%async_computation | async-start | bytes 786432 | tf_op jit(solution)/shard_map/all_to_all | solution.py:142
  166.2 1.8 %fusion.47 = bf16[1,256,512]{2,1,0:T(8,128)(2,1)} fusion(bf16[256,512]{1,0:T(8,128)(2,1)S(1)} %collective-permute-done.36, f32[256,512]{1,0:T(8,128)S(1)} %get-tuple-element.70, bf16[256,512]{1,0:T(8,128)(2,1)S(1)} %collective-permute-done.31, bf16[1,256,2048]{2,1,0:T(8,128)(2,1)} %param.22, s32[]{:T(128)S(6)} %select_n.35, ...), kind=kLoop, calls=%fused_computation.62 | loop fusion | flops 1048576 | bytes 1573124 | tf_op jit(solution)/shard_map/broadcast_in_dim | solution.py:715
  168.0 6.2 %all-to-all-done = bf16[8,48,512]{2,1,0:T(8,128)(2,1)S(1)} async-done(((bf16[8,48,512]{2,1,0:T(8,128)(2,1)}), bf16[8,48,512]{2,1,0:T(8,128)(2,1)S(1)}, u32[]{:S(2)}, u32[]{:S(2)}) %all-to-all-start) | async-done | bytes 393248 | tf_op jit(solution)/shard_map/all_to_all | solution.py:142
  174.2 1.0 combine.3
  (129 shorter events, 22.2 us)
Async XLA Ops:
  0.6 47.5 %copy-start = (bf16[1,1024,512]{2,1,0:T(8,128)(2,1)S(1)}, bf16[1,1024,512]{2,1,0:T(8,128)(2,1)}, u32[]{:S(2)}) copy-start(bf16[1,1024,512]{2,1,0:T(8,128)(2,1)} %param.26) | copy-start | bytes 3145732
  0.6 8.4 %collective-permute-start.4 = (s32[2,128]{1,0:T(2,128)}, s32[2,128]{1,0:T(2,128)S(1)}, u32[]{:S(2)}, u32[]{:S(2)}) collective-permute-start(s32[2,128]{1,0:T(2,128)} %bitcast.88), channel_id=1, source_target_pairs={{0,2},{1,3},{2,0},{3,1},{4,6},{5,7},{6,4},{7,5},{8,10},{9,11},{10,... | collective-permute-start | bytes 3080 | tf_op jit(solution)/shard_map/ppermute | solution.py:38
  3.6 23.8 %collective-permute-start.5 = (s32[2,128]{1,0:T(2,128)}, s32[2,128]{1,0:T(2,128)S(1)}, u32[]{:S(2)}, u32[]{:S(2)}) collective-permute-start(s32[2,128]{1,0:T(2,128)} %bitcast.89), channel_id=1, source_target_pairs={{0,4},{4,0},{1,5},{5,1},{2,6},{6,2},{3,7},{7,3},{8,12},{12,8},{9,1... | collective-permute-start | bytes 3080 | tf_op jit(solution)/shard_map/ppermute | solution.py:38
  5.2 17.2 %collective-permute-start.1 = (bf16[128,2048]{1,0:T(8,128)(2,1)}, bf16[128,2048]{1,0:T(8,128)(2,1)S(1)}, u32[]{:S(2)}, u32[]{:S(2)}) collective-permute-start(bf16[128,2048]{1,0:T(8,128)(2,1)} %tokens_ref.1), channel_id=1, source_target_pairs={{0,2},{1,3},{2,0},{3,1},{4,6},{5,7},{6,4},{7,5},{8,10},{9,11},{10,... | collective-permute-start | bytes 1572872 | tf_op jit(solution)/shard_map/ppermute | solution.py:38
  5.7 13.0 %collective-permute-start = (bf16[128,2048]{1,0:T(8,128)(2,1)}, bf16[128,2048]{1,0:T(8,128)(2,1)S(1)}, u32[]{:S(2)}, u32[]{:S(2)}) collective-permute-start(bf16[128,2048]{1,0:T(8,128)(2,1)} %tokens_ref.1), channel_id=1, source_target_pairs={{0,4},{4,0},{1,5},{5,1},{2,6},{6,2},{3,7},{7,3},{8,12},{12,8},{9,1... | collective-permute-start | bytes 1572872 | tf_op jit(solution)/shard_map/ppermute | solution.py:38
  18.7 13.9 %collective-permute-start.7 = (bf16[128,2048]{1,0:T(8,128)(2,1)S(1)}, bf16[128,2048]{1,0:T(8,128)(2,1)S(1)}, u32[]{:S(2)}, u32[]{:S(2)}) collective-permute-start(bf16[128,2048]{1,0:T(8,128)(2,1)S(1)} %collective-permute-done.refs_2_), channel_id=1, source_target_pairs={{0,2},{1,3},{2,0},{3,1},{4,6},{5,7},{6,4},{7,5},{8,10},{9,11},{10,... | collective-permute-start | bytes 1572872 | tf_op jit(solution)/shard_map/ppermute | solution.py:38
  21.9 5.6 %collective-permute-start.6 = (s32[2,128]{1,0:T(2,128)S(1)}, s32[2,128]{1,0:T(2,128)S(1)}, u32[]{:S(2)}, u32[]{:S(2)}) collective-permute-start(s32[2,128]{1,0:T(2,128)S(1)} %collective-permute-done.4), channel_id=1, source_target_pairs={{0,4},{4,0},{1,5},{5,1},{2,6},{6,2},{3,7},{7,3},{8,12},{12,8},{9,1... | collective-permute-start | bytes 3080 | tf_op jit(solution)/shard_map/ppermute | solution.py:38
  22.4 7.2 %collective-permute-start.2 = (bf16[64,2048]{1,0:T(8,128)(2,1)}, bf16[64,2048]{1,0:T(8,128)(2,1)}, u32[]{:S(2)}, u32[]{:S(2)}) collective-permute-start(bf16[64,2048]{1,0:T(8,128)(2,1)} %constant_dynamic-slice_fusion.2), channel_id=1, source_target_pairs={{0,4},{4,0},{1,5},{5,1},{2,6},{6,2},{3,7},{7,3},{8,12},{12,8},{9,1... | collective-permute-start | bytes 786440 | tf_op jit(solution)/shard_map/ppermute | solution.py:38
  24.0 1.2 copy-start.4
  29.6 17.4 %collective-permute-start.3 = (bf16[256,1024]{1,0:T(8,128)(2,1)}, bf16[256,1024]{1,0:T(8,128)(2,1)S(1)}, u32[]{:S(2)}, u32[]{:S(2)}) collective-permute-start(bf16[256,1024]{1,0:T(8,128)(2,1)} %copy-done.23), channel_id=1, source_target_pairs={{0,4},{4,0},{1,5},{5,1},{2,6},{6,2},{3,7},{7,3},{8,12},{12,8},{9,1... | collective-permute-start | bytes 1572872 | tf_op jit(solution)/shard_map/ppermute | solution.py:38
  31.1 7.7 %collective-permute-start.9 = (bf16[64,2048]{1,0:T(8,128)(2,1)}, bf16[64,2048]{1,0:T(8,128)(2,1)S(1)}, u32[]{:S(2)}, u32[]{:S(2)}) collective-permute-start(bf16[64,2048]{1,0:T(8,128)(2,1)} %collective-permute-done.2), channel_id=1, source_target_pairs={{0,8},{8,0},{16,24},{24,16},{1,9},{9,1},{17,25},{25,17},{2,10},{10... | collective-permute-start | bytes 786440 | tf_op jit(solution)/shard_map/ppermute | solution.py:38
  32.7 6.6 %collective-permute-start.10 = (bf16[64,2048]{1,0:T(8,128)(2,1)}, bf16[64,2048]{1,0:T(8,128)(2,1)S(1)}, u32[]{:S(2)}, u32[]{:S(2)}) collective-permute-start(bf16[64,2048]{1,0:T(8,128)(2,1)} %constant_dynamic-slice_fusion.2), channel_id=1, source_target_pairs={{0,2},{1,3},{2,0},{3,1},{4,6},{5,7},{6,4},{7,5},{8,10},{9,11},{10,... | collective-permute-start | bytes 786440 | tf_op jit(solution)/shard_map/ppermute | solution.py:38
  33.2 1.0 copy-start.1
  34.2 5.0 %copy-start.25 = (bf16[1,1024,2048]{2,1,0:T(8,128)(2,1)S(1)}, bf16[1,1024,2048]{2,1,0:T(8,128)(2,1)}, u32[]{:S(2)}) copy-start(bf16[1,1024,2048]{2,1,0:T(8,128)(2,1)} %param.20) | copy-start | bytes 12582916
  35.5 8.5 %collective-permute-start.8 = (bf16[192,2048]{1,0:T(8,128)(2,1)S(1)}, bf16[192,2048]{1,0:T(8,128)(2,1)S(1)}, u32[]{:S(2)}, u32[]{:S(2)}) collective-permute-start(bf16[192,2048]{1,0:T(8,128)(2,1)S(1)} %get-tuple-element.48), channel_id=1, source_target_pairs={{0,1},{1,0},{2,3},{3,2},{4,5},{5,4},{6,7},{7,6},{8,9},{9,8},{10,11... | collective-permute-start | bytes 2359304 | tf_op jit(solution)/shard_map/ppermute | solution.py:38
  38.8 5.2 %copy-start.24 = (bf16[1,2048,1024]{2,1,0:T(8,128)(2,1)S(1)}, bf16[1,2048,1024]{2,1,0:T(8,128)(2,1)}, u32[]{:S(2)}) copy-start(bf16[1,2048,1024]{2,1,0:T(8,128)(2,1)} %param.19) | copy-start | bytes 12582916
  40.4 8.9 %collective-permute-start.17 = (bf16[48,2048]{1,0:T(8,128)(2,1)S(1)}, bf16[48,2048]{1,0:T(8,128)(2,1)S(1)}, u32[]{:S(2)}, u32[]{:S(2)}) collective-permute-start(bf16[48,2048]{1,0:T(8,128)(2,1)S(1)} %get-tuple-element.89), channel_id=1, source_target_pairs={{0,6},{1,7},{2,4},{3,5},{4,2},{5,3},{6,0},{7,1},{8,14},{9,15},{10,... | collective-permute-start | bytes 589832 | tf_op jit(solution)/shard_map/ppermute | solution.py:223
  41.5 11.0 %collective-permute-start.16 = (bf16[48,2048]{1,0:T(8,128)(2,1)S(1)}, bf16[48,2048]{1,0:T(8,128)(2,1)S(1)}, u32[]{:S(2)}, u32[]{:S(2)}) collective-permute-start(bf16[48,2048]{1,0:T(8,128)(2,1)S(1)} %get-tuple-element.90), channel_id=1, source_target_pairs={{0,4},{1,5},{2,6},{3,7},{4,0},{5,1},{6,2},{7,3},{8,12},{9,13},{10,... | collective-permute-start | bytes 589832 | tf_op jit(solution)/shard_map/ppermute | solution.py:223
  43.0 10.2 %collective-permute-start.15 = (bf16[48,2048]{1,0:T(8,128)(2,1)S(1)}, bf16[48,2048]{1,0:T(8,128)(2,1)S(1)}, u32[]{:S(2)}, u32[]{:S(2)}) collective-permute-start(bf16[48,2048]{1,0:T(8,128)(2,1)S(1)} %get-tuple-element.91), channel_id=1, source_target_pairs={{0,2},{1,3},{2,0},{3,1},{4,6},{5,7},{6,4},{7,5},{8,10},{9,11},{10,... | collective-permute-start | bytes 589832 | tf_op jit(solution)/shard_map/ppermute | solution.py:223
  46.1 16.0 %copy-start.33 = (f32[128,2]{0,1:T(2,128)S(1)}, f32[128,2]{0,1:T(2,128)}, u32[]{:S(2)}) copy-start(f32[128,2]{0,1:T(2,128)} %param.17) | copy-start | bytes 3076
  46.9 41.5 %copy-start.5 = (bf16[128,2048]{1,0:T(8,128)(2,1)S(1)}, bf16[128,2048]{1,0:T(8,128)(2,1)}, u32[]{:S(2)}) copy-start(bf16[128,2048]{1,0:T(8,128)(2,1)} %refs_0_.3) | copy-start | bytes 1572868
  46.9 9.4 %collective-permute-start.14 = (bf16[48,2048]{1,0:T(8,128)(2,1)S(1)}, bf16[48,2048]{1,0:T(8,128)(2,1)S(1)}, u32[]{:S(2)}, u32[]{:S(2)}) collective-permute-start(bf16[48,2048]{1,0:T(8,128)(2,1)S(1)} %get-tuple-element.85), channel_id=1, source_target_pairs={{0,1},{1,0},{2,3},{3,2},{4,5},{5,4},{6,7},{7,6},{8,9},{9,8},{10,11... | collective-permute-start | bytes 589832 | tf_op jit(solution)/shard_map/ppermute | solution.py:223
  46.9 10.1 %collective-permute-start.11 = (bf16[48,2048]{1,0:T(8,128)(2,1)S(1)}, bf16[48,2048]{1,0:T(8,128)(2,1)S(1)}, u32[]{:S(2)}, u32[]{:S(2)}) collective-permute-start(bf16[48,2048]{1,0:T(8,128)(2,1)S(1)} %get-tuple-element.87), channel_id=1, source_target_pairs={{0,3},{1,2},{2,1},{3,0},{4,7},{5,6},{6,5},{7,4},{8,11},{9,10},{10,... | collective-permute-start | bytes 589832 | tf_op jit(solution)/shard_map/ppermute | solution.py:223
  53.9 8.3 %collective-permute-start.18 = (bf16[64,2048]{1,0:T(8,128)(2,1)S(1)}, bf16[64,2048]{1,0:T(8,128)(2,1)S(1)}, u32[]{:S(2)}, u32[]{:S(2)}) collective-permute-start(bf16[64,2048]{1,0:T(8,128)(2,1)S(1)} %collective-permute-done.10.refs_1_), channel_id=1, source_target_pairs={{0,8},{8,0},{16,24},{24,16},{1,9},{9,1},{17,25},{25,17},{2,10},{10... | collective-permute-start | bytes 786440 | tf_op jit(solution)/shard_map/ppermute | solution.py:38
  54.4 8.5 %collective-permute-start.19 = (bf16[48,2048]{1,0:T(8,128)(2,1)}, bf16[48,2048]{1,0:T(8,128)(2,1)}, u32[]{:S(2)}, u32[]{:S(2)}) collective-permute-start(bf16[48,2048]{1,0:T(8,128)(2,1)} %get-tuple-element.84), channel_id=1, source_target_pairs={{0,7},{1,6},{2,5},{3,4},{4,3},{5,2},{6,1},{7,0},{8,15},{9,14},{10,... | collective-permute-start | bytes 589832 | tf_op jit(solution)/shard_map/ppermute | solution.py:223
  55.1 11.5 %collective-permute-start.12 = (bf16[48,2048]{1,0:T(8,128)(2,1)}, bf16[48,2048]{1,0:T(8,128)(2,1)}, u32[]{:S(2)}, u32[]{:S(2)}) collective-permute-start(bf16[48,2048]{1,0:T(8,128)(2,1)} %get-tuple-element.86), channel_id=1, source_target_pairs={{0,5},{1,4},{2,7},{3,6},{4,1},{5,0},{6,3},{7,2},{8,13},{9,12},{10,... | collective-permute-start | bytes 589832 | tf_op jit(solution)/shard_map/ppermute | solution.py:223
  66.6 0.9 copy-start.11
  67.5 0.9 copy-start.13
  68.5 0.9 copy-start.15
  69.4 0.9 copy-start.17
  70.3 0.9 copy-start.19
  73.1 8.4 %collective-permute-start.20 = (bf16[2,128,512]{2,1,0:T(8,128)(2,1)S(1)}, bf16[2,128,512]{2,1,0:T(8,128)(2,1)S(1)}, u32[]{:S(2)}, u32[]{:S(2)}) collective-permute-start(bf16[2,128,512]{2,1,0:T(8,128)(2,1)S(1)} %get-tuple-element.61), channel_id=1, source_target_pairs={{0,8},{8,0},{16,24},{24,16},{1,9},{9,1},{17,25},{25,17},{2,10},{10... | collective-permute-start | bytes 786440 | tf_op jit(solution)/shard_map/ppermute | solution.py:38
  74.8 13.7 %collective-permute-start.21 = (bf16[128,2048]{1,0:T(8,128)(2,1)S(1)}, bf16[128,2048]{1,0:T(8,128)(2,1)S(1)}, u32[]{:S(2)}, u32[]{:S(2)}) collective-permute-start(bf16[128,2048]{1,0:T(8,128)(2,1)S(1)} %constant_dynamic-update-slice_fusion.refs_3_), channel_id=1, source_target_pairs={{0,2},{1,3},{2,0},{3,1},{4,6},{5,7},{6,4},{7,5},{8,10},{9,11},{10,... | collective-permute-start | bytes 1572872 | tf_op jit(solution)/shard_map/ppermute | solution.py:38
  74.9 15.9 %collective-permute-start.13 = (bf16[256,512]{1,0:T(8,128)(2,1)}, bf16[256,512]{1,0:T(8,128)(2,1)S(1)}, u32[]{:S(2)}, u32[]{:S(2)}) collective-permute-start(bf16[256,512]{1,0:T(8,128)(2,1)} %fusion.1), channel_id=1, source_target_pairs={{0,4},{4,0},{1,5},{5,1},{2,6},{6,2},{3,7},{7,3},{8,12},{12,8},{9,1... | collective-permute-start | bytes 786440 | tf_op jit(solution)/shard_map/ppermute | solution.py:38
  76.9 29.9 %collective-permute-start.26 = (bf16[1024,512]{1,0:T(8,128)(2,1)}, bf16[1024,512]{1,0:T(8,128)(2,1)S(1)}, u32[]{:S(2)}, u32[]{:S(2)}) collective-permute-start(bf16[1024,512]{1,0:T(8,128)(2,1)} %bitcast.85), channel_id=1, source_target_pairs={{0,4},{4,0},{1,5},{5,1},{2,6},{6,2},{3,7},{7,3},{8,12},{12,8},{9,1... | collective-permute-start | bytes 3145736 | tf_op jit(solution)/shard_map/ppermute | solution.py:38
  81.5 9.3 %collective-permute-start.22 = (bf16[128,512]{1,0:T(8,128)(2,1)S(1)}, bf16[128,512]{1,0:T(8,128)(2,1)S(1)}, u32[]{:S(2)}, u32[]{:S(2)}) collective-permute-start(bf16[128,512]{1,0:T(8,128)(2,1)S(1)} %fusion.50), channel_id=1, source_target_pairs={{0,16},{8,24},{16,0},{24,8},{1,17},{9,25},{17,1},{25,9},{2,18},{10... | collective-permute-start | bytes 393224 | tf_op jit(solution)/shard_map/ppermute | solution.py:38
  90.8 16.0 %collective-permute-start.32 = (bf16[192,2048]{1,0:T(8,128)(2,1)S(1)}, bf16[192,2048]{1,0:T(8,128)(2,1)S(1)}, u32[]{:S(2)}, u32[]{:S(2)}) collective-permute-start(bf16[192,2048]{1,0:T(8,128)(2,1)S(1)} %get-tuple-element.64), channel_id=1, source_target_pairs={{0,1},{1,0},{2,3},{3,2},{4,5},{5,4},{6,7},{7,6},{8,9},{9,8},{10,11... | collective-permute-start | bytes 2359304 | tf_op jit(solution)/shard_map/ppermute | solution.py:38
  90.8 24.3 %copy-start.31 = (bf16[256,512]{1,0:T(8,128)(2,1)}, bf16[256,512]{1,0:T(8,128)(2,1)S(1)}, u32[]{:S(2)}) copy-start(bf16[256,512]{1,0:T(8,128)(2,1)S(1)} %collective-permute-done.13) | copy-start | bytes 786436
  90.9 6.0 %collective-permute-start.23 = (bf16[128,512]{1,0:T(8,128)(2,1)S(1)}, bf16[128,512]{1,0:T(8,128)(2,1)S(1)}, u32[]{:S(2)}, u32[]{:S(2)}) collective-permute-start(bf16[128,512]{1,0:T(8,128)(2,1)S(1)} %fusion.49.refs_0_), channel_id=1, source_target_pairs={{0,8},{8,0},{16,24},{24,16},{1,9},{9,1},{17,25},{25,17},{2,10},{10... | collective-permute-start | bytes 393224 | tf_op jit(solution)/shard_map/ppermute | solution.py:38
  96.9 32.5 %collective-permute-start.27 = (bf16[1024,512]{1,0:T(8,128)(2,1)}, bf16[1024,512]{1,0:T(8,128)(2,1)}, u32[]{:S(2)}, u32[]{:S(2)}) collective-permute-start(bf16[1024,512]{1,0:T(8,128)(2,1)} %bitcast.24.refs_4_), channel_id=1, source_target_pairs={{0,4},{4,0},{1,5},{5,1},{2,6},{6,2},{3,7},{7,3},{8,12},{12,8},{9,1... | collective-permute-start | bytes 3145736 | tf_op jit(solution)/shard_map/ppermute | solution.py:38
  97.5 24.2 %collective-permute-start.24 = (bf16[2,128,512]{2,1,0:T(8,128)(2,1)S(1)}, bf16[2,128,512]{2,1,0:T(8,128)(2,1)S(1)}, u32[]{:S(2)}, u32[]{:S(2)}) collective-permute-start(bf16[2,128,512]{2,1,0:T(8,128)(2,1)S(1)} %pad_maximum_fusion), channel_id=1, source_target_pairs={{0,16},{8,24},{16,0},{24,8},{1,17},{9,25},{17,1},{25,9},{2,18},{10... | collective-permute-start | bytes 786440 | tf_op jit(solution)/shard_map/ppermute | solution.py:38
  106.8 14.2 %copy-start.26 = (bf16[1024,512]{1,0:T(8,128)(2,1)}, bf16[1024,512]{1,0:T(8,128)(2,1)S(1)}, u32[]{:S(2)}) copy-start(bf16[1024,512]{1,0:T(8,128)(2,1)S(1)} %collective-permute-done.26.refs_3_) | copy-start | bytes 3145732
  106.8 0.9 copy-start.27
  115.1 6.6 %copy-start.2 = (bf16[128,2048]{1,0:T(8,128)(2,1)S(1)}, bf16[128,2048]{1,0:T(8,128)(2,1)}, u32[]{:S(2)}) copy-start(bf16[128,2048]{1,0:T(8,128)(2,1)} %tokens_ref.1) | copy-start | bytes 1572868
  115.1 6.6 %copy-start.21 = (f32[2048]{0:T(1024)S(1)}, f32[2048]{0:T(1024)}, u32[]{:S(2)}) copy-start(f32[2048]{0:T(1024)} %param.21) | copy-start | bytes 24580
  115.1 8.9 %copy-start.6 = (bf16[1,512,1024]{2,1,0:T(8,128)(2,1)S(1)}, bf16[1,512,1024]{2,1,0:T(8,128)(2,1)}, u32[]{:S(2)}) copy-start(bf16[1,512,1024]{2,1,0:T(8,128)(2,1)} %param.29) | copy-start | bytes 3145732
  115.2 10.2 %copy-start.32 = (bf16[256,512]{1,0:T(8,128)(2,1)S(1)}, bf16[256,512]{1,0:T(8,128)(2,1)}, u32[]{:S(2)}) copy-start(bf16[256,512]{1,0:T(8,128)(2,1)} %copy-done.31) | copy-start | bytes 786436
  121.0 17.5 %collective-permute-start.33 = (bf16[2,384,512]{2,1,0:T(8,128)(2,1)}, bf16[2,384,512]{2,1,0:T(8,128)(2,1)}, u32[]{:S(2)}, u32[]{:S(2)}) collective-permute-start(bf16[2,384,512]{2,1,0:T(8,128)(2,1)} %get-tuple-element.77), channel_id=1, source_target_pairs={{0,8},{8,0},{16,24},{24,16},{1,9},{9,1},{17,25},{25,17},{2,10},{10... | collective-permute-start | bytes 2359304 | tf_op jit(solution)/shard_map/ppermute | solution.py:38
  122.2 7.2 %copy-start.3 = (bf16[128,2048]{1,0:T(8,128)(2,1)}, bf16[128,2048]{1,0:T(8,128)(2,1)S(1)}, u32[]{:S(2)}) copy-start(bf16[128,2048]{1,0:T(8,128)(2,1)S(1)} %memory.1.refs_0_) | copy-start | bytes 1572868
  122.2 4.4 %collective-permute-start.25 = (bf16[128,2048]{1,0:T(8,128)(2,1)S(1)}, bf16[128,2048]{1,0:T(8,128)(2,1)}, u32[]{:S(2)}, u32[]{:S(2)}) collective-permute-start(bf16[128,2048]{1,0:T(8,128)(2,1)S(1)} %memory.1.refs_0_), channel_id=1, source_target_pairs={{0,1},{1,0},{2,3},{3,2},{4,5},{5,4},{6,7},{7,6},{8,9},{9,8},{10,11... | collective-permute-start | bytes 1572872 | tf_op jit(solution)/shard_map/ppermute | solution.py:38
  122.3 14.4 %collective-permute-start.28 = (bf16[128,2048]{1,0:T(8,128)(2,1)S(1)}, bf16[128,2048]{1,0:T(8,128)(2,1)}, u32[]{:S(2)}, u32[]{:S(2)}) collective-permute-start(bf16[128,2048]{1,0:T(8,128)(2,1)S(1)} %memory.1.refs_0_), channel_id=1, source_target_pairs={{0,2},{1,3},{2,0},{3,1},{4,6},{5,7},{6,4},{7,5},{8,10},{9,11},{10,... | collective-permute-start | bytes 1572872 | tf_op jit(solution)/shard_map/ppermute | solution.py:38
  124.0 26.6 %collective-permute-start.30 = (bf16[512,1024]{1,0:T(8,128)(2,1)S(1)}, bf16[512,1024]{1,0:T(8,128)(2,1)}, u32[]{:S(2)}, u32[]{:S(2)}) collective-permute-start(bf16[512,1024]{1,0:T(8,128)(2,1)S(1)} %bitcast.79), channel_id=1, source_target_pairs={{0,4},{4,0},{1,5},{5,1},{2,6},{6,2},{3,7},{7,3},{8,12},{12,8},{9,1... | collective-permute-start | bytes 3145736 | tf_op jit(solution)/shard_map/ppermute | solution.py:38
  125.4 13.2 %copy-start.28 = (f32[384,512]{1,0:T(8,128)S(1)}, f32[384,512]{1,0:T(8,128)}, u32[]{:S(2)}) copy-start(f32[384,512]{1,0:T(8,128)} %get-tuple-element.76) | copy-start | bytes 2359300
  134.8 15.8 %copy-start.8 = (bf16[128,512]{1,0:T(8,128)(2,1)S(1)}, bf16[128,512]{1,0:T(8,128)(2,1)}, u32[]{:S(2)}) copy-start(bf16[128,512]{1,0:T(8,128)(2,1)} %attend_sentence.2.mine_ref) | copy-start | bytes 393220
  134.8 15.8 %copy-start.22 = (s32[3]{0:T(128)S(1)}, s32[3]{0:T(128)}, u32[]{:S(2)}) copy-start(s32[3]{0:T(128)} %pad_add_fusion.1.place_ref) | copy-start | bytes 40
  136.7 6.2 %collective-permute-start.29 = (bf16[128,2048]{1,0:T(8,128)(2,1)}, bf16[128,2048]{1,0:T(8,128)(2,1)S(1)}, u32[]{:S(2)}, u32[]{:S(2)}) collective-permute-start(bf16[128,2048]{1,0:T(8,128)(2,1)} %collective-permute-done.28.refs_0_), channel_id=1, source_target_pairs={{0,1},{1,0},{2,3},{3,2},{4,5},{5,4},{6,7},{7,6},{8,9},{9,8},{10,11... | collective-permute-start | bytes 1572872 | tf_op jit(solution)/shard_map/ppermute | solution.py:38
  139.6 19.1 %collective-permute-start.34 = (bf16[384,512]{1,0:T(8,128)(2,1)S(1)}, bf16[384,512]{1,0:T(8,128)(2,1)S(1)}, u32[]{:S(2)}, u32[]{:S(2)}) collective-permute-start(bf16[384,512]{1,0:T(8,128)(2,1)S(1)} %fusion.35), channel_id=1, source_target_pairs={{0,16},{8,24},{16,0},{24,8},{1,17},{9,25},{17,1},{25,9},{2,18},{10... | collective-permute-start | bytes 1179656 | tf_op jit(solution)/shard_map/ppermute | solution.py:38
  143.7 16.9 %copy-start.29 = (f32[384,512]{1,0:T(8,128)S(1)}, f32[384,512]{1,0:T(8,128)}, u32[]{:S(2)}) copy-start(f32[384,512]{1,0:T(8,128)} %get-tuple-element.80) | copy-start | bytes 2359300
  150.7 0.9 copy-start.9
  151.6 14.4 %copy-start.34 = (s32[2]{0:T(128)S(1)}, s32[2]{0:T(128)}, u32[]{:S(2)}) copy-start(s32[2]{0:T(128)} %param.24) | copy-start | bytes 28
  153.5 5.2 %collective-permute-start.35 = (bf16[256,512]{1,0:T(8,128)(2,1)S(1)}, bf16[256,512]{1,0:T(8,128)(2,1)S(1)}, u32[]{:S(2)}, u32[]{:S(2)}) collective-permute-start(bf16[256,512]{1,0:T(8,128)(2,1)S(1)} %get-tuple-element.79), channel_id=1, source_target_pairs={{0,1},{1,0},{2,3},{3,2},{4,5},{5,4},{6,7},{7,6},{8,9},{9,8},{10,11... | collective-permute-start | bytes 786440 | tf_op jit(solution)/shard_map/ppermute | solution.py:38
  153.6 12.5 %collective-permute-start.31 = (bf16[256,512]{1,0:T(8,128)(2,1)S(1)}, bf16[256,512]{1,0:T(8,128)(2,1)S(1)}, u32[]{:S(2)}, u32[]{:S(2)}) collective-permute-start(bf16[256,512]{1,0:T(8,128)(2,1)S(1)} %get-tuple-element.71), channel_id=1, source_target_pairs={{0,1},{1,0},{2,3},{3,2},{4,5},{5,4},{6,7},{7,6},{8,9},{9,8},{10,11... | collective-permute-start | bytes 786440 | tf_op jit(solution)/shard_map/ppermute | solution.py:38
  158.8 7.3 %collective-permute-start.36 = (bf16[256,512]{1,0:T(8,128)(2,1)S(1)}, bf16[256,512]{1,0:T(8,128)(2,1)S(1)}, u32[]{:S(2)}, u32[]{:S(2)}) collective-permute-start(bf16[256,512]{1,0:T(8,128)(2,1)S(1)} %convert_add_fusion.3), channel_id=1, source_target_pairs={{0,2},{1,3},{2,0},{3,1},{4,6},{5,7},{6,4},{7,5},{8,10},{9,11},{10,... | collective-permute-start | bytes 786440 | tf_op jit(solution)/shard_map/ppermute | solution.py:38
  162.5 11.7 %all-to-all-start = ((bf16[8,48,512]{2,1,0:T(8,128)(2,1)}), bf16[8,48,512]{2,1,0:T(8,128)(2,1)S(1)}, u32[]{:S(2)}, u32[]{:S(2)}) async-start(bf16[8,48,512]{2,1,0:T(8,128)(2,1)} %bitcast.31), calls=%async_computation | async-start | bytes 786432 | tf_op jit(solution)/shard_map/all_to_all | solution.py:142
  (9 other events, 6.7 us)

commit v16 on v12

--- a/solution.py
+++ b/solution.py
@@ -627,7 +627,6 @@
     pre_core, part_core = forward(gate(rows_core, part_own))
     home = send_home(part_own, near_codes, capacity) + send_home(part_core, core_codes, capacity)
     grad_y = jnp.concatenate([gate(half_y, home[4]), other_y], axis=0)
-    query_back = swap(gate(query_there.astype(jnp.bfloat16), home[5], home[6]), "expert", 1)
 
     rise_own, rise_core = slope_of(gate(pre_own, home[1])), slope_of(gate(pre_core, home[1]))
     held_gates = gate(gate_weights, rise_own, rise_core, query_there, grad_y)
@@ -640,6 +639,7 @@
     mixed_sum = first + from_pair[0].astype(jnp.float32)
     mixed_slice = (mixed_sum + from_other.astype(jnp.float32)).astype(jnp.bfloat16)
     key_other = swap(gate(key_own, first), "expert", 1)
+    query_back = swap(gate(query_there.astype(jnp.bfloat16), key_other), "expert", 1)
     mixed_near = swap(mixed_slice, "section", 1)
     grads_own, grads_sent = dispatch(
         which_section,

time: 173 us -> 179 us (1.035)
  waiting for transfers between devices: 60.7 us -> 66.8 us
    ppermute x29, waiting for transfers between devices: 46.1 us -> 52.3 us  [swap(): return lax.ppermute(value, axis, [(i, i ^ mask) for i in range(size)])]
  transfers between devices with their start and end apart: 37 -> 37, of which waited for: 15 -> 13; matrix products, arithmetic and copies ran while one was open for 15% -> 15% of each run, Pallas kernels for 17% -> 17%
where the time goes in v16:
time: 179 us
  waiting for transfers between devices  66.8 us (37%)
  starting transfers between devices  42.6 us (24%)
  Pallas kernels  33 us (18%)
  local copies, waits for them, and re-layouts  15.8 us (9%)
  other arithmetic  11.2 us (6%)
  matrix products  8.24 us (5%)
    ppermute x29, waiting for transfers between devices, swap(): return lax.ppermute(value, axis, [(i, i ^ mask) for i in range(size)])  52.3 us
    ppermute x29, starting transfers between devices, swap(): return lax.ppermute(value, axis, [(i, i ^ mask) for i in range(size)])  32.3 us
    pallas_call x2, Pallas kernels, attend_sentence(): pl.pallas_call(attend_kernel, out_shape=jax.ShapeDtypeStruct(query.shape,...  10.9 us
    unnamed x59, local copies, waits for them, and re-layouts  10.8 us
    ppermute x7, waiting for transfers between devices, send_home(): lax.ppermute(block, ('expert', 'dp'), [(i, i ^ code) for i in range(size)])  9.08 us
    pallas_call x1, Pallas kernels, expert_slope(): pl.pallas_call(functools.partial(slope_kernel, codes), out_shape=jax.Shap...  7.34 us
    ppermute x7, starting transfers between devices, send_home(): lax.ppermute(block, ('expert', 'dp'), [(i, i ^ code) for i in range(size)])  6.88 us
    pallas_call x1, Pallas kernels, expert_backward(): pl.pallas_call(functools.partial(backward_kernel, split), out_shape=(jax....  5.84 us
  transfers between devices with their start and end apart: 37, of which 13 were waited for; matrix products, arithmetic and copies ran while one was open for 15% of the time, Pallas kernels for 17%

profile of v16, /device:TPU:0, one launch (start us, length us, event | category | flops | bytes accessed | tf_op | source)
XLA Modules:
  0.0 178.7 jit_solution(4675076972658846623)
XLA Ops:
  0.6 3.0 %collective-permute-start = (bf16[128,2048]{1,0:T(8,128)(2,1)}, bf16[128,2048]{1,0:T(8,128)(2,1)S(1)}, u32[]{:S(2)}, u32[]{:S(2)}) collective-permute-start(bf16[128,2048]{1,0:T(8,128)(2,1)} %tokens_ref), channel_id=1, source_target_pairs={{0,4},{4,0},{1,5},{5,1},{2,6},{6,2},{3,7},{7,3},{8,12},{12,8},{9,1... | collective-permute-start | bytes 1572872 | tf_op jit(solution)/shard_map/ppermute | solution.py:38
  3.7 1.5 collective-permute-start.3
  5.8 1.0 constant_dynamic-slice_fusion.2
  7.5 8.4 %collective-permute-done.4 = s32[2,128]{1,0:T(2,128)S(1)} collective-permute-done((s32[2,128]{1,0:T(2,128)}, s32[2,128]{1,0:T(2,128)S(1)}, u32[]{:S(2)}, u32[]{:S(2)}) %collective-permute-start.4) | collective-permute-done | bytes 1056 | tf_op jit(solution)/shard_map/ppermute | solution.py:38
  15.9 1.7 collective-permute-start.7
  17.7 1.5 collective-permute-start.1
  21.1 1.2 copy-done.4
  23.8 0.8 copy-done.15
  27.7 1.5 collective-permute-start.2
  29.3 1.6 collective-permute-start.8
  30.9 1.0 copy-done.1
  31.9 1.3 dispatch.2
  33.2 3.2 %fusion.61 = f32[192,1024]{1,0:T(8,128)S(1)} fusion(bf16[192,2048]{1,0:T(8,128)(2,1)S(1)} %get-tuple-element.46, bf16[1,2048,1024]{2,1,0:T(8,128)(2,1)} %param.19), kind=kOutput, calls=%fused_computation.101 | convolution fusion | flops 805306368 | bytes 5767168 | tf_op jit(solution)/shard_map/dot_general | solution.py:610
  36.5 1.1 convolution_convert_fusion.1
  37.6 0.8 fusion.73
  39.7 2.3 %collective-permute-start.13 = (bf16[48,2048]{1,0:T(8,128)(2,1)}, bf16[48,2048]{1,0:T(8,128)(2,1)}, u32[]{:S(2)}, u32[]{:S(2)}) collective-permute-start(bf16[48,2048]{1,0:T(8,128)(2,1)} %get-tuple-element.84), channel_id=1, source_target_pairs={{0,6},{1,7},{2,4},{3,5},{4,2},{5,3},{6,0},{7,1},{8,14},{9,15},{10,... | collective-permute-start | bytes 589832 | tf_op jit(solution)/shard_map/ppermute | solution.py:223
  42.0 4.1 %collective-permute-done.9.refs_1_ = bf16[48,2048]{1,0:T(8,128)(2,1)S(1)} collective-permute-done((bf16[48,2048]{1,0:T(8,128)(2,1)S(1)}, bf16[48,2048]{1,0:T(8,128)(2,1)S(1)}, u32[]{:S(2)}, u32[]{:S(2)}) %collective-permute-start.9) | collective-permute-done | bytes 196640 | tf_op jit(solution)/shard_map/ppermute | solution.py:223
  46.1 1.2 fusion.1
  47.3 1.0 fusion.59
  48.3 1.1 convolution_convert_fusion
  49.4 0.8 fusion.72
  51.1 2.1 %fusion.10 = (f32[192,1024]{1,0:T(8,128)}, f32[192,1024]{1,0:T(8,128)}) fusion(f32[192,1024]{1,0:T(8,128)S(1)} %fusion.61, f32[192,1024]{1,0:T(8,128)S(1)} %fusion.59), kind=kLoop, calls=%fused_computation.20 | loop fusion | flops 6684672 | bytes 3145728 | tf_op jit(solution)/shard_map/transpose(jvp())/add_any | solution.py:616
  53.9 2.5 %collective-permute-start.16 = (bf16[48,2048]{1,0:T(8,128)(2,1)}, bf16[48,2048]{1,0:T(8,128)(2,1)}, u32[]{:S(2)}, u32[]{:S(2)}) collective-permute-start(bf16[48,2048]{1,0:T(8,128)(2,1)} %get-tuple-element.80), channel_id=1, source_target_pairs={{0,7},{1,6},{2,5},{3,4},{4,3},{5,2},{6,1},{7,0},{8,15},{9,14},{10,... | collective-permute-start | bytes 589832 | tf_op jit(solution)/shard_map/ppermute | solution.py:223
  56.3 1.0 constant_dynamic-update-slice_fusion.1
  57.5 5.0 %collective-permute-done.15.refs_6_ = bf16[48,2048]{1,0:T(8,128)(2,1)} collective-permute-done((bf16[48,2048]{1,0:T(8,128)(2,1)}, bf16[48,2048]{1,0:T(8,128)(2,1)}, u32[]{:S(2)}, u32[]{:S(2)}) %collective-permute-start.15) | collective-permute-done | bytes 196640 | tf_op jit(solution)/shard_map/ppermute | solution.py:223
  62.5 0.9 copy-done.11
  63.4 2.1 %combine.2 = (bf16[2,128,512]{2,1,0:T(8,128)(2,1)S(1)}, f32[128,512]{1,0:T(8,128)S(1)}, f32[128,512]{1,0:T(8,128)S(1)}) custom-call(s32[1]{0:T(128)} %bitcast.8.section_ref, s32[128,2]{1,0:T(8,128)S(1)} %get-tuple-element.93.position_ref, f32[128,2]{1,0:T(8,128)S(1)} %copy.39.gates_ref, bf16[48,2048]{1,0:T(8,128)(2,1)S(1)} %get-tuple-element.86.refs_0_, ...), custom_call_target="tpu_custom_call" | custom-call | flops 1 | bytes 1 | tf_op jit(solution)/shard_map/combine/pallas_call | solution.py:264
  65.5 0.8 collective-permute-start.19
  66.3 1.5 collective-permute-start.30
  68.3 0.9 collective-permute-start.17
  69.2 4.6 %collective-permute-done.19 = bf16[2,128,512]{2,1,0:T(8,128)(2,1)S(1)} collective-permute-done((bf16[2,128,512]{2,1,0:T(8,128)(2,1)S(1)}, bf16[2,128,512]{2,1,0:T(8,128)(2,1)S(1)}, u32[]{:S(2)}, u32[]{:S(2)}) %collective-permute-start.19) | collective-permute-done | bytes 262176 | tf_op jit(solution)/shard_map/ppermute | solution.py:38
  73.9 2.7 %collective-permute-start.20 = (bf16[128,512]{1,0:T(8,128)(2,1)S(1)}, bf16[128,512]{1,0:T(8,128)(2,1)S(1)}, u32[]{:S(2)}, u32[]{:S(2)}) collective-permute-start(bf16[128,512]{1,0:T(8,128)(2,1)S(1)} %fusion.48), channel_id=1, source_target_pairs={{0,16},{8,24},{16,0},{24,8},{1,17},{9,25},{17,1},{25,9},{2,18},{10... | collective-permute-start | bytes 393224 | tf_op jit(solution)/shard_map/ppermute | solution.py:38
  76.5 5.8 %collective-permute-done.20 = bf16[128,512]{1,0:T(8,128)(2,1)S(1)} collective-permute-done((bf16[128,512]{1,0:T(8,128)(2,1)S(1)}, bf16[128,512]{1,0:T(8,128)(2,1)S(1)}, u32[]{:S(2)}, u32[]{:S(2)}) %collective-permute-start.20) | collective-permute-done | bytes 131104 | tf_op jit(solution)/shard_map/ppermute | solution.py:38
  83.1 4.3 %collective-permute-done.21.refs_1_ = bf16[128,512]{1,0:T(8,128)(2,1)S(1)} collective-permute-done((bf16[128,512]{1,0:T(8,128)(2,1)S(1)}, bf16[128,512]{1,0:T(8,128)(2,1)S(1)}, u32[]{:S(2)}, u32[]{:S(2)}) %collective-permute-start.21) | collective-permute-done | bytes 131104 | tf_op jit(solution)/shard_map/ppermute | solution.py:38
  87.4 4.1 %collective-permute-done.29.refs_1_ = bf16[128,2048]{1,0:T(8,128)(2,1)S(1)} collective-permute-done((bf16[128,2048]{1,0:T(8,128)(2,1)S(1)}, bf16[128,2048]{1,0:T(8,128)(2,1)S(1)}, u32[]{:S(2)}, u32[]{:S(2)}) %collective-permute-start.29) | collective-permute-done | bytes 524320 | tf_op jit(solution)/shard_map/ppermute | solution.py:38
  91.6 1.4 dispatch.3
  93.0 0.9 copy-done.7
  93.9 0.9 collective-permute-start.24
  94.9 1.1 collective-permute-start.18
  96.0 2.7 %collective-permute-start.22 = (bf16[2,128,512]{2,1,0:T(8,128)(2,1)S(1)}, bf16[2,128,512]{2,1,0:T(8,128)(2,1)S(1)}, u32[]{:S(2)}, u32[]{:S(2)}) collective-permute-start(bf16[2,128,512]{2,1,0:T(8,128)(2,1)S(1)} %pad_maximum_fusion), channel_id=1, source_target_pairs={{0,16},{8,24},{16,0},{24,8},{1,17},{9,25},{17,1},{25,9},{2,18},{10... | collective-permute-start | bytes 786440 | tf_op jit(solution)/shard_map/ppermute | solution.py:38
  98.7 0.9 copy-done.19
  99.6 7.3 %expert_slope.1.slope_ref = bf16[384,1024]{1,0:T(8,128)(2,1)} custom-call(s32[1]{0:T(128)} %bitcast.27.here_ref, bf16[192,2048]{1,0:T(8,128)(2,1)} %copy-done.7, bf16[192,2048]{1,0:T(8,128)(2,1)} %copy-done.19, f32[192,1024]{1,0:T(8,128)} %get-tuple-element.94.rise_own, f32[192,1024]{1,0:T(8,128)} %get-tuple-element.95.rise_core, bf16[1024,2048]{1,0:T(8,128)(2,1)} %bitcast.84), custom_call_target="tpu_custom_call" | custom-call | flops 1 | bytes 1 | tf_op jit(solution)/shard_map/expert_slope/pallas_call | solution.py:478
  107.0 5.8 %expert_backward.1 = (bf16[2,384,512]{2,1,0:T(8,128)(2,1)}, f32[384,512]{1,0:T(8,128)}, f32[384,512]{1,0:T(8,128)}) custom-call(s32[1]{0:T(128)} %bitcast.8.section_ref, bf16[384,1024]{1,0:T(8,128)(2,1)} %expert_slope.1.slope_ref, bf16[2048,1024]{1,0:T(8,128)(2,1)} %bitcast.83), custom_call_target="tpu_custom_call" | custom-call | flops 1 | bytes 1 | tf_op jit(solution)/shard_map/expert_backward/pallas_call | solution.py:520
  112.8 1.0 collective-permute-start.32
  113.8 11.5 %collective-permute-done.18 = bf16[256,512]{1,0:T(8,128)(2,1)S(1)} collective-permute-done((bf16[256,512]{1,0:T(8,128)(2,1)S(1)}, bf16[256,512]{1,0:T(8,128)(2,1)S(1)}, u32[]{:S(2)}, u32[]{:S(2)}) %collective-permute-start.18) | collective-permute-done | bytes 262176 | tf_op jit(solution)/shard_map/ppermute | solution.py:38
  125.9 1.6 collective-permute-start.25
  127.4 0.9 collective-permute-start.27
  130.2 5.4 %attend_sentence.2.mine_ref = bf16[128,512]{1,0:T(8,128)(2,1)} custom-call(s32[3]{0:T(128)} %pad_add_fusion.1.place_ref, s32[2]{0:T(128)} %lengths_ref.3, bf16[128,512]{1,0:T(8,128)(2,1)} %get-tuple-element.89.query_ref, bf16[128,2048]{1,0:T(8,128)(2,1)} %copy-done.3, bf16[128,2048]{1,0:T(8,128)(2,1)} %collective-permute-done.23.refs_1_, ...), custom_call_target="tpu_custom_call" | custom-call | flops 1 | bytes 1 | tf_op jit(solution)/shard_map/attend_sentence/pallas_call | solution.py:380
  135.6 4.7 %collective-permute-done.25.refs_0_ = bf16[128,2048]{1,0:T(8,128)(2,1)} collective-permute-done((bf16[128,2048]{1,0:T(8,128)(2,1)S(1)}, bf16[128,2048]{1,0:T(8,128)(2,1)}, u32[]{:S(2)}, u32[]{:S(2)}) %collective-permute-start.25) | collective-permute-done | bytes 524320 | tf_op jit(solution)/shard_map/ppermute | solution.py:38
  140.3 1.1 fusion.35
  141.5 2.7 %collective-permute-start.33 = (bf16[384,512]{1,0:T(8,128)(2,1)S(1)}, bf16[384,512]{1,0:T(8,128)(2,1)S(1)}, u32[]{:S(2)}, u32[]{:S(2)}) collective-permute-start(bf16[384,512]{1,0:T(8,128)(2,1)S(1)} %fusion.35), channel_id=1, source_target_pairs={{0,16},{8,24},{16,0},{24,8},{1,17},{9,25},{17,1},{25,9},{2,18},{10... | collective-permute-start | bytes 1179656 | tf_op jit(solution)/shard_map/ppermute | solution.py:38
  144.7 0.8 copy-done.22
  145.5 5.5 %attend_sentence.3.done_ref = bf16[128,512]{1,0:T(8,128)(2,1)} custom-call(s32[3]{0:T(128)} %pad_add_fusion.3.place_ref, s32[2]{0:T(128)} %lengths_ref.3, bf16[128,512]{1,0:T(8,128)(2,1)} %get-tuple-element.88.query_ref, bf16[128,2048]{1,0:T(8,128)(2,1)} %collective-permute-done.25.refs_0_, bf16[128,2048]{1,0:T(8,128)(2,1)} %copy-done.22, ...), custom_call_target="tpu_custom_call" | custom-call | flops 1 | bytes 1 | tf_op jit(solution)/shard_map/attend_sentence/pallas_call | solution.py:380
  151.0 1.7 collective-permute-done.27.other_ref
  152.8 0.9 copy-done.9
  153.7 2.0 %project.1 = (bf16[256,512]{1,0:T(8,128)(2,1)S(1)}, bf16[256,512]{1,0:T(8,128)(2,1)S(1)}, f32[256,512]{1,0:T(8,128)S(1)}, f32[256,512]{1,0:T(8,128)S(1)}) custom-call(s32[3]{0:T(128)S(1)} %copy-done.14, bf16[128,512]{1,0:T(8,128)(2,1)S(1)} %copy-done.8, bf16[128,512]{1,0:T(8,128)(2,1)S(1)} %copy-done.9, bf16[512,1024]{1,0:T(8,128)(2,1)S(1)} %bitcast.80, ...), custom_call_target="tpu_custom_call" | custom-call | flops 1 | bytes 1 | tf_op jit(solution)/shard_map/project/pallas_call | solution.py:431
  156.2 6.1 %collective-permute-done.33 = bf16[384,512]{1,0:T(8,128)(2,1)S(1)} collective-permute-done((bf16[384,512]{1,0:T(8,128)(2,1)S(1)}, bf16[384,512]{1,0:T(8,128)(2,1)S(1)}, u32[]{:S(2)}, u32[]{:S(2)}) %collective-permute-start.33) | collective-permute-done | bytes 393248 | tf_op jit(solution)/shard_map/ppermute | solution.py:38
  162.5 1.6 collective-permute-start.35
  164.0 1.9 %fusion.34 = bf16[384,512]{1,0:T(8,128)(2,1)} fusion(f32[384,512]{1,0:T(8,128)S(1)} %copy-done.21, bf16[384,512]{1,0:T(8,128)(2,1)S(1)} %collective-permute-done.33, bf16[2,384,512]{2,1,0:T(8,128)(2,1)} %collective-permute-done.32), kind=kLoop, calls=%fused_computation.45 | loop fusion | flops 983040 | bytes 1966080 | tf_op jit(solution)/shard_map/convert_element_type | solution.py:709
  166.0 3.5 %all-to-all-start = ((bf16[8,48,512]{2,1,0:T(8,128)(2,1)}), bf16[8,48,512]{2,1,0:T(8,128)(2,1)S(1)}, u32[]{:S(2)}, u32[]{:S(2)}) async-start(bf16[8,48,512]{2,1,0:T(8,128)(2,1)} %bitcast.31), calls=%async_computation | async-start | bytes 786432 | tf_op jit(solution)/shard_map/all_to_all | solution.py:142
  169.6 0.9 collective-permute-done.35
  170.5 1.8 %fusion.47 = bf16[1,256,512]{2,1,0:T(8,128)(2,1)} fusion(bf16[256,512]{1,0:T(8,128)(2,1)S(1)} %collective-permute-done.35, f32[256,512]{1,0:T(8,128)S(1)} %get-tuple-element.64, bf16[256,512]{1,0:T(8,128)(2,1)S(1)} %collective-permute-done.28, bf16[1,256,2048]{2,1,0:T(8,128)(2,1)} %param.22, s32[]{:T(128)S(6)} %select_n.35, ...), kind=kLoop, calls=%fused_computation.62 | loop fusion | flops 1048576 | bytes 1573124 | tf_op jit(solution)/shard_map/broadcast_in_dim | solution.py:714
  172.3 5.4 %all-to-all-done = bf16[8,48,512]{2,1,0:T(8,128)(2,1)S(1)} async-done(((bf16[8,48,512]{2,1,0:T(8,128)(2,1)}), bf16[8,48,512]{2,1,0:T(8,128)(2,1)S(1)}, u32[]{:S(2)}, u32[]{:S(2)}) %all-to-all-start) | async-done | bytes 393248 | tf_op jit(solution)/shard_map/all_to_all | solution.py:142
  177.7 1.0 combine.3
  (113 shorter events, 16.1 us)
Async XLA Ops:
  0.6 45.5 %copy-start = (bf16[1,1024,512]{2,1,0:T(8,128)(2,1)S(1)}, bf16[1,1024,512]{2,1,0:T(8,128)(2,1)}, u32[]{:S(2)}) copy-start(bf16[1,1024,512]{2,1,0:T(8,128)(2,1)} %param.26) | copy-start | bytes 3145732
  0.6 15.2 %collective-permute-start = (bf16[128,2048]{1,0:T(8,128)(2,1)}, bf16[128,2048]{1,0:T(8,128)(2,1)S(1)}, u32[]{:S(2)}, u32[]{:S(2)}) collective-permute-start(bf16[128,2048]{1,0:T(8,128)(2,1)} %tokens_ref), channel_id=1, source_target_pairs={{0,4},{4,0},{1,5},{5,1},{2,6},{6,2},{3,7},{7,3},{8,12},{12,8},{9,1... | collective-permute-start | bytes 1572872 | tf_op jit(solution)/shard_map/ppermute | solution.py:38
  3.7 3.8 %collective-permute-start.3 = (s32[2,128]{1,0:T(2,128)}, s32[2,128]{1,0:T(2,128)S(1)}, u32[]{:S(2)}, u32[]{:S(2)}) collective-permute-start(s32[2,128]{1,0:T(2,128)} %bitcast.88), channel_id=1, source_target_pairs={{0,2},{1,3},{2,0},{3,1},{4,6},{5,7},{6,4},{7,5},{8,10},{9,11},{10,... | collective-permute-start | bytes 3080 | tf_op jit(solution)/shard_map/ppermute | solution.py:38
  5.2 10.7 %collective-permute-start.4 = (s32[2,128]{1,0:T(2,128)}, s32[2,128]{1,0:T(2,128)S(1)}, u32[]{:S(2)}, u32[]{:S(2)}) collective-permute-start(s32[2,128]{1,0:T(2,128)} %bitcast.89), channel_id=1, source_target_pairs={{0,4},{4,0},{1,5},{5,1},{2,6},{6,2},{3,7},{7,3},{8,12},{12,8},{9,1... | collective-permute-start | bytes 3080 | tf_op jit(solution)/shard_map/ppermute | solution.py:38
  5.7 25.2 %collective-permute-start.6 = (bf16[128,2048]{1,0:T(8,128)(2,1)}, bf16[128,2048]{1,0:T(8,128)(2,1)S(1)}, u32[]{:S(2)}, u32[]{:S(2)}) collective-permute-start(bf16[128,2048]{1,0:T(8,128)(2,1)} %tokens_ref), channel_id=1, source_target_pairs={{0,2},{1,3},{2,0},{3,1},{4,6},{5,7},{6,4},{7,5},{8,10},{9,11},{10,... | collective-permute-start | bytes 1572872 | tf_op jit(solution)/shard_map/ppermute | solution.py:38
  15.9 15.0 %collective-permute-start.7 = (bf16[128,2048]{1,0:T(8,128)(2,1)S(1)}, bf16[128,2048]{1,0:T(8,128)(2,1)S(1)}, u32[]{:S(2)}, u32[]{:S(2)}) collective-permute-start(bf16[128,2048]{1,0:T(8,128)(2,1)S(1)} %collective-permute-done.refs_2_), channel_id=1, source_target_pairs={{0,2},{1,3},{2,0},{3,1},{4,6},{5,7},{6,4},{7,5},{8,10},{9,11},{10,... | collective-permute-start | bytes 1572872 | tf_op jit(solution)/shard_map/ppermute | solution.py:38
  17.7 10.0 %collective-permute-start.1 = (bf16[64,2048]{1,0:T(8,128)(2,1)S(1)}, bf16[64,2048]{1,0:T(8,128)(2,1)}, u32[]{:S(2)}, u32[]{:S(2)}) collective-permute-start(bf16[64,2048]{1,0:T(8,128)(2,1)S(1)} %constant_dynamic-slice_fusion.2), channel_id=1, source_target_pairs={{0,4},{4,0},{1,5},{5,1},{2,6},{6,2},{3,7},{7,3},{8,12},{12,8},{9,1... | collective-permute-start | bytes 786440 | tf_op jit(solution)/shard_map/ppermute | solution.py:38
  19.9 7.0 %collective-permute-start.5 = (s32[2,128]{1,0:T(2,128)S(1)}, s32[2,128]{1,0:T(2,128)S(1)}, u32[]{:S(2)}, u32[]{:S(2)}) collective-permute-start(s32[2,128]{1,0:T(2,128)S(1)} %collective-permute-done.3), channel_id=1, source_target_pairs={{0,4},{4,0},{1,5},{5,1},{2,6},{6,2},{3,7},{7,3},{8,12},{12,8},{9,1... | collective-permute-start | bytes 3080 | tf_op jit(solution)/shard_map/ppermute | solution.py:38
  21.1 1.2 copy-start.4
  22.4 0.7 copy-start.12
  23.8 0.8 copy-start.15
  27.7 18.4 %collective-permute-start.2 = (bf16[256,1024]{1,0:T(8,128)(2,1)}, bf16[256,1024]{1,0:T(8,128)(2,1)S(1)}, u32[]{:S(2)}, u32[]{:S(2)}) collective-permute-start(bf16[256,1024]{1,0:T(8,128)(2,1)} %copy-done.15), channel_id=1, source_target_pairs={{0,4},{4,0},{1,5},{5,1},{2,6},{6,2},{3,7},{7,3},{8,12},{12,8},{9,1... | collective-permute-start | bytes 1572872 | tf_op jit(solution)/shard_map/ppermute | solution.py:38
  29.3 7.1 %collective-permute-start.8 = (bf16[64,2048]{1,0:T(8,128)(2,1)}, bf16[64,2048]{1,0:T(8,128)(2,1)S(1)}, u32[]{:S(2)}, u32[]{:S(2)}) collective-permute-start(bf16[64,2048]{1,0:T(8,128)(2,1)} %collective-permute-done.1), channel_id=1, source_target_pairs={{0,8},{8,0},{16,24},{24,16},{1,9},{9,1},{17,25},{25,17},{2,10},{10... | collective-permute-start | bytes 786440 | tf_op jit(solution)/shard_map/ppermute | solution.py:38
  30.9 1.0 copy-start.1
  31.9 4.6 %copy-start.17 = (bf16[1,1024,2048]{2,1,0:T(8,128)(2,1)S(1)}, bf16[1,1024,2048]{2,1,0:T(8,128)(2,1)}, u32[]{:S(2)}) copy-start(bf16[1,1024,2048]{2,1,0:T(8,128)(2,1)} %param.20) | copy-start | bytes 12582916
  36.4 2.6 %copy-start.24 = (s32[128,2]{1,0:T(8,128)S(1)}, s32[128,2]{1,0:T(8,128)}, u32[]{:S(2)}) copy-start(s32[128,2]{1,0:T(8,128)} %copy.38) | copy-start | bytes 3076
  36.4 2.6 %copy-start.25 = (s32[128,2]{1,0:T(8,128)S(1)}, s32[128,2]{1,0:T(8,128)}, u32[]{:S(2)}) copy-start(s32[128,2]{1,0:T(8,128)} %copy.41) | copy-start | bytes 3076
  36.4 10.9 %copy-start.16 = (bf16[1,2048,1024]{2,1,0:T(8,128)(2,1)S(1)}, bf16[1,2048,1024]{2,1,0:T(8,128)(2,1)}, u32[]{:S(2)}) copy-start(bf16[1,2048,1024]{2,1,0:T(8,128)(2,1)} %param.19) | copy-start | bytes 12582916
  36.4 10.9 %collective-permute-start.10 = (bf16[192,2048]{1,0:T(8,128)(2,1)S(1)}, bf16[192,2048]{1,0:T(8,128)(2,1)S(1)}, u32[]{:S(2)}, u32[]{:S(2)}) collective-permute-start(bf16[192,2048]{1,0:T(8,128)(2,1)S(1)} %get-tuple-element.49), channel_id=1, source_target_pairs={{0,1},{1,0},{2,3},{3,2},{4,5},{5,4},{6,7},{7,6},{8,9},{9,8},{10,11... | collective-permute-start | bytes 2359304 | tf_op jit(solution)/shard_map/ppermute | solution.py:38
  38.4 7.7 %collective-permute-start.9 = (bf16[48,2048]{1,0:T(8,128)(2,1)S(1)}, bf16[48,2048]{1,0:T(8,128)(2,1)S(1)}, u32[]{:S(2)}, u32[]{:S(2)}) collective-permute-start(bf16[48,2048]{1,0:T(8,128)(2,1)S(1)} %get-tuple-element.87), channel_id=1, source_target_pairs={{0,2},{1,3},{2,0},{3,1},{4,6},{5,7},{6,4},{7,5},{8,10},{9,11},{10,... | collective-permute-start | bytes 589832 | tf_op jit(solution)/shard_map/ppermute | solution.py:223
  39.0 18.5 %collective-permute-start.12 = (bf16[48,2048]{1,0:T(8,128)(2,1)}, bf16[48,2048]{1,0:T(8,128)(2,1)S(1)}, u32[]{:S(2)}, u32[]{:S(2)}) collective-permute-start(bf16[48,2048]{1,0:T(8,128)(2,1)} %get-tuple-element.85), channel_id=1, source_target_pairs={{0,4},{1,5},{2,6},{3,7},{4,0},{5,1},{6,2},{7,3},{8,12},{9,13},{10,... | collective-permute-start | bytes 589832 | tf_op jit(solution)/shard_map/ppermute | solution.py:223
  39.7 17.8 %collective-permute-start.13 = (bf16[48,2048]{1,0:T(8,128)(2,1)}, bf16[48,2048]{1,0:T(8,128)(2,1)}, u32[]{:S(2)}, u32[]{:S(2)}) collective-permute-start(bf16[48,2048]{1,0:T(8,128)(2,1)} %get-tuple-element.84), channel_id=1, source_target_pairs={{0,6},{1,7},{2,4},{3,5},{4,2},{5,3},{6,0},{7,1},{8,14},{9,15},{10,... | collective-permute-start | bytes 589832 | tf_op jit(solution)/shard_map/ppermute | solution.py:223
  49.4 8.0 %copy-start.26 = (f32[128,2]{0,1:T(2,128)S(1)}, f32[128,2]{0,1:T(2,128)}, u32[]{:S(2)}) copy-start(f32[128,2]{0,1:T(2,128)} %param.17) | copy-start | bytes 3076
  49.4 18.4 %copy-start.5 = (bf16[128,2048]{1,0:T(8,128)(2,1)S(1)}, bf16[128,2048]{1,0:T(8,128)(2,1)}, u32[]{:S(2)}) copy-start(bf16[128,2048]{1,0:T(8,128)(2,1)} %refs_0_.3) | copy-start | bytes 1572868
  50.3 2.9 %collective-permute-start.11 = (bf16[48,2048]{1,0:T(8,128)(2,1)S(1)}, bf16[48,2048]{1,0:T(8,128)(2,1)S(1)}, u32[]{:S(2)}, u32[]{:S(2)}) collective-permute-start(bf16[48,2048]{1,0:T(8,128)(2,1)S(1)} %get-tuple-element.83), channel_id=1, source_target_pairs={{0,1},{1,0},{2,3},{3,2},{4,5},{5,4},{6,7},{7,6},{8,9},{9,8},{10,11... | collective-permute-start | bytes 589832 | tf_op jit(solution)/shard_map/ppermute | solution.py:223
  50.3 7.2 %collective-permute-start.14 = (bf16[48,2048]{1,0:T(8,128)(2,1)}, bf16[48,2048]{1,0:T(8,128)(2,1)}, u32[]{:S(2)}, u32[]{:S(2)}) collective-permute-start(bf16[48,2048]{1,0:T(8,128)(2,1)} %get-tuple-element.82), channel_id=1, source_target_pairs={{0,3},{1,2},{2,1},{3,0},{4,7},{5,6},{6,5},{7,4},{8,11},{9,10},{10,... | collective-permute-start | bytes 589832 | tf_op jit(solution)/shard_map/ppermute | solution.py:223
  50.9 11.5 %collective-permute-start.15 = (bf16[48,2048]{1,0:T(8,128)(2,1)}, bf16[48,2048]{1,0:T(8,128)(2,1)}, u32[]{:S(2)}, u32[]{:S(2)}) collective-permute-start(bf16[48,2048]{1,0:T(8,128)(2,1)} %get-tuple-element.81), channel_id=1, source_target_pairs={{0,5},{1,4},{2,7},{3,6},{4,1},{5,0},{6,3},{7,2},{8,13},{9,12},{10,... | collective-permute-start | bytes 589832 | tf_op jit(solution)/shard_map/ppermute | solution.py:223
  53.9 8.6 %collective-permute-start.16 = (bf16[48,2048]{1,0:T(8,128)(2,1)}, bf16[48,2048]{1,0:T(8,128)(2,1)}, u32[]{:S(2)}, u32[]{:S(2)}) collective-permute-start(bf16[48,2048]{1,0:T(8,128)(2,1)} %get-tuple-element.80), channel_id=1, source_target_pairs={{0,7},{1,6},{2,5},{3,4},{4,3},{5,2},{6,1},{7,0},{8,15},{9,14},{10,... | collective-permute-start | bytes 589832 | tf_op jit(solution)/shard_map/ppermute | solution.py:223
  62.5 0.9 copy-start.11
  63.4 31.5 %copy-start.23 = (bf16[256,512]{1,0:T(8,128)(2,1)S(1)}, bf16[256,512]{1,0:T(8,128)(2,1)}, u32[]{:S(2)}) copy-start(bf16[256,512]{1,0:T(8,128)(2,1)} %fusion.1) | copy-start | bytes 786436
  65.5 8.4 %collective-permute-start.19 = (bf16[2,128,512]{2,1,0:T(8,128)(2,1)S(1)}, bf16[2,128,512]{2,1,0:T(8,128)(2,1)S(1)}, u32[]{:S(2)}, u32[]{:S(2)}) collective-permute-start(bf16[2,128,512]{2,1,0:T(8,128)(2,1)S(1)} %get-tuple-element.58), channel_id=1, source_target_pairs={{0,8},{8,0},{16,24},{24,16},{1,9},{9,1},{17,25},{25,17},{2,10},{10... | collective-permute-start | bytes 786440 | tf_op jit(solution)/shard_map/ppermute | solution.py:38
  66.3 21.1 %collective-permute-start.30 = (bf16[128,2048]{1,0:T(8,128)(2,1)S(1)}, bf16[128,2048]{1,0:T(8,128)(2,1)S(1)}, u32[]{:S(2)}, u32[]{:S(2)}) collective-permute-start(bf16[128,2048]{1,0:T(8,128)(2,1)S(1)} %constant_dynamic-update-slice_fusion.refs_2_), channel_id=1, source_target_pairs={{0,2},{1,3},{2,0},{3,1},{4,6},{5,7},{6,4},{7,5},{8,10},{9,11},{10,... | collective-permute-start | bytes 1572872 | tf_op jit(solution)/shard_map/ppermute | solution.py:38
  67.8 23.8 %collective-permute-start.29 = (bf16[128,2048]{1,0:T(8,128)(2,1)S(1)}, bf16[128,2048]{1,0:T(8,128)(2,1)S(1)}, u32[]{:S(2)}, u32[]{:S(2)}) collective-permute-start(bf16[128,2048]{1,0:T(8,128)(2,1)S(1)} %copy-done.5), channel_id=1, source_target_pairs={{0,2},{1,3},{2,0},{3,1},{4,6},{5,7},{6,4},{7,5},{8,10},{9,11},{10,... | collective-permute-start | bytes 1572872 | tf_op jit(solution)/shard_map/ppermute | solution.py:38
  68.3 26.5 %collective-permute-start.17 = (bf16[1024,512]{1,0:T(8,128)(2,1)}, bf16[1024,512]{1,0:T(8,128)(2,1)S(1)}, u32[]{:S(2)}, u32[]{:S(2)}) collective-permute-start(bf16[1024,512]{1,0:T(8,128)(2,1)} %bitcast.85), channel_id=1, source_target_pairs={{0,4},{4,0},{1,5},{5,1},{2,6},{6,2},{3,7},{7,3},{8,12},{12,8},{9,1... | collective-permute-start | bytes 3145736 | tf_op jit(solution)/shard_map/ppermute | solution.py:38
  73.9 8.5 %collective-permute-start.20 = (bf16[128,512]{1,0:T(8,128)(2,1)S(1)}, bf16[128,512]{1,0:T(8,128)(2,1)S(1)}, u32[]{:S(2)}, u32[]{:S(2)}) collective-permute-start(bf16[128,512]{1,0:T(8,128)(2,1)S(1)} %fusion.48), channel_id=1, source_target_pairs={{0,16},{8,24},{16,0},{24,8},{1,17},{9,25},{17,1},{25,9},{2,18},{10... | collective-permute-start | bytes 393224 | tf_op jit(solution)/shard_map/ppermute | solution.py:38
  82.4 5.0 %collective-permute-start.21 = (bf16[128,512]{1,0:T(8,128)(2,1)S(1)}, bf16[128,512]{1,0:T(8,128)(2,1)S(1)}, u32[]{:S(2)}, u32[]{:S(2)}) collective-permute-start(bf16[128,512]{1,0:T(8,128)(2,1)S(1)} %fusion.50.refs_0_), channel_id=1, source_target_pairs={{0,8},{8,0},{16,24},{24,16},{1,9},{9,1},{17,25},{25,17},{2,10},{10... | collective-permute-start | bytes 393224 | tf_op jit(solution)/shard_map/ppermute | solution.py:38
  93.0 0.9 copy-start.7
  93.9 4.8 %collective-permute-start.31 = (bf16[192,2048]{1,0:T(8,128)(2,1)S(1)}, bf16[192,2048]{1,0:T(8,128)(2,1)S(1)}, u32[]{:S(2)}, u32[]{:S(2)}) collective-permute-start(bf16[192,2048]{1,0:T(8,128)(2,1)S(1)} %get-tuple-element.71), channel_id=1, source_target_pairs={{0,1},{1,0},{2,3},{3,2},{4,5},{5,4},{6,7},{7,6},{8,9},{9,8},{10,11... | collective-permute-start | bytes 2359304 | tf_op jit(solution)/shard_map/ppermute | solution.py:38
  93.9 36.3 %collective-permute-start.24 = (bf16[1024,512]{1,0:T(8,128)(2,1)}, bf16[1024,512]{1,0:T(8,128)(2,1)}, u32[]{:S(2)}, u32[]{:S(2)}) collective-permute-start(bf16[1024,512]{1,0:T(8,128)(2,1)} %bitcast.24.refs_4_), channel_id=1, source_target_pairs={{0,4},{4,0},{1,5},{5,1},{2,6},{6,2},{3,7},{7,3},{8,12},{12,8},{9,1... | collective-permute-start | bytes 3145736 | tf_op jit(solution)/shard_map/ppermute | solution.py:38
  94.9 12.1 %copy-start.18 = (bf16[1024,512]{1,0:T(8,128)(2,1)}, bf16[1024,512]{1,0:T(8,128)(2,1)S(1)}, u32[]{:S(2)}) copy-start(bf16[1024,512]{1,0:T(8,128)(2,1)S(1)} %collective-permute-done.17.refs_3_) | copy-start | bytes 3145732
  94.9 30.4 %collective-permute-start.18 = (bf16[256,512]{1,0:T(8,128)(2,1)S(1)}, bf16[256,512]{1,0:T(8,128)(2,1)S(1)}, u32[]{:S(2)}, u32[]{:S(2)}) collective-permute-start(bf16[256,512]{1,0:T(8,128)(2,1)S(1)} %copy-done.23), channel_id=1, source_target_pairs={{0,4},{4,0},{1,5},{5,1},{2,6},{6,2},{3,7},{7,3},{8,12},{12,8},{9,1... | collective-permute-start | bytes 786440 | tf_op jit(solution)/shard_map/ppermute | solution.py:38
  96.0 29.3 %collective-permute-start.22 = (bf16[2,128,512]{2,1,0:T(8,128)(2,1)S(1)}, bf16[2,128,512]{2,1,0:T(8,128)(2,1)S(1)}, u32[]{:S(2)}, u32[]{:S(2)}) collective-permute-start(bf16[2,128,512]{2,1,0:T(8,128)(2,1)S(1)} %pad_maximum_fusion), channel_id=1, source_target_pairs={{0,16},{8,24},{16,0},{24,8},{1,17},{9,25},{17,1},{25,9},{2,18},{10... | collective-permute-start | bytes 786440 | tf_op jit(solution)/shard_map/ppermute | solution.py:38
  98.7 0.9 copy-start.19
  107.0 18.4 %copy-start.2 = (bf16[128,2048]{1,0:T(8,128)(2,1)S(1)}, bf16[128,2048]{1,0:T(8,128)(2,1)}, u32[]{:S(2)}) copy-start(bf16[128,2048]{1,0:T(8,128)(2,1)} %tokens_ref) | copy-start | bytes 1572868
  107.0 18.4 %copy-start.13 = (f32[2048]{0:T(1024)S(1)}, f32[2048]{0:T(1024)}, u32[]{:S(2)}) copy-start(f32[2048]{0:T(1024)} %param.21) | copy-start | bytes 24580
  107.0 20.4 %copy-start.6 = (bf16[1,512,1024]{2,1,0:T(8,128)(2,1)S(1)}, bf16[1,512,1024]{2,1,0:T(8,128)(2,1)}, u32[]{:S(2)}) copy-start(bf16[1,512,1024]{2,1,0:T(8,128)(2,1)} %param.29) | copy-start | bytes 3145732
  112.8 27.5 %collective-permute-start.32 = (bf16[2,384,512]{2,1,0:T(8,128)(2,1)}, bf16[2,384,512]{2,1,0:T(8,128)(2,1)}, u32[]{:S(2)}, u32[]{:S(2)}) collective-permute-start(bf16[2,384,512]{2,1,0:T(8,128)(2,1)} %get-tuple-element.73), channel_id=1, source_target_pairs={{0,8},{8,0},{16,24},{24,16},{1,9},{9,1},{17,25},{25,17},{2,10},{10... | collective-permute-start | bytes 2359304 | tf_op jit(solution)/shard_map/ppermute | solution.py:38
  125.8 4.4 %copy-start.3 = (bf16[128,2048]{1,0:T(8,128)(2,1)}, bf16[128,2048]{1,0:T(8,128)(2,1)S(1)}, u32[]{:S(2)}) copy-start(bf16[128,2048]{1,0:T(8,128)(2,1)S(1)} %memory.1.refs_0_) | copy-start | bytes 1572868
  125.8 4.4 %collective-permute-start.23 = (bf16[128,2048]{1,0:T(8,128)(2,1)S(1)}, bf16[128,2048]{1,0:T(8,128)(2,1)}, u32[]{:S(2)}, u32[]{:S(2)}) collective-permute-start(bf16[128,2048]{1,0:T(8,128)(2,1)S(1)} %memory.1.refs_0_), channel_id=1, source_target_pairs={{0,1},{1,0},{2,3},{3,2},{4,5},{5,4},{6,7},{7,6},{8,9},{9,8},{10,11... | collective-permute-start | bytes 1572872 | tf_op jit(solution)/shard_map/ppermute | solution.py:38
  125.9 14.4 %collective-permute-start.25 = (bf16[128,2048]{1,0:T(8,128)(2,1)S(1)}, bf16[128,2048]{1,0:T(8,128)(2,1)}, u32[]{:S(2)}, u32[]{:S(2)}) collective-permute-start(bf16[128,2048]{1,0:T(8,128)(2,1)S(1)} %memory.1.refs_0_), channel_id=1, source_target_pairs={{0,2},{1,3},{2,0},{3,1},{4,6},{5,7},{6,4},{7,5},{8,10},{9,11},{10,... | collective-permute-start | bytes 1572872 | tf_op jit(solution)/shard_map/ppermute | solution.py:38
  127.4 25.3 %collective-permute-start.27 = (bf16[512,1024]{1,0:T(8,128)(2,1)S(1)}, bf16[512,1024]{1,0:T(8,128)(2,1)}, u32[]{:S(2)}, u32[]{:S(2)}) collective-permute-start(bf16[512,1024]{1,0:T(8,128)(2,1)S(1)} %bitcast.79), channel_id=1, source_target_pairs={{0,4},{4,0},{1,5},{5,1},{2,6},{6,2},{3,7},{7,3},{8,12},{12,8},{9,1... | collective-permute-start | bytes 3145736 | tf_op jit(solution)/shard_map/ppermute | solution.py:38
  129.0 11.3 %copy-start.20 = (f32[384,512]{1,0:T(8,128)S(1)}, f32[384,512]{1,0:T(8,128)}, u32[]{:S(2)}) copy-start(f32[384,512]{1,0:T(8,128)} %get-tuple-element.72) | copy-start | bytes 2359300
  135.6 17.2 %copy-start.8 = (bf16[128,512]{1,0:T(8,128)(2,1)S(1)}, bf16[128,512]{1,0:T(8,128)(2,1)}, u32[]{:S(2)}) copy-start(bf16[128,512]{1,0:T(8,128)(2,1)} %attend_sentence.2.mine_ref) | copy-start | bytes 393220
  135.6 17.2 %copy-start.14 = (s32[3]{0:T(128)S(1)}, s32[3]{0:T(128)}, u32[]{:S(2)}) copy-start(s32[3]{0:T(128)} %pad_add_fusion.1.place_ref) | copy-start | bytes 40
  140.3 4.4 %collective-permute-start.26 = (bf16[128,2048]{1,0:T(8,128)(2,1)}, bf16[128,2048]{1,0:T(8,128)(2,1)S(1)}, u32[]{:S(2)}, u32[]{:S(2)}) collective-permute-start(bf16[128,2048]{1,0:T(8,128)(2,1)} %collective-permute-done.25.refs_0_), channel_id=1, source_target_pairs={{0,1},{1,0},{2,3},{3,2},{4,5},{5,4},{6,7},{7,6},{8,9},{9,8},{10,11... | collective-permute-start | bytes 1572872 | tf_op jit(solution)/shard_map/ppermute | solution.py:38
  141.5 20.9 %collective-permute-start.33 = (bf16[384,512]{1,0:T(8,128)(2,1)S(1)}, bf16[384,512]{1,0:T(8,128)(2,1)S(1)}, u32[]{:S(2)}, u32[]{:S(2)}) collective-permute-start(bf16[384,512]{1,0:T(8,128)(2,1)S(1)} %fusion.35), channel_id=1, source_target_pairs={{0,16},{8,24},{16,0},{24,8},{1,17},{9,25},{17,1},{25,9},{2,18},{10... | collective-permute-start | bytes 1179656 | tf_op jit(solution)/shard_map/ppermute | solution.py:38
  144.7 0.8 copy-start.22
  145.5 18.5 %copy-start.21 = (f32[384,512]{1,0:T(8,128)S(1)}, f32[384,512]{1,0:T(8,128)}, u32[]{:S(2)}) copy-start(f32[384,512]{1,0:T(8,128)} %get-tuple-element.76) | copy-start | bytes 2359300
  152.8 0.9 copy-start.9
  153.7 15.8 %copy-start.27 = (s32[2]{0:T(128)S(1)}, s32[2]{0:T(128)}, u32[]{:S(2)}) copy-start(s32[2]{0:T(128)} %param.24) | copy-start | bytes 28
  155.7 6.7 %collective-permute-start.34 = (bf16[256,512]{1,0:T(8,128)(2,1)S(1)}, bf16[256,512]{1,0:T(8,128)(2,1)S(1)}, u32[]{:S(2)}, u32[]{:S(2)}) collective-permute-start(bf16[256,512]{1,0:T(8,128)(2,1)S(1)} %get-tuple-element.75), channel_id=1, source_target_pairs={{0,1},{1,0},{2,3},{3,2},{4,5},{5,4},{6,7},{7,6},{8,9},{9,8},{10,11... | collective-permute-start | bytes 786440 | tf_op jit(solution)/shard_map/ppermute | solution.py:38
  155.7 13.9 %collective-permute-start.28 = (bf16[256,512]{1,0:T(8,128)(2,1)S(1)}, bf16[256,512]{1,0:T(8,128)(2,1)S(1)}, u32[]{:S(2)}, u32[]{:S(2)}) collective-permute-start(bf16[256,512]{1,0:T(8,128)(2,1)S(1)} %get-tuple-element.65), channel_id=1, source_target_pairs={{0,1},{1,0},{2,3},{3,2},{4,5},{5,4},{6,7},{7,6},{8,9},{9,8},{10,11... | collective-permute-start | bytes 786440 | tf_op jit(solution)/shard_map/ppermute | solution.py:38
  162.5 8.0 %collective-permute-start.35 = (bf16[256,512]{1,0:T(8,128)(2,1)S(1)}, bf16[256,512]{1,0:T(8,128)(2,1)S(1)}, u32[]{:S(2)}, u32[]{:S(2)}) collective-permute-start(bf16[256,512]{1,0:T(8,128)(2,1)S(1)} %convert_add_fusion.3), channel_id=1, source_target_pairs={{0,2},{1,3},{2,0},{3,1},{4,6},{5,7},{6,4},{7,5},{8,10},{9,11},{10,... | collective-permute-start | bytes 786440 | tf_op jit(solution)/shard_map/ppermute | solution.py:38
  166.0 11.7 %all-to-all-start = ((bf16[8,48,512]{2,1,0:T(8,128)(2,1)}), bf16[8,48,512]{2,1,0:T(8,128)(2,1)S(1)}, u32[]{:S(2)}, u32[]{:S(2)}) async-start(bf16[8,48,512]{2,1,0:T(8,128)(2,1)} %bitcast.31), calls=%async_computation | async-start | bytes 786432 | tf_op jit(solution)/shard_map/all_to_all | solution.py:142
  (1 other events, 0.7 us)

commit v17 on v16

--- a/solution.py
+++ b/solution.py
@@ -654,7 +654,6 @@
         capacity,
     )
     grads_core = swap(grads_sent, "dp", 1)
-    grads_core = swap(grads_sent, "dp", 1)
     slope = expert_slope(
         here.astype(jnp.int32).reshape(1),
         near_codes + core_codes,
@@ -675,7 +674,7 @@
     query_here = jnp.dot(normed_own, query_own, preferred_element_type=jnp.float32)
     query = (query_here + query_back.astype(jnp.float32)).astype(jnp.bfloat16)
 
-    memory = make_memory(which_section, gate(tokens, query_back), slices, final_gain)
+    memory = make_memory(which_section, tokens, slices, final_gain)
     out_other = swap(gate(out_own, memory), "expert", 1)
     memory_x = swap(memory, "dp", 2)
     memory_core = swap(memory, "dp", 1)

time: 179 us -> 176 us (0.983)
  starting transfers between devices: 42.6 us -> 40.4 us
    ppermute x29, starting transfers between devices: 32.3 us -> 30 us  [swap(): return lax.ppermute(value, axis, [(i, i ^ mask) for i in range(size)])]
  transfers between devices with their start and end apart: 37 -> 37, of which waited for: 13 -> 13; matrix products, arithmetic and copies ran while one was open for 15% -> 14% of each run, Pallas kernels for 17% -> 17%
where the time goes in v17:
time: 176 us; the launch traced here: 175 us
  waiting for transfers between devices  65.8 us (37%)
  starting transfers between devices  40.4 us (23%)
  Pallas kernels  33.2 us (19%)
  local copies, waits for them, and re-layouts  16 us (9%)
  other arithmetic  10.2 us (6%)
  matrix products  8.24 us (5%)
    ppermute x29, waiting for transfers between devices, swap(): return lax.ppermute(value, axis, [(i, i ^ mask) for i in range(size)])  52.3 us
    ppermute x29, starting transfers between devices, swap(): return lax.ppermute(value, axis, [(i, i ^ mask) for i in range(size)])  30 us
    unnamed x59, local copies, waits for them, and re-layouts  11 us
    pallas_call x2, Pallas kernels, attend_sentence(): pl.pallas_call(attend_kernel, out_shape=jax.ShapeDtypeStruct(query.shape,...  10.9 us
    ppermute x7, waiting for transfers between devices, send_home(): lax.ppermute(block, ('expert', 'dp'), [(i, i ^ code) for i in range(size)])  9.08 us
    pallas_call x1, Pallas kernels, expert_slope(): pl.pallas_call(functools.partial(slope_kernel, codes), out_shape=jax.Shap...  7.34 us
    ppermute x7, starting transfers between devices, send_home(): lax.ppermute(block, ('expert', 'dp'), [(i, i ^ code) for i in range(size)])  6.88 us
    pallas_call x1, Pallas kernels, expert_backward(): pl.pallas_call(functools.partial(backward_kernel, split), out_shape=(jax....  5.84 us
  transfers between devices with their start and end apart: 37, of which 13 were waited for; matrix products, arithmetic and copies ran while one was open for 14% of the time, Pallas kernels for 17%

profile of v17, /device:TPU:0, one launch (start us, length us, event | category | flops | bytes accessed | tf_op | source)
XLA Modules:
  0.0 174.9 jit_solution(15568183227219132221)
XLA Ops:
  0.6 3.0 %collective-permute-start = (bf16[128,2048]{1,0:T(8,128)(2,1)}, bf16[128,2048]{1,0:T(8,128)(2,1)S(1)}, u32[]{:S(2)}, u32[]{:S(2)}) collective-permute-start(bf16[128,2048]{1,0:T(8,128)(2,1)} %tokens_ref.1), channel_id=1, source_target_pairs={{0,4},{4,0},{1,5},{5,1},{2,6},{6,2},{3,7},{7,3},{8,12},{12,8},{9,1... | collective-permute-start | bytes 1572872 | tf_op jit(solution)/shard_map/ppermute | solution.py:38
  3.7 1.5 collective-permute-start.3
  5.8 1.0 constant_dynamic-slice_fusion.2
  7.5 8.4 %collective-permute-done.4 = s32[2,128]{1,0:T(2,128)S(1)} collective-permute-done((s32[2,128]{1,0:T(2,128)}, s32[2,128]{1,0:T(2,128)S(1)}, u32[]{:S(2)}, u32[]{:S(2)}) %collective-permute-start.4) | collective-permute-done | bytes 1056 | tf_op jit(solution)/shard_map/ppermute | solution.py:38
  15.9 1.7 collective-permute-start.7
  17.7 1.5 collective-permute-start.1
  21.1 1.2 copy-done.4
  23.1 0.8 normed.1
  23.8 0.8 copy-done.15
  24.6 0.8 copy.36
  27.7 1.5 collective-permute-start.2
  29.3 1.6 collective-permute-start.8
  30.9 1.0 copy-done.1
  31.9 1.3 dispatch.2
  33.2 3.2 %fusion.61 = f32[192,1024]{1,0:T(8,128)S(1)} fusion(bf16[192,2048]{1,0:T(8,128)(2,1)S(1)} %get-tuple-element.45, bf16[1,2048,1024]{2,1,0:T(8,128)(2,1)} %param.19), kind=kOutput, calls=%fused_computation.101 | convolution fusion | flops 805306368 | bytes 5767168 | tf_op jit(solution)/shard_map/dot_general | solution.py:610
  36.5 1.1 convolution_convert_fusion.1
  37.6 0.8 fusion.73
  39.7 2.3 %collective-permute-start.13 = (bf16[48,2048]{1,0:T(8,128)(2,1)}, bf16[48,2048]{1,0:T(8,128)(2,1)}, u32[]{:S(2)}, u32[]{:S(2)}) collective-permute-start(bf16[48,2048]{1,0:T(8,128)(2,1)} %get-tuple-element.82), channel_id=1, source_target_pairs={{0,6},{1,7},{2,4},{3,5},{4,2},{5,3},{6,0},{7,1},{8,14},{9,15},{10,... | collective-permute-start | bytes 589832 | tf_op jit(solution)/shard_map/ppermute | solution.py:223
  42.0 4.1 %collective-permute-done.9.refs_1_ = bf16[48,2048]{1,0:T(8,128)(2,1)S(1)} collective-permute-done((bf16[48,2048]{1,0:T(8,128)(2,1)S(1)}, bf16[48,2048]{1,0:T(8,128)(2,1)S(1)}, u32[]{:S(2)}, u32[]{:S(2)}) %collective-permute-start.9) | collective-permute-done | bytes 196640 | tf_op jit(solution)/shard_map/ppermute | solution.py:223
  46.1 1.2 fusion.1
  47.3 1.0 fusion.59
  48.3 1.1 convolution_convert_fusion
  49.4 0.8 fusion.72
  51.1 2.1 %fusion.10 = (f32[192,1024]{1,0:T(8,128)}, f32[192,1024]{1,0:T(8,128)}) fusion(f32[192,1024]{1,0:T(8,128)S(1)} %fusion.61, f32[192,1024]{1,0:T(8,128)S(1)} %fusion.59), kind=kLoop, calls=%fused_computation.20 | loop fusion | flops 6684672 | bytes 3145728 | tf_op jit(solution)/shard_map/transpose(jvp())/add_any | solution.py:616
  53.9 2.5 %collective-permute-start.16 = (bf16[48,2048]{1,0:T(8,128)(2,1)}, bf16[48,2048]{1,0:T(8,128)(2,1)}, u32[]{:S(2)}, u32[]{:S(2)}) collective-permute-start(bf16[48,2048]{1,0:T(8,128)(2,1)} %get-tuple-element.78), channel_id=1, source_target_pairs={{0,7},{1,6},{2,5},{3,4},{4,3},{5,2},{6,1},{7,0},{8,15},{9,14},{10,... | collective-permute-start | bytes 589832 | tf_op jit(solution)/shard_map/ppermute | solution.py:223
  56.4 1.0 constant_dynamic-update-slice_fusion.1
  57.5 5.0 %collective-permute-done.15.refs_6_ = bf16[48,2048]{1,0:T(8,128)(2,1)} collective-permute-done((bf16[48,2048]{1,0:T(8,128)(2,1)}, bf16[48,2048]{1,0:T(8,128)(2,1)}, u32[]{:S(2)}, u32[]{:S(2)}) %collective-permute-start.15) | collective-permute-done | bytes 196640 | tf_op jit(solution)/shard_map/ppermute | solution.py:223
  62.5 0.9 copy-done.11
  63.4 2.0 %combine.2 = (bf16[2,128,512]{2,1,0:T(8,128)(2,1)S(1)}, f32[128,512]{1,0:T(8,128)S(1)}, f32[128,512]{1,0:T(8,128)S(1)}) custom-call(s32[1]{0:T(128)} %bitcast.8.section_ref, s32[128,2]{1,0:T(8,128)S(1)} %get-tuple-element.91.position_ref, f32[128,2]{1,0:T(8,128)S(1)} %copy.39.gates_ref, bf16[48,2048]{1,0:T(8,128)(2,1)S(1)} %get-tuple-element.84.refs_0_, ...), custom_call_target="tpu_custom_call" | custom-call | flops 1 | bytes 1 | tf_op jit(solution)/shard_map/combine/pallas_call | solution.py:264
  65.4 0.8 collective-permute-start.19
  66.3 1.5 collective-permute-start.30
  68.3 0.9 collective-permute-start.17
  69.2 4.6 %collective-permute-done.19 = bf16[2,128,512]{2,1,0:T(8,128)(2,1)S(1)} collective-permute-done((bf16[2,128,512]{2,1,0:T(8,128)(2,1)S(1)}, bf16[2,128,512]{2,1,0:T(8,128)(2,1)S(1)}, u32[]{:S(2)}, u32[]{:S(2)}) %collective-permute-start.19) | collective-permute-done | bytes 262176 | tf_op jit(solution)/shard_map/ppermute | solution.py:38
  73.9 2.7 %collective-permute-start.20 = (bf16[128,512]{1,0:T(8,128)(2,1)S(1)}, bf16[128,512]{1,0:T(8,128)(2,1)S(1)}, u32[]{:S(2)}, u32[]{:S(2)}) collective-permute-start(bf16[128,512]{1,0:T(8,128)(2,1)S(1)} %fusion.48), channel_id=1, source_target_pairs={{0,16},{8,24},{16,0},{24,8},{1,17},{9,25},{17,1},{25,9},{2,18},{10... | collective-permute-start | bytes 393224 | tf_op jit(solution)/shard_map/ppermute | solution.py:38
  76.5 5.9 %collective-permute-done.20 = bf16[128,512]{1,0:T(8,128)(2,1)S(1)} collective-permute-done((bf16[128,512]{1,0:T(8,128)(2,1)S(1)}, bf16[128,512]{1,0:T(8,128)(2,1)S(1)}, u32[]{:S(2)}, u32[]{:S(2)}) %collective-permute-start.20) | collective-permute-done | bytes 131104 | tf_op jit(solution)/shard_map/ppermute | solution.py:38
  83.2 4.3 %collective-permute-done.21.refs_1_ = bf16[128,512]{1,0:T(8,128)(2,1)S(1)} collective-permute-done((bf16[128,512]{1,0:T(8,128)(2,1)S(1)}, bf16[128,512]{1,0:T(8,128)(2,1)S(1)}, u32[]{:S(2)}, u32[]{:S(2)}) %collective-permute-start.21) | collective-permute-done | bytes 131104 | tf_op jit(solution)/shard_map/ppermute | solution.py:38
  87.5 4.0 %collective-permute-done.29.refs_1_ = bf16[128,2048]{1,0:T(8,128)(2,1)S(1)} collective-permute-done((bf16[128,2048]{1,0:T(8,128)(2,1)S(1)}, bf16[128,2048]{1,0:T(8,128)(2,1)S(1)}, u32[]{:S(2)}, u32[]{:S(2)}) %collective-permute-start.29) | collective-permute-done | bytes 524320 | tf_op jit(solution)/shard_map/ppermute | solution.py:38
  91.5 2.4 %dispatch.3 = (bf16[192,2048]{1,0:T(8,128)(2,1)S(1)}, bf16[192,2048]{1,0:T(8,128)(2,1)}) custom-call(s32[1]{0:T(128)} %bitcast.8.section_ref, s32[8,128]{1,0:T(8,128)S(1)} %fusion.code_ref, bf16[128,2048]{1,0:T(8,128)(2,1)S(1)} %copy-done.5, bf16[128,2048]{1,0:T(8,128)(2,1)S(1)} %collective-permute-done.29.refs_1_, ...), custom_call_target="tpu_custom_call" | custom-call | flops 1 | bytes 1 | tf_op jit(solution)/shard_map/dispatch/pallas_call | solution.py:198
  93.9 0.9 copy-done.7
  94.8 2.7 %collective-permute-start.22 = (bf16[2,128,512]{2,1,0:T(8,128)(2,1)S(1)}, bf16[2,128,512]{2,1,0:T(8,128)(2,1)S(1)}, u32[]{:S(2)}, u32[]{:S(2)}) collective-permute-start(bf16[2,128,512]{2,1,0:T(8,128)(2,1)S(1)} %pad_maximum_fusion), channel_id=1, source_target_pairs={{0,16},{8,24},{16,0},{24,8},{1,17},{9,25},{17,1},{25,9},{2,18},{10... | collective-permute-start | bytes 786440 | tf_op jit(solution)/shard_map/ppermute | solution.py:38
  97.5 0.9 collective-permute-start.24
  98.4 1.1 collective-permute-start.18
  100.1 7.3 %expert_slope.1.slope_ref = bf16[384,1024]{1,0:T(8,128)(2,1)} custom-call(s32[1]{0:T(128)} %bitcast.27.here_ref, bf16[192,2048]{1,0:T(8,128)(2,1)} %copy-done.7, bf16[192,2048]{1,0:T(8,128)(2,1)} %collective-permute-done.31.core_ref, f32[192,1024]{1,0:T(8,128)} %get-tuple-element.92.rise_own, f32[192,1024]{1,0:T(8,128)} %get-tuple-element.93.rise_core, ...), custom_call_target="tpu_custom_call" | custom-call | flops 1 | bytes 1 | tf_op jit(solution)/shard_map/expert_slope/pallas_call | solution.py:478
  107.5 5.8 %expert_backward.1 = (bf16[2,384,512]{2,1,0:T(8,128)(2,1)}, f32[384,512]{1,0:T(8,128)}, f32[384,512]{1,0:T(8,128)}) custom-call(s32[1]{0:T(128)} %bitcast.8.section_ref, bf16[384,1024]{1,0:T(8,128)(2,1)} %expert_slope.1.slope_ref, bf16[2048,1024]{1,0:T(8,128)(2,1)} %bitcast.81), custom_call_target="tpu_custom_call" | custom-call | flops 1 | bytes 1 | tf_op jit(solution)/shard_map/expert_backward/pallas_call | solution.py:520
  113.3 0.9 collective-permute-start.32
  114.8 1.6 collective-permute-start.25
  116.4 12.3 %collective-permute-done.18 = bf16[256,512]{1,0:T(8,128)(2,1)} collective-permute-done((bf16[256,512]{1,0:T(8,128)(2,1)}, bf16[256,512]{1,0:T(8,128)(2,1)}, u32[]{:S(2)}, u32[]{:S(2)}) %collective-permute-start.18) | collective-permute-done | bytes 262176 | tf_op jit(solution)/shard_map/ppermute | solution.py:38
  128.7 0.9 collective-permute-start.27
  130.1 1.0 add_convert_fusion
  131.9 0.8 copy-done.22
  133.0 5.4 %attend_sentence.2.mine_ref = bf16[128,512]{1,0:T(8,128)(2,1)} custom-call(s32[3]{0:T(128)} %pad_add_fusion.1.place_ref, s32[2]{0:T(128)} %lengths_ref.3, bf16[128,512]{1,0:T(8,128)(2,1)} %get-tuple-element.87.query_ref, bf16[128,2048]{1,0:T(8,128)(2,1)} %copy-done.3, bf16[128,2048]{1,0:T(8,128)(2,1)} %copy-done.22, bf16[1024,512]{1,0:T(8,128)(2,1)} %bitcast.84, ...), custom_call_target="tpu_custom_call" | custom-call | flops 1 | bytes 1 | tf_op jit(solution)/shard_map/attend_sentence/pallas_call | solution.py:380
  140.4 0.8 copy-done.23
  141.2 5.5 %attend_sentence.3.done_ref = bf16[128,512]{1,0:T(8,128)(2,1)} custom-call(s32[3]{0:T(128)} %pad_add_fusion.3.place_ref, s32[2]{0:T(128)} %lengths_ref.3, bf16[128,512]{1,0:T(8,128)(2,1)} %get-tuple-element.86.query_ref, bf16[128,2048]{1,0:T(8,128)(2,1)} %copy-done.21, bf16[128,2048]{1,0:T(8,128)(2,1)} %copy-done.23, bf16[1024,512]{1,0:T(8,128)(2,1)} %bitcast.85, ...), custom_call_target="tpu_custom_call" | custom-call | flops 1 | bytes 1 | tf_op jit(solution)/shard_map/attend_sentence/pallas_call | solution.py:380
  146.7 6.5 %collective-permute-done.27.other_ref = bf16[512,1024]{1,0:T(8,128)(2,1)S(1)} collective-permute-done((bf16[512,1024]{1,0:T(8,128)(2,1)S(1)}, bf16[512,1024]{1,0:T(8,128)(2,1)S(1)}, u32[]{:S(2)}, u32[]{:S(2)}) %collective-permute-start.27) | collective-permute-done | bytes 1048608 | tf_op jit(solution)/shard_map/ppermute | solution.py:38
  153.2 0.9 copy-done.9
  154.1 1.3 project.1
  156.0 3.6 %collective-permute-done.33 = bf16[384,512]{1,0:T(8,128)(2,1)S(1)} collective-permute-done((bf16[384,512]{1,0:T(8,128)(2,1)S(1)}, bf16[384,512]{1,0:T(8,128)(2,1)S(1)}, u32[]{:S(2)}, u32[]{:S(2)}) %collective-permute-start.33) | collective-permute-done | bytes 393248 | tf_op jit(solution)/shard_map/ppermute | solution.py:38
  159.7 1.6 collective-permute-start.35
  161.2 0.9 fusion.34
  162.2 3.5 %all-to-all-start = ((bf16[8,48,512]{2,1,0:T(8,128)(2,1)}), bf16[8,48,512]{2,1,0:T(8,128)(2,1)S(1)}, u32[]{:S(2)}, u32[]{:S(2)}) async-start(bf16[8,48,512]{2,1,0:T(8,128)(2,1)} %bitcast.31), calls=%async_computation | async-start | bytes 786432 | tf_op jit(solution)/shard_map/all_to_all | solution.py:142
  165.8 1.8 %collective-permute-done.35 = bf16[256,512]{1,0:T(8,128)(2,1)S(1)} collective-permute-done((bf16[256,512]{1,0:T(8,128)(2,1)S(1)}, bf16[256,512]{1,0:T(8,128)(2,1)S(1)}, u32[]{:S(2)}, u32[]{:S(2)}) %collective-permute-start.35) | collective-permute-done | bytes 262176 | tf_op jit(solution)/shard_map/ppermute | solution.py:38
  167.7 1.8 %fusion.47 = bf16[1,256,512]{2,1,0:T(8,128)(2,1)} fusion(bf16[256,512]{1,0:T(8,128)(2,1)S(1)} %collective-permute-done.35, f32[256,512]{1,0:T(8,128)S(1)} %get-tuple-element.62, bf16[256,512]{1,0:T(8,128)(2,1)S(1)} %collective-permute-done.28, bf16[1,256,2048]{2,1,0:T(8,128)(2,1)} %param.22, s32[]{:T(128)S(6)} %select_n.35, ...), kind=kLoop, calls=%fused_computation.62 | loop fusion | flops 1048576 | bytes 1573124 | tf_op jit(solution)/shard_map/broadcast_in_dim | solution.py:713
  169.5 4.4 %all-to-all-done = bf16[8,48,512]{2,1,0:T(8,128)(2,1)S(1)} async-done(((bf16[8,48,512]{2,1,0:T(8,128)(2,1)}), bf16[8,48,512]{2,1,0:T(8,128)(2,1)S(1)}, u32[]{:S(2)}, u32[]{:S(2)}) %all-to-all-start) | async-done | bytes 393248 | tf_op jit(solution)/shard_map/all_to_all | solution.py:142
  173.9 1.0 combine.3
  (114 shorter events, 16.2 us)
Async XLA Ops:
  0.6 45.5 %copy-start = (bf16[1,1024,512]{2,1,0:T(8,128)(2,1)S(1)}, bf16[1,1024,512]{2,1,0:T(8,128)(2,1)}, u32[]{:S(2)}) copy-start(bf16[1,1024,512]{2,1,0:T(8,128)(2,1)} %param.26) | copy-start | bytes 3145732
  0.6 15.2 %collective-permute-start = (bf16[128,2048]{1,0:T(8,128)(2,1)}, bf16[128,2048]{1,0:T(8,128)(2,1)S(1)}, u32[]{:S(2)}, u32[]{:S(2)}) collective-permute-start(bf16[128,2048]{1,0:T(8,128)(2,1)} %tokens_ref.1), channel_id=1, source_target_pairs={{0,4},{4,0},{1,5},{5,1},{2,6},{6,2},{3,7},{7,3},{8,12},{12,8},{9,1... | collective-permute-start | bytes 1572872 | tf_op jit(solution)/shard_map/ppermute | solution.py:38
  3.7 3.8 %collective-permute-start.3 = (s32[2,128]{1,0:T(2,128)}, s32[2,128]{1,0:T(2,128)S(1)}, u32[]{:S(2)}, u32[]{:S(2)}) collective-permute-start(s32[2,128]{1,0:T(2,128)} %bitcast.86), channel_id=1, source_target_pairs={{0,2},{1,3},{2,0},{3,1},{4,6},{5,7},{6,4},{7,5},{8,10},{9,11},{10,... | collective-permute-start | bytes 3080 | tf_op jit(solution)/shard_map/ppermute | solution.py:38
  5.2 10.7 %collective-permute-start.4 = (s32[2,128]{1,0:T(2,128)}, s32[2,128]{1,0:T(2,128)S(1)}, u32[]{:S(2)}, u32[]{:S(2)}) collective-permute-start(s32[2,128]{1,0:T(2,128)} %bitcast.87), channel_id=1, source_target_pairs={{0,4},{4,0},{1,5},{5,1},{2,6},{6,2},{3,7},{7,3},{8,12},{12,8},{9,1... | collective-permute-start | bytes 3080 | tf_op jit(solution)/shard_map/ppermute | solution.py:38
  5.7 25.2 %collective-permute-start.6 = (bf16[128,2048]{1,0:T(8,128)(2,1)}, bf16[128,2048]{1,0:T(8,128)(2,1)S(1)}, u32[]{:S(2)}, u32[]{:S(2)}) collective-permute-start(bf16[128,2048]{1,0:T(8,128)(2,1)} %tokens_ref.1), channel_id=1, source_target_pairs={{0,2},{1,3},{2,0},{3,1},{4,6},{5,7},{6,4},{7,5},{8,10},{9,11},{10,... | collective-permute-start | bytes 1572872 | tf_op jit(solution)/shard_map/ppermute | solution.py:38
  15.9 15.0 %collective-permute-start.7 = (bf16[128,2048]{1,0:T(8,128)(2,1)S(1)}, bf16[128,2048]{1,0:T(8,128)(2,1)S(1)}, u32[]{:S(2)}, u32[]{:S(2)}) collective-permute-start(bf16[128,2048]{1,0:T(8,128)(2,1)S(1)} %collective-permute-done.refs_2_), channel_id=1, source_target_pairs={{0,2},{1,3},{2,0},{3,1},{4,6},{5,7},{6,4},{7,5},{8,10},{9,11},{10,... | collective-permute-start | bytes 1572872 | tf_op jit(solution)/shard_map/ppermute | solution.py:38
  17.7 10.0 %collective-permute-start.1 = (bf16[64,2048]{1,0:T(8,128)(2,1)S(1)}, bf16[64,2048]{1,0:T(8,128)(2,1)}, u32[]{:S(2)}, u32[]{:S(2)}) collective-permute-start(bf16[64,2048]{1,0:T(8,128)(2,1)S(1)} %constant_dynamic-slice_fusion.2), channel_id=1, source_target_pairs={{0,4},{4,0},{1,5},{5,1},{2,6},{6,2},{3,7},{7,3},{8,12},{12,8},{9,1... | collective-permute-start | bytes 786440 | tf_op jit(solution)/shard_map/ppermute | solution.py:38
  19.9 7.0 %collective-permute-start.5 = (s32[2,128]{1,0:T(2,128)S(1)}, s32[2,128]{1,0:T(2,128)S(1)}, u32[]{:S(2)}, u32[]{:S(2)}) collective-permute-start(s32[2,128]{1,0:T(2,128)S(1)} %collective-permute-done.3), channel_id=1, source_target_pairs={{0,4},{4,0},{1,5},{5,1},{2,6},{6,2},{3,7},{7,3},{8,12},{12,8},{9,1... | collective-permute-start | bytes 3080 | tf_op jit(solution)/shard_map/ppermute | solution.py:38
  21.1 1.2 copy-start.4
  22.4 0.7 copy-start.12
  23.8 0.8 copy-start.15
  27.7 18.4 %collective-permute-start.2 = (bf16[256,1024]{1,0:T(8,128)(2,1)}, bf16[256,1024]{1,0:T(8,128)(2,1)S(1)}, u32[]{:S(2)}, u32[]{:S(2)}) collective-permute-start(bf16[256,1024]{1,0:T(8,128)(2,1)} %copy-done.15), channel_id=1, source_target_pairs={{0,4},{4,0},{1,5},{5,1},{2,6},{6,2},{3,7},{7,3},{8,12},{12,8},{9,1... | collective-permute-start | bytes 1572872 | tf_op jit(solution)/shard_map/ppermute | solution.py:38
  29.3 7.1 %collective-permute-start.8 = (bf16[64,2048]{1,0:T(8,128)(2,1)}, bf16[64,2048]{1,0:T(8,128)(2,1)S(1)}, u32[]{:S(2)}, u32[]{:S(2)}) collective-permute-start(bf16[64,2048]{1,0:T(8,128)(2,1)} %collective-permute-done.1), channel_id=1, source_target_pairs={{0,8},{8,0},{16,24},{24,16},{1,9},{9,1},{17,25},{25,17},{2,10},{10... | collective-permute-start | bytes 786440 | tf_op jit(solution)/shard_map/ppermute | solution.py:38
  30.9 1.0 copy-start.1
  31.9 4.6 %copy-start.17 = (bf16[1,1024,2048]{2,1,0:T(8,128)(2,1)S(1)}, bf16[1,1024,2048]{2,1,0:T(8,128)(2,1)}, u32[]{:S(2)}) copy-start(bf16[1,1024,2048]{2,1,0:T(8,128)(2,1)} %param.20) | copy-start | bytes 12582916
  36.4 2.6 %copy-start.24 = (s32[128,2]{1,0:T(8,128)S(1)}, s32[128,2]{1,0:T(8,128)}, u32[]{:S(2)}) copy-start(s32[128,2]{1,0:T(8,128)} %copy.38) | copy-start | bytes 3076
  36.4 2.6 %copy-start.25 = (s32[128,2]{1,0:T(8,128)S(1)}, s32[128,2]{1,0:T(8,128)}, u32[]{:S(2)}) copy-start(s32[128,2]{1,0:T(8,128)} %copy.41) | copy-start | bytes 3076
  36.4 10.9 %copy-start.16 = (bf16[1,2048,1024]{2,1,0:T(8,128)(2,1)S(1)}, bf16[1,2048,1024]{2,1,0:T(8,128)(2,1)}, u32[]{:S(2)}) copy-start(bf16[1,2048,1024]{2,1,0:T(8,128)(2,1)} %param.19) | copy-start | bytes 12582916
  36.4 10.9 %collective-permute-start.10 = (bf16[192,2048]{1,0:T(8,128)(2,1)S(1)}, bf16[192,2048]{1,0:T(8,128)(2,1)S(1)}, u32[]{:S(2)}, u32[]{:S(2)}) collective-permute-start(bf16[192,2048]{1,0:T(8,128)(2,1)S(1)} %get-tuple-element.48), channel_id=1, source_target_pairs={{0,1},{1,0},{2,3},{3,2},{4,5},{5,4},{6,7},{7,6},{8,9},{9,8},{10,11... | collective-permute-start | bytes 2359304 | tf_op jit(solution)/shard_map/ppermute | solution.py:38
  38.4 7.7 %collective-permute-start.9 = (bf16[48,2048]{1,0:T(8,128)(2,1)S(1)}, bf16[48,2048]{1,0:T(8,128)(2,1)S(1)}, u32[]{:S(2)}, u32[]{:S(2)}) collective-permute-start(bf16[48,2048]{1,0:T(8,128)(2,1)S(1)} %get-tuple-element.85), channel_id=1, source_target_pairs={{0,2},{1,3},{2,0},{3,1},{4,6},{5,7},{6,4},{7,5},{8,10},{9,11},{10,... | collective-permute-start | bytes 589832 | tf_op jit(solution)/shard_map/ppermute | solution.py:223
  39.0 18.5 %collective-permute-start.12 = (bf16[48,2048]{1,0:T(8,128)(2,1)}, bf16[48,2048]{1,0:T(8,128)(2,1)S(1)}, u32[]{:S(2)}, u32[]{:S(2)}) collective-permute-start(bf16[48,2048]{1,0:T(8,128)(2,1)} %get-tuple-element.83), channel_id=1, source_target_pairs={{0,4},{1,5},{2,6},{3,7},{4,0},{5,1},{6,2},{7,3},{8,12},{9,13},{10,... | collective-permute-start | bytes 589832 | tf_op jit(solution)/shard_map/ppermute | solution.py:223
  39.7 17.8 %collective-permute-start.13 = (bf16[48,2048]{1,0:T(8,128)(2,1)}, bf16[48,2048]{1,0:T(8,128)(2,1)}, u32[]{:S(2)}, u32[]{:S(2)}) collective-permute-start(bf16[48,2048]{1,0:T(8,128)(2,1)} %get-tuple-element.82), channel_id=1, source_target_pairs={{0,6},{1,7},{2,4},{3,5},{4,2},{5,3},{6,0},{7,1},{8,14},{9,15},{10,... | collective-permute-start | bytes 589832 | tf_op jit(solution)/shard_map/ppermute | solution.py:223
  49.4 7.9 %copy-start.26 = (f32[128,2]{0,1:T(2,128)S(1)}, f32[128,2]{0,1:T(2,128)}, u32[]{:S(2)}) copy-start(f32[128,2]{0,1:T(2,128)} %param.17) | copy-start | bytes 3076
  49.4 18.4 %copy-start.5 = (bf16[128,2048]{1,0:T(8,128)(2,1)S(1)}, bf16[128,2048]{1,0:T(8,128)(2,1)}, u32[]{:S(2)}) copy-start(bf16[128,2048]{1,0:T(8,128)(2,1)} %refs_0_.3) | copy-start | bytes 1572868
  50.3 2.9 %collective-permute-start.11 = (bf16[48,2048]{1,0:T(8,128)(2,1)S(1)}, bf16[48,2048]{1,0:T(8,128)(2,1)S(1)}, u32[]{:S(2)}, u32[]{:S(2)}) collective-permute-start(bf16[48,2048]{1,0:T(8,128)(2,1)S(1)} %get-tuple-element.81), channel_id=1, source_target_pairs={{0,1},{1,0},{2,3},{3,2},{4,5},{5,4},{6,7},{7,6},{8,9},{9,8},{10,11... | collective-permute-start | bytes 589832 | tf_op jit(solution)/shard_map/ppermute | solution.py:223
  50.3 7.2 %collective-permute-start.14 = (bf16[48,2048]{1,0:T(8,128)(2,1)}, bf16[48,2048]{1,0:T(8,128)(2,1)}, u32[]{:S(2)}, u32[]{:S(2)}) collective-permute-start(bf16[48,2048]{1,0:T(8,128)(2,1)} %get-tuple-element.80), channel_id=1, source_target_pairs={{0,3},{1,2},{2,1},{3,0},{4,7},{5,6},{6,5},{7,4},{8,11},{9,10},{10,... | collective-permute-start | bytes 589832 | tf_op jit(solution)/shard_map/ppermute | solution.py:223
  50.9 11.5 %collective-permute-start.15 = (bf16[48,2048]{1,0:T(8,128)(2,1)}, bf16[48,2048]{1,0:T(8,128)(2,1)}, u32[]{:S(2)}, u32[]{:S(2)}) collective-permute-start(bf16[48,2048]{1,0:T(8,128)(2,1)} %get-tuple-element.79), channel_id=1, source_target_pairs={{0,5},{1,4},{2,7},{3,6},{4,1},{5,0},{6,3},{7,2},{8,13},{9,12},{10,... | collective-permute-start | bytes 589832 | tf_op jit(solution)/shard_map/ppermute | solution.py:223
  53.9 8.6 %collective-permute-start.16 = (bf16[48,2048]{1,0:T(8,128)(2,1)}, bf16[48,2048]{1,0:T(8,128)(2,1)}, u32[]{:S(2)}, u32[]{:S(2)}) collective-permute-start(bf16[48,2048]{1,0:T(8,128)(2,1)} %get-tuple-element.78), channel_id=1, source_target_pairs={{0,7},{1,6},{2,5},{3,4},{4,3},{5,2},{6,1},{7,0},{8,15},{9,14},{10,... | collective-permute-start | bytes 589832 | tf_op jit(solution)/shard_map/ppermute | solution.py:223
  62.5 0.9 copy-start.11
  65.4 8.4 %collective-permute-start.19 = (bf16[2,128,512]{2,1,0:T(8,128)(2,1)S(1)}, bf16[2,128,512]{2,1,0:T(8,128)(2,1)S(1)}, u32[]{:S(2)}, u32[]{:S(2)}) collective-permute-start(bf16[2,128,512]{2,1,0:T(8,128)(2,1)S(1)} %get-tuple-element.56), channel_id=1, source_target_pairs={{0,8},{8,0},{16,24},{24,16},{1,9},{9,1},{17,25},{25,17},{2,10},{10... | collective-permute-start | bytes 786440 | tf_op jit(solution)/shard_map/ppermute | solution.py:38
  66.3 21.2 %collective-permute-start.30 = (bf16[128,2048]{1,0:T(8,128)(2,1)S(1)}, bf16[128,2048]{1,0:T(8,128)(2,1)S(1)}, u32[]{:S(2)}, u32[]{:S(2)}) collective-permute-start(bf16[128,2048]{1,0:T(8,128)(2,1)S(1)} %constant_dynamic-update-slice_fusion.refs_2_), channel_id=1, source_target_pairs={{0,2},{1,3},{2,0},{3,1},{4,6},{5,7},{6,4},{7,5},{8,10},{9,11},{10,... | collective-permute-start | bytes 1572872 | tf_op jit(solution)/shard_map/ppermute | solution.py:38
  67.8 23.8 %collective-permute-start.29 = (bf16[128,2048]{1,0:T(8,128)(2,1)S(1)}, bf16[128,2048]{1,0:T(8,128)(2,1)S(1)}, u32[]{:S(2)}, u32[]{:S(2)}) collective-permute-start(bf16[128,2048]{1,0:T(8,128)(2,1)S(1)} %copy-done.5), channel_id=1, source_target_pairs={{0,2},{1,3},{2,0},{3,1},{4,6},{5,7},{6,4},{7,5},{8,10},{9,11},{10,... | collective-permute-start | bytes 1572872 | tf_op jit(solution)/shard_map/ppermute | solution.py:38
  68.3 26.5 %collective-permute-start.17 = (bf16[1024,512]{1,0:T(8,128)(2,1)}, bf16[1024,512]{1,0:T(8,128)(2,1)}, u32[]{:S(2)}, u32[]{:S(2)}) collective-permute-start(bf16[1024,512]{1,0:T(8,128)(2,1)} %bitcast.83), channel_id=1, source_target_pairs={{0,4},{4,0},{1,5},{5,1},{2,6},{6,2},{3,7},{7,3},{8,12},{12,8},{9,1... | collective-permute-start | bytes 3145736 | tf_op jit(solution)/shard_map/ppermute | solution.py:38
  73.9 8.6 %collective-permute-start.20 = (bf16[128,512]{1,0:T(8,128)(2,1)S(1)}, bf16[128,512]{1,0:T(8,128)(2,1)S(1)}, u32[]{:S(2)}, u32[]{:S(2)}) collective-permute-start(bf16[128,512]{1,0:T(8,128)(2,1)S(1)} %fusion.48), channel_id=1, source_target_pairs={{0,16},{8,24},{16,0},{24,8},{1,17},{9,25},{17,1},{25,9},{2,18},{10... | collective-permute-start | bytes 393224 | tf_op jit(solution)/shard_map/ppermute | solution.py:38
  82.5 5.0 %collective-permute-start.21 = (bf16[128,512]{1,0:T(8,128)(2,1)S(1)}, bf16[128,512]{1,0:T(8,128)(2,1)S(1)}, u32[]{:S(2)}, u32[]{:S(2)}) collective-permute-start(bf16[128,512]{1,0:T(8,128)(2,1)S(1)} %fusion.50.refs_0_), channel_id=1, source_target_pairs={{0,8},{8,0},{16,24},{24,16},{1,9},{9,1},{17,25},{25,17},{2,10},{10... | collective-permute-start | bytes 393224 | tf_op jit(solution)/shard_map/ppermute | solution.py:38
  93.9 0.9 copy-start.7
  94.8 5.3 %collective-permute-start.31 = (bf16[192,2048]{1,0:T(8,128)(2,1)}, bf16[192,2048]{1,0:T(8,128)(2,1)}, u32[]{:S(2)}, u32[]{:S(2)}) collective-permute-start(bf16[192,2048]{1,0:T(8,128)(2,1)} %get-tuple-element.69), channel_id=1, source_target_pairs={{0,1},{1,0},{2,3},{3,2},{4,5},{5,4},{6,7},{7,6},{8,9},{9,8},{10,11... | collective-permute-start | bytes 2359304 | tf_op jit(solution)/shard_map/ppermute | solution.py:38
  94.8 19.5 %collective-permute-start.22 = (bf16[2,128,512]{2,1,0:T(8,128)(2,1)S(1)}, bf16[2,128,512]{2,1,0:T(8,128)(2,1)S(1)}, u32[]{:S(2)}, u32[]{:S(2)}) collective-permute-start(bf16[2,128,512]{2,1,0:T(8,128)(2,1)S(1)} %pad_maximum_fusion), channel_id=1, source_target_pairs={{0,16},{8,24},{16,0},{24,8},{1,17},{9,25},{17,1},{25,9},{2,18},{10... | collective-permute-start | bytes 786440 | tf_op jit(solution)/shard_map/ppermute | solution.py:38
  97.5 34.4 %collective-permute-start.24 = (bf16[1024,512]{1,0:T(8,128)(2,1)}, bf16[1024,512]{1,0:T(8,128)(2,1)S(1)}, u32[]{:S(2)}, u32[]{:S(2)}) collective-permute-start(bf16[1024,512]{1,0:T(8,128)(2,1)} %bitcast.24.refs_4_), channel_id=1, source_target_pairs={{0,4},{4,0},{1,5},{5,1},{2,6},{6,2},{3,7},{7,3},{8,12},{12,8},{9,1... | collective-permute-start | bytes 3145736 | tf_op jit(solution)/shard_map/ppermute | solution.py:38
  98.4 30.3 %collective-permute-start.18 = (bf16[256,512]{1,0:T(8,128)(2,1)}, bf16[256,512]{1,0:T(8,128)(2,1)}, u32[]{:S(2)}, u32[]{:S(2)}) collective-permute-start(bf16[256,512]{1,0:T(8,128)(2,1)} %fusion.1), channel_id=1, source_target_pairs={{0,4},{4,0},{1,5},{5,1},{2,6},{6,2},{3,7},{7,3},{8,12},{12,8},{9,1... | collective-permute-start | bytes 786440 | tf_op jit(solution)/shard_map/ppermute | solution.py:38
  107.5 6.9 %copy-start.2 = (bf16[128,2048]{1,0:T(8,128)(2,1)S(1)}, bf16[128,2048]{1,0:T(8,128)(2,1)}, u32[]{:S(2)}) copy-start(bf16[128,2048]{1,0:T(8,128)(2,1)} %tokens_ref.1) | copy-start | bytes 1572868
  107.5 6.9 %copy-start.13 = (f32[2048]{0:T(1024)S(1)}, f32[2048]{0:T(1024)}, u32[]{:S(2)}) copy-start(f32[2048]{0:T(1024)} %param.21) | copy-start | bytes 24580
  107.5 21.2 %copy-start.6 = (bf16[1,512,1024]{2,1,0:T(8,128)(2,1)S(1)}, bf16[1,512,1024]{2,1,0:T(8,128)(2,1)}, u32[]{:S(2)}) copy-start(bf16[1,512,1024]{2,1,0:T(8,128)(2,1)} %param.29) | copy-start | bytes 3145732
  113.3 25.2 %collective-permute-start.32 = (bf16[2,384,512]{2,1,0:T(8,128)(2,1)}, bf16[2,384,512]{2,1,0:T(8,128)(2,1)S(1)}, u32[]{:S(2)}, u32[]{:S(2)}) collective-permute-start(bf16[2,384,512]{2,1,0:T(8,128)(2,1)} %get-tuple-element.71), channel_id=1, source_target_pairs={{0,8},{8,0},{16,24},{24,16},{1,9},{9,1},{17,25},{25,17},{2,10},{10... | collective-permute-start | bytes 2359304 | tf_op jit(solution)/shard_map/ppermute | solution.py:38
  114.8 17.9 %copy-start.3 = (bf16[128,2048]{1,0:T(8,128)(2,1)}, bf16[128,2048]{1,0:T(8,128)(2,1)S(1)}, u32[]{:S(2)}) copy-start(bf16[128,2048]{1,0:T(8,128)(2,1)S(1)} %memory.1.refs_0_) | copy-start | bytes 1572868
  114.8 17.1 %collective-permute-start.23 = (bf16[128,2048]{1,0:T(8,128)(2,1)S(1)}, bf16[128,2048]{1,0:T(8,128)(2,1)S(1)}, u32[]{:S(2)}, u32[]{:S(2)}) collective-permute-start(bf16[128,2048]{1,0:T(8,128)(2,1)S(1)} %memory.1.refs_0_), channel_id=1, source_target_pairs={{0,1},{1,0},{2,3},{3,2},{4,5},{5,4},{6,7},{7,6},{8,9},{9,8},{10,11... | collective-permute-start | bytes 1572872 | tf_op jit(solution)/shard_map/ppermute | solution.py:38
  114.8 23.6 %collective-permute-start.25 = (bf16[128,2048]{1,0:T(8,128)(2,1)S(1)}, bf16[128,2048]{1,0:T(8,128)(2,1)S(1)}, u32[]{:S(2)}, u32[]{:S(2)}) collective-permute-start(bf16[128,2048]{1,0:T(8,128)(2,1)S(1)} %memory.1.refs_0_), channel_id=1, source_target_pairs={{0,2},{1,3},{2,0},{3,1},{4,6},{5,7},{6,4},{7,5},{8,10},{9,11},{10,... | collective-permute-start | bytes 1572872 | tf_op jit(solution)/shard_map/ppermute | solution.py:38
  128.7 24.5 %collective-permute-start.27 = (bf16[512,1024]{1,0:T(8,128)(2,1)S(1)}, bf16[512,1024]{1,0:T(8,128)(2,1)S(1)}, u32[]{:S(2)}, u32[]{:S(2)}) collective-permute-start(bf16[512,1024]{1,0:T(8,128)(2,1)S(1)} %bitcast.77), channel_id=1, source_target_pairs={{0,4},{4,0},{1,5},{5,1},{2,6},{6,2},{3,7},{7,3},{8,12},{12,8},{9,1... | collective-permute-start | bytes 3145736 | tf_op jit(solution)/shard_map/ppermute | solution.py:38
  129.7 8.9 %copy-start.19 = (f32[384,512]{1,0:T(8,128)S(1)}, f32[384,512]{1,0:T(8,128)}, u32[]{:S(2)}) copy-start(f32[384,512]{1,0:T(8,128)} %get-tuple-element.70) | copy-start | bytes 2359300
  131.9 1.1 copy-start.18
  131.9 0.8 copy-start.22
  138.4 14.8 %copy-start.8 = (bf16[128,512]{1,0:T(8,128)(2,1)S(1)}, bf16[128,512]{1,0:T(8,128)(2,1)}, u32[]{:S(2)}) copy-start(bf16[128,512]{1,0:T(8,128)(2,1)} %attend_sentence.2.mine_ref) | copy-start | bytes 393220
  138.4 14.8 %copy-start.14 = (s32[3]{0:T(128)S(1)}, s32[3]{0:T(128)}, u32[]{:S(2)}) copy-start(s32[3]{0:T(128)} %pad_add_fusion.1.place_ref) | copy-start | bytes 40
  138.5 2.0 %copy-start.21 = (bf16[128,2048]{1,0:T(8,128)(2,1)}, bf16[128,2048]{1,0:T(8,128)(2,1)S(1)}, u32[]{:S(2)}) copy-start(bf16[128,2048]{1,0:T(8,128)(2,1)S(1)} %collective-permute-done.25.refs_0_) | copy-start | bytes 1572868
  138.5 2.0 %collective-permute-start.26 = (bf16[128,2048]{1,0:T(8,128)(2,1)S(1)}, bf16[128,2048]{1,0:T(8,128)(2,1)S(1)}, u32[]{:S(2)}, u32[]{:S(2)}) collective-permute-start(bf16[128,2048]{1,0:T(8,128)(2,1)S(1)} %collective-permute-done.25.refs_0_), channel_id=1, source_target_pairs={{0,1},{1,0},{2,3},{3,2},{4,5},{5,4},{6,7},{7,6},{8,9},{9,8},{10,11... | collective-permute-start | bytes 1572872 | tf_op jit(solution)/shard_map/ppermute | solution.py:38
  138.7 20.9 %collective-permute-start.33 = (bf16[384,512]{1,0:T(8,128)(2,1)S(1)}, bf16[384,512]{1,0:T(8,128)(2,1)S(1)}, u32[]{:S(2)}, u32[]{:S(2)}) collective-permute-start(bf16[384,512]{1,0:T(8,128)(2,1)S(1)} %fusion.35), channel_id=1, source_target_pairs={{0,16},{8,24},{16,0},{24,8},{1,17},{9,25},{17,1},{25,9},{2,18},{10... | collective-permute-start | bytes 1179656 | tf_op jit(solution)/shard_map/ppermute | solution.py:38
  140.4 0.8 copy-start.23
  141.2 20.0 %copy-start.20 = (f32[384,512]{1,0:T(8,128)S(1)}, f32[384,512]{1,0:T(8,128)}, u32[]{:S(2)}) copy-start(f32[384,512]{1,0:T(8,128)} %get-tuple-element.74) | copy-start | bytes 2359300
  153.2 0.9 copy-start.9
  154.1 11.5 %copy-start.27 = (s32[2]{0:T(128)S(1)}, s32[2]{0:T(128)}, u32[]{:S(2)}) copy-start(s32[2]{0:T(128)} %param.24) | copy-start | bytes 28
  155.4 4.2 %collective-permute-start.34 = (bf16[256,512]{1,0:T(8,128)(2,1)S(1)}, bf16[256,512]{1,0:T(8,128)(2,1)S(1)}, u32[]{:S(2)}, u32[]{:S(2)}) collective-permute-start(bf16[256,512]{1,0:T(8,128)(2,1)S(1)} %get-tuple-element.73), channel_id=1, source_target_pairs={{0,1},{1,0},{2,3},{3,2},{4,5},{5,4},{6,7},{7,6},{8,9},{9,8},{10,11... | collective-permute-start | bytes 786440 | tf_op jit(solution)/shard_map/ppermute | solution.py:38
  155.5 10.4 %collective-permute-start.28 = (bf16[256,512]{1,0:T(8,128)(2,1)S(1)}, bf16[256,512]{1,0:T(8,128)(2,1)S(1)}, u32[]{:S(2)}, u32[]{:S(2)}) collective-permute-start(bf16[256,512]{1,0:T(8,128)(2,1)S(1)} %get-tuple-element.63), channel_id=1, source_target_pairs={{0,1},{1,0},{2,3},{3,2},{4,5},{5,4},{6,7},{7,6},{8,9},{9,8},{10,11... | collective-permute-start | bytes 786440 | tf_op jit(solution)/shard_map/ppermute | solution.py:38
  159.7 8.0 %collective-permute-start.35 = (bf16[256,512]{1,0:T(8,128)(2,1)S(1)}, bf16[256,512]{1,0:T(8,128)(2,1)S(1)}, u32[]{:S(2)}, u32[]{:S(2)}) collective-permute-start(bf16[256,512]{1,0:T(8,128)(2,1)S(1)} %convert_add_fusion.3), channel_id=1, source_target_pairs={{0,2},{1,3},{2,0},{3,1},{4,6},{5,7},{6,4},{7,5},{8,10},{9,11},{10,... | collective-permute-start | bytes 786440 | tf_op jit(solution)/shard_map/ppermute | solution.py:38
  162.2 11.7 %all-to-all-start = ((bf16[8,48,512]{2,1,0:T(8,128)(2,1)}), bf16[8,48,512]{2,1,0:T(8,128)(2,1)S(1)}, u32[]{:S(2)}, u32[]{:S(2)}) async-start(bf16[8,48,512]{2,1,0:T(8,128)(2,1)} %bitcast.31), calls=%async_computation | async-start | bytes 786432 | tf_op jit(solution)/shard_map/all_to_all | solution.py:142
  (1 other events, 0.7 us)

commit v18 on v17

--- a/solution.py
+++ b/solution.py
@@ -632,14 +632,14 @@
     held_gates = gate(gate_weights, rise_own, rise_core, query_there, grad_y)
     sent_pair, first, second = combine(which_section, position, held_gates, home, sections)
     from_pair = swap(sent_pair, "section", 1)
+    query_back = swap(gate(query_there.astype(jnp.bfloat16), home[5], home[6]), "expert", 1)
     grad_x = swap(gate(out_grad, home[5]), "dp", 2)
     grad_far = swap(gate(grad_y, first), "dp", 2)
     to_other = (second + from_pair[1].astype(jnp.float32)).astype(jnp.bfloat16)
     from_other = swap(to_other, "section", 2)
-    mixed_sum = first + from_pair[0].astype(jnp.float32)
+    mixed_sum = gate(first, query_back) + from_pair[0].astype(jnp.float32)
     mixed_slice = (mixed_sum + from_other.astype(jnp.float32)).astype(jnp.bfloat16)
     key_other = swap(gate(key_own, first), "expert", 1)
-    query_back = swap(gate(query_there.astype(jnp.bfloat16), key_other), "expert", 1)
     mixed_near = swap(mixed_slice, "section", 1)
     grads_own, grads_sent = dispatch(
         which_section,

time: 176 us -> 171 us (0.972)
  waiting for transfers between devices: 65.8 us -> 62.7 us
  starting transfers between devices: 40.4 us -> 37.8 us
    ppermute x29, waiting for transfers between devices: 52.3 us -> 49.3 us  [swap(): return lax.ppermute(value, axis, [(i, i ^ mask) for i in range(size)])]
    ppermute x29, starting transfers between devices: 30 us -> 27.5 us  [swap(): return lax.ppermute(value, axis, [(i, i ^ mask) for i in range(size)])]
    unnamed x59 -> x57, local copies, waits for them, and re-layouts: 11 us -> 10.8 us
  transfers between devices with their start and end apart: 37 -> 37, of which waited for: 13 -> 16; matrix products, arithmetic and copies ran while one was open for 14% -> 15% of each run, Pallas kernels for 17% -> 18%
where the time goes in v18:
time: 171 us; the launch traced here: 170 us
  waiting for transfers between devices  62.7 us (37%)
  starting transfers between devices  37.8 us (22%)
  Pallas kernels  33 us (19%)
  local copies, waits for them, and re-layouts  15.8 us (9%)
  other arithmetic  11.2 us (7%)
  matrix products  8.24 us (5%)
    ppermute x29, waiting for transfers between devices, swap(): return lax.ppermute(value, axis, [(i, i ^ mask) for i in range(size)])  49.3 us
    ppermute x29, starting transfers between devices, swap(): return lax.ppermute(value, axis, [(i, i ^ mask) for i in range(size)])  27.5 us
    pallas_call x2, Pallas kernels, attend_sentence(): pl.pallas_call(attend_kernel, out_shape=jax.ShapeDtypeStruct(query.shape,...  10.9 us
    unnamed x57, local copies, waits for them, and re-layouts  10.8 us
    ppermute x7, waiting for transfers between devices, send_home(): lax.ppermute(block, ('expert', 'dp'), [(i, i ^ code) for i in range(size)])  9.08 us
    pallas_call x1, Pallas kernels, expert_slope(): pl.pallas_call(functools.partial(slope_kernel, codes), out_shape=jax.Shap...  7.34 us
    ppermute x7, starting transfers between devices, send_home(): lax.ppermute(block, ('expert', 'dp'), [(i, i ^ code) for i in range(size)])  6.88 us
    pallas_call x1, Pallas kernels, expert_backward(): pl.pallas_call(functools.partial(backward_kernel, split), out_shape=(jax....  5.85 us
  transfers between devices with their start and end apart: 37, of which 16 were waited for; matrix products, arithmetic and copies ran while one was open for 15% of the time, Pallas kernels for 18%

profile of v18, /device:TPU:0, one launch (start us, length us, event | category | flops | bytes accessed | tf_op | source)
XLA Modules:
  0.0 169.8 jit_solution(12527601517624301358)
XLA Ops:
  0.6 3.0 %collective-permute-start = (bf16[128,2048]{1,0:T(8,128)(2,1)}, bf16[128,2048]{1,0:T(8,128)(2,1)S(1)}, u32[]{:S(2)}, u32[]{:S(2)}) collective-permute-start(bf16[128,2048]{1,0:T(8,128)(2,1)} %tokens_ref.1), channel_id=1, source_target_pairs={{0,4},{4,0},{1,5},{5,1},{2,6},{6,2},{3,7},{7,3},{8,12},{12,8},{9,1... | collective-permute-start | bytes 1572872 | tf_op jit(solution)/shard_map/ppermute | solution.py:38
  3.7 1.5 collective-permute-start.3
  5.8 1.0 constant_dynamic-slice_fusion.2
  7.5 8.4 %collective-permute-done.4 = s32[2,128]{1,0:T(2,128)S(1)} collective-permute-done((s32[2,128]{1,0:T(2,128)}, s32[2,128]{1,0:T(2,128)S(1)}, u32[]{:S(2)}, u32[]{:S(2)}) %collective-permute-start.4) | collective-permute-done | bytes 1056 | tf_op jit(solution)/shard_map/ppermute | solution.py:38
  15.9 1.7 %collective-permute-start.7 = (bf16[128,2048]{1,0:T(8,128)(2,1)S(1)}, bf16[128,2048]{1,0:T(8,128)(2,1)S(1)}, u32[]{:S(2)}, u32[]{:S(2)}) collective-permute-start(bf16[128,2048]{1,0:T(8,128)(2,1)S(1)} %collective-permute-done.refs_2_), channel_id=1, source_target_pairs={{0,2},{1,3},{2,0},{3,1},{4,6},{5,7},{6,4},{7,5},{8,10},{9,11},{10,... | collective-permute-start | bytes 1572872 | tf_op jit(solution)/shard_map/ppermute | solution.py:38
  17.7 1.5 collective-permute-start.1
  21.1 1.2 copy-done.4
  23.1 0.8 normed.1
  23.8 0.8 copy-done.15
  24.6 0.8 copy.36
  27.7 1.5 collective-permute-start.2
  29.3 1.6 collective-permute-start.9
  30.9 1.0 copy-done.1
  31.9 1.3 dispatch.2
  33.2 3.2 %fusion.61 = f32[192,1024]{1,0:T(8,128)S(1)} fusion(bf16[192,2048]{1,0:T(8,128)(2,1)S(1)} %get-tuple-element.47, bf16[1,2048,1024]{2,1,0:T(8,128)(2,1)} %param.19), kind=kOutput, calls=%fused_computation.101 | convolution fusion | flops 805306368 | bytes 5767168 | tf_op jit(solution)/shard_map/dot_general | solution.py:610
  36.5 1.1 convolution_convert_fusion.1
  37.6 0.8 fusion.73
  39.7 2.3 %collective-permute-start.16 = (bf16[48,2048]{1,0:T(8,128)(2,1)}, bf16[48,2048]{1,0:T(8,128)(2,1)}, u32[]{:S(2)}, u32[]{:S(2)}) collective-permute-start(bf16[48,2048]{1,0:T(8,128)(2,1)} %get-tuple-element.84), channel_id=1, source_target_pairs={{0,6},{1,7},{2,4},{3,5},{4,2},{5,3},{6,0},{7,1},{8,14},{9,15},{10,... | collective-permute-start | bytes 589832 | tf_op jit(solution)/shard_map/ppermute | solution.py:223
  42.0 4.1 %collective-permute-done.13.refs_1_ = bf16[48,2048]{1,0:T(8,128)(2,1)S(1)} collective-permute-done((bf16[48,2048]{1,0:T(8,128)(2,1)S(1)}, bf16[48,2048]{1,0:T(8,128)(2,1)S(1)}, u32[]{:S(2)}, u32[]{:S(2)}) %collective-permute-start.13) | collective-permute-done | bytes 196640 | tf_op jit(solution)/shard_map/ppermute | solution.py:223
  46.1 1.2 fusion.1
  47.3 1.0 fusion.59
  48.3 1.1 convolution_convert_fusion
  49.4 0.8 fusion.72
  51.1 2.1 %fusion.10 = (f32[192,1024]{1,0:T(8,128)}, f32[192,1024]{1,0:T(8,128)}) fusion(f32[192,1024]{1,0:T(8,128)S(1)} %fusion.61, f32[192,1024]{1,0:T(8,128)S(1)} %fusion.59), kind=kLoop, calls=%fused_computation.20 | loop fusion | flops 6684672 | bytes 3145728 | tf_op jit(solution)/shard_map/transpose(jvp())/add_any | solution.py:616
  53.9 2.5 %collective-permute-start.17 = (bf16[48,2048]{1,0:T(8,128)(2,1)}, bf16[48,2048]{1,0:T(8,128)(2,1)}, u32[]{:S(2)}, u32[]{:S(2)}) collective-permute-start(bf16[48,2048]{1,0:T(8,128)(2,1)} %get-tuple-element.80), channel_id=1, source_target_pairs={{0,7},{1,6},{2,5},{3,4},{4,3},{5,2},{6,1},{7,0},{8,15},{9,14},{10,... | collective-permute-start | bytes 589832 | tf_op jit(solution)/shard_map/ppermute | solution.py:223
  56.4 1.0 constant_dynamic-update-slice_fusion.1
  57.5 5.0 %collective-permute-done.11.refs_6_ = bf16[48,2048]{1,0:T(8,128)(2,1)} collective-permute-done((bf16[48,2048]{1,0:T(8,128)(2,1)}, bf16[48,2048]{1,0:T(8,128)(2,1)}, u32[]{:S(2)}, u32[]{:S(2)}) %collective-permute-start.11) | collective-permute-done | bytes 196640 | tf_op jit(solution)/shard_map/ppermute | solution.py:223
  62.5 0.9 copy-done.11
  63.4 2.1 %combine.2 = (bf16[2,128,512]{2,1,0:T(8,128)(2,1)S(1)}, f32[128,512]{1,0:T(8,128)S(1)}, f32[128,512]{1,0:T(8,128)S(1)}) custom-call(s32[1]{0:T(128)} %bitcast.7.section_ref, s32[128,2]{1,0:T(8,128)S(1)} %get-tuple-element.93.position_ref, f32[128,2]{1,0:T(8,128)S(1)} %copy.39.gates_ref, bf16[48,2048]{1,0:T(8,128)(2,1)S(1)} %get-tuple-element.86.refs_0_, ...), custom_call_target="tpu_custom_call" | custom-call | flops 1 | bytes 1 | tf_op jit(solution)/shard_map/combine/pallas_call | solution.py:264
  65.4 0.8 collective-permute-start.18
  66.3 1.5 collective-permute-start.30
  67.8 0.9 collective-permute-start.12
  69.2 1.1 collective-permute-start.21
  70.3 3.5 %collective-permute-done.18 = bf16[2,128,512]{2,1,0:T(8,128)(2,1)S(1)} collective-permute-done((bf16[2,128,512]{2,1,0:T(8,128)(2,1)S(1)}, bf16[2,128,512]{2,1,0:T(8,128)(2,1)S(1)}, u32[]{:S(2)}, u32[]{:S(2)}) %collective-permute-start.18) | collective-permute-done | bytes 262176 | tf_op jit(solution)/shard_map/ppermute | solution.py:38
  73.9 2.6 %collective-permute-start.19 = (bf16[128,512]{1,0:T(8,128)(2,1)S(1)}, bf16[128,512]{1,0:T(8,128)(2,1)S(1)}, u32[]{:S(2)}, u32[]{:S(2)}) collective-permute-start(bf16[128,512]{1,0:T(8,128)(2,1)S(1)} %fusion.48), channel_id=1, source_target_pairs={{0,16},{8,24},{16,0},{24,8},{1,17},{9,25},{17,1},{25,9},{2,18},{10... | collective-permute-start | bytes 393224 | tf_op jit(solution)/shard_map/ppermute | solution.py:38
  77.2 5.1 %collective-permute-done.19 = bf16[128,512]{1,0:T(8,128)(2,1)S(1)} collective-permute-done((bf16[128,512]{1,0:T(8,128)(2,1)S(1)}, bf16[128,512]{1,0:T(8,128)(2,1)S(1)}, u32[]{:S(2)}, u32[]{:S(2)}) %collective-permute-start.19) | collective-permute-done | bytes 131104 | tf_op jit(solution)/shard_map/ppermute | solution.py:38
  83.1 4.3 %collective-permute-done.20.refs_1_ = bf16[128,512]{1,0:T(8,128)(2,1)S(1)} collective-permute-done((bf16[128,512]{1,0:T(8,128)(2,1)S(1)}, bf16[128,512]{1,0:T(8,128)(2,1)S(1)}, u32[]{:S(2)}, u32[]{:S(2)}) %collective-permute-start.20) | collective-permute-done | bytes 131104 | tf_op jit(solution)/shard_map/ppermute | solution.py:38
  87.4 4.1 %collective-permute-done.29.refs_1_ = bf16[128,2048]{1,0:T(8,128)(2,1)S(1)} collective-permute-done((bf16[128,2048]{1,0:T(8,128)(2,1)S(1)}, bf16[128,2048]{1,0:T(8,128)(2,1)S(1)}, u32[]{:S(2)}, u32[]{:S(2)}) %collective-permute-start.29) | collective-permute-done | bytes 524320 | tf_op jit(solution)/shard_map/ppermute | solution.py:38
  91.5 1.4 dispatch.3
  93.0 0.9 copy-done.7
  93.9 0.9 collective-permute-start.24
  94.8 4.8 %collective-permute-done.21.refs_3_ = bf16[1024,512]{1,0:T(8,128)(2,1)S(1)} collective-permute-done((bf16[1024,512]{1,0:T(8,128)(2,1)}, bf16[1024,512]{1,0:T(8,128)(2,1)S(1)}, u32[]{:S(2)}, u32[]{:S(2)}) %collective-permute-start.21) | collective-permute-done | bytes 1048608 | tf_op jit(solution)/shard_map/ppermute | solution.py:38
  99.7 2.7 %collective-permute-start.22 = (bf16[2,128,512]{2,1,0:T(8,128)(2,1)S(1)}, bf16[2,128,512]{2,1,0:T(8,128)(2,1)S(1)}, u32[]{:S(2)}, u32[]{:S(2)}) collective-permute-start(bf16[2,128,512]{2,1,0:T(8,128)(2,1)S(1)} %pad_maximum_fusion), channel_id=1, source_target_pairs={{0,16},{8,24},{16,0},{24,8},{1,17},{9,25},{17,1},{25,9},{2,18},{10... | collective-permute-start | bytes 786440 | tf_op jit(solution)/shard_map/ppermute | solution.py:38
  102.3 0.9 copy-done.19
  103.2 7.3 %expert_slope.1.slope_ref = bf16[384,1024]{1,0:T(8,128)(2,1)} custom-call(s32[1]{0:T(128)} %bitcast.27.here_ref, bf16[192,2048]{1,0:T(8,128)(2,1)} %copy-done.7, bf16[192,2048]{1,0:T(8,128)(2,1)} %copy-done.19, f32[192,1024]{1,0:T(8,128)} %get-tuple-element.94.rise_own, f32[192,1024]{1,0:T(8,128)} %get-tuple-element.95.rise_core, bf16[1024,2048]{1,0:T(8,128)(2,1)} %bitcast.84), custom_call_target="tpu_custom_call" | custom-call | flops 1 | bytes 1 | tf_op jit(solution)/shard_map/expert_slope/pallas_call | solution.py:478
  110.6 5.8 %expert_backward.1 = (bf16[2,384,512]{2,1,0:T(8,128)(2,1)}, f32[384,512]{1,0:T(8,128)}, f32[384,512]{1,0:T(8,128)}) custom-call(s32[1]{0:T(128)} %bitcast.7.section_ref, bf16[384,1024]{1,0:T(8,128)(2,1)} %expert_slope.1.slope_ref, bf16[2048,1024]{1,0:T(8,128)(2,1)} %bitcast.83), custom_call_target="tpu_custom_call" | custom-call | flops 1 | bytes 1 | tf_op jit(solution)/shard_map/expert_backward/pallas_call | solution.py:520
  116.5 1.2 collective-permute-start.32
  118.3 0.8 collective-permute-start.27
  121.2 5.4 %attend_sentence.2.mine_ref = bf16[128,512]{1,0:T(8,128)(2,1)} custom-call(s32[3]{0:T(128)} %pad_add_fusion.1.place_ref, s32[2]{0:T(128)} %lengths_ref.3, bf16[128,512]{1,0:T(8,128)(2,1)} %get-tuple-element.89.query_ref, bf16[128,2048]{1,0:T(8,128)(2,1)} %copy-done.3, bf16[128,2048]{1,0:T(8,128)(2,1)} %collective-permute-done.23.refs_1_, ...), custom_call_target="tpu_custom_call" | custom-call | flops 1 | bytes 1 | tf_op jit(solution)/shard_map/attend_sentence/pallas_call | solution.py:380
  126.6 6.1 %collective-permute-done.25.refs_0_ = bf16[128,2048]{1,0:T(8,128)(2,1)} collective-permute-done((bf16[128,2048]{1,0:T(8,128)(2,1)S(1)}, bf16[128,2048]{1,0:T(8,128)(2,1)}, u32[]{:S(2)}, u32[]{:S(2)}) %collective-permute-start.25) | collective-permute-done | bytes 524320 | tf_op jit(solution)/shard_map/ppermute | solution.py:38
  132.7 1.3 collective-permute-done.32
  134.0 1.1 fusion.35
  136.3 0.8 copy-done.22
  137.1 5.5 %attend_sentence.3.done_ref = bf16[128,512]{1,0:T(8,128)(2,1)} custom-call(s32[3]{0:T(128)} %pad_add_fusion.3.place_ref, s32[2]{0:T(128)} %lengths_ref.3, bf16[128,512]{1,0:T(8,128)(2,1)} %get-tuple-element.88.query_ref, bf16[128,2048]{1,0:T(8,128)(2,1)} %collective-permute-done.25.refs_0_, bf16[128,2048]{1,0:T(8,128)(2,1)} %copy-done.22, ...), custom_call_target="tpu_custom_call" | custom-call | flops 1 | bytes 1 | tf_op jit(solution)/shard_map/attend_sentence/pallas_call | solution.py:380
  142.6 1.3 collective-permute-done.27.other_ref
  143.9 0.9 copy-done.9
  144.8 2.0 %project.1 = (bf16[256,512]{1,0:T(8,128)(2,1)S(1)}, bf16[256,512]{1,0:T(8,128)(2,1)S(1)}, f32[256,512]{1,0:T(8,128)S(1)}, f32[256,512]{1,0:T(8,128)S(1)}) custom-call(s32[3]{0:T(128)S(1)} %copy-done.14, bf16[128,512]{1,0:T(8,128)(2,1)S(1)} %copy-done.8, bf16[128,512]{1,0:T(8,128)(2,1)S(1)} %copy-done.9, bf16[512,1024]{1,0:T(8,128)(2,1)S(1)} %bitcast.80, ...), custom_call_target="tpu_custom_call" | custom-call | flops 1 | bytes 1 | tf_op jit(solution)/shard_map/project/pallas_call | solution.py:431
  147.4 7.4 %collective-permute-done.33 = bf16[384,512]{1,0:T(8,128)(2,1)S(1)} collective-permute-done((bf16[384,512]{1,0:T(8,128)(2,1)S(1)}, bf16[384,512]{1,0:T(8,128)(2,1)S(1)}, u32[]{:S(2)}, u32[]{:S(2)}) %collective-permute-start.33) | collective-permute-done | bytes 393248 | tf_op jit(solution)/shard_map/ppermute | solution.py:38
  155.2 1.9 %fusion.34 = bf16[384,512]{1,0:T(8,128)(2,1)} fusion(f32[384,512]{1,0:T(8,128)S(1)} %copy-done.21, bf16[384,512]{1,0:T(8,128)(2,1)S(1)} %collective-permute-done.33, bf16[2,384,512]{2,1,0:T(8,128)(2,1)} %collective-permute-done.32), kind=kLoop, calls=%fused_computation.45 | loop fusion | flops 983040 | bytes 1966080 | tf_op jit(solution)/shard_map/convert_element_type | solution.py:708
  157.1 3.5 %all-to-all-start = ((bf16[8,48,512]{2,1,0:T(8,128)(2,1)}), bf16[8,48,512]{2,1,0:T(8,128)(2,1)S(1)}, u32[]{:S(2)}, u32[]{:S(2)}) async-start(bf16[8,48,512]{2,1,0:T(8,128)(2,1)} %bitcast.31), calls=%async_computation | async-start | bytes 786432 | tf_op jit(solution)/shard_map/all_to_all | solution.py:142
  160.8 2.0 %collective-permute-done.35 = bf16[256,512]{1,0:T(8,128)(2,1)S(1)} collective-permute-done((bf16[256,512]{1,0:T(8,128)(2,1)S(1)}, bf16[256,512]{1,0:T(8,128)(2,1)S(1)}, u32[]{:S(2)}, u32[]{:S(2)}) %collective-permute-start.35) | collective-permute-done | bytes 262176 | tf_op jit(solution)/shard_map/ppermute | solution.py:38
  162.7 1.8 %fusion.47 = bf16[1,256,512]{2,1,0:T(8,128)(2,1)} fusion(bf16[256,512]{1,0:T(8,128)(2,1)S(1)} %collective-permute-done.35, f32[256,512]{1,0:T(8,128)S(1)} %get-tuple-element.64, bf16[256,512]{1,0:T(8,128)(2,1)S(1)} %collective-permute-done.28, bf16[1,256,2048]{2,1,0:T(8,128)(2,1)} %param.22, s32[]{:T(128)S(6)} %select_n.35, ...), kind=kLoop, calls=%fused_computation.62 | loop fusion | flops 1048576 | bytes 1573124 | tf_op jit(solution)/shard_map/broadcast_in_dim | solution.py:713
  164.5 4.3 %all-to-all-done = bf16[8,48,512]{2,1,0:T(8,128)(2,1)S(1)} async-done(((bf16[8,48,512]{2,1,0:T(8,128)(2,1)}), bf16[8,48,512]{2,1,0:T(8,128)(2,1)S(1)}, u32[]{:S(2)}, u32[]{:S(2)}) %all-to-all-start) | async-done | bytes 393248 | tf_op jit(solution)/shard_map/all_to_all | solution.py:142
  168.8 1.0 combine.3
  (111 shorter events, 16.5 us)
Async XLA Ops:
  0.6 45.5 %copy-start = (bf16[1,1024,512]{2,1,0:T(8,128)(2,1)S(1)}, bf16[1,1024,512]{2,1,0:T(8,128)(2,1)}, u32[]{:S(2)}) copy-start(bf16[1,1024,512]{2,1,0:T(8,128)(2,1)} %param.26) | copy-start | bytes 3145732
  0.6 15.2 %collective-permute-start = (bf16[128,2048]{1,0:T(8,128)(2,1)}, bf16[128,2048]{1,0:T(8,128)(2,1)S(1)}, u32[]{:S(2)}, u32[]{:S(2)}) collective-permute-start(bf16[128,2048]{1,0:T(8,128)(2,1)} %tokens_ref.1), channel_id=1, source_target_pairs={{0,4},{4,0},{1,5},{5,1},{2,6},{6,2},{3,7},{7,3},{8,12},{12,8},{9,1... | collective-permute-start | bytes 1572872 | tf_op jit(solution)/shard_map/ppermute | solution.py:38
  3.7 3.8 %collective-permute-start.3 = (s32[2,128]{1,0:T(2,128)}, s32[2,128]{1,0:T(2,128)S(1)}, u32[]{:S(2)}, u32[]{:S(2)}) collective-permute-start(s32[2,128]{1,0:T(2,128)} %bitcast.88), channel_id=1, source_target_pairs={{0,2},{1,3},{2,0},{3,1},{4,6},{5,7},{6,4},{7,5},{8,10},{9,11},{10,... | collective-permute-start | bytes 3080 | tf_op jit(solution)/shard_map/ppermute | solution.py:38
  5.2 10.7 %collective-permute-start.4 = (s32[2,128]{1,0:T(2,128)}, s32[2,128]{1,0:T(2,128)S(1)}, u32[]{:S(2)}, u32[]{:S(2)}) collective-permute-start(s32[2,128]{1,0:T(2,128)} %bitcast.89), channel_id=1, source_target_pairs={{0,4},{4,0},{1,5},{5,1},{2,6},{6,2},{3,7},{7,3},{8,12},{12,8},{9,1... | collective-permute-start | bytes 3080 | tf_op jit(solution)/shard_map/ppermute | solution.py:38
  5.7 25.2 %collective-permute-start.6 = (bf16[128,2048]{1,0:T(8,128)(2,1)}, bf16[128,2048]{1,0:T(8,128)(2,1)S(1)}, u32[]{:S(2)}, u32[]{:S(2)}) collective-permute-start(bf16[128,2048]{1,0:T(8,128)(2,1)} %tokens_ref.1), channel_id=1, source_target_pairs={{0,2},{1,3},{2,0},{3,1},{4,6},{5,7},{6,4},{7,5},{8,10},{9,11},{10,... | collective-permute-start | bytes 1572872 | tf_op jit(solution)/shard_map/ppermute | solution.py:38
  15.9 15.0 %collective-permute-start.7 = (bf16[128,2048]{1,0:T(8,128)(2,1)S(1)}, bf16[128,2048]{1,0:T(8,128)(2,1)S(1)}, u32[]{:S(2)}, u32[]{:S(2)}) collective-permute-start(bf16[128,2048]{1,0:T(8,128)(2,1)S(1)} %collective-permute-done.refs_2_), channel_id=1, source_target_pairs={{0,2},{1,3},{2,0},{3,1},{4,6},{5,7},{6,4},{7,5},{8,10},{9,11},{10,... | collective-permute-start | bytes 1572872 | tf_op jit(solution)/shard_map/ppermute | solution.py:38
  17.7 10.0 %collective-permute-start.1 = (bf16[64,2048]{1,0:T(8,128)(2,1)S(1)}, bf16[64,2048]{1,0:T(8,128)(2,1)}, u32[]{:S(2)}, u32[]{:S(2)}) collective-permute-start(bf16[64,2048]{1,0:T(8,128)(2,1)S(1)} %constant_dynamic-slice_fusion.2), channel_id=1, source_target_pairs={{0,4},{4,0},{1,5},{5,1},{2,6},{6,2},{3,7},{7,3},{8,12},{12,8},{9,1... | collective-permute-start | bytes 786440 | tf_op jit(solution)/shard_map/ppermute | solution.py:38
  19.9 7.0 %collective-permute-start.5 = (s32[2,128]{1,0:T(2,128)S(1)}, s32[2,128]{1,0:T(2,128)S(1)}, u32[]{:S(2)}, u32[]{:S(2)}) collective-permute-start(s32[2,128]{1,0:T(2,128)S(1)} %collective-permute-done.3), channel_id=1, source_target_pairs={{0,4},{4,0},{1,5},{5,1},{2,6},{6,2},{3,7},{7,3},{8,12},{12,8},{9,1... | collective-permute-start | bytes 3080 | tf_op jit(solution)/shard_map/ppermute | solution.py:38
  21.1 1.2 copy-start.4
  22.4 0.7 copy-start.12
  23.8 0.8 copy-start.15
  27.7 18.4 %collective-permute-start.2 = (bf16[256,1024]{1,0:T(8,128)(2,1)}, bf16[256,1024]{1,0:T(8,128)(2,1)S(1)}, u32[]{:S(2)}, u32[]{:S(2)}) collective-permute-start(bf16[256,1024]{1,0:T(8,128)(2,1)} %copy-done.15), channel_id=1, source_target_pairs={{0,4},{4,0},{1,5},{5,1},{2,6},{6,2},{3,7},{7,3},{8,12},{12,8},{9,1... | collective-permute-start | bytes 1572872 | tf_op jit(solution)/shard_map/ppermute | solution.py:38
  29.3 7.1 %collective-permute-start.9 = (bf16[64,2048]{1,0:T(8,128)(2,1)}, bf16[64,2048]{1,0:T(8,128)(2,1)S(1)}, u32[]{:S(2)}, u32[]{:S(2)}) collective-permute-start(bf16[64,2048]{1,0:T(8,128)(2,1)} %collective-permute-done.1), channel_id=1, source_target_pairs={{0,8},{8,0},{16,24},{24,16},{1,9},{9,1},{17,25},{25,17},{2,10},{10... | collective-permute-start | bytes 786440 | tf_op jit(solution)/shard_map/ppermute | solution.py:38
  30.9 1.0 copy-start.1
  31.9 4.6 %copy-start.17 = (bf16[1,1024,2048]{2,1,0:T(8,128)(2,1)S(1)}, bf16[1,1024,2048]{2,1,0:T(8,128)(2,1)}, u32[]{:S(2)}) copy-start(bf16[1,1024,2048]{2,1,0:T(8,128)(2,1)} %param.20) | copy-start | bytes 12582916
  36.4 2.6 %copy-start.23 = (s32[128,2]{1,0:T(8,128)S(1)}, s32[128,2]{1,0:T(8,128)}, u32[]{:S(2)}) copy-start(s32[128,2]{1,0:T(8,128)} %copy.38) | copy-start | bytes 3076
  36.4 2.6 %copy-start.24 = (s32[128,2]{1,0:T(8,128)S(1)}, s32[128,2]{1,0:T(8,128)}, u32[]{:S(2)}) copy-start(s32[128,2]{1,0:T(8,128)} %copy.41) | copy-start | bytes 3076
  36.4 10.9 %copy-start.16 = (bf16[1,2048,1024]{2,1,0:T(8,128)(2,1)S(1)}, bf16[1,2048,1024]{2,1,0:T(8,128)(2,1)}, u32[]{:S(2)}) copy-start(bf16[1,2048,1024]{2,1,0:T(8,128)(2,1)} %param.19) | copy-start | bytes 12582916
  36.4 10.9 %collective-permute-start.8 = (bf16[192,2048]{1,0:T(8,128)(2,1)S(1)}, bf16[192,2048]{1,0:T(8,128)(2,1)S(1)}, u32[]{:S(2)}, u32[]{:S(2)}) collective-permute-start(bf16[192,2048]{1,0:T(8,128)(2,1)S(1)} %get-tuple-element.46), channel_id=1, source_target_pairs={{0,1},{1,0},{2,3},{3,2},{4,5},{5,4},{6,7},{7,6},{8,9},{9,8},{10,11... | collective-permute-start | bytes 2359304 | tf_op jit(solution)/shard_map/ppermute | solution.py:38
  38.4 7.7 %collective-permute-start.13 = (bf16[48,2048]{1,0:T(8,128)(2,1)S(1)}, bf16[48,2048]{1,0:T(8,128)(2,1)S(1)}, u32[]{:S(2)}, u32[]{:S(2)}) collective-permute-start(bf16[48,2048]{1,0:T(8,128)(2,1)S(1)} %get-tuple-element.87), channel_id=1, source_target_pairs={{0,2},{1,3},{2,0},{3,1},{4,6},{5,7},{6,4},{7,5},{8,10},{9,11},{10,... | collective-permute-start | bytes 589832 | tf_op jit(solution)/shard_map/ppermute | solution.py:223
  39.0 18.5 %collective-permute-start.15 = (bf16[48,2048]{1,0:T(8,128)(2,1)}, bf16[48,2048]{1,0:T(8,128)(2,1)S(1)}, u32[]{:S(2)}, u32[]{:S(2)}) collective-permute-start(bf16[48,2048]{1,0:T(8,128)(2,1)} %get-tuple-element.85), channel_id=1, source_target_pairs={{0,4},{1,5},{2,6},{3,7},{4,0},{5,1},{6,2},{7,3},{8,12},{9,13},{10,... | collective-permute-start | bytes 589832 | tf_op jit(solution)/shard_map/ppermute | solution.py:223
  39.7 17.8 %collective-permute-start.16 = (bf16[48,2048]{1,0:T(8,128)(2,1)}, bf16[48,2048]{1,0:T(8,128)(2,1)}, u32[]{:S(2)}, u32[]{:S(2)}) collective-permute-start(bf16[48,2048]{1,0:T(8,128)(2,1)} %get-tuple-element.84), channel_id=1, source_target_pairs={{0,6},{1,7},{2,4},{3,5},{4,2},{5,3},{6,0},{7,1},{8,14},{9,15},{10,... | collective-permute-start | bytes 589832 | tf_op jit(solution)/shard_map/ppermute | solution.py:223
  49.4 8.0 %copy-start.25 = (f32[128,2]{0,1:T(2,128)S(1)}, f32[128,2]{0,1:T(2,128)}, u32[]{:S(2)}) copy-start(f32[128,2]{0,1:T(2,128)} %param.17) | copy-start | bytes 3076
  49.4 19.2 %copy-start.5 = (bf16[128,2048]{1,0:T(8,128)(2,1)S(1)}, bf16[128,2048]{1,0:T(8,128)(2,1)}, u32[]{:S(2)}) copy-start(bf16[128,2048]{1,0:T(8,128)(2,1)} %refs_0_.3) | copy-start | bytes 1572868
  50.3 3.0 %collective-permute-start.14 = (bf16[48,2048]{1,0:T(8,128)(2,1)S(1)}, bf16[48,2048]{1,0:T(8,128)(2,1)S(1)}, u32[]{:S(2)}, u32[]{:S(2)}) collective-permute-start(bf16[48,2048]{1,0:T(8,128)(2,1)S(1)} %get-tuple-element.81), channel_id=1, source_target_pairs={{0,1},{1,0},{2,3},{3,2},{4,5},{5,4},{6,7},{7,6},{8,9},{9,8},{10,11... | collective-permute-start | bytes 589832 | tf_op jit(solution)/shard_map/ppermute | solution.py:223
  50.3 7.2 %collective-permute-start.10 = (bf16[48,2048]{1,0:T(8,128)(2,1)}, bf16[48,2048]{1,0:T(8,128)(2,1)}, u32[]{:S(2)}, u32[]{:S(2)}) collective-permute-start(bf16[48,2048]{1,0:T(8,128)(2,1)} %get-tuple-element.83), channel_id=1, source_target_pairs={{0,3},{1,2},{2,1},{3,0},{4,7},{5,6},{6,5},{7,4},{8,11},{9,10},{10,... | collective-permute-start | bytes 589832 | tf_op jit(solution)/shard_map/ppermute | solution.py:223
  50.9 11.5 %collective-permute-start.11 = (bf16[48,2048]{1,0:T(8,128)(2,1)}, bf16[48,2048]{1,0:T(8,128)(2,1)}, u32[]{:S(2)}, u32[]{:S(2)}) collective-permute-start(bf16[48,2048]{1,0:T(8,128)(2,1)} %get-tuple-element.82), channel_id=1, source_target_pairs={{0,5},{1,4},{2,7},{3,6},{4,1},{5,0},{6,3},{7,2},{8,13},{9,12},{10,... | collective-permute-start | bytes 589832 | tf_op jit(solution)/shard_map/ppermute | solution.py:223
  53.2 0.7 copy-start.10
  53.9 8.6 %collective-permute-start.17 = (bf16[48,2048]{1,0:T(8,128)(2,1)}, bf16[48,2048]{1,0:T(8,128)(2,1)}, u32[]{:S(2)}, u32[]{:S(2)}) collective-permute-start(bf16[48,2048]{1,0:T(8,128)(2,1)} %get-tuple-element.80), channel_id=1, source_target_pairs={{0,7},{1,6},{2,5},{3,4},{4,3},{5,2},{6,1},{7,0},{8,15},{9,14},{10,... | collective-permute-start | bytes 589832 | tf_op jit(solution)/shard_map/ppermute | solution.py:223
  62.5 0.9 copy-start.11
  65.4 8.4 %collective-permute-start.18 = (bf16[2,128,512]{2,1,0:T(8,128)(2,1)S(1)}, bf16[2,128,512]{2,1,0:T(8,128)(2,1)S(1)}, u32[]{:S(2)}, u32[]{:S(2)}) collective-permute-start(bf16[2,128,512]{2,1,0:T(8,128)(2,1)S(1)} %get-tuple-element.57), channel_id=1, source_target_pairs={{0,8},{8,0},{16,24},{24,16},{1,9},{9,1},{17,25},{25,17},{2,10},{10... | collective-permute-start | bytes 786440 | tf_op jit(solution)/shard_map/ppermute | solution.py:38
  66.3 21.1 %collective-permute-start.30 = (bf16[128,2048]{1,0:T(8,128)(2,1)S(1)}, bf16[128,2048]{1,0:T(8,128)(2,1)S(1)}, u32[]{:S(2)}, u32[]{:S(2)}) collective-permute-start(bf16[128,2048]{1,0:T(8,128)(2,1)S(1)} %constant_dynamic-update-slice_fusion.refs_2_), channel_id=1, source_target_pairs={{0,2},{1,3},{2,0},{3,1},{4,6},{5,7},{6,4},{7,5},{8,10},{9,11},{10,... | collective-permute-start | bytes 1572872 | tf_op jit(solution)/shard_map/ppermute | solution.py:38
  67.8 9.4 %collective-permute-start.12 = (bf16[256,512]{1,0:T(8,128)(2,1)}, bf16[256,512]{1,0:T(8,128)(2,1)S(1)}, u32[]{:S(2)}, u32[]{:S(2)}) collective-permute-start(bf16[256,512]{1,0:T(8,128)(2,1)} %fusion.1), channel_id=1, source_target_pairs={{0,4},{4,0},{1,5},{5,1},{2,6},{6,2},{3,7},{7,3},{8,12},{12,8},{9,1... | collective-permute-start | bytes 786440 | tf_op jit(solution)/shard_map/ppermute | solution.py:38
  68.6 22.9 %collective-permute-start.29 = (bf16[128,2048]{1,0:T(8,128)(2,1)S(1)}, bf16[128,2048]{1,0:T(8,128)(2,1)S(1)}, u32[]{:S(2)}, u32[]{:S(2)}) collective-permute-start(bf16[128,2048]{1,0:T(8,128)(2,1)S(1)} %copy-done.5), channel_id=1, source_target_pairs={{0,2},{1,3},{2,0},{3,1},{4,6},{5,7},{6,4},{7,5},{8,10},{9,11},{10,... | collective-permute-start | bytes 1572872 | tf_op jit(solution)/shard_map/ppermute | solution.py:38
  69.2 30.4 %collective-permute-start.21 = (bf16[1024,512]{1,0:T(8,128)(2,1)}, bf16[1024,512]{1,0:T(8,128)(2,1)S(1)}, u32[]{:S(2)}, u32[]{:S(2)}) collective-permute-start(bf16[1024,512]{1,0:T(8,128)(2,1)} %bitcast.85), channel_id=1, source_target_pairs={{0,4},{4,0},{1,5},{5,1},{2,6},{6,2},{3,7},{7,3},{8,12},{12,8},{9,1... | collective-permute-start | bytes 3145736 | tf_op jit(solution)/shard_map/ppermute | solution.py:38
  73.9 8.4 %collective-permute-start.19 = (bf16[128,512]{1,0:T(8,128)(2,1)S(1)}, bf16[128,512]{1,0:T(8,128)(2,1)S(1)}, u32[]{:S(2)}, u32[]{:S(2)}) collective-permute-start(bf16[128,512]{1,0:T(8,128)(2,1)S(1)} %fusion.48), channel_id=1, source_target_pairs={{0,16},{8,24},{16,0},{24,8},{1,17},{9,25},{17,1},{25,9},{2,18},{10... | collective-permute-start | bytes 393224 | tf_op jit(solution)/shard_map/ppermute | solution.py:38
  82.4 5.0 %collective-permute-start.20 = (bf16[128,512]{1,0:T(8,128)(2,1)S(1)}, bf16[128,512]{1,0:T(8,128)(2,1)S(1)}, u32[]{:S(2)}, u32[]{:S(2)}) collective-permute-start(bf16[128,512]{1,0:T(8,128)(2,1)S(1)} %fusion.50.refs_0_), channel_id=1, source_target_pairs={{0,8},{8,0},{16,24},{24,16},{1,9},{9,1},{17,25},{25,17},{2,10},{10... | collective-permute-start | bytes 393224 | tf_op jit(solution)/shard_map/ppermute | solution.py:38
  93.0 0.9 copy-start.7
  93.9 8.5 %collective-permute-start.31 = (bf16[192,2048]{1,0:T(8,128)(2,1)S(1)}, bf16[192,2048]{1,0:T(8,128)(2,1)S(1)}, u32[]{:S(2)}, u32[]{:S(2)}) collective-permute-start(bf16[192,2048]{1,0:T(8,128)(2,1)S(1)} %get-tuple-element.71), channel_id=1, source_target_pairs={{0,1},{1,0},{2,3},{3,2},{4,5},{5,4},{6,7},{7,6},{8,9},{9,8},{10,11... | collective-permute-start | bytes 2359304 | tf_op jit(solution)/shard_map/ppermute | solution.py:38
  93.9 27.3 %collective-permute-start.24 = (bf16[1024,512]{1,0:T(8,128)(2,1)}, bf16[1024,512]{1,0:T(8,128)(2,1)}, u32[]{:S(2)}, u32[]{:S(2)}) collective-permute-start(bf16[1024,512]{1,0:T(8,128)(2,1)} %bitcast.24.refs_4_), channel_id=1, source_target_pairs={{0,4},{4,0},{1,5},{5,1},{2,6},{6,2},{3,7},{7,3},{8,12},{12,8},{9,1... | collective-permute-start | bytes 3145736 | tf_op jit(solution)/shard_map/ppermute | solution.py:38
  99.6 11.0 %copy-start.18 = (bf16[1024,512]{1,0:T(8,128)(2,1)}, bf16[1024,512]{1,0:T(8,128)(2,1)S(1)}, u32[]{:S(2)}) copy-start(bf16[1024,512]{1,0:T(8,128)(2,1)S(1)} %collective-permute-done.21.refs_3_) | copy-start | bytes 3145732
  99.7 18.0 %collective-permute-start.22 = (bf16[2,128,512]{2,1,0:T(8,128)(2,1)S(1)}, bf16[2,128,512]{2,1,0:T(8,128)(2,1)S(1)}, u32[]{:S(2)}, u32[]{:S(2)}) collective-permute-start(bf16[2,128,512]{2,1,0:T(8,128)(2,1)S(1)} %pad_maximum_fusion), channel_id=1, source_target_pairs={{0,16},{8,24},{16,0},{24,8},{1,17},{9,25},{17,1},{25,9},{2,18},{10... | collective-permute-start | bytes 786440 | tf_op jit(solution)/shard_map/ppermute | solution.py:38
  102.3 0.9 copy-start.19
  110.6 7.1 %copy-start.2 = (bf16[128,2048]{1,0:T(8,128)(2,1)S(1)}, bf16[128,2048]{1,0:T(8,128)(2,1)}, u32[]{:S(2)}) copy-start(bf16[128,2048]{1,0:T(8,128)(2,1)} %tokens_ref.1) | copy-start | bytes 1572868
  110.6 7.1 %copy-start.13 = (f32[2048]{0:T(1024)S(1)}, f32[2048]{0:T(1024)}, u32[]{:S(2)}) copy-start(f32[2048]{0:T(1024)} %param.21) | copy-start | bytes 24580
  110.6 7.7 %copy-start.6 = (bf16[1,512,1024]{2,1,0:T(8,128)(2,1)S(1)}, bf16[1,512,1024]{2,1,0:T(8,128)(2,1)}, u32[]{:S(2)}) copy-start(bf16[1,512,1024]{2,1,0:T(8,128)(2,1)} %param.29) | copy-start | bytes 3145732
  116.5 17.5 %collective-permute-start.32 = (bf16[2,384,512]{2,1,0:T(8,128)(2,1)}, bf16[2,384,512]{2,1,0:T(8,128)(2,1)}, u32[]{:S(2)}, u32[]{:S(2)}) collective-permute-start(bf16[2,384,512]{2,1,0:T(8,128)(2,1)} %get-tuple-element.73), channel_id=1, source_target_pairs={{0,8},{8,0},{16,24},{24,16},{1,9},{9,1},{17,25},{25,17},{2,10},{10... | collective-permute-start | bytes 2359304 | tf_op jit(solution)/shard_map/ppermute | solution.py:38
  118.2 3.0 %copy-start.3 = (bf16[128,2048]{1,0:T(8,128)(2,1)}, bf16[128,2048]{1,0:T(8,128)(2,1)S(1)}, u32[]{:S(2)}) copy-start(bf16[128,2048]{1,0:T(8,128)(2,1)S(1)} %memory.1.refs_0_) | copy-start | bytes 1572868
  118.2 3.0 %collective-permute-start.23 = (bf16[128,2048]{1,0:T(8,128)(2,1)S(1)}, bf16[128,2048]{1,0:T(8,128)(2,1)}, u32[]{:S(2)}, u32[]{:S(2)}) collective-permute-start(bf16[128,2048]{1,0:T(8,128)(2,1)S(1)} %memory.1.refs_0_), channel_id=1, source_target_pairs={{0,1},{1,0},{2,3},{3,2},{4,5},{5,4},{6,7},{7,6},{8,9},{9,8},{10,11... | collective-permute-start | bytes 1572872 | tf_op jit(solution)/shard_map/ppermute | solution.py:38
  118.3 14.4 %collective-permute-start.25 = (bf16[128,2048]{1,0:T(8,128)(2,1)S(1)}, bf16[128,2048]{1,0:T(8,128)(2,1)}, u32[]{:S(2)}, u32[]{:S(2)}) collective-permute-start(bf16[128,2048]{1,0:T(8,128)(2,1)S(1)} %memory.1.refs_0_), channel_id=1, source_target_pairs={{0,2},{1,3},{2,0},{3,1},{4,6},{5,7},{6,4},{7,5},{8,10},{9,11},{10,... | collective-permute-start | bytes 1572872 | tf_op jit(solution)/shard_map/ppermute | solution.py:38
  118.3 25.6 %collective-permute-start.27 = (bf16[512,1024]{1,0:T(8,128)(2,1)S(1)}, bf16[512,1024]{1,0:T(8,128)(2,1)}, u32[]{:S(2)}, u32[]{:S(2)}) collective-permute-start(bf16[512,1024]{1,0:T(8,128)(2,1)S(1)} %bitcast.79), channel_id=1, source_target_pairs={{0,4},{4,0},{1,5},{5,1},{2,6},{6,2},{3,7},{7,3},{8,12},{12,8},{9,1... | collective-permute-start | bytes 3145736 | tf_op jit(solution)/shard_map/ppermute | solution.py:38
  119.7 14.3 %copy-start.20 = (f32[384,512]{1,0:T(8,128)S(1)}, f32[384,512]{1,0:T(8,128)}, u32[]{:S(2)}) copy-start(f32[384,512]{1,0:T(8,128)} %get-tuple-element.72) | copy-start | bytes 2359300
  126.6 17.4 %copy-start.8 = (bf16[128,512]{1,0:T(8,128)(2,1)S(1)}, bf16[128,512]{1,0:T(8,128)(2,1)}, u32[]{:S(2)}) copy-start(bf16[128,512]{1,0:T(8,128)(2,1)} %attend_sentence.2.mine_ref) | copy-start | bytes 393220
  126.6 17.4 %copy-start.14 = (s32[3]{0:T(128)S(1)}, s32[3]{0:T(128)}, u32[]{:S(2)}) copy-start(s32[3]{0:T(128)} %pad_add_fusion.1.place_ref) | copy-start | bytes 40
  132.7 3.6 %collective-permute-start.26 = (bf16[128,2048]{1,0:T(8,128)(2,1)}, bf16[128,2048]{1,0:T(8,128)(2,1)S(1)}, u32[]{:S(2)}, u32[]{:S(2)}) collective-permute-start(bf16[128,2048]{1,0:T(8,128)(2,1)} %collective-permute-done.25.refs_0_), channel_id=1, source_target_pairs={{0,1},{1,0},{2,3},{3,2},{4,5},{5,4},{6,7},{7,6},{8,9},{9,8},{10,11... | collective-permute-start | bytes 1572872 | tf_op jit(solution)/shard_map/ppermute | solution.py:38
  135.1 19.6 %collective-permute-start.33 = (bf16[384,512]{1,0:T(8,128)(2,1)S(1)}, bf16[384,512]{1,0:T(8,128)(2,1)S(1)}, u32[]{:S(2)}, u32[]{:S(2)}) collective-permute-start(bf16[384,512]{1,0:T(8,128)(2,1)S(1)} %fusion.35), channel_id=1, source_target_pairs={{0,16},{8,24},{16,0},{24,8},{1,17},{9,25},{17,1},{25,9},{2,18},{10... | collective-permute-start | bytes 1179656 | tf_op jit(solution)/shard_map/ppermute | solution.py:38
  136.3 0.8 copy-start.22
  137.1 18.1 %copy-start.21 = (f32[384,512]{1,0:T(8,128)S(1)}, f32[384,512]{1,0:T(8,128)}, u32[]{:S(2)}) copy-start(f32[384,512]{1,0:T(8,128)} %get-tuple-element.76) | copy-start | bytes 2359300
  143.9 0.9 copy-start.9
  144.8 15.7 %copy-start.26 = (s32[2]{0:T(128)S(1)}, s32[2]{0:T(128)}, u32[]{:S(2)}) copy-start(s32[2]{0:T(128)} %param.24) | copy-start | bytes 28
  146.8 7.9 %collective-permute-start.34 = (bf16[256,512]{1,0:T(8,128)(2,1)S(1)}, bf16[256,512]{1,0:T(8,128)(2,1)S(1)}, u32[]{:S(2)}, u32[]{:S(2)}) collective-permute-start(bf16[256,512]{1,0:T(8,128)(2,1)S(1)} %get-tuple-element.75), channel_id=1, source_target_pairs={{0,1},{1,0},{2,3},{3,2},{4,5},{5,4},{6,7},{7,6},{8,9},{9,8},{10,11... | collective-permute-start | bytes 786440 | tf_op jit(solution)/shard_map/ppermute | solution.py:38
  146.9 13.9 %collective-permute-start.28 = (bf16[256,512]{1,0:T(8,128)(2,1)S(1)}, bf16[256,512]{1,0:T(8,128)(2,1)S(1)}, u32[]{:S(2)}, u32[]{:S(2)}) collective-permute-start(bf16[256,512]{1,0:T(8,128)(2,1)S(1)} %get-tuple-element.65), channel_id=1, source_target_pairs={{0,1},{1,0},{2,3},{3,2},{4,5},{5,4},{6,7},{7,6},{8,9},{9,8},{10,11... | collective-permute-start | bytes 786440 | tf_op jit(solution)/shard_map/ppermute | solution.py:38
  154.8 7.9 %collective-permute-start.35 = (bf16[256,512]{1,0:T(8,128)(2,1)S(1)}, bf16[256,512]{1,0:T(8,128)(2,1)S(1)}, u32[]{:S(2)}, u32[]{:S(2)}) collective-permute-start(bf16[256,512]{1,0:T(8,128)(2,1)S(1)} %convert_add_fusion.3), channel_id=1, source_target_pairs={{0,2},{1,3},{2,0},{3,1},{4,6},{5,7},{6,4},{7,5},{8,10},{9,11},{10,... | collective-permute-start | bytes 786440 | tf_op jit(solution)/shard_map/ppermute | solution.py:38
  157.1 11.7 %all-to-all-start = ((bf16[8,48,512]{2,1,0:T(8,128)(2,1)}), bf16[8,48,512]{2,1,0:T(8,128)(2,1)S(1)}, u32[]{:S(2)}, u32[]{:S(2)}) async-start(bf16[8,48,512]{2,1,0:T(8,128)(2,1)} %bitcast.31), calls=%async_computation | async-start | bytes 786432 | tf_op jit(solution)/shard_map/all_to_all | solution.py:142

commit v19 on v18

--- a/solution.py
+++ b/solution.py
@@ -669,7 +669,7 @@
     mixed_far = swap(jnp.stack([mixed_slice, gate(mixed_near, key_other)]), "section", 2)
     slices = [mixed_slice, mixed_near, mixed_far[0], mixed_far[1]]
 
-    value_other = swap(gate(value_own, mixed_near), "expert", 1)
+    value_other = swap(gate(value_own, mixed_near, key_other), "expert", 1)
 
     query_here = jnp.dot(normed_own, query_own, preferred_element_type=jnp.float32)
     query = (query_here + query_back.astype(jnp.float32)).astype(jnp.bfloat16)

time: 171 us -> 171 us (level)
  no operation moved by 1% of the time
where the time goes in v19:
time: 171 us; the launch traced here: 170 us
  waiting for transfers between devices  62.4 us (36%)
  starting transfers between devices  38 us (22%)
  Pallas kernels  33 us (19%)
  local copies, waits for them, and re-layouts  15.8 us (9%)
  other arithmetic  11.2 us (7%)
  matrix products  8.24 us (5%)
    ppermute x29, waiting for transfers between devices, swap(): return lax.ppermute(value, axis, [(i, i ^ mask) for i in range(size)])  49.7 us
    ppermute x29, starting transfers between devices, swap(): return lax.ppermute(value, axis, [(i, i ^ mask) for i in range(size)])  27.7 us
    pallas_call x2, Pallas kernels, attend_sentence(): pl.pallas_call(attend_kernel, out_shape=jax.ShapeDtypeStruct(query.shape,...  10.9 us
    unnamed x57, local copies, waits for them, and re-layouts  10.8 us
    ppermute x7, waiting for transfers between devices, send_home(): lax.ppermute(block, ('expert', 'dp'), [(i, i ^ code) for i in range(size)])  9.08 us
    pallas_call x1, Pallas kernels, expert_slope(): pl.pallas_call(functools.partial(slope_kernel, codes), out_shape=jax.Shap...  7.34 us
    ppermute x7, starting transfers between devices, send_home(): lax.ppermute(block, ('expert', 'dp'), [(i, i ^ code) for i in range(size)])  6.88 us
    pallas_call x1, Pallas kernels, expert_backward(): pl.pallas_call(functools.partial(backward_kernel, split), out_shape=(jax....  5.85 us
  transfers between devices with their start and end apart: 37, of which 16 were waited for; matrix products, arithmetic and copies ran while one was open for 15% of the time, Pallas kernels for 18%

profile of v19, /device:TPU:0, one launch (start us, length us, event | category | flops | bytes accessed | tf_op | source)
XLA Modules:
  0.0 169.7 jit_solution(16308581200204027052)
XLA Ops:
  0.6 3.0 %collective-permute-start = (bf16[128,2048]{1,0:T(8,128)(2,1)}, bf16[128,2048]{1,0:T(8,128)(2,1)S(1)}, u32[]{:S(2)}, u32[]{:S(2)}) collective-permute-start(bf16[128,2048]{1,0:T(8,128)(2,1)} %tokens_ref.1), channel_id=1, source_target_pairs={{0,4},{4,0},{1,5},{5,1},{2,6},{6,2},{3,7},{7,3},{8,12},{12,8},{9,1... | collective-permute-start | bytes 1572872 | tf_op jit(solution)/shard_map/ppermute | solution.py:38
  3.7 1.5 collective-permute-start.3
  5.8 1.0 constant_dynamic-slice_fusion.2
  7.5 8.4 %collective-permute-done.4 = s32[2,128]{1,0:T(2,128)S(1)} collective-permute-done((s32[2,128]{1,0:T(2,128)}, s32[2,128]{1,0:T(2,128)S(1)}, u32[]{:S(2)}, u32[]{:S(2)}) %collective-permute-start.4) | collective-permute-done | bytes 1056 | tf_op jit(solution)/shard_map/ppermute | solution.py:38
  15.9 1.7 %collective-permute-start.7 = (bf16[128,2048]{1,0:T(8,128)(2,1)S(1)}, bf16[128,2048]{1,0:T(8,128)(2,1)S(1)}, u32[]{:S(2)}, u32[]{:S(2)}) collective-permute-start(bf16[128,2048]{1,0:T(8,128)(2,1)S(1)} %collective-permute-done.refs_2_), channel_id=1, source_target_pairs={{0,2},{1,3},{2,0},{3,1},{4,6},{5,7},{6,4},{7,5},{8,10},{9,11},{10,... | collective-permute-start | bytes 1572872 | tf_op jit(solution)/shard_map/ppermute | solution.py:38
  17.7 1.5 collective-permute-start.1
  21.1 1.2 copy-done.4
  23.8 0.8 copy-done.15
  24.6 0.8 copy.36
  27.7 1.5 collective-permute-start.2
  29.3 1.6 collective-permute-start.9
  30.9 1.0 copy-done.1
  31.9 1.3 dispatch.2
  33.2 3.2 %fusion.61 = f32[192,1024]{1,0:T(8,128)S(1)} fusion(bf16[192,2048]{1,0:T(8,128)(2,1)S(1)} %get-tuple-element.47, bf16[1,2048,1024]{2,1,0:T(8,128)(2,1)} %param.19), kind=kOutput, calls=%fused_computation.101 | convolution fusion | flops 805306368 | bytes 5767168 | tf_op jit(solution)/shard_map/dot_general | solution.py:610
  36.5 1.1 convolution_convert_fusion.1
  37.6 0.8 fusion.73
  39.7 2.3 %collective-permute-start.16 = (bf16[48,2048]{1,0:T(8,128)(2,1)}, bf16[48,2048]{1,0:T(8,128)(2,1)}, u32[]{:S(2)}, u32[]{:S(2)}) collective-permute-start(bf16[48,2048]{1,0:T(8,128)(2,1)} %get-tuple-element.84), channel_id=1, source_target_pairs={{0,6},{1,7},{2,4},{3,5},{4,2},{5,3},{6,0},{7,1},{8,14},{9,15},{10,... | collective-permute-start | bytes 589832 | tf_op jit(solution)/shard_map/ppermute | solution.py:223
  42.0 4.1 %collective-permute-done.13.refs_1_ = bf16[48,2048]{1,0:T(8,128)(2,1)S(1)} collective-permute-done((bf16[48,2048]{1,0:T(8,128)(2,1)S(1)}, bf16[48,2048]{1,0:T(8,128)(2,1)S(1)}, u32[]{:S(2)}, u32[]{:S(2)}) %collective-permute-start.13) | collective-permute-done | bytes 196640 | tf_op jit(solution)/shard_map/ppermute | solution.py:223
  46.1 1.2 fusion.1
  47.3 1.0 fusion.59
  48.3 1.1 convolution_convert_fusion
  49.4 0.8 fusion.72
  51.1 2.1 %fusion.10 = (f32[192,1024]{1,0:T(8,128)}, f32[192,1024]{1,0:T(8,128)}) fusion(f32[192,1024]{1,0:T(8,128)S(1)} %fusion.61, f32[192,1024]{1,0:T(8,128)S(1)} %fusion.59), kind=kLoop, calls=%fused_computation.20 | loop fusion | flops 6684672 | bytes 3145728 | tf_op jit(solution)/shard_map/transpose(jvp())/add_any | solution.py:616
  53.9 2.5 %collective-permute-start.17 = (bf16[48,2048]{1,0:T(8,128)(2,1)}, bf16[48,2048]{1,0:T(8,128)(2,1)}, u32[]{:S(2)}, u32[]{:S(2)}) collective-permute-start(bf16[48,2048]{1,0:T(8,128)(2,1)} %get-tuple-element.80), channel_id=1, source_target_pairs={{0,7},{1,6},{2,5},{3,4},{4,3},{5,2},{6,1},{7,0},{8,15},{9,14},{10,... | collective-permute-start | bytes 589832 | tf_op jit(solution)/shard_map/ppermute | solution.py:223
  56.4 1.0 constant_dynamic-update-slice_fusion.1
  57.5 5.0 %collective-permute-done.11.refs_6_ = bf16[48,2048]{1,0:T(8,128)(2,1)} collective-permute-done((bf16[48,2048]{1,0:T(8,128)(2,1)}, bf16[48,2048]{1,0:T(8,128)(2,1)}, u32[]{:S(2)}, u32[]{:S(2)}) %collective-permute-start.11) | collective-permute-done | bytes 196640 | tf_op jit(solution)/shard_map/ppermute | solution.py:223
  62.5 0.9 copy-done.11
  63.4 2.1 %combine.2 = (bf16[2,128,512]{2,1,0:T(8,128)(2,1)S(1)}, f32[128,512]{1,0:T(8,128)S(1)}, f32[128,512]{1,0:T(8,128)S(1)}) custom-call(s32[1]{0:T(128)} %bitcast.7.section_ref, s32[128,2]{1,0:T(8,128)S(1)} %get-tuple-element.93.position_ref, f32[128,2]{1,0:T(8,128)S(1)} %copy.39.gates_ref, bf16[48,2048]{1,0:T(8,128)(2,1)S(1)} %get-tuple-element.86.refs_0_, ...), custom_call_target="tpu_custom_call" | custom-call | flops 1 | bytes 1 | tf_op jit(solution)/shard_map/combine/pallas_call | solution.py:264
  65.4 0.8 collective-permute-start.18
  66.3 1.5 collective-permute-start.30
  67.8 0.9 collective-permute-start.12
  69.2 1.1 collective-permute-start.21
  70.3 3.5 %collective-permute-done.18 = bf16[2,128,512]{2,1,0:T(8,128)(2,1)S(1)} collective-permute-done((bf16[2,128,512]{2,1,0:T(8,128)(2,1)S(1)}, bf16[2,128,512]{2,1,0:T(8,128)(2,1)S(1)}, u32[]{:S(2)}, u32[]{:S(2)}) %collective-permute-start.18) | collective-permute-done | bytes 262176 | tf_op jit(solution)/shard_map/ppermute | solution.py:38
  73.9 2.6 %collective-permute-start.19 = (bf16[128,512]{1,0:T(8,128)(2,1)S(1)}, bf16[128,512]{1,0:T(8,128)(2,1)S(1)}, u32[]{:S(2)}, u32[]{:S(2)}) collective-permute-start(bf16[128,512]{1,0:T(8,128)(2,1)S(1)} %fusion.48), channel_id=1, source_target_pairs={{0,16},{8,24},{16,0},{24,8},{1,17},{9,25},{17,1},{25,9},{2,18},{10... | collective-permute-start | bytes 393224 | tf_op jit(solution)/shard_map/ppermute | solution.py:38
  77.2 5.1 %collective-permute-done.19 = bf16[128,512]{1,0:T(8,128)(2,1)S(1)} collective-permute-done((bf16[128,512]{1,0:T(8,128)(2,1)S(1)}, bf16[128,512]{1,0:T(8,128)(2,1)S(1)}, u32[]{:S(2)}, u32[]{:S(2)}) %collective-permute-start.19) | collective-permute-done | bytes 131104 | tf_op jit(solution)/shard_map/ppermute | solution.py:38
  83.1 4.3 %collective-permute-done.20.refs_1_ = bf16[128,512]{1,0:T(8,128)(2,1)S(1)} collective-permute-done((bf16[128,512]{1,0:T(8,128)(2,1)S(1)}, bf16[128,512]{1,0:T(8,128)(2,1)S(1)}, u32[]{:S(2)}, u32[]{:S(2)}) %collective-permute-start.20) | collective-permute-done | bytes 131104 | tf_op jit(solution)/shard_map/ppermute | solution.py:38
  87.4 4.1 %collective-permute-done.29.refs_1_ = bf16[128,2048]{1,0:T(8,128)(2,1)S(1)} collective-permute-done((bf16[128,2048]{1,0:T(8,128)(2,1)S(1)}, bf16[128,2048]{1,0:T(8,128)(2,1)S(1)}, u32[]{:S(2)}, u32[]{:S(2)}) %collective-permute-start.29) | collective-permute-done | bytes 524320 | tf_op jit(solution)/shard_map/ppermute | solution.py:38
  91.5 1.4 dispatch.3
  93.0 0.9 copy-done.7
  93.9 4.7 %collective-permute-done.21.refs_3_ = bf16[1024,512]{1,0:T(8,128)(2,1)S(1)} collective-permute-done((bf16[1024,512]{1,0:T(8,128)(2,1)}, bf16[1024,512]{1,0:T(8,128)(2,1)S(1)}, u32[]{:S(2)}, u32[]{:S(2)}) %collective-permute-start.21) | collective-permute-done | bytes 1048608 | tf_op jit(solution)/shard_map/ppermute | solution.py:38
  98.6 0.9 collective-permute-start.24
  99.5 2.7 %collective-permute-start.22 = (bf16[2,128,512]{2,1,0:T(8,128)(2,1)S(1)}, bf16[2,128,512]{2,1,0:T(8,128)(2,1)S(1)}, u32[]{:S(2)}, u32[]{:S(2)}) collective-permute-start(bf16[2,128,512]{2,1,0:T(8,128)(2,1)S(1)} %pad_maximum_fusion), channel_id=1, source_target_pairs={{0,16},{8,24},{16,0},{24,8},{1,17},{9,25},{17,1},{25,9},{2,18},{10... | collective-permute-start | bytes 786440 | tf_op jit(solution)/shard_map/ppermute | solution.py:38
  102.2 0.9 copy-done.19
  103.1 7.3 %expert_slope.1.slope_ref = bf16[384,1024]{1,0:T(8,128)(2,1)} custom-call(s32[1]{0:T(128)} %bitcast.27.here_ref, bf16[192,2048]{1,0:T(8,128)(2,1)} %copy-done.7, bf16[192,2048]{1,0:T(8,128)(2,1)} %copy-done.19, f32[192,1024]{1,0:T(8,128)} %get-tuple-element.94.rise_own, f32[192,1024]{1,0:T(8,128)} %get-tuple-element.95.rise_core, bf16[1024,2048]{1,0:T(8,128)(2,1)} %bitcast.84), custom_call_target="tpu_custom_call" | custom-call | flops 1 | bytes 1 | tf_op jit(solution)/shard_map/expert_slope/pallas_call | solution.py:478
  110.5 5.8 %expert_backward.1 = (bf16[2,384,512]{2,1,0:T(8,128)(2,1)}, f32[384,512]{1,0:T(8,128)}, f32[384,512]{1,0:T(8,128)}) custom-call(s32[1]{0:T(128)} %bitcast.7.section_ref, bf16[384,1024]{1,0:T(8,128)(2,1)} %expert_slope.1.slope_ref, bf16[2048,1024]{1,0:T(8,128)(2,1)} %bitcast.83), custom_call_target="tpu_custom_call" | custom-call | flops 1 | bytes 1 | tf_op jit(solution)/shard_map/expert_backward/pallas_call | solution.py:520
  116.4 1.0 collective-permute-start.32
  118.5 1.1 collective-permute-start.27
  121.3 3.2 %collective-permute-done.24.refs_5_ = bf16[1024,512]{1,0:T(8,128)(2,1)} collective-permute-done((bf16[1024,512]{1,0:T(8,128)(2,1)}, bf16[1024,512]{1,0:T(8,128)(2,1)}, u32[]{:S(2)}, u32[]{:S(2)}) %collective-permute-start.24) | collective-permute-done | bytes 1048608 | tf_op jit(solution)/shard_map/ppermute | solution.py:38
  124.6 5.4 %attend_sentence.2.mine_ref = bf16[128,512]{1,0:T(8,128)(2,1)} custom-call(s32[3]{0:T(128)} %pad_add_fusion.1.place_ref, s32[2]{0:T(128)} %lengths_ref.3, bf16[128,512]{1,0:T(8,128)(2,1)} %get-tuple-element.89.query_ref, bf16[128,2048]{1,0:T(8,128)(2,1)} %copy-done.3, bf16[128,2048]{1,0:T(8,128)(2,1)} %collective-permute-done.23.refs_1_, ...), custom_call_target="tpu_custom_call" | custom-call | flops 1 | bytes 1 | tf_op jit(solution)/shard_map/attend_sentence/pallas_call | solution.py:380
  130.0 2.4 %collective-permute-done.25.refs_0_ = bf16[128,2048]{1,0:T(8,128)(2,1)} collective-permute-done((bf16[128,2048]{1,0:T(8,128)(2,1)S(1)}, bf16[128,2048]{1,0:T(8,128)(2,1)}, u32[]{:S(2)}, u32[]{:S(2)}) %collective-permute-start.25) | collective-permute-done | bytes 524320 | tf_op jit(solution)/shard_map/ppermute | solution.py:38
  132.4 2.4 %collective-permute-done.32 = bf16[2,384,512]{2,1,0:T(8,128)(2,1)} collective-permute-done((bf16[2,384,512]{2,1,0:T(8,128)(2,1)}, bf16[2,384,512]{2,1,0:T(8,128)(2,1)}, u32[]{:S(2)}, u32[]{:S(2)}) %collective-permute-start.32) | collective-permute-done | bytes 786464 | tf_op jit(solution)/shard_map/ppermute | solution.py:38
  134.8 1.1 fusion.35
  136.9 0.8 copy-done.22
  137.7 5.5 %attend_sentence.3.done_ref = bf16[128,512]{1,0:T(8,128)(2,1)} custom-call(s32[3]{0:T(128)} %pad_add_fusion.3.place_ref, s32[2]{0:T(128)} %lengths_ref.3, bf16[128,512]{1,0:T(8,128)(2,1)} %get-tuple-element.88.query_ref, bf16[128,2048]{1,0:T(8,128)(2,1)} %collective-permute-done.25.refs_0_, bf16[128,2048]{1,0:T(8,128)(2,1)} %copy-done.22, ...), custom_call_target="tpu_custom_call" | custom-call | flops 1 | bytes 1 | tf_op jit(solution)/shard_map/attend_sentence/pallas_call | solution.py:380
  143.2 2.3 %collective-permute-done.27.other_ref = bf16[512,1024]{1,0:T(8,128)(2,1)} collective-permute-done((bf16[512,1024]{1,0:T(8,128)(2,1)S(1)}, bf16[512,1024]{1,0:T(8,128)(2,1)}, u32[]{:S(2)}, u32[]{:S(2)}) %collective-permute-start.27) | collective-permute-done | bytes 1048608 | tf_op jit(solution)/shard_map/ppermute | solution.py:38
  145.5 0.9 copy-done.9
  146.4 2.0 %project.1 = (bf16[256,512]{1,0:T(8,128)(2,1)S(1)}, bf16[256,512]{1,0:T(8,128)(2,1)S(1)}, f32[256,512]{1,0:T(8,128)S(1)}, f32[256,512]{1,0:T(8,128)S(1)}) custom-call(s32[3]{0:T(128)S(1)} %copy-done.14, bf16[128,512]{1,0:T(8,128)(2,1)S(1)} %copy-done.8, bf16[128,512]{1,0:T(8,128)(2,1)S(1)} %copy-done.9, bf16[512,1024]{1,0:T(8,128)(2,1)S(1)} %bitcast.80, ...), custom_call_target="tpu_custom_call" | custom-call | flops 1 | bytes 1 | tf_op jit(solution)/shard_map/project/pallas_call | solution.py:431
  148.4 6.0 %collective-permute-done.33 = bf16[384,512]{1,0:T(8,128)(2,1)S(1)} collective-permute-done((bf16[384,512]{1,0:T(8,128)(2,1)S(1)}, bf16[384,512]{1,0:T(8,128)(2,1)S(1)}, u32[]{:S(2)}, u32[]{:S(2)}) %collective-permute-start.33) | collective-permute-done | bytes 393248 | tf_op jit(solution)/shard_map/ppermute | solution.py:38
  155.1 1.9 %fusion.34 = bf16[384,512]{1,0:T(8,128)(2,1)} fusion(f32[384,512]{1,0:T(8,128)S(1)} %copy-done.21, bf16[384,512]{1,0:T(8,128)(2,1)S(1)} %collective-permute-done.33, bf16[2,384,512]{2,1,0:T(8,128)(2,1)} %collective-permute-done.32), kind=kLoop, calls=%fused_computation.45 | loop fusion | flops 983040 | bytes 1966080 | tf_op jit(solution)/shard_map/convert_element_type | solution.py:708
  157.0 3.5 %all-to-all-start = ((bf16[8,48,512]{2,1,0:T(8,128)(2,1)}), bf16[8,48,512]{2,1,0:T(8,128)(2,1)S(1)}, u32[]{:S(2)}, u32[]{:S(2)}) async-start(bf16[8,48,512]{2,1,0:T(8,128)(2,1)} %bitcast.31), calls=%async_computation | async-start | bytes 786432 | tf_op jit(solution)/shard_map/all_to_all | solution.py:142
  160.7 2.6 %collective-permute-done.35 = bf16[256,512]{1,0:T(8,128)(2,1)S(1)} collective-permute-done((bf16[256,512]{1,0:T(8,128)(2,1)S(1)}, bf16[256,512]{1,0:T(8,128)(2,1)S(1)}, u32[]{:S(2)}, u32[]{:S(2)}) %collective-permute-start.35) | collective-permute-done | bytes 262176 | tf_op jit(solution)/shard_map/ppermute | solution.py:38
  163.3 1.8 %fusion.47 = bf16[1,256,512]{2,1,0:T(8,128)(2,1)} fusion(bf16[256,512]{1,0:T(8,128)(2,1)S(1)} %collective-permute-done.35, f32[256,512]{1,0:T(8,128)S(1)} %get-tuple-element.64, bf16[256,512]{1,0:T(8,128)(2,1)S(1)} %collective-permute-done.28, bf16[1,256,2048]{2,1,0:T(8,128)(2,1)} %param.22, s32[]{:T(128)S(6)} %select_n.35, ...), kind=kLoop, calls=%fused_computation.62 | loop fusion | flops 1048576 | bytes 1573124 | tf_op jit(solution)/shard_map/broadcast_in_dim | solution.py:713
  165.1 3.7 %all-to-all-done = bf16[8,48,512]{2,1,0:T(8,128)(2,1)S(1)} async-done(((bf16[8,48,512]{2,1,0:T(8,128)(2,1)}), bf16[8,48,512]{2,1,0:T(8,128)(2,1)S(1)}, u32[]{:S(2)}, u32[]{:S(2)}) %all-to-all-start) | async-done | bytes 393248 | tf_op jit(solution)/shard_map/all_to_all | solution.py:142
  168.7 1.0 combine.3
  (111 shorter events, 17.1 us)
Async XLA Ops:
  0.6 45.5 %copy-start = (bf16[1,1024,512]{2,1,0:T(8,128)(2,1)S(1)}, bf16[1,1024,512]{2,1,0:T(8,128)(2,1)}, u32[]{:S(2)}) copy-start(bf16[1,1024,512]{2,1,0:T(8,128)(2,1)} %param.26) | copy-start | bytes 3145732
  0.6 15.2 %collective-permute-start = (bf16[128,2048]{1,0:T(8,128)(2,1)}, bf16[128,2048]{1,0:T(8,128)(2,1)S(1)}, u32[]{:S(2)}, u32[]{:S(2)}) collective-permute-start(bf16[128,2048]{1,0:T(8,128)(2,1)} %tokens_ref.1), channel_id=1, source_target_pairs={{0,4},{4,0},{1,5},{5,1},{2,6},{6,2},{3,7},{7,3},{8,12},{12,8},{9,1... | collective-permute-start | bytes 1572872 | tf_op jit(solution)/shard_map/ppermute | solution.py:38
  3.7 3.8 %collective-permute-start.3 = (s32[2,128]{1,0:T(2,128)}, s32[2,128]{1,0:T(2,128)S(1)}, u32[]{:S(2)}, u32[]{:S(2)}) collective-permute-start(s32[2,128]{1,0:T(2,128)} %bitcast.88), channel_id=1, source_target_pairs={{0,2},{1,3},{2,0},{3,1},{4,6},{5,7},{6,4},{7,5},{8,10},{9,11},{10,... | collective-permute-start | bytes 3080 | tf_op jit(solution)/shard_map/ppermute | solution.py:38
  5.2 10.7 %collective-permute-start.4 = (s32[2,128]{1,0:T(2,128)}, s32[2,128]{1,0:T(2,128)S(1)}, u32[]{:S(2)}, u32[]{:S(2)}) collective-permute-start(s32[2,128]{1,0:T(2,128)} %bitcast.89), channel_id=1, source_target_pairs={{0,4},{4,0},{1,5},{5,1},{2,6},{6,2},{3,7},{7,3},{8,12},{12,8},{9,1... | collective-permute-start | bytes 3080 | tf_op jit(solution)/shard_map/ppermute | solution.py:38
  5.7 25.2 %collective-permute-start.6 = (bf16[128,2048]{1,0:T(8,128)(2,1)}, bf16[128,2048]{1,0:T(8,128)(2,1)S(1)}, u32[]{:S(2)}, u32[]{:S(2)}) collective-permute-start(bf16[128,2048]{1,0:T(8,128)(2,1)} %tokens_ref.1), channel_id=1, source_target_pairs={{0,2},{1,3},{2,0},{3,1},{4,6},{5,7},{6,4},{7,5},{8,10},{9,11},{10,... | collective-permute-start | bytes 1572872 | tf_op jit(solution)/shard_map/ppermute | solution.py:38
  15.9 15.0 %collective-permute-start.7 = (bf16[128,2048]{1,0:T(8,128)(2,1)S(1)}, bf16[128,2048]{1,0:T(8,128)(2,1)S(1)}, u32[]{:S(2)}, u32[]{:S(2)}) collective-permute-start(bf16[128,2048]{1,0:T(8,128)(2,1)S(1)} %collective-permute-done.refs_2_), channel_id=1, source_target_pairs={{0,2},{1,3},{2,0},{3,1},{4,6},{5,7},{6,4},{7,5},{8,10},{9,11},{10,... | collective-permute-start | bytes 1572872 | tf_op jit(solution)/shard_map/ppermute | solution.py:38
  17.7 10.0 %collective-permute-start.1 = (bf16[64,2048]{1,0:T(8,128)(2,1)S(1)}, bf16[64,2048]{1,0:T(8,128)(2,1)}, u32[]{:S(2)}, u32[]{:S(2)}) collective-permute-start(bf16[64,2048]{1,0:T(8,128)(2,1)S(1)} %constant_dynamic-slice_fusion.2), channel_id=1, source_target_pairs={{0,4},{4,0},{1,5},{5,1},{2,6},{6,2},{3,7},{7,3},{8,12},{12,8},{9,1... | collective-permute-start | bytes 786440 | tf_op jit(solution)/shard_map/ppermute | solution.py:38
  19.9 7.0 %collective-permute-start.5 = (s32[2,128]{1,0:T(2,128)S(1)}, s32[2,128]{1,0:T(2,128)S(1)}, u32[]{:S(2)}, u32[]{:S(2)}) collective-permute-start(s32[2,128]{1,0:T(2,128)S(1)} %collective-permute-done.3), channel_id=1, source_target_pairs={{0,4},{4,0},{1,5},{5,1},{2,6},{6,2},{3,7},{7,3},{8,12},{12,8},{9,1... | collective-permute-start | bytes 3080 | tf_op jit(solution)/shard_map/ppermute | solution.py:38
  21.1 1.2 copy-start.4
  22.4 0.7 copy-start.12
  23.8 0.8 copy-start.15
  27.7 18.4 %collective-permute-start.2 = (bf16[256,1024]{1,0:T(8,128)(2,1)}, bf16[256,1024]{1,0:T(8,128)(2,1)S(1)}, u32[]{:S(2)}, u32[]{:S(2)}) collective-permute-start(bf16[256,1024]{1,0:T(8,128)(2,1)} %copy-done.15), channel_id=1, source_target_pairs={{0,4},{4,0},{1,5},{5,1},{2,6},{6,2},{3,7},{7,3},{8,12},{12,8},{9,1... | collective-permute-start | bytes 1572872 | tf_op jit(solution)/shard_map/ppermute | solution.py:38
  29.3 7.1 %collective-permute-start.9 = (bf16[64,2048]{1,0:T(8,128)(2,1)}, bf16[64,2048]{1,0:T(8,128)(2,1)S(1)}, u32[]{:S(2)}, u32[]{:S(2)}) collective-permute-start(bf16[64,2048]{1,0:T(8,128)(2,1)} %collective-permute-done.1), channel_id=1, source_target_pairs={{0,8},{8,0},{16,24},{24,16},{1,9},{9,1},{17,25},{25,17},{2,10},{10... | collective-permute-start | bytes 786440 | tf_op jit(solution)/shard_map/ppermute | solution.py:38
  30.9 1.0 copy-start.1
  31.9 4.6 %copy-start.17 = (bf16[1,1024,2048]{2,1,0:T(8,128)(2,1)S(1)}, bf16[1,1024,2048]{2,1,0:T(8,128)(2,1)}, u32[]{:S(2)}) copy-start(bf16[1,1024,2048]{2,1,0:T(8,128)(2,1)} %param.20) | copy-start | bytes 12582916
  36.4 2.6 %copy-start.23 = (s32[128,2]{1,0:T(8,128)S(1)}, s32[128,2]{1,0:T(8,128)}, u32[]{:S(2)}) copy-start(s32[128,2]{1,0:T(8,128)} %copy.38) | copy-start | bytes 3076
  36.4 2.6 %copy-start.24 = (s32[128,2]{1,0:T(8,128)S(1)}, s32[128,2]{1,0:T(8,128)}, u32[]{:S(2)}) copy-start(s32[128,2]{1,0:T(8,128)} %copy.41) | copy-start | bytes 3076
  36.4 10.9 %copy-start.16 = (bf16[1,2048,1024]{2,1,0:T(8,128)(2,1)S(1)}, bf16[1,2048,1024]{2,1,0:T(8,128)(2,1)}, u32[]{:S(2)}) copy-start(bf16[1,2048,1024]{2,1,0:T(8,128)(2,1)} %param.19) | copy-start | bytes 12582916
  36.4 10.9 %collective-permute-start.8 = (bf16[192,2048]{1,0:T(8,128)(2,1)S(1)}, bf16[192,2048]{1,0:T(8,128)(2,1)S(1)}, u32[]{:S(2)}, u32[]{:S(2)}) collective-permute-start(bf16[192,2048]{1,0:T(8,128)(2,1)S(1)} %get-tuple-element.46), channel_id=1, source_target_pairs={{0,1},{1,0},{2,3},{3,2},{4,5},{5,4},{6,7},{7,6},{8,9},{9,8},{10,11... | collective-permute-start | bytes 2359304 | tf_op jit(solution)/shard_map/ppermute | solution.py:38
  38.4 7.7 %collective-permute-start.13 = (bf16[48,2048]{1,0:T(8,128)(2,1)S(1)}, bf16[48,2048]{1,0:T(8,128)(2,1)S(1)}, u32[]{:S(2)}, u32[]{:S(2)}) collective-permute-start(bf16[48,2048]{1,0:T(8,128)(2,1)S(1)} %get-tuple-element.87), channel_id=1, source_target_pairs={{0,2},{1,3},{2,0},{3,1},{4,6},{5,7},{6,4},{7,5},{8,10},{9,11},{10,... | collective-permute-start | bytes 589832 | tf_op jit(solution)/shard_map/ppermute | solution.py:223
  39.0 18.5 %collective-permute-start.15 = (bf16[48,2048]{1,0:T(8,128)(2,1)}, bf16[48,2048]{1,0:T(8,128)(2,1)S(1)}, u32[]{:S(2)}, u32[]{:S(2)}) collective-permute-start(bf16[48,2048]{1,0:T(8,128)(2,1)} %get-tuple-element.85), channel_id=1, source_target_pairs={{0,4},{1,5},{2,6},{3,7},{4,0},{5,1},{6,2},{7,3},{8,12},{9,13},{10,... | collective-permute-start | bytes 589832 | tf_op jit(solution)/shard_map/ppermute | solution.py:223
  39.7 17.8 %collective-permute-start.16 = (bf16[48,2048]{1,0:T(8,128)(2,1)}, bf16[48,2048]{1,0:T(8,128)(2,1)}, u32[]{:S(2)}, u32[]{:S(2)}) collective-permute-start(bf16[48,2048]{1,0:T(8,128)(2,1)} %get-tuple-element.84), channel_id=1, source_target_pairs={{0,6},{1,7},{2,4},{3,5},{4,2},{5,3},{6,0},{7,1},{8,14},{9,15},{10,... | collective-permute-start | bytes 589832 | tf_op jit(solution)/shard_map/ppermute | solution.py:223
  49.4 8.0 %copy-start.25 = (f32[128,2]{0,1:T(2,128)S(1)}, f32[128,2]{0,1:T(2,128)}, u32[]{:S(2)}) copy-start(f32[128,2]{0,1:T(2,128)} %param.17) | copy-start | bytes 3076
  49.4 19.2 %copy-start.5 = (bf16[128,2048]{1,0:T(8,128)(2,1)S(1)}, bf16[128,2048]{1,0:T(8,128)(2,1)}, u32[]{:S(2)}) copy-start(bf16[128,2048]{1,0:T(8,128)(2,1)} %refs_0_.3) | copy-start | bytes 1572868
  50.3 3.0 %collective-permute-start.14 = (bf16[48,2048]{1,0:T(8,128)(2,1)S(1)}, bf16[48,2048]{1,0:T(8,128)(2,1)S(1)}, u32[]{:S(2)}, u32[]{:S(2)}) collective-permute-start(bf16[48,2048]{1,0:T(8,128)(2,1)S(1)} %get-tuple-element.81), channel_id=1, source_target_pairs={{0,1},{1,0},{2,3},{3,2},{4,5},{5,4},{6,7},{7,6},{8,9},{9,8},{10,11... | collective-permute-start | bytes 589832 | tf_op jit(solution)/shard_map/ppermute | solution.py:223
  50.3 7.2 %collective-permute-start.10 = (bf16[48,2048]{1,0:T(8,128)(2,1)}, bf16[48,2048]{1,0:T(8,128)(2,1)}, u32[]{:S(2)}, u32[]{:S(2)}) collective-permute-start(bf16[48,2048]{1,0:T(8,128)(2,1)} %get-tuple-element.83), channel_id=1, source_target_pairs={{0,3},{1,2},{2,1},{3,0},{4,7},{5,6},{6,5},{7,4},{8,11},{9,10},{10,... | collective-permute-start | bytes 589832 | tf_op jit(solution)/shard_map/ppermute | solution.py:223
  50.9 11.5 %collective-permute-start.11 = (bf16[48,2048]{1,0:T(8,128)(2,1)}, bf16[48,2048]{1,0:T(8,128)(2,1)}, u32[]{:S(2)}, u32[]{:S(2)}) collective-permute-start(bf16[48,2048]{1,0:T(8,128)(2,1)} %get-tuple-element.82), channel_id=1, source_target_pairs={{0,5},{1,4},{2,7},{3,6},{4,1},{5,0},{6,3},{7,2},{8,13},{9,12},{10,... | collective-permute-start | bytes 589832 | tf_op jit(solution)/shard_map/ppermute | solution.py:223
  53.2 0.7 copy-start.10
  53.9 8.6 %collective-permute-start.17 = (bf16[48,2048]{1,0:T(8,128)(2,1)}, bf16[48,2048]{1,0:T(8,128)(2,1)}, u32[]{:S(2)}, u32[]{:S(2)}) collective-permute-start(bf16[48,2048]{1,0:T(8,128)(2,1)} %get-tuple-element.80), channel_id=1, source_target_pairs={{0,7},{1,6},{2,5},{3,4},{4,3},{5,2},{6,1},{7,0},{8,15},{9,14},{10,... | collective-permute-start | bytes 589832 | tf_op jit(solution)/shard_map/ppermute | solution.py:223
  62.5 0.9 copy-start.11
  65.4 8.4 %collective-permute-start.18 = (bf16[2,128,512]{2,1,0:T(8,128)(2,1)S(1)}, bf16[2,128,512]{2,1,0:T(8,128)(2,1)S(1)}, u32[]{:S(2)}, u32[]{:S(2)}) collective-permute-start(bf16[2,128,512]{2,1,0:T(8,128)(2,1)S(1)} %get-tuple-element.57), channel_id=1, source_target_pairs={{0,8},{8,0},{16,24},{24,16},{1,9},{9,1},{17,25},{25,17},{2,10},{10... | collective-permute-start | bytes 786440 | tf_op jit(solution)/shard_map/ppermute | solution.py:38
  66.3 21.1 %collective-permute-start.30 = (bf16[128,2048]{1,0:T(8,128)(2,1)S(1)}, bf16[128,2048]{1,0:T(8,128)(2,1)S(1)}, u32[]{:S(2)}, u32[]{:S(2)}) collective-permute-start(bf16[128,2048]{1,0:T(8,128)(2,1)S(1)} %constant_dynamic-update-slice_fusion.refs_2_), channel_id=1, source_target_pairs={{0,2},{1,3},{2,0},{3,1},{4,6},{5,7},{6,4},{7,5},{8,10},{9,11},{10,... | collective-permute-start | bytes 1572872 | tf_op jit(solution)/shard_map/ppermute | solution.py:38
  67.8 9.4 %collective-permute-start.12 = (bf16[256,512]{1,0:T(8,128)(2,1)}, bf16[256,512]{1,0:T(8,128)(2,1)S(1)}, u32[]{:S(2)}, u32[]{:S(2)}) collective-permute-start(bf16[256,512]{1,0:T(8,128)(2,1)} %fusion.1), channel_id=1, source_target_pairs={{0,4},{4,0},{1,5},{5,1},{2,6},{6,2},{3,7},{7,3},{8,12},{12,8},{9,1... | collective-permute-start | bytes 786440 | tf_op jit(solution)/shard_map/ppermute | solution.py:38
  68.6 22.9 %collective-permute-start.29 = (bf16[128,2048]{1,0:T(8,128)(2,1)S(1)}, bf16[128,2048]{1,0:T(8,128)(2,1)S(1)}, u32[]{:S(2)}, u32[]{:S(2)}) collective-permute-start(bf16[128,2048]{1,0:T(8,128)(2,1)S(1)} %copy-done.5), channel_id=1, source_target_pairs={{0,2},{1,3},{2,0},{3,1},{4,6},{5,7},{6,4},{7,5},{8,10},{9,11},{10,... | collective-permute-start | bytes 1572872 | tf_op jit(solution)/shard_map/ppermute | solution.py:38
  69.2 29.4 %collective-permute-start.21 = (bf16[1024,512]{1,0:T(8,128)(2,1)}, bf16[1024,512]{1,0:T(8,128)(2,1)S(1)}, u32[]{:S(2)}, u32[]{:S(2)}) collective-permute-start(bf16[1024,512]{1,0:T(8,128)(2,1)} %bitcast.85), channel_id=1, source_target_pairs={{0,4},{4,0},{1,5},{5,1},{2,6},{6,2},{3,7},{7,3},{8,12},{12,8},{9,1... | collective-permute-start | bytes 3145736 | tf_op jit(solution)/shard_map/ppermute | solution.py:38
  73.9 8.4 %collective-permute-start.19 = (bf16[128,512]{1,0:T(8,128)(2,1)S(1)}, bf16[128,512]{1,0:T(8,128)(2,1)S(1)}, u32[]{:S(2)}, u32[]{:S(2)}) collective-permute-start(bf16[128,512]{1,0:T(8,128)(2,1)S(1)} %fusion.48), channel_id=1, source_target_pairs={{0,16},{8,24},{16,0},{24,8},{1,17},{9,25},{17,1},{25,9},{2,18},{10... | collective-permute-start | bytes 393224 | tf_op jit(solution)/shard_map/ppermute | solution.py:38
  82.4 5.0 %collective-permute-start.20 = (bf16[128,512]{1,0:T(8,128)(2,1)S(1)}, bf16[128,512]{1,0:T(8,128)(2,1)S(1)}, u32[]{:S(2)}, u32[]{:S(2)}) collective-permute-start(bf16[128,512]{1,0:T(8,128)(2,1)S(1)} %fusion.50.refs_0_), channel_id=1, source_target_pairs={{0,8},{8,0},{16,24},{24,16},{1,9},{9,1},{17,25},{25,17},{2,10},{10... | collective-permute-start | bytes 393224 | tf_op jit(solution)/shard_map/ppermute | solution.py:38
  93.0 0.9 copy-start.7
  93.9 8.3 %collective-permute-start.31 = (bf16[192,2048]{1,0:T(8,128)(2,1)S(1)}, bf16[192,2048]{1,0:T(8,128)(2,1)S(1)}, u32[]{:S(2)}, u32[]{:S(2)}) collective-permute-start(bf16[192,2048]{1,0:T(8,128)(2,1)S(1)} %get-tuple-element.71), channel_id=1, source_target_pairs={{0,1},{1,0},{2,3},{3,2},{4,5},{5,4},{6,7},{7,6},{8,9},{9,8},{10,11... | collective-permute-start | bytes 2359304 | tf_op jit(solution)/shard_map/ppermute | solution.py:38
  98.6 11.9 %copy-start.18 = (bf16[1024,512]{1,0:T(8,128)(2,1)}, bf16[1024,512]{1,0:T(8,128)(2,1)S(1)}, u32[]{:S(2)}) copy-start(bf16[1024,512]{1,0:T(8,128)(2,1)S(1)} %collective-permute-done.21.refs_3_) | copy-start | bytes 3145732
  98.6 26.0 %collective-permute-start.24 = (bf16[1024,512]{1,0:T(8,128)(2,1)}, bf16[1024,512]{1,0:T(8,128)(2,1)}, u32[]{:S(2)}, u32[]{:S(2)}) collective-permute-start(bf16[1024,512]{1,0:T(8,128)(2,1)} %bitcast.24.refs_4_), channel_id=1, source_target_pairs={{0,4},{4,0},{1,5},{5,1},{2,6},{6,2},{3,7},{7,3},{8,12},{12,8},{9,1... | collective-permute-start | bytes 3145736 | tf_op jit(solution)/shard_map/ppermute | solution.py:38
  99.5 17.8 %collective-permute-start.22 = (bf16[2,128,512]{2,1,0:T(8,128)(2,1)S(1)}, bf16[2,128,512]{2,1,0:T(8,128)(2,1)S(1)}, u32[]{:S(2)}, u32[]{:S(2)}) collective-permute-start(bf16[2,128,512]{2,1,0:T(8,128)(2,1)S(1)} %pad_maximum_fusion), channel_id=1, source_target_pairs={{0,16},{8,24},{16,0},{24,8},{1,17},{9,25},{17,1},{25,9},{2,18},{10... | collective-permute-start | bytes 786440 | tf_op jit(solution)/shard_map/ppermute | solution.py:38
  102.2 0.9 copy-start.19
  110.5 6.9 %copy-start.2 = (bf16[128,2048]{1,0:T(8,128)(2,1)S(1)}, bf16[128,2048]{1,0:T(8,128)(2,1)}, u32[]{:S(2)}) copy-start(bf16[128,2048]{1,0:T(8,128)(2,1)} %tokens_ref.1) | copy-start | bytes 1572868
  110.5 6.9 %copy-start.13 = (f32[2048]{0:T(1024)S(1)}, f32[2048]{0:T(1024)}, u32[]{:S(2)}) copy-start(f32[2048]{0:T(1024)} %param.21) | copy-start | bytes 24580
  110.5 8.0 %copy-start.6 = (bf16[1,512,1024]{2,1,0:T(8,128)(2,1)S(1)}, bf16[1,512,1024]{2,1,0:T(8,128)(2,1)}, u32[]{:S(2)}) copy-start(bf16[1,512,1024]{2,1,0:T(8,128)(2,1)} %param.29) | copy-start | bytes 3145732
  116.4 18.4 %collective-permute-start.32 = (bf16[2,384,512]{2,1,0:T(8,128)(2,1)}, bf16[2,384,512]{2,1,0:T(8,128)(2,1)}, u32[]{:S(2)}, u32[]{:S(2)}) collective-permute-start(bf16[2,384,512]{2,1,0:T(8,128)(2,1)} %get-tuple-element.73), channel_id=1, source_target_pairs={{0,8},{8,0},{16,24},{24,16},{1,9},{9,1},{17,25},{25,17},{2,10},{10... | collective-permute-start | bytes 2359304 | tf_op jit(solution)/shard_map/ppermute | solution.py:38
  117.8 6.7 %copy-start.3 = (bf16[128,2048]{1,0:T(8,128)(2,1)}, bf16[128,2048]{1,0:T(8,128)(2,1)S(1)}, u32[]{:S(2)}) copy-start(bf16[128,2048]{1,0:T(8,128)(2,1)S(1)} %memory.1.refs_0_) | copy-start | bytes 1572868
  117.8 3.5 %collective-permute-start.23 = (bf16[128,2048]{1,0:T(8,128)(2,1)S(1)}, bf16[128,2048]{1,0:T(8,128)(2,1)}, u32[]{:S(2)}, u32[]{:S(2)}) collective-permute-start(bf16[128,2048]{1,0:T(8,128)(2,1)S(1)} %memory.1.refs_0_), channel_id=1, source_target_pairs={{0,1},{1,0},{2,3},{3,2},{4,5},{5,4},{6,7},{7,6},{8,9},{9,8},{10,11... | collective-permute-start | bytes 1572872 | tf_op jit(solution)/shard_map/ppermute | solution.py:38
  117.9 14.4 %collective-permute-start.25 = (bf16[128,2048]{1,0:T(8,128)(2,1)S(1)}, bf16[128,2048]{1,0:T(8,128)(2,1)}, u32[]{:S(2)}, u32[]{:S(2)}) collective-permute-start(bf16[128,2048]{1,0:T(8,128)(2,1)S(1)} %memory.1.refs_0_), channel_id=1, source_target_pairs={{0,2},{1,3},{2,0},{3,1},{4,6},{5,7},{6,4},{7,5},{8,10},{9,11},{10,... | collective-permute-start | bytes 1572872 | tf_op jit(solution)/shard_map/ppermute | solution.py:38
  118.5 27.0 %collective-permute-start.27 = (bf16[512,1024]{1,0:T(8,128)(2,1)S(1)}, bf16[512,1024]{1,0:T(8,128)(2,1)}, u32[]{:S(2)}, u32[]{:S(2)}) collective-permute-start(bf16[512,1024]{1,0:T(8,128)(2,1)S(1)} %bitcast.79), channel_id=1, source_target_pairs={{0,4},{4,0},{1,5},{5,1},{2,6},{6,2},{3,7},{7,3},{8,12},{12,8},{9,1... | collective-permute-start | bytes 3145736 | tf_op jit(solution)/shard_map/ppermute | solution.py:38
  120.2 14.6 %copy-start.20 = (f32[384,512]{1,0:T(8,128)S(1)}, f32[384,512]{1,0:T(8,128)}, u32[]{:S(2)}) copy-start(f32[384,512]{1,0:T(8,128)} %get-tuple-element.72) | copy-start | bytes 2359300
  130.0 15.5 %copy-start.8 = (bf16[128,512]{1,0:T(8,128)(2,1)S(1)}, bf16[128,512]{1,0:T(8,128)(2,1)}, u32[]{:S(2)}) copy-start(bf16[128,512]{1,0:T(8,128)(2,1)} %attend_sentence.2.mine_ref) | copy-start | bytes 393220
  130.0 15.5 %copy-start.14 = (s32[3]{0:T(128)S(1)}, s32[3]{0:T(128)}, u32[]{:S(2)}) copy-start(s32[3]{0:T(128)} %pad_add_fusion.1.place_ref) | copy-start | bytes 40
  132.4 4.6 %collective-permute-start.26 = (bf16[128,2048]{1,0:T(8,128)(2,1)}, bf16[128,2048]{1,0:T(8,128)(2,1)S(1)}, u32[]{:S(2)}, u32[]{:S(2)}) collective-permute-start(bf16[128,2048]{1,0:T(8,128)(2,1)} %collective-permute-done.25.refs_0_), channel_id=1, source_target_pairs={{0,1},{1,0},{2,3},{3,2},{4,5},{5,4},{6,7},{7,6},{8,9},{9,8},{10,11... | collective-permute-start | bytes 1572872 | tf_op jit(solution)/shard_map/ppermute | solution.py:38
  135.9 18.5 %collective-permute-start.33 = (bf16[384,512]{1,0:T(8,128)(2,1)S(1)}, bf16[384,512]{1,0:T(8,128)(2,1)S(1)}, u32[]{:S(2)}, u32[]{:S(2)}) collective-permute-start(bf16[384,512]{1,0:T(8,128)(2,1)S(1)} %fusion.35), channel_id=1, source_target_pairs={{0,16},{8,24},{16,0},{24,8},{1,17},{9,25},{17,1},{25,9},{2,18},{10... | collective-permute-start | bytes 1179656 | tf_op jit(solution)/shard_map/ppermute | solution.py:38
  136.9 0.8 copy-start.22
  137.7 17.4 %copy-start.21 = (f32[384,512]{1,0:T(8,128)S(1)}, f32[384,512]{1,0:T(8,128)}, u32[]{:S(2)}) copy-start(f32[384,512]{1,0:T(8,128)} %get-tuple-element.76) | copy-start | bytes 2359300
  145.5 0.9 copy-start.9
  146.4 14.1 %copy-start.26 = (s32[2]{0:T(128)S(1)}, s32[2]{0:T(128)}, u32[]{:S(2)}) copy-start(s32[2]{0:T(128)} %param.24) | copy-start | bytes 28
  148.4 6.0 %collective-permute-start.34 = (bf16[256,512]{1,0:T(8,128)(2,1)S(1)}, bf16[256,512]{1,0:T(8,128)(2,1)S(1)}, u32[]{:S(2)}, u32[]{:S(2)}) collective-permute-start(bf16[256,512]{1,0:T(8,128)(2,1)S(1)} %get-tuple-element.75), channel_id=1, source_target_pairs={{0,1},{1,0},{2,3},{3,2},{4,5},{5,4},{6,7},{7,6},{8,9},{9,8},{10,11... | collective-permute-start | bytes 786440 | tf_op jit(solution)/shard_map/ppermute | solution.py:38
  154.4 6.3 %collective-permute-start.28 = (bf16[256,512]{1,0:T(8,128)(2,1)S(1)}, bf16[256,512]{1,0:T(8,128)(2,1)S(1)}, u32[]{:S(2)}, u32[]{:S(2)}) collective-permute-start(bf16[256,512]{1,0:T(8,128)(2,1)S(1)} %get-tuple-element.65), channel_id=1, source_target_pairs={{0,1},{1,0},{2,3},{3,2},{4,5},{5,4},{6,7},{7,6},{8,9},{9,8},{10,11... | collective-permute-start | bytes 786440 | tf_op jit(solution)/shard_map/ppermute | solution.py:38
  154.5 8.8 %collective-permute-start.35 = (bf16[256,512]{1,0:T(8,128)(2,1)S(1)}, bf16[256,512]{1,0:T(8,128)(2,1)S(1)}, u32[]{:S(2)}, u32[]{:S(2)}) collective-permute-start(bf16[256,512]{1,0:T(8,128)(2,1)S(1)} %convert_add_fusion.3), channel_id=1, source_target_pairs={{0,2},{1,3},{2,0},{3,1},{4,6},{5,7},{6,4},{7,5},{8,10},{9,11},{10,... | collective-permute-start | bytes 786440 | tf_op jit(solution)/shard_map/ppermute | solution.py:38
  157.0 11.7 %all-to-all-start = ((bf16[8,48,512]{2,1,0:T(8,128)(2,1)}), bf16[8,48,512]{2,1,0:T(8,128)(2,1)S(1)}, u32[]{:S(2)}, u32[]{:S(2)}) async-start(bf16[8,48,512]{2,1,0:T(8,128)(2,1)} %bitcast.31), calls=%async_computation | async-start | bytes 786432 | tf_op jit(solution)/shard_map/all_to_all | solution.py:142
